TPU v7x, 32 devices: a whole 2x2x4 slice. The times are simulated.
32 devices in a mesh: row: 8 (over y, x, core), col: 4 (over z).
Axes of the slice: x: 2, y: 2, z: 4, core: 2. Of those that a mesh axis runs over, the one named last changes fastest.
Arguments:
- features: bfloat16 [64, 512, 256], P('row', 'col'), may hold values from -6 to 6
- target: bfloat16 [64, 512, 256], P('row', 'col'), may hold values from -6 to 6
- hole_mask: int32 [64, 512], P('row', 'col'), may hold values 0 or 1
- kernel_first: bfloat16 [3, 3, 256, 256], replicated, may hold values from -0.125 to 0.125
- kernel_second: bfloat16 [3, 3, 256, 256], replicated, may hold values from -0.125 to 0.125
- inputs: bfloat16 [64, 512, 512], P(('row', 'col')), may hold values from -6 to 6
- weight_in: bfloat16 [512, 192], replicated, may hold values from -0.25 to 0.25
- weight_out: bfloat16 [192, 256], replicated, may hold values from -0.4375 to 0.4375
- weight_local: bfloat16 [512, 256], replicated, may hold values from -0.25 to 0.25
- weight_mix: bfloat16 [384, 384], replicated, may hold values from -0.3125 to 0.3125
Outputs:
- grad_inputs: bfloat16 [64, 512, 512], P(('row', 'col'))
Inputs may be any that keep to these rules, and one draw needn't show every extreme that they name: `hole_mask`: 1 marks a pixel to be filled.
All inputs are finite; a program needn't handle non-finite values. No bound on the sum of `hole_mask` on one device may be relied on, other than what follows from the above.
Results may differ from a plain program's by a relative error of at most 0.0095.
Values may be sent and summed in bfloat16 or wider, within the bound.
No kernel may reach another device: no remote copies, remote signals or barrier semaphores. Data moves between devices by JAX's collectives and lax.ppermute only.
A program may use at most 64 MiB of HBM per device.

v0:
```python
import math

import jax
import jax.numpy as jnp
from jax import lax
from jax.sharding import PartitionSpec as P


def padded_2(shard, sides, width):
    for axis, dim in sides:
        size, length = (lax.axis_size(axis), shard.shape[dim])
        up = [(i, (i + 1) % size) for i in range(size - 1)]
        down = [(j, i) for i, j in up]
        last = lax.slice_in_dim(shard, length - width, length, axis=dim)
        initial = lax.slice_in_dim(shard, 0, width, axis=dim)
        before = lax.ppermute(last, axis, up)
        after = lax.ppermute(initial, axis, down)
        shard = jnp.concatenate([before, shard, after], axis=dim)
    return shard


def conv_valid(padded, kernel):
    output = lax.conv_general_dilated(
        padded[None],
        kernel,
        (1, 1),
        "VALID",
        rhs_dilation=(2, 2),
        dimension_numbers=("NHWC", "HWIO", "NHWC"),
        preferred_element_type=jnp.float32,
    )
    return output[0]


def adjoint_kernel(kernel):
    return jnp.transpose(jnp.flip(kernel, (0, 1)), (0, 1, 3, 2))


def silu_slope(pre_value):
    sigmoid_value = jax.nn.sigmoid(pre_value)
    return sigmoid_value * (1.0 + pre_value * (1.0 - sigmoid_value))


def dft_tables(first_ids, second_ids, length):
    phases = first_ids[:, None] * second_ids[None, :] % length
    angles = phases.astype(jnp.float32) * (2.0 * math.pi / length)
    return (jnp.cos(angles).astype(jnp.bfloat16), jnp.sin(angles).astype(jnp.bfloat16))


def column_tables(grid_width):
    freq_ids = jnp.arange(grid_width // 2, dtype=jnp.int32)
    col_ids = jnp.arange(grid_width, dtype=jnp.int32)
    cos_table, sin_table = dft_tables(freq_ids, col_ids, grid_width)
    alternate = (2 * (col_ids % 2) - 1).astype(jnp.float32).astype(jnp.bfloat16)
    sin_table = jnp.where((freq_ids == 0)[:, None], alternate[None, :], sin_table)
    return (cos_table, sin_table)


def column_transform(signal, cos_table, sin_table, norm_factor):
    cosine_part = jnp.einsum("rws,kw->rks", signal, cos_table, preferred_element_type=jnp.float32)
    sine_part = jnp.einsum("rws,kw->rks", signal, sin_table, preferred_element_type=jnp.float32)
    return (jnp.concatenate([cosine_part, -sine_part], axis=-1) * norm_factor).astype(jnp.bfloat16)


def row_forward(spectrum, cos_table, sin_table, norm_factor, half_width):
    cosine_part = jnp.einsum("kp,pmc->kmc", cos_table, spectrum, preferred_element_type=jnp.float32)
    sine_part = jnp.einsum("kp,pmc->kmc", sin_table, spectrum, preferred_element_type=jnp.float32)
    real_part = cosine_part[..., :half_width] + sine_part[..., half_width:]
    imag_part = cosine_part[..., half_width:] - sine_part[..., :half_width]
    return jnp.concatenate([real_part, imag_part], axis=-1) * norm_factor


def row_inverse(spectrum, cos_table, sin_table, norm_factor, half_width):
    cosine_part = jnp.einsum("kp,kmc->pmc", cos_table, spectrum, preferred_element_type=jnp.float32)
    sine_part = jnp.einsum("kp,kmc->pmc", sin_table, spectrum, preferred_element_type=jnp.float32)
    real_part = cosine_part[..., :half_width] - sine_part[..., half_width:]
    imag_part = cosine_part[..., half_width:] + sine_part[..., :half_width]
    return (jnp.concatenate([real_part, imag_part], axis=-1) * norm_factor).astype(jnp.bfloat16)


def column_inverse(spectrum, cos_table, sin_table, norm_factor, half_width):
    cosine_part = jnp.einsum(
        "rks,kw->rws", spectrum[..., :half_width], cos_table, preferred_element_type=jnp.float32
    )
    sine_part = jnp.einsum(
        "rks,kw->rws", spectrum[..., half_width:], sin_table, preferred_element_type=jnp.float32
    )
    return ((cosine_part - sine_part) * norm_factor).astype(jnp.bfloat16)


def shards(
    features,
    target,
    hole_mask,
    kernel_first,
    kernel_second,
    inputs,
    weight_in,
    weight_out,
    weight_local,
    weight_mix,
):
    tile_rows = features.shape[0]
    tile_cols = features.shape[1]
    row_devices = lax.axis_size("row")
    col_devices = lax.axis_size("col")
    height = tile_rows * row_devices
    grid_width = tile_cols * col_devices
    half_width = weight_in.shape[1]
    wide_feat = padded_2(features, (("row", 0), ("col", 1)), 4)
    pre_wide = conv_valid(wide_feat, kernel_first)
    row_ids = lax.axis_index("row") * tile_rows - 2 + jnp.arange(tile_rows + 4, dtype=jnp.int32)
    col_ids = lax.axis_index("col") * tile_cols - 2 + jnp.arange(tile_cols + 4, dtype=jnp.int32)
    row_inside = (row_ids >= 0) & (row_ids < height)
    col_inside = (col_ids >= 0) & (col_ids < grid_width)
    inside_mask = row_inside[:, None] & col_inside[None, :]
    act_wide = jnp.where(inside_mask[:, :, None], jax.nn.silu(pre_wide), 0.0).astype(jnp.bfloat16)
    pre_first = pre_wide[2:-2, 2:-2]
    pre_second = conv_valid(act_wide, kernel_second)
    hole_weight = 1.0 + 2.0 * hole_mask.astype(jnp.float32)
    loss_grad = (hole_weight[:, :, None] * (pre_second - target.astype(jnp.float32))).astype(
        jnp.bfloat16
    )
    loss_wide = padded_2(loss_grad, (("row", 0), ("col", 1)), 2)
    grad_act = conv_valid(loss_wide, adjoint_kernel(kernel_second))
    grad_pre = (grad_act * silu_slope(pre_first)).astype(jnp.bfloat16)
    grad_wide = padded_2(grad_pre, (("row", 0), ("col", 1)), 2)
    grad_feat = conv_valid(grad_wide, adjoint_kernel(kernel_first)).astype(jnp.bfloat16)
    strip_grad = lax.all_to_all(grad_feat, "col", split_axis=0, concat_axis=1, tiled=True)
    spatial = jnp.einsum(
        "rwf,fs->rws", inputs, weight_in, preferred_element_type=jnp.float32
    ).astype(jnp.bfloat16)
    cos_cols, sin_cols = column_tables(grid_width)
    col_factor = 1.0 / math.sqrt(grid_width)
    row_factor = 1.0 / math.sqrt(height)
    spatial_cols = column_transform(spatial, cos_cols, sin_cols, col_factor)
    grad_spec = jnp.einsum(
        "rwc,sc->rws", strip_grad, weight_out, preferred_element_type=jnp.float32
    ).astype(jnp.bfloat16)
    grad_cols = column_transform(grad_spec, cos_cols, sin_cols, col_factor)
    grad_local = jnp.einsum(
        "rwc,fc->rwf", strip_grad, weight_local, preferred_element_type=jnp.float32
    )
    strip_rows = inputs.shape[0]
    slot_ids = jnp.arange(height, dtype=jnp.int32)
    spatial_moved, grad_moved = (
        lax.all_to_all(spatial_cols, "row", split_axis=1, concat_axis=0, tiled=True),
        lax.all_to_all(grad_cols, "row", split_axis=1, concat_axis=0, tiled=True),
    )
    spatial_moved, grad_moved = (
        lax.all_to_all(spatial_moved, "col", split_axis=1, concat_axis=0, tiled=True),
        lax.all_to_all(grad_moved, "col", split_axis=1, concat_axis=0, tiled=True),
    )
    block_ids = slot_ids // strip_rows
    within_ids = slot_ids % strip_rows
    source_col = block_ids // row_devices
    source_row = block_ids % row_devices
    row_order = (source_row * col_devices + source_col) * strip_rows + within_ids
    cos_rows, sin_rows = dft_tables(slot_ids, row_order, height)
    spatial_freq = row_forward(spatial_moved, cos_rows, sin_rows, row_factor, half_width)
    grad_freq = row_forward(grad_moved, cos_rows, sin_rows, row_factor, half_width)
    pre_mix = jnp.einsum(
        "kmc,cd->kmd",
        spatial_freq.astype(jnp.bfloat16),
        weight_mix,
        preferred_element_type=jnp.float32,
    )
    grad_mix = (grad_freq * silu_slope(pre_mix)).astype(jnp.bfloat16)
    grad_back = jnp.einsum(
        "kmd,cd->kmc", grad_mix, weight_mix, preferred_element_type=jnp.float32
    ).astype(jnp.bfloat16)
    grad_rows = row_inverse(grad_back, cos_rows, sin_rows, row_factor, half_width)
    returned = lax.all_to_all(grad_rows, "col", split_axis=0, concat_axis=1, tiled=True)
    returned = lax.all_to_all(returned, "row", split_axis=0, concat_axis=1, tiled=True)
    grad_spatial = column_inverse(returned, cos_cols, sin_cols, col_factor, half_width)
    grad_total = (
        jnp.einsum("rws,fs->rwf", grad_spatial, weight_in, preferred_element_type=jnp.float32)
        + grad_local
    )
    return grad_total.astype(jnp.bfloat16)


def solution(mesh):
    in_specs = (
        P("row", "col", None),
        P("row", "col", None),
        P("row", "col"),
        P(),
        P(),
        P(("row", "col"), None, None),
        P(),
        P(),
        P(),
        P(),
    )
    out_specs = P(("row", "col"), None, None)
    return jax.shard_map(shards, mesh=mesh, in_specs=in_specs, out_specs=out_specs, check_vma=False)
```

profile of v0, /device:TPU:1, one launch (start us, length us, event | category | flops | bytes accessed | tf_op | source)
XLA Modules:
  0.0 182.9 jit_solution(6590072714757528469)
XLA Ops:
  1.6 4.5 %collective-permute-start = (bf16[4,128,256]{2,0,1:T(4,128)(2,1)S(1)}, bf16[4,128,256]{2,0,1:T(4,128)(2,1)S(1)}, u32[]{:S(2)}, u32[]{:S(2)}) collective-permute-start(bf16[4,128,256]{2,0,1:T(4,128)(2,1)S(1)} %get-tuple-element.21), channel_id=1, source_target_pairs={{0,4},{4,8},{8,12},{12,16},{16,20},{20,24},{24,28},{1,5},{5,9},{9,... | collective-permute-start | bytes 786440 | tf_op jit(solution)/shard_map/ppermute | solution.py:16
  6.1 1.9 %collective-permute-start.1 = (bf16[4,128,256]{2,0,1:T(4,128)(2,1)S(1)}, bf16[4,128,256]{2,0,1:T(4,128)(2,1)S(1)}, u32[]{:S(2)}, u32[]{:S(2)}) collective-permute-start(bf16[4,128,256]{2,0,1:T(4,128)(2,1)S(1)} %get-tuple-element.22), channel_id=1, source_target_pairs={{4,0},{8,4},{12,8},{16,12},{20,16},{24,20},{28,24},{5,1},{9,5},{13... | collective-permute-start | bytes 786440 | tf_op jit(solution)/shard_map/ppermute | solution.py:17
  9.4 4.5 %collective-permute-done.1 = bf16[4,128,256]{2,0,1:T(4,128)(2,1)S(1)} collective-permute-done((bf16[4,128,256]{2,0,1:T(4,128)(2,1)S(1)}, bf16[4,128,256]{2,0,1:T(4,128)(2,1)S(1)}, u32[]{:S(2)}, u32[]{:S(2)}) %collective-permute-start.1) | collective-permute-done | bytes 262176 | tf_op jit(solution)/shard_map/ppermute | solution.py:17
  13.9 3.2 %collective-permute-start.2 = (bf16[16,4,256]{2,0,1:T(8,128)(2,1)S(1)}, bf16[16,4,256]{2,0,1:T(8,128)(2,1)S(1)}, u32[]{:S(2)}, u32[]{:S(2)}) collective-permute-start(bf16[16,4,256]{2,0,1:T(8,128)(2,1)S(1)} %get-tuple-element.11), channel_id=1, source_target_pairs={{0,1},{1,2},{2,3},{4,5},{5,6},{6,7},{8,9},{9,10},{10,11},{12,13},{... | collective-permute-start | bytes 98312 | tf_op jit(solution)/shard_map/ppermute | solution.py:16
  18.6 3.2 %collective-permute-done.3 = bf16[16,4,256]{2,0,1:T(8,128)(2,1)S(1)} collective-permute-done((bf16[16,4,256]{2,0,1:T(8,128)(2,1)S(1)}, bf16[16,4,256]{2,0,1:T(8,128)(2,1)S(1)}, u32[]{:S(2)}, u32[]{:S(2)}) %collective-permute-start.3) | collective-permute-done | bytes 32800 | tf_op jit(solution)/shard_map/ppermute | solution.py:17
  23.2 3.5 %divide_multiply_fusion = (bf16[12,8,17,256]{3,1,2,0:T(8,128)(2,1)S(1)}, f32[12,8,17,256]{3,1,2,0:T(8,128)}) fusion(bf16[3,3,256,256]{3,2,1,0:T(8,128)(2,1)S(1)} %copy-done, bf16[16,1,7,4,256]{4,2,3,0,1:T(8,128)(2,1)S(1)} %slice.119, bf16[16,1,8,17,256]{4,2,3,0,1:T(8,128)(2,1)S(1)} %copy.116, pred[8,17]{0,1:T(8,128)(4,1)S(1)} %copy-done.12), kind=kOutput, calls=%fused_computation.10 | convolution fusion | flops 1931821056 | bytes 5030024 | tf_op jit(solution)/shard_map/conv_general_dilated | solution.py:23
  32.3 3.2 %collective-permute-start.4 = (bf16[2,128,256]{2,0,1:T(2,128)(2,1)S(1)}, bf16[2,128,256]{2,0,1:T(2,128)(2,1)S(1)}, u32[]{:S(2)}, u32[]{:S(2)}) collective-permute-start(bf16[2,128,256]{2,0,1:T(2,128)(2,1)S(1)} %get-tuple-element.19), channel_id=1, source_target_pairs={{0,4},{4,8},{8,12},{12,16},{16,20},{20,24},{24,28},{1,5},{5,9},{9,... | collective-permute-start | bytes 393224 | tf_op jit(solution)/shard_map/ppermute | solution.py:16
  35.4 1.9 %collective-permute-start.5 = (bf16[2,128,256]{2,0,1:T(2,128)(2,1)S(1)}, bf16[2,128,256]{2,0,1:T(2,128)(2,1)S(1)}, u32[]{:S(2)}, u32[]{:S(2)}) collective-permute-start(bf16[2,128,256]{2,0,1:T(2,128)(2,1)S(1)} %get-tuple-element.20), channel_id=1, source_target_pairs={{4,0},{8,4},{12,8},{16,12},{20,16},{24,20},{28,24},{5,1},{9,5},{13... | collective-permute-start | bytes 393224 | tf_op jit(solution)/shard_map/ppermute | solution.py:17
  38.0 3.8 %collective-permute-done.5 = bf16[2,128,256]{2,0,1:T(2,128)(2,1)S(1)} collective-permute-done((bf16[2,128,256]{2,0,1:T(2,128)(2,1)S(1)}, bf16[2,128,256]{2,0,1:T(2,128)(2,1)S(1)}, u32[]{:S(2)}, u32[]{:S(2)}) %collective-permute-start.5) | collective-permute-done | bytes 131104 | tf_op jit(solution)/shard_map/ppermute | solution.py:17
  41.7 3.2 %collective-permute-start.6 = (bf16[12,2,256]{2,0,1:T(8,128)(2,1)S(1)}, bf16[12,2,256]{2,0,1:T(8,128)(2,1)S(1)}, u32[]{:S(2)}, u32[]{:S(2)}) collective-permute-start(bf16[12,2,256]{2,0,1:T(8,128)(2,1)S(1)} %get-tuple-element.15), channel_id=1, source_target_pairs={{0,1},{1,2},{2,3},{4,5},{5,6},{6,7},{8,9},{9,10},{10,11},{12,13},{... | collective-permute-start | bytes 36872 | tf_op jit(solution)/shard_map/ppermute | solution.py:16
  46.6 2.8 %collective-permute-done.7 = bf16[12,2,256]{2,0,1:T(8,128)(2,1)S(1)} collective-permute-done((bf16[12,2,256]{2,0,1:T(8,128)(2,1)S(1)}, bf16[12,2,256]{2,0,1:T(8,128)(2,1)S(1)}, u32[]{:S(2)}, u32[]{:S(2)}) %collective-permute-start.7) | collective-permute-done | bytes 12320 | tf_op jit(solution)/shard_map/ppermute | solution.py:17
  53.2 3.2 %collective-permute-start.8 = (bf16[2,128,256]{2,0,1:T(2,128)(2,1)S(1)}, bf16[2,128,256]{2,0,1:T(2,128)(2,1)S(1)}, u32[]{:S(2)}, u32[]{:S(2)}) collective-permute-start(bf16[2,128,256]{2,0,1:T(2,128)(2,1)S(1)} %get-tuple-element.17), channel_id=1, source_target_pairs={{0,4},{4,8},{8,12},{12,16},{16,20},{20,24},{24,28},{1,5},{5,9},{9,... | collective-permute-start | bytes 393224 | tf_op jit(solution)/shard_map/ppermute | solution.py:16
  56.4 1.9 %collective-permute-start.9 = (bf16[2,128,256]{2,0,1:T(2,128)(2,1)S(1)}, bf16[2,128,256]{2,0,1:T(2,128)(2,1)S(1)}, u32[]{:S(2)}, u32[]{:S(2)}) collective-permute-start(bf16[2,128,256]{2,0,1:T(2,128)(2,1)S(1)} %get-tuple-element.18), channel_id=1, source_target_pairs={{4,0},{8,4},{12,8},{16,12},{20,16},{24,20},{28,24},{5,1},{9,5},{13... | collective-permute-start | bytes 393224 | tf_op jit(solution)/shard_map/ppermute | solution.py:17
  58.9 4.2 %collective-permute-done.9 = bf16[2,128,256]{2,0,1:T(2,128)(2,1)S(1)} collective-permute-done((bf16[2,128,256]{2,0,1:T(2,128)(2,1)S(1)}, bf16[2,128,256]{2,0,1:T(2,128)(2,1)S(1)}, u32[]{:S(2)}, u32[]{:S(2)}) %collective-permute-start.9) | collective-permute-done | bytes 131104 | tf_op jit(solution)/shard_map/ppermute | solution.py:17
  63.1 3.2 %collective-permute-start.10 = (bf16[12,2,256]{2,0,1:T(8,128)(2,1)S(1)}, bf16[12,2,256]{2,0,1:T(8,128)(2,1)S(1)}, u32[]{:S(2)}, u32[]{:S(2)}) collective-permute-start(bf16[12,2,256]{2,0,1:T(8,128)(2,1)S(1)} %get-tuple-element.13), channel_id=1, source_target_pairs={{0,1},{1,2},{2,3},{4,5},{5,6},{6,7},{8,9},{9,10},{10,11},{12,13},{... | collective-permute-start | bytes 36872 | tf_op jit(solution)/shard_map/ppermute | solution.py:16
  67.6 3.1 %fusion.67 = f32[256,384]{0,1} fusion(bf16[512,384]{0,1:T(8,128)(2,1)S(1)} %bitcast.184), kind=kOutput, calls=%fused_computation.100 | convolution fusion | flops 102629376 | bytes 786432
  74.6 3.5 %all-to-all-start = ((bf16[8,128,256]{2,1,0:T(8,128)(2,1)}), bf16[8,128,256]{2,1,0:T(8,128)(2,1)S(1)}, u32[]{:S(2)}, u32[]{:S(2)}) async-start(bf16[8,128,256]{2,1,0:T(8,128)(2,1)} %copy.132), calls=%async_computation | async-start | bytes 1048576 | tf_op jit(solution)/shard_map/all_to_all | solution.py:129
  78.1 2.2 %fusion.71 = f32[256,384]{0,1:S(1)} fusion(bf16[512,384]{0,1:T(8,128)(2,1)S(1)} %bitcast.185, pred[256]{0:T(512)(128)(4,1)S(1)} %iota_compare_fusion.2, bf16[512]{0:T(512)(128)(2,1)S(1)} %fusion.105), kind=kOutput, calls=%fused_computation.103 | convolution fusion | flops 102760448 | bytes 787712
  81.5 9.7 %all-to-all-done = bf16[8,128,256]{2,1,0:T(8,128)(2,1)S(1)} async-done(((bf16[8,128,256]{2,1,0:T(8,128)(2,1)}), bf16[8,128,256]{2,1,0:T(8,128)(2,1)S(1)}, u32[]{:S(2)}, u32[]{:S(2)}) %all-to-all-start) | async-done | bytes 524320 | tf_op jit(solution)/shard_map/all_to_all | solution.py:129
  91.2 5.0 %all-to-all-start.3 = ((bf16[2,256,384]{2,0,1:T(2,128)(2,1)}), bf16[2,256,384]{2,0,1:T(2,128)(2,1)S(1)}, u32[]{:S(2)}, u32[]{:S(2)}) async-start(bf16[2,256,384]{2,0,1:T(2,128)(2,1)} %copy.142), calls=%async_computation.3 | async-start | bytes 786432 | tf_op jit(solution)/shard_map/all_to_all | solution.py:147
  96.7 2.2 %fusion.73 = f32[256,384]{0,1:S(1)} fusion(bf16[512,384]{0,1:T(8,128)(2,1)S(1)} %bitcast.188, pred[256]{0:T(512)(128)(4,1)S(1)} %iota_compare_fusion.2, bf16[512]{0:T(512)(128)(2,1)S(1)} %fusion.105), kind=kOutput, calls=%fused_computation.104 | convolution fusion | flops 102760448 | bytes 787712
  98.8 2.1 %fusion.68 = f32[256,384]{0,1:S(1)} fusion(bf16[512,384]{0,1:T(8,128)(2,1)S(1)} %bitcast.189), kind=kOutput, calls=%fused_computation.101 | convolution fusion | flops 102629376 | bytes 786432
  102.3 5.7 %all-to-all-start.1 = ((bf16[2,256,384]{2,0,1:T(2,128)(2,1)}), bf16[2,256,384]{2,0,1:T(2,128)(2,1)S(1)}, u32[]{:S(2)}, u32[]{:S(2)}) async-start(bf16[2,256,384]{2,0,1:T(2,128)(2,1)} %copy.134), calls=%async_computation.1 | async-start | bytes 786432 | tf_op jit(solution)/shard_map/all_to_all | solution.py:148
  109.0 5.1 %all-to-all-done.1 = bf16[2,256,384]{2,0,1:T(2,128)(2,1)S(1)} async-done(((bf16[2,256,384]{2,0,1:T(2,128)(2,1)}), bf16[2,256,384]{2,0,1:T(2,128)(2,1)S(1)}, u32[]{:S(2)}, u32[]{:S(2)}) %all-to-all-start.1) | async-done | bytes 393248 | tf_op jit(solution)/shard_map/all_to_all | solution.py:148
  114.0 3.5 %all-to-all-start.4 = ((bf16[16,32,384]{2,0,1:T(8,128)(2,1)}), bf16[16,32,384]{2,0,1:T(8,128)(2,1)S(1)}, u32[]{:S(2)}, u32[]{:S(2)}) async-start(bf16[16,32,384]{2,0,1:T(8,128)(2,1)} %copy.145), calls=%async_computation.4 | async-start | bytes 786432 | tf_op jit(solution)/shard_map/all_to_all | solution.py:151
  118.5 8.0 %all-to-all-done.4 = bf16[16,32,384]{2,0,1:T(8,128)(2,1)S(1)} async-done(((bf16[16,32,384]{2,0,1:T(8,128)(2,1)}), bf16[16,32,384]{2,0,1:T(8,128)(2,1)S(1)}, u32[]{:S(2)}, u32[]{:S(2)}) %all-to-all-start.4) | async-done | bytes 393248 | tf_op jit(solution)/shard_map/all_to_all | solution.py:151
  126.6 4.2 %all-to-all-start.2 = ((bf16[16,32,384]{2,0,1:T(8,128)(2,1)}), bf16[16,32,384]{2,0,1:T(8,128)(2,1)}, u32[]{:S(2)}, u32[]{:S(2)}) async-start(bf16[16,32,384]{2,0,1:T(8,128)(2,1)} %copy.137), calls=%async_computation.2 | async-start | bytes 786432 | tf_op jit(solution)/shard_map/all_to_all | solution.py:152
  131.8 6.8 %all-to-all-done.2 = bf16[16,32,384]{2,0,1:T(8,128)(2,1)} async-done(((bf16[16,32,384]{2,0,1:T(8,128)(2,1)}), bf16[16,32,384]{2,0,1:T(8,128)(2,1)}, u32[]{:S(2)}, u32[]{:S(2)}) %all-to-all-start.2) | async-done | bytes 393248 | tf_op jit(solution)/shard_map/all_to_all | solution.py:152
  144.3 14.1 %all_to_all.126 = bf16[64,8,384]{2,1,0:T(8,128)(2,1)S(1)} all-to-all(bf16[64,8,384]{2,1,0:T(8,128)(2,1)S(1)} %copy.156), channel_id=1, replica_groups=mesh['row'=8,'col'=4] {'col'}, dimensions={0} | all-to-all | bytes 786432 | tf_op jit(solution)/shard_map/all_to_all | solution.py:173
  158.5 17.0 %all_to_all.127 = bf16[16,32,384]{2,1,0:T(8,128)(2,1)S(1)} all-to-all(bf16[16,32,384]{2,1,0:T(8,128)(2,1)S(1)} %bitcast.178), channel_id=1, replica_groups=mesh['row'=8,'col'=4] {'row'}, dimensions={0} | all-to-all | bytes 786432 | tf_op jit(solution)/shard_map/all_to_all | solution.py:174
  175.8 2.2 %fusion.69 = f32[512,384]{0,1:S(1)} fusion(bf16[256,384]{0,1:T(8,128)(2,1)S(1)} %bitcast.190, pred[256]{0:T(512)(128)(4,1)S(1)} %iota_compare_fusion.2, bf16[512]{0:T(512)(128)(2,1)S(1)} %fusion.105), kind=kOutput, calls=%fused_computation.102 | convolution fusion | flops 102760448 | bytes 984320
  178.2 2.3 %fusion.66 = f32[512,384]{0,1:S(1)} fusion(bf16[256,384]{0,1:T(8,128)(2,1)S(1)} %bitcast.191), kind=kOutput, calls=%fused_computation.99 | convolution fusion | flops 102629376 | bytes 983040
  (118 shorter events, 37.2 us)
Async XLA Ops:
  0.0 23.0 %copy-start = (bf16[3,3,256,256]{3,2,1,0:T(8,128)(2,1)S(1)}, bf16[3,3,256,256]{3,2,1,0:T(8,128)(2,1)}, u32[]{:S(2)}) copy-start(bf16[3,3,256,256]{3,2,1,0:T(8,128)(2,1)} %param.13) | copy-start | bytes 3538948
  0.0 8.1 %copy-start.9 = (s32[8,128]{1,0:T(8,128)S(1)}, s32[8,128]{1,0:T(8,128)}, u32[]{:S(2)}) copy-start(s32[8,128]{1,0:T(8,128)} %param.12) | copy-start | bytes 12292
  1.6 7.8 %collective-permute-start = (bf16[4,128,256]{2,0,1:T(4,128)(2,1)S(1)}, bf16[4,128,256]{2,0,1:T(4,128)(2,1)S(1)}, u32[]{:S(2)}, u32[]{:S(2)}) collective-permute-start(bf16[4,128,256]{2,0,1:T(4,128)(2,1)S(1)} %get-tuple-element.21), channel_id=1, source_target_pairs={{0,4},{4,8},{8,12},{12,16},{16,20},{20,24},{24,28},{1,5},{5,9},{9,... | collective-permute-start | bytes 786440 | tf_op jit(solution)/shard_map/ppermute | solution.py:16
  6.1 7.8 %collective-permute-start.1 = (bf16[4,128,256]{2,0,1:T(4,128)(2,1)S(1)}, bf16[4,128,256]{2,0,1:T(4,128)(2,1)S(1)}, u32[]{:S(2)}, u32[]{:S(2)}) collective-permute-start(bf16[4,128,256]{2,0,1:T(4,128)(2,1)S(1)} %get-tuple-element.22), channel_id=1, source_target_pairs={{4,0},{8,4},{12,8},{16,12},{20,16},{24,20},{28,24},{5,1},{9,5},{13... | collective-permute-start | bytes 786440 | tf_op jit(solution)/shard_map/ppermute | solution.py:17
  13.9 4.7 %collective-permute-start.2 = (bf16[16,4,256]{2,0,1:T(8,128)(2,1)S(1)}, bf16[16,4,256]{2,0,1:T(8,128)(2,1)S(1)}, u32[]{:S(2)}, u32[]{:S(2)}) collective-permute-start(bf16[16,4,256]{2,0,1:T(8,128)(2,1)S(1)} %get-tuple-element.11), channel_id=1, source_target_pairs={{0,1},{1,2},{2,3},{4,5},{5,6},{6,7},{8,9},{9,10},{10,11},{12,13},{... | collective-permute-start | bytes 98312 | tf_op jit(solution)/shard_map/ppermute | solution.py:16
  17.2 4.7 %collective-permute-start.3 = (bf16[16,4,256]{2,0,1:T(8,128)(2,1)S(1)}, bf16[16,4,256]{2,0,1:T(8,128)(2,1)S(1)}, u32[]{:S(2)}, u32[]{:S(2)}) collective-permute-start(bf16[16,4,256]{2,0,1:T(8,128)(2,1)S(1)} %get-tuple-element.12), channel_id=1, source_target_pairs={{1,0},{2,1},{3,2},{5,4},{6,5},{7,6},{9,8},{10,9},{11,10},{13,12},{... | collective-permute-start | bytes 98312 | tf_op jit(solution)/shard_map/ppermute | solution.py:17
  22.5 0.7 copy-start.12
  27.9 1.3 copy-start.10
  27.9 1.3 copy-start.11
  30.7 1.0 copy-start.4
  31.0 6.3 %copy-start.1 = (f32[12,8,17,256]{3,1,2,0:T(8,128)S(1)}, f32[12,8,17,256]{3,1,2,0:T(8,128)}, u32[]{:S(2)}) copy-start(f32[12,8,17,256]{3,1,2,0:T(8,128)} %get-tuple-element.26) | copy-start | bytes 5013508
  32.3 5.7 %collective-permute-start.4 = (bf16[2,128,256]{2,0,1:T(2,128)(2,1)S(1)}, bf16[2,128,256]{2,0,1:T(2,128)(2,1)S(1)}, u32[]{:S(2)}, u32[]{:S(2)}) collective-permute-start(bf16[2,128,256]{2,0,1:T(2,128)(2,1)S(1)} %get-tuple-element.19), channel_id=1, source_target_pairs={{0,4},{4,8},{8,12},{12,16},{16,20},{20,24},{24,28},{1,5},{5,9},{9,... | collective-permute-start | bytes 393224 | tf_op jit(solution)/shard_map/ppermute | solution.py:16
  35.4 6.3 %collective-permute-start.5 = (bf16[2,128,256]{2,0,1:T(2,128)(2,1)S(1)}, bf16[2,128,256]{2,0,1:T(2,128)(2,1)S(1)}, u32[]{:S(2)}, u32[]{:S(2)}) collective-permute-start(bf16[2,128,256]{2,0,1:T(2,128)(2,1)S(1)} %get-tuple-element.20), channel_id=1, source_target_pairs={{4,0},{8,4},{12,8},{16,12},{20,16},{24,20},{28,24},{5,1},{9,5},{13... | collective-permute-start | bytes 393224 | tf_op jit(solution)/shard_map/ppermute | solution.py:17
  41.7 4.9 %collective-permute-start.6 = (bf16[12,2,256]{2,0,1:T(8,128)(2,1)S(1)}, bf16[12,2,256]{2,0,1:T(8,128)(2,1)S(1)}, u32[]{:S(2)}, u32[]{:S(2)}) collective-permute-start(bf16[12,2,256]{2,0,1:T(8,128)(2,1)S(1)} %get-tuple-element.15), channel_id=1, source_target_pairs={{0,1},{1,2},{2,3},{4,5},{5,6},{6,7},{8,9},{9,10},{10,11},{12,13},{... | collective-permute-start | bytes 36872 | tf_op jit(solution)/shard_map/ppermute | solution.py:16
  45.0 4.5 %collective-permute-start.7 = (bf16[12,2,256]{2,0,1:T(8,128)(2,1)S(1)}, bf16[12,2,256]{2,0,1:T(8,128)(2,1)S(1)}, u32[]{:S(2)}, u32[]{:S(2)}) collective-permute-start(bf16[12,2,256]{2,0,1:T(8,128)(2,1)S(1)} %get-tuple-element.16), channel_id=1, source_target_pairs={{1,0},{2,1},{3,2},{5,4},{6,5},{7,6},{9,8},{10,9},{11,10},{13,12},{... | collective-permute-start | bytes 36872 | tf_op jit(solution)/shard_map/ppermute | solution.py:17
  52.5 5.8 %copy-start.2 = (bf16[2,512,512]{2,1,0:T(8,128)(2,1)S(1)}, bf16[2,512,512]{2,1,0:T(8,128)(2,1)}, u32[]{:S(2)}) copy-start(bf16[2,512,512]{2,1,0:T(8,128)(2,1)} %param.15) | copy-start | bytes 3145732
  52.6 5.8 %copy-start.3 = (bf16[512,192]{0,1:T(8,128)(2,1)S(1)}, bf16[512,192]{0,1:T(8,128)(2,1)}, u32[]{:S(2)}) copy-start(bf16[512,192]{0,1:T(8,128)(2,1)} %param.16) | copy-start | bytes 589828
  53.2 5.7 %collective-permute-start.8 = (bf16[2,128,256]{2,0,1:T(2,128)(2,1)S(1)}, bf16[2,128,256]{2,0,1:T(2,128)(2,1)S(1)}, u32[]{:S(2)}, u32[]{:S(2)}) collective-permute-start(bf16[2,128,256]{2,0,1:T(2,128)(2,1)S(1)} %get-tuple-element.17), channel_id=1, source_target_pairs={{0,4},{4,8},{8,12},{12,16},{16,20},{20,24},{24,28},{1,5},{5,9},{9,... | collective-permute-start | bytes 393224 | tf_op jit(solution)/shard_map/ppermute | solution.py:16
  56.4 6.7 %collective-permute-start.9 = (bf16[2,128,256]{2,0,1:T(2,128)(2,1)S(1)}, bf16[2,128,256]{2,0,1:T(2,128)(2,1)S(1)}, u32[]{:S(2)}, u32[]{:S(2)}) collective-permute-start(bf16[2,128,256]{2,0,1:T(2,128)(2,1)S(1)} %get-tuple-element.18), channel_id=1, source_target_pairs={{4,0},{8,4},{12,8},{16,12},{20,16},{24,20},{28,24},{5,1},{9,5},{13... | collective-permute-start | bytes 393224 | tf_op jit(solution)/shard_map/ppermute | solution.py:17
  63.1 7.6 %collective-permute-start.10 = (bf16[12,2,256]{2,0,1:T(8,128)(2,1)S(1)}, bf16[12,2,256]{2,0,1:T(8,128)(2,1)S(1)}, u32[]{:S(2)}, u32[]{:S(2)}) collective-permute-start(bf16[12,2,256]{2,0,1:T(8,128)(2,1)S(1)} %get-tuple-element.13), channel_id=1, source_target_pairs={{0,1},{1,2},{2,3},{4,5},{5,6},{6,7},{8,9},{9,10},{10,11},{12,13},{... | collective-permute-start | bytes 36872 | tf_op jit(solution)/shard_map/ppermute | solution.py:16
  66.3 4.5 %collective-permute-start.11 = (bf16[12,2,256]{2,0,1:T(8,128)(2,1)S(1)}, bf16[12,2,256]{2,0,1:T(8,128)(2,1)S(1)}, u32[]{:S(2)}, u32[]{:S(2)}) collective-permute-start(bf16[12,2,256]{2,0,1:T(8,128)(2,1)S(1)} %get-tuple-element.14), channel_id=1, source_target_pairs={{1,0},{2,1},{3,2},{5,4},{6,5},{7,6},{9,8},{10,9},{11,10},{13,12},{... | collective-permute-start | bytes 36872 | tf_op jit(solution)/shard_map/ppermute | solution.py:17
  74.6 16.7 %all-to-all-start = ((bf16[8,128,256]{2,1,0:T(8,128)(2,1)}), bf16[8,128,256]{2,1,0:T(8,128)(2,1)S(1)}, u32[]{:S(2)}, u32[]{:S(2)}) async-start(bf16[8,128,256]{2,1,0:T(8,128)(2,1)} %copy.132), calls=%async_computation | async-start | bytes 1048576 | tf_op jit(solution)/shard_map/all_to_all | solution.py:129
  78.1 2.2 %copy-start.5 = (f32[256,384]{0,1:S(1)}, f32[256,384]{0,1}, u32[]{:S(2)}) copy-start(f32[256,384]{0,1} %fusion.67) | copy-start | bytes 1179652
  80.3 16.0 %copy-start.8 = (bf16[192,256]{1,0:T(8,128)(2,1)S(1)}, bf16[192,256]{1,0:T(8,128)(2,1)}, u32[]{:S(2)}) copy-start(bf16[192,256]{1,0:T(8,128)(2,1)} %param.17) | copy-start | bytes 294916
  91.2 11.1 %all-to-all-start.3 = ((bf16[2,256,384]{2,0,1:T(2,128)(2,1)}), bf16[2,256,384]{2,0,1:T(2,128)(2,1)S(1)}, u32[]{:S(2)}, u32[]{:S(2)}) async-start(bf16[2,256,384]{2,0,1:T(2,128)(2,1)} %copy.142), calls=%async_computation.3 | async-start | bytes 786432 | tf_op jit(solution)/shard_map/all_to_all | solution.py:147
  102.3 11.7 %all-to-all-start.1 = ((bf16[2,256,384]{2,0,1:T(2,128)(2,1)}), bf16[2,256,384]{2,0,1:T(2,128)(2,1)S(1)}, u32[]{:S(2)}, u32[]{:S(2)}) async-start(bf16[2,256,384]{2,0,1:T(2,128)(2,1)} %copy.134), calls=%async_computation.1 | async-start | bytes 786432 | tf_op jit(solution)/shard_map/all_to_all | solution.py:148
  114.0 12.5 %all-to-all-start.4 = ((bf16[16,32,384]{2,0,1:T(8,128)(2,1)}), bf16[16,32,384]{2,0,1:T(8,128)(2,1)S(1)}, u32[]{:S(2)}, u32[]{:S(2)}) async-start(bf16[16,32,384]{2,0,1:T(8,128)(2,1)} %copy.145), calls=%async_computation.4 | async-start | bytes 786432 | tf_op jit(solution)/shard_map/all_to_all | solution.py:151
  126.6 12.0 %all-to-all-start.2 = ((bf16[16,32,384]{2,0,1:T(8,128)(2,1)}), bf16[16,32,384]{2,0,1:T(8,128)(2,1)}, u32[]{:S(2)}, u32[]{:S(2)}) async-start(bf16[16,32,384]{2,0,1:T(8,128)(2,1)} %copy.137), calls=%async_computation.2 | async-start | bytes 786432 | tf_op jit(solution)/shard_map/all_to_all | solution.py:152
  140.6 1.0 copy-start.6
  180.5 1.0 copy-start.7
where the time goes:
time: 185 us; the launch traced here: 183 us
  starting transfers between devices  52.2 us (28%)
  waiting for transfers between devices  49.5 us (27%)
  blocking collectives  31.1 us (17%)
  matrix products  28.7 us (16%)
  local copies, waits for them, and re-layouts  15.8 us (9%)
  other arithmetic  4.79 us (3%)
    ppermute x6, starting transfers between devices, padded_2(): before = lax.ppermute(last, axis, up)  20.5 us
    ppermute x6, waiting for transfers between devices, padded_2(): after = lax.ppermute(initial, axis, down)  18.5 us
    all_to_all x1, blocking collectives, shards(): lax.all_to_all(returned, 'row', split_axis=0, concat_axis=1, tiled=True)  17 us
    unnamed x6, matrix products  14.1 us
    all_to_all x1, blocking collectives, shards(): lax.all_to_all(grad_rows, 'col', split_axis=0, concat_axis=1, tiled=True)  14.1 us
    ppermute x6, starting transfers between devices, padded_2(): after = lax.ppermute(initial, axis, down)  9.82 us
    all_to_all x1, waiting for transfers between devices, shards(): lax.all_to_all(grad_feat, 'col', split_axis=0, concat_axis=1, tiled=True)  9.7 us
    all_to_all x1, waiting for transfers between devices, shards(): lax.all_to_all(spatial_moved, 'col', split_axis=1, concat_axis=0, tiled=T...  8.05 us
  transfers between devices with their start and end apart: 17, of which 12 were waited for; matrix products, arithmetic and copies ran while one was open for 9% of the time, Pallas kernels for 0%

commit v1 on v0

v1 whole, which is shorter than its diff:
```python
import functools
import math

import jax
import jax.numpy as jnp
import ml_dtypes
import numpy as np
from jax import lax
from jax.experimental import pallas as pl
from jax.experimental.pallas import tpu as pltpu
from jax.sharding import PartitionSpec as P

REACH = 8
LIMIT = 56 * 1024 * 1024


def dot(left, right):
    return jnp.dot(left, right, preferred_element_type=jnp.float32)


def dot_t(left, right):
    return lax.dot_general(left, right, (((1,), (1,)), ((), ())), preferred_element_type=jnp.float32)


def vmem_call(body, shapes, *operands, flops=0):
    spec = pl.BlockSpec(memory_space=pltpu.VMEM)
    size = sum(math.prod(a.shape) * a.dtype.itemsize for a in (*operands, *shapes))
    return pl.pallas_call(
        body,
        out_shape=shapes,
        in_specs=[spec] * len(operands),
        out_specs=[spec] * len(shapes),
        compiler_params=pltpu.CompilerParams(vmem_limit_bytes=LIMIT),
        cost_estimate=pl.CostEstimate(flops=flops, bytes_accessed=size, transcendentals=0),
    )(*operands)


def phases(first, second, length):
    angle = (first[:, None] * second[None, :] % length) * (2.0 * math.pi / length)
    return np.cos(angle).astype(ml_dtypes.bfloat16), np.sin(angle).astype(ml_dtypes.bfloat16)


def column_matrix(width, devices):
    half = width // 2
    freq, col = np.arange(half), np.arange(width)
    cos, sin = phases(freq, col, width)
    sin[0] = (2 * (col % 2) - 1).astype(ml_dtypes.bfloat16)
    both = np.stack([cos, -sin]).reshape(2, devices, half // devices, width)
    return np.ascontiguousarray(both.transpose(1, 0, 2, 3)).reshape(width, width)


def row_matrices(height, devices, owned):
    strip = height // devices
    result = []
    for row in range(strip):
        cos, sin = phases(np.arange(height), np.arange(devices) * strip + row, height)
        out = np.zeros((2, height, owned, devices, 2, owned), ml_dtypes.bfloat16)
        for freq in range(owned):
            out[0, :, freq, :, 0, freq] = cos
            out[0, :, freq, :, 1, freq] = sin
            out[1, :, freq, :, 0, freq] = -sin
            out[1, :, freq, :, 1, freq] = cos
        result.append(out.reshape(2 * height * owned, devices * 2 * owned))
    return result


def spectrum_kernel(transposed, norm, signal, weight, table, out):
    product = dot_t if transposed else dot
    rows = [product(signal[r], weight[...]).astype(jnp.bfloat16) for r in range(signal.shape[0])]
    out[...] = (dot(table[...], jnp.concatenate(rows, axis=1)) * norm).astype(jnp.bfloat16)


def row_spectrum(moved, tables, norm):
    half = moved.shape[1] // len(tables)
    total = 0.0
    for r, table in enumerate(tables):
        total = total + dot(table[...], moved[:, r * half : (r + 1) * half])
    cells = total.shape[0] // 2
    return total[:cells] * norm, total[cells:] * norm


def slope_kernel(norm, moved, mix, *rest):
    *tables, out = rest
    real, imag = row_spectrum(moved, tables, norm)
    half = real.shape[1]
    pre = dot(real.astype(jnp.bfloat16), mix[:half]) + dot(imag.astype(jnp.bfloat16), mix[half:])
    s = 1.0 / (1.0 + jnp.exp(-pre))
    out[...] = s * (1.0 + pre * (1.0 - s))


def mix_kernel(norm, strip, moved, slope, mix, *rest):
    *tables, out = rest
    real, imag = row_spectrum(moved, tables[:strip], norm)
    half = real.shape[1]
    grad = jnp.concatenate([real, imag], axis=1) * slope[...]
    back = dot_t(grad.astype(jnp.bfloat16), mix[...]).astype(jnp.bfloat16)
    stacked = jnp.concatenate([back[:, :half], back[:, half:]], axis=0)
    rows = [dot(table[...], stacked) for table in tables[strip:]]
    out[...] = (jnp.concatenate(rows, axis=1) * norm).astype(jnp.bfloat16)


def output_kernel(norm, moved, strip_grad, weight_in, weight_local, table, out):
    spatial = (dot(table[...], moved[...]) * norm).astype(jnp.bfloat16)
    half = weight_in.shape[1]
    for r in range(strip_grad.shape[0]):
        total = dot_t(spatial[:, r * half : (r + 1) * half], weight_in[...])
        total = total + dot_t(strip_grad[r], weight_local[...])
        out[r] = total.astype(jnp.bfloat16)


def conv_valid(padded, kernel):
    output = lax.conv_general_dilated(
        padded[None],
        kernel,
        (1, 1),
        "VALID",
        rhs_dilation=(2, 2),
        dimension_numbers=("NHWC", "HWIO", "NHWC"),
        preferred_element_type=jnp.float32,
    )
    return output[0]


def adjoint_kernel(kernel):
    return jnp.transpose(jnp.flip(kernel, (0, 1)), (0, 1, 3, 2))


def silu_slope(pre_value):
    sigmoid_value = jax.nn.sigmoid(pre_value)
    return sigmoid_value * (1.0 + pre_value * (1.0 - sigmoid_value))


def neighbours(axis):
    size = lax.axis_size(axis)
    up = [(i, i + 1) for i in range(size - 1)]
    return up, [(j, i) for i, j in up]


def shards(
    features,
    target,
    hole_mask,
    kernel_first,
    kernel_second,
    inputs,
    weight_in,
    weight_out,
    weight_local,
    weight_mix,
):
    tile_rows, tile_cols, channels = features.shape
    row_devices, col_devices = lax.axis_size("row"), lax.axis_size("col")
    devices = row_devices * col_devices
    height, width = tile_rows * row_devices, tile_cols * col_devices
    strip, half = inputs.shape[0], weight_in.shape[1]
    owned = width // 2 // devices
    col_norm, row_norm = 1.0 / math.sqrt(width), 1.0 / math.sqrt(height)
    table = column_matrix(width, devices)
    row_tables = row_matrices(height, devices, owned)
    table_back = jnp.asarray(np.ascontiguousarray(table.T))
    table = jnp.asarray(table)
    row_back = [jnp.asarray(np.ascontiguousarray(t.T)) for t in row_tables]
    row_tables = [jnp.asarray(t) for t in row_tables]
    axes = ("row", "col")
    bf16 = jnp.bfloat16

    def swap(spectrum):
        return lax.all_to_all(spectrum, axes, split_axis=0, concat_axis=0, tiled=True)

    up, down = neighbours("row")
    near = REACH // 2
    above = lax.ppermute(features, "row", up)
    below = lax.ppermute(features, "row", down)
    target_above = lax.ppermute(target[-near:], "row", up)
    target_below = lax.ppermute(target[:near], "row", down)
    all_mask = lax.all_gather(lax.all_gather(hole_mask, "col", axis=1, tiled=True), "row", tiled=True)

    cells = [jax.ShapeDtypeStruct((width, strip * half), bf16)]
    spatial_cols = vmem_call(
        functools.partial(spectrum_kernel, False, col_norm), cells, inputs, weight_in, table
    )[0]
    spatial_moved = swap(spatial_cols)

    tall = jnp.concatenate([above, features, below], axis=0)
    tall_target = jnp.concatenate([target_above, target, target_below], axis=0)
    left, right = neighbours("col")
    stacked = jnp.concatenate([tall, tall_target], axis=0)
    before = lax.ppermute(stacked[:, -REACH:], "col", left)
    after = lax.ppermute(stacked[:, :REACH], "col", right)
    rows_tall = tall.shape[0]
    wide = jnp.concatenate([before[:rows_tall], tall, after[:rows_tall]], axis=1)
    wide_target = jnp.concatenate(
        [before[rows_tall:, near:], tall_target, after[rows_tall:, :near]], axis=1
    )
    row0, col0 = lax.axis_index("row") * tile_rows, lax.axis_index("col") * tile_cols
    weights = jnp.pad(1.0 + 2.0 * all_mask.astype(jnp.float32), near)
    hole_weight = lax.dynamic_slice(
        weights, (row0, col0), (tile_rows + 2 * near, tile_cols + 2 * near)
    )

    def inside(margin):
        row_ids = row0 - margin + jnp.arange(tile_rows + 2 * margin, dtype=jnp.int32)
        col_ids = col0 - margin + jnp.arange(tile_cols + 2 * margin, dtype=jnp.int32)
        ok_row = (row_ids >= 0) & (row_ids < height)
        ok_col = (col_ids >= 0) & (col_ids < width)
        return (ok_row[:, None] & ok_col[None, :])[:, :, None]

    pre_first = conv_valid(wide, kernel_first)
    act = jnp.where(inside(6), jax.nn.silu(pre_first), 0.0).astype(bf16)
    pre_second = conv_valid(act, kernel_second)
    loss_grad = (hole_weight[:, :, None] * (pre_second - wide_target.astype(jnp.float32))).astype(bf16)
    grad_act = conv_valid(loss_grad, adjoint_kernel(kernel_second))
    slope_first = silu_slope(pre_first[4:-4, 4:-4])
    grad_pre = jnp.where(inside(2), grad_act * slope_first, 0.0).astype(bf16)
    grad_feat = conv_valid(grad_pre, adjoint_kernel(kernel_first)).astype(bf16)

    cell_count = height * owned
    slope = vmem_call(
        functools.partial(slope_kernel, row_norm),
        [jax.ShapeDtypeStruct((cell_count, 2 * half), jnp.float32)],
        spatial_moved,
        weight_mix,
        *row_tables,
    )[0]

    strip_grad = lax.all_to_all(grad_feat, "col", split_axis=0, concat_axis=1, tiled=True)
    grad_cols = vmem_call(
        functools.partial(spectrum_kernel, True, col_norm), cells, strip_grad, weight_out, table
    )[0]
    grad_moved = swap(grad_cols)
    grad_rows = vmem_call(
        functools.partial(mix_kernel, row_norm, strip),
        cells,
        grad_moved,
        slope,
        weight_mix,
        *row_tables,
        *row_back,
    )[0]
    returned = swap(grad_rows)
    return vmem_call(
        functools.partial(output_kernel, col_norm),
        [jax.ShapeDtypeStruct(inputs.shape, bf16)],
        returned,
        strip_grad,
        weight_in,
        weight_local,
        table_back,
    )[0]


def solution(mesh):
    in_specs = (
        P("row", "col", None),
        P("row", "col", None),
        P("row", "col"),
        P(),
        P(),
        P(("row", "col"), None, None),
        P(),
        P(),
        P(),
        P(),
    )
    out_specs = P(("row", "col"), None, None)
    return jax.shard_map(shards, mesh=mesh, in_specs=in_specs, out_specs=out_specs, check_vma=False)
```

time: 185 us -> 204 us (1.10)
  matrix products: 28.7 us -> 63 us
  starting transfers between devices: 52.2 us -> 27.1 us
  Pallas kernels: 0 us -> 19.7 us
  waiting for transfers between devices: 49.5 us -> 30.5 us
  blocking collectives: 31.1 us -> 40.8 us
  local copies, waits for them, and re-layouts: 15.8 us -> 8.88 us
  other arithmetic: 4.79 us -> 9.53 us
    conv_general_dilated x4, matrix products: 7.98 us -> 63 us  [conv_valid(): lax.conv_general_dilated(padded[None], kernel, (1, 1), 'VALID', rhs_dilat...]
    all_gather x0 -> x2, blocking collectives: none -> 25 us  [the longest x1 14.4 us: shards(): lax.all_gather(lax.all_gather(hole_mask, 'col', axis=1, tiled=True), 'row...]
    pallas_call x0 -> x5, Pallas kernels: none -> 19.7 us  [vmem_call(): pl.pallas_call(body, out_shape=shapes, in_specs=[spec] * len(operands), o...]
    ppermute x12 -> x6, waiting for transfers between devices: 19.8 us -> 2.78 us  [the longest x1 2.76 us: shards(): after = lax.ppermute(stacked[:, :REACH], 'col', right)]
    all_to_all x2 -> x1, blocking collectives: 31.1 us -> 15.8 us  [swap(): lax.all_to_all(spectrum, axes, split_axis=0, concat_axis=0, tiled=True)]
    unnamed x6 -> x0, matrix products: 14.1 us -> none
    ppermute x12 -> x6, starting transfers between devices: 30.3 us -> 16.7 us  [the longest x1 4.63 us: shards(): above = lax.ppermute(features, 'row', up)]
    all_to_all x4 -> x2, starting transfers between devices: 18.4 us -> 6.86 us  [swap(): lax.all_to_all(spectrum, axes, split_axis=0, concat_axis=0, tiled=True)]
  transfers between devices with their start and end apart: 17 -> 9, of which waited for: 12 -> 4; matrix products, arithmetic and copies ran while one was open for 9% -> 4% of each run, Pallas kernels for 0% -> 5%
where the time goes in v1:
time: 204 us; the launch traced here: 200 us
  matrix products  63 us (31%)
  blocking collectives  40.8 us (20%)
  waiting for transfers between devices  30.5 us (15%)
  starting transfers between devices  27.1 us (13%)
  Pallas kernels  19.7 us (10%)
  other arithmetic  9.53 us (5%)
  local copies, waits for them, and re-layouts  8.88 us (4%)
    conv_general_dilated x4, matrix products, conv_valid(): lax.conv_general_dilated(padded[None], kernel, (1, 1), 'VALID', rhs_dilat...  63 us
    pallas_call x5, Pallas kernels, vmem_call(): pl.pallas_call(body, out_shape=shapes, in_specs=[spec] * len(operands), o...  19.7 us
    all_to_all x2, waiting for transfers between devices, swap(): lax.all_to_all(spectrum, axes, split_axis=0, concat_axis=0, tiled=True)  17.7 us
    all_to_all x1, blocking collectives, swap(): lax.all_to_all(spectrum, axes, split_axis=0, concat_axis=0, tiled=True)  15.8 us
    all_gather x1, blocking collectives, shards(): lax.all_gather(lax.all_gather(hole_mask, 'col', axis=1, tiled=True), 'row...  14.4 us
    all_gather x1, blocking collectives, shards(): lax.all_gather(hole_mask, 'col', axis=1, tiled=True)  10.6 us
    all_to_all x1, waiting for transfers between devices, shards(): lax.all_to_all(grad_feat, 'col', split_axis=0, concat_axis=1, tiled=True)  10 us
    conv_general_dilated x1, other arithmetic, conv_valid(): lax.conv_general_dilated(padded[None], kernel, (1, 1), 'VALID', rhs_dilat...  7.09 us
  transfers between devices with their start and end apart: 9, of which 4 were waited for; matrix products, arithmetic and copies ran while one was open for 4% of the time, Pallas kernels for 5%

profile of v1, /device:TPU:1, one launch (start us, length us, event | category | flops | bytes accessed | tf_op | source)
XLA Modules:
  0.0 200.0 jit_solution(6619085470332578656)
XLA Ops:
  0.0 4.6 %collective-permute-start = (bf16[8,128,256]{2,1,0:T(8,128)(2,1)}, bf16[8,128,256]{2,1,0:T(8,128)(2,1)S(1)}, u32[]{:S(2)}, u32[]{:S(2)}) collective-permute-start(bf16[8,128,256]{2,1,0:T(8,128)(2,1)} %param.16), channel_id=1, source_target_pairs={{0,4},{4,8},{8,12},{12,16},{16,20},{20,24},{24,28},{1,5},{5,9},{9,... | collective-permute-start | bytes 1572872 | tf_op jit(solution)/shard_map/ppermute | solution.py:172
  4.6 1.9 collective-permute-start.1
  6.6 1.9 fusion.27
  8.4 3.8 %collective-permute-start.2 = (bf16[4,128,256]{2,1,0:T(8,128)(2,1)}, bf16[4,128,256]{2,1,0:T(8,128)(2,1)S(1)}, u32[]{:S(2)}, u32[]{:S(2)}) collective-permute-start(bf16[4,128,256]{2,1,0:T(8,128)(2,1)} %get-tuple-element.8), channel_id=1, source_target_pairs={{0,4},{4,8},{8,12},{12,16},{16,20},{20,24},{24,28},{1,5},{5,9},{9,... | collective-permute-start | bytes 786440 | tf_op jit(solution)/shard_map/ppermute | solution.py:174
  12.2 1.9 collective-permute-start.3
  14.3 10.6 %all_gather.6 = s32[8,512]{1,0:T(8,128)S(1)} all-gather(s32[8,128]{1,0:T(8,128)} %param.18), channel_id=1, replica_groups=mesh['row'=8,'col'=4] {'col'}, dimensions={1}, use_global_device_ids=true | all-gather | bytes 20480 | tf_op jit(solution)/shard_map/all_gather | solution.py:176
  24.9 14.4 %all_gather.7 = s32[64,512]{1,0:T(8,128)S(1)} all-gather(s32[8,512]{1,0:T(8,128)S(1)} %all_gather.6), channel_id=1, replica_groups=mesh['row'=8,'col'=4] {'row'}, dimensions={0}, use_global_device_ids=true | all-gather | bytes 147456 | tf_op jit(solution)/shard_map/all_gather | solution.py:176
  39.6 1.0 constant_dynamic-update-slice_fusion
  40.6 3.2 %collective-permute-start.4 = (bf16[40,8,256]{2,1,0:T(8,128)(2,1)S(1)}, bf16[40,8,256]{2,1,0:T(8,128)(2,1)S(1)}, u32[]{:S(2)}, u32[]{:S(2)}) collective-permute-start(bf16[40,8,256]{2,1,0:T(8,128)(2,1)S(1)} %get-tuple-element.5), channel_id=1, source_target_pairs={{0,1},{1,2},{2,3},{4,5},{5,6},{6,7},{8,9},{9,10},{10,11},{12,13},{... | collective-permute-start | bytes 491528 | tf_op jit(solution)/shard_map/ppermute | solution.py:188
  43.8 1.3 collective-permute-start.5
  45.2 1.1 maximum_bitcast_fusion.1
  46.3 1.9 copy.42
  48.3 2.8 %collective-permute-done.5 = bf16[40,8,256]{2,1,0:T(8,128)(2,1)S(1)} collective-permute-done((bf16[40,8,256]{2,1,0:T(8,128)(2,1)S(1)}, bf16[40,8,256]{2,1,0:T(8,128)(2,1)S(1)}, u32[]{:S(2)}, u32[]{:S(2)}) %collective-permute-start.5) | collective-permute-done | bytes 163872 | tf_op jit(solution)/shard_map/ppermute | solution.py:189
  51.2 21.5 %fusion = f32[1,20,140,256]{3,0,2,1:T(1,128)S(1)} fusion(bf16[3,3,256,256]{3,2,1,0:T(8,128)(2,1)S(1)} %copy-done, bf16[1,24,144,256]{3,2,1,0:T(8,128)(2,1)S(1)} %maximum_bitcast_fusion), kind=kOutput, calls=%fused_computation.1 | convolution fusion | flops 3303014400 | bytes 5816320 | tf_op jit(solution)/shard_map/conv_general_dilated | solution.py:112
  73.0 7.1 %fusion.37 = bf16[1,20,140,256]{3,0,2,1:T(2,128)(2,1)S(1)} fusion(pred[20,140]{1,0:T(8,128)(4,1)S(1)} %broadcast_and_fusion, f32[1,20,140,256]{3,0,2,1:T(1,128)S(1)} %fusion), kind=kLoop, calls=%fused_computation.5.clone.clone.clone.clone.clone.clone.clone.clone.1 | loop fusion | flops 4300800 | bytes 4303600 | tf_op jit(solution)/shard_map/conv_general_dilated | solution.py:112
  80.3 23.4 %fusion.11 = bf16[1,16,136,256]{3,0,2,1:T(2,128)(2,1)S(1)} fusion(bf16[3,3,256,256]{3,2,1,0:T(8,128)(2,1)S(1)} %copy-done.6, bf16[1,16,4,256]{3,0,2,1:T(2,128)(2,1)S(1)} %copy.43, bf16[1,16,128,256]{3,0,2,1:T(2,128)(2,1)S(1)} %copy.42, bf16[1,16,4,256]{3,0,2,1:T(2,128)(2,1)S(1)} %copy.41, f32[16,136]{1,0:T(8,128)S(1)} %pad_dynamic-slice_fusion, ...), kind=kOutput, calls=%fused_computation.9 | convolution fusion | flops 2570256384 | bytes 4850176 | tf_op jit(solution)/shard_map/conv_general_dilated | solution.py:112
  103.7 11.2 %fusion.28 = f32[1,12,132,256]{3,0,2,1:T(1,128)S(1)} fusion(bf16[1,16,136,256]{3,0,2,1:T(2,128)(2,1)S(1)} %fusion.11, bf16[3,3,256,256]{3,2,1,0:T(8,128)(2,1)S(1)} %copy-done.6), kind=kOutput, calls=%fused_computation.43 | convolution fusion | flops 1868562432 | bytes 3915776 | tf_op jit(solution)/shard_map/conv_general_dilated | solution.py:112
  114.9 1.0 fusion.23
  115.9 6.9 %fusion.20 = bf16[1,8,128,256]{3,0,2,1:T(2,128)(2,1)S(1)} fusion(bf16[3,3,256,256]{3,2,1,0:T(8,128)(2,1)S(1)} %copy-done, bf16[1,12,132,256]{3,2,1,0:T(8,128)(2,1)S(1)} %fusion.23), kind=kOutput, calls=%fused_computation.19 | convolution fusion | flops 1208221696 | bytes 2514944 | tf_op jit(solution)/shard_map/conv_general_dilated | solution.py:112
  122.9 0.9 copy.67
  123.8 3.5 %all-to-all-start = ((bf16[8,128,256]{2,1,0:T(8,128)(2,1)}), bf16[8,128,256]{2,1,0:T(8,128)(2,1)S(1)}, u32[]{:S(2)}, u32[]{:S(2)}) async-start(bf16[8,128,256]{2,1,0:T(8,128)(2,1)} %bitcast.40), calls=%async_computation | async-start | bytes 1048576 | tf_op jit(solution)/shard_map/all_to_all | solution.py:226
  128.1 3.1 %shard_map.155 = bf16[512,384]{1,0:T(8,128)(2,1)} custom-call(bf16[2,512,512]{2,1,0:T(8,128)(2,1)} %signal.1, bf16[512,192]{1,0:T(8,128)(2,1)} %copy.46.weight.weight_in, bf16[512,512]{1,0:T(8,128)(2,1)} %constant.60.clone.table), custom_call_target="tpu_custom_call" | custom-call | bytes 2162688 | tf_op jit(solution)/shard_map/pallas_call | solution.py:28
  131.2 10.0 %all-to-all-done = bf16[8,128,256]{2,1,0:T(8,128)(2,1)S(1)} async-done(((bf16[8,128,256]{2,1,0:T(8,128)(2,1)}), bf16[8,128,256]{2,1,0:T(8,128)(2,1)S(1)}, u32[]{:S(2)}, u32[]{:S(2)}) %all-to-all-start) | async-done | bytes 524320 | tf_op jit(solution)/shard_map/all_to_all | solution.py:226
  141.2 3.9 %all-to-all-start.2 = ((bf16[32,16,384]{2,1,0:T(8,128)(2,1)}), bf16[32,16,384]{2,1,0:T(8,128)(2,1)S(1)}, u32[]{:S(2)}, u32[]{:S(2)}) async-start(bf16[32,16,384]{2,1,0:T(8,128)(2,1)} %bitcast.49), calls=%async_computation.2 | async-start | bytes 786432 | tf_op jit(solution)/shard_map/all_to_all | solution.py:168
  146.0 2.7 %shard_map.154 = bf16[512,384]{1,0:T(8,128)(2,1)} custom-call(bf16[2,512,256]{2,1,0:T(8,128)(2,1)} %bitcast.42, bf16[192,256]{1,0:T(8,128)(2,1)} %weight.2, bf16[512,512]{1,0:T(8,128)(2,1)} %constant.60.clone.table), custom_call_target="tpu_custom_call" | custom-call | bytes 1540096 | tf_op jit(solution)/shard_map/pallas_call | solution.py:28
  148.7 9.2 %all-to-all-done.2 = bf16[32,16,384]{2,1,0:T(8,128)(2,1)S(1)} async-done(((bf16[32,16,384]{2,1,0:T(8,128)(2,1)}), bf16[32,16,384]{2,1,0:T(8,128)(2,1)S(1)}, u32[]{:S(2)}, u32[]{:S(2)}) %all-to-all-start.2) | async-done | bytes 393248 | tf_op jit(solution)/shard_map/all_to_all | solution.py:168
  157.9 2.9 %all-to-all-start.1 = ((bf16[32,16,384]{2,1,0:T(8,128)(2,1)}), bf16[32,16,384]{2,1,0:T(8,128)(2,1)S(1)}, u32[]{:S(2)}, u32[]{:S(2)}) async-start(bf16[32,16,384]{2,1,0:T(8,128)(2,1)} %bitcast.48), calls=%async_computation.1 | async-start | bytes 786432 | tf_op jit(solution)/shard_map/all_to_all | solution.py:168
  160.9 4.2 %shard_map.156.slope = f32[512,384]{1,0:T(8,128)} custom-call(bf16[512,384]{1,0:T(8,128)(2,1)} %bitcast.45, bf16[384,384]{1,0:T(8,128)(2,1)} %mix.3, bf16[1024,512]{1,0:T(8,128)(2,1)} %constant.63.clone.rest_0_, bf16[1024,512]{1,0:T(8,128)(2,1)} %constant.64.clone.rest_1_), custom_call_target="tpu_custom_call" | custom-call | bytes 3571712 | tf_op jit(solution)/shard_map/pallas_call | solution.py:28
  165.1 8.5 %all-to-all-done.1 = bf16[32,16,384]{2,1,0:T(8,128)(2,1)S(1)} async-done(((bf16[32,16,384]{2,1,0:T(8,128)(2,1)}), bf16[32,16,384]{2,1,0:T(8,128)(2,1)S(1)}, u32[]{:S(2)}, u32[]{:S(2)}) %all-to-all-start.1) | async-done | bytes 393248 | tf_op jit(solution)/shard_map/all_to_all | solution.py:168
  174.3 6.2 %shard_map.157 = bf16[512,384]{1,0:T(8,128)(2,1)} custom-call(bf16[512,384]{1,0:T(8,128)(2,1)} %bitcast.46, f32[512,384]{1,0:T(8,128)} %shard_map.156.slope, bf16[384,384]{1,0:T(8,128)(2,1)} %mix.3, bf16[1024,512]{1,0:T(8,128)(2,1)} %constant.63.clone.rest_0_, bf16[1024,512]{1,0:T(8,128)(2,1)} %constant.64.clone.rest_1_, ...), custom_call_target="tpu_custom_call" | custom-call | bytes 6062080 | tf_op jit(solution)/shard_map/pallas_call | solution.py:28
  180.6 15.8 %all_to_all.51 = bf16[32,16,384]{2,1,0:T(8,128)(2,1)} all-to-all(bf16[32,16,384]{2,1,0:T(8,128)(2,1)} %bitcast.47), channel_id=1, replica_groups=mesh['row'=8,'col'=4] {'row','col'}, dimensions={0} | all-to-all | bytes 786432 | tf_op jit(solution)/shard_map/all_to_all | solution.py:168
  196.4 3.4 %shard_map.158 = bf16[2,512,512]{2,1,0:T(8,128)(2,1)} custom-call(bf16[512,384]{1,0:T(8,128)(2,1)} %bitcast.50, bf16[2,512,256]{2,1,0:T(8,128)(2,1)} %bitcast.43, bf16[512,192]{1,0:T(8,128)(2,1)} %copy.46.weight.weight_in, bf16[512,256]{1,0:T(8,128)(2,1)} %weight_local.1, bf16[512,512]{1,0:T(8,128)(2,1)} %constant.59.clone.table), custom_call_target="tpu_custom_call" | custom-call | bytes 2949120 | tf_op jit(solution)/shard_map/pallas_call | solution.py:28
  (43 shorter events, 3.6 us)
Async XLA Ops:
  0.0 51.2 %copy-start = (bf16[3,3,256,256]{3,2,1,0:T(8,128)(2,1)S(1)}, bf16[3,3,256,256]{3,2,1,0:T(8,128)(2,1)}, u32[]{:S(2)}) copy-start(bf16[3,3,256,256]{3,2,1,0:T(8,128)(2,1)} %param.19) | copy-start | bytes 3538948
  0.0 39.4 %copy-start.2 = (bf16[8,128,256]{2,1,0:T(8,128)(2,1)S(1)}, bf16[8,128,256]{2,1,0:T(8,128)(2,1)}, u32[]{:S(2)}) copy-start(bf16[8,128,256]{2,1,0:T(8,128)(2,1)} %param.16) | copy-start | bytes 1572868
  0.0 39.3 %collective-permute-start = (bf16[8,128,256]{2,1,0:T(8,128)(2,1)}, bf16[8,128,256]{2,1,0:T(8,128)(2,1)S(1)}, u32[]{:S(2)}, u32[]{:S(2)}) collective-permute-start(bf16[8,128,256]{2,1,0:T(8,128)(2,1)} %param.16), channel_id=1, source_target_pairs={{0,4},{4,8},{8,12},{12,16},{16,20},{20,24},{24,28},{1,5},{5,9},{9,... | collective-permute-start | bytes 1572872 | tf_op jit(solution)/shard_map/ppermute | solution.py:172
  4.6 34.8 %collective-permute-start.1 = (bf16[8,128,256]{2,1,0:T(8,128)(2,1)}, bf16[8,128,256]{2,1,0:T(8,128)(2,1)S(1)}, u32[]{:S(2)}, u32[]{:S(2)}) collective-permute-start(bf16[8,128,256]{2,1,0:T(8,128)(2,1)} %param.16), channel_id=1, source_target_pairs={{4,0},{8,4},{12,8},{16,12},{20,16},{24,20},{28,24},{5,1},{9,5},{13... | collective-permute-start | bytes 1572872 | tf_op jit(solution)/shard_map/ppermute | solution.py:173
  8.4 31.1 %copy-start.1 = (bf16[8,128,256]{2,1,0:T(8,128)(2,1)S(1)}, bf16[8,128,256]{2,1,0:T(8,128)(2,1)}, u32[]{:S(2)}) copy-start(bf16[8,128,256]{2,1,0:T(8,128)(2,1)} %param.17) | copy-start | bytes 1572868
  8.4 31.1 %collective-permute-start.2 = (bf16[4,128,256]{2,1,0:T(8,128)(2,1)}, bf16[4,128,256]{2,1,0:T(8,128)(2,1)S(1)}, u32[]{:S(2)}, u32[]{:S(2)}) collective-permute-start(bf16[4,128,256]{2,1,0:T(8,128)(2,1)} %get-tuple-element.8), channel_id=1, source_target_pairs={{0,4},{4,8},{8,12},{12,16},{16,20},{20,24},{24,28},{1,5},{5,9},{9,... | collective-permute-start | bytes 786440 | tf_op jit(solution)/shard_map/ppermute | solution.py:174
  12.2 27.4 %collective-permute-start.3 = (bf16[4,128,256]{2,1,0:T(8,128)(2,1)}, bf16[4,128,256]{2,1,0:T(8,128)(2,1)}, u32[]{:S(2)}, u32[]{:S(2)}) collective-permute-start(bf16[4,128,256]{2,1,0:T(8,128)(2,1)} %get-tuple-element.7), channel_id=1, source_target_pairs={{4,0},{8,4},{12,8},{16,12},{20,16},{24,20},{28,24},{5,1},{9,5},{13... | collective-permute-start | bytes 786440 | tf_op jit(solution)/shard_map/ppermute | solution.py:175
  40.6 7.7 %collective-permute-start.4 = (bf16[40,8,256]{2,1,0:T(8,128)(2,1)S(1)}, bf16[40,8,256]{2,1,0:T(8,128)(2,1)S(1)}, u32[]{:S(2)}, u32[]{:S(2)}) collective-permute-start(bf16[40,8,256]{2,1,0:T(8,128)(2,1)S(1)} %get-tuple-element.5), channel_id=1, source_target_pairs={{0,1},{1,2},{2,3},{4,5},{5,6},{6,7},{8,9},{9,10},{10,11},{12,13},{... | collective-permute-start | bytes 491528 | tf_op jit(solution)/shard_map/ppermute | solution.py:188
  43.8 7.2 %collective-permute-start.5 = (bf16[40,8,256]{2,1,0:T(8,128)(2,1)S(1)}, bf16[40,8,256]{2,1,0:T(8,128)(2,1)S(1)}, u32[]{:S(2)}, u32[]{:S(2)}) collective-permute-start(bf16[40,8,256]{2,1,0:T(8,128)(2,1)S(1)} %get-tuple-element.6), channel_id=1, source_target_pairs={{1,0},{2,1},{3,2},{5,4},{6,5},{7,6},{9,8},{10,9},{11,10},{13,12},{... | collective-permute-start | bytes 491528 | tf_op jit(solution)/shard_map/ppermute | solution.py:189
  73.0 7.3 %copy-start.6 = (bf16[3,3,256,256]{3,2,1,0:T(8,128)(2,1)S(1)}, bf16[3,3,256,256]{3,2,1,0:T(8,128)(2,1)}, u32[]{:S(2)}) copy-start(bf16[3,3,256,256]{3,2,1,0:T(8,128)(2,1)} %param.20) | copy-start | bytes 3538948
  122.9 4.4 %copy-start.5 = (bf16[512,192]{0,1:T(8,128)(2,1)S(1)}, bf16[512,192]{0,1:T(8,128)(2,1)}, u32[]{:S(2)}) copy-start(bf16[512,192]{0,1:T(8,128)(2,1)} %param.22) | copy-start | bytes 589828
  123.8 17.4 %all-to-all-start = ((bf16[8,128,256]{2,1,0:T(8,128)(2,1)}), bf16[8,128,256]{2,1,0:T(8,128)(2,1)S(1)}, u32[]{:S(2)}, u32[]{:S(2)}) async-start(bf16[8,128,256]{2,1,0:T(8,128)(2,1)} %bitcast.40), calls=%async_computation | async-start | bytes 1048576 | tf_op jit(solution)/shard_map/all_to_all | solution.py:226
  141.2 16.7 %all-to-all-start.2 = ((bf16[32,16,384]{2,1,0:T(8,128)(2,1)}), bf16[32,16,384]{2,1,0:T(8,128)(2,1)S(1)}, u32[]{:S(2)}, u32[]{:S(2)}) async-start(bf16[32,16,384]{2,1,0:T(8,128)(2,1)} %bitcast.49), calls=%async_computation.2 | async-start | bytes 786432 | tf_op jit(solution)/shard_map/all_to_all | solution.py:168
  157.9 3.0 %copy-start.3 = (bf16[32,16,384]{2,1,0:T(8,128)(2,1)}, bf16[32,16,384]{2,1,0:T(8,128)(2,1)S(1)}, u32[]{:S(2)}) copy-start(bf16[32,16,384]{2,1,0:T(8,128)(2,1)S(1)} %all-to-all-done.2) | copy-start | bytes 1179652
  157.9 15.7 %all-to-all-start.1 = ((bf16[32,16,384]{2,1,0:T(8,128)(2,1)}), bf16[32,16,384]{2,1,0:T(8,128)(2,1)S(1)}, u32[]{:S(2)}, u32[]{:S(2)}) async-start(bf16[32,16,384]{2,1,0:T(8,128)(2,1)} %bitcast.48), calls=%async_computation.1 | async-start | bytes 786432 | tf_op jit(solution)/shard_map/all_to_all | solution.py:168
  173.6 0.8 copy-start.4

commit v2 on v1

v2 whole, which is shorter than its diff:
```python
import functools
import math

import jax
import jax.numpy as jnp
import ml_dtypes
import numpy as np
from jax import lax
from jax.experimental import pallas as pl
from jax.experimental.pallas import tpu as pltpu
from jax.sharding import PartitionSpec as P

REACH = 8
NEAR = 4
MIB = 1024 * 1024
LANES = 128


def dot(left, right):
    return jnp.dot(left, right, preferred_element_type=jnp.float32)


def dot_t(left, right):
    return lax.dot_general(left, right, (((1,), (1,)), ((), ())), preferred_element_type=jnp.float32)


def vmem_call(body, shapes, *operands, flops=0, scratch=(), limit=16):
    spec = pl.BlockSpec(memory_space=pltpu.VMEM)
    size = sum(math.prod(a.shape) * a.dtype.itemsize for a in (*operands, *shapes))
    return pl.pallas_call(
        body,
        out_shape=shapes,
        in_specs=[spec] * len(operands),
        out_specs=[spec] * len(shapes),
        scratch_shapes=list(scratch),
        compiler_params=pltpu.CompilerParams(vmem_limit_bytes=limit * MIB),
        cost_estimate=pl.CostEstimate(flops=flops, bytes_accessed=size, transcendentals=0),
    )(*operands)


def phases(first, second, length):
    angle = (first[:, None] * second[None, :] % length) * (2.0 * math.pi / length)
    return np.cos(angle).astype(ml_dtypes.bfloat16), np.sin(angle).astype(ml_dtypes.bfloat16)


def column_matrix(width, devices):
    half = width // 2
    freq, col = np.arange(half), np.arange(width)
    cos, sin = phases(freq, col, width)
    sin[0] = (2 * (col % 2) - 1).astype(ml_dtypes.bfloat16)
    both = np.stack([cos, -sin]).reshape(2, devices, half // devices, width)
    return np.ascontiguousarray(both.transpose(1, 0, 2, 3)).reshape(width, width)


def row_matrix(height, devices):
    strip = height // devices
    rows = (np.arange(devices)[None, :] * strip + np.arange(strip)[:, None]).reshape(-1)
    cos, sin = phases(np.arange(height), rows, height)
    return np.block([[cos, sin], [-sin, cos]])


def spectrum_kernel(transposed, norm, signal, weight, table, out):
    product = dot_t if transposed else dot
    rows = [product(signal[r], weight[...]).astype(jnp.bfloat16) for r in range(signal.shape[0])]
    out[...] = (dot(table[...], jnp.concatenate(rows, axis=1)) * norm).astype(jnp.bfloat16)


def row_spectrum(moved, table, wide, norm, owned, devices):
    groups = moved.shape[1] // LANES
    for g in range(groups):
        wide[g] = moved[:, g * LANES : (g + 1) * LANES].astype(jnp.float32)
    strip = table.shape[1] // (2 * devices)
    half = moved.shape[1] // strip
    height = table.shape[0] // 2
    real, imag = [], []
    for freq in range(owned):
        parts = []
        for part in range(2):
            where = pl.ds(part * owned + freq, devices, stride=2 * owned)
            block = jnp.concatenate([wide[g, where, :] for g in range(groups)], axis=1)
            parts += [block[:, r * half : (r + 1) * half] for r in range(strip)]
        result = dot(table[...], jnp.concatenate(parts, axis=0).astype(jnp.bfloat16)) * norm
        real.append(result[:height])
        imag.append(result[height:])
    return jnp.concatenate(real, axis=0), jnp.concatenate(imag, axis=0)


def slope_kernel(norm, owned, devices, moved, mix, table, out, wide):
    parts = row_spectrum(moved, table, wide, norm, owned, devices)
    real, imag = [part.astype(jnp.bfloat16) for part in parts]
    for part in range(2):
        pre = dot(real, mix[0, part]) + dot(imag, mix[1, part])
        s = 1.0 / (1.0 + jnp.exp(-pre))
        out[part] = s * (1.0 + pre * (1.0 - s))


def mix_kernel(norm, owned, devices, moved, slope, mix, table, back_table, out, wide):
    real, imag = row_spectrum(moved, table, wide, norm, owned, devices)
    real = (real * slope[0]).astype(jnp.bfloat16)
    imag = (imag * slope[1]).astype(jnp.bfloat16)
    back = [(dot_t(real, mix[p, 0]) + dot_t(imag, mix[p, 1])).astype(jnp.bfloat16) for p in range(2)]
    height = table.shape[0] // 2
    strip = height // devices
    groups = out.shape[1] // LANES
    for freq in range(owned):
        cells = slice(freq * height, (freq + 1) * height)
        stacked = jnp.concatenate([back[0][cells], back[1][cells]], axis=0)
        result = dot(back_table[...], stacked) * norm
        for part in range(2):
            rows = [
                result[(part * strip + r) * devices : (part * strip + r + 1) * devices]
                for r in range(strip)
            ]
            where = pl.ds(part * owned + freq, devices, stride=2 * owned)
            values = jnp.concatenate(rows, axis=1)
            for g in range(groups):
                wide[g, where, :] = values[:, g * LANES : (g + 1) * LANES]
    for g in range(groups):
        out[:, g * LANES : (g + 1) * LANES] = wide[g].astype(jnp.bfloat16)


def output_kernel(norm, moved, strip_grad, weight_in, weight_local, table, out):
    spatial = (dot(table[...], moved[...]) * norm).astype(jnp.bfloat16)
    half = weight_in.shape[1]
    for r in range(strip_grad.shape[0]):
        total = dot_t(spatial[:, r * half : (r + 1) * half], weight_in[...])
        total = total + dot_t(strip_grad[r], weight_local[...])
        out[r] = total.astype(jnp.bfloat16)


def conv_kernel(
    above,
    features,
    below,
    target_above,
    target,
    target_below,
    before,
    after,
    guard,
    first,
    second,
    second_adjoint,
    first_adjoint,
    out,
    wide0,
    wide1,
    wide2,
    wide3,
    slopes,
):
    tile_rows, tile_cols, channels = features.shape
    stride = tile_cols + 2 * REACH
    block = NEAR
    size = block * stride
    tall = tile_rows + 2 * REACH

    def rows_of(left, middle, right):
        parts = [part.astype(jnp.float32) for part in (left, middle, right)]
        return jnp.concatenate(parts, axis=1).reshape(size, channels)

    def put(wide, row, value):
        spot = pl.ds(row * stride, size)
        wide[spot, :channels] = pltpu.roll(value, 2, 0).astype(jnp.bfloat16)
        wide[spot, channels : 2 * channels] = value.astype(jnp.bfloat16)
        wide[spot, 2 * channels :] = pltpu.roll(value, size - 2, 0).astype(jnp.bfloat16)

    def conv(wide, row, kernel):
        taps = [wide[pl.ds((row + 2 * a) * stride, size), :] for a in range(3)]
        return dot(jnp.concatenate(taps, axis=1), kernel[...])

    def lanes(start):
        columns = [guard[:, start + i : start + i + 1] for i in range(block)]
        return jnp.concatenate(columns, axis=0)

    for part, source in enumerate((above, features, below)):
        for row in range(0, tile_rows, block):
            at = part * tile_rows + row
            put(
                wide0,
                at,
                rows_of(before[at : at + block], source[row : row + block], after[at : at + block]),
            )
    for row in range(0, tall - 4, block):
        pre = conv(wide0, row, first)
        s = 1.0 / (1.0 + jnp.exp(-pre))
        ok = lanes(row + 2)
        put(wide1, row, pre * s * ok)
        if NEAR <= row < tall - 4 - NEAR:
            slopes[pl.ds((row - NEAR) * stride, size), :] = s * (1.0 + pre * (1.0 - s)) * ok
    sources = [(target_above, 0)] + [(target, r) for r in range(0, tile_rows, block)] + [(target_below, 0)]
    for index, (source, at) in enumerate(sources):
        row = index * block
        value = conv(wide1, row, second)
        edge = tall + row
        goal = rows_of(
            before[edge : edge + block], source[at : at + block], after[edge : edge + block]
        )
        put(wide2, row, lanes(tall + row) * (value - goal))
    for row in range(0, tile_rows + 4, block):
        value = conv(wide2, row, second_adjoint)
        put(wide3, row, value * slopes[pl.ds(row * stride, size), :])
    for row in range(0, tile_rows, block):
        value = conv(wide3, row, first_adjoint).reshape(block, stride, channels)
        out[row : row + block] = value[:, REACH : REACH + tile_cols].astype(jnp.bfloat16)


def conv_chain(pieces, guard, kernel_first, kernel_second):
    features = pieces[1]
    tile_rows, tile_cols, channels = features.shape
    stride = tile_cols + 2 * REACH
    bf16 = jnp.bfloat16

    def plain(kernel):
        return kernel.reshape(9 * channels, channels)

    def adjoint(kernel):
        return jnp.transpose(jnp.flip(kernel, (0, 1)), (0, 1, 3, 2)).reshape(9 * channels, channels)

    wides = [pltpu.VMEM(((tile_rows + h) * stride, 3 * channels), bf16) for h in (16, 12, 8, 4)]
    pixels = sum((tile_rows + h) * stride for h in (12, 8, 4, 0))
    return vmem_call(
        conv_kernel,
        [jax.ShapeDtypeStruct(features.shape, bf16)],
        *pieces,
        guard,
        plain(kernel_first),
        plain(kernel_second),
        adjoint(kernel_second),
        adjoint(kernel_first),
        flops=2 * 9 * channels * channels * pixels,
        scratch=[*wides, pltpu.VMEM(((tile_rows + 4) * stride, channels), jnp.float32)],
        limit=40,
    )[0]


def neighbours(axis):
    size = lax.axis_size(axis)
    up = [(i, i + 1) for i in range(size - 1)]
    return up, [(j, i) for i, j in up]


def shards(
    features,
    target,
    hole_mask,
    kernel_first,
    kernel_second,
    inputs,
    weight_in,
    weight_out,
    weight_local,
    weight_mix,
):
    tile_rows, tile_cols, channels = features.shape
    row_devices, col_devices = lax.axis_size("row"), lax.axis_size("col")
    devices = row_devices * col_devices
    height, width = tile_rows * row_devices, tile_cols * col_devices
    strip, half = inputs.shape[0], weight_in.shape[1]
    owned = width // 2 // devices
    col_norm, row_norm = 1.0 / math.sqrt(width), 1.0 / math.sqrt(height)
    table = column_matrix(width, devices)
    table_back = jnp.asarray(np.ascontiguousarray(table.T))
    table = jnp.asarray(table)
    row_table = row_matrix(height, devices)
    row_back = jnp.asarray(np.ascontiguousarray(row_table.T))
    row_table = jnp.asarray(row_table)
    bf16 = jnp.bfloat16

    def swap(spectrum):
        return lax.all_to_all(spectrum, ("row", "col"), split_axis=0, concat_axis=0, tiled=True)

    up, down = neighbours("row")
    left, right = neighbours("col")

    def mask_lanes(mask):
        return jnp.pad(mask.astype(bf16).T, ((0, 0), (0, channels - mask.shape[0])))[None]

    above = lax.ppermute(features, "row", up)
    below = lax.ppermute(features, "row", down)
    packed_above = jnp.concatenate([target[-NEAR:], mask_lanes(hole_mask[-NEAR:])], axis=0)
    packed_below = jnp.concatenate([target[:NEAR], mask_lanes(hole_mask[:NEAR])], axis=0)
    packed_above = lax.ppermute(packed_above, "row", up)
    packed_below = lax.ppermute(packed_below, "row", down)

    cells = [jax.ShapeDtypeStruct((width, strip * half), bf16)]
    spatial_cols = vmem_call(
        functools.partial(spectrum_kernel, False, col_norm), cells, inputs, weight_in, table
    )[0]
    spatial_moved = swap(spatial_cols)

    mask_tall = jnp.concatenate(
        [packed_above[NEAR, :, :NEAR], hole_mask.astype(bf16).T, packed_below[NEAR, :, :NEAR]], axis=1
    )
    mask_row = jnp.pad(mask_tall, ((0, 0), (0, channels - mask_tall.shape[1])))[None]

    def edge(cols):
        parts = [above, features, below, packed_above[:NEAR], target, packed_below[:NEAR], mask_row]
        return jnp.concatenate([part[:, cols] for part in parts], axis=0)

    before = lax.ppermute(edge(slice(tile_cols - REACH, None)), "col", left)
    after = lax.ppermute(edge(slice(0, REACH)), "col", right)

    row0, col0 = lax.axis_index("row") * tile_rows, lax.axis_index("col") * tile_cols
    tall = tile_rows + 2 * REACH
    row_ids = row0 - REACH + jnp.arange(tall, dtype=jnp.int32)
    col_ids = col0 - REACH + jnp.arange(tile_cols + 2 * REACH, dtype=jnp.int32)
    ok = ((col_ids >= 0) & (col_ids < width))[:, None] & ((row_ids >= 0) & (row_ids < height))[None]
    ok = ok.astype(jnp.float32)
    near_rows = tile_rows + 2 * NEAR
    mask_wide = jnp.concatenate(
        [before[-1, :, :near_rows], mask_tall, after[-1, :, :near_rows]], axis=0
    ).astype(jnp.float32)
    weights = (1.0 + 2.0 * mask_wide) * ok[:, NEAR : NEAR + near_rows]
    guard = jnp.concatenate([ok, weights], axis=1)

    pieces = (
        above,
        features,
        below,
        packed_above,
        target,
        packed_below,
        before,
        after,
    )
    grad_feat = conv_chain(pieces, guard, kernel_first, kernel_second)

    cell_count = height * owned
    mix = weight_mix.reshape(2, half, 2, half).transpose(0, 2, 1, 3)
    wide = [pltpu.VMEM((strip * half // LANES, width, LANES), jnp.float32)]
    slope = vmem_call(
        functools.partial(slope_kernel, row_norm, owned, devices),
        [jax.ShapeDtypeStruct((2, cell_count, half), jnp.float32)],
        spatial_moved,
        mix,
        row_table,
        scratch=wide,
    )[0]

    strip_grad = lax.all_to_all(grad_feat, "col", split_axis=0, concat_axis=1, tiled=True)
    grad_cols = vmem_call(
        functools.partial(spectrum_kernel, True, col_norm), cells, strip_grad, weight_out, table
    )[0]
    grad_moved = swap(grad_cols)
    grad_rows = vmem_call(
        functools.partial(mix_kernel, row_norm, owned, devices),
        cells,
        grad_moved,
        slope,
        mix,
        row_table,
        row_back,
        scratch=wide,
    )[0]
    returned = swap(grad_rows)
    return vmem_call(
        functools.partial(output_kernel, col_norm),
        [jax.ShapeDtypeStruct(inputs.shape, bf16)],
        returned,
        strip_grad,
        weight_in,
        weight_local,
        table_back,
    )[0]


def solution(mesh):
    in_specs = (
        P("row", "col", None),
        P("row", "col", None),
        P("row", "col"),
        P(),
        P(),
        P(("row", "col"), None, None),
        P(),
        P(),
        P(),
        P(),
    )
    out_specs = P(("row", "col"), None, None)
    return jax.shard_map(shards, mesh=mesh, in_specs=in_specs, out_specs=out_specs, check_vma=False)
```

time: 204 us -> 127 us (0.62); the launches traced: 200 us -> 125 us
  matrix products: 63 us -> 0 us
  blocking collectives: 40.8 us -> 15.5 us
  local copies, waits for them, and re-layouts: 8.88 us -> 19.6 us
  waiting for transfers between devices: 30.5 us -> 37.7 us
  other arithmetic: 9.53 us -> 2.84 us
  starting transfers between devices: 27.1 us -> 30.9 us
    conv_general_dilated x4 -> x0, matrix products: 63 us -> none  [conv_valid(): lax.conv_general_dilated(padded[None], kernel, (1, 1), 'VALID', rhs_dilat...]
    all_gather x2 -> x0, blocking collectives: 25 us -> none  [the longest x1 14.4 us: shards(): lax.all_gather(lax.all_gather(hole_mask, 'col', axis=1, tiled=True), 'row...]
    unnamed x22 -> x40, local copies, waits for them, and re-layouts: 3.01 us -> 10.2 us
    conv_general_dilated x1 -> x0, other arithmetic: 7.09 us -> none  [conv_valid(): lax.conv_general_dilated(padded[None], kernel, (1, 1), 'VALID', rhs_dilat...]
    transpose x0 -> x5, local copies, waits for them, and re-layouts: none -> 6.36 us  [the longest x4 6.28 us: adjoint(): jnp.transpose(jnp.flip(kernel, (0, 1)), (0, 1, 3, 2))]
    all_to_all x2, waiting for transfers between devices: 17.7 us -> 22.6 us  [swap(): lax.all_to_all(spectrum, ('row', 'col'), split_axis=0, concat_axis=0, til...]
    concatenate x6 -> x1, local copies, waits for them, and re-layouts: 3.05 us -> 0.01 us  [edge(): return jnp.concatenate([part[:, cols] for part in parts], axis=0)]
    pallas_call x5 -> x6, Pallas kernels: 19.7 us -> 18.6 us  [vmem_call(): pl.pallas_call(body, out_shape=shapes, in_specs=[spec] * len(operands), o...]
  transfers between devices with their start and end apart: 9 -> 9, of which waited for: 4 -> 6; matrix products, arithmetic and copies ran while one was open for 4% -> 12% of each run, Pallas kernels for 5% -> 3%
where the time goes in v2:
time: 127 us; the launch traced here: 125 us
  waiting for transfers between devices  37.7 us (30%)
  starting transfers between devices  30.9 us (24%)
  local copies, waits for them, and re-layouts  19.6 us (15%)
  Pallas kernels  18.6 us (15%)
  blocking collectives  15.5 us (12%)
  other arithmetic  2.84 us (2%)
    all_to_all x2, waiting for transfers between devices, swap(): lax.all_to_all(spectrum, ('row', 'col'), split_axis=0, concat_axis=0, til...  22.6 us
    pallas_call x6, Pallas kernels, vmem_call(): pl.pallas_call(body, out_shape=shapes, in_specs=[spec] * len(operands), o...  18.6 us
    all_to_all x1, blocking collectives, swap(): lax.all_to_all(spectrum, ('row', 'col'), split_axis=0, concat_axis=0, til...  15.5 us
    all_to_all x1, waiting for transfers between devices, shards(): lax.all_to_all(grad_feat, 'col', split_axis=0, concat_axis=1, tiled=True)  11 us
    unnamed x40, local copies, waits for them, and re-layouts  10.2 us
    all_to_all x2, starting transfers between devices, swap(): lax.all_to_all(spectrum, ('row', 'col'), split_axis=0, concat_axis=0, til...  8.28 us
    transpose x4, local copies, waits for them, and re-layouts, adjoint(): jnp.transpose(jnp.flip(kernel, (0, 1)), (0, 1, 3, 2))  6.28 us
    all_to_all x1, starting transfers between devices, shards(): lax.all_to_all(grad_feat, 'col', split_axis=0, concat_axis=1, tiled=True)  5.33 us
  transfers between devices with their start and end apart: 9, of which 6 were waited for; matrix products, arithmetic and copies ran while one was open for 12% of the time, Pallas kernels for 3%

profile of v2, /device:TPU:1, one launch (start us, length us, event | category | flops | bytes accessed | tf_op | source)
XLA Modules:
  0.0 125.4 jit_solution(15163763401060562331)
XLA Ops:
  0.0 4.5 %collective-permute-start = (bf16[8,128,256]{2,1,0:T(8,128)(2,1)}, bf16[8,128,256]{2,1,0:T(8,128)(2,1)}, u32[]{:S(2)}, u32[]{:S(2)}) collective-permute-start(bf16[8,128,256]{2,1,0:T(8,128)(2,1)} %features.1), channel_id=1, source_target_pairs={{0,4},{4,8},{8,12},{12,16},{16,20},{20,24},{24,28},{1,5},{5,9},{9,... | collective-permute-start | bytes 1572872 | tf_op jit(solution)/shard_map/ppermute | solution.py:279
  4.5 1.9 %collective-permute-start.1 = (bf16[8,128,256]{2,1,0:T(8,128)(2,1)}, bf16[8,128,256]{2,1,0:T(8,128)(2,1)}, u32[]{:S(2)}, u32[]{:S(2)}) collective-permute-start(bf16[8,128,256]{2,1,0:T(8,128)(2,1)} %features.1), channel_id=1, source_target_pairs={{4,0},{8,4},{12,8},{16,12},{20,16},{24,20},{28,24},{5,1},{9,5},{13... | collective-permute-start | bytes 1572872 | tf_op jit(solution)/shard_map/ppermute | solution.py:280
  6.4 0.8 copy.42
  7.9 1.2 fusion.6
  9.8 3.6 %collective-permute-start.2 = (bf16[5,128,256]{2,1,0:T(8,128)(2,1)}, bf16[5,128,256]{2,1,0:T(8,128)(2,1)}, u32[]{:S(2)}, u32[]{:S(2)}) collective-permute-start(bf16[5,128,256]{2,1,0:T(8,128)(2,1)} %pad_maximum_fusion), channel_id=1, source_target_pairs={{0,4},{4,8},{8,12},{12,16},{16,20},{20,24},{24,28},{1,5},{5,9},{9,... | collective-permute-start | bytes 983048 | tf_op jit(solution)/shard_map/ppermute | solution.py:283
  14.2 1.9 %collective-permute-start.3 = (bf16[5,128,256]{2,1,0:T(8,128)(2,1)}, bf16[5,128,256]{2,1,0:T(8,128)(2,1)}, u32[]{:S(2)}, u32[]{:S(2)}) collective-permute-start(bf16[5,128,256]{2,1,0:T(8,128)(2,1)} %pad_maximum_fusion.1), channel_id=1, source_target_pairs={{4,0},{8,4},{12,8},{16,12},{20,16},{24,20},{28,24},{5,1},{9,5},{13... | collective-permute-start | bytes 983048 | tf_op jit(solution)/shard_map/ppermute | solution.py:284
  16.2 1.1 reverse_bitcast_fusion.1
  17.3 1.7 %copy.43 = bf16[3,3,256,256]{3,2,1,0:T(8,128)(2,1)S(1)} copy(bf16[3,3,256,256]{2,3,1,0:T(8,128)(2,1)} %reverse_bitcast_fusion.1) | data formatting | bytes 2359296 | tf_op jit(solution)/shard_map/transpose | solution.py:218
  19.0 1.1 reverse_bitcast_fusion
  20.1 2.4 %copy.44 = bf16[3,3,256,256]{3,2,1,0:T(8,128)(2,1)} copy(bf16[3,3,256,256]{2,3,1,0:T(8,128)(2,1)} %reverse_bitcast_fusion) | data formatting | bytes 2359296 | tf_op jit(solution)/shard_map/transpose | solution.py:218
  22.5 0.9 convert_bitcast_fusion
  23.4 1.8 %collective-permute-done.3.target_below = bf16[5,128,256]{2,1,0:T(8,128)(2,1)} collective-permute-done((bf16[5,128,256]{2,1,0:T(8,128)(2,1)}, bf16[5,128,256]{2,1,0:T(8,128)(2,1)}, u32[]{:S(2)}, u32[]{:S(2)}) %collective-permute-start.3) | collective-permute-done | bytes 327712 | tf_op jit(solution)/shard_map/ppermute | solution.py:284
  31.5 1.3 %collective-permute-start.5 = (bf16[41,8,256]{2,1,0:T(8,128)(2,1)S(1)}, bf16[41,8,256]{2,1,0:T(8,128)(2,1)S(1)}, u32[]{:S(2)}, u32[]{:S(2)}) collective-permute-start(bf16[41,8,256]{2,1,0:T(8,128)(2,1)S(1)} %get-tuple-element.19), channel_id=1, source_target_pairs={{1,0},{2,1},{3,2},{5,4},{6,5},{7,6},{9,8},{10,9},{11,10},{13,12},{... | collective-permute-start | bytes 503816 | tf_op jit(solution)/shard_map/ppermute | solution.py:302
  32.8 4.0 %collective-permute-start.4 = (bf16[41,8,256]{2,1,0:T(8,128)(2,1)S(1)}, bf16[41,8,256]{2,1,0:T(8,128)(2,1)S(1)}, u32[]{:S(2)}, u32[]{:S(2)}) collective-permute-start(bf16[41,8,256]{2,1,0:T(8,128)(2,1)S(1)} %get-tuple-element.20), channel_id=1, source_target_pairs={{0,1},{1,2},{2,3},{4,5},{5,6},{6,7},{8,9},{9,10},{10,11},{12,13},{... | collective-permute-start | bytes 503816 | tf_op jit(solution)/shard_map/ppermute | solution.py:301
  37.6 1.6 %collective-permute-done.4.before = bf16[41,8,256]{2,1,0:T(8,128)(2,1)S(1)} collective-permute-done((bf16[41,8,256]{2,1,0:T(8,128)(2,1)S(1)}, bf16[41,8,256]{2,1,0:T(8,128)(2,1)S(1)}, u32[]{:S(2)}, u32[]{:S(2)}) %collective-permute-start.4) | collective-permute-done | bytes 167968 | tf_op jit(solution)/shard_map/ppermute | solution.py:301
  39.4 1.0 copy-done.5
  40.4 1.0 copy-done.12
  41.4 11.4 %shard_map.136 = bf16[8,128,256]{2,1,0:T(8,128)(2,1)S(1)} custom-call(bf16[8,128,256]{2,1,0:T(8,128)(2,1)} %collective-permute-done.above, bf16[8,128,256]{2,1,0:T(8,128)(2,1)S(1)} %copy-done.12, bf16[8,128,256]{2,1,0:T(8,128)(2,1)} %collective-permute-done.1.below, bf16[5,128,256]{2,1,0:T(8,128)(2,1)} %collective-permute-done.2.target_above, ...), custom_call_target="tpu_custom_call" | custom-call | flops 9512681472 | bytes 8354304 | tf_op jit(solution)/shard_map/pallas_call | solution.py:30
  52.9 0.8 copy-done.6
  53.7 5.3 %all-to-all-start = ((bf16[8,128,256]{2,1,0:T(8,128)(2,1)}), bf16[8,128,256]{2,1,0:T(8,128)(2,1)S(1)}, u32[]{:S(2)}, u32[]{:S(2)}) async-start(bf16[8,128,256]{2,1,0:T(8,128)(2,1)} %copy-done.6), calls=%async_computation | async-start | bytes 1048576 | tf_op jit(solution)/shard_map/all_to_all | solution.py:341
  59.2 1.2 copy-done.4
  60.4 1.6 %shard_map.138 = bf16[512,384]{1,0:T(8,128)(2,1)} custom-call(bf16[2,512,512]{2,1,0:T(8,128)(2,1)S(1)} %copy-done.4, bf16[512,192]{1,0:T(8,128)(2,1)S(1)} %copy.46.weight.weight_in, bf16[512,512]{1,0:T(8,128)(2,1)S(1)} %copy-done), custom_call_target="tpu_custom_call" | custom-call | bytes 2162688 | tf_op jit(solution)/shard_map/pallas_call | solution.py:30
  62.0 11.0 %all-to-all-done = bf16[8,128,256]{2,1,0:T(8,128)(2,1)S(1)} async-done(((bf16[8,128,256]{2,1,0:T(8,128)(2,1)}), bf16[8,128,256]{2,1,0:T(8,128)(2,1)S(1)}, u32[]{:S(2)}, u32[]{:S(2)}) %all-to-all-start) | async-done | bytes 524320 | tf_op jit(solution)/shard_map/all_to_all | solution.py:341
  73.0 5.3 %all-to-all-start.2 = ((bf16[32,16,384]{2,1,0:T(8,128)(2,1)}), bf16[32,16,384]{2,1,0:T(8,128)(2,1)S(1)}, u32[]{:S(2)}, u32[]{:S(2)}) async-start(bf16[32,16,384]{2,1,0:T(8,128)(2,1)} %bitcast.21), calls=%async_computation.2 | async-start | bytes 786432 | tf_op jit(solution)/shard_map/all_to_all | solution.py:271
  78.4 1.5 %shard_map.137 = bf16[512,384]{1,0:T(8,128)(2,1)} custom-call(bf16[2,512,256]{2,1,0:T(8,128)(2,1)S(1)} %bitcast.41, bf16[192,256]{1,0:T(8,128)(2,1)S(1)} %copy-done.10, bf16[512,512]{1,0:T(8,128)(2,1)S(1)} %copy-done), custom_call_target="tpu_custom_call" | custom-call | bytes 1540096 | tf_op jit(solution)/shard_map/pallas_call | solution.py:30
  79.9 11.2 %all-to-all-done.2 = bf16[32,16,384]{2,1,0:T(8,128)(2,1)S(1)} async-done(((bf16[32,16,384]{2,1,0:T(8,128)(2,1)}), bf16[32,16,384]{2,1,0:T(8,128)(2,1)S(1)}, u32[]{:S(2)}, u32[]{:S(2)}) %all-to-all-start.2) | async-done | bytes 393248 | tf_op jit(solution)/shard_map/all_to_all | solution.py:271
  91.1 2.9 %all-to-all-start.1 = ((bf16[32,16,384]{2,1,0:T(8,128)(2,1)}), bf16[32,16,384]{2,1,0:T(8,128)(2,1)S(1)}, u32[]{:S(2)}, u32[]{:S(2)}) async-start(bf16[32,16,384]{2,1,0:T(8,128)(2,1)} %bitcast.19), calls=%async_computation.1 | async-start | bytes 786432 | tf_op jit(solution)/shard_map/all_to_all | solution.py:271
  94.4 1.0 shard_map.139.slope
  95.3 11.4 %all-to-all-done.1 = bf16[32,16,384]{2,1,0:T(8,128)(2,1)S(1)} async-done(((bf16[32,16,384]{2,1,0:T(8,128)(2,1)}), bf16[32,16,384]{2,1,0:T(8,128)(2,1)S(1)}, u32[]{:S(2)}, u32[]{:S(2)}) %all-to-all-start.1) | async-done | bytes 393248 | tf_op jit(solution)/shard_map/all_to_all | solution.py:271
  106.8 1.1 shard_map.140
  107.9 15.5 %all_to_all.51 = bf16[32,16,384]{2,1,0:T(8,128)(2,1)S(1)} all-to-all(bf16[32,16,384]{2,1,0:T(8,128)(2,1)S(1)} %bitcast.47), channel_id=1, replica_groups=mesh['row'=8,'col'=4] {'row','col'}, dimensions={0} | all-to-all | bytes 786432 | tf_op jit(solution)/shard_map/all_to_all | solution.py:271
  123.4 2.0 %shard_map.141 = bf16[2,512,512]{2,1,0:T(8,128)(2,1)} custom-call(bf16[512,384]{1,0:T(8,128)(2,1)S(1)} %bitcast.48, bf16[2,512,256]{2,1,0:T(8,128)(2,1)S(1)} %bitcast.42, bf16[512,192]{1,0:T(8,128)(2,1)S(1)} %copy.46.weight.weight_in, bf16[512,256]{1,0:T(8,128)(2,1)S(1)} %copy-done.8, bf16[512,512]{1,0:T(8,128)(2,1)S(1)} %copy-done.7), custom_call_target="tpu_custom_call" | custom-call | bytes 2949120 | tf_op jit(solution)/shard_map/pallas_call | solution.py:30
  (59 shorter events, 9.9 us)
Async XLA Ops:
  0.0 26.8 %collective-permute-start = (bf16[8,128,256]{2,1,0:T(8,128)(2,1)}, bf16[8,128,256]{2,1,0:T(8,128)(2,1)}, u32[]{:S(2)}, u32[]{:S(2)}) collective-permute-start(bf16[8,128,256]{2,1,0:T(8,128)(2,1)} %features.1), channel_id=1, source_target_pairs={{0,4},{4,8},{8,12},{12,16},{16,20},{20,24},{24,28},{1,5},{5,9},{9,... | collective-permute-start | bytes 1572872 | tf_op jit(solution)/shard_map/ppermute | solution.py:279
  4.5 23.9 %collective-permute-start.1 = (bf16[8,128,256]{2,1,0:T(8,128)(2,1)}, bf16[8,128,256]{2,1,0:T(8,128)(2,1)}, u32[]{:S(2)}, u32[]{:S(2)}) collective-permute-start(bf16[8,128,256]{2,1,0:T(8,128)(2,1)} %features.1), channel_id=1, source_target_pairs={{4,0},{8,4},{12,8},{16,12},{20,16},{24,20},{28,24},{5,1},{9,5},{13... | collective-permute-start | bytes 1572872 | tf_op jit(solution)/shard_map/ppermute | solution.py:280
  7.2 0.6 copy-start.13
  7.9 8.3 %copy-start.2 = (bf16[3,3,256,256]{3,2,1,0:T(8,128)(2,1)S(1)}, bf16[3,3,256,256]{3,2,1,0:T(8,128)(2,1)}, u32[]{:S(2)}) copy-start(bf16[3,3,256,256]{3,2,1,0:T(8,128)(2,1)} %param.18) | copy-start | bytes 3538948
  9.8 16.2 %collective-permute-start.2 = (bf16[5,128,256]{2,1,0:T(8,128)(2,1)}, bf16[5,128,256]{2,1,0:T(8,128)(2,1)}, u32[]{:S(2)}, u32[]{:S(2)}) collective-permute-start(bf16[5,128,256]{2,1,0:T(8,128)(2,1)} %pad_maximum_fusion), channel_id=1, source_target_pairs={{0,4},{4,8},{8,12},{12,16},{16,20},{20,24},{24,28},{1,5},{5,9},{9,... | collective-permute-start | bytes 983048 | tf_op jit(solution)/shard_map/ppermute | solution.py:283
  14.2 11.0 %collective-permute-start.3 = (bf16[5,128,256]{2,1,0:T(8,128)(2,1)}, bf16[5,128,256]{2,1,0:T(8,128)(2,1)}, u32[]{:S(2)}, u32[]{:S(2)}) collective-permute-start(bf16[5,128,256]{2,1,0:T(8,128)(2,1)} %pad_maximum_fusion.1), channel_id=1, source_target_pairs={{4,0},{8,4},{12,8},{16,12},{20,16},{24,20},{28,24},{5,1},{9,5},{13... | collective-permute-start | bytes 983048 | tf_op jit(solution)/shard_map/ppermute | solution.py:284
  17.3 1.7 %copy-start.1 = (bf16[3,3,256,256]{3,2,1,0:T(8,128)(2,1)S(1)}, bf16[3,3,256,256]{3,2,1,0:T(8,128)(2,1)}, u32[]{:S(2)}) copy-start(bf16[3,3,256,256]{3,2,1,0:T(8,128)(2,1)} %param.17) | copy-start | bytes 3538948
  22.5 16.9 %copy-start.3 = (bf16[3,3,256,256]{3,2,1,0:T(8,128)(2,1)S(1)}, bf16[3,3,256,256]{3,2,1,0:T(8,128)(2,1)}, u32[]{:S(2)}) copy-start(bf16[3,3,256,256]{3,2,1,0:T(8,128)(2,1)} %copy.44) | copy-start | bytes 3538948
  31.5 6.1 %collective-permute-start.5 = (bf16[41,8,256]{2,1,0:T(8,128)(2,1)S(1)}, bf16[41,8,256]{2,1,0:T(8,128)(2,1)S(1)}, u32[]{:S(2)}, u32[]{:S(2)}) collective-permute-start(bf16[41,8,256]{2,1,0:T(8,128)(2,1)S(1)} %get-tuple-element.19), channel_id=1, source_target_pairs={{1,0},{2,1},{3,2},{5,4},{6,5},{7,6},{9,8},{10,9},{11,10},{13,12},{... | collective-permute-start | bytes 503816 | tf_op jit(solution)/shard_map/ppermute | solution.py:302
  32.8 6.3 %collective-permute-start.4 = (bf16[41,8,256]{2,1,0:T(8,128)(2,1)S(1)}, bf16[41,8,256]{2,1,0:T(8,128)(2,1)S(1)}, u32[]{:S(2)}, u32[]{:S(2)}) collective-permute-start(bf16[41,8,256]{2,1,0:T(8,128)(2,1)S(1)} %get-tuple-element.20), channel_id=1, source_target_pairs={{0,1},{1,2},{2,3},{4,5},{5,6},{6,7},{8,9},{9,10},{10,11},{12,13},{... | collective-permute-start | bytes 503816 | tf_op jit(solution)/shard_map/ppermute | solution.py:301
  39.3 1.0 copy-start.5
  40.4 1.0 copy-start.12
  52.9 0.8 copy-start.6
  53.7 5.3 %copy-start.15 = (bf16[512,192]{0,1:T(8,128)(2,1)S(1)}, bf16[512,192]{0,1:T(8,128)(2,1)}, u32[]{:S(2)}) copy-start(bf16[512,192]{0,1:T(8,128)(2,1)} %param.20) | copy-start | bytes 589828
  53.7 5.5 %copy-start = (bf16[512,512]{1,0:T(8,128)(2,1)S(1)}, bf16[512,512]{1,0:T(8,128)(2,1)}, u32[]{:S(2)}) copy-start(bf16[512,512]{1,0:T(8,128)(2,1)} %constant.39.clone.table) | copy-start | bytes 1572868
  53.7 19.3 %all-to-all-start = ((bf16[8,128,256]{2,1,0:T(8,128)(2,1)}), bf16[8,128,256]{2,1,0:T(8,128)(2,1)S(1)}, u32[]{:S(2)}, u32[]{:S(2)}) async-start(bf16[8,128,256]{2,1,0:T(8,128)(2,1)} %copy-done.6), calls=%async_computation | async-start | bytes 1048576 | tf_op jit(solution)/shard_map/all_to_all | solution.py:341
  59.2 1.2 copy-start.4
  62.0 16.4 %copy-start.10 = (bf16[192,256]{1,0:T(8,128)(2,1)S(1)}, bf16[192,256]{1,0:T(8,128)(2,1)}, u32[]{:S(2)}) copy-start(bf16[192,256]{1,0:T(8,128)(2,1)} %weight.2) | copy-start | bytes 294916
  73.0 18.1 %all-to-all-start.2 = ((bf16[32,16,384]{2,1,0:T(8,128)(2,1)}), bf16[32,16,384]{2,1,0:T(8,128)(2,1)S(1)}, u32[]{:S(2)}, u32[]{:S(2)}) async-start(bf16[32,16,384]{2,1,0:T(8,128)(2,1)} %bitcast.21), calls=%async_computation.2 | async-start | bytes 786432 | tf_op jit(solution)/shard_map/all_to_all | solution.py:271
  78.4 15.6 %copy-start.14 = (bf16[384,384]{1,0:T(8,128)(2,1)S(1)}, bf16[384,384]{1,0:T(8,128)(2,1)}, u32[]{:S(2)}) copy-start(bf16[384,384]{1,0:T(8,128)(2,1)} %param.23) | copy-start | bytes 884740
  79.9 14.5 %copy-start.9 = (bf16[128,128]{1,0:T(8,128)(2,1)S(1)}, bf16[128,128]{1,0:T(8,128)(2,1)}, u32[]{:S(2)}) copy-start(bf16[128,128]{1,0:T(8,128)(2,1)} %constant.41.clone.table) | copy-start | bytes 98308
  91.1 15.7 %all-to-all-start.1 = ((bf16[32,16,384]{2,1,0:T(8,128)(2,1)}), bf16[32,16,384]{2,1,0:T(8,128)(2,1)S(1)}, u32[]{:S(2)}, u32[]{:S(2)}) async-start(bf16[32,16,384]{2,1,0:T(8,128)(2,1)} %bitcast.19), calls=%async_computation.1 | async-start | bytes 786432 | tf_op jit(solution)/shard_map/all_to_all | solution.py:271
  94.3 12.5 %copy-start.11 = (bf16[128,128]{1,0:T(8,128)(2,1)S(1)}, bf16[128,128]{1,0:T(8,128)(2,1)}, u32[]{:S(2)}) copy-start(bf16[128,128]{1,0:T(8,128)(2,1)} %constant.40.clone.back_table) | copy-start | bytes 98308
  106.8 16.6 %copy-start.7 = (bf16[512,512]{1,0:T(8,128)(2,1)S(1)}, bf16[512,512]{1,0:T(8,128)(2,1)}, u32[]{:S(2)}) copy-start(bf16[512,512]{1,0:T(8,128)(2,1)} %constant.38.clone.table) | copy-start | bytes 1572868
  106.8 16.6 %copy-start.8 = (bf16[512,256]{1,0:T(8,128)(2,1)S(1)}, bf16[512,256]{1,0:T(8,128)(2,1)}, u32[]{:S(2)}) copy-start(bf16[512,256]{1,0:T(8,128)(2,1)} %weight_local.1) | copy-start | bytes 786436

commit v3 on v2

--- a/solution.py
+++ b/solution.py
@@ -59,9 +59,16 @@
     return np.block([[cos, sin], [-sin, cos]])
 
 
+def strip_row(signal, r):
+    if len(signal.shape) == 3:
+        return signal[r]
+    return jnp.concatenate([signal[block, r] for block in range(signal.shape[0])], axis=0)
+
+
 def spectrum_kernel(transposed, norm, signal, weight, table, out):
     product = dot_t if transposed else dot
-    rows = [product(signal[r], weight[...]).astype(jnp.bfloat16) for r in range(signal.shape[0])]
+    count = signal.shape[0 if len(signal.shape) == 3 else 1]
+    rows = [product(strip_row(signal, r), weight[...]).astype(jnp.bfloat16) for r in range(count)]
     out[...] = (dot(table[...], jnp.concatenate(rows, axis=1)) * norm).astype(jnp.bfloat16)
 
 
@@ -122,26 +129,77 @@
 def output_kernel(norm, moved, strip_grad, weight_in, weight_local, table, out):
     spatial = (dot(table[...], moved[...]) * norm).astype(jnp.bfloat16)
     half = weight_in.shape[1]
-    for r in range(strip_grad.shape[0]):
+    for r in range(out.shape[0]):
         total = dot_t(spatial[:, r * half : (r + 1) * half], weight_in[...])
-        total = total + dot_t(strip_grad[r], weight_local[...])
+        total = total + dot_t(strip_row(strip_grad, r), weight_local[...])
         out[r] = total.astype(jnp.bfloat16)
+
+
+def row_pack_kernel(features, target, mask, down, up):
+    tile_rows, tile_cols, channels = features.shape
+    lanes = jnp.concatenate(
+        [
+            mask[...].astype(jnp.float32),
+            jnp.zeros((tile_cols - tile_rows, tile_cols), jnp.float32),
+        ],
+        axis=0,
+    ).T
+    row = jnp.concatenate([lanes] + [jnp.zeros_like(lanes)] * (channels // tile_cols - 1), axis=1)
+    for pack, start in ((down, tile_rows - NEAR), (up, 0)):
+        pack[:tile_rows] = features[...]
+        pack[tile_rows : tile_rows + NEAR] = target[start : start + NEAR]
+        pack[tile_rows + NEAR] = row.astype(jnp.bfloat16)
+
+
+def row_packs(features, target, mask):
+    tile_rows, tile_cols, channels = features.shape
+    pack = jax.ShapeDtypeStruct((tile_rows + NEAR + 1, tile_cols, channels), features.dtype)
+    return vmem_call(row_pack_kernel, [pack, pack], features, target, mask)
+
+
+def edge_kernel(*refs):
+    sources, outs = refs[:-2], refs[-2:]
+    count = len(sources) // 2
+    for out, group in zip(outs, (sources[:count], sources[count:])):
+        row = 0
+        for ref in group:
+            out[row : row + ref.shape[0]] = ref[...]
+            row += ref.shape[0]
+
+
+def edges(above, features, target, mask_row, below):
+    parts = [above, features, target, mask_row, below]
+    channels = features.shape[2]
+    last = features.shape[1] // REACH - 1
+
+    def specs(at):
+        return [pl.BlockSpec((p.shape[0], REACH, channels), lambda i, at=at: (0, at, 0)) for p in parts]
+
+    rows = sum(p.shape[0] for p in parts)
+    shape = jax.ShapeDtypeStruct((rows, REACH, channels), features.dtype)
+    return pl.pallas_call(
+        edge_kernel,
+        grid=(1,),
+        out_shape=[shape, shape],
+        in_specs=specs(last) + specs(0),
+        out_specs=[pl.BlockSpec(shape.shape, lambda i: (0, 0, 0))] * 2,
+        cost_estimate=pl.CostEstimate(
+            flops=0, bytes_accessed=8 * rows * REACH * channels, transcendentals=0
+        ),
+    )(*parts, *parts)
 
 
 def conv_kernel(
     above,
     features,
+    target,
+    mask_row,
     below,
-    target_above,
-    target,
-    target_below,
     before,
     after,
-    guard,
+    ok,
     first,
     second,
-    second_adjoint,
-    first_adjoint,
     out,
     wide0,
     wide1,
@@ -154,10 +212,13 @@
     block = NEAR
     size = block * stride
     tall = tile_rows + 2 * REACH
-
-    def rows_of(left, middle, right):
-        parts = [part.astype(jnp.float32) for part in (left, middle, right)]
-        return jnp.concatenate(parts, axis=1).reshape(size, channels)
+    pack = above.shape[0]
+    below_at = pack + 2 * tile_rows + 1
+
+    def rows_of(edge, source, row, count=block):
+        parts = [before[edge : edge + count], source[row : row + count], after[edge : edge + count]]
+        parts = [part.astype(jnp.float32) for part in parts]
+        return jnp.concatenate(parts, axis=1).reshape(count * stride, channels)
 
     def put(wide, row, value):
         spot = pl.ds(row * stride, size)
@@ -165,69 +226,68 @@
         wide[spot, channels : 2 * channels] = value.astype(jnp.bfloat16)
         wide[spot, 2 * channels :] = pltpu.roll(value, size - 2, 0).astype(jnp.bfloat16)
 
+    def taps(wide, row):
+        return jnp.concatenate(
+            [wide[pl.ds((row + 2 * a) * stride, size), :] for a in range(3)], axis=1
+        )
+
     def conv(wide, row, kernel):
-        taps = [wide[pl.ds((row + 2 * a) * stride, size), :] for a in range(3)]
-        return dot(jnp.concatenate(taps, axis=1), kernel[...])
-
-    def lanes(start):
-        columns = [guard[:, start + i : start + i + 1] for i in range(block)]
-        return jnp.concatenate(columns, axis=0)
-
-    for part, source in enumerate((above, features, below)):
+        return dot(taps(wide, row), kernel[...].reshape(9 * channels, channels))
+
+    def conv_adjoint(wide, row, kernel):
+        flipped = [kernel[2 - a, 2 - b] for a in range(3) for b in range(3)]
+        return dot_t(taps(wide, row), jnp.concatenate(flipped, axis=1))
+
+    def inside(row):
+        return jnp.concatenate([ok[:, row + i : row + i + 1] for i in range(block)], axis=0)
+
+    sources = ((above, 0), (features, pack), (below, below_at))
+    for part, (source, edge) in enumerate(sources):
         for row in range(0, tile_rows, block):
-            at = part * tile_rows + row
-            put(
-                wide0,
-                at,
-                rows_of(before[at : at + block], source[row : row + block], after[at : at + block]),
-            )
+            put(wide0, part * tile_rows + row, rows_of(edge + row, source, row))
     for row in range(0, tall - 4, block):
         pre = conv(wide0, row, first)
         s = 1.0 / (1.0 + jnp.exp(-pre))
-        ok = lanes(row + 2)
-        put(wide1, row, pre * s * ok)
+        kept = inside(row + 2)
+        put(wide1, row, pre * s * kept)
         if NEAR <= row < tall - 4 - NEAR:
-            slopes[pl.ds((row - NEAR) * stride, size), :] = s * (1.0 + pre * (1.0 - s)) * ok
-    sources = [(target_above, 0)] + [(target, r) for r in range(0, tile_rows, block)] + [(target_below, 0)]
-    for index, (source, at) in enumerate(sources):
+            slopes[pl.ds((row - NEAR) * stride, size), :] = s * (1.0 + pre * (1.0 - s)) * kept
+    masks = [
+        rows_of(pack - 1, above, pack - 1, 1),
+        rows_of(pack + 2 * tile_rows, mask_row, 0, 1),
+        rows_of(below_at + pack - 1, below, pack - 1, 1),
+    ]
+    goals = [(tile_rows, above, tile_rows, masks[0], tile_rows - NEAR)]
+    goals += [(pack + tile_rows + r, target, r, masks[1], r) for r in range(0, tile_rows, block)]
+    goals += [(below_at + tile_rows, below, tile_rows, masks[2], 0)]
+    for index, (edge, source, at, mask, lane) in enumerate(goals):
         row = index * block
         value = conv(wide1, row, second)
-        edge = tall + row
-        goal = rows_of(
-            before[edge : edge + block], source[at : at + block], after[edge : edge + block]
-        )
-        put(wide2, row, lanes(tall + row) * (value - goal))
+        holes = jnp.concatenate([mask[:, lane + i : lane + i + 1] for i in range(block)], axis=0)
+        weight = (1.0 + 2.0 * holes) * inside(row + NEAR)
+        put(wide2, row, weight * (value - rows_of(edge, source, at)))
     for row in range(0, tile_rows + 4, block):
-        value = conv(wide2, row, second_adjoint)
+        value = conv_adjoint(wide2, row, second)
         put(wide3, row, value * slopes[pl.ds(row * stride, size), :])
     for row in range(0, tile_rows, block):
-        value = conv(wide3, row, first_adjoint).reshape(block, stride, channels)
+        value = conv_adjoint(wide3, row, first).reshape(block, stride, channels)
         out[row : row + block] = value[:, REACH : REACH + tile_cols].astype(jnp.bfloat16)
 
 
-def conv_chain(pieces, guard, kernel_first, kernel_second):
-    features = pieces[1]
+def conv_chain(features, *others):
     tile_rows, tile_cols, channels = features.shape
     stride = tile_cols + 2 * REACH
-    bf16 = jnp.bfloat16
-
-    def plain(kernel):
-        return kernel.reshape(9 * channels, channels)
-
-    def adjoint(kernel):
-        return jnp.transpose(jnp.flip(kernel, (0, 1)), (0, 1, 3, 2)).reshape(9 * channels, channels)
-
-    wides = [pltpu.VMEM(((tile_rows + h) * stride, 3 * channels), bf16) for h in (16, 12, 8, 4)]
+    above, *rest = others
+    wides = [
+        pltpu.VMEM(((tile_rows + h) * stride, 3 * channels), jnp.bfloat16) for h in (16, 12, 8, 4)
+    ]
     pixels = sum((tile_rows + h) * stride for h in (12, 8, 4, 0))
     return vmem_call(
         conv_kernel,
-        [jax.ShapeDtypeStruct(features.shape, bf16)],
-        *pieces,
-        guard,
-        plain(kernel_first),
-        plain(kernel_second),
-        adjoint(kernel_second),
-        adjoint(kernel_first),
+        [jax.ShapeDtypeStruct(features.shape, jnp.bfloat16)],
+        above,
+        features,
+        *rest,
         flops=2 * 9 * channels * channels * pixels,
         scratch=[*wides, pltpu.VMEM(((tile_rows + 4) * stride, channels), jnp.float32)],
         limit=40,
@@ -270,61 +330,32 @@
     def swap(spectrum):
         return lax.all_to_all(spectrum, ("row", "col"), split_axis=0, concat_axis=0, tiled=True)
 
-    up, down = neighbours("row")
-    left, right = neighbours("col")
-
-    def mask_lanes(mask):
-        return jnp.pad(mask.astype(bf16).T, ((0, 0), (0, channels - mask.shape[0])))[None]
-
-    above = lax.ppermute(features, "row", up)
-    below = lax.ppermute(features, "row", down)
-    packed_above = jnp.concatenate([target[-NEAR:], mask_lanes(hole_mask[-NEAR:])], axis=0)
-    packed_below = jnp.concatenate([target[:NEAR], mask_lanes(hole_mask[:NEAR])], axis=0)
-    packed_above = lax.ppermute(packed_above, "row", up)
-    packed_below = lax.ppermute(packed_below, "row", down)
-
     cells = [jax.ShapeDtypeStruct((width, strip * half), bf16)]
     spatial_cols = vmem_call(
         functools.partial(spectrum_kernel, False, col_norm), cells, inputs, weight_in, table
     )[0]
     spatial_moved = swap(spatial_cols)
 
-    mask_tall = jnp.concatenate(
-        [packed_above[NEAR, :, :NEAR], hole_mask.astype(bf16).T, packed_below[NEAR, :, :NEAR]], axis=1
-    )
-    mask_row = jnp.pad(mask_tall, ((0, 0), (0, channels - mask_tall.shape[1])))[None]
-
-    def edge(cols):
-        parts = [above, features, below, packed_above[:NEAR], target, packed_below[:NEAR], mask_row]
-        return jnp.concatenate([part[:, cols] for part in parts], axis=0)
-
-    before = lax.ppermute(edge(slice(tile_cols - REACH, None)), "col", left)
-    after = lax.ppermute(edge(slice(0, REACH)), "col", right)
+    up, down = neighbours("row")
+    left, right = neighbours("col")
+    pack_down, pack_up = row_packs(features, target, hole_mask)
+    mask_row = pack_up[-1:]
+    above = lax.ppermute(pack_down, "row", up)
+    below = lax.ppermute(pack_up, "row", down)
+    above, spatial_cols = lax.optimization_barrier((above, spatial_cols))
+    last, initial = edges(above, features, target, mask_row, below)
+    before = lax.ppermute(last, "col", left)
+    after = lax.ppermute(initial, "col", right)
+    before, spatial_moved = lax.optimization_barrier((before, spatial_moved))
 
     row0, col0 = lax.axis_index("row") * tile_rows, lax.axis_index("col") * tile_cols
-    tall = tile_rows + 2 * REACH
-    row_ids = row0 - REACH + jnp.arange(tall, dtype=jnp.int32)
+    row_ids = row0 - REACH + jnp.arange(tile_rows + 2 * REACH, dtype=jnp.int32)
     col_ids = col0 - REACH + jnp.arange(tile_cols + 2 * REACH, dtype=jnp.int32)
     ok = ((col_ids >= 0) & (col_ids < width))[:, None] & ((row_ids >= 0) & (row_ids < height))[None]
     ok = ok.astype(jnp.float32)
-    near_rows = tile_rows + 2 * NEAR
-    mask_wide = jnp.concatenate(
-        [before[-1, :, :near_rows], mask_tall, after[-1, :, :near_rows]], axis=0
-    ).astype(jnp.float32)
-    weights = (1.0 + 2.0 * mask_wide) * ok[:, NEAR : NEAR + near_rows]
-    guard = jnp.concatenate([ok, weights], axis=1)
-
-    pieces = (
-        above,
-        features,
-        below,
-        packed_above,
-        target,
-        packed_below,
-        before,
-        after,
+    grad_feat = conv_chain(
+        features, above, target, mask_row, below, before, after, ok, kernel_first, kernel_second
     )
-    grad_feat = conv_chain(pieces, guard, kernel_first, kernel_second)
 
     cell_count = height * owned
     mix = weight_mix.reshape(2, half, 2, half).transpose(0, 2, 1, 3)
@@ -338,7 +369,9 @@
         scratch=wide,
     )[0]
 
-    strip_grad = lax.all_to_all(grad_feat, "col", split_axis=0, concat_axis=1, tiled=True)
+    strip_grad = lax.all_to_all(
+        grad_feat.reshape(col_devices, strip, tile_cols, channels), "col", split_axis=0, concat_axis=0
+    )
     grad_cols = vmem_call(
         functools.partial(spectrum_kernel, True, col_norm), cells, strip_grad, weight_out, table
     )[0]

time: 127 us -> 118 us (0.929)
  blocking collectives: 15.5 us -> 28 us
  waiting for transfers between devices: 37.7 us -> 27 us
  local copies, waits for them, and re-layouts: 19.6 us -> 12.6 us
  starting transfers between devices: 30.9 us -> 27.5 us
  other arithmetic: 2.84 us -> 0.1 us
  Pallas kernels: 18.6 us -> 21.3 us
    all_to_all x0 -> x1, blocking collectives: none -> 12.5 us  [shards(): lax.all_to_all(grad_feat.reshape(col_devices, strip, tile_cols, channels)...]
    ppermute x6 -> x4, waiting for transfers between devices: 4.08 us -> 16.6 us  [the longest x1 11.6 us: shards(): below = lax.ppermute(pack_up, 'row', down)]
    all_to_all x2, waiting for transfers between devices: 22.6 us -> 10.5 us  [swap(): lax.all_to_all(spectrum, ('row', 'col'), split_axis=0, concat_axis=0, til...]
    all_to_all x1 -> x0, waiting for transfers between devices: 11 us -> none  [shards(): lax.all_to_all(grad_feat, 'col', split_axis=0, concat_axis=1, tiled=True)]
    all_to_all x2, starting transfers between devices: 8.28 us -> 16.6 us  [swap(): lax.all_to_all(spectrum, ('row', 'col'), split_axis=0, concat_axis=0, til...]
    transpose x5 -> x0, local copies, waits for them, and re-layouts: 6.36 us -> none  [the longest x4 6.28 us: adjoint(): jnp.transpose(jnp.flip(kernel, (0, 1)), (0, 1, 3, 2))]
    ppermute x6 -> x4, starting transfers between devices: 17.2 us -> 10.9 us  [the longest x1 4.5 us: shards(): above = lax.ppermute(pack_down, 'row', up)]
    all_to_all x1 -> x0, starting transfers between devices: 5.33 us -> none  [shards(): lax.all_to_all(grad_feat, 'col', split_axis=0, concat_axis=1, tiled=True)]
  transfers between devices with their start and end apart: 9 -> 6, of which waited for: 6 -> 4; matrix products, arithmetic and copies ran while one was open for 12% -> 2% of each run, Pallas kernels for 3% -> 5%
where the time goes in v3:
time: 118 us; the launch traced here: 117 us
  blocking collectives  28 us (24%)
  starting transfers between devices  27.5 us (23%)
  waiting for transfers between devices  27 us (23%)
  Pallas kernels  21.3 us (18%)
  local copies, waits for them, and re-layouts  12.6 us (11%)
    pallas_call x7, Pallas kernels, vmem_call(): pl.pallas_call(body, out_shape=shapes, in_specs=[spec] * len(operands), o...  19.6 us
    all_to_all x2, starting transfers between devices, swap(): lax.all_to_all(spectrum, ('row', 'col'), split_axis=0, concat_axis=0, til...  16.6 us
    all_to_all x1, blocking collectives, swap(): lax.all_to_all(spectrum, ('row', 'col'), split_axis=0, concat_axis=0, til...  15.5 us
    all_to_all x1, blocking collectives, shards(): lax.all_to_all(grad_feat.reshape(col_devices, strip, tile_cols, channels)...  12.5 us
    ppermute x1, waiting for transfers between devices, shards(): below = lax.ppermute(pack_up, 'row', down)  11.6 us
    unnamed x43, local copies, waits for them, and re-layouts  10.8 us
    all_to_all x2, waiting for transfers between devices, swap(): lax.all_to_all(spectrum, ('row', 'col'), split_axis=0, concat_axis=0, til...  10.5 us
    ppermute x1, starting transfers between devices, shards(): above = lax.ppermute(pack_down, 'row', up)  4.5 us
  transfers between devices with their start and end apart: 6, of which 4 were waited for; matrix products, arithmetic and copies ran while one was open for 2% of the time, Pallas kernels for 5%

profile of v3, /device:TPU:1, one launch (start us, length us, event | category | flops | bytes accessed | tf_op | source)
XLA Modules:
  0.0 116.6 jit_solution(17122464730809254473)
XLA Ops:
  0.0 1.0 copy-done
  1.0 1.0 copy-done.2
  2.1 0.7 copy-done.16
  2.8 1.4 %shard_map.136 = (bf16[13,128,256]{2,1,0:T(8,128)(2,1)}, bf16[13,128,256]{2,1,0:T(8,128)(2,1)}) custom-call(bf16[8,128,256]{2,1,0:T(8,128)(2,1)S(1)} %copy-done, bf16[8,128,256]{2,1,0:T(8,128)(2,1)S(1)} %copy-done.2, s32[8,128]{1,0:T(8,128)S(1)} %copy-done.16), custom_call_target="tpu_custom_call" | custom-call | bytes 2756608 | tf_op jit(solution)/shard_map/pallas_call | solution.py:30
  4.1 4.5 %collective-permute-start = (bf16[13,128,256]{2,1,0:T(8,128)(2,1)}, bf16[13,128,256]{2,1,0:T(8,128)(2,1)S(1)}, u32[]{:S(2)}, u32[]{:S(2)}) collective-permute-start(bf16[13,128,256]{2,1,0:T(8,128)(2,1)} %get-tuple-element.12), channel_id=1, source_target_pairs={{0,4},{4,8},{8,12},{12,16},{16,20},{20,24},{24,28},{1,5},{5,9},{9,... | collective-permute-start | bytes 2555912 | tf_op jit(solution)/shard_map/ppermute | solution.py:343
  8.6 1.9 %collective-permute-start.1 = (bf16[13,128,256]{2,1,0:T(8,128)(2,1)}, bf16[13,128,256]{2,1,0:T(8,128)(2,1)S(1)}, u32[]{:S(2)}, u32[]{:S(2)}) collective-permute-start(bf16[13,128,256]{2,1,0:T(8,128)(2,1)} %get-tuple-element.14), channel_id=1, source_target_pairs={{4,0},{8,4},{12,8},{16,12},{20,16},{24,20},{28,24},{5,1},{9,5},{13... | collective-permute-start | bytes 2555912 | tf_op jit(solution)/shard_map/ppermute | solution.py:344
  10.7 1.2 %copy-done.9 = bf16[2,512,512]{2,1,0:T(8,128)(2,1)S(1)} copy-done((bf16[2,512,512]{2,1,0:T(8,128)(2,1)S(1)}, bf16[2,512,512]{2,1,0:T(8,128)(2,1)}, u32[]{:S(2)}) %copy-start.9) | copy-done | bytes 1048600
  12.0 1.6 %shard_map.137 = bf16[512,384]{1,0:T(8,128)(2,1)} custom-call(bf16[2,512,512]{2,1,0:T(8,128)(2,1)S(1)} %copy-done.9, bf16[512,192]{1,0:T(8,128)(2,1)S(1)} %copy.17.weight.weight_in, bf16[512,512]{1,0:T(8,128)(2,1)S(1)} %copy-done.8), custom_call_target="tpu_custom_call" | custom-call | bytes 2162688 | tf_op jit(solution)/shard_map/pallas_call | solution.py:30
  13.6 6.3 %all-to-all-start = ((bf16[32,16,384]{2,1,0:T(8,128)(2,1)}), bf16[32,16,384]{2,1,0:T(8,128)(2,1)}, u32[]{:S(2)}, u32[]{:S(2)}) async-start(bf16[32,16,384]{2,1,0:T(8,128)(2,1)} %bitcast), calls=%async_computation | async-start | bytes 786432 | tf_op jit(solution)/shard_map/all_to_all | solution.py:331
  19.8 1.5 %slice.3.refs_3_.refs_8_.mask_row = bf16[1,128,256]{2,1,0:T(8,128)(2,1)} slice(bf16[13,128,256]{2,1,0:T(8,128)(2,1)} %get-tuple-element.14), slice={[12:13], [0:128], [0:256]} | slice | bytes 131072 | tf_op jit(solution)/shard_map/slice | solution.py:342
  21.4 11.6 %collective-permute-done.1.refs_4_.refs_9_.below = bf16[13,128,256]{2,1,0:T(8,128)(2,1)S(1)} collective-permute-done((bf16[13,128,256]{2,1,0:T(8,128)(2,1)}, bf16[13,128,256]{2,1,0:T(8,128)(2,1)S(1)}, u32[]{:S(2)}, u32[]{:S(2)}) %collective-permute-start.1) | collective-permute-done | bytes 852000 | tf_op jit(solution)/shard_map/ppermute | solution.py:344
  32.9 1.0 copy-done.6
  33.9 1.7 %shard_map.138 = (bf16[43,8,256]{2,1,0:T(8,128)(2,1)}, bf16[43,8,256]{2,1,0:T(8,128)(2,1)}) custom-call(bf16[13,128,256]{2,1,0:T(8,128)(2,1)} %copy-done.4, bf16[8,128,256]{2,1,0:T(8,128)(2,1)} %features.3, bf16[8,128,256]{2,1,0:T(8,128)(2,1)} %target.3, bf16[1,128,256]{2,1,0:T(8,128)(2,1)} %slice.3.refs_3_.refs_8_.mask_row, ...), custom_call_target="tpu_custom_call" | custom-call | bytes 704512 | tf_op jit(solution)/shard_map/pallas_call | solution.py:180
  35.6 3.2 %collective-permute-start.2 = (bf16[43,8,256]{2,1,0:T(8,128)(2,1)}, bf16[43,8,256]{2,1,0:T(8,128)(2,1)S(1)}, u32[]{:S(2)}, u32[]{:S(2)}) collective-permute-start(bf16[43,8,256]{2,1,0:T(8,128)(2,1)} %get-tuple-element.15), channel_id=1, source_target_pairs={{0,1},{1,2},{2,3},{4,5},{5,6},{6,7},{8,9},{9,10},{10,11},{12,13},{... | collective-permute-start | bytes 528392 | tf_op jit(solution)/shard_map/ppermute | solution.py:347
  38.8 1.3 %collective-permute-start.3 = (bf16[43,8,256]{2,1,0:T(8,128)(2,1)}, bf16[43,8,256]{2,1,0:T(8,128)(2,1)S(1)}, u32[]{:S(2)}, u32[]{:S(2)}) collective-permute-start(bf16[43,8,256]{2,1,0:T(8,128)(2,1)} %get-tuple-element.17), channel_id=1, source_target_pairs={{1,0},{2,1},{3,2},{5,4},{6,5},{7,6},{9,8},{10,9},{11,10},{13,12},{... | collective-permute-start | bytes 528392 | tf_op jit(solution)/shard_map/ppermute | solution.py:348
  40.2 1.3 %collective-permute-done.2.before = bf16[43,8,256]{2,1,0:T(8,128)(2,1)S(1)} collective-permute-done((bf16[43,8,256]{2,1,0:T(8,128)(2,1)}, bf16[43,8,256]{2,1,0:T(8,128)(2,1)S(1)}, u32[]{:S(2)}, u32[]{:S(2)}) %collective-permute-start.2) | collective-permute-done | bytes 176160 | tf_op jit(solution)/shard_map/ppermute | solution.py:347
  41.5 3.7 %collective-permute-done.3.after = bf16[43,8,256]{2,1,0:T(8,128)(2,1)S(1)} collective-permute-done((bf16[43,8,256]{2,1,0:T(8,128)(2,1)}, bf16[43,8,256]{2,1,0:T(8,128)(2,1)S(1)}, u32[]{:S(2)}, u32[]{:S(2)}) %collective-permute-start.3) | collective-permute-done | bytes 176160 | tf_op jit(solution)/shard_map/ppermute | solution.py:348
  45.2 1.2 copy-done.5
  46.4 1.2 copy-done.7
  47.5 0.8 copy-done.10
  48.4 1.3 %copy-done.17 = bf16[3,3,256,256]{3,2,1,0:T(8,128)(2,1)S(1)} copy-done((bf16[3,3,256,256]{3,2,1,0:T(8,128)(2,1)S(1)}, bf16[3,3,256,256]{3,2,1,0:T(8,128)(2,1)}, u32[]{:S(2)}) %copy-start.17) | copy-done | bytes 1179672
  49.6 1.3 %copy-done.18 = bf16[3,3,256,256]{3,2,1,0:T(8,128)(2,1)S(1)} copy-done((bf16[3,3,256,256]{3,2,1,0:T(8,128)(2,1)S(1)}, bf16[3,3,256,256]{3,2,1,0:T(8,128)(2,1)}, u32[]{:S(2)}) %copy-start.18) | copy-done | bytes 1179672
  50.9 10.1 %shard_map.139 = bf16[8,128,256]{2,1,0:T(8,128)(2,1)S(1)} custom-call(bf16[13,128,256]{2,1,0:T(8,128)(2,1)S(1)} %copy-done.5, bf16[8,128,256]{2,1,0:T(8,128)(2,1)S(1)} %copy-done.1, bf16[8,128,256]{2,1,0:T(8,128)(2,1)S(1)} %copy-done.3, bf16[1,128,256]{2,1,0:T(8,128)(2,1)S(1)} %copy-done.10, bf16[13,128,256]{2,1,0:T(8,128)(2,1)S(1)} %copy-done.7, ...), custom_call_target="tpu_custom_call" | custom-call | flops 9512681472 | bytes 6067712 | tf_op jit(solution)/shard_map/pallas_call | solution.py:30
  61.0 12.5 %all_to_all.39.signal.strip_grad = bf16[4,2,128,256]{3,2,1,0:T(8,128)(2,1)S(1)} all-to-all(bf16[4,2,128,256]{3,2,1,0:T(8,128)(2,1)S(1)} %bitcast.15), channel_id=1, replica_groups=mesh['row'=8,'col'=4] {'col'}, dimensions={0} | all-to-all | bytes 1048576 | tf_op jit(solution)/shard_map/all_to_all | solution.py:372
  73.5 1.5 %shard_map.140 = bf16[512,384]{1,0:T(8,128)(2,1)} custom-call(bf16[4,2,128,256]{3,2,1,0:T(8,128)(2,1)S(1)} %all_to_all.39.signal.strip_grad, bf16[192,256]{1,0:T(8,128)(2,1)S(1)} %copy-done.14, bf16[512,512]{1,0:T(8,128)(2,1)S(1)} %copy-done.8), custom_call_target="tpu_custom_call" | custom-call | bytes 1540096 | tf_op jit(solution)/shard_map/pallas_call | solution.py:30
  75.0 10.3 %all-to-all-start.2 = ((bf16[32,16,384]{2,1,0:T(8,128)(2,1)}), bf16[32,16,384]{2,1,0:T(8,128)(2,1)S(1)}, u32[]{:S(2)}, u32[]{:S(2)}) async-start(bf16[32,16,384]{2,1,0:T(8,128)(2,1)} %bitcast.3), calls=%async_computation.2 | async-start | bytes 786432 | tf_op jit(solution)/shard_map/all_to_all | solution.py:331
  85.3 0.2 reshape.27
  85.6 1.9 %shard_map.141.slope = f32[2,512,192]{2,1,0:T(8,128)S(1)} custom-call(bf16[512,384]{1,0:T(8,128)(2,1)} %bitcast.1.moved, bf16[2,2,192,192]{3,2,1,0:T(8,128)(2,1)S(1)} %bitcast.10, bf16[128,128]{1,0:T(8,128)(2,1)S(1)} %copy-done.13), custom_call_target="tpu_custom_call" | custom-call | bytes 1507328 | tf_op jit(solution)/shard_map/pallas_call | solution.py:30
  87.6 10.5 %all-to-all-done.2 = bf16[32,16,384]{2,1,0:T(8,128)(2,1)S(1)} async-done(((bf16[32,16,384]{2,1,0:T(8,128)(2,1)}), bf16[32,16,384]{2,1,0:T(8,128)(2,1)S(1)}, u32[]{:S(2)}, u32[]{:S(2)}) %all-to-all-start.2) | async-done | bytes 393248 | tf_op jit(solution)/shard_map/all_to_all | solution.py:331
  98.0 1.1 shard_map.142
  99.2 15.5 %all_to_all.40 = bf16[32,16,384]{2,1,0:T(8,128)(2,1)S(1)} all-to-all(bf16[32,16,384]{2,1,0:T(8,128)(2,1)S(1)} %bitcast.13), channel_id=1, replica_groups=mesh['row'=8,'col'=4] {'row','col'}, dimensions={0} | all-to-all | bytes 786432 | tf_op jit(solution)/shard_map/all_to_all | solution.py:331
  114.7 2.0 %shard_map.143 = bf16[2,512,512]{2,1,0:T(8,128)(2,1)} custom-call(bf16[512,384]{1,0:T(8,128)(2,1)S(1)} %bitcast.14, bf16[4,2,128,256]{3,2,1,0:T(8,128)(2,1)S(1)} %all_to_all.39.signal.strip_grad, bf16[512,192]{1,0:T(8,128)(2,1)S(1)} %copy.17.weight.weight_in, bf16[512,256]{1,0:T(8,128)(2,1)S(1)} %copy-done.12, bf16[512,512]{1,0:T(8,128)(2,1)S(1)} %copy-done.11), custom_call_target="tpu_custom_call" | custom-call | bytes 2949120 | tf_op jit(solution)/shard_map/pallas_call | solution.py:30
  (39 shorter events, 0.3 us)
Async XLA Ops:
  0.0 1.0 copy-start
  1.0 1.0 copy-start.2
  2.1 0.7 copy-start.16
  2.8 7.8 %copy-start.20 = (bf16[512,192]{0,1:T(8,128)(2,1)S(1)}, bf16[512,192]{0,1:T(8,128)(2,1)}, u32[]{:S(2)}) copy-start(bf16[512,192]{0,1:T(8,128)(2,1)} %param.20) | copy-start | bytes 589828
  2.8 7.9 %copy-start.8 = (bf16[512,512]{1,0:T(8,128)(2,1)S(1)}, bf16[512,512]{1,0:T(8,128)(2,1)}, u32[]{:S(2)}) copy-start(bf16[512,512]{1,0:T(8,128)(2,1)} %constant.32.clone.table) | copy-start | bytes 1572868
  4.1 17.2 %collective-permute-start = (bf16[13,128,256]{2,1,0:T(8,128)(2,1)}, bf16[13,128,256]{2,1,0:T(8,128)(2,1)S(1)}, u32[]{:S(2)}, u32[]{:S(2)}) collective-permute-start(bf16[13,128,256]{2,1,0:T(8,128)(2,1)} %get-tuple-element.12), channel_id=1, source_target_pairs={{0,4},{4,8},{8,12},{12,16},{16,20},{20,24},{24,28},{1,5},{5,9},{9,... | collective-permute-start | bytes 2555912 | tf_op jit(solution)/shard_map/ppermute | solution.py:343
  8.6 24.3 %collective-permute-start.1 = (bf16[13,128,256]{2,1,0:T(8,128)(2,1)}, bf16[13,128,256]{2,1,0:T(8,128)(2,1)S(1)}, u32[]{:S(2)}, u32[]{:S(2)}) collective-permute-start(bf16[13,128,256]{2,1,0:T(8,128)(2,1)} %get-tuple-element.14), channel_id=1, source_target_pairs={{4,0},{8,4},{12,8},{16,12},{20,16},{24,20},{28,24},{5,1},{9,5},{13... | collective-permute-start | bytes 2555912 | tf_op jit(solution)/shard_map/ppermute | solution.py:344
  10.7 1.2 %copy-start.9 = (bf16[2,512,512]{2,1,0:T(8,128)(2,1)S(1)}, bf16[2,512,512]{2,1,0:T(8,128)(2,1)}, u32[]{:S(2)}) copy-start(bf16[2,512,512]{2,1,0:T(8,128)(2,1)} %signal.1) | copy-start | bytes 3145732
  13.6 26.6 %all-to-all-start = ((bf16[32,16,384]{2,1,0:T(8,128)(2,1)}), bf16[32,16,384]{2,1,0:T(8,128)(2,1)}, u32[]{:S(2)}, u32[]{:S(2)}) async-start(bf16[32,16,384]{2,1,0:T(8,128)(2,1)} %bitcast), calls=%async_computation | async-start | bytes 786432 | tf_op jit(solution)/shard_map/all_to_all | solution.py:331
  21.3 23.9 %copy-start.1 = (bf16[8,128,256]{2,1,0:T(8,128)(2,1)S(1)}, bf16[8,128,256]{2,1,0:T(8,128)(2,1)}, u32[]{:S(2)}) copy-start(bf16[8,128,256]{2,1,0:T(8,128)(2,1)} %features.3) | copy-start | bytes 1572868
  21.3 23.9 %copy-start.3 = (bf16[8,128,256]{2,1,0:T(8,128)(2,1)S(1)}, bf16[8,128,256]{2,1,0:T(8,128)(2,1)}, u32[]{:S(2)}) copy-start(bf16[8,128,256]{2,1,0:T(8,128)(2,1)} %target.3) | copy-start | bytes 1572868
  21.4 11.6 %copy-start.4 = (bf16[13,128,256]{2,1,0:T(8,128)(2,1)}, bf16[13,128,256]{2,1,0:T(8,128)(2,1)S(1)}, u32[]{:S(2)}) copy-start(bf16[13,128,256]{2,1,0:T(8,128)(2,1)S(1)} %collective-permute-done.refs_0_.refs_5_.above) | copy-start | bytes 2555908
  32.9 1.0 copy-start.6
  35.6 5.9 %collective-permute-start.2 = (bf16[43,8,256]{2,1,0:T(8,128)(2,1)}, bf16[43,8,256]{2,1,0:T(8,128)(2,1)S(1)}, u32[]{:S(2)}, u32[]{:S(2)}) collective-permute-start(bf16[43,8,256]{2,1,0:T(8,128)(2,1)} %get-tuple-element.15), channel_id=1, source_target_pairs={{0,1},{1,2},{2,3},{4,5},{5,6},{6,7},{8,9},{9,10},{10,11},{12,13},{... | collective-permute-start | bytes 528392 | tf_op jit(solution)/shard_map/ppermute | solution.py:347
  38.8 6.4 %collective-permute-start.3 = (bf16[43,8,256]{2,1,0:T(8,128)(2,1)}, bf16[43,8,256]{2,1,0:T(8,128)(2,1)S(1)}, u32[]{:S(2)}, u32[]{:S(2)}) collective-permute-start(bf16[43,8,256]{2,1,0:T(8,128)(2,1)} %get-tuple-element.17), channel_id=1, source_target_pairs={{1,0},{2,1},{3,2},{5,4},{6,5},{7,6},{9,8},{10,9},{11,10},{13,12},{... | collective-permute-start | bytes 528392 | tf_op jit(solution)/shard_map/ppermute | solution.py:348
  45.2 1.2 copy-start.5
  46.4 1.2 copy-start.7
  47.5 0.8 copy-start.10
  48.4 1.3 %copy-start.17 = (bf16[3,3,256,256]{3,2,1,0:T(8,128)(2,1)S(1)}, bf16[3,3,256,256]{3,2,1,0:T(8,128)(2,1)}, u32[]{:S(2)}) copy-start(bf16[3,3,256,256]{3,2,1,0:T(8,128)(2,1)} %first.1) | copy-start | bytes 3538948
  49.6 1.3 %copy-start.18 = (bf16[3,3,256,256]{3,2,1,0:T(8,128)(2,1)S(1)}, bf16[3,3,256,256]{3,2,1,0:T(8,128)(2,1)}, u32[]{:S(2)}) copy-start(bf16[3,3,256,256]{3,2,1,0:T(8,128)(2,1)} %second.1) | copy-start | bytes 3538948
  50.9 22.6 %copy-start.14 = (bf16[192,256]{1,0:T(8,128)(2,1)S(1)}, bf16[192,256]{1,0:T(8,128)(2,1)}, u32[]{:S(2)}) copy-start(bf16[192,256]{1,0:T(8,128)(2,1)} %weight.2) | copy-start | bytes 294916
  73.5 11.8 %copy-start.19 = (bf16[384,384]{1,0:T(8,128)(2,1)S(1)}, bf16[384,384]{1,0:T(8,128)(2,1)}, u32[]{:S(2)}) copy-start(bf16[384,384]{1,0:T(8,128)(2,1)} %param.23) | copy-start | bytes 884740
  75.0 10.6 %copy-start.13 = (bf16[128,128]{1,0:T(8,128)(2,1)S(1)}, bf16[128,128]{1,0:T(8,128)(2,1)}, u32[]{:S(2)}) copy-start(bf16[128,128]{1,0:T(8,128)(2,1)} %constant.34.clone.table) | copy-start | bytes 98308
  75.0 23.0 %all-to-all-start.2 = ((bf16[32,16,384]{2,1,0:T(8,128)(2,1)}), bf16[32,16,384]{2,1,0:T(8,128)(2,1)S(1)}, u32[]{:S(2)}, u32[]{:S(2)}) async-start(bf16[32,16,384]{2,1,0:T(8,128)(2,1)} %bitcast.3), calls=%async_computation.2 | async-start | bytes 786432 | tf_op jit(solution)/shard_map/all_to_all | solution.py:331
  85.5 12.5 %copy-start.15 = (bf16[128,128]{1,0:T(8,128)(2,1)S(1)}, bf16[128,128]{1,0:T(8,128)(2,1)}, u32[]{:S(2)}) copy-start(bf16[128,128]{1,0:T(8,128)(2,1)} %constant.33.clone.back_table) | copy-start | bytes 98308
  98.0 16.6 %copy-start.11 = (bf16[512,512]{1,0:T(8,128)(2,1)S(1)}, bf16[512,512]{1,0:T(8,128)(2,1)}, u32[]{:S(2)}) copy-start(bf16[512,512]{1,0:T(8,128)(2,1)} %constant.31.clone.table) | copy-start | bytes 1572868
  98.0 16.6 %copy-start.12 = (bf16[512,256]{1,0:T(8,128)(2,1)S(1)}, bf16[512,256]{1,0:T(8,128)(2,1)}, u32[]{:S(2)}) copy-start(bf16[512,256]{1,0:T(8,128)(2,1)} %weight_local.1) | copy-start | bytes 786436

commit v4 on v3

--- a/solution.py
+++ b/solution.py
@@ -135,8 +135,9 @@
         out[r] = total.astype(jnp.bfloat16)
 
 
-def row_pack_kernel(features, target, mask, down, up):
-    tile_rows, tile_cols, channels = features.shape
+def target_pack_kernel(first, last, mask, down, up, row):
+    tile_rows, tile_cols = mask.shape
+    channels = first.shape[2]
     lanes = jnp.concatenate(
         [
             mask[...].astype(jnp.float32),
@@ -144,17 +145,29 @@
         ],
         axis=0,
     ).T
-    row = jnp.concatenate([lanes] + [jnp.zeros_like(lanes)] * (channels // tile_cols - 1), axis=1)
-    for pack, start in ((down, tile_rows - NEAR), (up, 0)):
-        pack[:tile_rows] = features[...]
-        pack[tile_rows : tile_rows + NEAR] = target[start : start + NEAR]
-        pack[tile_rows + NEAR] = row.astype(jnp.bfloat16)
-
-
-def row_packs(features, target, mask):
-    tile_rows, tile_cols, channels = features.shape
-    pack = jax.ShapeDtypeStruct((tile_rows + NEAR + 1, tile_cols, channels), features.dtype)
-    return vmem_call(row_pack_kernel, [pack, pack], features, target, mask)
+    lanes = jnp.concatenate([lanes] + [jnp.zeros_like(lanes)] * (channels // tile_cols - 1), axis=1)
+    lanes = lanes.astype(jnp.bfloat16)
+    row[0] = lanes
+    for pack, part in ((down, last), (up, first)):
+        pack[:NEAR] = part[...]
+        pack[NEAR] = lanes
+
+
+def target_packs(target, mask):
+    tile_rows, tile_cols, channels = target.shape
+    block = (NEAR, tile_cols, channels)
+    shapes = [jax.ShapeDtypeStruct((n, tile_cols, channels), target.dtype) for n in (NEAR + 1, NEAR + 1, 1)]
+    return pl.pallas_call(
+        target_pack_kernel,
+        grid=(1,),
+        out_shape=shapes,
+        in_specs=[
+            pl.BlockSpec(block, lambda i: (0, 0, 0)),
+            pl.BlockSpec(block, lambda i: (tile_rows // NEAR - 1, 0, 0)),
+            pl.BlockSpec(mask.shape, lambda i: (0, 0)),
+        ],
+        out_specs=[pl.BlockSpec(shape.shape, lambda i: (0, 0, 0)) for shape in shapes],
+    )(target, target, mask)
 
 
 def edge_kernel(*refs):
@@ -167,8 +180,8 @@
             row += ref.shape[0]
 
 
-def edges(above, features, target, mask_row, below):
-    parts = [above, features, target, mask_row, below]
+def edges(*parts):
+    features = parts[1]
     channels = features.shape[2]
     last = features.shape[1] // REACH - 1
 
@@ -189,31 +202,23 @@
     )(*parts, *parts)
 
 
-def conv_kernel(
-    above,
-    features,
-    target,
-    mask_row,
-    below,
-    before,
-    after,
-    ok,
-    first,
-    second,
-    out,
-    wide0,
-    wide1,
-    wide2,
-    wide3,
-    slopes,
-):
+FETCHED = 11
+
+
+def conv_kernel(*refs):
+    ok, out = refs[FETCHED : FETCHED + 2]
+    held = refs[FETCHED + 2 : 2 * FETCHED + 2]
+    wide0, wide1, wide2, wide3, slopes, arrived = refs[2 * FETCHED + 2 :]
+    copies = [pltpu.make_async_copy(refs[i], held[i], arrived.at[i]) for i in range(FETCHED)]
+    for copy in copies:
+        copy.start()
+    before, after, above, features, below, first = held[:6]
+    target_above, target, target_below, mask_row, second = held[6:]
     tile_rows, tile_cols, channels = features.shape
     stride = tile_cols + 2 * REACH
     block = NEAR
     size = block * stride
     tall = tile_rows + 2 * REACH
-    pack = above.shape[0]
-    below_at = pack + 2 * tile_rows + 1
 
     def rows_of(edge, source, row, count=block):
         parts = [before[edge : edge + count], source[row : row + count], after[edge : edge + count]]
@@ -241,10 +246,14 @@
     def inside(row):
         return jnp.concatenate([ok[:, row + i : row + i + 1] for i in range(block)], axis=0)
 
-    sources = ((above, 0), (features, pack), (below, below_at))
-    for part, (source, edge) in enumerate(sources):
+    copies[0].wait()
+    copies[1].wait()
+    for part, source in enumerate((above, features, below)):
+        copies[2 + part].wait()
         for row in range(0, tile_rows, block):
-            put(wide0, part * tile_rows + row, rows_of(edge + row, source, row))
+            at = part * tile_rows + row
+            put(wide0, at, rows_of(at, source, row))
+    copies[5].wait()
     for row in range(0, tall - 4, block):
         pre = conv(wide0, row, first)
         s = 1.0 / (1.0 + jnp.exp(-pre))
@@ -252,14 +261,17 @@
         put(wide1, row, pre * s * kept)
         if NEAR <= row < tall - 4 - NEAR:
             slopes[pl.ds((row - NEAR) * stride, size), :] = s * (1.0 + pre * (1.0 - s)) * kept
+    for copy in copies[6:]:
+        copy.wait()
+    own = tall + NEAR + 1
     masks = [
-        rows_of(pack - 1, above, pack - 1, 1),
-        rows_of(pack + 2 * tile_rows, mask_row, 0, 1),
-        rows_of(below_at + pack - 1, below, pack - 1, 1),
+        rows_of(tall + NEAR, target_above, NEAR, 1),
+        rows_of(own + tile_rows, mask_row, 0, 1),
+        rows_of(own + tile_rows + 1 + NEAR, target_below, NEAR, 1),
     ]
-    goals = [(tile_rows, above, tile_rows, masks[0], tile_rows - NEAR)]
-    goals += [(pack + tile_rows + r, target, r, masks[1], r) for r in range(0, tile_rows, block)]
-    goals += [(below_at + tile_rows, below, tile_rows, masks[2], 0)]
+    goals = [(tall, target_above, 0, masks[0], tile_rows - NEAR)]
+    goals += [(own + r, target, r, masks[1], r) for r in range(0, tile_rows, block)]
+    goals += [(own + tile_rows + 1, target_below, 0, masks[2], 0)]
     for index, (edge, source, at, mask, lane) in enumerate(goals):
         row = index * block
         value = conv(wide1, row, second)
@@ -274,24 +286,27 @@
         out[row : row + block] = value[:, REACH : REACH + tile_cols].astype(jnp.bfloat16)
 
 
-def conv_chain(features, *others):
-    tile_rows, tile_cols, channels = features.shape
+def conv_chain(fetched, ok, shape):
+    tile_rows, tile_cols, channels = shape
     stride = tile_cols + 2 * REACH
-    above, *rest = others
+    held = [pltpu.VMEM(a.shape, a.dtype) for a in fetched]
     wides = [
         pltpu.VMEM(((tile_rows + h) * stride, 3 * channels), jnp.bfloat16) for h in (16, 12, 8, 4)
     ]
+    slopes = pltpu.VMEM(((tile_rows + 4) * stride, channels), jnp.float32)
     pixels = sum((tile_rows + h) * stride for h in (12, 8, 4, 0))
-    return vmem_call(
+    in_vmem = pl.BlockSpec(memory_space=pltpu.VMEM)
+    return pl.pallas_call(
         conv_kernel,
-        [jax.ShapeDtypeStruct(features.shape, jnp.bfloat16)],
-        above,
-        features,
-        *rest,
-        flops=2 * 9 * channels * channels * pixels,
-        scratch=[*wides, pltpu.VMEM(((tile_rows + 4) * stride, channels), jnp.float32)],
-        limit=40,
-    )[0]
+        out_shape=jax.ShapeDtypeStruct(shape, jnp.bfloat16),
+        in_specs=[pl.BlockSpec(memory_space=pltpu.HBM)] * FETCHED + [in_vmem],
+        out_specs=in_vmem,
+        scratch_shapes=[*held, *wides, slopes, pltpu.SemaphoreType.DMA((FETCHED,))],
+        compiler_params=pltpu.CompilerParams(vmem_limit_bytes=48 * MIB),
+        cost_estimate=pl.CostEstimate(
+            flops=2 * 9 * channels * channels * pixels, bytes_accessed=6 * MIB, transcendentals=0
+        ),
+    )(*fetched, ok)
 
 
 def neighbours(axis):
@@ -338,24 +353,24 @@
 
     up, down = neighbours("row")
     left, right = neighbours("col")
-    pack_down, pack_up = row_packs(features, target, hole_mask)
-    mask_row = pack_up[-1:]
-    above = lax.ppermute(pack_down, "row", up)
-    below = lax.ppermute(pack_up, "row", down)
-    above, spatial_cols = lax.optimization_barrier((above, spatial_cols))
-    last, initial = edges(above, features, target, mask_row, below)
+    above = lax.ppermute(features, "row", up)
+    below = lax.ppermute(features, "row", down)
+    pack_down, pack_up, mask_row = target_packs(target, hole_mask)
+    target_above = lax.ppermute(pack_down, "row", up)
+    target_below = lax.ppermute(pack_up, "row", down)
+    last, initial = edges(above, features, below, target_above, target, mask_row, target_below)
     before = lax.ppermute(last, "col", left)
     after = lax.ppermute(initial, "col", right)
-    before, spatial_moved = lax.optimization_barrier((before, spatial_moved))
 
     row0, col0 = lax.axis_index("row") * tile_rows, lax.axis_index("col") * tile_cols
     row_ids = row0 - REACH + jnp.arange(tile_rows + 2 * REACH, dtype=jnp.int32)
     col_ids = col0 - REACH + jnp.arange(tile_cols + 2 * REACH, dtype=jnp.int32)
     ok = ((col_ids >= 0) & (col_ids < width))[:, None] & ((row_ids >= 0) & (row_ids < height))[None]
     ok = ok.astype(jnp.float32)
-    grad_feat = conv_chain(
-        features, above, target, mask_row, below, before, after, ok, kernel_first, kernel_second
-    )
+    fetched = (before, after, above, features, below, kernel_first)
+    fetched += (target_above, target, target_below, mask_row, kernel_second)
+    grad_feat = conv_chain(fetched, ok, features.shape)
+    grad_feat, spatial_moved = lax.optimization_barrier((grad_feat, spatial_moved))
 
     cell_count = height * owned
     mix = weight_mix.reshape(2, half, 2, half).transpose(0, 2, 1, 3)

time: 118 us -> 116 us (0.983)
  waiting for transfers between devices: 27 us -> 19.3 us
  blocking collectives: 28 us -> 33.1 us
  Pallas kernels: 21.3 us -> 25.4 us
  local copies, waits for them, and re-layouts: 12.6 us -> 9.75 us
    pallas_call x0 -> x2, Pallas kernels: none -> 16.6 us  [the longest x1 14.6 us: conv_chain(): pl.pallas_call(conv_kernel, out_shape=jax.ShapeDtypeStruct(shape, jnp.bfl...]
    pallas_call x7 -> x5, Pallas kernels: 19.6 us -> 7.12 us  [vmem_call(): pl.pallas_call(body, out_shape=shapes, in_specs=[spec] * len(operands), o...]
    ppermute x2 -> x4, waiting for transfers between devices: 11.6 us -> 0.99 us  [the longest x1 0.98 us: shards(): target_below = lax.ppermute(pack_up, 'row', down)]
    ppermute x2 -> x4, starting transfers between devices: 6.42 us -> 12.1 us  [the longest x1 4.63 us: shards(): above = lax.ppermute(features, 'row', up)]
    all_to_all x2, starting transfers between devices: 16.6 us -> 11.2 us  [swap(): lax.all_to_all(spectrum, ('row', 'col'), split_axis=0, concat_axis=0, til...]
    all_to_all x1, blocking collectives: 12.5 us -> 17.6 us  [shards(): lax.all_to_all(grad_feat.reshape(col_devices, strip, tile_cols, channels)...]
    ppermute x1, waiting for transfers between devices: 1.28 us -> 3.12 us  [shards(): before = lax.ppermute(last, 'col', left)]
    slice x1 -> x0, local copies, waits for them, and re-layouts: 1.47 us -> none  [shards(): mask_row = pack_up[-1:]]
  transfers between devices with their start and end apart: 6 -> 8, of which waited for: 4 -> 4; matrix products, arithmetic and copies ran while one was open for 2% -> 0% of each run, Pallas kernels for 5% -> 18%
where the time goes in v4:
time: 116 us
  blocking collectives  33.1 us (29%)
  starting transfers between devices  27.8 us (24%)
  Pallas kernels  25.4 us (22%)
  waiting for transfers between devices  19.3 us (17%)
  local copies, waits for them, and re-layouts  9.75 us (8%)
    all_to_all x1, blocking collectives, shards(): lax.all_to_all(grad_feat.reshape(col_devices, strip, tile_cols, channels)...  17.6 us
    all_to_all x1, blocking collectives, swap(): lax.all_to_all(spectrum, ('row', 'col'), split_axis=0, concat_axis=0, til...  15.5 us
    pallas_call x1, Pallas kernels, conv_chain(): pl.pallas_call(conv_kernel, out_shape=jax.ShapeDtypeStruct(shape, jnp.bfl...  14.6 us
    all_to_all x2, waiting for transfers between devices, swap(): lax.all_to_all(spectrum, ('row', 'col'), split_axis=0, concat_axis=0, til...  11.4 us
    all_to_all x2, starting transfers between devices, swap(): lax.all_to_all(spectrum, ('row', 'col'), split_axis=0, concat_axis=0, til...  11.2 us
    unnamed x49, local copies, waits for them, and re-layouts  9.48 us
    pallas_call x5, Pallas kernels, vmem_call(): pl.pallas_call(body, out_shape=shapes, in_specs=[spec] * len(operands), o...  7.12 us
    ppermute x1, starting transfers between devices, shards(): above = lax.ppermute(features, 'row', up)  4.63 us
  transfers between devices with their start and end apart: 8, of which 4 were waited for; matrix products, arithmetic and copies ran while one was open for 0% of the time, Pallas kernels for 18%

profile of v4, /device:TPU:1, one launch (start us, length us, event | category | flops | bytes accessed | tf_op | source)
XLA Modules:
  0.0 115.7 jit_solution(5420781807744773977)
XLA Ops:
  0.0 4.6 %collective-permute-start = (bf16[8,128,256]{2,1,0:T(8,128)(2,1)}, bf16[8,128,256]{2,1,0:T(8,128)(2,1)S(1)}, u32[]{:S(2)}, u32[]{:S(2)}) collective-permute-start(bf16[8,128,256]{2,1,0:T(8,128)(2,1)} %refs_3_.1), channel_id=1, source_target_pairs={{0,4},{4,8},{8,12},{12,16},{16,20},{20,24},{24,28},{1,5},{5,9},{9,... | collective-permute-start | bytes 1572872 | tf_op jit(solution)/shard_map/ppermute | solution.py:356
  4.6 1.9 %collective-permute-start.1 = (bf16[8,128,256]{2,1,0:T(8,128)(2,1)}, bf16[8,128,256]{2,1,0:T(8,128)(2,1)S(1)}, u32[]{:S(2)}, u32[]{:S(2)}) collective-permute-start(bf16[8,128,256]{2,1,0:T(8,128)(2,1)} %refs_3_.1), channel_id=1, source_target_pairs={{4,0},{8,4},{12,8},{16,12},{20,16},{24,20},{28,24},{5,1},{9,5},{13... | collective-permute-start | bytes 1572872 | tf_op jit(solution)/shard_map/ppermute | solution.py:357
  6.6 2.0 %shard_map.136 = (bf16[5,128,256]{2,1,0:T(8,128)(2,1)}, bf16[5,128,256]{2,1,0:T(8,128)(2,1)}, bf16[1,128,256]{2,1,0:T(8,128)(2,1)}) custom-call(bf16[8,128,256]{2,1,0:T(8,128)(2,1)} %refs_7_.1, bf16[8,128,256]{2,1,0:T(8,128)(2,1)} %refs_7_.1, s32[8,128]{1,0:T(8,128)} %mask.1), custom_call_target="tpu_custom_call" | custom-call | tf_op jit(solution)/shard_map/pallas_call | solution.py:160
  8.6 3.6 %collective-permute-start.2 = (bf16[5,128,256]{2,1,0:T(8,128)(2,1)}, bf16[5,128,256]{2,1,0:T(8,128)(2,1)S(1)}, u32[]{:S(2)}, u32[]{:S(2)}) collective-permute-start(bf16[5,128,256]{2,1,0:T(8,128)(2,1)} %get-tuple-element.12), channel_id=1, source_target_pairs={{0,4},{4,8},{8,12},{12,16},{16,20},{20,24},{24,28},{1,5},{5,9},{9,... | collective-permute-start | bytes 983048 | tf_op jit(solution)/shard_map/ppermute | solution.py:359
  12.2 1.9 %collective-permute-start.3 = (bf16[5,128,256]{2,1,0:T(8,128)(2,1)}, bf16[5,128,256]{2,1,0:T(8,128)(2,1)S(1)}, u32[]{:S(2)}, u32[]{:S(2)}) collective-permute-start(bf16[5,128,256]{2,1,0:T(8,128)(2,1)} %get-tuple-element.14), channel_id=1, source_target_pairs={{4,0},{8,4},{12,8},{16,12},{20,16},{24,20},{28,24},{5,1},{9,5},{13... | collective-permute-start | bytes 983048 | tf_op jit(solution)/shard_map/ppermute | solution.py:360
  14.3 1.2 %copy-done.13 = bf16[2,512,512]{2,1,0:T(8,128)(2,1)S(1)} copy-done((bf16[2,512,512]{2,1,0:T(8,128)(2,1)S(1)}, bf16[2,512,512]{2,1,0:T(8,128)(2,1)}, u32[]{:S(2)}) %copy-start.13) | copy-done | bytes 1048600
  15.5 1.6 %shard_map.139 = bf16[512,384]{1,0:T(8,128)(2,1)} custom-call(bf16[2,512,512]{2,1,0:T(8,128)(2,1)S(1)} %copy-done.13, bf16[512,192]{1,0:T(8,128)(2,1)S(1)} %copy.17.weight.weight_in, bf16[512,512]{1,0:T(8,128)(2,1)S(1)} %copy-done.1), custom_call_target="tpu_custom_call" | custom-call | bytes 2162688 | tf_op jit(solution)/shard_map/pallas_call | solution.py:30
  17.1 7.1 %all-to-all-start = ((bf16[32,16,384]{2,1,0:T(8,128)(2,1)}), bf16[32,16,384]{2,1,0:T(8,128)(2,1)S(1)}, u32[]{:S(2)}, u32[]{:S(2)}) async-start(bf16[32,16,384]{2,1,0:T(8,128)(2,1)} %bitcast), calls=%async_computation | async-start | bytes 786432 | tf_op jit(solution)/shard_map/all_to_all | solution.py:346
  24.3 1.0 collective-permute-done.3.refs_6_.refs_13_.refs_8_
  25.3 0.7 copy-done.11
  26.1 0.6 copy-done.5
  26.8 1.7 %shard_map.137 = (bf16[43,8,256]{2,1,0:T(8,128)(2,1)}, bf16[43,8,256]{2,1,0:T(8,128)(2,1)}) custom-call(bf16[8,128,256]{2,1,0:T(8,128)(2,1)} %copy-done.3, bf16[8,128,256]{2,1,0:T(8,128)(2,1)} %refs_3_.1, bf16[8,128,256]{2,1,0:T(8,128)(2,1)} %copy-done.5, bf16[5,128,256]{2,1,0:T(8,128)(2,1)} %copy-done.9, bf16[8,128,256]{2,1,0:T(8,128)(2,1)} %refs_7_.1, ...), custom_call_target="tpu_custom_call" | custom-call | bytes 704512 | tf_op jit(solution)/shard_map/pallas_call | solution.py:193
  28.5 3.2 %collective-permute-start.4 = (bf16[43,8,256]{2,1,0:T(8,128)(2,1)}, bf16[43,8,256]{2,1,0:T(8,128)(2,1)S(1)}, u32[]{:S(2)}, u32[]{:S(2)}) collective-permute-start(bf16[43,8,256]{2,1,0:T(8,128)(2,1)} %get-tuple-element.15), channel_id=1, source_target_pairs={{0,1},{1,2},{2,3},{4,5},{5,6},{6,7},{8,9},{9,10},{10,11},{12,13},{... | collective-permute-start | bytes 528392 | tf_op jit(solution)/shard_map/ppermute | solution.py:362
  31.7 1.3 %collective-permute-start.5 = (bf16[43,8,256]{2,1,0:T(8,128)(2,1)}, bf16[43,8,256]{2,1,0:T(8,128)(2,1)S(1)}, u32[]{:S(2)}, u32[]{:S(2)}) collective-permute-start(bf16[43,8,256]{2,1,0:T(8,128)(2,1)} %get-tuple-element.16), channel_id=1, source_target_pairs={{1,0},{2,1},{3,2},{5,4},{6,5},{7,6},{9,8},{10,9},{11,10},{13,12},{... | collective-permute-start | bytes 528392 | tf_op jit(solution)/shard_map/ppermute | solution.py:363
  33.1 3.1 %collective-permute-done.4.refs_0_ = bf16[43,8,256]{2,1,0:T(8,128)(2,1)S(1)} collective-permute-done((bf16[43,8,256]{2,1,0:T(8,128)(2,1)}, bf16[43,8,256]{2,1,0:T(8,128)(2,1)S(1)}, u32[]{:S(2)}, u32[]{:S(2)}) %collective-permute-start.4) | collective-permute-done | bytes 176160 | tf_op jit(solution)/shard_map/ppermute | solution.py:362
  36.2 3.7 %collective-permute-done.5.refs_1_ = bf16[43,8,256]{2,1,0:T(8,128)(2,1)S(1)} collective-permute-done((bf16[43,8,256]{2,1,0:T(8,128)(2,1)}, bf16[43,8,256]{2,1,0:T(8,128)(2,1)S(1)}, u32[]{:S(2)}, u32[]{:S(2)}) %collective-permute-start.5) | collective-permute-done | bytes 176160 | tf_op jit(solution)/shard_map/ppermute | solution.py:363
  40.0 1.0 copy-done.4
  41.0 1.0 copy-done.6
  42.1 1.0 copy-done.10
  43.0 1.0 copy-done.12
  44.0 1.3 %copy-done.20 = bf16[3,3,256,256]{3,2,1,0:T(8,128)(2,1)S(1)} copy-done((bf16[3,3,256,256]{3,2,1,0:T(8,128)(2,1)S(1)}, bf16[3,3,256,256]{3,2,1,0:T(8,128)(2,1)}, u32[]{:S(2)}) %copy-start.20) | copy-done | bytes 1179672
  45.3 1.3 %copy-done.21 = bf16[3,3,256,256]{3,2,1,0:T(8,128)(2,1)S(1)} copy-done((bf16[3,3,256,256]{3,2,1,0:T(8,128)(2,1)S(1)}, bf16[3,3,256,256]{3,2,1,0:T(8,128)(2,1)}, u32[]{:S(2)}) %copy-start.21) | copy-done | bytes 1179672
  46.6 14.6 %shard_map.138 = bf16[8,128,256]{2,1,0:T(8,128)(2,1)S(1)} custom-call(bf16[43,8,256]{2,1,0:T(8,128)(2,1)S(1)} %collective-permute-done.4.refs_0_, bf16[43,8,256]{2,1,0:T(8,128)(2,1)S(1)} %collective-permute-done.5.refs_1_, bf16[8,128,256]{2,1,0:T(8,128)(2,1)S(1)} %copy-done.4, bf16[8,128,256]{2,1,0:T(8,128)(2,1)S(1)} %copy-done.2, ...), custom_call_target="tpu_custom_call" | custom-call | flops 9512681472 | bytes 6291456 | tf_op jit(solution)/shard_map/pallas_call | solution.py:299
  61.2 17.6 %all_to_all.39.signal.strip_grad = bf16[4,2,128,256]{3,2,1,0:T(8,128)(2,1)S(1)} all-to-all(bf16[4,2,128,256]{3,2,1,0:T(8,128)(2,1)S(1)} %bitcast.16), channel_id=1, replica_groups=mesh['row'=8,'col'=4] {'col'}, dimensions={0} | all-to-all | bytes 1048576 | tf_op jit(solution)/shard_map/all_to_all | solution.py:387
  78.7 1.5 %shard_map.140 = bf16[512,384]{1,0:T(8,128)(2,1)} custom-call(bf16[4,2,128,256]{3,2,1,0:T(8,128)(2,1)S(1)} %all_to_all.39.signal.strip_grad, bf16[192,256]{1,0:T(8,128)(2,1)S(1)} %copy-done.18, bf16[512,512]{1,0:T(8,128)(2,1)S(1)} %copy-done.1), custom_call_target="tpu_custom_call" | custom-call | bytes 1540096 | tf_op jit(solution)/shard_map/pallas_call | solution.py:30
  80.2 4.1 %all-to-all-start.2 = ((bf16[32,16,384]{2,1,0:T(8,128)(2,1)}), bf16[32,16,384]{2,1,0:T(8,128)(2,1)S(1)}, u32[]{:S(2)}, u32[]{:S(2)}) async-start(bf16[32,16,384]{2,1,0:T(8,128)(2,1)} %bitcast.3), calls=%async_computation.2 | async-start | bytes 786432 | tf_op jit(solution)/shard_map/all_to_all | solution.py:346
  84.3 0.2 reshape.27
  84.7 1.0 shard_map.141.slope
  85.6 11.4 %all-to-all-done.2 = bf16[32,16,384]{2,1,0:T(8,128)(2,1)S(1)} async-done(((bf16[32,16,384]{2,1,0:T(8,128)(2,1)}), bf16[32,16,384]{2,1,0:T(8,128)(2,1)S(1)}, u32[]{:S(2)}, u32[]{:S(2)}) %all-to-all-start.2) | async-done | bytes 393248 | tf_op jit(solution)/shard_map/all_to_all | solution.py:346
  97.1 1.1 shard_map.142
  98.2 15.5 %all_to_all.40 = bf16[32,16,384]{2,1,0:T(8,128)(2,1)S(1)} all-to-all(bf16[32,16,384]{2,1,0:T(8,128)(2,1)S(1)} %bitcast.14), channel_id=1, replica_groups=mesh['row'=8,'col'=4] {'row','col'}, dimensions={0} | all-to-all | bytes 786432 | tf_op jit(solution)/shard_map/all_to_all | solution.py:346
  113.7 2.0 %shard_map.143 = bf16[2,512,512]{2,1,0:T(8,128)(2,1)} custom-call(bf16[512,384]{1,0:T(8,128)(2,1)S(1)} %bitcast.15, bf16[4,2,128,256]{3,2,1,0:T(8,128)(2,1)S(1)} %all_to_all.39.signal.strip_grad, bf16[512,192]{1,0:T(8,128)(2,1)S(1)} %copy.17.weight.weight_in, bf16[512,256]{1,0:T(8,128)(2,1)S(1)} %copy-done.16, bf16[512,512]{1,0:T(8,128)(2,1)S(1)} %copy-done.14), custom_call_target="tpu_custom_call" | custom-call | bytes 2949120 | tf_op jit(solution)/shard_map/pallas_call | solution.py:30
  (48 shorter events, 0.5 us)
Async XLA Ops:
  0.0 14.3 %copy-start.1 = (bf16[512,512]{1,0:T(8,128)(2,1)S(1)}, bf16[512,512]{1,0:T(8,128)(2,1)}, u32[]{:S(2)}) copy-start(bf16[512,512]{1,0:T(8,128)(2,1)} %constant.32.clone.table) | copy-start | bytes 1572868
  0.0 14.1 %copy-start.23 = (bf16[512,192]{0,1:T(8,128)(2,1)S(1)}, bf16[512,192]{0,1:T(8,128)(2,1)}, u32[]{:S(2)}) copy-start(bf16[512,192]{0,1:T(8,128)(2,1)} %param.20) | copy-start | bytes 589828
  0.0 25.2 %collective-permute-start = (bf16[8,128,256]{2,1,0:T(8,128)(2,1)}, bf16[8,128,256]{2,1,0:T(8,128)(2,1)S(1)}, u32[]{:S(2)}, u32[]{:S(2)}) collective-permute-start(bf16[8,128,256]{2,1,0:T(8,128)(2,1)} %refs_3_.1), channel_id=1, source_target_pairs={{0,4},{4,8},{8,12},{12,16},{16,20},{20,24},{24,28},{1,5},{5,9},{9,... | collective-permute-start | bytes 1572872 | tf_op jit(solution)/shard_map/ppermute | solution.py:356
  4.6 20.6 %collective-permute-start.1 = (bf16[8,128,256]{2,1,0:T(8,128)(2,1)}, bf16[8,128,256]{2,1,0:T(8,128)(2,1)S(1)}, u32[]{:S(2)}, u32[]{:S(2)}) collective-permute-start(bf16[8,128,256]{2,1,0:T(8,128)(2,1)} %refs_3_.1), channel_id=1, source_target_pairs={{4,0},{8,4},{12,8},{16,12},{20,16},{24,20},{28,24},{5,1},{9,5},{13... | collective-permute-start | bytes 1572872 | tf_op jit(solution)/shard_map/ppermute | solution.py:357
  8.6 15.7 %collective-permute-start.2 = (bf16[5,128,256]{2,1,0:T(8,128)(2,1)}, bf16[5,128,256]{2,1,0:T(8,128)(2,1)S(1)}, u32[]{:S(2)}, u32[]{:S(2)}) collective-permute-start(bf16[5,128,256]{2,1,0:T(8,128)(2,1)} %get-tuple-element.12), channel_id=1, source_target_pairs={{0,4},{4,8},{8,12},{12,16},{16,20},{20,24},{24,28},{1,5},{5,9},{9,... | collective-permute-start | bytes 983048 | tf_op jit(solution)/shard_map/ppermute | solution.py:359
  12.2 13.1 %collective-permute-start.3 = (bf16[5,128,256]{2,1,0:T(8,128)(2,1)}, bf16[5,128,256]{2,1,0:T(8,128)(2,1)S(1)}, u32[]{:S(2)}, u32[]{:S(2)}) collective-permute-start(bf16[5,128,256]{2,1,0:T(8,128)(2,1)} %get-tuple-element.14), channel_id=1, source_target_pairs={{4,0},{8,4},{12,8},{16,12},{20,16},{24,20},{28,24},{5,1},{9,5},{13... | collective-permute-start | bytes 983048 | tf_op jit(solution)/shard_map/ppermute | solution.py:360
  14.3 1.2 %copy-start.13 = (bf16[2,512,512]{2,1,0:T(8,128)(2,1)S(1)}, bf16[2,512,512]{2,1,0:T(8,128)(2,1)}, u32[]{:S(2)}) copy-start(bf16[2,512,512]{2,1,0:T(8,128)(2,1)} %signal.1) | copy-start | bytes 3145732
  17.1 44.1 %all-to-all-start = ((bf16[32,16,384]{2,1,0:T(8,128)(2,1)}), bf16[32,16,384]{2,1,0:T(8,128)(2,1)S(1)}, u32[]{:S(2)}, u32[]{:S(2)}) async-start(bf16[32,16,384]{2,1,0:T(8,128)(2,1)} %bitcast), calls=%async_computation | async-start | bytes 786432 | tf_op jit(solution)/shard_map/all_to_all | solution.py:346
  24.3 1.0 copy-start.9
  25.2 0.7 copy-start.11
  25.3 0.9 copy-start.3
  26.0 0.8 copy-start.5
  26.8 13.2 %copy-start = (bf16[8,128,256]{2,1,0:T(8,128)(2,1)S(1)}, bf16[8,128,256]{2,1,0:T(8,128)(2,1)}, u32[]{:S(2)}) copy-start(bf16[8,128,256]{2,1,0:T(8,128)(2,1)} %refs_7_.1) | copy-start | bytes 1572868
  26.8 13.2 %copy-start.2 = (bf16[8,128,256]{2,1,0:T(8,128)(2,1)S(1)}, bf16[8,128,256]{2,1,0:T(8,128)(2,1)}, u32[]{:S(2)}) copy-start(bf16[8,128,256]{2,1,0:T(8,128)(2,1)} %refs_3_.1) | copy-start | bytes 1572868
  26.8 13.2 %copy-start.15 = (bf16[1,128,256]{2,1,0:T(8,128)(2,1)S(1)}, bf16[1,128,256]{2,1,0:T(8,128)(2,1)}, u32[]{:S(2)}) copy-start(bf16[1,128,256]{2,1,0:T(8,128)(2,1)} %get-tuple-element.13.refs_5_.refs_12_.refs_9_) | copy-start | bytes 196612
  28.5 7.7 %collective-permute-start.4 = (bf16[43,8,256]{2,1,0:T(8,128)(2,1)}, bf16[43,8,256]{2,1,0:T(8,128)(2,1)S(1)}, u32[]{:S(2)}, u32[]{:S(2)}) collective-permute-start(bf16[43,8,256]{2,1,0:T(8,128)(2,1)} %get-tuple-element.15), channel_id=1, source_target_pairs={{0,1},{1,2},{2,3},{4,5},{5,6},{6,7},{8,9},{9,10},{10,11},{12,13},{... | collective-permute-start | bytes 528392 | tf_op jit(solution)/shard_map/ppermute | solution.py:362
  31.7 8.2 %collective-permute-start.5 = (bf16[43,8,256]{2,1,0:T(8,128)(2,1)}, bf16[43,8,256]{2,1,0:T(8,128)(2,1)S(1)}, u32[]{:S(2)}, u32[]{:S(2)}) collective-permute-start(bf16[43,8,256]{2,1,0:T(8,128)(2,1)} %get-tuple-element.16), channel_id=1, source_target_pairs={{1,0},{2,1},{3,2},{5,4},{6,5},{7,6},{9,8},{10,9},{11,10},{13,12},{... | collective-permute-start | bytes 528392 | tf_op jit(solution)/shard_map/ppermute | solution.py:363
  40.0 1.0 copy-start.4
  41.0 1.0 copy-start.6
  42.1 1.0 copy-start.10
  43.0 1.0 copy-start.12
  44.0 1.3 %copy-start.20 = (bf16[3,3,256,256]{3,2,1,0:T(8,128)(2,1)S(1)}, bf16[3,3,256,256]{3,2,1,0:T(8,128)(2,1)}, u32[]{:S(2)}) copy-start(bf16[3,3,256,256]{3,2,1,0:T(8,128)(2,1)} %refs_5_.1) | copy-start | bytes 3538948
  45.3 1.3 %copy-start.21 = (bf16[3,3,256,256]{3,2,1,0:T(8,128)(2,1)S(1)}, bf16[3,3,256,256]{3,2,1,0:T(8,128)(2,1)}, u32[]{:S(2)}) copy-start(bf16[3,3,256,256]{3,2,1,0:T(8,128)(2,1)} %refs_10_.1) | copy-start | bytes 3538948
  46.6 32.2 %copy-start.18 = (bf16[192,256]{1,0:T(8,128)(2,1)S(1)}, bf16[192,256]{1,0:T(8,128)(2,1)}, u32[]{:S(2)}) copy-start(bf16[192,256]{1,0:T(8,128)(2,1)} %weight.2) | copy-start | bytes 294916
  61.2 19.1 %copy-start.7 = (bf16[32,16,384]{2,1,0:T(8,128)(2,1)}, bf16[32,16,384]{2,1,0:T(8,128)(2,1)S(1)}, u32[]{:S(2)}) copy-start(bf16[32,16,384]{2,1,0:T(8,128)(2,1)S(1)} %all-to-all-done) | copy-start | bytes 1179652
  78.7 5.6 %copy-start.22 = (bf16[384,384]{1,0:T(8,128)(2,1)S(1)}, bf16[384,384]{1,0:T(8,128)(2,1)}, u32[]{:S(2)}) copy-start(bf16[384,384]{1,0:T(8,128)(2,1)} %param.23) | copy-start | bytes 884740
  80.2 4.4 %copy-start.17 = (bf16[128,128]{1,0:T(8,128)(2,1)S(1)}, bf16[128,128]{1,0:T(8,128)(2,1)}, u32[]{:S(2)}) copy-start(bf16[128,128]{1,0:T(8,128)(2,1)} %constant.34.clone.table) | copy-start | bytes 98308
  80.2 4.4 %copy-start.8 = (bf16[32,16,384]{2,1,0:T(8,128)(2,1)S(1)}, bf16[32,16,384]{2,1,0:T(8,128)(2,1)}, u32[]{:S(2)}) copy-start(bf16[32,16,384]{2,1,0:T(8,128)(2,1)} %copy-done.7) | copy-start | bytes 1179652
  80.2 16.8 %all-to-all-start.2 = ((bf16[32,16,384]{2,1,0:T(8,128)(2,1)}), bf16[32,16,384]{2,1,0:T(8,128)(2,1)S(1)}, u32[]{:S(2)}, u32[]{:S(2)}) async-start(bf16[32,16,384]{2,1,0:T(8,128)(2,1)} %bitcast.3), calls=%async_computation.2 | async-start | bytes 786432 | tf_op jit(solution)/shard_map/all_to_all | solution.py:346
  84.6 12.5 %copy-start.19 = (bf16[128,128]{1,0:T(8,128)(2,1)S(1)}, bf16[128,128]{1,0:T(8,128)(2,1)}, u32[]{:S(2)}) copy-start(bf16[128,128]{1,0:T(8,128)(2,1)} %constant.33.clone.back_table) | copy-start | bytes 98308
  97.1 16.6 %copy-start.14 = (bf16[512,512]{1,0:T(8,128)(2,1)S(1)}, bf16[512,512]{1,0:T(8,128)(2,1)}, u32[]{:S(2)}) copy-start(bf16[512,512]{1,0:T(8,128)(2,1)} %constant.31.clone.table) | copy-start | bytes 1572868
  97.1 16.6 %copy-start.16 = (bf16[512,256]{1,0:T(8,128)(2,1)S(1)}, bf16[512,256]{1,0:T(8,128)(2,1)}, u32[]{:S(2)}) copy-start(bf16[512,256]{1,0:T(8,128)(2,1)} %weight_local.1) | copy-start | bytes 786436

commit v5 on v4

--- a/solution.py
+++ b/solution.py
@@ -24,7 +24,7 @@
     return lax.dot_general(left, right, (((1,), (1,)), ((), ())), preferred_element_type=jnp.float32)
 
 
-def vmem_call(body, shapes, *operands, flops=0, scratch=(), limit=16):
+def vmem_call(body, shapes, *operands, flops=0, scratch=(), limit=10):
     spec = pl.BlockSpec(memory_space=pltpu.VMEM)
     size = sum(math.prod(a.shape) * a.dtype.itemsize for a in (*operands, *shapes))
     return pl.pallas_call(
@@ -202,18 +202,24 @@
     )(*parts, *parts)
 
 
-FETCHED = 11
-
-
-def conv_kernel(*refs):
-    ok, out = refs[FETCHED : FETCHED + 2]
-    held = refs[FETCHED + 2 : 2 * FETCHED + 2]
-    wide0, wide1, wide2, wide3, slopes, arrived = refs[2 * FETCHED + 2 :]
-    copies = [pltpu.make_async_copy(refs[i], held[i], arrived.at[i]) for i in range(FETCHED)]
-    for copy in copies:
-        copy.start()
-    before, after, above, features, below, first = held[:6]
-    target_above, target, target_below, mask_row, second = held[6:]
+def conv_kernel(
+    before,
+    after,
+    above,
+    features,
+    below,
+    first,
+    target_above,
+    target,
+    target_below,
+    mask_row,
+    second,
+    ok,
+    out,
+    wide_even,
+    wide_odd,
+    slopes,
+):
     tile_rows, tile_cols, channels = features.shape
     stride = tile_cols + 2 * REACH
     block = NEAR
@@ -246,23 +252,17 @@
     def inside(row):
         return jnp.concatenate([ok[:, row + i : row + i + 1] for i in range(block)], axis=0)
 
-    copies[0].wait()
-    copies[1].wait()
     for part, source in enumerate((above, features, below)):
-        copies[2 + part].wait()
         for row in range(0, tile_rows, block):
             at = part * tile_rows + row
-            put(wide0, at, rows_of(at, source, row))
-    copies[5].wait()
+            put(wide_even, at, rows_of(at, source, row))
     for row in range(0, tall - 4, block):
-        pre = conv(wide0, row, first)
+        pre = conv(wide_even, row, first)
         s = 1.0 / (1.0 + jnp.exp(-pre))
         kept = inside(row + 2)
-        put(wide1, row, pre * s * kept)
+        put(wide_odd, row, pre * s * kept)
         if NEAR <= row < tall - 4 - NEAR:
             slopes[pl.ds((row - NEAR) * stride, size), :] = s * (1.0 + pre * (1.0 - s)) * kept
-    for copy in copies[6:]:
-        copy.wait()
     own = tall + NEAR + 1
     masks = [
         rows_of(tall + NEAR, target_above, NEAR, 1),
@@ -274,39 +274,31 @@
     goals += [(own + tile_rows + 1, target_below, 0, masks[2], 0)]
     for index, (edge, source, at, mask, lane) in enumerate(goals):
         row = index * block
-        value = conv(wide1, row, second)
+        value = conv(wide_odd, row, second)
         holes = jnp.concatenate([mask[:, lane + i : lane + i + 1] for i in range(block)], axis=0)
         weight = (1.0 + 2.0 * holes) * inside(row + NEAR)
-        put(wide2, row, weight * (value - rows_of(edge, source, at)))
+        put(wide_even, row, weight * (value - rows_of(edge, source, at)))
     for row in range(0, tile_rows + 4, block):
-        value = conv_adjoint(wide2, row, second)
-        put(wide3, row, value * slopes[pl.ds(row * stride, size), :])
+        value = conv_adjoint(wide_even, row, second)
+        put(wide_odd, row, value * slopes[pl.ds(row * stride, size), :])
     for row in range(0, tile_rows, block):
-        value = conv_adjoint(wide3, row, first).reshape(block, stride, channels)
+        value = conv_adjoint(wide_odd, row, first).reshape(block, stride, channels)
         out[row : row + block] = value[:, REACH : REACH + tile_cols].astype(jnp.bfloat16)
 
 
-def conv_chain(fetched, ok, shape):
+def conv_chain(shape, *operands):
     tile_rows, tile_cols, channels = shape
     stride = tile_cols + 2 * REACH
-    held = [pltpu.VMEM(a.shape, a.dtype) for a in fetched]
-    wides = [
-        pltpu.VMEM(((tile_rows + h) * stride, 3 * channels), jnp.bfloat16) for h in (16, 12, 8, 4)
-    ]
-    slopes = pltpu.VMEM(((tile_rows + 4) * stride, channels), jnp.float32)
+    wides = [pltpu.VMEM(((tile_rows + h) * stride, 3 * channels), jnp.bfloat16) for h in (16, 12)]
     pixels = sum((tile_rows + h) * stride for h in (12, 8, 4, 0))
-    in_vmem = pl.BlockSpec(memory_space=pltpu.VMEM)
-    return pl.pallas_call(
+    return vmem_call(
         conv_kernel,
-        out_shape=jax.ShapeDtypeStruct(shape, jnp.bfloat16),
-        in_specs=[pl.BlockSpec(memory_space=pltpu.HBM)] * FETCHED + [in_vmem],
-        out_specs=in_vmem,
-        scratch_shapes=[*held, *wides, slopes, pltpu.SemaphoreType.DMA((FETCHED,))],
-        compiler_params=pltpu.CompilerParams(vmem_limit_bytes=48 * MIB),
-        cost_estimate=pl.CostEstimate(
-            flops=2 * 9 * channels * channels * pixels, bytes_accessed=6 * MIB, transcendentals=0
-        ),
-    )(*fetched, ok)
+        [jax.ShapeDtypeStruct(shape, jnp.bfloat16)],
+        *operands,
+        flops=2 * 9 * channels * channels * pixels,
+        scratch=[*wides, pltpu.VMEM(((tile_rows + 4) * stride, channels), jnp.float32)],
+        limit=20,
+    )[0]
 
 
 def neighbours(axis):
@@ -349,8 +341,6 @@
     spatial_cols = vmem_call(
         functools.partial(spectrum_kernel, False, col_norm), cells, inputs, weight_in, table
     )[0]
-    spatial_moved = swap(spatial_cols)
-
     up, down = neighbours("row")
     left, right = neighbours("col")
     above = lax.ppermute(features, "row", up)
@@ -361,15 +351,29 @@
     last, initial = edges(above, features, below, target_above, target, mask_row, target_below)
     before = lax.ppermute(last, "col", left)
     after = lax.ppermute(initial, "col", right)
+    after, spatial_cols = lax.optimization_barrier((after, spatial_cols))
+    spatial_moved = swap(spatial_cols)
 
     row0, col0 = lax.axis_index("row") * tile_rows, lax.axis_index("col") * tile_cols
     row_ids = row0 - REACH + jnp.arange(tile_rows + 2 * REACH, dtype=jnp.int32)
     col_ids = col0 - REACH + jnp.arange(tile_cols + 2 * REACH, dtype=jnp.int32)
     ok = ((col_ids >= 0) & (col_ids < width))[:, None] & ((row_ids >= 0) & (row_ids < height))[None]
     ok = ok.astype(jnp.float32)
-    fetched = (before, after, above, features, below, kernel_first)
-    fetched += (target_above, target, target_below, mask_row, kernel_second)
-    grad_feat = conv_chain(fetched, ok, features.shape)
+    grad_feat = conv_chain(
+        features.shape,
+        before,
+        after,
+        above,
+        features,
+        below,
+        kernel_first,
+        target_above,
+        target,
+        target_below,
+        mask_row,
+        kernel_second,
+        ok,
+    )
     grad_feat, spatial_moved = lax.optimization_barrier((grad_feat, spatial_moved))
 
     cell_count = height * owned

time: 116 us -> 115 us (level)
  Pallas kernels: 25.4 us -> 21 us
  local copies, waits for them, and re-layouts: 9.75 us -> 11.3 us
  waiting for transfers between devices: 19.3 us -> 20.8 us
    pallas_call x1 -> x0, Pallas kernels: 14.6 us -> none  [conv_chain(): pl.pallas_call(conv_kernel, out_shape=jax.ShapeDtypeStruct(shape, jnp.bfl...]
    pallas_call x5 -> x6, Pallas kernels: 7.12 us -> 17.3 us  [vmem_call(): pl.pallas_call(body, out_shape=shapes, in_specs=[spec] * len(operands), o...]
    ppermute x1, waiting for transfers between devices: 0.98 us -> 8.39 us  [shards(): target_below = lax.ppermute(pack_up, 'row', down)]
    ppermute x1, waiting for transfers between devices: 3.12 us -> 0.01 us  [shards(): before = lax.ppermute(last, 'col', left)]
    ppermute x1, waiting for transfers between devices: 3.74 us -> 1.01 us  [shards(): after = lax.ppermute(initial, 'col', right)]
    unnamed x49, local copies, waits for them, and re-layouts: 9.48 us -> 11.1 us
    all_to_all x2, starting transfers between devices: 11.2 us -> 9.76 us  [swap(): lax.all_to_all(spectrum, ('row', 'col'), split_axis=0, concat_axis=0, til...]
  transfers between devices with their start and end apart: 8 -> 8, of which waited for: 4 -> 3; matrix products, arithmetic and copies ran while one was open for 0% -> 0% of each run, Pallas kernels for 18% -> 13%
where the time goes in v5:
time: 115 us
  blocking collectives  33.8 us (29%)
  starting transfers between devices  27.1 us (24%)
  Pallas kernels  21 us (18%)
  waiting for transfers between devices  20.8 us (18%)
  local copies, waits for them, and re-layouts  11.3 us (10%)
    all_to_all x1, blocking collectives, shards(): lax.all_to_all(grad_feat.reshape(col_devices, strip, tile_cols, channels)...  18.3 us
    pallas_call x6, Pallas kernels, vmem_call(): pl.pallas_call(body, out_shape=shapes, in_specs=[spec] * len(operands), o...  17.3 us
    all_to_all x1, blocking collectives, swap(): lax.all_to_all(spectrum, ('row', 'col'), split_axis=0, concat_axis=0, til...  15.5 us
    all_to_all x2, waiting for transfers between devices, swap(): lax.all_to_all(spectrum, ('row', 'col'), split_axis=0, concat_axis=0, til...  11.4 us
    unnamed x49, local copies, waits for them, and re-layouts  11.1 us
    all_to_all x2, starting transfers between devices, swap(): lax.all_to_all(spectrum, ('row', 'col'), split_axis=0, concat_axis=0, til...  9.76 us
    ppermute x1, waiting for transfers between devices, shards(): target_below = lax.ppermute(pack_up, 'row', down)  8.39 us
    ppermute x1, starting transfers between devices, shards(): above = lax.ppermute(features, 'row', up)  4.63 us
  transfers between devices with their start and end apart: 8, of which 3 were waited for; matrix products, arithmetic and copies ran while one was open for 0% of the time, Pallas kernels for 13%

profile of v5, /device:TPU:1, one launch (start us, length us, event | category | flops | bytes accessed | tf_op | source)
XLA Modules:
  0.0 114.5 jit_solution(14684611691984823769)
XLA Ops:
  0.0 4.6 %collective-permute-start = (bf16[8,128,256]{2,1,0:T(8,128)(2,1)}, bf16[8,128,256]{2,1,0:T(8,128)(2,1)S(1)}, u32[]{:S(2)}, u32[]{:S(2)}) collective-permute-start(bf16[8,128,256]{2,1,0:T(8,128)(2,1)} %features.1), channel_id=1, source_target_pairs={{0,4},{4,8},{8,12},{12,16},{16,20},{20,24},{24,28},{1,5},{5,9},{9,... | collective-permute-start | bytes 1572872 | tf_op jit(solution)/shard_map/ppermute | solution.py:346
  4.6 1.9 %collective-permute-start.1 = (bf16[8,128,256]{2,1,0:T(8,128)(2,1)}, bf16[8,128,256]{2,1,0:T(8,128)(2,1)S(1)}, u32[]{:S(2)}, u32[]{:S(2)}) collective-permute-start(bf16[8,128,256]{2,1,0:T(8,128)(2,1)} %features.1), channel_id=1, source_target_pairs={{4,0},{8,4},{12,8},{16,12},{20,16},{24,20},{28,24},{5,1},{9,5},{13... | collective-permute-start | bytes 1572872 | tf_op jit(solution)/shard_map/ppermute | solution.py:347
  6.6 2.0 %shard_map.136 = (bf16[5,128,256]{2,1,0:T(8,128)(2,1)}, bf16[5,128,256]{2,1,0:T(8,128)(2,1)}, bf16[1,128,256]{2,1,0:T(8,128)(2,1)}) custom-call(bf16[8,128,256]{2,1,0:T(8,128)(2,1)} %target.1, bf16[8,128,256]{2,1,0:T(8,128)(2,1)} %target.1, s32[8,128]{1,0:T(8,128)} %mask.1), custom_call_target="tpu_custom_call" | custom-call | tf_op jit(solution)/shard_map/pallas_call | solution.py:160
  8.6 3.6 %collective-permute-start.2 = (bf16[5,128,256]{2,1,0:T(8,128)(2,1)}, bf16[5,128,256]{2,1,0:T(8,128)(2,1)S(1)}, u32[]{:S(2)}, u32[]{:S(2)}) collective-permute-start(bf16[5,128,256]{2,1,0:T(8,128)(2,1)} %get-tuple-element.14), channel_id=1, source_target_pairs={{0,4},{4,8},{8,12},{12,16},{16,20},{20,24},{24,28},{1,5},{5,9},{9,... | collective-permute-start | bytes 983048 | tf_op jit(solution)/shard_map/ppermute | solution.py:349
  12.2 1.9 %collective-permute-start.3 = (bf16[5,128,256]{2,1,0:T(8,128)(2,1)}, bf16[5,128,256]{2,1,0:T(8,128)(2,1)S(1)}, u32[]{:S(2)}, u32[]{:S(2)}) collective-permute-start(bf16[5,128,256]{2,1,0:T(8,128)(2,1)} %get-tuple-element.16), channel_id=1, source_target_pairs={{4,0},{8,4},{12,8},{16,12},{20,16},{24,20},{28,24},{5,1},{9,5},{13... | collective-permute-start | bytes 983048 | tf_op jit(solution)/shard_map/ppermute | solution.py:350
  14.3 1.2 %copy-done.11 = bf16[2,512,512]{2,1,0:T(8,128)(2,1)S(1)} copy-done((bf16[2,512,512]{2,1,0:T(8,128)(2,1)S(1)}, bf16[2,512,512]{2,1,0:T(8,128)(2,1)}, u32[]{:S(2)}) %copy-start.11) | copy-done | bytes 1048600
  15.5 1.6 %shard_map.138 = bf16[512,384]{1,0:T(8,128)(2,1)} custom-call(bf16[2,512,512]{2,1,0:T(8,128)(2,1)S(1)} %copy-done.11, bf16[512,192]{1,0:T(8,128)(2,1)S(1)} %copy.17.weight.weight_in, bf16[512,512]{1,0:T(8,128)(2,1)S(1)} %copy-done.1), custom_call_target="tpu_custom_call" | custom-call | bytes 2162688 | tf_op jit(solution)/shard_map/pallas_call | solution.py:30
  17.2 8.4 %collective-permute-done.3.refs_6_.refs_13_.target_below = bf16[5,128,256]{2,1,0:T(8,128)(2,1)S(1)} collective-permute-done((bf16[5,128,256]{2,1,0:T(8,128)(2,1)}, bf16[5,128,256]{2,1,0:T(8,128)(2,1)S(1)}, u32[]{:S(2)}, u32[]{:S(2)}) %collective-permute-start.3) | collective-permute-done | bytes 327712 | tf_op jit(solution)/shard_map/ppermute | solution.py:350
  25.6 0.7 copy-done.9
  26.4 0.6 copy-done.5
  27.1 1.7 %shard_map.137 = (bf16[43,8,256]{2,1,0:T(8,128)(2,1)}, bf16[43,8,256]{2,1,0:T(8,128)(2,1)}) custom-call(bf16[8,128,256]{2,1,0:T(8,128)(2,1)} %copy-done.3, bf16[8,128,256]{2,1,0:T(8,128)(2,1)} %features.1, bf16[8,128,256]{2,1,0:T(8,128)(2,1)} %copy-done.5, bf16[5,128,256]{2,1,0:T(8,128)(2,1)} %copy-done.7, bf16[8,128,256]{2,1,0:T(8,128)(2,1)} %target.1, ...), custom_call_target="tpu_custom_call" | custom-call | bytes 704512 | tf_op jit(solution)/shard_map/pallas_call | solution.py:193
  28.8 1.3 %collective-permute-start.5 = (bf16[43,8,256]{2,1,0:T(8,128)(2,1)}, bf16[43,8,256]{2,1,0:T(8,128)(2,1)S(1)}, u32[]{:S(2)}, u32[]{:S(2)}) collective-permute-start(bf16[43,8,256]{2,1,0:T(8,128)(2,1)} %get-tuple-element.18), channel_id=1, source_target_pairs={{1,0},{2,1},{3,2},{5,4},{6,5},{7,6},{9,8},{10,9},{11,10},{13,12},{... | collective-permute-start | bytes 528392 | tf_op jit(solution)/shard_map/ppermute | solution.py:353
  30.1 4.0 %collective-permute-start.4 = (bf16[43,8,256]{2,1,0:T(8,128)(2,1)}, bf16[43,8,256]{2,1,0:T(8,128)(2,1)S(1)}, u32[]{:S(2)}, u32[]{:S(2)}) collective-permute-start(bf16[43,8,256]{2,1,0:T(8,128)(2,1)} %get-tuple-element.17), channel_id=1, source_target_pairs={{0,1},{1,2},{2,3},{4,5},{5,6},{6,7},{8,9},{9,10},{10,11},{12,13},{... | collective-permute-start | bytes 528392 | tf_op jit(solution)/shard_map/ppermute | solution.py:352
  34.2 1.0 collective-permute-done.5.after
  35.2 4.9 %all-to-all-start = ((bf16[32,16,384]{2,1,0:T(8,128)(2,1)}), bf16[32,16,384]{2,1,0:T(8,128)(2,1)S(1)}, u32[]{:S(2)}, u32[]{:S(2)}) async-start(bf16[32,16,384]{2,1,0:T(8,128)(2,1)} %bitcast), calls=%async_computation | async-start | bytes 786432 | tf_op jit(solution)/shard_map/all_to_all | solution.py:338
  40.2 0.7 copy-done.20
  40.8 1.0 copy-done.4
  41.9 1.0 copy-done.6
  42.9 1.0 copy-done.8
  43.9 1.0 copy-done.10
  44.9 1.3 %copy-done.18 = bf16[3,3,256,256]{3,2,1,0:T(8,128)(2,1)S(1)} copy-done((bf16[3,3,256,256]{3,2,1,0:T(8,128)(2,1)S(1)}, bf16[3,3,256,256]{3,2,1,0:T(8,128)(2,1)}, u32[]{:S(2)}) %copy-start.18) | copy-done | bytes 1179672
  46.1 1.3 %copy-done.19 = bf16[3,3,256,256]{3,2,1,0:T(8,128)(2,1)S(1)} copy-done((bf16[3,3,256,256]{3,2,1,0:T(8,128)(2,1)S(1)}, bf16[3,3,256,256]{3,2,1,0:T(8,128)(2,1)}, u32[]{:S(2)}) %copy-start.19) | copy-done | bytes 1179672
  47.4 0.9 copy-done.21
  48.3 10.2 %shard_map.139 = bf16[8,128,256]{2,1,0:T(8,128)(2,1)S(1)} custom-call(bf16[43,8,256]{2,1,0:T(8,128)(2,1)S(1)} %copy-done.21, bf16[43,8,256]{2,1,0:T(8,128)(2,1)S(1)} %collective-permute-done.5.after, bf16[8,128,256]{2,1,0:T(8,128)(2,1)S(1)} %copy-done.4, bf16[8,128,256]{2,1,0:T(8,128)(2,1)S(1)} %copy-done.2, bf16[8,128,256]{2,1,0:T(8,128)(2,1)S(1)} %copy-done.6, ...), custom_call_target="tpu_custom_call" | custom-call | flops 9512681472 | bytes 6067712 | tf_op jit(solution)/shard_map/pallas_call | solution.py:30
  58.5 18.3 %all_to_all.39.signal.strip_grad = bf16[4,2,128,256]{3,2,1,0:T(8,128)(2,1)S(1)} all-to-all(bf16[4,2,128,256]{3,2,1,0:T(8,128)(2,1)S(1)} %bitcast.16), channel_id=1, replica_groups=mesh['row'=8,'col'=4] {'col'}, dimensions={0} | all-to-all | bytes 1048576 | tf_op jit(solution)/shard_map/all_to_all | solution.py:391
  76.9 1.5 %shard_map.140 = bf16[512,384]{1,0:T(8,128)(2,1)} custom-call(bf16[4,2,128,256]{3,2,1,0:T(8,128)(2,1)S(1)} %all_to_all.39.signal.strip_grad, bf16[192,256]{1,0:T(8,128)(2,1)S(1)} %copy-done.16, bf16[512,512]{1,0:T(8,128)(2,1)S(1)} %copy-done.1), custom_call_target="tpu_custom_call" | custom-call | bytes 1540096 | tf_op jit(solution)/shard_map/pallas_call | solution.py:30
  78.3 4.8 %all-to-all-start.2 = ((bf16[32,16,384]{2,1,0:T(8,128)(2,1)}), bf16[32,16,384]{2,1,0:T(8,128)(2,1)S(1)}, u32[]{:S(2)}, u32[]{:S(2)}) async-start(bf16[32,16,384]{2,1,0:T(8,128)(2,1)} %bitcast.3), calls=%async_computation.2 | async-start | bytes 786432 | tf_op jit(solution)/shard_map/all_to_all | solution.py:338
  83.5 1.0 shard_map.141.slope
  84.5 11.4 %all-to-all-done.2 = bf16[32,16,384]{2,1,0:T(8,128)(2,1)S(1)} async-done(((bf16[32,16,384]{2,1,0:T(8,128)(2,1)}), bf16[32,16,384]{2,1,0:T(8,128)(2,1)S(1)}, u32[]{:S(2)}, u32[]{:S(2)}) %all-to-all-start.2) | async-done | bytes 393248 | tf_op jit(solution)/shard_map/all_to_all | solution.py:338
  95.9 1.1 shard_map.142
  97.1 15.5 %all_to_all.40 = bf16[32,16,384]{2,1,0:T(8,128)(2,1)S(1)} all-to-all(bf16[32,16,384]{2,1,0:T(8,128)(2,1)S(1)} %bitcast.14), channel_id=1, replica_groups=mesh['row'=8,'col'=4] {'row','col'}, dimensions={0} | all-to-all | bytes 786432 | tf_op jit(solution)/shard_map/all_to_all | solution.py:338
  112.6 2.0 %shard_map.143 = bf16[2,512,512]{2,1,0:T(8,128)(2,1)} custom-call(bf16[512,384]{1,0:T(8,128)(2,1)S(1)} %bitcast.15, bf16[4,2,128,256]{3,2,1,0:T(8,128)(2,1)S(1)} %all_to_all.39.signal.strip_grad, bf16[512,192]{1,0:T(8,128)(2,1)S(1)} %copy.17.weight.weight_in, bf16[512,256]{1,0:T(8,128)(2,1)S(1)} %copy-done.14, bf16[512,512]{1,0:T(8,128)(2,1)S(1)} %copy-done.12), custom_call_target="tpu_custom_call" | custom-call | bytes 2949120 | tf_op jit(solution)/shard_map/pallas_call | solution.py:30
  (48 shorter events, 0.8 us)
Async XLA Ops:
  0.0 14.3 %copy-start.1 = (bf16[512,512]{1,0:T(8,128)(2,1)S(1)}, bf16[512,512]{1,0:T(8,128)(2,1)}, u32[]{:S(2)}) copy-start(bf16[512,512]{1,0:T(8,128)(2,1)} %constant.32.clone.table) | copy-start | bytes 1572868
  0.0 14.1 %copy-start.23 = (bf16[512,192]{0,1:T(8,128)(2,1)S(1)}, bf16[512,192]{0,1:T(8,128)(2,1)}, u32[]{:S(2)}) copy-start(bf16[512,192]{0,1:T(8,128)(2,1)} %param.20) | copy-start | bytes 589828
  0.0 25.5 %collective-permute-start = (bf16[8,128,256]{2,1,0:T(8,128)(2,1)}, bf16[8,128,256]{2,1,0:T(8,128)(2,1)S(1)}, u32[]{:S(2)}, u32[]{:S(2)}) collective-permute-start(bf16[8,128,256]{2,1,0:T(8,128)(2,1)} %features.1), channel_id=1, source_target_pairs={{0,4},{4,8},{8,12},{12,16},{16,20},{20,24},{24,28},{1,5},{5,9},{9,... | collective-permute-start | bytes 1572872 | tf_op jit(solution)/shard_map/ppermute | solution.py:346
  4.6 20.9 %collective-permute-start.1 = (bf16[8,128,256]{2,1,0:T(8,128)(2,1)}, bf16[8,128,256]{2,1,0:T(8,128)(2,1)S(1)}, u32[]{:S(2)}, u32[]{:S(2)}) collective-permute-start(bf16[8,128,256]{2,1,0:T(8,128)(2,1)} %features.1), channel_id=1, source_target_pairs={{4,0},{8,4},{12,8},{16,12},{20,16},{24,20},{28,24},{5,1},{9,5},{13... | collective-permute-start | bytes 1572872 | tf_op jit(solution)/shard_map/ppermute | solution.py:347
  8.6 8.6 %collective-permute-start.2 = (bf16[5,128,256]{2,1,0:T(8,128)(2,1)}, bf16[5,128,256]{2,1,0:T(8,128)(2,1)S(1)}, u32[]{:S(2)}, u32[]{:S(2)}) collective-permute-start(bf16[5,128,256]{2,1,0:T(8,128)(2,1)} %get-tuple-element.14), channel_id=1, source_target_pairs={{0,4},{4,8},{8,12},{12,16},{16,20},{20,24},{24,28},{1,5},{5,9},{9,... | collective-permute-start | bytes 983048 | tf_op jit(solution)/shard_map/ppermute | solution.py:349
  12.2 13.4 %collective-permute-start.3 = (bf16[5,128,256]{2,1,0:T(8,128)(2,1)}, bf16[5,128,256]{2,1,0:T(8,128)(2,1)S(1)}, u32[]{:S(2)}, u32[]{:S(2)}) collective-permute-start(bf16[5,128,256]{2,1,0:T(8,128)(2,1)} %get-tuple-element.16), channel_id=1, source_target_pairs={{4,0},{8,4},{12,8},{16,12},{20,16},{24,20},{28,24},{5,1},{9,5},{13... | collective-permute-start | bytes 983048 | tf_op jit(solution)/shard_map/ppermute | solution.py:350
  14.3 1.2 %copy-start.11 = (bf16[2,512,512]{2,1,0:T(8,128)(2,1)S(1)}, bf16[2,512,512]{2,1,0:T(8,128)(2,1)}, u32[]{:S(2)}) copy-start(bf16[2,512,512]{2,1,0:T(8,128)(2,1)} %signal.1) | copy-start | bytes 3145732
  17.1 9.1 %copy-start.7 = (bf16[5,128,256]{2,1,0:T(8,128)(2,1)}, bf16[5,128,256]{2,1,0:T(8,128)(2,1)S(1)}, u32[]{:S(2)}) copy-start(bf16[5,128,256]{2,1,0:T(8,128)(2,1)S(1)} %collective-permute-done.2.refs_3_.refs_10_.target_above) | copy-start | bytes 983044
  25.5 0.7 copy-start.9
  25.5 0.9 copy-start.3
  26.3 0.8 copy-start.5
  27.1 13.8 %copy-start = (bf16[8,128,256]{2,1,0:T(8,128)(2,1)S(1)}, bf16[8,128,256]{2,1,0:T(8,128)(2,1)}, u32[]{:S(2)}) copy-start(bf16[8,128,256]{2,1,0:T(8,128)(2,1)} %target.1) | copy-start | bytes 1572868
  27.1 13.8 %copy-start.2 = (bf16[8,128,256]{2,1,0:T(8,128)(2,1)S(1)}, bf16[8,128,256]{2,1,0:T(8,128)(2,1)}, u32[]{:S(2)}) copy-start(bf16[8,128,256]{2,1,0:T(8,128)(2,1)} %features.1) | copy-start | bytes 1572868
  27.1 13.8 %copy-start.13 = (bf16[1,128,256]{2,1,0:T(8,128)(2,1)S(1)}, bf16[1,128,256]{2,1,0:T(8,128)(2,1)}, u32[]{:S(2)}) copy-start(bf16[1,128,256]{2,1,0:T(8,128)(2,1)} %get-tuple-element.15.refs_5_.refs_12_.mask_row) | copy-start | bytes 196612
  28.8 6.4 %collective-permute-start.5 = (bf16[43,8,256]{2,1,0:T(8,128)(2,1)}, bf16[43,8,256]{2,1,0:T(8,128)(2,1)S(1)}, u32[]{:S(2)}, u32[]{:S(2)}) collective-permute-start(bf16[43,8,256]{2,1,0:T(8,128)(2,1)} %get-tuple-element.18), channel_id=1, source_target_pairs={{1,0},{2,1},{3,2},{5,4},{6,5},{7,6},{9,8},{10,9},{11,10},{13,12},{... | collective-permute-start | bytes 528392 | tf_op jit(solution)/shard_map/ppermute | solution.py:353
  30.1 10.0 %collective-permute-start.4 = (bf16[43,8,256]{2,1,0:T(8,128)(2,1)}, bf16[43,8,256]{2,1,0:T(8,128)(2,1)S(1)}, u32[]{:S(2)}, u32[]{:S(2)}) collective-permute-start(bf16[43,8,256]{2,1,0:T(8,128)(2,1)} %get-tuple-element.17), channel_id=1, source_target_pairs={{0,1},{1,2},{2,3},{4,5},{5,6},{6,7},{8,9},{9,10},{10,11},{12,13},{... | collective-permute-start | bytes 528392 | tf_op jit(solution)/shard_map/ppermute | solution.py:352
  35.2 23.3 %all-to-all-start = ((bf16[32,16,384]{2,1,0:T(8,128)(2,1)}), bf16[32,16,384]{2,1,0:T(8,128)(2,1)S(1)}, u32[]{:S(2)}, u32[]{:S(2)}) async-start(bf16[32,16,384]{2,1,0:T(8,128)(2,1)} %bitcast), calls=%async_computation | async-start | bytes 786432 | tf_op jit(solution)/shard_map/all_to_all | solution.py:338
  40.2 0.7 copy-start.20
  40.8 1.0 copy-start.4
  41.9 1.0 copy-start.6
  42.9 1.0 copy-start.8
  43.9 1.0 copy-start.10
  44.9 1.3 %copy-start.18 = (bf16[3,3,256,256]{3,2,1,0:T(8,128)(2,1)S(1)}, bf16[3,3,256,256]{3,2,1,0:T(8,128)(2,1)}, u32[]{:S(2)}) copy-start(bf16[3,3,256,256]{3,2,1,0:T(8,128)(2,1)} %first.3) | copy-start | bytes 3538948
  46.1 1.3 %copy-start.19 = (bf16[3,3,256,256]{3,2,1,0:T(8,128)(2,1)S(1)}, bf16[3,3,256,256]{3,2,1,0:T(8,128)(2,1)}, u32[]{:S(2)}) copy-start(bf16[3,3,256,256]{3,2,1,0:T(8,128)(2,1)} %second.1) | copy-start | bytes 3538948
  47.4 0.9 copy-start.21
  48.3 28.5 %copy-start.16 = (bf16[192,256]{1,0:T(8,128)(2,1)S(1)}, bf16[192,256]{1,0:T(8,128)(2,1)}, u32[]{:S(2)}) copy-start(bf16[192,256]{1,0:T(8,128)(2,1)} %weight.2) | copy-start | bytes 294916
  76.9 6.3 %copy-start.22 = (bf16[384,384]{1,0:T(8,128)(2,1)S(1)}, bf16[384,384]{1,0:T(8,128)(2,1)}, u32[]{:S(2)}) copy-start(bf16[384,384]{1,0:T(8,128)(2,1)} %param.23) | copy-start | bytes 884740
  78.3 5.2 %copy-start.15 = (bf16[128,128]{1,0:T(8,128)(2,1)S(1)}, bf16[128,128]{1,0:T(8,128)(2,1)}, u32[]{:S(2)}) copy-start(bf16[128,128]{1,0:T(8,128)(2,1)} %constant.34.clone.table) | copy-start | bytes 98308
  78.3 17.6 %all-to-all-start.2 = ((bf16[32,16,384]{2,1,0:T(8,128)(2,1)}), bf16[32,16,384]{2,1,0:T(8,128)(2,1)S(1)}, u32[]{:S(2)}, u32[]{:S(2)}) async-start(bf16[32,16,384]{2,1,0:T(8,128)(2,1)} %bitcast.3), calls=%async_computation.2 | async-start | bytes 786432 | tf_op jit(solution)/shard_map/all_to_all | solution.py:338
  83.4 12.5 %copy-start.17 = (bf16[128,128]{1,0:T(8,128)(2,1)S(1)}, bf16[128,128]{1,0:T(8,128)(2,1)}, u32[]{:S(2)}) copy-start(bf16[128,128]{1,0:T(8,128)(2,1)} %constant.33.clone.back_table) | copy-start | bytes 98308
  95.9 16.6 %copy-start.12 = (bf16[512,512]{1,0:T(8,128)(2,1)S(1)}, bf16[512,512]{1,0:T(8,128)(2,1)}, u32[]{:S(2)}) copy-start(bf16[512,512]{1,0:T(8,128)(2,1)} %constant.31.clone.table) | copy-start | bytes 1572868
  95.9 16.6 %copy-start.14 = (bf16[512,256]{1,0:T(8,128)(2,1)S(1)}, bf16[512,256]{1,0:T(8,128)(2,1)}, u32[]{:S(2)}) copy-start(bf16[512,256]{1,0:T(8,128)(2,1)} %weight_local.1) | copy-start | bytes 786436

commit v6 on v5

--- a/solution.py
+++ b/solution.py
@@ -65,15 +65,24 @@
     return jnp.concatenate([signal[block, r] for block in range(signal.shape[0])], axis=0)
 
 
-def spectrum_kernel(transposed, norm, signal, weight, table, out):
-    product = dot_t if transposed else dot
+def strip_spectrum(signal, product, weight, table, norm):
     count = signal.shape[0 if len(signal.shape) == 3 else 1]
     rows = [product(strip_row(signal, r), weight[...]).astype(jnp.bfloat16) for r in range(count)]
-    out[...] = (dot(table[...], jnp.concatenate(rows, axis=1)) * norm).astype(jnp.bfloat16)
+    return (dot(table[...], jnp.concatenate(rows, axis=1)) * norm).astype(jnp.bfloat16)
+
+
+def spatial_kernel(norm, signal, weight, table, out):
+    out[...] = strip_spectrum(signal, dot, weight, table, norm)
+
+
+def grad_kernel(norm, signal, weight, table, spatial, out):
+    width = spatial.shape[1]
+    out[:, :width] = spatial[...]
+    out[:, width:] = strip_spectrum(signal, dot_t, weight, table, norm)
 
 
 def row_spectrum(moved, table, wide, norm, owned, devices):
-    groups = moved.shape[1] // LANES
+    groups = wide.shape[0]
     for g in range(groups):
         wide[g] = moved[:, g * LANES : (g + 1) * LANES].astype(jnp.float32)
     strip = table.shape[1] // (2 * devices)
@@ -92,23 +101,21 @@
     return jnp.concatenate(real, axis=0), jnp.concatenate(imag, axis=0)
 
 
-def slope_kernel(norm, owned, devices, moved, mix, table, out, wide):
-    parts = row_spectrum(moved, table, wide, norm, owned, devices)
+def mix_kernel(norm, owned, devices, moved, mix, table, back_table, out, wide, wide_grad):
+    width = out.shape[1]
+    parts = row_spectrum(moved.at[:, :width], table, wide, norm, owned, devices)
     real, imag = [part.astype(jnp.bfloat16) for part in parts]
-    for part in range(2):
+    grads = row_spectrum(moved.at[:, width:], table, wide_grad, norm, owned, devices)
+    mixed = []
+    for part, grad in enumerate(grads):
         pre = dot(real, mix[0, part]) + dot(imag, mix[1, part])
         s = 1.0 / (1.0 + jnp.exp(-pre))
-        out[part] = s * (1.0 + pre * (1.0 - s))
-
-
-def mix_kernel(norm, owned, devices, moved, slope, mix, table, back_table, out, wide):
-    real, imag = row_spectrum(moved, table, wide, norm, owned, devices)
-    real = (real * slope[0]).astype(jnp.bfloat16)
-    imag = (imag * slope[1]).astype(jnp.bfloat16)
-    back = [(dot_t(real, mix[p, 0]) + dot_t(imag, mix[p, 1])).astype(jnp.bfloat16) for p in range(2)]
+        mixed.append((grad * (s * (1.0 + pre * (1.0 - s)))).astype(jnp.bfloat16))
+    back = [dot_t(mixed[0], mix[p, 0]) + dot_t(mixed[1], mix[p, 1]) for p in range(2)]
+    back = [part.astype(jnp.bfloat16) for part in back]
     height = table.shape[0] // 2
     strip = height // devices
-    groups = out.shape[1] // LANES
+    groups = wide.shape[0]
     for freq in range(owned):
         cells = slice(freq * height, (freq + 1) * height)
         stacked = jnp.concatenate([back[0][cells], back[1][cells]], axis=0)
@@ -167,6 +174,7 @@
             pl.BlockSpec(mask.shape, lambda i: (0, 0)),
         ],
         out_specs=[pl.BlockSpec(shape.shape, lambda i: (0, 0, 0)) for shape in shapes],
+        compiler_params=pltpu.CompilerParams(vmem_limit_bytes=6 * MIB),
     )(target, target, mask)
 
 
@@ -196,6 +204,7 @@
         out_shape=[shape, shape],
         in_specs=specs(last) + specs(0),
         out_specs=[pl.BlockSpec(shape.shape, lambda i: (0, 0, 0))] * 2,
+        compiler_params=pltpu.CompilerParams(vmem_limit_bytes=6 * MIB),
         cost_estimate=pl.CostEstimate(
             flops=0, bytes_accessed=8 * rows * REACH * channels, transcendentals=0
         ),
@@ -339,7 +348,7 @@
 
     cells = [jax.ShapeDtypeStruct((width, strip * half), bf16)]
     spatial_cols = vmem_call(
-        functools.partial(spectrum_kernel, False, col_norm), cells, inputs, weight_in, table
+        functools.partial(spatial_kernel, col_norm), cells, inputs, weight_in, table
     )[0]
     up, down = neighbours("row")
     left, right = neighbours("col")
@@ -348,11 +357,10 @@
     pack_down, pack_up, mask_row = target_packs(target, hole_mask)
     target_above = lax.ppermute(pack_down, "row", up)
     target_below = lax.ppermute(pack_up, "row", down)
+    above, spatial_cols = lax.optimization_barrier((above, spatial_cols))
     last, initial = edges(above, features, below, target_above, target, mask_row, target_below)
     before = lax.ppermute(last, "col", left)
     after = lax.ppermute(initial, "col", right)
-    after, spatial_cols = lax.optimization_barrier((after, spatial_cols))
-    spatial_moved = swap(spatial_cols)
 
     row0, col0 = lax.axis_index("row") * tile_rows, lax.axis_index("col") * tile_cols
     row_ids = row0 - REACH + jnp.arange(tile_rows + 2 * REACH, dtype=jnp.int32)
@@ -374,36 +382,28 @@
         kernel_second,
         ok,
     )
-    grad_feat, spatial_moved = lax.optimization_barrier((grad_feat, spatial_moved))
-
-    cell_count = height * owned
-    mix = weight_mix.reshape(2, half, 2, half).transpose(0, 2, 1, 3)
-    wide = [pltpu.VMEM((strip * half // LANES, width, LANES), jnp.float32)]
-    slope = vmem_call(
-        functools.partial(slope_kernel, row_norm, owned, devices),
-        [jax.ShapeDtypeStruct((2, cell_count, half), jnp.float32)],
-        spatial_moved,
-        mix,
-        row_table,
-        scratch=wide,
-    )[0]
 
     strip_grad = lax.all_to_all(
         grad_feat.reshape(col_devices, strip, tile_cols, channels), "col", split_axis=0, concat_axis=0
     )
-    grad_cols = vmem_call(
-        functools.partial(spectrum_kernel, True, col_norm), cells, strip_grad, weight_out, table
+    both_cols = vmem_call(
+        functools.partial(grad_kernel, col_norm),
+        [jax.ShapeDtypeStruct((width, 2 * strip * half), bf16)],
+        strip_grad,
+        weight_out,
+        table,
+        spatial_cols,
     )[0]
-    grad_moved = swap(grad_cols)
+    mix = weight_mix.reshape(2, half, 2, half).transpose(0, 2, 1, 3)
+    wide = pltpu.VMEM((strip * half // LANES, width, LANES), jnp.float32)
     grad_rows = vmem_call(
         functools.partial(mix_kernel, row_norm, owned, devices),
         cells,
-        grad_moved,
-        slope,
+        swap(both_cols),
         mix,
         row_table,
         row_back,
-        scratch=wide,
+        scratch=[wide, wide],
     )[0]
     returned = swap(grad_rows)
     return vmem_call(

time: 115 us -> 112 us (0.974)
  waiting for transfers between devices: 20.8 us -> 33.4 us
  local copies, waits for them, and re-layouts: 11.3 us -> 3.49 us
  blocking collectives: 33.8 us -> 28.2 us
  Pallas kernels: 21 us -> 19.5 us
    all_to_all x2 -> x1, waiting for transfers between devices: 11.4 us -> 20.5 us  [swap(): lax.all_to_all(spectrum, ('row', 'col'), split_axis=0, concat_axis=0, til...]
    unnamed x49 -> x31, local copies, waits for them, and re-layouts: 11.1 us -> 3.21 us
    all_to_all x1, blocking collectives: 18.3 us -> 12.5 us  [shards(): lax.all_to_all(grad_feat.reshape(col_devices, strip, tile_cols, channels)...]
    ppermute x1, waiting for transfers between devices: 1.01 us -> 3.83 us  [shards(): after = lax.ppermute(initial, 'col', right)]
    all_to_all x2 -> x1, starting transfers between devices: 9.76 us -> 10.2 us  [swap(): lax.all_to_all(spectrum, ('row', 'col'), split_axis=0, concat_axis=0, til...]
    pallas_call x6 -> x5, Pallas kernels: 17.3 us -> 17.6 us  [vmem_call(): pl.pallas_call(body, out_shape=shapes, in_specs=[spec] * len(operands), o...]
  transfers between devices with their start and end apart: 8 -> 7, of which waited for: 3 -> 4; matrix products, arithmetic and copies ran while one was open for 0% -> 0% of each run, Pallas kernels for 13% -> 2%
where the time goes in v6:
time: 112 us
  waiting for transfers between devices  33.4 us (30%)
  blocking collectives  28.2 us (25%)
  starting transfers between devices  26.7 us (24%)
  Pallas kernels  19.5 us (17%)
  local copies, waits for them, and re-layouts  3.49 us (3%)
    all_to_all x1, waiting for transfers between devices, swap(): lax.all_to_all(spectrum, ('row', 'col'), split_axis=0, concat_axis=0, til...  20.5 us
    pallas_call x5, Pallas kernels, vmem_call(): pl.pallas_call(body, out_shape=shapes, in_specs=[spec] * len(operands), o...  17.6 us
    all_to_all x1, blocking collectives, swap(): lax.all_to_all(spectrum, ('row', 'col'), split_axis=0, concat_axis=0, til...  15.7 us
    all_to_all x1, blocking collectives, shards(): lax.all_to_all(grad_feat.reshape(col_devices, strip, tile_cols, channels)...  12.5 us
    all_to_all x1, starting transfers between devices, swap(): lax.all_to_all(spectrum, ('row', 'col'), split_axis=0, concat_axis=0, til...  10.2 us
    ppermute x1, waiting for transfers between devices, shards(): target_below = lax.ppermute(pack_up, 'row', down)  8.12 us
    ppermute x1, starting transfers between devices, shards(): above = lax.ppermute(features, 'row', up)  4.5 us
    ppermute x1, waiting for transfers between devices, shards(): after = lax.ppermute(initial, 'col', right)  3.83 us
  transfers between devices with their start and end apart: 7, of which 4 were waited for; matrix products, arithmetic and copies ran while one was open for 0% of the time, Pallas kernels for 2%

profile of v6, /device:TPU:1, one launch (start us, length us, event | category | flops | bytes accessed | tf_op | source)
XLA Modules:
  0.0 111.6 jit_solution(697440600206561485)
XLA Ops:
  0.0 4.5 %collective-permute-start = (bf16[8,128,256]{2,1,0:T(8,128)(2,1)}, bf16[8,128,256]{2,1,0:T(8,128)(2,1)S(1)}, u32[]{:S(2)}, u32[]{:S(2)}) collective-permute-start(bf16[8,128,256]{2,1,0:T(8,128)(2,1)} %features.1), channel_id=1, source_target_pairs={{0,4},{4,8},{8,12},{12,16},{16,20},{20,24},{24,28},{1,5},{5,9},{9,... | collective-permute-start | bytes 1572872 | tf_op jit(solution)/shard_map/ppermute | solution.py:355
  4.5 1.9 %collective-permute-start.1 = (bf16[8,128,256]{2,1,0:T(8,128)(2,1)}, bf16[8,128,256]{2,1,0:T(8,128)(2,1)S(1)}, u32[]{:S(2)}, u32[]{:S(2)}) collective-permute-start(bf16[8,128,256]{2,1,0:T(8,128)(2,1)} %features.1), channel_id=1, source_target_pairs={{4,0},{8,4},{12,8},{16,12},{20,16},{24,20},{28,24},{5,1},{9,5},{13... | collective-permute-start | bytes 1572872 | tf_op jit(solution)/shard_map/ppermute | solution.py:356
  6.4 0.0 copy-start
  6.5 1.0 copy-done
  7.5 0.7 copy-done.10
  8.2 0.9 shard_map.137
  9.1 3.6 %collective-permute-start.2 = (bf16[5,128,256]{2,1,0:T(8,128)(2,1)}, bf16[5,128,256]{2,1,0:T(8,128)(2,1)S(1)}, u32[]{:S(2)}, u32[]{:S(2)}) collective-permute-start(bf16[5,128,256]{2,1,0:T(8,128)(2,1)} %get-tuple-element.13), channel_id=1, source_target_pairs={{0,4},{4,8},{8,12},{12,16},{16,20},{20,24},{24,28},{1,5},{5,9},{9,... | collective-permute-start | bytes 983048 | tf_op jit(solution)/shard_map/ppermute | solution.py:358
  12.8 1.9 %collective-permute-start.3 = (bf16[5,128,256]{2,1,0:T(8,128)(2,1)}, bf16[5,128,256]{2,1,0:T(8,128)(2,1)}, u32[]{:S(2)}, u32[]{:S(2)}) collective-permute-start(bf16[5,128,256]{2,1,0:T(8,128)(2,1)} %get-tuple-element.15), channel_id=1, source_target_pairs={{4,0},{8,4},{12,8},{16,12},{20,16},{24,20},{28,24},{5,1},{9,5},{13... | collective-permute-start | bytes 983048 | tf_op jit(solution)/shard_map/ppermute | solution.py:359
  14.7 0.1 copy.17.weight.weight_in
  14.8 0.0 copy-start.1
  14.9 0.0 copy-start.3
  14.9 1.3 %copy-done.4 = bf16[2,512,512]{2,1,0:T(8,128)(2,1)S(1)} copy-done((bf16[2,512,512]{2,1,0:T(8,128)(2,1)S(1)}, bf16[2,512,512]{2,1,0:T(8,128)(2,1)}, u32[]{:S(2)}) %copy-start.4) | copy-done | bytes 1048600
  16.2 0.8 shard_map.136.spatial
  17.1 8.1 %collective-permute-done.3.refs_6_.refs_13_.target_below = bf16[5,128,256]{2,1,0:T(8,128)(2,1)} collective-permute-done((bf16[5,128,256]{2,1,0:T(8,128)(2,1)}, bf16[5,128,256]{2,1,0:T(8,128)(2,1)}, u32[]{:S(2)}, u32[]{:S(2)}) %collective-permute-start.3) | collective-permute-done | bytes 327712 | tf_op jit(solution)/shard_map/ppermute | solution.py:359
  25.2 0.0 copy-start.11
  25.2 0.0 copy-start.12
  25.3 0.9 shard_map.138
  26.2 3.2 %collective-permute-start.4 = (bf16[43,8,256]{2,1,0:T(8,128)(2,1)S(1)}, bf16[43,8,256]{2,1,0:T(8,128)(2,1)S(1)}, u32[]{:S(2)}, u32[]{:S(2)}) collective-permute-start(bf16[43,8,256]{2,1,0:T(8,128)(2,1)S(1)} %get-tuple-element.16), channel_id=1, source_target_pairs={{0,1},{1,2},{2,3},{4,5},{5,6},{6,7},{8,9},{9,10},{10,11},{12,13},{... | collective-permute-start | bytes 528392 | tf_op jit(solution)/shard_map/ppermute | solution.py:362
  29.4 1.3 %collective-permute-start.5 = (bf16[43,8,256]{2,1,0:T(8,128)(2,1)S(1)}, bf16[43,8,256]{2,1,0:T(8,128)(2,1)S(1)}, u32[]{:S(2)}, u32[]{:S(2)}) collective-permute-start(bf16[43,8,256]{2,1,0:T(8,128)(2,1)S(1)} %get-tuple-element.17), channel_id=1, source_target_pairs={{1,0},{2,1},{3,2},{5,4},{6,5},{7,6},{9,8},{10,9},{11,10},{13,12},{... | collective-permute-start | bytes 528392 | tf_op jit(solution)/shard_map/ppermute | solution.py:363
  30.7 0.1 and_convert_fusion.ok
  30.8 0.0 copy-start.7
  30.8 1.0 collective-permute-done.4.before
  31.8 3.8 %collective-permute-done.5.after = bf16[43,8,256]{2,1,0:T(8,128)(2,1)S(1)} collective-permute-done((bf16[43,8,256]{2,1,0:T(8,128)(2,1)S(1)}, bf16[43,8,256]{2,1,0:T(8,128)(2,1)S(1)}, u32[]{:S(2)}, u32[]{:S(2)}) %collective-permute-start.5) | collective-permute-done | bytes 176160 | tf_op jit(solution)/shard_map/ppermute | solution.py:363
  35.6 11.2 %shard_map.139 = bf16[8,128,256]{2,1,0:T(8,128)(2,1)S(1)} custom-call(bf16[43,8,256]{2,1,0:T(8,128)(2,1)S(1)} %collective-permute-done.4.before, bf16[43,8,256]{2,1,0:T(8,128)(2,1)S(1)} %collective-permute-done.5.after, bf16[8,128,256]{2,1,0:T(8,128)(2,1)S(1)} %collective-permute-done.refs_0_.refs_7_.above, bf16[8,128,256]{2,1,0:T(8,128)(2,1)S(1)} %copy-done.3, ...), custom_call_target="tpu_custom_call" | custom-call | flops 9512681472 | bytes 6067712 | tf_op jit(solution)/shard_map/pallas_call | solution.py:30
  46.8 12.5 %all_to_all.27.signal.strip_grad = bf16[4,2,128,256]{3,2,1,0:T(8,128)(2,1)S(1)} all-to-all(bf16[4,2,128,256]{3,2,1,0:T(8,128)(2,1)S(1)} %bitcast.12), channel_id=1, replica_groups=mesh['row'=8,'col'=4] {'col'}, dimensions={0} | all-to-all | bytes 1048576 | tf_op jit(solution)/shard_map/all_to_all | solution.py:386
  59.3 1.6 %shard_map.140 = bf16[512,768]{1,0:T(8,128)(2,1)} custom-call(bf16[4,2,128,256]{3,2,1,0:T(8,128)(2,1)S(1)} %all_to_all.27.signal.strip_grad, bf16[192,256]{1,0:T(8,128)(2,1)S(1)} %copy-done.7, bf16[512,512]{1,0:T(8,128)(2,1)S(1)} %copy-done.2, bf16[512,384]{1,0:T(8,128)(2,1)S(1)} %shard_map.136.spatial), custom_call_target="tpu_custom_call" | custom-call | bytes 2326528 | tf_op jit(solution)/shard_map/pallas_call | solution.py:30
  60.9 10.2 %all-to-all-start.1 = ((bf16[32,16,768]{2,1,0:T(8,128)(2,1)}), bf16[32,16,768]{2,1,0:T(8,128)(2,1)S(1)}, u32[]{:S(2)}, u32[]{:S(2)}) async-start(bf16[32,16,768]{2,1,0:T(8,128)(2,1)} %bitcast.1), calls=%async_computation.1 | async-start | bytes 1572864 | tf_op jit(solution)/shard_map/all_to_all | solution.py:347
  71.1 0.2 reshape.25
  71.4 20.5 %all-to-all-done.1 = bf16[32,16,768]{2,1,0:T(8,128)(2,1)S(1)} async-done(((bf16[32,16,768]{2,1,0:T(8,128)(2,1)}), bf16[32,16,768]{2,1,0:T(8,128)(2,1)S(1)}, u32[]{:S(2)}, u32[]{:S(2)}) %all-to-all-start.1) | async-done | bytes 786464 | tf_op jit(solution)/shard_map/all_to_all | solution.py:347
  91.9 2.1 %shard_map.141 = bf16[512,384]{1,0:T(8,128)(2,1)S(1)} custom-call(bf16[512,768]{1,0:T(8,128)(2,1)S(1)} %bitcast.8, bf16[2,2,192,192]{3,2,1,0:T(8,128)(2,1)S(1)} %bitcast.9, bf16[128,128]{1,0:T(8,128)(2,1)S(1)} %copy-done.9, bf16[128,128]{1,0:T(8,128)(2,1)S(1)} %copy-done.8), custom_call_target="tpu_custom_call" | custom-call | bytes 1540096 | tf_op jit(solution)/shard_map/pallas_call | solution.py:30
  94.0 15.7 %all_to_all.28 = bf16[32,16,384]{2,1,0:T(8,128)(2,1)S(1)} all-to-all(bf16[32,16,384]{2,1,0:T(8,128)(2,1)S(1)} %bitcast.10), channel_id=1, replica_groups=mesh['row'=8,'col'=4] {'row','col'}, dimensions={0} | all-to-all | bytes 786432 | tf_op jit(solution)/shard_map/all_to_all | solution.py:347
  109.7 2.0 %shard_map.142 = bf16[2,512,512]{2,1,0:T(8,128)(2,1)} custom-call(bf16[512,384]{1,0:T(8,128)(2,1)S(1)} %bitcast.11, bf16[4,2,128,256]{3,2,1,0:T(8,128)(2,1)S(1)} %all_to_all.27.signal.strip_grad, bf16[512,192]{1,0:T(8,128)(2,1)S(1)} %copy.17.weight.weight_in, bf16[512,256]{1,0:T(8,128)(2,1)S(1)} %copy-done.6, bf16[512,512]{1,0:T(8,128)(2,1)S(1)} %copy-done.5), custom_call_target="tpu_custom_call" | custom-call | bytes 2949120 | tf_op jit(solution)/shard_map/pallas_call | solution.py:30
  (27 shorter events, 0.1 us)
Async XLA Ops:
  0.0 17.1 %collective-permute-start = (bf16[8,128,256]{2,1,0:T(8,128)(2,1)}, bf16[8,128,256]{2,1,0:T(8,128)(2,1)S(1)}, u32[]{:S(2)}, u32[]{:S(2)}) collective-permute-start(bf16[8,128,256]{2,1,0:T(8,128)(2,1)} %features.1), channel_id=1, source_target_pairs={{0,4},{4,8},{8,12},{12,16},{16,20},{20,24},{24,28},{1,5},{5,9},{9,... | collective-permute-start | bytes 1572872 | tf_op jit(solution)/shard_map/ppermute | solution.py:355
  4.5 20.7 %collective-permute-start.1 = (bf16[8,128,256]{2,1,0:T(8,128)(2,1)}, bf16[8,128,256]{2,1,0:T(8,128)(2,1)S(1)}, u32[]{:S(2)}, u32[]{:S(2)}) collective-permute-start(bf16[8,128,256]{2,1,0:T(8,128)(2,1)} %features.1), channel_id=1, source_target_pairs={{4,0},{8,4},{12,8},{16,12},{20,16},{24,20},{28,24},{5,1},{9,5},{13... | collective-permute-start | bytes 1572872 | tf_op jit(solution)/shard_map/ppermute | solution.py:356
  6.4 1.0 copy-start
  7.5 0.7 copy-start.10
  8.2 6.5 %copy-start.14 = (bf16[512,192]{0,1:T(8,128)(2,1)S(1)}, bf16[512,192]{0,1:T(8,128)(2,1)}, u32[]{:S(2)}) copy-start(bf16[512,192]{0,1:T(8,128)(2,1)} %param.20) | copy-start | bytes 589828
  8.2 6.7 %copy-start.2 = (bf16[512,512]{1,0:T(8,128)(2,1)S(1)}, bf16[512,512]{1,0:T(8,128)(2,1)}, u32[]{:S(2)}) copy-start(bf16[512,512]{1,0:T(8,128)(2,1)} %constant.32.clone.table) | copy-start | bytes 1572868
  9.1 8.0 %collective-permute-start.2 = (bf16[5,128,256]{2,1,0:T(8,128)(2,1)}, bf16[5,128,256]{2,1,0:T(8,128)(2,1)S(1)}, u32[]{:S(2)}, u32[]{:S(2)}) collective-permute-start(bf16[5,128,256]{2,1,0:T(8,128)(2,1)} %get-tuple-element.13), channel_id=1, source_target_pairs={{0,4},{4,8},{8,12},{12,16},{16,20},{20,24},{24,28},{1,5},{5,9},{9,... | collective-permute-start | bytes 983048 | tf_op jit(solution)/shard_map/ppermute | solution.py:358
  12.8 12.5 %collective-permute-start.3 = (bf16[5,128,256]{2,1,0:T(8,128)(2,1)}, bf16[5,128,256]{2,1,0:T(8,128)(2,1)}, u32[]{:S(2)}, u32[]{:S(2)}) collective-permute-start(bf16[5,128,256]{2,1,0:T(8,128)(2,1)} %get-tuple-element.15), channel_id=1, source_target_pairs={{4,0},{8,4},{12,8},{16,12},{20,16},{24,20},{28,24},{5,1},{9,5},{13... | collective-permute-start | bytes 983048 | tf_op jit(solution)/shard_map/ppermute | solution.py:359
  14.8 10.4 %copy-start.1 = (bf16[8,128,256]{2,1,0:T(8,128)(2,1)S(1)}, bf16[8,128,256]{2,1,0:T(8,128)(2,1)}, u32[]{:S(2)}) copy-start(bf16[8,128,256]{2,1,0:T(8,128)(2,1)} %target.1) | copy-start | bytes 1572868
  14.9 10.4 %copy-start.3 = (bf16[8,128,256]{2,1,0:T(8,128)(2,1)S(1)}, bf16[8,128,256]{2,1,0:T(8,128)(2,1)}, u32[]{:S(2)}) copy-start(bf16[8,128,256]{2,1,0:T(8,128)(2,1)} %features.1) | copy-start | bytes 1572868
  14.9 1.3 %copy-start.4 = (bf16[2,512,512]{2,1,0:T(8,128)(2,1)S(1)}, bf16[2,512,512]{2,1,0:T(8,128)(2,1)}, u32[]{:S(2)}) copy-start(bf16[2,512,512]{2,1,0:T(8,128)(2,1)} %signal.1) | copy-start | bytes 3145732
  25.2 10.4 %copy-start.11 = (bf16[3,3,256,256]{3,2,1,0:T(8,128)(2,1)S(1)}, bf16[3,3,256,256]{3,2,1,0:T(8,128)(2,1)}, u32[]{:S(2)}) copy-start(bf16[3,3,256,256]{3,2,1,0:T(8,128)(2,1)} %first.3) | copy-start | bytes 3538948
  25.2 10.4 %copy-start.12 = (bf16[3,3,256,256]{3,2,1,0:T(8,128)(2,1)S(1)}, bf16[3,3,256,256]{3,2,1,0:T(8,128)(2,1)}, u32[]{:S(2)}) copy-start(bf16[3,3,256,256]{3,2,1,0:T(8,128)(2,1)} %second.1) | copy-start | bytes 3538948
  26.2 5.6 %collective-permute-start.4 = (bf16[43,8,256]{2,1,0:T(8,128)(2,1)S(1)}, bf16[43,8,256]{2,1,0:T(8,128)(2,1)S(1)}, u32[]{:S(2)}, u32[]{:S(2)}) collective-permute-start(bf16[43,8,256]{2,1,0:T(8,128)(2,1)S(1)} %get-tuple-element.16), channel_id=1, source_target_pairs={{0,1},{1,2},{2,3},{4,5},{5,6},{6,7},{8,9},{9,10},{10,11},{12,13},{... | collective-permute-start | bytes 528392 | tf_op jit(solution)/shard_map/ppermute | solution.py:362
  29.4 6.2 %collective-permute-start.5 = (bf16[43,8,256]{2,1,0:T(8,128)(2,1)S(1)}, bf16[43,8,256]{2,1,0:T(8,128)(2,1)S(1)}, u32[]{:S(2)}, u32[]{:S(2)}) collective-permute-start(bf16[43,8,256]{2,1,0:T(8,128)(2,1)S(1)} %get-tuple-element.17), channel_id=1, source_target_pairs={{1,0},{2,1},{3,2},{5,4},{6,5},{7,6},{9,8},{10,9},{11,10},{13,12},{... | collective-permute-start | bytes 528392 | tf_op jit(solution)/shard_map/ppermute | solution.py:363
  30.8 28.5 %copy-start.7 = (bf16[192,256]{1,0:T(8,128)(2,1)S(1)}, bf16[192,256]{1,0:T(8,128)(2,1)}, u32[]{:S(2)}) copy-start(bf16[192,256]{1,0:T(8,128)(2,1)} %weight.2) | copy-start | bytes 294916
  60.9 10.2 %copy-start.13 = (bf16[384,384]{1,0:T(8,128)(2,1)S(1)}, bf16[384,384]{1,0:T(8,128)(2,1)}, u32[]{:S(2)}) copy-start(bf16[384,384]{1,0:T(8,128)(2,1)} %param.23) | copy-start | bytes 884740
  60.9 31.0 %copy-start.8 = (bf16[128,128]{1,0:T(8,128)(2,1)S(1)}, bf16[128,128]{1,0:T(8,128)(2,1)}, u32[]{:S(2)}) copy-start(bf16[128,128]{1,0:T(8,128)(2,1)} %constant.33.clone.back_table) | copy-start | bytes 98308
  60.9 31.0 %copy-start.9 = (bf16[128,128]{1,0:T(8,128)(2,1)S(1)}, bf16[128,128]{1,0:T(8,128)(2,1)}, u32[]{:S(2)}) copy-start(bf16[128,128]{1,0:T(8,128)(2,1)} %constant.34.clone.table) | copy-start | bytes 98308
  60.9 31.0 %all-to-all-start.1 = ((bf16[32,16,768]{2,1,0:T(8,128)(2,1)}), bf16[32,16,768]{2,1,0:T(8,128)(2,1)S(1)}, u32[]{:S(2)}, u32[]{:S(2)}) async-start(bf16[32,16,768]{2,1,0:T(8,128)(2,1)} %bitcast.1), calls=%async_computation.1 | async-start | bytes 1572864 | tf_op jit(solution)/shard_map/all_to_all | solution.py:347
  91.9 17.8 %copy-start.5 = (bf16[512,512]{1,0:T(8,128)(2,1)S(1)}, bf16[512,512]{1,0:T(8,128)(2,1)}, u32[]{:S(2)}) copy-start(bf16[512,512]{1,0:T(8,128)(2,1)} %constant.31.clone.table) | copy-start | bytes 1572868
  91.9 17.8 %copy-start.6 = (bf16[512,256]{1,0:T(8,128)(2,1)S(1)}, bf16[512,256]{1,0:T(8,128)(2,1)}, u32[]{:S(2)}) copy-start(bf16[512,256]{1,0:T(8,128)(2,1)} %weight_local.1) | copy-start | bytes 786436

commit v7 on v6

--- a/solution.py
+++ b/solution.py
@@ -211,102 +211,276 @@
     )(*parts, *parts)
 
 
-def conv_kernel(
+def put(wide, row, value, stride):
+    size, channels = value.shape
+    spot = pl.ds(row * stride, size)
+    wide[spot, :channels] = pltpu.roll(value, 2, 0).astype(jnp.bfloat16)
+    wide[spot, channels : 2 * channels] = value.astype(jnp.bfloat16)
+    wide[spot, 2 * channels :] = pltpu.roll(value, size - 2, 0).astype(jnp.bfloat16)
+
+
+def taps(wide, row, count, stride):
+    parts = [wide[pl.ds((row + 2 * a) * stride, count * stride), :] for a in range(3)]
+    return jnp.concatenate(parts, axis=1)
+
+
+def conv(wide, row, count, stride, kernel):
+    channels = kernel.shape[-1]
+    return dot(taps(wide, row, count, stride), kernel[...].reshape(9 * channels, channels))
+
+
+def conv_adjoint(wide, row, count, stride, kernel):
+    flipped = [kernel[2 - a, 2 - b] for a in range(3) for b in range(3)]
+    return dot_t(taps(wide, row, count, stride), jnp.concatenate(flipped, axis=1))
+
+
+def stacked(piece, rows):
+    return jnp.concatenate([piece(row) for row in rows], axis=0)
+
+
+def first_stages(stride, blocks, rows, feature, inside, first, second, wide_even, wide_odd, slopes, use):
+    tall = rows + 2 * REACH
+    for row in range(0, tall, NEAR):
+        put(wide_even, row, stacked(feature, range(row, row + NEAR)), stride)
+    count = blocks[0]
+    for row in range(0, tall - 4, count):
+        pre = conv(wide_even, row, count, stride, first)
+        s = 1.0 / (1.0 + jnp.exp(-pre))
+        kept = stacked(inside, range(row + 2, row + 2 + count))
+        put(wide_odd, row, pre * s * kept, stride)
+        low, high = max(row, NEAR), min(row + count, tall - 4 - NEAR)
+        if low < high:
+            part = slice((low - row) * stride, (high - row) * stride)
+            slope = (s * (1.0 + pre * (1.0 - s)) * kept)[part]
+            slopes[pl.ds((low - NEAR) * stride, (high - low) * stride), :] = slope
+    count = blocks[1]
+    for row in range(0, rows + 2 * NEAR, count):
+        use(row, count, conv(wide_odd, row, count, stride, second))
+
+
+def last_stages(stride, blocks, rows, first, second, wide_even, wide_odd, slopes, use):
+    count = blocks[2]
+    for row in range(0, rows + 4, count):
+        value = conv_adjoint(wide_even, row, count, stride, second)
+        value = value * slopes[pl.ds(row * stride, count * stride), :]
+        put(wide_odd, row, value, stride)
+    count = blocks[3]
+    for row in range(0, rows, count):
+        use(row, count, conv_adjoint(wide_odd, row, count, stride, first))
+
+
+def loss_grad(row, count, value, target, hole, inside):
+    near = range(row, row + count)
+    weight = (1.0 + 2.0 * stacked(hole, near)) * stacked(inside, range(row + NEAR, row + count + NEAR))
+    return weight * (value - stacked(target, near))
+
+
+def part_of(rows, edge, above, own, below):
+    def find(row):
+        if row < edge:
+            return above, row
+        if row < edge + rows:
+            return own, row - edge
+        return below, row - edge - rows
+
+    return find
+
+
+TILE_BLOCKS = (4, 4, 4, 4)
+SIDE_BLOCKS = (10, 8, 12, 8)
+
+
+def tile_forward_kernel(above, features, below, first, second, ok, pre, slopes, wide_even, wide_odd):
+    rows, stride, _ = features.shape
+    find = part_of(rows, REACH, above, features, below)
+
+    def feature(row):
+        source, at = find(row)
+        return source[at].astype(jnp.float32)
+
+    def inside(row):
+        return ok[REACH : REACH + stride, row : row + 1]
+
+    def use(row, count, value):
+        pre[pl.ds(row * stride, count * stride), :] = value
+
+    first_stages(
+        stride, TILE_BLOCKS, rows, feature, inside, first, second, wide_even, wide_odd, slopes, use
+    )
+
+
+def tile_backward_kernel(
+    pre,
+    slopes,
+    target_above,
+    target,
+    target_below,
+    mask_row,
+    first,
+    second,
+    ok,
+    out,
+    wide_even,
+    wide_odd,
+):
+    rows, stride, channels = target.shape
+    find = part_of(rows, NEAR, target_above, target, target_below)
+
+    def goal(row):
+        source, at = find(row)
+        return source[at].astype(jnp.float32)
+
+    masks = [m[at].astype(jnp.float32) for m, at in ((target_above, NEAR), (mask_row, 0), (target_below, NEAR))]
+    find_mask = part_of(rows, NEAR, (masks[0], rows - NEAR), (masks[1], 0), (masks[2], 0))
+
+    def hole(row):
+        (mask, start), at = find_mask(row)
+        return mask[:, start + at : start + at + 1]
+
+    def inside(row):
+        return ok[REACH : REACH + stride, row : row + 1]
+
+    count = NEAR
+    for row in range(0, rows + 2 * NEAR, count):
+        value = pre[pl.ds(row * stride, count * stride), :]
+        put(wide_even, row, loss_grad(row, count, value, goal, hole, inside), stride)
+
+    def use(row, count, value):
+        out[row : row + count] = value.reshape(count, stride, channels).astype(jnp.bfloat16)
+
+    last_stages(stride, TILE_BLOCKS, rows, first, second, wide_even, wide_odd, slopes, use)
+
+
+def side_kernel(
     before,
     after,
     above,
     features,
     below,
-    first,
     target_above,
     target,
     target_below,
     mask_row,
+    first,
     second,
     ok,
+    tile,
     out,
     wide_even,
     wide_odd,
     slopes,
 ):
-    tile_rows, tile_cols, channels = features.shape
-    stride = tile_cols + 2 * REACH
-    block = NEAR
-    size = block * stride
-    tall = tile_rows + 2 * REACH
-
-    def rows_of(edge, source, row, count=block):
-        parts = [before[edge : edge + count], source[row : row + count], after[edge : edge + count]]
-        parts = [part.astype(jnp.float32) for part in parts]
-        return jnp.concatenate(parts, axis=1).reshape(count * stride, channels)
-
-    def put(wide, row, value):
-        spot = pl.ds(row * stride, size)
-        wide[spot, :channels] = pltpu.roll(value, 2, 0).astype(jnp.bfloat16)
-        wide[spot, channels : 2 * channels] = value.astype(jnp.bfloat16)
-        wide[spot, 2 * channels :] = pltpu.roll(value, size - 2, 0).astype(jnp.bfloat16)
-
-    def taps(wide, row):
-        return jnp.concatenate(
-            [wide[pl.ds((row + 2 * a) * stride, size), :] for a in range(3)], axis=1
-        )
-
-    def conv(wide, row, kernel):
-        return dot(taps(wide, row), kernel[...].reshape(9 * channels, channels))
-
-    def conv_adjoint(wide, row, kernel):
-        flipped = [kernel[2 - a, 2 - b] for a in range(3) for b in range(3)]
-        return dot_t(taps(wide, row), jnp.concatenate(flipped, axis=1))
+    rows, tile_cols, channels = features.shape
+    keep = 2 * REACH
+    stride = 2 * (REACH + keep)
+    tall = rows + 2 * REACH
+    own = tall + NEAR + 1
+
+    def joined(edge, source, at):
+        parts = [before[edge], source[at, :keep], source[at, tile_cols - keep :], after[edge]]
+        return jnp.concatenate([part.astype(jnp.float32) for part in parts], axis=0)
+
+    find = part_of(rows, REACH, above, features, below)
+    find_target = part_of(
+        rows, NEAR, (target_above, tall), (target, own), (target_below, own + rows + 1)
+    )
+
+    def feature(row):
+        return joined(row, *find(row))
+
+    def goal(row):
+        (source, edge), at = find_target(row)
+        return joined(edge + at, source, at)
+
+    masks = [
+        joined(tall + NEAR, target_above, NEAR),
+        joined(own + rows, mask_row, 0),
+        joined(own + rows + 1 + NEAR, target_below, NEAR),
+    ]
+    find_mask = part_of(rows, NEAR, (masks[0], rows - NEAR), (masks[1], 0), (masks[2], 0))
+
+    def hole(row):
+        (mask, start), at = find_mask(row)
+        return mask[:, start + at : start + at + 1]
+
+    width = ok.shape[0]
+    kept = jnp.concatenate([ok[: REACH + keep], ok[width - REACH - keep :]], axis=0)
 
     def inside(row):
-        return jnp.concatenate([ok[:, row + i : row + i + 1] for i in range(block)], axis=0)
-
-    for part, source in enumerate((above, features, below)):
-        for row in range(0, tile_rows, block):
-            at = part * tile_rows + row
-            put(wide_even, at, rows_of(at, source, row))
-    for row in range(0, tall - 4, block):
-        pre = conv(wide_even, row, first)
-        s = 1.0 / (1.0 + jnp.exp(-pre))
-        kept = inside(row + 2)
-        put(wide_odd, row, pre * s * kept)
-        if NEAR <= row < tall - 4 - NEAR:
-            slopes[pl.ds((row - NEAR) * stride, size), :] = s * (1.0 + pre * (1.0 - s)) * kept
-    own = tall + NEAR + 1
-    masks = [
-        rows_of(tall + NEAR, target_above, NEAR, 1),
-        rows_of(own + tile_rows, mask_row, 0, 1),
-        rows_of(own + tile_rows + 1 + NEAR, target_below, NEAR, 1),
+        return kept[:, row : row + 1]
+
+    def use_forward(row, count, value):
+        put(wide_even, row, loss_grad(row, count, value, goal, hole, inside), stride)
+
+    first_stages(
+        stride, SIDE_BLOCKS, rows, feature, inside, first, second, wide_even, wide_odd, slopes, use_forward
+    )
+    out[:, REACH : tile_cols - REACH] = tile[:, REACH : tile_cols - REACH]
+
+    def use(row, count, value):
+        value = value.reshape(count, stride, channels).astype(jnp.bfloat16)
+        out[row : row + count, :REACH] = value[:, REACH : 2 * REACH]
+        out[row : row + count, tile_cols - REACH :] = value[:, stride - 2 * REACH : stride - REACH]
+
+    last_stages(stride, SIDE_BLOCKS, rows, first, second, wide_even, wide_odd, slopes, use)
+
+
+def wide_buffer(rows, stride, channels):
+    return pltpu.VMEM((rows * stride, 3 * channels), jnp.bfloat16)
+
+
+def tile_forward(above, features, below, first, second, ok):
+    rows, stride, channels = features.shape
+    shapes = [
+        jax.ShapeDtypeStruct(((rows + h) * stride, channels), jnp.float32) for h in (2 * NEAR, 4)
     ]
-    goals = [(tall, target_above, 0, masks[0], tile_rows - NEAR)]
-    goals += [(own + r, target, r, masks[1], r) for r in range(0, tile_rows, block)]
-    goals += [(own + tile_rows + 1, target_below, 0, masks[2], 0)]
-    for index, (edge, source, at, mask, lane) in enumerate(goals):
-        row = index * block
-        value = conv(wide_odd, row, second)
-        holes = jnp.concatenate([mask[:, lane + i : lane + i + 1] for i in range(block)], axis=0)
-        weight = (1.0 + 2.0 * holes) * inside(row + NEAR)
-        put(wide_even, row, weight * (value - rows_of(edge, source, at)))
-    for row in range(0, tile_rows + 4, block):
-        value = conv_adjoint(wide_even, row, second)
-        put(wide_odd, row, value * slopes[pl.ds(row * stride, size), :])
-    for row in range(0, tile_rows, block):
-        value = conv_adjoint(wide_odd, row, first).reshape(block, stride, channels)
-        out[row : row + block] = value[:, REACH : REACH + tile_cols].astype(jnp.bfloat16)
-
-
-def conv_chain(shape, *operands):
-    tile_rows, tile_cols, channels = shape
-    stride = tile_cols + 2 * REACH
-    wides = [pltpu.VMEM(((tile_rows + h) * stride, 3 * channels), jnp.bfloat16) for h in (16, 12)]
-    pixels = sum((tile_rows + h) * stride for h in (12, 8, 4, 0))
     return vmem_call(
-        conv_kernel,
-        [jax.ShapeDtypeStruct(shape, jnp.bfloat16)],
+        tile_forward_kernel,
+        shapes,
+        above,
+        features,
+        below,
+        first,
+        second,
+        ok,
+        flops=2 * 9 * channels * channels * stride * (2 * rows + 20),
+        scratch=[wide_buffer(rows + h, stride, channels) for h in (16, 12)],
+        limit=18,
+    )
+
+
+def tile_backward(pre, slopes, target_above, target, target_below, mask_row, first, second, ok):
+    rows, stride, channels = target.shape
+    return vmem_call(
+        tile_backward_kernel,
+        [jax.ShapeDtypeStruct(target.shape, jnp.bfloat16)],
+        pre,
+        slopes,
+        target_above,
+        target,
+        target_below,
+        mask_row,
+        first,
+        second,
+        ok,
+        flops=2 * 9 * channels * channels * stride * (2 * rows + 4),
+        scratch=[wide_buffer(rows + h, stride, channels) for h in (8, 4)],
+        limit=16,
+    )[0]
+
+
+def sides(tile, *operands):
+    rows, _, channels = tile.shape
+    stride = 6 * REACH
+    return vmem_call(
+        side_kernel,
+        [jax.ShapeDtypeStruct(tile.shape, jnp.bfloat16)],
         *operands,
-        flops=2 * 9 * channels * channels * pixels,
-        scratch=[*wides, pltpu.VMEM(((tile_rows + 4) * stride, channels), jnp.float32)],
-        limit=20,
+        tile,
+        flops=2 * 9 * channels * channels * stride * (4 * rows + 24),
+        scratch=[wide_buffer(rows + h, stride, channels) for h in (16, 12)]
+        + [pltpu.VMEM(((rows + 4) * stride, channels), jnp.float32)],
+        limit=14,
     )[0]
 
 
@@ -350,6 +524,12 @@
     spatial_cols = vmem_call(
         functools.partial(spatial_kernel, col_norm), cells, inputs, weight_in, table
     )[0]
+    row0, col0 = lax.axis_index("row") * tile_rows, lax.axis_index("col") * tile_cols
+    row_ids = row0 - REACH + jnp.arange(tile_rows + 2 * REACH, dtype=jnp.int32)
+    col_ids = col0 - REACH + jnp.arange(tile_cols + 2 * REACH, dtype=jnp.int32)
+    ok = ((col_ids >= 0) & (col_ids < width))[:, None] & ((row_ids >= 0) & (row_ids < height))[None]
+    ok = ok.astype(jnp.float32)
+
     up, down = neighbours("row")
     left, right = neighbours("col")
     above = lax.ppermute(features, "row", up)
@@ -357,28 +537,26 @@
     pack_down, pack_up, mask_row = target_packs(target, hole_mask)
     target_above = lax.ppermute(pack_down, "row", up)
     target_below = lax.ppermute(pack_up, "row", down)
-    above, spatial_cols = lax.optimization_barrier((above, spatial_cols))
+    pre, slopes = tile_forward(above, features, below, kernel_first, kernel_second, ok)
+    target_above, pre, spatial_cols = lax.optimization_barrier((target_above, pre, spatial_cols))
     last, initial = edges(above, features, below, target_above, target, mask_row, target_below)
     before = lax.ppermute(last, "col", left)
     after = lax.ppermute(initial, "col", right)
-
-    row0, col0 = lax.axis_index("row") * tile_rows, lax.axis_index("col") * tile_cols
-    row_ids = row0 - REACH + jnp.arange(tile_rows + 2 * REACH, dtype=jnp.int32)
-    col_ids = col0 - REACH + jnp.arange(tile_cols + 2 * REACH, dtype=jnp.int32)
-    ok = ((col_ids >= 0) & (col_ids < width))[:, None] & ((row_ids >= 0) & (row_ids < height))[None]
-    ok = ok.astype(jnp.float32)
-    grad_feat = conv_chain(
-        features.shape,
+    tile = tile_backward(
+        pre, slopes, target_above, target, target_below, mask_row, kernel_first, kernel_second, ok
+    )
+    grad_feat = sides(
+        tile,
         before,
         after,
         above,
         features,
         below,
-        kernel_first,
         target_above,
         target,
         target_below,
         mask_row,
+        kernel_first,
         kernel_second,
         ok,
     )

time: 112 us -> 107 us (0.955)
  waiting for transfers between devices: 33.4 us -> 23.3 us
  blocking collectives: 28.2 us -> 32.6 us
  starting transfers between devices: 26.7 us -> 23 us
  Pallas kernels: 19.5 us -> 21.8 us
  local copies, waits for them, and re-layouts: 3.49 us -> 5.6 us
    ppermute x1, waiting for transfers between devices: 8.12 us -> 0.01 us  [shards(): target_below = lax.ppermute(pack_up, 'row', down)]
    all_to_all x1, blocking collectives: 12.5 us -> 16.9 us  [shards(): lax.all_to_all(grad_feat.reshape(col_devices, strip, tile_cols, channels)...]
    all_to_all x1, starting transfers between devices: 10.2 us -> 6.23 us  [swap(): lax.all_to_all(spectrum, ('row', 'col'), split_axis=0, concat_axis=0, til...]
    pallas_call x5 -> x7, Pallas kernels: 17.6 us -> 20.9 us  [vmem_call(): pl.pallas_call(body, out_shape=shapes, in_specs=[spec] * len(operands), o...]
    ppermute x1, waiting for transfers between devices: 3.83 us -> 0.95 us  [shards(): after = lax.ppermute(initial, 'col', right)]
    unnamed x31, local copies, waits for them, and re-layouts: 3.21 us -> 5.33 us
    ppermute x1, waiting for transfers between devices: 0.01 us -> 1.87 us  [shards(): below = lax.ppermute(features, 'row', down)]
  transfers between devices with their start and end apart: 7 -> 7, of which waited for: 4 -> 3; matrix products, arithmetic and copies ran while one was open for 0% -> 1% of each run, Pallas kernels for 2% -> 11%
where the time goes in v7:
time: 107 us
  blocking collectives  32.6 us (30%)
  waiting for transfers between devices  23.3 us (22%)
  starting transfers between devices  23 us (21%)
  Pallas kernels  21.8 us (20%)
  local copies, waits for them, and re-layouts  5.6 us (5%)
    pallas_call x7, Pallas kernels, vmem_call(): pl.pallas_call(body, out_shape=shapes, in_specs=[spec] * len(operands), o...  20.9 us
    all_to_all x1, waiting for transfers between devices, swap(): lax.all_to_all(spectrum, ('row', 'col'), split_axis=0, concat_axis=0, til...  20.5 us
    all_to_all x1, blocking collectives, shards(): lax.all_to_all(grad_feat.reshape(col_devices, strip, tile_cols, channels)...  16.9 us
    all_to_all x1, blocking collectives, swap(): lax.all_to_all(spectrum, ('row', 'col'), split_axis=0, concat_axis=0, til...  15.7 us
    all_to_all x1, starting transfers between devices, swap(): lax.all_to_all(spectrum, ('row', 'col'), split_axis=0, concat_axis=0, til...  6.23 us
    unnamed x31, local copies, waits for them, and re-layouts  5.33 us
    ppermute x1, starting transfers between devices, shards(): above = lax.ppermute(features, 'row', up)  4.5 us
    ppermute x1, starting transfers between devices, shards(): target_above = lax.ppermute(pack_down, 'row', up)  3.76 us
  transfers between devices with their start and end apart: 7, of which 3 were waited for; matrix products, arithmetic and copies ran while one was open for 1% of the time, Pallas kernels for 11%

profile of v7, /device:TPU:1, one launch (start us, length us, event | category | flops | bytes accessed | tf_op | source)
XLA Modules:
  0.0 106.7 jit_solution(1369965946418943397)
XLA Ops:
  0.0 4.5 %collective-permute-start = (bf16[8,128,256]{2,1,0:T(8,128)(2,1)}, bf16[8,128,256]{2,1,0:T(8,128)(2,1)S(1)}, u32[]{:S(2)}, u32[]{:S(2)}) collective-permute-start(bf16[8,128,256]{2,1,0:T(8,128)(2,1)} %features.3), channel_id=1, source_target_pairs={{0,4},{4,8},{8,12},{12,16},{16,20},{20,24},{24,28},{1,5},{5,9},{9,... | collective-permute-start | bytes 1572872 | tf_op jit(solution)/shard_map/ppermute | solution.py:535
  4.5 1.9 %collective-permute-start.1 = (bf16[8,128,256]{2,1,0:T(8,128)(2,1)}, bf16[8,128,256]{2,1,0:T(8,128)(2,1)S(1)}, u32[]{:S(2)}, u32[]{:S(2)}) collective-permute-start(bf16[8,128,256]{2,1,0:T(8,128)(2,1)} %features.3), channel_id=1, source_target_pairs={{4,0},{8,4},{12,8},{16,12},{20,16},{24,20},{28,24},{5,1},{9,5},{13... | collective-permute-start | bytes 1572872 | tf_op jit(solution)/shard_map/ppermute | solution.py:536
  6.4 0.0 copy-start
  6.5 1.0 copy-done
  7.5 0.7 copy-done.10
  8.2 0.9 shard_map.136
  9.1 3.8 %collective-permute-start.2 = (bf16[5,128,256]{2,1,0:T(8,128)(2,1)}, bf16[5,128,256]{2,1,0:T(8,128)(2,1)S(1)}, u32[]{:S(2)}, u32[]{:S(2)}) collective-permute-start(bf16[5,128,256]{2,1,0:T(8,128)(2,1)} %get-tuple-element.15), channel_id=1, source_target_pairs={{0,4},{4,8},{8,12},{12,16},{16,20},{20,24},{24,28},{1,5},{5,9},{9,... | collective-permute-start | bytes 983048 | tf_op jit(solution)/shard_map/ppermute | solution.py:538
  12.9 1.9 %collective-permute-start.3 = (bf16[5,128,256]{2,1,0:T(8,128)(2,1)}, bf16[5,128,256]{2,1,0:T(8,128)(2,1)S(1)}, u32[]{:S(2)}, u32[]{:S(2)}) collective-permute-start(bf16[5,128,256]{2,1,0:T(8,128)(2,1)} %get-tuple-element.19), channel_id=1, source_target_pairs={{4,0},{8,4},{12,8},{16,12},{20,16},{24,20},{28,24},{5,1},{9,5},{13... | collective-permute-start | bytes 983048 | tf_op jit(solution)/shard_map/ppermute | solution.py:539
  14.8 1.1 copy.17.weight.weight_in
  15.9 0.0 copy-start.4
  15.9 1.2 %copy-done.4 = bf16[2,512,512]{2,1,0:T(8,128)(2,1)S(1)} copy-done((bf16[2,512,512]{2,1,0:T(8,128)(2,1)S(1)}, bf16[2,512,512]{2,1,0:T(8,128)(2,1)}, u32[]{:S(2)}) %copy-start.4) | copy-done | bytes 1048600
  17.1 0.8 shard_map.138.spatial
  18.0 0.1 and_convert_fusion.ok
  18.1 1.9 %collective-permute-done.1.below.refs_2_.refs_9_ = bf16[8,128,256]{2,1,0:T(8,128)(2,1)S(1)} collective-permute-done((bf16[8,128,256]{2,1,0:T(8,128)(2,1)}, bf16[8,128,256]{2,1,0:T(8,128)(2,1)S(1)}, u32[]{:S(2)}, u32[]{:S(2)}) %collective-permute-start.1) | collective-permute-done | bytes 524320 | tf_op jit(solution)/shard_map/ppermute | solution.py:536
  20.0 1.3 %copy-done.12 = bf16[3,3,256,256]{3,2,1,0:T(8,128)(2,1)S(1)} copy-done((bf16[3,3,256,256]{3,2,1,0:T(8,128)(2,1)S(1)}, bf16[3,3,256,256]{3,2,1,0:T(8,128)(2,1)}, u32[]{:S(2)}) %copy-start.12) | copy-done | bytes 1179672
  21.3 5.9 %shard_map.137 = (f32[2048,256]{1,0:T(8,128)S(1)}, f32[1536,256]{1,0:T(8,128)S(1)}) custom-call(bf16[8,128,256]{2,1,0:T(8,128)(2,1)S(1)} %collective-permute-done.above.refs_0_.refs_7_, bf16[8,128,256]{2,1,0:T(8,128)(2,1)S(1)} %copy-done.3, bf16[8,128,256]{2,1,0:T(8,128)(2,1)S(1)} %collective-permute-done.1.below.refs_2_.refs_9_, ...), custom_call_target="tpu_custom_call" | custom-call | flops 5435817984 | bytes 7616000 | tf_op jit(solution)/shard_map/pallas_call | solution.py:30
  27.3 3.2 %collective-permute-start.4 = (bf16[43,8,256]{2,1,0:T(8,128)(2,1)S(1)}, bf16[43,8,256]{2,1,0:T(8,128)(2,1)S(1)}, u32[]{:S(2)}, u32[]{:S(2)}) collective-permute-start(bf16[43,8,256]{2,1,0:T(8,128)(2,1)S(1)} %get-tuple-element.20), channel_id=1, source_target_pairs={{0,1},{1,2},{2,3},{4,5},{5,6},{6,7},{8,9},{9,10},{10,11},{12,13},{... | collective-permute-start | bytes 528392 | tf_op jit(solution)/shard_map/ppermute | solution.py:543
  30.5 1.5 %collective-permute-start.5 = (bf16[43,8,256]{2,1,0:T(8,128)(2,1)S(1)}, bf16[43,8,256]{2,1,0:T(8,128)(2,1)S(1)}, u32[]{:S(2)}, u32[]{:S(2)}) collective-permute-start(bf16[43,8,256]{2,1,0:T(8,128)(2,1)S(1)} %get-tuple-element.21), channel_id=1, source_target_pairs={{1,0},{2,1},{3,2},{5,4},{6,5},{7,6},{9,8},{10,9},{11,10},{13,12},{... | collective-permute-start | bytes 528392 | tf_op jit(solution)/shard_map/ppermute | solution.py:544
  32.0 0.0 copy-start.13
  32.0 3.7 %shard_map.140.tile = bf16[8,128,256]{2,1,0:T(8,128)(2,1)S(1)} custom-call(f32[2048,256]{1,0:T(8,128)S(1)} %get-tuple-element.22.pre, f32[1536,256]{1,0:T(8,128)S(1)} %get-tuple-element.23.slopes, bf16[5,128,256]{2,1,0:T(8,128)(2,1)S(1)} %collective-permute-done.2.refs_3_.refs_10_.target_above, bf16[8,128,256]{2,1,0:T(8,128)(2,1)S(1)} %copy-done.1, ...), custom_call_target="tpu_custom_call" | custom-call | flops 3019898880 | bytes 7812608 | tf_op jit(solution)/shard_map/pallas_call | solution.py:30
  35.7 0.0 copy-start.7
  35.7 0.9 collective-permute-done.5.after
  36.7 4.8 %shard_map.141 = bf16[8,128,256]{2,1,0:T(8,128)(2,1)S(1)} custom-call(bf16[43,8,256]{2,1,0:T(8,128)(2,1)S(1)} %collective-permute-done.4.before, bf16[43,8,256]{2,1,0:T(8,128)(2,1)S(1)} %collective-permute-done.5.after, bf16[8,128,256]{2,1,0:T(8,128)(2,1)S(1)} %collective-permute-done.above.refs_0_.refs_7_, bf16[8,128,256]{2,1,0:T(8,128)(2,1)S(1)} %copy-done.3, ...), custom_call_target="tpu_custom_call" | custom-call | flops 3170893824 | bytes 6592000 | tf_op jit(solution)/shard_map/pallas_call | solution.py:30
  41.5 16.9 %all_to_all.27.signal.strip_grad = bf16[4,2,128,256]{3,2,1,0:T(8,128)(2,1)S(1)} all-to-all(bf16[4,2,128,256]{3,2,1,0:T(8,128)(2,1)S(1)} %bitcast.12), channel_id=1, replica_groups=mesh['row'=8,'col'=4] {'col'}, dimensions={0} | all-to-all | bytes 1048576 | tf_op jit(solution)/shard_map/all_to_all | solution.py:564
  58.3 1.6 %shard_map.142 = bf16[512,768]{1,0:T(8,128)(2,1)} custom-call(bf16[4,2,128,256]{3,2,1,0:T(8,128)(2,1)S(1)} %all_to_all.27.signal.strip_grad, bf16[192,256]{1,0:T(8,128)(2,1)S(1)} %copy-done.7, bf16[512,512]{1,0:T(8,128)(2,1)S(1)} %copy-done.2, bf16[512,384]{1,0:T(8,128)(2,1)S(1)} %shard_map.138.spatial), custom_call_target="tpu_custom_call" | custom-call | bytes 2326528 | tf_op jit(solution)/shard_map/pallas_call | solution.py:30
  59.9 6.2 %all-to-all-start.1 = ((bf16[32,16,768]{2,1,0:T(8,128)(2,1)}), bf16[32,16,768]{2,1,0:T(8,128)(2,1)S(1)}, u32[]{:S(2)}, u32[]{:S(2)}) async-start(bf16[32,16,768]{2,1,0:T(8,128)(2,1)} %bitcast.1), calls=%async_computation.1 | async-start | bytes 1572864 | tf_op jit(solution)/shard_map/all_to_all | solution.py:521
  66.2 0.2 reshape.25
  66.4 0.0 copy-start.5
  66.5 20.5 %all-to-all-done.1 = bf16[32,16,768]{2,1,0:T(8,128)(2,1)S(1)} async-done(((bf16[32,16,768]{2,1,0:T(8,128)(2,1)}), bf16[32,16,768]{2,1,0:T(8,128)(2,1)S(1)}, u32[]{:S(2)}, u32[]{:S(2)}) %all-to-all-start.1) | async-done | bytes 786464 | tf_op jit(solution)/shard_map/all_to_all | solution.py:521
  87.0 2.0 %shard_map.143 = bf16[512,384]{1,0:T(8,128)(2,1)S(1)} custom-call(bf16[512,768]{1,0:T(8,128)(2,1)S(1)} %bitcast.8, bf16[2,2,192,192]{3,2,1,0:T(8,128)(2,1)S(1)} %bitcast.9, bf16[128,128]{1,0:T(8,128)(2,1)S(1)} %copy-done.9, bf16[128,128]{1,0:T(8,128)(2,1)S(1)} %copy-done.8), custom_call_target="tpu_custom_call" | custom-call | bytes 1540096 | tf_op jit(solution)/shard_map/pallas_call | solution.py:30
  89.0 15.7 %all_to_all.28 = bf16[32,16,384]{2,1,0:T(8,128)(2,1)S(1)} all-to-all(bf16[32,16,384]{2,1,0:T(8,128)(2,1)S(1)} %bitcast.10), channel_id=1, replica_groups=mesh['row'=8,'col'=4] {'row','col'}, dimensions={0} | all-to-all | bytes 786432 | tf_op jit(solution)/shard_map/all_to_all | solution.py:521
  104.8 2.0 %shard_map.144 = bf16[2,512,512]{2,1,0:T(8,128)(2,1)} custom-call(bf16[512,384]{1,0:T(8,128)(2,1)S(1)} %bitcast.11, bf16[4,2,128,256]{3,2,1,0:T(8,128)(2,1)S(1)} %all_to_all.27.signal.strip_grad, bf16[512,192]{1,0:T(8,128)(2,1)S(1)} %copy.17.weight.weight_in, bf16[512,256]{1,0:T(8,128)(2,1)S(1)} %copy-done.6, bf16[512,512]{1,0:T(8,128)(2,1)S(1)} %copy-done.5), custom_call_target="tpu_custom_call" | custom-call | bytes 2949120 | tf_op jit(solution)/shard_map/pallas_call | solution.py:30
  (29 shorter events, 0.1 us)
Async XLA Ops:
  0.0 18.1 %collective-permute-start = (bf16[8,128,256]{2,1,0:T(8,128)(2,1)}, bf16[8,128,256]{2,1,0:T(8,128)(2,1)S(1)}, u32[]{:S(2)}, u32[]{:S(2)}) collective-permute-start(bf16[8,128,256]{2,1,0:T(8,128)(2,1)} %features.3), channel_id=1, source_target_pairs={{0,4},{4,8},{8,12},{12,16},{16,20},{20,24},{24,28},{1,5},{5,9},{9,... | collective-permute-start | bytes 1572872 | tf_op jit(solution)/shard_map/ppermute | solution.py:535
  4.5 15.5 %collective-permute-start.1 = (bf16[8,128,256]{2,1,0:T(8,128)(2,1)}, bf16[8,128,256]{2,1,0:T(8,128)(2,1)S(1)}, u32[]{:S(2)}, u32[]{:S(2)}) collective-permute-start(bf16[8,128,256]{2,1,0:T(8,128)(2,1)} %features.3), channel_id=1, source_target_pairs={{4,0},{8,4},{12,8},{16,12},{20,16},{24,20},{28,24},{5,1},{9,5},{13... | collective-permute-start | bytes 1572872 | tf_op jit(solution)/shard_map/ppermute | solution.py:536
  6.4 1.0 copy-start
  7.5 0.7 copy-start.10
  8.2 7.7 %copy-start.2 = (bf16[512,512]{1,0:T(8,128)(2,1)S(1)}, bf16[512,512]{1,0:T(8,128)(2,1)}, u32[]{:S(2)}) copy-start(bf16[512,512]{1,0:T(8,128)(2,1)} %constant.32.clone.table) | copy-start | bytes 1572868
  9.1 10.9 %copy-start.3 = (bf16[8,128,256]{2,1,0:T(8,128)(2,1)S(1)}, bf16[8,128,256]{2,1,0:T(8,128)(2,1)}, u32[]{:S(2)}) copy-start(bf16[8,128,256]{2,1,0:T(8,128)(2,1)} %features.3) | copy-start | bytes 1572868
  9.1 18.1 %collective-permute-start.2 = (bf16[5,128,256]{2,1,0:T(8,128)(2,1)}, bf16[5,128,256]{2,1,0:T(8,128)(2,1)S(1)}, u32[]{:S(2)}, u32[]{:S(2)}) collective-permute-start(bf16[5,128,256]{2,1,0:T(8,128)(2,1)} %get-tuple-element.15), channel_id=1, source_target_pairs={{0,4},{4,8},{8,12},{12,16},{16,20},{20,24},{24,28},{1,5},{5,9},{9,... | collective-permute-start | bytes 983048 | tf_op jit(solution)/shard_map/ppermute | solution.py:538
  12.9 14.3 %collective-permute-start.3 = (bf16[5,128,256]{2,1,0:T(8,128)(2,1)}, bf16[5,128,256]{2,1,0:T(8,128)(2,1)S(1)}, u32[]{:S(2)}, u32[]{:S(2)}) collective-permute-start(bf16[5,128,256]{2,1,0:T(8,128)(2,1)} %get-tuple-element.19), channel_id=1, source_target_pairs={{4,0},{8,4},{12,8},{16,12},{20,16},{24,20},{28,24},{5,1},{9,5},{13... | collective-permute-start | bytes 983048 | tf_op jit(solution)/shard_map/ppermute | solution.py:539
  15.9 1.2 %copy-start.4 = (bf16[2,512,512]{2,1,0:T(8,128)(2,1)S(1)}, bf16[2,512,512]{2,1,0:T(8,128)(2,1)}, u32[]{:S(2)}) copy-start(bf16[2,512,512]{2,1,0:T(8,128)(2,1)} %signal.1) | copy-start | bytes 3145732
  17.1 2.9 %copy-start.11 = (bf16[3,3,256,256]{3,2,1,0:T(8,128)(2,1)S(1)}, bf16[3,3,256,256]{3,2,1,0:T(8,128)(2,1)}, u32[]{:S(2)}) copy-start(bf16[3,3,256,256]{3,2,1,0:T(8,128)(2,1)} %first.7) | copy-start | bytes 3538948
  18.1 9.1 %copy-start.1 = (bf16[8,128,256]{2,1,0:T(8,128)(2,1)S(1)}, bf16[8,128,256]{2,1,0:T(8,128)(2,1)}, u32[]{:S(2)}) copy-start(bf16[8,128,256]{2,1,0:T(8,128)(2,1)} %target.3) | copy-start | bytes 1572868
  20.0 1.3 %copy-start.12 = (bf16[3,3,256,256]{3,2,1,0:T(8,128)(2,1)S(1)}, bf16[3,3,256,256]{3,2,1,0:T(8,128)(2,1)}, u32[]{:S(2)}) copy-start(bf16[3,3,256,256]{3,2,1,0:T(8,128)(2,1)} %second.5) | copy-start | bytes 3538948
  27.3 8.5 %collective-permute-start.4 = (bf16[43,8,256]{2,1,0:T(8,128)(2,1)S(1)}, bf16[43,8,256]{2,1,0:T(8,128)(2,1)S(1)}, u32[]{:S(2)}, u32[]{:S(2)}) collective-permute-start(bf16[43,8,256]{2,1,0:T(8,128)(2,1)S(1)} %get-tuple-element.20), channel_id=1, source_target_pairs={{0,1},{1,2},{2,3},{4,5},{5,6},{6,7},{8,9},{9,10},{10,11},{12,13},{... | collective-permute-start | bytes 528392 | tf_op jit(solution)/shard_map/ppermute | solution.py:543
  30.5 6.2 %collective-permute-start.5 = (bf16[43,8,256]{2,1,0:T(8,128)(2,1)S(1)}, bf16[43,8,256]{2,1,0:T(8,128)(2,1)S(1)}, u32[]{:S(2)}, u32[]{:S(2)}) collective-permute-start(bf16[43,8,256]{2,1,0:T(8,128)(2,1)S(1)} %get-tuple-element.21), channel_id=1, source_target_pairs={{1,0},{2,1},{3,2},{5,4},{6,5},{7,6},{9,8},{10,9},{11,10},{13,12},{... | collective-permute-start | bytes 528392 | tf_op jit(solution)/shard_map/ppermute | solution.py:544
  32.0 4.7 %copy-start.13 = (bf16[3,3,256,256]{3,2,1,0:T(8,128)(2,1)S(1)}, bf16[3,3,256,256]{3,2,1,0:T(8,128)(2,1)}, u32[]{:S(2)}) copy-start(bf16[3,3,256,256]{3,2,1,0:T(8,128)(2,1)} %second.5) | copy-start | bytes 3538948
  35.7 22.6 %copy-start.7 = (bf16[192,256]{1,0:T(8,128)(2,1)S(1)}, bf16[192,256]{1,0:T(8,128)(2,1)}, u32[]{:S(2)}) copy-start(bf16[192,256]{1,0:T(8,128)(2,1)} %weight.2) | copy-start | bytes 294916
  58.3 7.9 %copy-start.14 = (bf16[384,384]{1,0:T(8,128)(2,1)S(1)}, bf16[384,384]{1,0:T(8,128)(2,1)}, u32[]{:S(2)}) copy-start(bf16[384,384]{1,0:T(8,128)(2,1)} %param.23) | copy-start | bytes 884740
  59.9 27.1 %copy-start.8 = (bf16[128,128]{1,0:T(8,128)(2,1)S(1)}, bf16[128,128]{1,0:T(8,128)(2,1)}, u32[]{:S(2)}) copy-start(bf16[128,128]{1,0:T(8,128)(2,1)} %constant.33.clone.back_table) | copy-start | bytes 98308
  59.9 27.1 %copy-start.9 = (bf16[128,128]{1,0:T(8,128)(2,1)S(1)}, bf16[128,128]{1,0:T(8,128)(2,1)}, u32[]{:S(2)}) copy-start(bf16[128,128]{1,0:T(8,128)(2,1)} %constant.34.clone.table) | copy-start | bytes 98308
  59.9 27.1 %all-to-all-start.1 = ((bf16[32,16,768]{2,1,0:T(8,128)(2,1)}), bf16[32,16,768]{2,1,0:T(8,128)(2,1)S(1)}, u32[]{:S(2)}, u32[]{:S(2)}) async-start(bf16[32,16,768]{2,1,0:T(8,128)(2,1)} %bitcast.1), calls=%async_computation.1 | async-start | bytes 1572864 | tf_op jit(solution)/shard_map/all_to_all | solution.py:521
  66.4 38.3 %copy-start.5 = (bf16[512,512]{1,0:T(8,128)(2,1)S(1)}, bf16[512,512]{1,0:T(8,128)(2,1)}, u32[]{:S(2)}) copy-start(bf16[512,512]{1,0:T(8,128)(2,1)} %constant.31.clone.table) | copy-start | bytes 1572868
  66.4 38.3 %copy-start.6 = (bf16[512,256]{1,0:T(8,128)(2,1)S(1)}, bf16[512,256]{1,0:T(8,128)(2,1)}, u32[]{:S(2)}) copy-start(bf16[512,256]{1,0:T(8,128)(2,1)} %weight_local.1) | copy-start | bytes 786436

commit v8 on v7

--- a/solution.py
+++ b/solution.py
@@ -65,20 +65,14 @@
     return jnp.concatenate([signal[block, r] for block in range(signal.shape[0])], axis=0)
 
 
-def strip_spectrum(signal, product, weight, table, norm):
+def strip_spectrum(signal, weight, table, norm):
     count = signal.shape[0 if len(signal.shape) == 3 else 1]
-    rows = [product(strip_row(signal, r), weight[...]).astype(jnp.bfloat16) for r in range(count)]
+    rows = [dot_t(strip_row(signal, r), weight[...]).astype(jnp.bfloat16) for r in range(count)]
     return (dot(table[...], jnp.concatenate(rows, axis=1)) * norm).astype(jnp.bfloat16)
 
 
-def spatial_kernel(norm, signal, weight, table, out):
-    out[...] = strip_spectrum(signal, dot, weight, table, norm)
-
-
-def grad_kernel(norm, signal, weight, table, spatial, out):
-    width = spatial.shape[1]
-    out[:, :width] = spatial[...]
-    out[:, width:] = strip_spectrum(signal, dot_t, weight, table, norm)
+def spectrum_kernel(norm, signal, weight, table, out):
+    out[...] = strip_spectrum(signal, weight, table, norm)
 
 
 def row_spectrum(moved, table, wide, norm, owned, devices):
@@ -101,17 +95,18 @@
     return jnp.concatenate(real, axis=0), jnp.concatenate(imag, axis=0)
 
 
-def mix_kernel(norm, owned, devices, moved, mix, table, back_table, out, wide, wide_grad):
-    width = out.shape[1]
-    parts = row_spectrum(moved.at[:, :width], table, wide, norm, owned, devices)
+def mix_kernel(norm, owned, devices, spatial, grad, mix, table, back_table, out, wide, wide_grad):
+    parts = row_spectrum(spatial, table, wide, norm, owned, devices)
     real, imag = [part.astype(jnp.bfloat16) for part in parts]
-    grads = row_spectrum(moved.at[:, width:], table, wide_grad, norm, owned, devices)
+    grads = row_spectrum(grad, table, wide_grad, norm, owned, devices)
+    half = real.shape[1]
+    spans = (slice(0, half), slice(half, 2 * half))
     mixed = []
-    for part, grad in enumerate(grads):
-        pre = dot(real, mix[0, part]) + dot(imag, mix[1, part])
+    for span, value in zip(spans, grads):
+        pre = dot(real, mix[spans[0], span]) + dot(imag, mix[spans[1], span])
         s = 1.0 / (1.0 + jnp.exp(-pre))
-        mixed.append((grad * (s * (1.0 + pre * (1.0 - s)))).astype(jnp.bfloat16))
-    back = [dot_t(mixed[0], mix[p, 0]) + dot_t(mixed[1], mix[p, 1]) for p in range(2)]
+        mixed.append((value * (s * (1.0 + pre * (1.0 - s)))).astype(jnp.bfloat16))
+    back = [dot_t(mixed[0], mix[p, spans[0]]) + dot_t(mixed[1], mix[p, spans[1]]) for p in spans]
     back = [part.astype(jnp.bfloat16) for part in back]
     height = table.shape[0] // 2
     strip = height // devices
@@ -135,9 +130,9 @@
 
 def output_kernel(norm, moved, strip_grad, weight_in, weight_local, table, out):
     spatial = (dot(table[...], moved[...]) * norm).astype(jnp.bfloat16)
-    half = weight_in.shape[1]
+    half = weight_in.shape[0]
     for r in range(out.shape[0]):
-        total = dot_t(spatial[:, r * half : (r + 1) * half], weight_in[...])
+        total = dot(spatial[:, r * half : (r + 1) * half], weight_in[...])
         total = total + dot_t(strip_row(strip_grad, r), weight_local[...])
         out[r] = total.astype(jnp.bfloat16)
 
@@ -521,9 +516,11 @@
         return lax.all_to_all(spectrum, ("row", "col"), split_axis=0, concat_axis=0, tiled=True)
 
     cells = [jax.ShapeDtypeStruct((width, strip * half), bf16)]
+    weight_in = weight_in.T
     spatial_cols = vmem_call(
-        functools.partial(spatial_kernel, col_norm), cells, inputs, weight_in, table
+        functools.partial(spectrum_kernel, col_norm), cells, inputs, weight_in, table
     )[0]
+    spatial_moved = swap(spatial_cols)
     row0, col0 = lax.axis_index("row") * tile_rows, lax.axis_index("col") * tile_cols
     row_ids = row0 - REACH + jnp.arange(tile_rows + 2 * REACH, dtype=jnp.int32)
     col_ids = col0 - REACH + jnp.arange(tile_cols + 2 * REACH, dtype=jnp.int32)
@@ -537,8 +534,9 @@
     pack_down, pack_up, mask_row = target_packs(target, hole_mask)
     target_above = lax.ppermute(pack_down, "row", up)
     target_below = lax.ppermute(pack_up, "row", down)
+    above, spatial_cols = lax.optimization_barrier((above, spatial_cols))
     pre, slopes = tile_forward(above, features, below, kernel_first, kernel_second, ok)
-    target_above, pre, spatial_cols = lax.optimization_barrier((target_above, pre, spatial_cols))
+    target_above, pre = lax.optimization_barrier((target_above, pre))
     last, initial = edges(above, features, below, target_above, target, mask_row, target_below)
     before = lax.ppermute(last, "col", left)
     after = lax.ppermute(initial, "col", right)
@@ -561,24 +559,21 @@
         ok,
     )
 
+    grad_feat, spatial_moved = lax.optimization_barrier((grad_feat, spatial_moved))
+
     strip_grad = lax.all_to_all(
         grad_feat.reshape(col_devices, strip, tile_cols, channels), "col", split_axis=0, concat_axis=0
     )
-    both_cols = vmem_call(
-        functools.partial(grad_kernel, col_norm),
-        [jax.ShapeDtypeStruct((width, 2 * strip * half), bf16)],
-        strip_grad,
-        weight_out,
-        table,
-        spatial_cols,
+    grad_cols = vmem_call(
+        functools.partial(spectrum_kernel, col_norm), cells, strip_grad, weight_out, table
     )[0]
-    mix = weight_mix.reshape(2, half, 2, half).transpose(0, 2, 1, 3)
     wide = pltpu.VMEM((strip * half // LANES, width, LANES), jnp.float32)
     grad_rows = vmem_call(
         functools.partial(mix_kernel, row_norm, owned, devices),
         cells,
-        swap(both_cols),
-        mix,
+        spatial_moved,
+        swap(grad_cols),
+        weight_mix,
         row_table,
         row_back,
         scratch=[wide, wide],

time: 107 us -> 105 us (0.981)
  waiting for transfers between devices: 23.3 us -> 2.06 us
  blocking collectives: 32.6 us -> 50.1 us
  local copies, waits for them, and re-layouts: 5.6 us -> 7.55 us
    all_to_all x1, waiting for transfers between devices: 20.5 us -> 0.01 us  [swap(): lax.all_to_all(spectrum, ('row', 'col'), split_axis=0, concat_axis=0, til...]
    all_to_all x1 -> x2, blocking collectives: 15.7 us -> 32.3 us  [swap(): lax.all_to_all(spectrum, ('row', 'col'), split_axis=0, concat_axis=0, til...]
    unnamed x31 -> x42, local copies, waits for them, and re-layouts: 5.33 us -> 7.55 us
    ppermute x1, waiting for transfers between devices: 1.87 us -> 0.01 us  [shards(): below = lax.ppermute(features, 'row', down)]
  transfers between devices with their start and end apart: 7 -> 7, of which waited for: 3 -> 2; matrix products, arithmetic and copies ran while one was open for 1% -> 0% of each run, Pallas kernels for 11% -> 16%
where the time goes in v8:
time: 105 us
  blocking collectives  50.1 us (48%)
  starting transfers between devices  22.9 us (22%)
  Pallas kernels  21.6 us (21%)
  local copies, waits for them, and re-layouts  7.55 us (7%)
  waiting for transfers between devices  2.06 us (2%)
    all_to_all x2, blocking collectives, swap(): lax.all_to_all(spectrum, ('row', 'col'), split_axis=0, concat_axis=0, til...  32.3 us
    pallas_call x7, Pallas kernels, vmem_call(): pl.pallas_call(body, out_shape=shapes, in_specs=[spec] * len(operands), o...  20.7 us
    all_to_all x1, blocking collectives, shards(): lax.all_to_all(grad_feat.reshape(col_devices, strip, tile_cols, channels)...  17.8 us
    unnamed x42, local copies, waits for them, and re-layouts  7.55 us
    all_to_all x1, starting transfers between devices, swap(): lax.all_to_all(spectrum, ('row', 'col'), split_axis=0, concat_axis=0, til...  6.22 us
    ppermute x1, starting transfers between devices, shards(): above = lax.ppermute(features, 'row', up)  4.63 us
    ppermute x1, starting transfers between devices, shards(): target_above = lax.ppermute(pack_down, 'row', up)  3.53 us
    ppermute x1, starting transfers between devices, shards(): before = lax.ppermute(last, 'col', left)  3.25 us
  transfers between devices with their start and end apart: 7, of which 2 were waited for; matrix products, arithmetic and copies ran while one was open for 0% of the time, Pallas kernels for 16%

profile of v8, /device:TPU:1, one launch (start us, length us, event | category | flops | bytes accessed | tf_op | source)
XLA Modules:
  0.0 104.6 jit_solution(10595761400767979041)
XLA Ops:
  0.0 4.6 %collective-permute-start = (bf16[8,128,256]{2,1,0:T(8,128)(2,1)}, bf16[8,128,256]{2,1,0:T(8,128)(2,1)S(1)}, u32[]{:S(2)}, u32[]{:S(2)}) collective-permute-start(bf16[8,128,256]{2,1,0:T(8,128)(2,1)} %features.3), channel_id=1, source_target_pairs={{0,4},{4,8},{8,12},{12,16},{16,20},{20,24},{24,28},{1,5},{5,9},{9,... | collective-permute-start | bytes 1572872 | tf_op jit(solution)/shard_map/ppermute | solution.py:532
  4.6 1.9 %collective-permute-start.1 = (bf16[8,128,256]{2,1,0:T(8,128)(2,1)}, bf16[8,128,256]{2,1,0:T(8,128)(2,1)S(1)}, u32[]{:S(2)}, u32[]{:S(2)}) collective-permute-start(bf16[8,128,256]{2,1,0:T(8,128)(2,1)} %features.3), channel_id=1, source_target_pairs={{4,0},{8,4},{12,8},{16,12},{20,16},{24,20},{28,24},{5,1},{9,5},{13... | collective-permute-start | bytes 1572872 | tf_op jit(solution)/shard_map/ppermute | solution.py:533
  6.6 0.0 copy-start.1
  6.6 1.0 copy-done.1
  7.6 1.2 %copy-done.6 = bf16[2,512,512]{2,1,0:T(8,128)(2,1)S(1)} copy-done((bf16[2,512,512]{2,1,0:T(8,128)(2,1)S(1)}, bf16[2,512,512]{2,1,0:T(8,128)(2,1)}, u32[]{:S(2)}) %copy-start.6) | copy-done | bytes 1048600
  8.8 0.9 copy-done.7
  9.8 1.6 %shard_map.136 = bf16[512,384]{1,0:T(8,128)(2,1)} custom-call(bf16[2,512,512]{2,1,0:T(8,128)(2,1)S(1)} %copy-done.6, bf16[192,512]{1,0:T(8,128)(2,1)S(1)} %bitcast.13, bf16[512,512]{1,0:T(8,128)(2,1)S(1)} %copy-done.1), custom_call_target="tpu_custom_call" | custom-call | bytes 2162688 | tf_op jit(solution)/shard_map/pallas_call | solution.py:30
  11.4 6.2 %all-to-all-start = ((bf16[32,16,384]{2,1,0:T(8,128)(2,1)}), bf16[32,16,384]{2,1,0:T(8,128)(2,1)S(1)}, u32[]{:S(2)}, u32[]{:S(2)}) async-start(bf16[32,16,384]{2,1,0:T(8,128)(2,1)} %bitcast.1), calls=%async_computation | async-start | bytes 786432 | tf_op jit(solution)/shard_map/all_to_all | solution.py:516
  17.7 0.9 shard_map.137
  18.6 3.5 %collective-permute-start.2 = (bf16[5,128,256]{2,1,0:T(8,128)(2,1)}, bf16[5,128,256]{2,1,0:T(8,128)(2,1)S(1)}, u32[]{:S(2)}, u32[]{:S(2)}) collective-permute-start(bf16[5,128,256]{2,1,0:T(8,128)(2,1)} %get-tuple-element.18), channel_id=1, source_target_pairs={{0,4},{4,8},{8,12},{12,16},{16,20},{20,24},{24,28},{1,5},{5,9},{9,... | collective-permute-start | bytes 983048 | tf_op jit(solution)/shard_map/ppermute | solution.py:535
  22.1 1.9 %collective-permute-start.3 = (bf16[5,128,256]{2,1,0:T(8,128)(2,1)}, bf16[5,128,256]{2,1,0:T(8,128)(2,1)S(1)}, u32[]{:S(2)}, u32[]{:S(2)}) collective-permute-start(bf16[5,128,256]{2,1,0:T(8,128)(2,1)} %get-tuple-element.22), channel_id=1, source_target_pairs={{4,0},{8,4},{12,8},{16,12},{20,16},{24,20},{28,24},{5,1},{9,5},{13... | collective-permute-start | bytes 983048 | tf_op jit(solution)/shard_map/ppermute | solution.py:536
  24.1 0.1 and_convert_fusion.ok
  24.2 1.3 %copy-done.17 = bf16[3,3,256,256]{3,2,1,0:T(8,128)(2,1)S(1)} copy-done((bf16[3,3,256,256]{3,2,1,0:T(8,128)(2,1)S(1)}, bf16[3,3,256,256]{3,2,1,0:T(8,128)(2,1)}, u32[]{:S(2)}) %copy-start.17) | copy-done | bytes 1179672
  25.5 1.3 %copy-done.19 = bf16[3,3,256,256]{3,2,1,0:T(8,128)(2,1)S(1)} copy-done((bf16[3,3,256,256]{3,2,1,0:T(8,128)(2,1)S(1)}, bf16[3,3,256,256]{3,2,1,0:T(8,128)(2,1)}, u32[]{:S(2)}) %copy-start.19) | copy-done | bytes 1179672
  26.8 5.9 %shard_map.138 = (f32[2048,256]{1,0:T(8,128)S(1)}, f32[1536,256]{1,0:T(8,128)S(1)}) custom-call(bf16[8,128,256]{2,1,0:T(8,128)(2,1)S(1)} %collective-permute-done.above.refs_0_.refs_7_, bf16[8,128,256]{2,1,0:T(8,128)(2,1)S(1)} %copy-done.3, bf16[8,128,256]{2,1,0:T(8,128)(2,1)S(1)} %collective-permute-done.1.below.refs_2_.refs_9_, ...), custom_call_target="tpu_custom_call" | custom-call | flops 5435817984 | bytes 7616000 | tf_op jit(solution)/shard_map/pallas_call | solution.py:30
  32.6 0.4 collective-permute-done.3.refs_6_.refs_13_.target_below
  33.1 3.2 %collective-permute-start.4 = (bf16[43,8,256]{2,1,0:T(8,128)(2,1)S(1)}, bf16[43,8,256]{2,1,0:T(8,128)(2,1)S(1)}, u32[]{:S(2)}, u32[]{:S(2)}) collective-permute-start(bf16[43,8,256]{2,1,0:T(8,128)(2,1)S(1)} %get-tuple-element.23), channel_id=1, source_target_pairs={{0,1},{1,2},{2,3},{4,5},{5,6},{6,7},{8,9},{9,10},{10,11},{12,13},{... | collective-permute-start | bytes 528392 | tf_op jit(solution)/shard_map/ppermute | solution.py:541
  36.3 1.5 %collective-permute-start.5 = (bf16[43,8,256]{2,1,0:T(8,128)(2,1)S(1)}, bf16[43,8,256]{2,1,0:T(8,128)(2,1)S(1)}, u32[]{:S(2)}, u32[]{:S(2)}) collective-permute-start(bf16[43,8,256]{2,1,0:T(8,128)(2,1)S(1)} %get-tuple-element.24), channel_id=1, source_target_pairs={{1,0},{2,1},{3,2},{5,4},{6,5},{7,6},{9,8},{10,9},{11,10},{13,12},{... | collective-permute-start | bytes 528392 | tf_op jit(solution)/shard_map/ppermute | solution.py:542
  37.9 3.7 %shard_map.140.tile = bf16[8,128,256]{2,1,0:T(8,128)(2,1)S(1)} custom-call(f32[2048,256]{1,0:T(8,128)S(1)} %get-tuple-element.25.pre, f32[1536,256]{1,0:T(8,128)S(1)} %get-tuple-element.26.slopes, bf16[5,128,256]{2,1,0:T(8,128)(2,1)S(1)} %collective-permute-done.2.refs_3_.refs_10_.target_above, bf16[8,128,256]{2,1,0:T(8,128)(2,1)S(1)} %copy-done, ...), custom_call_target="tpu_custom_call" | custom-call | flops 3019898880 | bytes 7812608 | tf_op jit(solution)/shard_map/pallas_call | solution.py:30
  41.6 0.0 copy-start.2
  41.6 1.6 %collective-permute-done.5.after = bf16[43,8,256]{2,1,0:T(8,128)(2,1)S(1)} collective-permute-done((bf16[43,8,256]{2,1,0:T(8,128)(2,1)S(1)}, bf16[43,8,256]{2,1,0:T(8,128)(2,1)S(1)}, u32[]{:S(2)}, u32[]{:S(2)}) %collective-permute-start.5) | collective-permute-done | bytes 176160 | tf_op jit(solution)/shard_map/ppermute | solution.py:542
  43.2 1.0 copy-done.5
  44.2 4.7 %shard_map.141 = bf16[8,128,256]{2,1,0:T(8,128)(2,1)S(1)} custom-call(bf16[43,8,256]{2,1,0:T(8,128)(2,1)S(1)} %collective-permute-done.4.before, bf16[43,8,256]{2,1,0:T(8,128)(2,1)S(1)} %collective-permute-done.5.after, bf16[8,128,256]{2,1,0:T(8,128)(2,1)S(1)} %collective-permute-done.above.refs_0_.refs_7_, bf16[8,128,256]{2,1,0:T(8,128)(2,1)S(1)} %copy-done.3, ...), custom_call_target="tpu_custom_call" | custom-call | flops 3170893824 | bytes 6592000 | tf_op jit(solution)/shard_map/pallas_call | solution.py:30
  48.9 0.0 copy-start.9
  48.9 0.8 copy-done.9
  49.7 17.8 %all_to_all.39.signal.strip_grad = bf16[4,2,128,256]{3,2,1,0:T(8,128)(2,1)S(1)} all-to-all(bf16[4,2,128,256]{3,2,1,0:T(8,128)(2,1)} %bitcast.15), channel_id=1, replica_groups=mesh['row'=8,'col'=4] {'col'}, dimensions={0} | all-to-all | bytes 1048576 | tf_op jit(solution)/shard_map/all_to_all | solution.py:564
  67.5 0.7 shard_map.142
  68.3 0.0 copy-start.10
  68.3 16.8 %all_to_all.40 = bf16[32,16,384]{2,1,0:T(8,128)(2,1)S(1)} all-to-all(bf16[32,16,384]{2,1,0:T(8,128)(2,1)S(1)} %bitcast.11), channel_id=1, replica_groups=mesh['row'=8,'col'=4] {'row','col'}, dimensions={0} | all-to-all | bytes 786432 | tf_op jit(solution)/shard_map/all_to_all | solution.py:516
  85.1 2.1 %shard_map.143 = bf16[512,384]{1,0:T(8,128)(2,1)S(1)} custom-call(bf16[512,384]{1,0:T(8,128)(2,1)S(1)} %bitcast.8, bf16[512,384]{1,0:T(8,128)(2,1)S(1)} %bitcast.9, bf16[384,384]{1,0:T(8,128)(2,1)S(1)} %copy-done.11, bf16[128,128]{1,0:T(8,128)(2,1)S(1)} %copy-done.14, bf16[128,128]{1,0:T(8,128)(2,1)S(1)} %copy-done.15), custom_call_target="tpu_custom_call" | custom-call | bytes 1540096 | tf_op jit(solution)/shard_map/pallas_call | solution.py:30
  87.2 15.5 %all_to_all.41 = bf16[32,16,384]{2,1,0:T(8,128)(2,1)S(1)} all-to-all(bf16[32,16,384]{2,1,0:T(8,128)(2,1)S(1)} %bitcast.10), channel_id=1, replica_groups=mesh['row'=8,'col'=4] {'row','col'}, dimensions={0} | all-to-all | bytes 786432 | tf_op jit(solution)/shard_map/all_to_all | solution.py:516
  102.7 2.0 %shard_map.144 = bf16[2,512,512]{2,1,0:T(8,128)(2,1)} custom-call(bf16[512,384]{1,0:T(8,128)(2,1)S(1)} %bitcast.12, bf16[4,2,128,256]{3,2,1,0:T(8,128)(2,1)S(1)} %all_to_all.39.signal.strip_grad, bf16[192,512]{1,0:T(8,128)(2,1)S(1)} %bitcast.14, bf16[512,256]{1,0:T(8,128)(2,1)S(1)} %copy-done.12, bf16[512,512]{1,0:T(8,128)(2,1)S(1)} %copy-done.10), custom_call_target="tpu_custom_call" | custom-call | bytes 2949120 | tf_op jit(solution)/shard_map/pallas_call | solution.py:30
  (39 shorter events, 0.1 us)
Async XLA Ops:
  0.0 17.6 %copy-start = (bf16[8,128,256]{2,1,0:T(8,128)(2,1)S(1)}, bf16[8,128,256]{2,1,0:T(8,128)(2,1)}, u32[]{:S(2)}) copy-start(bf16[8,128,256]{2,1,0:T(8,128)(2,1)} %target.3) | copy-start | bytes 1572868
  0.0 24.2 %collective-permute-start = (bf16[8,128,256]{2,1,0:T(8,128)(2,1)}, bf16[8,128,256]{2,1,0:T(8,128)(2,1)S(1)}, u32[]{:S(2)}, u32[]{:S(2)}) collective-permute-start(bf16[8,128,256]{2,1,0:T(8,128)(2,1)} %features.3), channel_id=1, source_target_pairs={{0,4},{4,8},{8,12},{12,16},{16,20},{20,24},{24,28},{1,5},{5,9},{9,... | collective-permute-start | bytes 1572872 | tf_op jit(solution)/shard_map/ppermute | solution.py:532
  4.6 19.6 %collective-permute-start.1 = (bf16[8,128,256]{2,1,0:T(8,128)(2,1)}, bf16[8,128,256]{2,1,0:T(8,128)(2,1)S(1)}, u32[]{:S(2)}, u32[]{:S(2)}) collective-permute-start(bf16[8,128,256]{2,1,0:T(8,128)(2,1)} %features.3), channel_id=1, source_target_pairs={{4,0},{8,4},{12,8},{16,12},{20,16},{24,20},{28,24},{5,1},{9,5},{13... | collective-permute-start | bytes 1572872 | tf_op jit(solution)/shard_map/ppermute | solution.py:533
  6.6 1.0 copy-start.1
  7.6 1.2 %copy-start.6 = (bf16[2,512,512]{2,1,0:T(8,128)(2,1)S(1)}, bf16[2,512,512]{2,1,0:T(8,128)(2,1)}, u32[]{:S(2)}) copy-start(bf16[2,512,512]{2,1,0:T(8,128)(2,1)} %signal.1) | copy-start | bytes 3145732
  8.8 0.9 copy-start.7
  9.8 7.9 %copy-start.16 = (s32[8,128]{1,0:T(8,128)S(1)}, s32[8,128]{1,0:T(8,128)}, u32[]{:S(2)}) copy-start(s32[8,128]{1,0:T(8,128)} %mask.1) | copy-start | bytes 12292
  9.8 14.4 %copy-start.3 = (bf16[8,128,256]{2,1,0:T(8,128)(2,1)S(1)}, bf16[8,128,256]{2,1,0:T(8,128)(2,1)}, u32[]{:S(2)}) copy-start(bf16[8,128,256]{2,1,0:T(8,128)(2,1)} %features.3) | copy-start | bytes 1572868
  11.4 38.3 %all-to-all-start = ((bf16[32,16,384]{2,1,0:T(8,128)(2,1)}), bf16[32,16,384]{2,1,0:T(8,128)(2,1)S(1)}, u32[]{:S(2)}, u32[]{:S(2)}) async-start(bf16[32,16,384]{2,1,0:T(8,128)(2,1)} %bitcast.1), calls=%async_computation | async-start | bytes 786432 | tf_op jit(solution)/shard_map/all_to_all | solution.py:516
  18.6 14.0 %collective-permute-start.2 = (bf16[5,128,256]{2,1,0:T(8,128)(2,1)}, bf16[5,128,256]{2,1,0:T(8,128)(2,1)S(1)}, u32[]{:S(2)}, u32[]{:S(2)}) collective-permute-start(bf16[5,128,256]{2,1,0:T(8,128)(2,1)} %get-tuple-element.18), channel_id=1, source_target_pairs={{0,4},{4,8},{8,12},{12,16},{16,20},{20,24},{24,28},{1,5},{5,9},{9,... | collective-permute-start | bytes 983048 | tf_op jit(solution)/shard_map/ppermute | solution.py:535
  22.1 10.9 %collective-permute-start.3 = (bf16[5,128,256]{2,1,0:T(8,128)(2,1)}, bf16[5,128,256]{2,1,0:T(8,128)(2,1)S(1)}, u32[]{:S(2)}, u32[]{:S(2)}) collective-permute-start(bf16[5,128,256]{2,1,0:T(8,128)(2,1)} %get-tuple-element.22), channel_id=1, source_target_pairs={{4,0},{8,4},{12,8},{16,12},{20,16},{24,20},{28,24},{5,1},{9,5},{13... | collective-permute-start | bytes 983048 | tf_op jit(solution)/shard_map/ppermute | solution.py:536
  24.2 1.3 %copy-start.17 = (bf16[3,3,256,256]{3,2,1,0:T(8,128)(2,1)S(1)}, bf16[3,3,256,256]{3,2,1,0:T(8,128)(2,1)}, u32[]{:S(2)}) copy-start(bf16[3,3,256,256]{3,2,1,0:T(8,128)(2,1)} %first.7) | copy-start | bytes 3538948
  25.5 1.3 %copy-start.19 = (bf16[3,3,256,256]{3,2,1,0:T(8,128)(2,1)S(1)}, bf16[3,3,256,256]{3,2,1,0:T(8,128)(2,1)}, u32[]{:S(2)}) copy-start(bf16[3,3,256,256]{3,2,1,0:T(8,128)(2,1)} %second.5) | copy-start | bytes 3538948
  33.0 4.8 %copy-start.4 = (bf16[5,128,256]{2,1,0:T(8,128)(2,1)}, bf16[5,128,256]{2,1,0:T(8,128)(2,1)S(1)}, u32[]{:S(2)}) copy-start(bf16[5,128,256]{2,1,0:T(8,128)(2,1)S(1)} %collective-permute-done.3.refs_6_.refs_13_.target_below) | copy-start | bytes 983044
  33.0 4.8 %copy-start.18 = (bf16[3,3,256,256]{3,2,1,0:T(8,128)(2,1)S(1)}, bf16[3,3,256,256]{3,2,1,0:T(8,128)(2,1)}, u32[]{:S(2)}) copy-start(bf16[3,3,256,256]{3,2,1,0:T(8,128)(2,1)} %first.7) | copy-start | bytes 3538948
  33.0 4.8 %copy-start.20 = (bf16[3,3,256,256]{3,2,1,0:T(8,128)(2,1)S(1)}, bf16[3,3,256,256]{3,2,1,0:T(8,128)(2,1)}, u32[]{:S(2)}) copy-start(bf16[3,3,256,256]{3,2,1,0:T(8,128)(2,1)} %second.5) | copy-start | bytes 3538948
  33.1 8.5 %collective-permute-start.4 = (bf16[43,8,256]{2,1,0:T(8,128)(2,1)S(1)}, bf16[43,8,256]{2,1,0:T(8,128)(2,1)S(1)}, u32[]{:S(2)}, u32[]{:S(2)}) collective-permute-start(bf16[43,8,256]{2,1,0:T(8,128)(2,1)S(1)} %get-tuple-element.23), channel_id=1, source_target_pairs={{0,1},{1,2},{2,3},{4,5},{5,6},{6,7},{8,9},{9,10},{10,11},{12,13},{... | collective-permute-start | bytes 528392 | tf_op jit(solution)/shard_map/ppermute | solution.py:541
  36.3 6.9 %collective-permute-start.5 = (bf16[43,8,256]{2,1,0:T(8,128)(2,1)S(1)}, bf16[43,8,256]{2,1,0:T(8,128)(2,1)S(1)}, u32[]{:S(2)}, u32[]{:S(2)}) collective-permute-start(bf16[43,8,256]{2,1,0:T(8,128)(2,1)S(1)} %get-tuple-element.24), channel_id=1, source_target_pairs={{1,0},{2,1},{3,2},{5,4},{6,5},{7,6},{9,8},{10,9},{11,10},{13,12},{... | collective-permute-start | bytes 528392 | tf_op jit(solution)/shard_map/ppermute | solution.py:542
  37.8 29.7 %copy-start.13 = (bf16[192,256]{1,0:T(8,128)(2,1)S(1)}, bf16[192,256]{1,0:T(8,128)(2,1)}, u32[]{:S(2)}) copy-start(bf16[192,256]{1,0:T(8,128)(2,1)} %weight.1) | copy-start | bytes 294916
  41.6 25.9 %copy-start.2 = (bf16[512,512]{1,0:T(8,128)(2,1)S(1)}, bf16[512,512]{1,0:T(8,128)(2,1)}, u32[]{:S(2)}) copy-start(bf16[512,512]{1,0:T(8,128)(2,1)} %constant.32.clone.table) | copy-start | bytes 1572868
  43.2 1.0 copy-start.5
  48.9 0.8 copy-start.9
  49.7 35.4 %copy-start.11 = (bf16[384,384]{1,0:T(8,128)(2,1)S(1)}, bf16[384,384]{1,0:T(8,128)(2,1)}, u32[]{:S(2)}) copy-start(bf16[384,384]{1,0:T(8,128)(2,1)} %mix.1) | copy-start | bytes 884740
  49.7 35.4 %copy-start.14 = (bf16[128,128]{1,0:T(8,128)(2,1)S(1)}, bf16[128,128]{1,0:T(8,128)(2,1)}, u32[]{:S(2)}) copy-start(bf16[128,128]{1,0:T(8,128)(2,1)} %constant.34.clone.table) | copy-start | bytes 98308
  49.7 35.4 %copy-start.15 = (bf16[128,128]{1,0:T(8,128)(2,1)S(1)}, bf16[128,128]{1,0:T(8,128)(2,1)}, u32[]{:S(2)}) copy-start(bf16[128,128]{1,0:T(8,128)(2,1)} %constant.33.clone.back_table) | copy-start | bytes 98308
  68.3 34.4 %copy-start.8 = (bf16[512,192]{0,1:T(8,128)(2,1)S(1)}, bf16[512,192]{0,1:T(8,128)(2,1)}, u32[]{:S(2)}) copy-start(bf16[512,192]{0,1:T(8,128)(2,1)} %param.20) | copy-start | bytes 589828
  68.3 34.4 %copy-start.10 = (bf16[512,512]{1,0:T(8,128)(2,1)S(1)}, bf16[512,512]{1,0:T(8,128)(2,1)}, u32[]{:S(2)}) copy-start(bf16[512,512]{1,0:T(8,128)(2,1)} %constant.31.clone.table) | copy-start | bytes 1572868
  68.3 34.4 %copy-start.12 = (bf16[512,256]{1,0:T(8,128)(2,1)S(1)}, bf16[512,256]{1,0:T(8,128)(2,1)}, u32[]{:S(2)}) copy-start(bf16[512,256]{1,0:T(8,128)(2,1)} %weight_local.1) | copy-start | bytes 786436

commit v9 on v8

--- a/solution.py
+++ b/solution.py
@@ -38,6 +38,10 @@
     )(*operands)
 
 
+def in_hbm(array):
+    return pltpu.with_memory_space_constraint(array, pltpu.HBM)
+
+
 def phases(first, second, length):
     angle = (first[:, None] * second[None, :] % length) * (2.0 * math.pi / length)
     return np.cos(angle).astype(ml_dtypes.bfloat16), np.sin(angle).astype(ml_dtypes.bfloat16)
@@ -52,9 +56,11 @@
     return np.ascontiguousarray(both.transpose(1, 0, 2, 3)).reshape(width, width)
 
 
-def row_matrix(height, devices):
+def row_matrix(height, row_devices, col_devices):
+    devices = row_devices * col_devices
     strip = height // devices
-    rows = (np.arange(devices)[None, :] * strip + np.arange(strip)[:, None]).reshape(-1)
+    strips = np.arange(devices).reshape(row_devices, col_devices).T.reshape(-1)
+    rows = (strips[None, :] * strip + np.arange(strip)[:, None]).reshape(-1)
     cos, sin = phases(np.arange(height), rows, height)
     return np.block([[cos, sin], [-sin, cos]])
 
@@ -73,6 +79,40 @@
 
 def spectrum_kernel(norm, signal, weight, table, out):
     out[...] = strip_spectrum(signal, weight, table, norm)
+
+
+def fetching_spectrum_kernel(norm, signal, weight, table, out, signal_held, weight_held, table_held, sems):
+    count = signal.shape[0]
+    copies = [pltpu.make_async_copy(weight, weight_held, sems.at[0])]
+    copies += [
+        pltpu.make_async_copy(signal.at[r], signal_held.at[r], sems.at[1 + r]) for r in range(count)
+    ]
+    copies.append(pltpu.make_async_copy(table, table_held, sems.at[1 + count]))
+    for copy in copies:
+        copy.start()
+    copies[0].wait()
+    rows = []
+    for r in range(count):
+        copies[1 + r].wait()
+        rows.append(dot_t(signal_held[r], weight_held[...]).astype(jnp.bfloat16))
+    copies[-1].wait()
+    out[...] = (dot(table_held[...], jnp.concatenate(rows, axis=1)) * norm).astype(jnp.bfloat16)
+
+
+def fetching_spectrum(norm, shape, signal, weight, table):
+    operands = (signal, weight, table)
+    return pl.pallas_call(
+        functools.partial(fetching_spectrum_kernel, norm),
+        out_shape=shape,
+        in_specs=[pl.BlockSpec(memory_space=pltpu.HBM)] * 3,
+        out_specs=pl.BlockSpec(memory_space=pltpu.VMEM),
+        scratch_shapes=[pltpu.VMEM(a.shape, a.dtype) for a in operands]
+        + [pltpu.SemaphoreType.DMA((signal.shape[0] + 2,))],
+        compiler_params=pltpu.CompilerParams(vmem_limit_bytes=12 * MIB),
+        cost_estimate=pl.CostEstimate(
+            flops=0, bytes_accessed=2 * MIB, transcendentals=0
+        ),
+    )(*[in_hbm(a) for a in operands])
 
 
 def row_spectrum(moved, table, wide, norm, owned, devices):
@@ -233,10 +273,14 @@
     return jnp.concatenate([piece(row) for row in rows], axis=0)
 
 
-def first_stages(stride, blocks, rows, feature, inside, first, second, wide_even, wide_odd, slopes, use):
+def first_stages(
+    stride, blocks, rows, feature, inside, first, second, wide_even, wide_odd, slopes, use, ready=None
+):
+    ready = ready or (lambda which: None)
     tall = rows + 2 * REACH
     for row in range(0, tall, NEAR):
         put(wide_even, row, stacked(feature, range(row, row + NEAR)), stride)
+    ready(0)
     count = blocks[0]
     for row in range(0, tall - 4, count):
         pre = conv(wide_even, row, count, stride, first)
@@ -248,6 +292,7 @@
             part = slice((low - row) * stride, (high - row) * stride)
             slope = (s * (1.0 + pre * (1.0 - s)) * kept)[part]
             slopes[pl.ds((low - NEAR) * stride, (high - low) * stride), :] = slope
+    ready(1)
     count = blocks[1]
     for row in range(0, rows + 2 * NEAR, count):
         use(row, count, conv(wide_odd, row, count, stride, second))
@@ -285,8 +330,19 @@
 SIDE_BLOCKS = (10, 8, 12, 8)
 
 
-def tile_forward_kernel(above, features, below, first, second, ok, pre, slopes, wide_even, wide_odd):
+def tile_forward_kernel(
+    above, features, below, first, second, ok, pre, slopes, wide_even, wide_odd, kernels, sems
+):
     rows, stride, _ = features.shape
+    copies = [
+        pltpu.make_async_copy(source, kernels.at[i], sems.at[i]) for i, source in enumerate((first, second))
+    ]
+    for copy in copies:
+        copy.start()
+
+    def ready(which):
+        copies[which].wait()
+
     find = part_of(rows, REACH, above, features, below)
 
     def feature(row):
@@ -300,7 +356,18 @@
         pre[pl.ds(row * stride, count * stride), :] = value
 
     first_stages(
-        stride, TILE_BLOCKS, rows, feature, inside, first, second, wide_even, wide_odd, slopes, use
+        stride,
+        TILE_BLOCKS,
+        rows,
+        feature,
+        inside,
+        kernels.at[0],
+        kernels.at[1],
+        wide_even,
+        wide_odd,
+        slopes,
+        use,
+        ready,
     )
 
 
@@ -429,19 +496,24 @@
     shapes = [
         jax.ShapeDtypeStruct(((rows + h) * stride, channels), jnp.float32) for h in (2 * NEAR, 4)
     ]
-    return vmem_call(
+    in_vmem, hbm = pl.BlockSpec(memory_space=pltpu.VMEM), pl.BlockSpec(memory_space=pltpu.HBM)
+    return pl.pallas_call(
         tile_forward_kernel,
-        shapes,
-        above,
-        features,
-        below,
-        first,
-        second,
-        ok,
-        flops=2 * 9 * channels * channels * stride * (2 * rows + 20),
-        scratch=[wide_buffer(rows + h, stride, channels) for h in (16, 12)],
-        limit=18,
-    )
+        out_shape=shapes,
+        in_specs=[in_vmem] * 3 + [hbm] * 2 + [in_vmem],
+        out_specs=[in_vmem] * 2,
+        scratch_shapes=[
+            *[wide_buffer(rows + h, stride, channels) for h in (16, 12)],
+            pltpu.VMEM((2, *first.shape), first.dtype),
+            pltpu.SemaphoreType.DMA((2,)),
+        ],
+        compiler_params=pltpu.CompilerParams(vmem_limit_bytes=20 * MIB),
+        cost_estimate=pl.CostEstimate(
+            flops=2 * 9 * channels * channels * stride * (2 * rows + 20),
+            bytes_accessed=8 * MIB,
+            transcendentals=0,
+        ),
+    )(above, features, below, in_hbm(first), in_hbm(second), ok)
 
 
 def tile_backward(pre, slopes, target_above, target, target_below, mask_row, first, second, ok):
@@ -507,19 +579,17 @@
     table = column_matrix(width, devices)
     table_back = jnp.asarray(np.ascontiguousarray(table.T))
     table = jnp.asarray(table)
-    row_table = row_matrix(height, devices)
+    row_table = row_matrix(height, row_devices, col_devices)
     row_back = jnp.asarray(np.ascontiguousarray(row_table.T))
     row_table = jnp.asarray(row_table)
     bf16 = jnp.bfloat16
 
     def swap(spectrum):
-        return lax.all_to_all(spectrum, ("row", "col"), split_axis=0, concat_axis=0, tiled=True)
+        return lax.all_to_all(spectrum, ("col", "row"), split_axis=0, concat_axis=0, tiled=True)
 
     cells = [jax.ShapeDtypeStruct((width, strip * half), bf16)]
     weight_in = weight_in.T
-    spatial_cols = vmem_call(
-        functools.partial(spectrum_kernel, col_norm), cells, inputs, weight_in, table
-    )[0]
+    spatial_cols = fetching_spectrum(col_norm, cells[0], inputs, weight_in, table)
     spatial_moved = swap(spatial_cols)
     row0, col0 = lax.axis_index("row") * tile_rows, lax.axis_index("col") * tile_cols
     row_ids = row0 - REACH + jnp.arange(tile_rows + 2 * REACH, dtype=jnp.int32)

time: 105 us -> 104 us (level)
  local copies, waits for them, and re-layouts: 7.55 us -> 1.83 us
  Pallas kernels: 21.6 us -> 25.4 us
    pallas_call x0 -> x2, Pallas kernels: none -> 11.3 us  [the longest x1 7.94 us: tile_forward(): pl.pallas_call(tile_forward_kernel, out_shape=shapes, in_specs=[in_vmem]...]
    pallas_call x7 -> x5, Pallas kernels: 20.7 us -> 13.2 us  [vmem_call(): pl.pallas_call(body, out_shape=shapes, in_specs=[spec] * len(operands), o...]
    unnamed x42 -> x32, local copies, waits for them, and re-layouts: 7.55 us -> 1.83 us
  transfers between devices with their start and end apart: 7 -> 7, of which waited for: 2 -> 2; matrix products, arithmetic and copies ran while one was open for 0% -> 0% of each run, Pallas kernels for 16% -> 20%
where the time goes in v9:
time: 104 us; the launch traced here: 103 us
  blocking collectives  50.2 us (48%)
  Pallas kernels  25.4 us (24%)
  starting transfers between devices  23.3 us (22%)
  local copies, waits for them, and re-layouts  1.83 us (2%)
  waiting for transfers between devices  1.73 us (2%)
    all_to_all x2, blocking collectives, swap(): lax.all_to_all(spectrum, ('col', 'row'), split_axis=0, concat_axis=0, til...  31.6 us
    all_to_all x1, blocking collectives, shards(): lax.all_to_all(grad_feat.reshape(col_devices, strip, tile_cols, channels)...  18.6 us
    pallas_call x5, Pallas kernels, vmem_call(): pl.pallas_call(body, out_shape=shapes, in_specs=[spec] * len(operands), o...  13.2 us
    pallas_call x1, Pallas kernels, tile_forward(): pl.pallas_call(tile_forward_kernel, out_shape=shapes, in_specs=[in_vmem]...  7.94 us
    all_to_all x1, starting transfers between devices, swap(): lax.all_to_all(spectrum, ('col', 'row'), split_axis=0, concat_axis=0, til...  6.24 us
    ppermute x1, starting transfers between devices, shards(): above = lax.ppermute(features, 'row', up)  4.63 us
    ppermute x1, starting transfers between devices, shards(): before = lax.ppermute(last, 'col', left)  3.59 us
    ppermute x1, starting transfers between devices, shards(): target_above = lax.ppermute(pack_down, 'row', up)  3.53 us
  transfers between devices with their start and end apart: 7, of which 2 were waited for; matrix products, arithmetic and copies ran while one was open for 0% of the time, Pallas kernels for 20%

profile of v9, /device:TPU:1, one launch (start us, length us, event | category | flops | bytes accessed | tf_op | source)
XLA Modules:
  0.0 102.9 jit_solution(17380442279930121539)
XLA Ops:
  0.0 4.6 %collective-permute-start = (bf16[8,128,256]{2,1,0:T(8,128)(2,1)}, bf16[8,128,256]{2,1,0:T(8,128)(2,1)S(1)}, u32[]{:S(2)}, u32[]{:S(2)}) collective-permute-start(bf16[8,128,256]{2,1,0:T(8,128)(2,1)} %features.3), channel_id=1, source_target_pairs={{0,4},{4,8},{8,12},{12,16},{16,20},{20,24},{24,28},{1,5},{5,9},{9,... | collective-permute-start | bytes 1572872 | tf_op jit(solution)/shard_map/ppermute | solution.py:602
  4.6 1.9 %collective-permute-start.1 = (bf16[8,128,256]{2,1,0:T(8,128)(2,1)}, bf16[8,128,256]{2,1,0:T(8,128)(2,1)S(1)}, u32[]{:S(2)}, u32[]{:S(2)}) collective-permute-start(bf16[8,128,256]{2,1,0:T(8,128)(2,1)} %features.3), channel_id=1, source_target_pairs={{4,0},{8,4},{12,8},{16,12},{20,16},{24,20},{28,24},{5,1},{9,5},{13... | collective-permute-start | bytes 1572872 | tf_op jit(solution)/shard_map/ppermute | solution.py:603
  6.6 3.4 %shard_map.136 = bf16[512,384]{1,0:T(8,128)(2,1)} custom-call(bf16[2,512,512]{2,1,0:T(8,128)(2,1)} %signal.1, bf16[192,512]{1,0:T(8,128)(2,1)} %bitcast.13, bf16[512,512]{1,0:T(8,128)(2,1)} %constant.32.clone.table), custom_call_target="tpu_custom_call" | custom-call | bytes 2097152 | tf_op jit(solution)/shard_map/pallas_call | solution.py:104
  9.9 6.2 %all-to-all-start = ((bf16[32,16,384]{2,1,0:T(8,128)(2,1)}), bf16[32,16,384]{2,1,0:T(8,128)(2,1)S(1)}, u32[]{:S(2)}, u32[]{:S(2)}) async-start(bf16[32,16,384]{2,1,0:T(8,128)(2,1)} %bitcast.1), calls=%async_computation | async-start | bytes 786432 | tf_op jit(solution)/shard_map/all_to_all | solution.py:588
  16.2 0.9 shard_map.137
  17.2 3.5 %collective-permute-start.2 = (bf16[5,128,256]{2,1,0:T(8,128)(2,1)}, bf16[5,128,256]{2,1,0:T(8,128)(2,1)S(1)}, u32[]{:S(2)}, u32[]{:S(2)}) collective-permute-start(bf16[5,128,256]{2,1,0:T(8,128)(2,1)} %get-tuple-element.18), channel_id=1, source_target_pairs={{0,4},{4,8},{8,12},{12,16},{16,20},{20,24},{24,28},{1,5},{5,9},{9,... | collective-permute-start | bytes 983048 | tf_op jit(solution)/shard_map/ppermute | solution.py:605
  20.7 1.9 %collective-permute-start.3 = (bf16[5,128,256]{2,1,0:T(8,128)(2,1)}, bf16[5,128,256]{2,1,0:T(8,128)(2,1)S(1)}, u32[]{:S(2)}, u32[]{:S(2)}) collective-permute-start(bf16[5,128,256]{2,1,0:T(8,128)(2,1)} %get-tuple-element.22), channel_id=1, source_target_pairs={{4,0},{8,4},{12,8},{16,12},{20,16},{24,20},{28,24},{5,1},{9,5},{13... | collective-permute-start | bytes 983048 | tf_op jit(solution)/shard_map/ppermute | solution.py:606
  22.7 0.1 and_convert_fusion.ok
  22.7 0.0 collective-permute-done.above.refs_0_.refs_7_
  22.8 7.9 %shard_map.138 = (f32[2048,256]{1,0:T(8,128)S(1)}, f32[1536,256]{1,0:T(8,128)S(1)}) custom-call(bf16[8,128,256]{2,1,0:T(8,128)(2,1)S(1)} %collective-permute-done.above.refs_0_.refs_7_, bf16[8,128,256]{2,1,0:T(8,128)(2,1)S(1)} %copy-done.2, bf16[8,128,256]{2,1,0:T(8,128)(2,1)S(1)} %collective-permute-done.1.below.refs_2_.refs_9_, ...), custom_call_target="tpu_custom_call" | custom-call | flops 5435817984 | bytes 8388608 | tf_op jit(solution)/shard_map/pallas_call | solution.py:500
  30.7 0.5 collective-permute-done.3.refs_6_.refs_13_.target_below
  31.3 3.6 %collective-permute-start.4 = (bf16[43,8,256]{2,1,0:T(8,128)(2,1)S(1)}, bf16[43,8,256]{2,1,0:T(8,128)(2,1)S(1)}, u32[]{:S(2)}, u32[]{:S(2)}) collective-permute-start(bf16[43,8,256]{2,1,0:T(8,128)(2,1)S(1)} %get-tuple-element.23), channel_id=1, source_target_pairs={{0,1},{1,2},{2,3},{4,5},{5,6},{6,7},{8,9},{9,10},{10,11},{12,13},{... | collective-permute-start | bytes 528392 | tf_op jit(solution)/shard_map/ppermute | solution.py:611
  34.9 1.5 %collective-permute-start.5 = (bf16[43,8,256]{2,1,0:T(8,128)(2,1)S(1)}, bf16[43,8,256]{2,1,0:T(8,128)(2,1)S(1)}, u32[]{:S(2)}, u32[]{:S(2)}) collective-permute-start(bf16[43,8,256]{2,1,0:T(8,128)(2,1)S(1)} %get-tuple-element.24), channel_id=1, source_target_pairs={{1,0},{2,1},{3,2},{5,4},{6,5},{7,6},{9,8},{10,9},{11,10},{13,12},{... | collective-permute-start | bytes 528392 | tf_op jit(solution)/shard_map/ppermute | solution.py:612
  36.4 0.0 copy-start.10
  36.4 3.7 %shard_map.140.tile = bf16[8,128,256]{2,1,0:T(8,128)(2,1)S(1)} custom-call(f32[2048,256]{1,0:T(8,128)S(1)} %get-tuple-element.25.pre, f32[1536,256]{1,0:T(8,128)S(1)} %get-tuple-element.26.slopes, bf16[5,128,256]{2,1,0:T(8,128)(2,1)S(1)} %collective-permute-done.2.refs_3_.refs_10_.target_above, bf16[8,128,256]{2,1,0:T(8,128)(2,1)S(1)} %copy-done, ...), custom_call_target="tpu_custom_call" | custom-call | flops 3019898880 | bytes 7812608 | tf_op jit(solution)/shard_map/pallas_call | solution.py:30
  40.1 0.0 copy-start.1
  40.1 0.0 collective-permute-done.4.before
  40.1 1.2 %collective-permute-done.5.after = bf16[43,8,256]{2,1,0:T(8,128)(2,1)S(1)} collective-permute-done((bf16[43,8,256]{2,1,0:T(8,128)(2,1)S(1)}, bf16[43,8,256]{2,1,0:T(8,128)(2,1)S(1)}, u32[]{:S(2)}, u32[]{:S(2)}) %collective-permute-start.5) | collective-permute-done | bytes 176160 | tf_op jit(solution)/shard_map/ppermute | solution.py:612
  41.4 1.0 copy-done.4
  42.3 4.7 %shard_map.141 = bf16[8,128,256]{2,1,0:T(8,128)(2,1)S(1)} custom-call(bf16[43,8,256]{2,1,0:T(8,128)(2,1)S(1)} %collective-permute-done.4.before, bf16[43,8,256]{2,1,0:T(8,128)(2,1)S(1)} %collective-permute-done.5.after, bf16[8,128,256]{2,1,0:T(8,128)(2,1)S(1)} %collective-permute-done.above.refs_0_.refs_7_, bf16[8,128,256]{2,1,0:T(8,128)(2,1)S(1)} %copy-done.2, ...), custom_call_target="tpu_custom_call" | custom-call | flops 3170893824 | bytes 6592000 | tf_op jit(solution)/shard_map/pallas_call | solution.py:30
  47.1 0.0 copy-start.6
  47.1 0.8 copy-done.6
  47.9 0.0 all-to-all-done
  47.9 18.6 %all_to_all.39.signal.strip_grad = bf16[4,2,128,256]{3,2,1,0:T(8,128)(2,1)S(1)} all-to-all(bf16[4,2,128,256]{3,2,1,0:T(8,128)(2,1)} %bitcast.15), channel_id=1, replica_groups=mesh['row'=8,'col'=4] {'col'}, dimensions={0} | all-to-all | bytes 1048576 | tf_op jit(solution)/shard_map/all_to_all | solution.py:634
  66.5 0.7 shard_map.142
  67.2 0.0 copy-start.5
  67.2 0.0 copy-start.7
  67.2 0.0 copy-start.9
  67.2 16.0 %all_to_all.40 = bf16[32,16,384]{2,1,0:T(8,128)(2,1)S(1)} all-to-all(bf16[32,16,384]{2,1,0:T(8,128)(2,1)S(1)} %bitcast.11), channel_id=1, replica_groups=mesh['row'=8,'col'=4] {'col','row'}, dimensions={0} | all-to-all | bytes 786432 | tf_op jit(solution)/shard_map/all_to_all | solution.py:588
  83.2 2.0 %shard_map.143 = bf16[512,384]{1,0:T(8,128)(2,1)S(1)} custom-call(bf16[512,384]{1,0:T(8,128)(2,1)S(1)} %bitcast.8, bf16[512,384]{1,0:T(8,128)(2,1)S(1)} %bitcast.9, bf16[384,384]{1,0:T(8,128)(2,1)S(1)} %copy-done.8, bf16[128,128]{1,0:T(8,128)(2,1)S(1)} %copy-done.11, bf16[128,128]{1,0:T(8,128)(2,1)S(1)} %copy-done.12), custom_call_target="tpu_custom_call" | custom-call | bytes 1540096 | tf_op jit(solution)/shard_map/pallas_call | solution.py:30
  85.3 15.6 %all_to_all.41 = bf16[32,16,384]{2,1,0:T(8,128)(2,1)S(1)} all-to-all(bf16[32,16,384]{2,1,0:T(8,128)(2,1)S(1)} %bitcast.10), channel_id=1, replica_groups=mesh['row'=8,'col'=4] {'col','row'}, dimensions={0} | all-to-all | bytes 786432 | tf_op jit(solution)/shard_map/all_to_all | solution.py:588
  100.9 2.0 %shard_map.144 = bf16[2,512,512]{2,1,0:T(8,128)(2,1)} custom-call(bf16[512,384]{1,0:T(8,128)(2,1)S(1)} %bitcast.12, bf16[4,2,128,256]{3,2,1,0:T(8,128)(2,1)S(1)} %all_to_all.39.signal.strip_grad, bf16[192,512]{1,0:T(8,128)(2,1)S(1)} %bitcast.14, bf16[512,256]{1,0:T(8,128)(2,1)S(1)} %copy-done.9, bf16[512,512]{1,0:T(8,128)(2,1)S(1)} %copy-done.7), custom_call_target="tpu_custom_call" | custom-call | bytes 2949120 | tf_op jit(solution)/shard_map/pallas_call | solution.py:30
  (29 shorter events, 0.1 us)
Async XLA Ops:
  0.0 16.2 %copy-start = (bf16[8,128,256]{2,1,0:T(8,128)(2,1)S(1)}, bf16[8,128,256]{2,1,0:T(8,128)(2,1)}, u32[]{:S(2)}) copy-start(bf16[8,128,256]{2,1,0:T(8,128)(2,1)} %target.3) | copy-start | bytes 1572868
  0.0 16.2 %copy-start.13 = (s32[8,128]{1,0:T(8,128)S(1)}, s32[8,128]{1,0:T(8,128)}, u32[]{:S(2)}) copy-start(s32[8,128]{1,0:T(8,128)} %mask.1) | copy-start | bytes 12292
  0.0 22.7 %collective-permute-start = (bf16[8,128,256]{2,1,0:T(8,128)(2,1)}, bf16[8,128,256]{2,1,0:T(8,128)(2,1)S(1)}, u32[]{:S(2)}, u32[]{:S(2)}) collective-permute-start(bf16[8,128,256]{2,1,0:T(8,128)(2,1)} %features.3), channel_id=1, source_target_pairs={{0,4},{4,8},{8,12},{12,16},{16,20},{20,24},{24,28},{1,5},{5,9},{9,... | collective-permute-start | bytes 1572872 | tf_op jit(solution)/shard_map/ppermute | solution.py:602
  4.6 18.1 %collective-permute-start.1 = (bf16[8,128,256]{2,1,0:T(8,128)(2,1)}, bf16[8,128,256]{2,1,0:T(8,128)(2,1)S(1)}, u32[]{:S(2)}, u32[]{:S(2)}) collective-permute-start(bf16[8,128,256]{2,1,0:T(8,128)(2,1)} %features.3), channel_id=1, source_target_pairs={{4,0},{8,4},{12,8},{16,12},{20,16},{24,20},{28,24},{5,1},{9,5},{13... | collective-permute-start | bytes 1572872 | tf_op jit(solution)/shard_map/ppermute | solution.py:603
  6.6 16.2 %copy-start.2 = (bf16[8,128,256]{2,1,0:T(8,128)(2,1)S(1)}, bf16[8,128,256]{2,1,0:T(8,128)(2,1)}, u32[]{:S(2)}) copy-start(bf16[8,128,256]{2,1,0:T(8,128)(2,1)} %features.3) | copy-start | bytes 1572868
  9.9 37.9 %all-to-all-start = ((bf16[32,16,384]{2,1,0:T(8,128)(2,1)}), bf16[32,16,384]{2,1,0:T(8,128)(2,1)S(1)}, u32[]{:S(2)}, u32[]{:S(2)}) async-start(bf16[32,16,384]{2,1,0:T(8,128)(2,1)} %bitcast.1), calls=%async_computation | async-start | bytes 786432 | tf_op jit(solution)/shard_map/all_to_all | solution.py:588
  17.2 13.6 %collective-permute-start.2 = (bf16[5,128,256]{2,1,0:T(8,128)(2,1)}, bf16[5,128,256]{2,1,0:T(8,128)(2,1)S(1)}, u32[]{:S(2)}, u32[]{:S(2)}) collective-permute-start(bf16[5,128,256]{2,1,0:T(8,128)(2,1)} %get-tuple-element.18), channel_id=1, source_target_pairs={{0,4},{4,8},{8,12},{12,16},{16,20},{20,24},{24,28},{1,5},{5,9},{9,... | collective-permute-start | bytes 983048 | tf_op jit(solution)/shard_map/ppermute | solution.py:605
  20.7 10.5 %collective-permute-start.3 = (bf16[5,128,256]{2,1,0:T(8,128)(2,1)}, bf16[5,128,256]{2,1,0:T(8,128)(2,1)S(1)}, u32[]{:S(2)}, u32[]{:S(2)}) collective-permute-start(bf16[5,128,256]{2,1,0:T(8,128)(2,1)} %get-tuple-element.22), channel_id=1, source_target_pairs={{4,0},{8,4},{12,8},{16,12},{20,16},{24,20},{28,24},{5,1},{9,5},{13... | collective-permute-start | bytes 983048 | tf_op jit(solution)/shard_map/ppermute | solution.py:606
  31.2 5.1 %copy-start.3 = (bf16[5,128,256]{2,1,0:T(8,128)(2,1)}, bf16[5,128,256]{2,1,0:T(8,128)(2,1)S(1)}, u32[]{:S(2)}) copy-start(bf16[5,128,256]{2,1,0:T(8,128)(2,1)S(1)} %collective-permute-done.3.refs_6_.refs_13_.target_below) | copy-start | bytes 983044
  31.2 5.1 %copy-start.14 = (bf16[3,3,256,256]{3,2,1,0:T(8,128)(2,1)S(1)}, bf16[3,3,256,256]{3,2,1,0:T(8,128)(2,1)}, u32[]{:S(2)}) copy-start(bf16[3,3,256,256]{3,2,1,0:T(8,128)(2,1)} %first.7) | copy-start | bytes 3538948
  31.2 5.1 %copy-start.15 = (bf16[3,3,256,256]{3,2,1,0:T(8,128)(2,1)S(1)}, bf16[3,3,256,256]{3,2,1,0:T(8,128)(2,1)}, u32[]{:S(2)}) copy-start(bf16[3,3,256,256]{3,2,1,0:T(8,128)(2,1)} %second.5) | copy-start | bytes 3538948
  31.3 8.9 %collective-permute-start.4 = (bf16[43,8,256]{2,1,0:T(8,128)(2,1)S(1)}, bf16[43,8,256]{2,1,0:T(8,128)(2,1)S(1)}, u32[]{:S(2)}, u32[]{:S(2)}) collective-permute-start(bf16[43,8,256]{2,1,0:T(8,128)(2,1)S(1)} %get-tuple-element.23), channel_id=1, source_target_pairs={{0,1},{1,2},{2,3},{4,5},{5,6},{6,7},{8,9},{9,10},{10,11},{12,13},{... | collective-permute-start | bytes 528392 | tf_op jit(solution)/shard_map/ppermute | solution.py:611
  34.9 6.5 %collective-permute-start.5 = (bf16[43,8,256]{2,1,0:T(8,128)(2,1)S(1)}, bf16[43,8,256]{2,1,0:T(8,128)(2,1)S(1)}, u32[]{:S(2)}, u32[]{:S(2)}) collective-permute-start(bf16[43,8,256]{2,1,0:T(8,128)(2,1)S(1)} %get-tuple-element.24), channel_id=1, source_target_pairs={{1,0},{2,1},{3,2},{5,4},{6,5},{7,6},{9,8},{10,9},{11,10},{13,12},{... | collective-permute-start | bytes 528392 | tf_op jit(solution)/shard_map/ppermute | solution.py:612
  36.4 30.1 %copy-start.10 = (bf16[192,256]{1,0:T(8,128)(2,1)S(1)}, bf16[192,256]{1,0:T(8,128)(2,1)}, u32[]{:S(2)}) copy-start(bf16[192,256]{1,0:T(8,128)(2,1)} %weight.1) | copy-start | bytes 294916
  40.1 26.3 %copy-start.1 = (bf16[512,512]{1,0:T(8,128)(2,1)S(1)}, bf16[512,512]{1,0:T(8,128)(2,1)}, u32[]{:S(2)}) copy-start(bf16[512,512]{1,0:T(8,128)(2,1)} %constant.32.clone.table) | copy-start | bytes 1572868
  41.4 1.0 copy-start.4
  47.1 0.8 copy-start.6
  47.9 35.4 %copy-start.8 = (bf16[384,384]{1,0:T(8,128)(2,1)S(1)}, bf16[384,384]{1,0:T(8,128)(2,1)}, u32[]{:S(2)}) copy-start(bf16[384,384]{1,0:T(8,128)(2,1)} %mix.1) | copy-start | bytes 884740
  47.9 35.4 %copy-start.11 = (bf16[128,128]{1,0:T(8,128)(2,1)S(1)}, bf16[128,128]{1,0:T(8,128)(2,1)}, u32[]{:S(2)}) copy-start(bf16[128,128]{1,0:T(8,128)(2,1)} %constant.34.clone.table) | copy-start | bytes 98308
  47.9 35.4 %copy-start.12 = (bf16[128,128]{1,0:T(8,128)(2,1)S(1)}, bf16[128,128]{1,0:T(8,128)(2,1)}, u32[]{:S(2)}) copy-start(bf16[128,128]{1,0:T(8,128)(2,1)} %constant.33.clone.back_table) | copy-start | bytes 98308
  67.2 33.7 %copy-start.5 = (bf16[512,192]{0,1:T(8,128)(2,1)S(1)}, bf16[512,192]{0,1:T(8,128)(2,1)}, u32[]{:S(2)}) copy-start(bf16[512,192]{0,1:T(8,128)(2,1)} %param.20) | copy-start | bytes 589828
  67.2 33.7 %copy-start.7 = (bf16[512,512]{1,0:T(8,128)(2,1)S(1)}, bf16[512,512]{1,0:T(8,128)(2,1)}, u32[]{:S(2)}) copy-start(bf16[512,512]{1,0:T(8,128)(2,1)} %constant.31.clone.table) | copy-start | bytes 1572868
  67.2 33.7 %copy-start.9 = (bf16[512,256]{1,0:T(8,128)(2,1)S(1)}, bf16[512,256]{1,0:T(8,128)(2,1)}, u32[]{:S(2)}) copy-start(bf16[512,256]{1,0:T(8,128)(2,1)} %weight_local.1) | copy-start | bytes 786436

commit v10 on v8

--- a/solution.py
+++ b/solution.py
@@ -38,6 +38,10 @@
     )(*operands)
 
 
+def in_hbm(array):
+    return pltpu.with_memory_space_constraint(array, pltpu.HBM)
+
+
 def phases(first, second, length):
     angle = (first[:, None] * second[None, :] % length) * (2.0 * math.pi / length)
     return np.cos(angle).astype(ml_dtypes.bfloat16), np.sin(angle).astype(ml_dtypes.bfloat16)
@@ -52,9 +56,11 @@
     return np.ascontiguousarray(both.transpose(1, 0, 2, 3)).reshape(width, width)
 
 
-def row_matrix(height, devices):
+def row_matrix(height, row_devices, col_devices):
+    devices = row_devices * col_devices
     strip = height // devices
-    rows = (np.arange(devices)[None, :] * strip + np.arange(strip)[:, None]).reshape(-1)
+    strips = np.arange(devices).reshape(row_devices, col_devices).T.reshape(-1)
+    rows = (strips[None, :] * strip + np.arange(strip)[:, None]).reshape(-1)
     cos, sin = phases(np.arange(height), rows, height)
     return np.block([[cos, sin], [-sin, cos]])
 
@@ -73,6 +79,90 @@
 
 def spectrum_kernel(norm, signal, weight, table, out):
     out[...] = strip_spectrum(signal, weight, table, norm)
+
+
+def prepare_kernel(
+    norm,
+    signal,
+    weight,
+    table,
+    target,
+    first,
+    second,
+    mask,
+    spectrum,
+    down,
+    up,
+    mask_row,
+    first_out,
+    second_out,
+    signal_held,
+    weight_held,
+    table_held,
+    sems,
+):
+    count = signal.shape[0]
+    tile_rows, tile_cols = mask.shape
+    channels = target.shape[2]
+    moves = [(weight, weight_held)]
+    moves += [(signal.at[r], signal_held.at[r]) for r in range(count)]
+    moves += [
+        (table, table_held),
+        (target.at[pl.ds(tile_rows - NEAR, NEAR)], down.at[pl.ds(0, NEAR)]),
+        (target.at[pl.ds(0, NEAR)], up.at[pl.ds(0, NEAR)]),
+        (first, first_out),
+        (second, second_out),
+    ]
+    copies = [pltpu.make_async_copy(*move, sems.at[i]) for i, move in enumerate(moves)]
+    for copy in copies:
+        copy.start()
+    lanes = jnp.concatenate(
+        [
+            mask[...].astype(jnp.float32),
+            jnp.zeros((tile_cols - tile_rows, tile_cols), jnp.float32),
+        ],
+        axis=0,
+    ).T
+    lanes = jnp.concatenate([lanes] + [jnp.zeros_like(lanes)] * (channels // tile_cols - 1), axis=1)
+    lanes = lanes.astype(jnp.bfloat16)
+    mask_row[0] = lanes
+    down[NEAR] = lanes
+    up[NEAR] = lanes
+    copies[0].wait()
+    rows = []
+    for r in range(count):
+        copies[1 + r].wait()
+        rows.append(dot_t(signal_held[r], weight_held[...]).astype(jnp.bfloat16))
+    copies[1 + count].wait()
+    product = dot(table_held[...], jnp.concatenate(rows, axis=1))
+    spectrum[...] = (product * norm).astype(jnp.bfloat16)
+    for copy in copies[2 + count :]:
+        copy.wait()
+
+
+def prepare(norm, signal, weight, table, target, first, second, mask):
+    rows, tile_cols, channels = target.shape
+    strip, width, _ = signal.shape
+    fetched = (signal, weight, table, target, first, second)
+    in_vmem, hbm = pl.BlockSpec(memory_space=pltpu.VMEM), pl.BlockSpec(memory_space=pltpu.HBM)
+    shapes = [
+        (width, strip * weight.shape[0]),
+        (NEAR + 1, tile_cols, channels),
+        (NEAR + 1, tile_cols, channels),
+        (1, tile_cols, channels),
+        first.shape,
+        second.shape,
+    ]
+    return pl.pallas_call(
+        functools.partial(prepare_kernel, norm),
+        out_shape=[jax.ShapeDtypeStruct(shape, jnp.bfloat16) for shape in shapes],
+        in_specs=[hbm] * len(fetched) + [in_vmem],
+        out_specs=[in_vmem] * len(shapes),
+        scratch_shapes=[pltpu.VMEM(a.shape, a.dtype) for a in (signal, weight, table)]
+        + [pltpu.SemaphoreType.DMA((strip + 6,))],
+        compiler_params=pltpu.CompilerParams(vmem_limit_bytes=12 * MIB),
+        cost_estimate=pl.CostEstimate(flops=0, bytes_accessed=5 * MIB, transcendentals=0),
+    )(*[in_hbm(a) for a in fetched], mask)
 
 
 def row_spectrum(moved, table, wide, norm, owned, devices):
@@ -95,17 +185,22 @@
     return jnp.concatenate(real, axis=0), jnp.concatenate(imag, axis=0)
 
 
-def mix_kernel(norm, owned, devices, spatial, grad, mix, table, back_table, out, wide, wide_grad):
-    parts = row_spectrum(spatial, table, wide, norm, owned, devices)
+def slope_kernel(norm, owned, devices, moved, mix, table, out, wide):
+    parts = row_spectrum(moved, table, wide, norm, owned, devices)
     real, imag = [part.astype(jnp.bfloat16) for part in parts]
-    grads = row_spectrum(grad, table, wide_grad, norm, owned, devices)
     half = real.shape[1]
     spans = (slice(0, half), slice(half, 2 * half))
-    mixed = []
-    for span, value in zip(spans, grads):
+    for part, span in enumerate(spans):
         pre = dot(real, mix[spans[0], span]) + dot(imag, mix[spans[1], span])
         s = 1.0 / (1.0 + jnp.exp(-pre))
-        mixed.append((value * (s * (1.0 + pre * (1.0 - s)))).astype(jnp.bfloat16))
+        out[part] = s * (1.0 + pre * (1.0 - s))
+
+
+def mix_kernel(norm, owned, devices, moved, slope, mix, table, back_table, out, wide):
+    grads = row_spectrum(moved, table, wide, norm, owned, devices)
+    half = grads[0].shape[1]
+    spans = (slice(0, half), slice(half, 2 * half))
+    mixed = [(grad * slope[part]).astype(jnp.bfloat16) for part, grad in enumerate(grads)]
     back = [dot_t(mixed[0], mix[p, spans[0]]) + dot_t(mixed[1], mix[p, spans[1]]) for p in spans]
     back = [part.astype(jnp.bfloat16) for part in back]
     height = table.shape[0] // 2
@@ -137,42 +232,6 @@
         out[r] = total.astype(jnp.bfloat16)
 
 
-def target_pack_kernel(first, last, mask, down, up, row):
-    tile_rows, tile_cols = mask.shape
-    channels = first.shape[2]
-    lanes = jnp.concatenate(
-        [
-            mask[...].astype(jnp.float32),
-            jnp.zeros((tile_cols - tile_rows, tile_cols), jnp.float32),
-        ],
-        axis=0,
-    ).T
-    lanes = jnp.concatenate([lanes] + [jnp.zeros_like(lanes)] * (channels // tile_cols - 1), axis=1)
-    lanes = lanes.astype(jnp.bfloat16)
-    row[0] = lanes
-    for pack, part in ((down, last), (up, first)):
-        pack[:NEAR] = part[...]
-        pack[NEAR] = lanes
-
-
-def target_packs(target, mask):
-    tile_rows, tile_cols, channels = target.shape
-    block = (NEAR, tile_cols, channels)
-    shapes = [jax.ShapeDtypeStruct((n, tile_cols, channels), target.dtype) for n in (NEAR + 1, NEAR + 1, 1)]
-    return pl.pallas_call(
-        target_pack_kernel,
-        grid=(1,),
-        out_shape=shapes,
-        in_specs=[
-            pl.BlockSpec(block, lambda i: (0, 0, 0)),
-            pl.BlockSpec(block, lambda i: (tile_rows // NEAR - 1, 0, 0)),
-            pl.BlockSpec(mask.shape, lambda i: (0, 0)),
-        ],
-        out_specs=[pl.BlockSpec(shape.shape, lambda i: (0, 0, 0)) for shape in shapes],
-        compiler_params=pltpu.CompilerParams(vmem_limit_bytes=6 * MIB),
-    )(target, target, mask)
-
-
 def edge_kernel(*refs):
     sources, outs = refs[:-2], refs[-2:]
     count = len(sources) // 2
@@ -233,7 +292,9 @@
     return jnp.concatenate([piece(row) for row in rows], axis=0)
 
 
-def first_stages(stride, blocks, rows, feature, inside, first, second, wide_even, wide_odd, slopes, use):
+def first_stages(
+    stride, blocks, rows, feature, inside, first, second, wide_even, wide_odd, slopes, use
+):
     tall = rows + 2 * REACH
     for row in range(0, tall, NEAR):
         put(wide_even, row, stacked(feature, range(row, row + NEAR)), stride)
@@ -507,19 +568,19 @@
     table = column_matrix(width, devices)
     table_back = jnp.asarray(np.ascontiguousarray(table.T))
     table = jnp.asarray(table)
-    row_table = row_matrix(height, devices)
+    row_table = row_matrix(height, row_devices, col_devices)
     row_back = jnp.asarray(np.ascontiguousarray(row_table.T))
     row_table = jnp.asarray(row_table)
     bf16 = jnp.bfloat16
 
     def swap(spectrum):
-        return lax.all_to_all(spectrum, ("row", "col"), split_axis=0, concat_axis=0, tiled=True)
+        return lax.all_to_all(spectrum, ("col", "row"), split_axis=0, concat_axis=0, tiled=True)
 
     cells = [jax.ShapeDtypeStruct((width, strip * half), bf16)]
     weight_in = weight_in.T
-    spatial_cols = vmem_call(
-        functools.partial(spectrum_kernel, col_norm), cells, inputs, weight_in, table
-    )[0]
+    spatial_cols, pack_down, pack_up, mask_row, kernel_first, kernel_second = prepare(
+        col_norm, inputs, weight_in, table, target, kernel_first, kernel_second, hole_mask
+    )
     spatial_moved = swap(spatial_cols)
     row0, col0 = lax.axis_index("row") * tile_rows, lax.axis_index("col") * tile_cols
     row_ids = row0 - REACH + jnp.arange(tile_rows + 2 * REACH, dtype=jnp.int32)
@@ -531,7 +592,6 @@
     left, right = neighbours("col")
     above = lax.ppermute(features, "row", up)
     below = lax.ppermute(features, "row", down)
-    pack_down, pack_up, mask_row = target_packs(target, hole_mask)
     target_above = lax.ppermute(pack_down, "row", up)
     target_below = lax.ppermute(pack_up, "row", down)
     above, spatial_cols = lax.optimization_barrier((above, spatial_cols))
@@ -567,16 +627,25 @@
     grad_cols = vmem_call(
         functools.partial(spectrum_kernel, col_norm), cells, strip_grad, weight_out, table
     )[0]
-    wide = pltpu.VMEM((strip * half // LANES, width, LANES), jnp.float32)
+    cell_count = height * owned
+    wide = [pltpu.VMEM((strip * half // LANES, width, LANES), jnp.float32)]
+    slope = vmem_call(
+        functools.partial(slope_kernel, row_norm, owned, devices),
+        [jax.ShapeDtypeStruct((2, cell_count, half), jnp.float32)],
+        spatial_moved,
+        weight_mix,
+        row_table,
+        scratch=wide,
+    )[0]
     grad_rows = vmem_call(
         functools.partial(mix_kernel, row_norm, owned, devices),
         cells,
-        spatial_moved,
         swap(grad_cols),
+        slope,
         weight_mix,
         row_table,
         row_back,
-        scratch=[wide, wide],
+        scratch=wide,
     )[0]
     returned = swap(grad_rows)
     return vmem_call(

time: 105 us -> 104 us (level); the launches traced: 105 us -> 103 us
  blocking collectives: 50.1 us -> 33.2 us
  waiting for transfers between devices: 2.06 us -> 13.1 us
  starting transfers between devices: 22.9 us -> 27.3 us
  local copies, waits for them, and re-layouts: 7.55 us -> 5.3 us
  Pallas kernels: 21.6 us -> 23.3 us
    all_to_all x2 -> x1, blocking collectives: 32.3 us -> 15.6 us  [swap(): lax.all_to_all(spectrum, ('col', 'row'), split_axis=0, concat_axis=0, til...]
    all_to_all x1 -> x2, waiting for transfers between devices: 0.01 us -> 11.4 us  [swap(): lax.all_to_all(spectrum, ('col', 'row'), split_axis=0, concat_axis=0, til...]
    all_to_all x1 -> x2, starting transfers between devices: 6.22 us -> 10.3 us  [swap(): lax.all_to_all(spectrum, ('col', 'row'), split_axis=0, concat_axis=0, til...]
    pallas_call x1, Pallas kernels: 0.94 us -> 3.39 us  [prepare(): pl.pallas_call(functools.partial(prepare_kernel, norm), out_shape=[jax.Sh...]
    unnamed x42 -> x34, local copies, waits for them, and re-layouts: 7.55 us -> 5.3 us
  transfers between devices with their start and end apart: 7 -> 8, of which waited for: 2 -> 3; matrix products, arithmetic and copies ran while one was open for 0% -> 0% of each run, Pallas kernels for 16% -> 18%
where the time goes in v10:
time: 104 us; the launch traced here: 103 us
  blocking collectives  33.2 us (32%)
  starting transfers between devices  27.3 us (26%)
  Pallas kernels  23.3 us (22%)
  waiting for transfers between devices  13.1 us (13%)
  local copies, waits for them, and re-layouts  5.3 us (5%)
    pallas_call x7, Pallas kernels, vmem_call(): pl.pallas_call(body, out_shape=shapes, in_specs=[spec] * len(operands), o...  19.9 us
    all_to_all x1, blocking collectives, shards(): lax.all_to_all(grad_feat.reshape(col_devices, strip, tile_cols, channels)...  17.6 us
    all_to_all x1, blocking collectives, swap(): lax.all_to_all(spectrum, ('col', 'row'), split_axis=0, concat_axis=0, til...  15.6 us
    all_to_all x2, waiting for transfers between devices, swap(): lax.all_to_all(spectrum, ('col', 'row'), split_axis=0, concat_axis=0, til...  11.4 us
    all_to_all x2, starting transfers between devices, swap(): lax.all_to_all(spectrum, ('col', 'row'), split_axis=0, concat_axis=0, til...  10.3 us
    unnamed x34, local copies, waits for them, and re-layouts  5.3 us
    ppermute x1, starting transfers between devices, shards(): above = lax.ppermute(features, 'row', up)  4.5 us
    ppermute x1, starting transfers between devices, shards(): before = lax.ppermute(last, 'col', left)  3.61 us
  transfers between devices with their start and end apart: 8, of which 3 were waited for; matrix products, arithmetic and copies ran while one was open for 0% of the time, Pallas kernels for 18%

profile of v10, /device:TPU:1, one launch (start us, length us, event | category | flops | bytes accessed | tf_op | source)
XLA Modules:
  0.0 102.6 jit_solution(5520992919816473775)
XLA Ops:
  0.0 4.5 %collective-permute-start = (bf16[8,128,256]{2,1,0:T(8,128)(2,1)}, bf16[8,128,256]{2,1,0:T(8,128)(2,1)S(1)}, u32[]{:S(2)}, u32[]{:S(2)}) collective-permute-start(bf16[8,128,256]{2,1,0:T(8,128)(2,1)} %features.3), channel_id=1, source_target_pairs={{0,4},{4,8},{8,12},{12,16},{16,20},{20,24},{24,28},{1,5},{5,9},{9,... | collective-permute-start | bytes 1572872 | tf_op jit(solution)/shard_map/ppermute | solution.py:593
  4.5 1.9 %collective-permute-start.1 = (bf16[8,128,256]{2,1,0:T(8,128)(2,1)}, bf16[8,128,256]{2,1,0:T(8,128)(2,1)S(1)}, u32[]{:S(2)}, u32[]{:S(2)}) collective-permute-start(bf16[8,128,256]{2,1,0:T(8,128)(2,1)} %features.3), channel_id=1, source_target_pairs={{4,0},{8,4},{12,8},{16,12},{20,16},{24,20},{28,24},{5,1},{9,5},{13... | collective-permute-start | bytes 1572872 | tf_op jit(solution)/shard_map/ppermute | solution.py:594
  6.4 0.7 copy-done.10
  7.1 3.4 %shard_map.136 = (bf16[512,384]{1,0:T(8,128)(2,1)}, bf16[5,128,256]{2,1,0:T(8,128)(2,1)S(1)}, bf16[5,128,256]{2,1,0:T(8,128)(2,1)S(1)}, bf16[1,128,256]{2,1,0:T(...) custom-call(bf16[2,512,512]{2,1,0:T(8,128)(2,1)} %signal.1, ...), custom_call_target="tpu_custom_call" | custom-call | bytes 5242880 | tf_op jit(solution)/shard_map/pallas_call | solution.py:156
  10.5 1.0 copy-done.11
  11.6 1.0 copy-done.14
  12.6 6.2 %all-to-all-start = ((bf16[32,16,384]{2,1,0:T(8,128)(2,1)}), bf16[32,16,384]{2,1,0:T(8,128)(2,1)S(1)}, u32[]{:S(2)}, u32[]{:S(2)}) async-start(bf16[32,16,384]{2,1,0:T(8,128)(2,1)} %bitcast.1), calls=%async_computation | async-start | bytes 786432 | tf_op jit(solution)/shard_map/all_to_all | solution.py:577
  18.8 3.5 %collective-permute-start.2 = (bf16[5,128,256]{2,1,0:T(8,128)(2,1)S(1)}, bf16[5,128,256]{2,1,0:T(8,128)(2,1)S(1)}, u32[]{:S(2)}, u32[]{:S(2)}) collective-permute-start(bf16[5,128,256]{2,1,0:T(8,128)(2,1)S(1)} %get-tuple-element.22), channel_id=1, source_target_pairs={{0,4},{4,8},{8,12},{12,16},{16,20},{20,24},{24,28},{1,5},{5,9},{9,... | collective-permute-start | bytes 983048 | tf_op jit(solution)/shard_map/ppermute | solution.py:595
  22.4 1.9 %collective-permute-start.3 = (bf16[5,128,256]{2,1,0:T(8,128)(2,1)S(1)}, bf16[5,128,256]{2,1,0:T(8,128)(2,1)S(1)}, u32[]{:S(2)}, u32[]{:S(2)}) collective-permute-start(bf16[5,128,256]{2,1,0:T(8,128)(2,1)S(1)} %get-tuple-element.28), channel_id=1, source_target_pairs={{4,0},{8,4},{12,8},{16,12},{20,16},{24,20},{28,24},{5,1},{9,5},{13... | collective-permute-start | bytes 983048 | tf_op jit(solution)/shard_map/ppermute | solution.py:596
  24.3 0.1 and_convert_fusion.ok
  24.4 0.0 collective-permute-done.1.below.refs_2_.refs_9_
  24.4 1.3 %copy-done.12 = bf16[3,3,256,256]{3,2,1,0:T(8,128)(2,1)S(1)} copy-done((bf16[3,3,256,256]{3,2,1,0:T(8,128)(2,1)S(1)}, bf16[3,3,256,256]{3,2,1,0:T(8,128)(2,1)}, u32[]{:S(2)}) %copy-start.12) | copy-done | bytes 1179672
  25.7 1.3 %copy-done.15 = bf16[3,3,256,256]{3,2,1,0:T(8,128)(2,1)S(1)} copy-done((bf16[3,3,256,256]{3,2,1,0:T(8,128)(2,1)S(1)}, bf16[3,3,256,256]{3,2,1,0:T(8,128)(2,1)}, u32[]{:S(2)}) %copy-start.15) | copy-done | bytes 1179672
  27.0 5.9 %shard_map.137 = (f32[2048,256]{1,0:T(8,128)S(1)}, f32[1536,256]{1,0:T(8,128)S(1)}) custom-call(bf16[8,128,256]{2,1,0:T(8,128)(2,1)S(1)} %collective-permute-done.above.refs_0_.refs_7_, bf16[8,128,256]{2,1,0:T(8,128)(2,1)S(1)} %copy-done.2, bf16[8,128,256]{2,1,0:T(8,128)(2,1)S(1)} %collective-permute-done.1.below.refs_2_.refs_9_, ...), custom_call_target="tpu_custom_call" | custom-call | flops 5435817984 | bytes 7616000 | tf_op jit(solution)/shard_map/pallas_call | solution.py:30
  32.9 0.0 collective-permute-done.2.refs_3_.refs_10_.target_above
  32.9 0.6 collective-permute-done.3.refs_6_.refs_13_.target_below
  33.5 3.6 %collective-permute-start.4 = (bf16[43,8,256]{2,1,0:T(8,128)(2,1)S(1)}, bf16[43,8,256]{2,1,0:T(8,128)(2,1)S(1)}, u32[]{:S(2)}, u32[]{:S(2)}) collective-permute-start(bf16[43,8,256]{2,1,0:T(8,128)(2,1)S(1)} %get-tuple-element.29), channel_id=1, source_target_pairs={{0,1},{1,2},{2,3},{4,5},{5,6},{6,7},{8,9},{9,10},{10,11},{12,13},{... | collective-permute-start | bytes 528392 | tf_op jit(solution)/shard_map/ppermute | solution.py:601
  37.1 1.5 %collective-permute-start.5 = (bf16[43,8,256]{2,1,0:T(8,128)(2,1)S(1)}, bf16[43,8,256]{2,1,0:T(8,128)(2,1)S(1)}, u32[]{:S(2)}, u32[]{:S(2)}) collective-permute-start(bf16[43,8,256]{2,1,0:T(8,128)(2,1)S(1)} %get-tuple-element.30), channel_id=1, source_target_pairs={{1,0},{2,1},{3,2},{5,4},{6,5},{7,6},{9,8},{10,9},{11,10},{13,12},{... | collective-permute-start | bytes 528392 | tf_op jit(solution)/shard_map/ppermute | solution.py:602
  38.6 3.7 %shard_map.139.tile = bf16[8,128,256]{2,1,0:T(8,128)(2,1)S(1)} custom-call(f32[2048,256]{1,0:T(8,128)S(1)} %get-tuple-element.31.pre, f32[1536,256]{1,0:T(8,128)S(1)} %get-tuple-element.32.slopes, bf16[5,128,256]{2,1,0:T(8,128)(2,1)S(1)} %collective-permute-done.2.refs_3_.refs_10_.target_above, bf16[8,128,256]{2,1,0:T(8,128)(2,1)S(1)} %copy-done, ...), custom_call_target="tpu_custom_call" | custom-call | flops 3019898880 | bytes 7812608 | tf_op jit(solution)/shard_map/pallas_call | solution.py:30
  42.4 0.0 copy-start.8
  42.4 1.1 %collective-permute-done.5.after = bf16[43,8,256]{2,1,0:T(8,128)(2,1)S(1)} collective-permute-done((bf16[43,8,256]{2,1,0:T(8,128)(2,1)S(1)}, bf16[43,8,256]{2,1,0:T(8,128)(2,1)S(1)}, u32[]{:S(2)}, u32[]{:S(2)}) %collective-permute-start.5) | collective-permute-done | bytes 176160 | tf_op jit(solution)/shard_map/ppermute | solution.py:602
  43.5 4.7 %shard_map.140 = bf16[8,128,256]{2,1,0:T(8,128)(2,1)S(1)} custom-call(bf16[43,8,256]{2,1,0:T(8,128)(2,1)S(1)} %collective-permute-done.4.before, bf16[43,8,256]{2,1,0:T(8,128)(2,1)S(1)} %collective-permute-done.5.after, bf16[8,128,256]{2,1,0:T(8,128)(2,1)S(1)} %collective-permute-done.above.refs_0_.refs_7_, bf16[8,128,256]{2,1,0:T(8,128)(2,1)S(1)} %copy-done.2, ...), custom_call_target="tpu_custom_call" | custom-call | flops 3170893824 | bytes 6592000 | tf_op jit(solution)/shard_map/pallas_call | solution.py:30
  48.2 0.0 copy-start.1
  48.2 0.0 all-to-all-done
  48.2 17.6 %all_to_all.39.signal.strip_grad = bf16[4,2,128,256]{3,2,1,0:T(8,128)(2,1)S(1)} all-to-all(bf16[4,2,128,256]{3,2,1,0:T(8,128)(2,1)S(1)} %bitcast.14), channel_id=1, replica_groups=mesh['row'=8,'col'=4] {'col'}, dimensions={0} | all-to-all | bytes 1048576 | tf_op jit(solution)/shard_map/all_to_all | solution.py:624
  65.8 1.5 %shard_map.141 = bf16[512,384]{1,0:T(8,128)(2,1)} custom-call(bf16[4,2,128,256]{3,2,1,0:T(8,128)(2,1)S(1)} %all_to_all.39.signal.strip_grad, bf16[192,256]{1,0:T(8,128)(2,1)S(1)} %copy-done.8, bf16[512,512]{1,0:T(8,128)(2,1)S(1)} %copy-done.1), custom_call_target="tpu_custom_call" | custom-call | bytes 1540096 | tf_op jit(solution)/shard_map/pallas_call | solution.py:30
  67.3 4.1 %all-to-all-start.2 = ((bf16[32,16,384]{2,1,0:T(8,128)(2,1)}), bf16[32,16,384]{2,1,0:T(8,128)(2,1)S(1)}, u32[]{:S(2)}, u32[]{:S(2)}) async-start(bf16[32,16,384]{2,1,0:T(8,128)(2,1)} %bitcast.4), calls=%async_computation.2 | async-start | bytes 786432 | tf_op jit(solution)/shard_map/all_to_all | solution.py:577
  71.4 1.0 shard_map.142.slope
  72.4 11.4 %all-to-all-done.2 = bf16[32,16,384]{2,1,0:T(8,128)(2,1)S(1)} async-done(((bf16[32,16,384]{2,1,0:T(8,128)(2,1)}), bf16[32,16,384]{2,1,0:T(8,128)(2,1)S(1)}, u32[]{:S(2)}, u32[]{:S(2)}) %all-to-all-start.2) | async-done | bytes 393248 | tf_op jit(solution)/shard_map/all_to_all | solution.py:577
  83.8 1.2 %shard_map.143 = bf16[512,384]{1,0:T(8,128)(2,1)S(1)} custom-call(bf16[512,384]{1,0:T(8,128)(2,1)S(1)} %bitcast.9, f32[2,512,192]{2,1,0:T(8,128)S(1)} %shard_map.142.slope, bf16[384,384]{1,0:T(8,128)(2,1)S(1)} %copy-done.3, bf16[128,128]{1,0:T(8,128)(2,1)S(1)} %copy-done.7, bf16[128,128]{1,0:T(8,128)(2,1)S(1)} %copy-done.9), custom_call_target="tpu_custom_call" | custom-call | bytes 1933312 | tf_op jit(solution)/shard_map/pallas_call | solution.py:30
  85.0 15.6 %all_to_all.40 = bf16[32,16,384]{2,1,0:T(8,128)(2,1)S(1)} all-to-all(bf16[32,16,384]{2,1,0:T(8,128)(2,1)S(1)} %bitcast.10), channel_id=1, replica_groups=mesh['row'=8,'col'=4] {'col','row'}, dimensions={0} | all-to-all | bytes 786432 | tf_op jit(solution)/shard_map/all_to_all | solution.py:577
  100.6 2.0 %shard_map.144 = bf16[2,512,512]{2,1,0:T(8,128)(2,1)} custom-call(bf16[512,384]{1,0:T(8,128)(2,1)S(1)} %bitcast.11, bf16[4,2,128,256]{3,2,1,0:T(8,128)(2,1)S(1)} %all_to_all.39.signal.strip_grad, bf16[192,512]{1,0:T(8,128)(2,1)S(1)} %bitcast.13, bf16[512,256]{1,0:T(8,128)(2,1)S(1)} %copy-done.6, bf16[512,512]{1,0:T(8,128)(2,1)S(1)} %copy-done.5), custom_call_target="tpu_custom_call" | custom-call | bytes 2949120 | tf_op jit(solution)/shard_map/pallas_call | solution.py:30
  (32 shorter events, 0.1 us)
Async XLA Ops:
  0.0 24.4 %collective-permute-start = (bf16[8,128,256]{2,1,0:T(8,128)(2,1)}, bf16[8,128,256]{2,1,0:T(8,128)(2,1)S(1)}, u32[]{:S(2)}, u32[]{:S(2)}) collective-permute-start(bf16[8,128,256]{2,1,0:T(8,128)(2,1)} %features.3), channel_id=1, source_target_pairs={{0,4},{4,8},{8,12},{12,16},{16,20},{20,24},{24,28},{1,5},{5,9},{9,... | collective-permute-start | bytes 1572872 | tf_op jit(solution)/shard_map/ppermute | solution.py:593
  4.5 19.9 %collective-permute-start.1 = (bf16[8,128,256]{2,1,0:T(8,128)(2,1)}, bf16[8,128,256]{2,1,0:T(8,128)(2,1)S(1)}, u32[]{:S(2)}, u32[]{:S(2)}) collective-permute-start(bf16[8,128,256]{2,1,0:T(8,128)(2,1)} %features.3), channel_id=1, source_target_pairs={{4,0},{8,4},{12,8},{16,12},{20,16},{24,20},{28,24},{5,1},{9,5},{13... | collective-permute-start | bytes 1572872 | tf_op jit(solution)/shard_map/ppermute | solution.py:594
  6.4 0.7 copy-start.10
  7.1 17.3 %copy-start.2 = (bf16[8,128,256]{2,1,0:T(8,128)(2,1)S(1)}, bf16[8,128,256]{2,1,0:T(8,128)(2,1)}, u32[]{:S(2)}) copy-start(bf16[8,128,256]{2,1,0:T(8,128)(2,1)} %features.3) | copy-start | bytes 1572868
  10.5 1.0 %copy-start.11 = (bf16[3,3,256,256]{3,2,1,0:T(8,128)(2,1)}, bf16[3,3,256,256]{3,2,1,0:T(8,128)(2,1)S(1)}, u32[]{:S(2)}) copy-start(bf16[3,3,256,256]{3,2,1,0:T(8,128)(2,1)S(1)} %get-tuple-element.23.first) | copy-start | bytes 3538948
  11.6 1.0 copy-start.14
  12.6 35.6 %all-to-all-start = ((bf16[32,16,384]{2,1,0:T(8,128)(2,1)}), bf16[32,16,384]{2,1,0:T(8,128)(2,1)S(1)}, u32[]{:S(2)}, u32[]{:S(2)}) async-start(bf16[32,16,384]{2,1,0:T(8,128)(2,1)} %bitcast.1), calls=%async_computation | async-start | bytes 786432 | tf_op jit(solution)/shard_map/all_to_all | solution.py:577
  18.8 14.0 %collective-permute-start.2 = (bf16[5,128,256]{2,1,0:T(8,128)(2,1)S(1)}, bf16[5,128,256]{2,1,0:T(8,128)(2,1)S(1)}, u32[]{:S(2)}, u32[]{:S(2)}) collective-permute-start(bf16[5,128,256]{2,1,0:T(8,128)(2,1)S(1)} %get-tuple-element.22), channel_id=1, source_target_pairs={{0,4},{4,8},{8,12},{12,16},{16,20},{20,24},{24,28},{1,5},{5,9},{9,... | collective-permute-start | bytes 983048 | tf_op jit(solution)/shard_map/ppermute | solution.py:595
  22.4 11.1 %collective-permute-start.3 = (bf16[5,128,256]{2,1,0:T(8,128)(2,1)S(1)}, bf16[5,128,256]{2,1,0:T(8,128)(2,1)S(1)}, u32[]{:S(2)}, u32[]{:S(2)}) collective-permute-start(bf16[5,128,256]{2,1,0:T(8,128)(2,1)S(1)} %get-tuple-element.28), channel_id=1, source_target_pairs={{4,0},{8,4},{12,8},{16,12},{20,16},{24,20},{28,24},{5,1},{9,5},{13... | collective-permute-start | bytes 983048 | tf_op jit(solution)/shard_map/ppermute | solution.py:596
  24.4 1.3 %copy-start.12 = (bf16[3,3,256,256]{3,2,1,0:T(8,128)(2,1)S(1)}, bf16[3,3,256,256]{3,2,1,0:T(8,128)(2,1)}, u32[]{:S(2)}) copy-start(bf16[3,3,256,256]{3,2,1,0:T(8,128)(2,1)} %copy-done.11) | copy-start | bytes 3538948
  25.7 1.3 %copy-start.15 = (bf16[3,3,256,256]{3,2,1,0:T(8,128)(2,1)S(1)}, bf16[3,3,256,256]{3,2,1,0:T(8,128)(2,1)}, u32[]{:S(2)}) copy-start(bf16[3,3,256,256]{3,2,1,0:T(8,128)(2,1)} %copy-done.14) | copy-start | bytes 3538948
  27.0 6.5 %copy-start = (bf16[8,128,256]{2,1,0:T(8,128)(2,1)S(1)}, bf16[8,128,256]{2,1,0:T(8,128)(2,1)}, u32[]{:S(2)}) copy-start(bf16[8,128,256]{2,1,0:T(8,128)(2,1)} %target.5) | copy-start | bytes 1572868
  33.5 5.1 %copy-start.13 = (bf16[3,3,256,256]{3,2,1,0:T(8,128)(2,1)S(1)}, bf16[3,3,256,256]{3,2,1,0:T(8,128)(2,1)}, u32[]{:S(2)}) copy-start(bf16[3,3,256,256]{3,2,1,0:T(8,128)(2,1)} %copy-done.11) | copy-start | bytes 3538948
  33.5 5.1 %copy-start.16 = (bf16[3,3,256,256]{3,2,1,0:T(8,128)(2,1)S(1)}, bf16[3,3,256,256]{3,2,1,0:T(8,128)(2,1)}, u32[]{:S(2)}) copy-start(bf16[3,3,256,256]{3,2,1,0:T(8,128)(2,1)} %copy-done.14) | copy-start | bytes 3538948
  33.5 8.9 %collective-permute-start.4 = (bf16[43,8,256]{2,1,0:T(8,128)(2,1)S(1)}, bf16[43,8,256]{2,1,0:T(8,128)(2,1)S(1)}, u32[]{:S(2)}, u32[]{:S(2)}) collective-permute-start(bf16[43,8,256]{2,1,0:T(8,128)(2,1)S(1)} %get-tuple-element.29), channel_id=1, source_target_pairs={{0,1},{1,2},{2,3},{4,5},{5,6},{6,7},{8,9},{9,10},{10,11},{12,13},{... | collective-permute-start | bytes 528392 | tf_op jit(solution)/shard_map/ppermute | solution.py:601
  37.1 6.4 %collective-permute-start.5 = (bf16[43,8,256]{2,1,0:T(8,128)(2,1)S(1)}, bf16[43,8,256]{2,1,0:T(8,128)(2,1)S(1)}, u32[]{:S(2)}, u32[]{:S(2)}) collective-permute-start(bf16[43,8,256]{2,1,0:T(8,128)(2,1)S(1)} %get-tuple-element.30), channel_id=1, source_target_pairs={{1,0},{2,1},{3,2},{5,4},{6,5},{7,6},{9,8},{10,9},{11,10},{13,12},{... | collective-permute-start | bytes 528392 | tf_op jit(solution)/shard_map/ppermute | solution.py:602
  42.4 23.4 %copy-start.8 = (bf16[192,256]{1,0:T(8,128)(2,1)S(1)}, bf16[192,256]{1,0:T(8,128)(2,1)}, u32[]{:S(2)}) copy-start(bf16[192,256]{1,0:T(8,128)(2,1)} %weight.1) | copy-start | bytes 294916
  48.2 17.6 %copy-start.1 = (bf16[512,512]{1,0:T(8,128)(2,1)S(1)}, bf16[512,512]{1,0:T(8,128)(2,1)}, u32[]{:S(2)}) copy-start(bf16[512,512]{1,0:T(8,128)(2,1)} %constant.32.clone.table) | copy-start | bytes 1572868
  65.8 5.6 %copy-start.3 = (bf16[384,384]{1,0:T(8,128)(2,1)S(1)}, bf16[384,384]{1,0:T(8,128)(2,1)}, u32[]{:S(2)}) copy-start(bf16[384,384]{1,0:T(8,128)(2,1)} %mix.3) | copy-start | bytes 884740
  65.8 5.6 %copy-start.7 = (bf16[128,128]{1,0:T(8,128)(2,1)S(1)}, bf16[128,128]{1,0:T(8,128)(2,1)}, u32[]{:S(2)}) copy-start(bf16[128,128]{1,0:T(8,128)(2,1)} %constant.34.clone.table) | copy-start | bytes 98308
  67.3 16.5 %copy-start.9 = (bf16[128,128]{1,0:T(8,128)(2,1)S(1)}, bf16[128,128]{1,0:T(8,128)(2,1)}, u32[]{:S(2)}) copy-start(bf16[128,128]{1,0:T(8,128)(2,1)} %constant.33.clone.back_table) | copy-start | bytes 98308
  67.3 16.5 %all-to-all-start.2 = ((bf16[32,16,384]{2,1,0:T(8,128)(2,1)}), bf16[32,16,384]{2,1,0:T(8,128)(2,1)S(1)}, u32[]{:S(2)}, u32[]{:S(2)}) async-start(bf16[32,16,384]{2,1,0:T(8,128)(2,1)} %bitcast.4), calls=%async_computation.2 | async-start | bytes 786432 | tf_op jit(solution)/shard_map/all_to_all | solution.py:577
  83.8 16.8 %copy-start.4 = (bf16[512,192]{0,1:T(8,128)(2,1)S(1)}, bf16[512,192]{0,1:T(8,128)(2,1)}, u32[]{:S(2)}) copy-start(bf16[512,192]{0,1:T(8,128)(2,1)} %param.20) | copy-start | bytes 589828
  83.8 16.8 %copy-start.5 = (bf16[512,512]{1,0:T(8,128)(2,1)S(1)}, bf16[512,512]{1,0:T(8,128)(2,1)}, u32[]{:S(2)}) copy-start(bf16[512,512]{1,0:T(8,128)(2,1)} %constant.31.clone.table) | copy-start | bytes 1572868
  83.8 16.8 %copy-start.6 = (bf16[512,256]{1,0:T(8,128)(2,1)S(1)}, bf16[512,256]{1,0:T(8,128)(2,1)}, u32[]{:S(2)}) copy-start(bf16[512,256]{1,0:T(8,128)(2,1)} %weight_local.1) | copy-start | bytes 786436

commit v11 on v9

--- a/solution.py
+++ b/solution.py
@@ -177,71 +177,83 @@
         out[r] = total.astype(jnp.bfloat16)
 
 
-def target_pack_kernel(first, last, mask, down, up, row):
+def prepare_kernel(target, mask, first, down, up, mask_row, first_out, mask_held, sems):
     tile_rows, tile_cols = mask.shape
-    channels = first.shape[2]
+    channels = target.shape[2]
+    moves = [
+        (mask, mask_held),
+        (target.at[pl.ds(tile_rows - NEAR, NEAR)], down.at[pl.ds(0, NEAR)]),
+        (target.at[pl.ds(0, NEAR)], up.at[pl.ds(0, NEAR)]),
+        (first, first_out),
+    ]
+    copies = [pltpu.make_async_copy(*move, sems.at[i]) for i, move in enumerate(moves)]
+    for copy in copies:
+        copy.start()
+    copies[0].wait()
     lanes = jnp.concatenate(
         [
-            mask[...].astype(jnp.float32),
+            mask_held[...].astype(jnp.float32),
             jnp.zeros((tile_cols - tile_rows, tile_cols), jnp.float32),
         ],
         axis=0,
     ).T
     lanes = jnp.concatenate([lanes] + [jnp.zeros_like(lanes)] * (channels // tile_cols - 1), axis=1)
     lanes = lanes.astype(jnp.bfloat16)
-    row[0] = lanes
-    for pack, part in ((down, last), (up, first)):
-        pack[:NEAR] = part[...]
-        pack[NEAR] = lanes
-
-
-def target_packs(target, mask):
-    tile_rows, tile_cols, channels = target.shape
-    block = (NEAR, tile_cols, channels)
-    shapes = [jax.ShapeDtypeStruct((n, tile_cols, channels), target.dtype) for n in (NEAR + 1, NEAR + 1, 1)]
+    mask_row[0] = lanes
+    down[NEAR] = lanes
+    up[NEAR] = lanes
+    for copy in copies[1:]:
+        copy.wait()
+
+
+def prepare(target, mask, first):
+    _, tile_cols, channels = target.shape
+    shapes = [(n, tile_cols, channels) for n in (NEAR + 1, NEAR + 1, 1)] + [first.shape]
     return pl.pallas_call(
-        target_pack_kernel,
-        grid=(1,),
-        out_shape=shapes,
-        in_specs=[
-            pl.BlockSpec(block, lambda i: (0, 0, 0)),
-            pl.BlockSpec(block, lambda i: (tile_rows // NEAR - 1, 0, 0)),
-            pl.BlockSpec(mask.shape, lambda i: (0, 0)),
-        ],
-        out_specs=[pl.BlockSpec(shape.shape, lambda i: (0, 0, 0)) for shape in shapes],
+        prepare_kernel,
+        out_shape=[jax.ShapeDtypeStruct(shape, jnp.bfloat16) for shape in shapes],
+        in_specs=[pl.BlockSpec(memory_space=pltpu.HBM)] * 3,
+        out_specs=[pl.BlockSpec(memory_space=pltpu.VMEM)] * len(shapes),
+        scratch_shapes=[pltpu.VMEM(mask.shape, mask.dtype), pltpu.SemaphoreType.DMA((4,))],
         compiler_params=pltpu.CompilerParams(vmem_limit_bytes=6 * MIB),
-    )(target, target, mask)
+        cost_estimate=pl.CostEstimate(flops=0, bytes_accessed=2 * MIB, transcendentals=0),
+    )(in_hbm(target), in_hbm(mask), in_hbm(first))
 
 
 def edge_kernel(*refs):
-    sources, outs = refs[:-2], refs[-2:]
+    sources, (last, initial, own) = refs[:-3], refs[-3:]
     count = len(sources) // 2
-    for out, group in zip(outs, (sources[:count], sources[count:])):
-        row = 0
-        for ref in group:
-            out[row : row + ref.shape[0]] = ref[...]
-            row += ref.shape[0]
+    keep = 2 * REACH
+    row = 0
+    for tail, head in zip(sources[:count], sources[count:]):
+        rows = slice(row, row + tail.shape[0])
+        last[rows] = tail[:, REACH:]
+        initial[rows] = head[:, :REACH]
+        own[rows, :keep] = head[...]
+        own[rows, keep:] = tail[...]
+        row += tail.shape[0]
 
 
 def edges(*parts):
     features = parts[1]
     channels = features.shape[2]
-    last = features.shape[1] // REACH - 1
+    keep = 2 * REACH
+    tail = features.shape[1] // keep - 1
 
     def specs(at):
-        return [pl.BlockSpec((p.shape[0], REACH, channels), lambda i, at=at: (0, at, 0)) for p in parts]
+        return [pl.BlockSpec((p.shape[0], keep, channels), lambda i, at=at: (0, at, 0)) for p in parts]
 
     rows = sum(p.shape[0] for p in parts)
-    shape = jax.ShapeDtypeStruct((rows, REACH, channels), features.dtype)
+    shapes = [(rows, columns, channels) for columns in (REACH, REACH, 2 * keep)]
     return pl.pallas_call(
         edge_kernel,
         grid=(1,),
-        out_shape=[shape, shape],
-        in_specs=specs(last) + specs(0),
-        out_specs=[pl.BlockSpec(shape.shape, lambda i: (0, 0, 0))] * 2,
-        compiler_params=pltpu.CompilerParams(vmem_limit_bytes=6 * MIB),
+        out_shape=[jax.ShapeDtypeStruct(shape, features.dtype) for shape in shapes],
+        in_specs=specs(tail) + specs(0),
+        out_specs=[pl.BlockSpec(shape, lambda i: (0, 0, 0)) for shape in shapes],
+        compiler_params=pltpu.CompilerParams(vmem_limit_bytes=8 * MIB),
         cost_estimate=pl.CostEstimate(
-            flops=0, bytes_accessed=8 * rows * REACH * channels, transcendentals=0
+            flops=0, bytes_accessed=16 * rows * keep * channels, transcendentals=0
         ),
     )(*parts, *parts)
 
@@ -274,13 +286,11 @@
 
 
 def first_stages(
-    stride, blocks, rows, feature, inside, first, second, wide_even, wide_odd, slopes, use, ready=None
+    stride, blocks, rows, feature, inside, first, second, wide_even, wide_odd, slopes, use, between=None
 ):
-    ready = ready or (lambda which: None)
     tall = rows + 2 * REACH
     for row in range(0, tall, NEAR):
         put(wide_even, row, stacked(feature, range(row, row + NEAR)), stride)
-    ready(0)
     count = blocks[0]
     for row in range(0, tall - 4, count):
         pre = conv(wide_even, row, count, stride, first)
@@ -292,7 +302,8 @@
             part = slice((low - row) * stride, (high - row) * stride)
             slope = (s * (1.0 + pre * (1.0 - s)) * kept)[part]
             slopes[pl.ds((low - NEAR) * stride, (high - low) * stride), :] = slope
-    ready(1)
+    if between is not None:
+        between()
     count = blocks[1]
     for row in range(0, rows + 2 * NEAR, count):
         use(row, count, conv(wide_odd, row, count, stride, second))
@@ -331,18 +342,11 @@
 
 
 def tile_forward_kernel(
-    above, features, below, first, second, ok, pre, slopes, wide_even, wide_odd, kernels, sems
+    above, features, below, first, second, ok, pre, slopes, wide_even, wide_odd, second_held, sem
 ):
     rows, stride, _ = features.shape
-    copies = [
-        pltpu.make_async_copy(source, kernels.at[i], sems.at[i]) for i, source in enumerate((first, second))
-    ]
-    for copy in copies:
-        copy.start()
-
-    def ready(which):
-        copies[which].wait()
-
+    copy = pltpu.make_async_copy(second, second_held, sem)
+    copy.start()
     find = part_of(rows, REACH, above, features, below)
 
     def feature(row):
@@ -361,13 +365,13 @@
         rows,
         feature,
         inside,
-        kernels.at[0],
-        kernels.at[1],
+        first,
+        second_held,
         wide_even,
         wide_odd,
         slopes,
         use,
-        ready,
+        copy.wait,
     )
 
 
@@ -413,52 +417,23 @@
     last_stages(stride, TILE_BLOCKS, rows, first, second, wide_even, wide_odd, slopes, use)
 
 
-def side_kernel(
-    before,
-    after,
-    above,
-    features,
-    below,
-    target_above,
-    target,
-    target_below,
-    mask_row,
-    first,
-    second,
-    ok,
-    tile,
-    out,
-    wide_even,
-    wide_odd,
-    slopes,
-):
-    rows, tile_cols, channels = features.shape
+def side_kernel(before, after, own, first, second, ok, tile, out, wide_even, wide_odd, slopes):
+    rows, tile_cols, channels = tile.shape
     keep = 2 * REACH
     stride = 2 * (REACH + keep)
     tall = rows + 2 * REACH
-    own = tall + NEAR + 1
-
-    def joined(edge, source, at):
-        parts = [before[edge], source[at, :keep], source[at, tile_cols - keep :], after[edge]]
-        return jnp.concatenate([part.astype(jnp.float32) for part in parts], axis=0)
-
-    find = part_of(rows, REACH, above, features, below)
-    find_target = part_of(
-        rows, NEAR, (target_above, tall), (target, own), (target_below, own + rows + 1)
-    )
 
     def feature(row):
-        return joined(row, *find(row))
+        parts = [part[row].astype(jnp.float32) for part in (before, own, after)]
+        return jnp.concatenate(parts, axis=0)
+
+    find = part_of(rows, NEAR, tall, tall + NEAR + 1, tall + NEAR + 1 + rows + 1)
 
     def goal(row):
-        (source, edge), at = find_target(row)
-        return joined(edge + at, source, at)
-
-    masks = [
-        joined(tall + NEAR, target_above, NEAR),
-        joined(own + rows, mask_row, 0),
-        joined(own + rows + 1 + NEAR, target_below, NEAR),
-    ]
+        start, at = find(row)
+        return feature(start + at)
+
+    masks = [feature(row) for row in (tall + NEAR, tall + NEAR + 1 + rows, before.shape[0] - 1)]
     find_mask = part_of(rows, NEAR, (masks[0], rows - NEAR), (masks[1], 0), (masks[2], 0))
 
     def hole(row):
@@ -500,20 +475,20 @@
     return pl.pallas_call(
         tile_forward_kernel,
         out_shape=shapes,
-        in_specs=[in_vmem] * 3 + [hbm] * 2 + [in_vmem],
+        in_specs=[in_vmem] * 4 + [hbm, in_vmem],
         out_specs=[in_vmem] * 2,
         scratch_shapes=[
             *[wide_buffer(rows + h, stride, channels) for h in (16, 12)],
-            pltpu.VMEM((2, *first.shape), first.dtype),
-            pltpu.SemaphoreType.DMA((2,)),
+            pltpu.VMEM(second.shape, second.dtype),
+            pltpu.SemaphoreType.DMA,
         ],
-        compiler_params=pltpu.CompilerParams(vmem_limit_bytes=20 * MIB),
+        compiler_params=pltpu.CompilerParams(vmem_limit_bytes=18 * MIB),
         cost_estimate=pl.CostEstimate(
             flops=2 * 9 * channels * channels * stride * (2 * rows + 20),
             bytes_accessed=8 * MIB,
             transcendentals=0,
         ),
-    )(above, features, below, in_hbm(first), in_hbm(second), ok)
+    )(above, features, below, first, in_hbm(second), ok)
 
 
 def tile_backward(pre, slopes, target_above, target, target_below, mask_row, first, second, ok):
@@ -601,34 +576,19 @@
     left, right = neighbours("col")
     above = lax.ppermute(features, "row", up)
     below = lax.ppermute(features, "row", down)
-    pack_down, pack_up, mask_row = target_packs(target, hole_mask)
+    target_after, spatial_cols = lax.optimization_barrier((target, spatial_cols))
+    pack_down, pack_up, mask_row, kernel_first = prepare(target_after, hole_mask, kernel_first)
     target_above = lax.ppermute(pack_down, "row", up)
     target_below = lax.ppermute(pack_up, "row", down)
-    above, spatial_cols = lax.optimization_barrier((above, spatial_cols))
     pre, slopes = tile_forward(above, features, below, kernel_first, kernel_second, ok)
     target_above, pre = lax.optimization_barrier((target_above, pre))
-    last, initial = edges(above, features, below, target_above, target, mask_row, target_below)
+    last, initial, own = edges(above, features, below, target_above, target, mask_row, target_below)
     before = lax.ppermute(last, "col", left)
     after = lax.ppermute(initial, "col", right)
     tile = tile_backward(
         pre, slopes, target_above, target, target_below, mask_row, kernel_first, kernel_second, ok
     )
-    grad_feat = sides(
-        tile,
-        before,
-        after,
-        above,
-        features,
-        below,
-        target_above,
-        target,
-        target_below,
-        mask_row,
-        kernel_first,
-        kernel_second,
-        ok,
-    )
-
+    grad_feat = sides(tile, before, after, own, kernel_first, kernel_second, ok)
     grad_feat, spatial_moved = lax.optimization_barrier((grad_feat, spatial_moved))
 
     strip_grad = lax.all_to_all(

time: 104 us -> 102 us (0.981)
  blocking collectives: 50.2 us -> 48.9 us
    pallas_call x1, Pallas kernels: 7.94 us -> 6.76 us  [tile_forward(): pl.pallas_call(tile_forward_kernel, out_shape=shapes, in_specs=[in_vmem]...]
    unnamed x32 -> x28, local copies, waits for them, and re-layouts: 1.83 us -> 2.34 us
  transfers between devices with their start and end apart: 7 -> 7, of which waited for: 2 -> 1; matrix products, arithmetic and copies ran while one was open for 0% -> 0% of each run, Pallas kernels for 20% -> 20%
where the time goes in v11:
time: 102 us; the launch traced here: 101 us
  blocking collectives  48.9 us (48%)
  Pallas kernels  24.8 us (24%)
  starting transfers between devices  22.3 us (22%)
  local copies, waits for them, and re-layouts  2.34 us (2%)
  waiting for transfers between devices  1.98 us (2%)
    all_to_all x2, blocking collectives, swap(): lax.all_to_all(spectrum, ('col', 'row'), split_axis=0, concat_axis=0, til...  31.3 us
    all_to_all x1, blocking collectives, shards(): lax.all_to_all(grad_feat.reshape(col_devices, strip, tile_cols, channels)...  17.5 us
    pallas_call x5, Pallas kernels, vmem_call(): pl.pallas_call(body, out_shape=shapes, in_specs=[spec] * len(operands), o...  13.2 us
    pallas_call x1, Pallas kernels, tile_forward(): pl.pallas_call(tile_forward_kernel, out_shape=shapes, in_specs=[in_vmem]...  6.76 us
    all_to_all x1, starting transfers between devices, swap(): lax.all_to_all(spectrum, ('col', 'row'), split_axis=0, concat_axis=0, til...  5.62 us
    ppermute x1, starting transfers between devices, shards(): above = lax.ppermute(features, 'row', up)  4.47 us
    ppermute x1, starting transfers between devices, shards(): target_above = lax.ppermute(pack_down, 'row', up)  3.53 us
    ppermute x1, starting transfers between devices, shards(): before = lax.ppermute(last, 'col', left)  3.37 us
  transfers between devices with their start and end apart: 7, of which 1 were waited for; matrix products, arithmetic and copies ran while one was open for 0% of the time, Pallas kernels for 20%

profile of v11, /device:TPU:1, one launch (start us, length us, event | category | flops | bytes accessed | tf_op | source)
XLA Modules:
  0.0 100.7 jit_solution(6001710379677210643)
XLA Ops:
  0.0 2.0 %collective-permute-start.1 = (bf16[8,128,256]{2,1,0:T(8,128)(2,1)}, bf16[8,128,256]{2,1,0:T(8,128)(2,1)S(1)}, u32[]{:S(2)}, u32[]{:S(2)}) collective-permute-start(bf16[8,128,256]{2,1,0:T(8,128)(2,1)} %refs_8_.1), channel_id=1, source_target_pairs={{4,0},{8,4},{12,8},{16,12},{20,16},{24,20},{28,24},{5,1},{9,5},{13... | collective-permute-start | bytes 1572872 | tf_op jit(solution)/shard_map/ppermute | solution.py:578
  2.0 4.5 %collective-permute-start = (bf16[8,128,256]{2,1,0:T(8,128)(2,1)}, bf16[8,128,256]{2,1,0:T(8,128)(2,1)S(1)}, u32[]{:S(2)}, u32[]{:S(2)}) collective-permute-start(bf16[8,128,256]{2,1,0:T(8,128)(2,1)} %refs_8_.1), channel_id=1, source_target_pairs={{0,4},{4,8},{8,12},{12,16},{16,20},{20,24},{24,28},{1,5},{5,9},{9,... | collective-permute-start | bytes 1572872 | tf_op jit(solution)/shard_map/ppermute | solution.py:577
  6.4 3.3 %shard_map.136 = bf16[512,384]{1,0:T(8,128)(2,1)} custom-call(bf16[2,512,512]{2,1,0:T(8,128)(2,1)} %signal.1, bf16[192,512]{1,0:T(8,128)(2,1)} %bitcast.13, bf16[512,512]{1,0:T(8,128)(2,1)} %constant.32.clone.table), custom_call_target="tpu_custom_call" | custom-call | bytes 2097152 | tf_op jit(solution)/shard_map/pallas_call | solution.py:104
  9.8 0.0 copy-start.2
  9.8 5.6 %all-to-all-start = ((bf16[32,16,384]{2,1,0:T(8,128)(2,1)}), bf16[32,16,384]{2,1,0:T(8,128)(2,1)S(1)}, u32[]{:S(2)}, u32[]{:S(2)}) async-start(bf16[32,16,384]{2,1,0:T(8,128)(2,1)} %bitcast.1), calls=%async_computation | async-start | bytes 786432 | tf_op jit(solution)/shard_map/all_to_all | solution.py:563
  15.4 1.5 %shard_map.137 = (bf16[5,128,256]{2,1,0:T(8,128)(2,1)S(1)}, bf16[5,128,256]{2,1,0:T(8,128)(2,1)S(1)}, bf16[1,128,256]{2,1,0:T(8,128)(2,1)S(1)}, bf16[3,3,256,256]{3,2,1,0:T(8,128)(2,1)S(1)}) custom-call(bf16[8,128,256]{2,1,0:T(8,128)(2,1)} %target.2, s32[8,128]{1,0:T(8,128)} %mask.1, bf16[3,3,256,256]{3,2,1,0:T(8,128)(2,1)} %first.1), custom_call_target="tpu_custom_call" | custom-call | bytes 2097152 | tf_op jit(solution)/shard_map/pallas_call | solution.py:212
  16.9 1.0 %copy-done.11 = bf16[3,3,256,256]{3,2,1,0:T(8,128)(2,1)} copy-done((bf16[3,3,256,256]{3,2,1,0:T(8,128)(2,1)}, bf16[3,3,256,256]{3,2,1,0:T(8,128)(2,1)S(1)}, u32[]{:S(2)}) %copy-start.11) | copy-done | bytes 1179672
  17.9 3.5 %collective-permute-start.2 = (bf16[5,128,256]{2,1,0:T(8,128)(2,1)S(1)}, bf16[5,128,256]{2,1,0:T(8,128)(2,1)S(1)}, u32[]{:S(2)}, u32[]{:S(2)}) collective-permute-start(bf16[5,128,256]{2,1,0:T(8,128)(2,1)S(1)} %get-tuple-element.20), channel_id=1, source_target_pairs={{0,4},{4,8},{8,12},{12,16},{16,20},{20,24},{24,28},{1,5},{5,9},{9,... | collective-permute-start | bytes 983048 | tf_op jit(solution)/shard_map/ppermute | solution.py:581
  21.5 1.9 %collective-permute-start.3 = (bf16[5,128,256]{2,1,0:T(8,128)(2,1)S(1)}, bf16[5,128,256]{2,1,0:T(8,128)(2,1)S(1)}, u32[]{:S(2)}, u32[]{:S(2)}) collective-permute-start(bf16[5,128,256]{2,1,0:T(8,128)(2,1)S(1)} %get-tuple-element.25), channel_id=1, source_target_pairs={{4,0},{8,4},{12,8},{16,12},{20,16},{24,20},{28,24},{5,1},{9,5},{13... | collective-permute-start | bytes 983048 | tf_op jit(solution)/shard_map/ppermute | solution.py:582
  23.4 0.1 and_convert_fusion.ok
  23.5 0.0 collective-permute-done.1.below.refs_2_.refs_9_
  23.5 0.0 collective-permute-done.above.refs_0_.refs_7_
  23.6 1.3 %copy-done.12 = bf16[3,3,256,256]{3,2,1,0:T(8,128)(2,1)S(1)} copy-done((bf16[3,3,256,256]{3,2,1,0:T(8,128)(2,1)S(1)}, bf16[3,3,256,256]{3,2,1,0:T(8,128)(2,1)}, u32[]{:S(2)}) %copy-start.12) | copy-done | bytes 1179672
  24.8 6.8 %shard_map.138 = (f32[2048,256]{1,0:T(8,128)S(1)}, f32[1536,256]{1,0:T(8,128)S(1)}) custom-call(bf16[8,128,256]{2,1,0:T(8,128)(2,1)S(1)} %collective-permute-done.above.refs_0_.refs_7_, bf16[8,128,256]{2,1,0:T(8,128)(2,1)S(1)} %copy-done.2, bf16[8,128,256]{2,1,0:T(8,128)(2,1)S(1)} %collective-permute-done.1.below.refs_2_.refs_9_, ...), custom_call_target="tpu_custom_call" | custom-call | flops 5435817984 | bytes 8388608 | tf_op jit(solution)/shard_map/pallas_call | solution.py:475
  31.6 0.0 collective-permute-done.2.refs_3_.refs_10_.target_above
  31.6 0.0 collective-permute-done.3.refs_6_.refs_13_.target_below
  31.6 0.1 shard_map.139
  31.7 3.4 %collective-permute-start.4 = (bf16[43,8,256]{2,1,0:T(8,128)(2,1)S(1)}, bf16[43,8,256]{2,1,0:T(8,128)(2,1)S(1)}, u32[]{:S(2)}, u32[]{:S(2)}) collective-permute-start(bf16[43,8,256]{2,1,0:T(8,128)(2,1)S(1)} %get-tuple-element.26), channel_id=1, source_target_pairs={{0,1},{1,2},{2,3},{4,5},{5,6},{6,7},{8,9},{9,10},{10,11},{12,13},{... | collective-permute-start | bytes 528392 | tf_op jit(solution)/shard_map/ppermute | solution.py:586
  35.1 1.5 %collective-permute-start.5 = (bf16[43,8,256]{2,1,0:T(8,128)(2,1)S(1)}, bf16[43,8,256]{2,1,0:T(8,128)(2,1)S(1)}, u32[]{:S(2)}, u32[]{:S(2)}) collective-permute-start(bf16[43,8,256]{2,1,0:T(8,128)(2,1)S(1)} %get-tuple-element.27), channel_id=1, source_target_pairs={{1,0},{2,1},{3,2},{5,4},{6,5},{7,6},{9,8},{10,9},{11,10},{13,12},{... | collective-permute-start | bytes 528392 | tf_op jit(solution)/shard_map/ppermute | solution.py:587
  36.6 3.7 %shard_map.140.tile = bf16[8,128,256]{2,1,0:T(8,128)(2,1)S(1)} custom-call(f32[2048,256]{1,0:T(8,128)S(1)} %get-tuple-element.29.pre, f32[1536,256]{1,0:T(8,128)S(1)} %get-tuple-element.30.slopes, bf16[5,128,256]{2,1,0:T(8,128)(2,1)S(1)} %collective-permute-done.2.refs_3_.refs_10_.target_above, bf16[8,128,256]{2,1,0:T(8,128)(2,1)S(1)} %copy-done, ...), custom_call_target="tpu_custom_call" | custom-call | flops 3019898880 | bytes 7812608 | tf_op jit(solution)/shard_map/pallas_call | solution.py:30
  40.3 0.0 collective-permute-done.4.before
  40.3 1.9 %collective-permute-done.5.after = bf16[43,8,256]{2,1,0:T(8,128)(2,1)S(1)} collective-permute-done((bf16[43,8,256]{2,1,0:T(8,128)(2,1)S(1)}, bf16[43,8,256]{2,1,0:T(8,128)(2,1)S(1)}, u32[]{:S(2)}, u32[]{:S(2)}) %collective-permute-start.5) | collective-permute-done | bytes 176160 | tf_op jit(solution)/shard_map/ppermute | solution.py:587
  42.3 4.7 %shard_map.141 = bf16[8,128,256]{2,1,0:T(8,128)(2,1)S(1)} custom-call(bf16[43,8,256]{2,1,0:T(8,128)(2,1)S(1)} %collective-permute-done.4.before, bf16[43,8,256]{2,1,0:T(8,128)(2,1)S(1)} %collective-permute-done.5.after, bf16[43,32,256]{2,1,0:T(8,128)(2,1)S(1)} %get-tuple-element.28.own, bf16[3,3,256,256]{3,2,1,0:T(8,128)(2,1)S(1)} %copy-done.13, ...), custom_call_target="tpu_custom_call" | custom-call | flops 3170893824 | bytes 4478464 | tf_op jit(solution)/shard_map/pallas_call | solution.py:30
  47.0 0.0 copy-start.1
  47.0 0.0 all-to-all-done
  47.0 17.5 %all_to_all.39.signal.strip_grad = bf16[4,2,128,256]{3,2,1,0:T(8,128)(2,1)S(1)} all-to-all(bf16[4,2,128,256]{3,2,1,0:T(8,128)(2,1)S(1)} %bitcast.15), channel_id=1, replica_groups=mesh['row'=8,'col'=4] {'col'}, dimensions={0} | all-to-all | bytes 1048576 | tf_op jit(solution)/shard_map/all_to_all | solution.py:594
  64.6 0.0 copy-start.9
  64.6 0.7 shard_map.142
  65.3 15.7 %all_to_all.40 = bf16[32,16,384]{2,1,0:T(8,128)(2,1)S(1)} all-to-all(bf16[32,16,384]{2,1,0:T(8,128)(2,1)S(1)} %bitcast.11), channel_id=1, replica_groups=mesh['row'=8,'col'=4] {'col','row'}, dimensions={0} | all-to-all | bytes 786432 | tf_op jit(solution)/shard_map/all_to_all | solution.py:563
  81.0 2.1 %shard_map.143 = bf16[512,384]{1,0:T(8,128)(2,1)S(1)} custom-call(bf16[512,384]{1,0:T(8,128)(2,1)S(1)} %bitcast.8, bf16[512,384]{1,0:T(8,128)(2,1)S(1)} %bitcast.9, bf16[384,384]{1,0:T(8,128)(2,1)S(1)} %copy-done.5, bf16[128,128]{1,0:T(8,128)(2,1)S(1)} %copy-done.8, bf16[128,128]{1,0:T(8,128)(2,1)S(1)} %copy-done.9), custom_call_target="tpu_custom_call" | custom-call | bytes 1540096 | tf_op jit(solution)/shard_map/pallas_call | solution.py:30
  83.1 15.6 %all_to_all.41 = bf16[32,16,384]{2,1,0:T(8,128)(2,1)S(1)} all-to-all(bf16[32,16,384]{2,1,0:T(8,128)(2,1)S(1)} %bitcast.10), channel_id=1, replica_groups=mesh['row'=8,'col'=4] {'col','row'}, dimensions={0} | all-to-all | bytes 786432 | tf_op jit(solution)/shard_map/all_to_all | solution.py:563
  98.7 2.0 %shard_map.144 = bf16[2,512,512]{2,1,0:T(8,128)(2,1)} custom-call(bf16[512,384]{1,0:T(8,128)(2,1)S(1)} %bitcast.12, bf16[4,2,128,256]{3,2,1,0:T(8,128)(2,1)S(1)} %all_to_all.39.signal.strip_grad, bf16[192,512]{1,0:T(8,128)(2,1)S(1)} %bitcast.14, bf16[512,256]{1,0:T(8,128)(2,1)S(1)} %copy-done.6, bf16[512,512]{1,0:T(8,128)(2,1)S(1)} %copy-done.4), custom_call_target="tpu_custom_call" | custom-call | bytes 2949120 | tf_op jit(solution)/shard_map/pallas_call | solution.py:30
  (25 shorter events, 0.1 us)
Async XLA Ops:
  0.0 23.5 %collective-permute-start.1 = (bf16[8,128,256]{2,1,0:T(8,128)(2,1)}, bf16[8,128,256]{2,1,0:T(8,128)(2,1)S(1)}, u32[]{:S(2)}, u32[]{:S(2)}) collective-permute-start(bf16[8,128,256]{2,1,0:T(8,128)(2,1)} %refs_8_.1), channel_id=1, source_target_pairs={{4,0},{8,4},{12,8},{16,12},{20,16},{24,20},{28,24},{5,1},{9,5},{13... | collective-permute-start | bytes 1572872 | tf_op jit(solution)/shard_map/ppermute | solution.py:578
  2.0 21.6 %collective-permute-start = (bf16[8,128,256]{2,1,0:T(8,128)(2,1)}, bf16[8,128,256]{2,1,0:T(8,128)(2,1)S(1)}, u32[]{:S(2)}, u32[]{:S(2)}) collective-permute-start(bf16[8,128,256]{2,1,0:T(8,128)(2,1)} %refs_8_.1), channel_id=1, source_target_pairs={{0,4},{4,8},{8,12},{12,16},{16,20},{20,24},{24,28},{1,5},{5,9},{9,... | collective-permute-start | bytes 1572872 | tf_op jit(solution)/shard_map/ppermute | solution.py:577
  9.8 13.8 %copy-start.2 = (bf16[8,128,256]{2,1,0:T(8,128)(2,1)S(1)}, bf16[8,128,256]{2,1,0:T(8,128)(2,1)}, u32[]{:S(2)}) copy-start(bf16[8,128,256]{2,1,0:T(8,128)(2,1)} %refs_8_.1) | copy-start | bytes 1572868
  9.8 37.2 %all-to-all-start = ((bf16[32,16,384]{2,1,0:T(8,128)(2,1)}), bf16[32,16,384]{2,1,0:T(8,128)(2,1)S(1)}, u32[]{:S(2)}, u32[]{:S(2)}) async-start(bf16[32,16,384]{2,1,0:T(8,128)(2,1)} %bitcast.1), calls=%async_computation | async-start | bytes 786432 | tf_op jit(solution)/shard_map/all_to_all | solution.py:563
  16.9 1.0 %copy-start.11 = (bf16[3,3,256,256]{3,2,1,0:T(8,128)(2,1)}, bf16[3,3,256,256]{3,2,1,0:T(8,128)(2,1)S(1)}, u32[]{:S(2)}) copy-start(bf16[3,3,256,256]{3,2,1,0:T(8,128)(2,1)S(1)} %get-tuple-element.21.first) | copy-start | bytes 3538948
  17.9 13.7 %collective-permute-start.2 = (bf16[5,128,256]{2,1,0:T(8,128)(2,1)S(1)}, bf16[5,128,256]{2,1,0:T(8,128)(2,1)S(1)}, u32[]{:S(2)}, u32[]{:S(2)}) collective-permute-start(bf16[5,128,256]{2,1,0:T(8,128)(2,1)S(1)} %get-tuple-element.20), channel_id=1, source_target_pairs={{0,4},{4,8},{8,12},{12,16},{16,20},{20,24},{24,28},{1,5},{5,9},{9,... | collective-permute-start | bytes 983048 | tf_op jit(solution)/shard_map/ppermute | solution.py:581
  21.5 10.2 %collective-permute-start.3 = (bf16[5,128,256]{2,1,0:T(8,128)(2,1)S(1)}, bf16[5,128,256]{2,1,0:T(8,128)(2,1)S(1)}, u32[]{:S(2)}, u32[]{:S(2)}) collective-permute-start(bf16[5,128,256]{2,1,0:T(8,128)(2,1)S(1)} %get-tuple-element.25), channel_id=1, source_target_pairs={{4,0},{8,4},{12,8},{16,12},{20,16},{24,20},{28,24},{5,1},{9,5},{13... | collective-permute-start | bytes 983048 | tf_op jit(solution)/shard_map/ppermute | solution.py:582
  23.5 1.3 %copy-start.12 = (bf16[3,3,256,256]{3,2,1,0:T(8,128)(2,1)S(1)}, bf16[3,3,256,256]{3,2,1,0:T(8,128)(2,1)}, u32[]{:S(2)}) copy-start(bf16[3,3,256,256]{3,2,1,0:T(8,128)(2,1)} %copy-done.11) | copy-start | bytes 3538948
  24.8 6.8 %copy-start = (bf16[8,128,256]{2,1,0:T(8,128)(2,1)S(1)}, bf16[8,128,256]{2,1,0:T(8,128)(2,1)}, u32[]{:S(2)}) copy-start(bf16[8,128,256]{2,1,0:T(8,128)(2,1)} %target.2) | copy-start | bytes 1572868
  31.6 5.0 %copy-start.10 = (bf16[3,3,256,256]{3,2,1,0:T(8,128)(2,1)S(1)}, bf16[3,3,256,256]{3,2,1,0:T(8,128)(2,1)}, u32[]{:S(2)}) copy-start(bf16[3,3,256,256]{3,2,1,0:T(8,128)(2,1)} %second.5) | copy-start | bytes 3538948
  31.6 5.0 %copy-start.13 = (bf16[3,3,256,256]{3,2,1,0:T(8,128)(2,1)S(1)}, bf16[3,3,256,256]{3,2,1,0:T(8,128)(2,1)}, u32[]{:S(2)}) copy-start(bf16[3,3,256,256]{3,2,1,0:T(8,128)(2,1)} %copy-done.11) | copy-start | bytes 3538948
  31.7 8.6 %collective-permute-start.4 = (bf16[43,8,256]{2,1,0:T(8,128)(2,1)S(1)}, bf16[43,8,256]{2,1,0:T(8,128)(2,1)S(1)}, u32[]{:S(2)}, u32[]{:S(2)}) collective-permute-start(bf16[43,8,256]{2,1,0:T(8,128)(2,1)S(1)} %get-tuple-element.26), channel_id=1, source_target_pairs={{0,1},{1,2},{2,3},{4,5},{5,6},{6,7},{8,9},{9,10},{10,11},{12,13},{... | collective-permute-start | bytes 528392 | tf_op jit(solution)/shard_map/ppermute | solution.py:586
  35.1 7.1 %collective-permute-start.5 = (bf16[43,8,256]{2,1,0:T(8,128)(2,1)S(1)}, bf16[43,8,256]{2,1,0:T(8,128)(2,1)S(1)}, u32[]{:S(2)}, u32[]{:S(2)}) collective-permute-start(bf16[43,8,256]{2,1,0:T(8,128)(2,1)S(1)} %get-tuple-element.27), channel_id=1, source_target_pairs={{1,0},{2,1},{3,2},{5,4},{6,5},{7,6},{9,8},{10,9},{11,10},{13,12},{... | collective-permute-start | bytes 528392 | tf_op jit(solution)/shard_map/ppermute | solution.py:587
  42.3 22.3 %copy-start.7 = (bf16[192,256]{1,0:T(8,128)(2,1)S(1)}, bf16[192,256]{1,0:T(8,128)(2,1)}, u32[]{:S(2)}) copy-start(bf16[192,256]{1,0:T(8,128)(2,1)} %weight.1) | copy-start | bytes 294916
  47.0 17.6 %copy-start.1 = (bf16[512,512]{1,0:T(8,128)(2,1)S(1)}, bf16[512,512]{1,0:T(8,128)(2,1)}, u32[]{:S(2)}) copy-start(bf16[512,512]{1,0:T(8,128)(2,1)} %constant.32.clone.table) | copy-start | bytes 1572868
  64.6 16.5 %copy-start.5 = (bf16[384,384]{1,0:T(8,128)(2,1)S(1)}, bf16[384,384]{1,0:T(8,128)(2,1)}, u32[]{:S(2)}) copy-start(bf16[384,384]{1,0:T(8,128)(2,1)} %mix.1) | copy-start | bytes 884740
  64.6 16.5 %copy-start.8 = (bf16[128,128]{1,0:T(8,128)(2,1)S(1)}, bf16[128,128]{1,0:T(8,128)(2,1)}, u32[]{:S(2)}) copy-start(bf16[128,128]{1,0:T(8,128)(2,1)} %constant.34.clone.table) | copy-start | bytes 98308
  64.6 16.5 %copy-start.9 = (bf16[128,128]{1,0:T(8,128)(2,1)S(1)}, bf16[128,128]{1,0:T(8,128)(2,1)}, u32[]{:S(2)}) copy-start(bf16[128,128]{1,0:T(8,128)(2,1)} %constant.33.clone.back_table) | copy-start | bytes 98308
  81.0 17.7 %copy-start.3 = (bf16[512,192]{0,1:T(8,128)(2,1)S(1)}, bf16[512,192]{0,1:T(8,128)(2,1)}, u32[]{:S(2)}) copy-start(bf16[512,192]{0,1:T(8,128)(2,1)} %param.20) | copy-start | bytes 589828
  81.0 17.7 %copy-start.4 = (bf16[512,512]{1,0:T(8,128)(2,1)S(1)}, bf16[512,512]{1,0:T(8,128)(2,1)}, u32[]{:S(2)}) copy-start(bf16[512,512]{1,0:T(8,128)(2,1)} %constant.31.clone.table) | copy-start | bytes 1572868
  81.0 17.7 %copy-start.6 = (bf16[512,256]{1,0:T(8,128)(2,1)S(1)}, bf16[512,256]{1,0:T(8,128)(2,1)}, u32[]{:S(2)}) copy-start(bf16[512,256]{1,0:T(8,128)(2,1)} %weight_local.1) | copy-start | bytes 786436

commit v12 on v11

--- a/solution.py
+++ b/solution.py
@@ -177,7 +177,9 @@
         out[r] = total.astype(jnp.bfloat16)
 
 
-def prepare_kernel(target, mask, first, down, up, mask_row, first_out, mask_held, sems):
+def prepare_kernel(
+    target, mask, first, second, down, up, mask_row, first_out, second_out, mask_held, sems
+):
     tile_rows, tile_cols = mask.shape
     channels = target.shape[2]
     moves = [
@@ -185,6 +187,7 @@
         (target.at[pl.ds(tile_rows - NEAR, NEAR)], down.at[pl.ds(0, NEAR)]),
         (target.at[pl.ds(0, NEAR)], up.at[pl.ds(0, NEAR)]),
         (first, first_out),
+        (second, second_out),
     ]
     copies = [pltpu.make_async_copy(*move, sems.at[i]) for i, move in enumerate(moves)]
     for copy in copies:
@@ -206,18 +209,19 @@
         copy.wait()
 
 
-def prepare(target, mask, first):
+def prepare(target, mask, first, second):
     _, tile_cols, channels = target.shape
-    shapes = [(n, tile_cols, channels) for n in (NEAR + 1, NEAR + 1, 1)] + [first.shape]
+    shapes = [(n, tile_cols, channels) for n in (NEAR + 1, NEAR + 1, 1)]
+    shapes += [first.shape, second.shape]
     return pl.pallas_call(
         prepare_kernel,
         out_shape=[jax.ShapeDtypeStruct(shape, jnp.bfloat16) for shape in shapes],
-        in_specs=[pl.BlockSpec(memory_space=pltpu.HBM)] * 3,
+        in_specs=[pl.BlockSpec(memory_space=pltpu.HBM)] * 4,
         out_specs=[pl.BlockSpec(memory_space=pltpu.VMEM)] * len(shapes),
-        scratch_shapes=[pltpu.VMEM(mask.shape, mask.dtype), pltpu.SemaphoreType.DMA((4,))],
+        scratch_shapes=[pltpu.VMEM(mask.shape, mask.dtype), pltpu.SemaphoreType.DMA((5,))],
         compiler_params=pltpu.CompilerParams(vmem_limit_bytes=6 * MIB),
         cost_estimate=pl.CostEstimate(flops=0, bytes_accessed=2 * MIB, transcendentals=0),
-    )(in_hbm(target), in_hbm(mask), in_hbm(first))
+    )(*[in_hbm(a) for a in (target, mask, first, second)])
 
 
 def edge_kernel(*refs):
@@ -286,7 +290,7 @@
 
 
 def first_stages(
-    stride, blocks, rows, feature, inside, first, second, wide_even, wide_odd, slopes, use, between=None
+    stride, blocks, rows, feature, inside, first, second, wide_even, wide_odd, slopes, use
 ):
     tall = rows + 2 * REACH
     for row in range(0, tall, NEAR):
@@ -302,8 +306,6 @@
             part = slice((low - row) * stride, (high - row) * stride)
             slope = (s * (1.0 + pre * (1.0 - s)) * kept)[part]
             slopes[pl.ds((low - NEAR) * stride, (high - low) * stride), :] = slope
-    if between is not None:
-        between()
     count = blocks[1]
     for row in range(0, rows + 2 * NEAR, count):
         use(row, count, conv(wide_odd, row, count, stride, second))
@@ -341,12 +343,8 @@
 SIDE_BLOCKS = (10, 8, 12, 8)
 
 
-def tile_forward_kernel(
-    above, features, below, first, second, ok, pre, slopes, wide_even, wide_odd, second_held, sem
-):
+def tile_forward_kernel(above, features, below, first, second, ok, pre, slopes, wide_even, wide_odd):
     rows, stride, _ = features.shape
-    copy = pltpu.make_async_copy(second, second_held, sem)
-    copy.start()
     find = part_of(rows, REACH, above, features, below)
 
     def feature(row):
@@ -360,18 +358,7 @@
         pre[pl.ds(row * stride, count * stride), :] = value
 
     first_stages(
-        stride,
-        TILE_BLOCKS,
-        rows,
-        feature,
-        inside,
-        first,
-        second_held,
-        wide_even,
-        wide_odd,
-        slopes,
-        use,
-        copy.wait,
+        stride, TILE_BLOCKS, rows, feature, inside, first, second, wide_even, wide_odd, slopes, use
     )
 
 
@@ -471,24 +458,19 @@
     shapes = [
         jax.ShapeDtypeStruct(((rows + h) * stride, channels), jnp.float32) for h in (2 * NEAR, 4)
     ]
-    in_vmem, hbm = pl.BlockSpec(memory_space=pltpu.VMEM), pl.BlockSpec(memory_space=pltpu.HBM)
-    return pl.pallas_call(
+    return vmem_call(
         tile_forward_kernel,
-        out_shape=shapes,
-        in_specs=[in_vmem] * 4 + [hbm, in_vmem],
-        out_specs=[in_vmem] * 2,
-        scratch_shapes=[
-            *[wide_buffer(rows + h, stride, channels) for h in (16, 12)],
-            pltpu.VMEM(second.shape, second.dtype),
-            pltpu.SemaphoreType.DMA,
-        ],
-        compiler_params=pltpu.CompilerParams(vmem_limit_bytes=18 * MIB),
-        cost_estimate=pl.CostEstimate(
-            flops=2 * 9 * channels * channels * stride * (2 * rows + 20),
-            bytes_accessed=8 * MIB,
-            transcendentals=0,
-        ),
-    )(above, features, below, first, in_hbm(second), ok)
+        shapes,
+        above,
+        features,
+        below,
+        first,
+        second,
+        ok,
+        flops=2 * 9 * channels * channels * stride * (2 * rows + 20),
+        scratch=[wide_buffer(rows + h, stride, channels) for h in (16, 12)],
+        limit=18,
+    )
 
 
 def tile_backward(pre, slopes, target_above, target, target_below, mask_row, first, second, ok):
@@ -562,22 +544,26 @@
     def swap(spectrum):
         return lax.all_to_all(spectrum, ("col", "row"), split_axis=0, concat_axis=0, tiled=True)
 
-    cells = [jax.ShapeDtypeStruct((width, strip * half), bf16)]
-    weight_in = weight_in.T
-    spatial_cols = fetching_spectrum(col_norm, cells[0], inputs, weight_in, table)
-    spatial_moved = swap(spatial_cols)
     row0, col0 = lax.axis_index("row") * tile_rows, lax.axis_index("col") * tile_cols
     row_ids = row0 - REACH + jnp.arange(tile_rows + 2 * REACH, dtype=jnp.int32)
     col_ids = col0 - REACH + jnp.arange(tile_cols + 2 * REACH, dtype=jnp.int32)
     ok = ((col_ids >= 0) & (col_ids < width))[:, None] & ((row_ids >= 0) & (row_ids < height))[None]
     ok = ok.astype(jnp.float32)
+    inputs, ok = lax.optimization_barrier((inputs, ok))
+
+    cells = [jax.ShapeDtypeStruct((width, strip * half), bf16)]
+    weight_in = weight_in.T
+    spatial_cols = fetching_spectrum(col_norm, cells[0], inputs, weight_in, table)
+    spatial_moved = swap(spatial_cols)
 
     up, down = neighbours("row")
     left, right = neighbours("col")
     above = lax.ppermute(features, "row", up)
     below = lax.ppermute(features, "row", down)
     target_after, spatial_cols = lax.optimization_barrier((target, spatial_cols))
-    pack_down, pack_up, mask_row, kernel_first = prepare(target_after, hole_mask, kernel_first)
+    pack_down, pack_up, mask_row, kernel_first, kernel_second = prepare(
+        target_after, hole_mask, kernel_first, kernel_second
+    )
     target_above = lax.ppermute(pack_down, "row", up)
     target_below = lax.ppermute(pack_up, "row", down)
     pre, slopes = tile_forward(above, features, below, kernel_first, kernel_second, ok)

time: 102 us -> 102 us (level)
  local copies, waits for them, and re-layouts: 2.34 us -> 0.05 us
  blocking collectives: 48.9 us -> 50.2 us
  waiting for transfers between devices: 1.98 us -> 3.08 us
    pallas_call x1 -> x0, Pallas kernels: 6.76 us -> none  [tile_forward(): pl.pallas_call(tile_forward_kernel, out_shape=shapes, in_specs=[in_vmem]...]
    pallas_call x5 -> x6, Pallas kernels: 13.2 us -> 19.3 us  [vmem_call(): pl.pallas_call(body, out_shape=shapes, in_specs=[spec] * len(operands), o...]
    all_to_all x2, blocking collectives: 31.3 us -> 33.6 us  [swap(): lax.all_to_all(spectrum, ('col', 'row'), split_axis=0, concat_axis=0, til...]
    unnamed x28 -> x20, local copies, waits for them, and re-layouts: 2.34 us -> 0.05 us
    ppermute x1, waiting for transfers between devices: 0.05 us -> 2.21 us  [shards(): target_below = lax.ppermute(pack_up, 'row', down)]
    ppermute x1, waiting for transfers between devices: 1.92 us -> 0.86 us  [shards(): after = lax.ppermute(initial, 'col', right)]
  transfers between devices with their start and end apart: 7 -> 7, of which waited for: 1 -> 2; matrix products, arithmetic and copies ran while one was open for 0% -> 0% of each run, Pallas kernels for 20% -> 20%
where the time goes in v12:
time: 102 us; the launch traced here: 100 us
  blocking collectives  50.2 us (49%)
  Pallas kernels  24.6 us (24%)
  starting transfers between devices  22.1 us (22%)
  waiting for transfers between devices  3.08 us (3%)
    all_to_all x2, blocking collectives, swap(): lax.all_to_all(spectrum, ('col', 'row'), split_axis=0, concat_axis=0, til...  33.6 us
    pallas_call x6, Pallas kernels, vmem_call(): pl.pallas_call(body, out_shape=shapes, in_specs=[spec] * len(operands), o...  19.3 us
    all_to_all x1, blocking collectives, shards(): lax.all_to_all(grad_feat.reshape(col_devices, strip, tile_cols, channels)...  16.6 us
    all_to_all x1, starting transfers between devices, swap(): lax.all_to_all(spectrum, ('col', 'row'), split_axis=0, concat_axis=0, til...  5.62 us
    ppermute x1, starting transfers between devices, shards(): above = lax.ppermute(features, 'row', up)  4.47 us
    ppermute x1, starting transfers between devices, shards(): target_above = lax.ppermute(pack_down, 'row', up)  3.54 us
    pallas_call x1, Pallas kernels, fetching_spectrum(): pl.pallas_call(functools.partial(fetching_spectrum_kernel, norm), out_sha...  3.31 us
    ppermute x1, starting transfers between devices, shards(): before = lax.ppermute(last, 'col', left)  3.15 us
  transfers between devices with their start and end apart: 7, of which 2 were waited for; matrix products, arithmetic and copies ran while one was open for 0% of the time, Pallas kernels for 20%

profile of v12, /device:TPU:1, one launch (start us, length us, event | category | flops | bytes accessed | tf_op | source)
XLA Modules:
  0.0 100.4 jit_solution(9853096127090091593)
XLA Ops:
  0.0 2.0 %collective-permute-start.1 = (bf16[8,128,256]{2,1,0:T(8,128)(2,1)}, bf16[8,128,256]{2,1,0:T(8,128)(2,1)S(1)}, u32[]{:S(2)}, u32[]{:S(2)}) collective-permute-start(bf16[8,128,256]{2,1,0:T(8,128)(2,1)} %refs_8_.1), channel_id=1, source_target_pairs={{4,0},{8,4},{12,8},{16,12},{20,16},{24,20},{28,24},{5,1},{9,5},{13... | collective-permute-start | bytes 1572872 | tf_op jit(solution)/shard_map/ppermute | solution.py:562
  2.0 4.5 %collective-permute-start = (bf16[8,128,256]{2,1,0:T(8,128)(2,1)}, bf16[8,128,256]{2,1,0:T(8,128)(2,1)S(1)}, u32[]{:S(2)}, u32[]{:S(2)}) collective-permute-start(bf16[8,128,256]{2,1,0:T(8,128)(2,1)} %refs_8_.1), channel_id=1, source_target_pairs={{0,4},{4,8},{8,12},{12,16},{16,20},{20,24},{24,28},{1,5},{5,9},{9,... | collective-permute-start | bytes 1572872 | tf_op jit(solution)/shard_map/ppermute | solution.py:561
  6.5 0.1 and_convert_fusion.ok
  6.6 3.3 %shard_map.136 = bf16[512,384]{1,0:T(8,128)(2,1)} custom-call(bf16[2,512,512]{2,1,0:T(8,128)(2,1)} %signal, bf16[192,512]{1,0:T(8,128)(2,1)} %bitcast.13, bf16[512,512]{1,0:T(8,128)(2,1)} %constant.32.clone.table), custom_call_target="tpu_custom_call" | custom-call | bytes 2097152 | tf_op jit(solution)/shard_map/pallas_call | solution.py:104
  9.9 5.6 %all-to-all-start = ((bf16[32,16,384]{2,1,0:T(8,128)(2,1)}), bf16[32,16,384]{2,1,0:T(8,128)(2,1)S(1)}, u32[]{:S(2)}, u32[]{:S(2)}) async-start(bf16[32,16,384]{2,1,0:T(8,128)(2,1)} %bitcast.1), calls=%async_computation | async-start | bytes 786432 | tf_op jit(solution)/shard_map/all_to_all | solution.py:545
  15.5 0.0 copy-start.2
  15.5 1.9 %shard_map.137 = (bf16[5,128,256]{2,1,0:T(8,128)(2,1)S(1)}, bf16[5,128,256]{2,1,0:T(8,128)(2,1)S(1)}, bf16[1,128,256]{2,1,0:T(8,128)(2,1)S(1)}, bf16[3,3,256,256...) custom-call(bf16[8,128,256]{2,1,0:T(8,128)(2,1)} %target.2, s32[8,128]{1,0:T(8,128)} %mask.1, ...), custom_call_target="tpu_custom_call" | custom-call | bytes 2097152 | tf_op jit(solution)/shard_map/pallas_call | solution.py:216
  17.4 3.5 %collective-permute-start.2 = (bf16[5,128,256]{2,1,0:T(8,128)(2,1)S(1)}, bf16[5,128,256]{2,1,0:T(8,128)(2,1)S(1)}, u32[]{:S(2)}, u32[]{:S(2)}) collective-permute-start(bf16[5,128,256]{2,1,0:T(8,128)(2,1)S(1)} %get-tuple-element.24), channel_id=1, source_target_pairs={{0,4},{4,8},{8,12},{12,16},{16,20},{20,24},{24,28},{1,5},{5,9},{9,... | collective-permute-start | bytes 983048 | tf_op jit(solution)/shard_map/ppermute | solution.py:567
  21.0 1.9 %collective-permute-start.3 = (bf16[5,128,256]{2,1,0:T(8,128)(2,1)S(1)}, bf16[5,128,256]{2,1,0:T(8,128)(2,1)S(1)}, u32[]{:S(2)}, u32[]{:S(2)}) collective-permute-start(bf16[5,128,256]{2,1,0:T(8,128)(2,1)S(1)} %get-tuple-element.31), channel_id=1, source_target_pairs={{4,0},{8,4},{12,8},{16,12},{20,16},{24,20},{28,24},{5,1},{9,5},{13... | collective-permute-start | bytes 983048 | tf_op jit(solution)/shard_map/ppermute | solution.py:568
  22.9 0.0 collective-permute-done.1.below.refs_2_.refs_9_
  22.9 0.0 collective-permute-done.above.refs_0_.refs_7_
  22.9 0.0 copy-start
  23.0 6.0 %shard_map.138 = (f32[2048,256]{1,0:T(8,128)S(1)}, f32[1536,256]{1,0:T(8,128)S(1)}) custom-call(bf16[8,128,256]{2,1,0:T(8,128)(2,1)S(1)} %collective-permute-done.above.refs_0_.refs_7_, bf16[8,128,256]{2,1,0:T(8,128)(2,1)S(1)} %copy-done.2, bf16[8,128,256]{2,1,0:T(8,128)(2,1)S(1)} %collective-permute-done.1.below.refs_2_.refs_9_, ...), custom_call_target="tpu_custom_call" | custom-call | flops 5435817984 | bytes 7616000 | tf_op jit(solution)/shard_map/pallas_call | solution.py:30
  28.9 0.0 collective-permute-done.2.refs_3_.refs_10_.target_above
  29.0 2.2 %collective-permute-done.3.refs_6_.refs_13_.target_below = bf16[5,128,256]{2,1,0:T(8,128)(2,1)S(1)} collective-permute-done((bf16[5,128,256]{2,1,0:T(8,128)(2,1)S(1)}, bf16[5,128,256]{2,1,0:T(8,128)(2,1)S(1)}, u32[]{:S(2)}, u32[]{:S(2)}) %collective-permute-start.3) | collective-permute-done | bytes 327712 | tf_op jit(solution)/shard_map/ppermute | solution.py:568
  31.2 0.0 copy-done
  31.2 0.1 shard_map.139
  31.3 3.1 %collective-permute-start.4 = (bf16[43,8,256]{2,1,0:T(8,128)(2,1)S(1)}, bf16[43,8,256]{2,1,0:T(8,128)(2,1)S(1)}, u32[]{:S(2)}, u32[]{:S(2)}) collective-permute-start(bf16[43,8,256]{2,1,0:T(8,128)(2,1)S(1)} %get-tuple-element.32), channel_id=1, source_target_pairs={{0,1},{1,2},{2,3},{4,5},{5,6},{6,7},{8,9},{9,10},{10,11},{12,13},{... | collective-permute-start | bytes 528392 | tf_op jit(solution)/shard_map/ppermute | solution.py:572
  34.4 1.5 %collective-permute-start.5 = (bf16[43,8,256]{2,1,0:T(8,128)(2,1)S(1)}, bf16[43,8,256]{2,1,0:T(8,128)(2,1)S(1)}, u32[]{:S(2)}, u32[]{:S(2)}) collective-permute-start(bf16[43,8,256]{2,1,0:T(8,128)(2,1)S(1)} %get-tuple-element.33), channel_id=1, source_target_pairs={{1,0},{2,1},{3,2},{5,4},{6,5},{7,6},{9,8},{10,9},{11,10},{13,12},{... | collective-permute-start | bytes 528392 | tf_op jit(solution)/shard_map/ppermute | solution.py:573
  35.9 3.8 %shard_map.140.tile = bf16[8,128,256]{2,1,0:T(8,128)(2,1)S(1)} custom-call(f32[2048,256]{1,0:T(8,128)S(1)} %get-tuple-element.35.pre, f32[1536,256]{1,0:T(8,128)S(1)} %get-tuple-element.36.slopes, bf16[5,128,256]{2,1,0:T(8,128)(2,1)S(1)} %collective-permute-done.2.refs_3_.refs_10_.target_above, bf16[8,128,256]{2,1,0:T(8,128)(2,1)S(1)} %copy-done, ...), custom_call_target="tpu_custom_call" | custom-call | flops 3019898880 | bytes 7812608 | tf_op jit(solution)/shard_map/pallas_call | solution.py:30
  39.7 0.0 collective-permute-done.4.before
  39.7 0.9 collective-permute-done.5.after
  40.6 4.8 %shard_map.141 = bf16[8,128,256]{2,1,0:T(8,128)(2,1)S(1)} custom-call(bf16[43,8,256]{2,1,0:T(8,128)(2,1)S(1)} %collective-permute-done.4.before, bf16[43,8,256]{2,1,0:T(8,128)(2,1)S(1)} %collective-permute-done.5.after, bf16[43,32,256]{2,1,0:T(8,128)(2,1)S(1)} %get-tuple-element.34.own, bf16[3,3,256,256]{3,2,1,0:T(8,128)(2,1)S(1)} %get-tuple-element.25.first, ...), custom_call_target="tpu_custom_call" | custom-call | flops 3170893824 | bytes 4478464 | tf_op jit(solution)/shard_map/pallas_call | solution.py:30
  45.4 0.0 copy-start.1
  45.4 0.0 all-to-all-done
  45.4 16.6 %all_to_all.39.signal.strip_grad = bf16[4,2,128,256]{3,2,1,0:T(8,128)(2,1)S(1)} all-to-all(bf16[4,2,128,256]{3,2,1,0:T(8,128)(2,1)S(1)} %bitcast.15), channel_id=1, replica_groups=mesh['row'=8,'col'=4] {'col'}, dimensions={0} | all-to-all | bytes 1048576 | tf_op jit(solution)/shard_map/all_to_all | solution.py:580
  62.0 0.0 copy-start.9
  62.0 0.7 shard_map.142
  62.8 18.0 %all_to_all.40 = bf16[32,16,384]{2,1,0:T(8,128)(2,1)S(1)} all-to-all(bf16[32,16,384]{2,1,0:T(8,128)(2,1)S(1)} %bitcast.11), channel_id=1, replica_groups=mesh['row'=8,'col'=4] {'col','row'}, dimensions={0} | all-to-all | bytes 786432 | tf_op jit(solution)/shard_map/all_to_all | solution.py:545
  80.8 2.0 %shard_map.143 = bf16[512,384]{1,0:T(8,128)(2,1)S(1)} custom-call(bf16[512,384]{1,0:T(8,128)(2,1)S(1)} %bitcast.8, bf16[512,384]{1,0:T(8,128)(2,1)S(1)} %bitcast.9, bf16[384,384]{1,0:T(8,128)(2,1)S(1)} %copy-done.5, bf16[128,128]{1,0:T(8,128)(2,1)S(1)} %copy-done.8, bf16[128,128]{1,0:T(8,128)(2,1)S(1)} %copy-done.9), custom_call_target="tpu_custom_call" | custom-call | bytes 1540096 | tf_op jit(solution)/shard_map/pallas_call | solution.py:30
  82.8 15.6 %all_to_all.41 = bf16[32,16,384]{2,1,0:T(8,128)(2,1)S(1)} all-to-all(bf16[32,16,384]{2,1,0:T(8,128)(2,1)S(1)} %bitcast.10), channel_id=1, replica_groups=mesh['row'=8,'col'=4] {'col','row'}, dimensions={0} | all-to-all | bytes 786432 | tf_op jit(solution)/shard_map/all_to_all | solution.py:545
  98.5 2.0 %shard_map.144 = bf16[2,512,512]{2,1,0:T(8,128)(2,1)} custom-call(bf16[512,384]{1,0:T(8,128)(2,1)S(1)} %bitcast.12, bf16[4,2,128,256]{3,2,1,0:T(8,128)(2,1)S(1)} %all_to_all.39.signal.strip_grad, bf16[192,512]{1,0:T(8,128)(2,1)S(1)} %bitcast.14, bf16[512,256]{1,0:T(8,128)(2,1)S(1)} %copy-done.6, bf16[512,512]{1,0:T(8,128)(2,1)S(1)} %copy-done.4), custom_call_target="tpu_custom_call" | custom-call | bytes 2949120 | tf_op jit(solution)/shard_map/pallas_call | solution.py:30
  (17 shorter events, 0.0 us)
Async XLA Ops:
  0.0 22.9 %collective-permute-start.1 = (bf16[8,128,256]{2,1,0:T(8,128)(2,1)}, bf16[8,128,256]{2,1,0:T(8,128)(2,1)S(1)}, u32[]{:S(2)}, u32[]{:S(2)}) collective-permute-start(bf16[8,128,256]{2,1,0:T(8,128)(2,1)} %refs_8_.1), channel_id=1, source_target_pairs={{4,0},{8,4},{12,8},{16,12},{20,16},{24,20},{28,24},{5,1},{9,5},{13... | collective-permute-start | bytes 1572872 | tf_op jit(solution)/shard_map/ppermute | solution.py:562
  2.0 21.0 %collective-permute-start = (bf16[8,128,256]{2,1,0:T(8,128)(2,1)}, bf16[8,128,256]{2,1,0:T(8,128)(2,1)S(1)}, u32[]{:S(2)}, u32[]{:S(2)}) collective-permute-start(bf16[8,128,256]{2,1,0:T(8,128)(2,1)} %refs_8_.1), channel_id=1, source_target_pairs={{0,4},{4,8},{8,12},{12,16},{16,20},{20,24},{24,28},{1,5},{5,9},{9,... | collective-permute-start | bytes 1572872 | tf_op jit(solution)/shard_map/ppermute | solution.py:561
  9.9 35.5 %all-to-all-start = ((bf16[32,16,384]{2,1,0:T(8,128)(2,1)}), bf16[32,16,384]{2,1,0:T(8,128)(2,1)S(1)}, u32[]{:S(2)}, u32[]{:S(2)}) async-start(bf16[32,16,384]{2,1,0:T(8,128)(2,1)} %bitcast.1), calls=%async_computation | async-start | bytes 786432 | tf_op jit(solution)/shard_map/all_to_all | solution.py:545
  15.5 7.4 %copy-start.2 = (bf16[8,128,256]{2,1,0:T(8,128)(2,1)S(1)}, bf16[8,128,256]{2,1,0:T(8,128)(2,1)}, u32[]{:S(2)}) copy-start(bf16[8,128,256]{2,1,0:T(8,128)(2,1)} %refs_8_.1) | copy-start | bytes 1572868
  17.4 11.5 %collective-permute-start.2 = (bf16[5,128,256]{2,1,0:T(8,128)(2,1)S(1)}, bf16[5,128,256]{2,1,0:T(8,128)(2,1)S(1)}, u32[]{:S(2)}, u32[]{:S(2)}) collective-permute-start(bf16[5,128,256]{2,1,0:T(8,128)(2,1)S(1)} %get-tuple-element.24), channel_id=1, source_target_pairs={{0,4},{4,8},{8,12},{12,16},{16,20},{20,24},{24,28},{1,5},{5,9},{9,... | collective-permute-start | bytes 983048 | tf_op jit(solution)/shard_map/ppermute | solution.py:567
  21.0 10.2 %collective-permute-start.3 = (bf16[5,128,256]{2,1,0:T(8,128)(2,1)S(1)}, bf16[5,128,256]{2,1,0:T(8,128)(2,1)S(1)}, u32[]{:S(2)}, u32[]{:S(2)}) collective-permute-start(bf16[5,128,256]{2,1,0:T(8,128)(2,1)S(1)} %get-tuple-element.31), channel_id=1, source_target_pairs={{4,0},{8,4},{12,8},{16,12},{20,16},{24,20},{28,24},{5,1},{9,5},{13... | collective-permute-start | bytes 983048 | tf_op jit(solution)/shard_map/ppermute | solution.py:568
  22.9 8.2 %copy-start = (bf16[8,128,256]{2,1,0:T(8,128)(2,1)S(1)}, bf16[8,128,256]{2,1,0:T(8,128)(2,1)}, u32[]{:S(2)}) copy-start(bf16[8,128,256]{2,1,0:T(8,128)(2,1)} %target.2) | copy-start | bytes 1572868
  31.3 8.5 %collective-permute-start.4 = (bf16[43,8,256]{2,1,0:T(8,128)(2,1)S(1)}, bf16[43,8,256]{2,1,0:T(8,128)(2,1)S(1)}, u32[]{:S(2)}, u32[]{:S(2)}) collective-permute-start(bf16[43,8,256]{2,1,0:T(8,128)(2,1)S(1)} %get-tuple-element.32), channel_id=1, source_target_pairs={{0,1},{1,2},{2,3},{4,5},{5,6},{6,7},{8,9},{9,10},{10,11},{12,13},{... | collective-permute-start | bytes 528392 | tf_op jit(solution)/shard_map/ppermute | solution.py:572
  34.4 6.2 %collective-permute-start.5 = (bf16[43,8,256]{2,1,0:T(8,128)(2,1)S(1)}, bf16[43,8,256]{2,1,0:T(8,128)(2,1)S(1)}, u32[]{:S(2)}, u32[]{:S(2)}) collective-permute-start(bf16[43,8,256]{2,1,0:T(8,128)(2,1)S(1)} %get-tuple-element.33), channel_id=1, source_target_pairs={{1,0},{2,1},{3,2},{5,4},{6,5},{7,6},{9,8},{10,9},{11,10},{13,12},{... | collective-permute-start | bytes 528392 | tf_op jit(solution)/shard_map/ppermute | solution.py:573
  40.6 21.4 %copy-start.7 = (bf16[192,256]{1,0:T(8,128)(2,1)S(1)}, bf16[192,256]{1,0:T(8,128)(2,1)}, u32[]{:S(2)}) copy-start(bf16[192,256]{1,0:T(8,128)(2,1)} %weight.1) | copy-start | bytes 294916
  45.4 16.6 %copy-start.1 = (bf16[512,512]{1,0:T(8,128)(2,1)S(1)}, bf16[512,512]{1,0:T(8,128)(2,1)}, u32[]{:S(2)}) copy-start(bf16[512,512]{1,0:T(8,128)(2,1)} %constant.32.clone.table) | copy-start | bytes 1572868
  62.0 18.8 %copy-start.5 = (bf16[384,384]{1,0:T(8,128)(2,1)S(1)}, bf16[384,384]{1,0:T(8,128)(2,1)}, u32[]{:S(2)}) copy-start(bf16[384,384]{1,0:T(8,128)(2,1)} %mix.1) | copy-start | bytes 884740
  62.0 18.8 %copy-start.8 = (bf16[128,128]{1,0:T(8,128)(2,1)S(1)}, bf16[128,128]{1,0:T(8,128)(2,1)}, u32[]{:S(2)}) copy-start(bf16[128,128]{1,0:T(8,128)(2,1)} %constant.34.clone.table) | copy-start | bytes 98308
  62.0 18.8 %copy-start.9 = (bf16[128,128]{1,0:T(8,128)(2,1)S(1)}, bf16[128,128]{1,0:T(8,128)(2,1)}, u32[]{:S(2)}) copy-start(bf16[128,128]{1,0:T(8,128)(2,1)} %constant.33.clone.back_table) | copy-start | bytes 98308
  80.8 17.7 %copy-start.3 = (bf16[512,192]{0,1:T(8,128)(2,1)S(1)}, bf16[512,192]{0,1:T(8,128)(2,1)}, u32[]{:S(2)}) copy-start(bf16[512,192]{0,1:T(8,128)(2,1)} %param.20) | copy-start | bytes 589828
  80.8 17.7 %copy-start.4 = (bf16[512,512]{1,0:T(8,128)(2,1)S(1)}, bf16[512,512]{1,0:T(8,128)(2,1)}, u32[]{:S(2)}) copy-start(bf16[512,512]{1,0:T(8,128)(2,1)} %constant.31.clone.table) | copy-start | bytes 1572868
  80.8 17.7 %copy-start.6 = (bf16[512,256]{1,0:T(8,128)(2,1)S(1)}, bf16[512,256]{1,0:T(8,128)(2,1)}, u32[]{:S(2)}) copy-start(bf16[512,256]{1,0:T(8,128)(2,1)} %weight_local.1) | copy-start | bytes 786436

commit v13 on v12

--- a/solution.py
+++ b/solution.py
@@ -66,19 +66,37 @@
 
 
 def strip_row(signal, r):
-    if len(signal.shape) == 3:
-        return signal[r]
     return jnp.concatenate([signal[block, r] for block in range(signal.shape[0])], axis=0)
 
 
-def strip_spectrum(signal, weight, table, norm):
-    count = signal.shape[0 if len(signal.shape) == 3 else 1]
-    rows = [dot_t(strip_row(signal, r), weight[...]).astype(jnp.bfloat16) for r in range(count)]
-    return (dot(table[...], jnp.concatenate(rows, axis=1)) * norm).astype(jnp.bfloat16)
-
-
-def spectrum_kernel(norm, signal, weight, table, out):
-    out[...] = strip_spectrum(signal, weight, table, norm)
+def grad_kernel(norm, col, *refs):
+    *pieces, weight, table, out, strip_out, projected = refs
+    tile_cols = pieces[0].shape[1]
+    for step, piece in enumerate(pieces):
+        block = col[0] ^ step
+        strip_out[block] = piece[...]
+        rows = [dot_t(piece[r], weight[...]).astype(jnp.bfloat16) for r in range(piece.shape[0])]
+        where = pl.ds(pl.multiple_of(block * tile_cols, tile_cols), tile_cols)
+        projected[where, :] = jnp.concatenate(rows, axis=1)
+    out[...] = (dot(table[...], projected[...]) * norm).astype(jnp.bfloat16)
+
+
+def grad_spectrum(norm, col, pieces, weight, table):
+    strip, tile_cols, channels = pieces[0].shape
+    shape = (table.shape[0], strip * weight.shape[0])
+    in_vmem = pl.BlockSpec(memory_space=pltpu.VMEM)
+    return pl.pallas_call(
+        functools.partial(grad_kernel, norm),
+        out_shape=[
+            jax.ShapeDtypeStruct(shape, jnp.bfloat16),
+            jax.ShapeDtypeStruct((len(pieces), strip, tile_cols, channels), jnp.bfloat16),
+        ],
+        in_specs=[pl.BlockSpec(memory_space=pltpu.SMEM)] + [in_vmem] * (len(pieces) + 2),
+        out_specs=[in_vmem] * 2,
+        scratch_shapes=[pltpu.VMEM(shape, jnp.bfloat16)],
+        compiler_params=pltpu.CompilerParams(vmem_limit_bytes=10 * MIB),
+        cost_estimate=pl.CostEstimate(flops=0, bytes_accessed=2 * MIB, transcendentals=0),
+    )(col, *pieces, weight, table)
 
 
 def fetching_spectrum_kernel(norm, signal, weight, table, out, signal_held, weight_held, table_held, sems):
@@ -177,89 +195,114 @@
         out[r] = total.astype(jnp.bfloat16)
 
 
+TAIL = 16
+
+
+def turned(rows):
+    count, columns = rows.shape
+    rows = rows.astype(jnp.float32)
+    return jnp.concatenate([rows, jnp.zeros((columns - count, columns), jnp.float32)], axis=0).T
+
+
+def filled(lanes, channels):
+    fill = jnp.zeros((lanes.shape[0], channels - lanes.shape[1]), jnp.float32)
+    return jnp.concatenate([lanes, fill], axis=1).astype(jnp.bfloat16)
+
+
 def prepare_kernel(
     target, mask, first, second, down, up, mask_row, first_out, second_out, mask_held, sems
 ):
     tile_rows, tile_cols = mask.shape
     channels = target.shape[2]
-    moves = [
-        (mask, mask_held),
-        (target.at[pl.ds(tile_rows - NEAR, NEAR)], down.at[pl.ds(0, NEAR)]),
-        (target.at[pl.ds(0, NEAR)], up.at[pl.ds(0, NEAR)]),
-        (first, first_out),
-        (second, second_out),
-    ]
+    moves = [(mask, mask_held)]
+    for pack, start in ((down, tile_rows - NEAR), (up, 0)):
+        moves += [
+            (target.at[start + i], pack.at[pl.ds(i * tile_cols, tile_cols)]) for i in range(NEAR)
+        ]
+    moves += [(first, first_out), (second, second_out)]
     copies = [pltpu.make_async_copy(*move, sems.at[i]) for i, move in enumerate(moves)]
     for copy in copies:
         copy.start()
     copies[0].wait()
-    lanes = jnp.concatenate(
-        [
-            mask_held[...].astype(jnp.float32),
-            jnp.zeros((tile_cols - tile_rows, tile_cols), jnp.float32),
-        ],
-        axis=0,
-    ).T
-    lanes = jnp.concatenate([lanes] + [jnp.zeros_like(lanes)] * (channels // tile_cols - 1), axis=1)
-    lanes = lanes.astype(jnp.bfloat16)
-    mask_row[0] = lanes
-    down[NEAR] = lanes
-    up[NEAR] = lanes
+    mask_row[0] = filled(turned(mask_held[...]), channels)
+    for pack, start in ((down, tile_rows - NEAR), (up, 0)):
+        rows = mask_held[start : start + NEAR].astype(jnp.float32)
+        rows = jnp.concatenate([rows, jnp.zeros((TAIL - NEAR, tile_cols), jnp.float32)], axis=0)
+        pack[NEAR * tile_cols :] = filled(rows, channels)
     for copy in copies[1:]:
         copy.wait()
 
 
 def prepare(target, mask, first, second):
     _, tile_cols, channels = target.shape
-    shapes = [(n, tile_cols, channels) for n in (NEAR + 1, NEAR + 1, 1)]
-    shapes += [first.shape, second.shape]
+    pack = (NEAR * tile_cols + TAIL, channels)
+    shapes = [pack, pack, (1, tile_cols, channels), first.shape, second.shape]
     return pl.pallas_call(
         prepare_kernel,
         out_shape=[jax.ShapeDtypeStruct(shape, jnp.bfloat16) for shape in shapes],
         in_specs=[pl.BlockSpec(memory_space=pltpu.HBM)] * 4,
         out_specs=[pl.BlockSpec(memory_space=pltpu.VMEM)] * len(shapes),
-        scratch_shapes=[pltpu.VMEM(mask.shape, mask.dtype), pltpu.SemaphoreType.DMA((5,))],
+        scratch_shapes=[pltpu.VMEM(mask.shape, mask.dtype), pltpu.SemaphoreType.DMA((2 * NEAR + 3,))],
         compiler_params=pltpu.CompilerParams(vmem_limit_bytes=6 * MIB),
         cost_estimate=pl.CostEstimate(flops=0, bytes_accessed=2 * MIB, transcendentals=0),
     )(*[in_hbm(a) for a in (target, mask, first, second)])
 
 
-def edge_kernel(*refs):
-    sources, (last, initial, own) = refs[:-3], refs[-3:]
+def edge_kernel(tile_cols, *refs):
+    above_pack, below_pack, *sources = refs[:-3]
+    last, initial, own = refs[-3:]
     count = len(sources) // 2
     keep = 2 * REACH
-    row = 0
-    for tail, head in zip(sources[:count], sources[count:]):
+    channels = own.shape[2]
+
+    def put_rows(row, tail, head):
         rows = slice(row, row + tail.shape[0])
         last[rows] = tail[:, REACH:]
         initial[rows] = head[:, :REACH]
-        own[rows, :keep] = head[...]
-        own[rows, keep:] = tail[...]
+        own[rows, :keep] = head
+        own[rows, keep:] = tail
+
+    def put_pack(row, pack):
+        for i in range(NEAR):
+            pixels = pack[i * tile_cols : (i + 1) * tile_cols]
+            put_rows(row + i, pixels[None, tile_cols - keep :], pixels[None, :keep])
+        mask = turned(pack[NEAR * tile_cols :, :tile_cols])
+        tail, head = [filled(m, channels)[None] for m in (mask[tile_cols - keep :], mask[:keep])]
+        put_rows(row + NEAR, tail, head)
+
+    row = 0
+    for index, (tail, head) in enumerate(zip(sources[:count], sources[count:])):
+        if index == 3:
+            put_pack(row, above_pack)
+            row += NEAR + 1
+        put_rows(row, tail[...], head[...])
         row += tail.shape[0]
-
-
-def edges(*parts):
-    features = parts[1]
-    channels = features.shape[2]
+    put_pack(row, below_pack)
+
+
+def edges(above, features, below, above_pack, target, mask_row, below_pack):
+    parts = (above, features, below, target, mask_row)
+    _, tile_cols, channels = features.shape
     keep = 2 * REACH
-    tail = features.shape[1] // keep - 1
+    tail = tile_cols // keep - 1
 
     def specs(at):
         return [pl.BlockSpec((p.shape[0], keep, channels), lambda i, at=at: (0, at, 0)) for p in parts]
 
-    rows = sum(p.shape[0] for p in parts)
+    whole = [pl.BlockSpec(above_pack.shape, lambda i: (0, 0))] * 2
+    rows = sum(p.shape[0] for p in parts) + 2 * (NEAR + 1)
     shapes = [(rows, columns, channels) for columns in (REACH, REACH, 2 * keep)]
     return pl.pallas_call(
-        edge_kernel,
+        functools.partial(edge_kernel, tile_cols),
         grid=(1,),
         out_shape=[jax.ShapeDtypeStruct(shape, features.dtype) for shape in shapes],
-        in_specs=specs(tail) + specs(0),
+        in_specs=whole + specs(tail) + specs(0),
         out_specs=[pl.BlockSpec(shape, lambda i: (0, 0, 0)) for shape in shapes],
         compiler_params=pltpu.CompilerParams(vmem_limit_bytes=8 * MIB),
         cost_estimate=pl.CostEstimate(
             flops=0, bytes_accessed=16 * rows * keep * channels, transcendentals=0
         ),
-    )(*parts, *parts)
+    )(above_pack, below_pack, *parts, *parts)
 
 
 def put(wide, row, value, stride):
@@ -381,10 +424,11 @@
 
     def goal(row):
         source, at = find(row)
-        return source[at].astype(jnp.float32)
-
-    masks = [m[at].astype(jnp.float32) for m, at in ((target_above, NEAR), (mask_row, 0), (target_below, NEAR))]
-    find_mask = part_of(rows, NEAR, (masks[0], rows - NEAR), (masks[1], 0), (masks[2], 0))
+        pixels = source[at] if source is target else source[at * stride : (at + 1) * stride]
+        return pixels.astype(jnp.float32)
+
+    masks = [turned(pack[NEAR * stride :, :stride]) for pack in (target_above, target_below)]
+    find_mask = part_of(rows, NEAR, (masks[0], 0), (mask_row[0].astype(jnp.float32), 0), (masks[1], 0))
 
     def hole(row):
         (mask, start), at = find_mask(row)
@@ -404,7 +448,8 @@
     last_stages(stride, TILE_BLOCKS, rows, first, second, wide_even, wide_odd, slopes, use)
 
 
-def side_kernel(before, after, own, first, second, ok, tile, out, wide_even, wide_odd, slopes):
+def side_kernel(col, before, after, own, first, second, ok, tile, *refs):
+    *pieces, out, wide_even, wide_odd, slopes = refs
     rows, tile_cols, channels = tile.shape
     keep = 2 * REACH
     stride = 2 * (REACH + keep)
@@ -421,7 +466,7 @@
         return feature(start + at)
 
     masks = [feature(row) for row in (tall + NEAR, tall + NEAR + 1 + rows, before.shape[0] - 1)]
-    find_mask = part_of(rows, NEAR, (masks[0], rows - NEAR), (masks[1], 0), (masks[2], 0))
+    find_mask = part_of(rows, NEAR, (masks[0], 0), (masks[1], 0), (masks[2], 0))
 
     def hole(row):
         (mask, start), at = find_mask(row)
@@ -447,6 +492,8 @@
         out[row : row + count, tile_cols - REACH :] = value[:, stride - 2 * REACH : stride - REACH]
 
     last_stages(stride, SIDE_BLOCKS, rows, first, second, wide_even, wide_odd, slopes, use)
+    for step, piece in enumerate(pieces):
+        piece[...] = out[pl.ds((col[0] ^ step) * piece.shape[0], piece.shape[0])]
 
 
 def wide_buffer(rows, stride, channels):
@@ -493,19 +540,29 @@
     )[0]
 
 
-def sides(tile, *operands):
-    rows, _, channels = tile.shape
+def sides(col, tile, *operands):
+    rows, tile_cols, channels = tile.shape
     stride = 6 * REACH
-    return vmem_call(
+    count = lax.axis_size("col")
+    piece = jax.ShapeDtypeStruct((rows // count, tile_cols, channels), jnp.bfloat16)
+    in_vmem = pl.BlockSpec(memory_space=pltpu.VMEM)
+    return pl.pallas_call(
         side_kernel,
-        [jax.ShapeDtypeStruct(tile.shape, jnp.bfloat16)],
-        *operands,
-        tile,
-        flops=2 * 9 * channels * channels * stride * (4 * rows + 24),
-        scratch=[wide_buffer(rows + h, stride, channels) for h in (16, 12)]
-        + [pltpu.VMEM(((rows + 4) * stride, channels), jnp.float32)],
-        limit=14,
-    )[0]
+        out_shape=[piece] * count,
+        in_specs=[pl.BlockSpec(memory_space=pltpu.SMEM)] + [in_vmem] * (len(operands) + 1),
+        out_specs=[in_vmem] * count,
+        scratch_shapes=[
+            pltpu.VMEM(tile.shape, tile.dtype),
+            *[wide_buffer(rows + h, stride, channels) for h in (16, 12)],
+            pltpu.VMEM(((rows + 4) * stride, channels), jnp.float32),
+        ],
+        compiler_params=pltpu.CompilerParams(vmem_limit_bytes=14 * MIB),
+        cost_estimate=pl.CostEstimate(
+            flops=2 * 9 * channels * channels * stride * (4 * rows + 24),
+            bytes_accessed=4 * MIB,
+            transcendentals=0,
+        ),
+    )(col, *operands, tile)
 
 
 def neighbours(axis):
@@ -549,7 +606,8 @@
     col_ids = col0 - REACH + jnp.arange(tile_cols + 2 * REACH, dtype=jnp.int32)
     ok = ((col_ids >= 0) & (col_ids < width))[:, None] & ((row_ids >= 0) & (row_ids < height))[None]
     ok = ok.astype(jnp.float32)
-    inputs, ok = lax.optimization_barrier((inputs, ok))
+    col = jnp.full((1,), lax.axis_index("col"), jnp.int32)
+    inputs, ok, col = lax.optimization_barrier((inputs, ok, col))
 
     cells = [jax.ShapeDtypeStruct((width, strip * half), bf16)]
     weight_in = weight_in.T
@@ -574,15 +632,13 @@
     tile = tile_backward(
         pre, slopes, target_above, target, target_below, mask_row, kernel_first, kernel_second, ok
     )
-    grad_feat = sides(tile, before, after, own, kernel_first, kernel_second, ok)
-    grad_feat, spatial_moved = lax.optimization_barrier((grad_feat, spatial_moved))
-
-    strip_grad = lax.all_to_all(
-        grad_feat.reshape(col_devices, strip, tile_cols, channels), "col", split_axis=0, concat_axis=0
-    )
-    grad_cols = vmem_call(
-        functools.partial(spectrum_kernel, col_norm), cells, strip_grad, weight_out, table
-    )[0]
+    pieces = sides(col, tile, before, after, own, kernel_first, kernel_second, ok)
+    pieces, spatial_moved = lax.optimization_barrier((pieces, spatial_moved))
+    moved = [pieces[0]]
+    for step in range(1, col_devices):
+        swaps = [(i, i ^ step) for i in range(col_devices)]
+        moved.append(lax.ppermute(pieces[step], "col", swaps))
+    grad_cols, strip_grad = grad_spectrum(col_norm, col, moved, weight_out, table)
     wide = pltpu.VMEM((strip * half // LANES, width, LANES), jnp.float32)
     grad_rows = vmem_call(
         functools.partial(mix_kernel, row_norm, owned, devices),

time: 102 us -> 98.9 us (0.970)
  blocking collectives: 50.2 us -> 34.8 us
  waiting for transfers between devices: 3.08 us -> 11.3 us
  starting transfers between devices: 22.1 us -> 25.8 us
    all_to_all x1 -> x0, blocking collectives: 16.6 us -> none  [shards(): lax.all_to_all(grad_feat.reshape(col_devices, strip, tile_cols, channels)...]
    ppermute x0 -> x3, waiting for transfers between devices: none -> 9.58 us  [shards(): moved.append(lax.ppermute(pieces[step], 'col', swaps))]
    pallas_call x1 -> x3, Pallas kernels: 0.08 us -> 5.84 us  [the longest x1 4.85 us: sides(): pl.pallas_call(side_kernel, out_shape=[piece] * count, in_specs=[pl.Block...]
    pallas_call x6 -> x4, Pallas kernels: 19.3 us -> 14 us  [vmem_call(): pl.pallas_call(body, out_shape=shapes, in_specs=[spec] * len(operands), o...]
    ppermute x0 -> x3, starting transfers between devices: none -> 3.61 us  [shards(): moved.append(lax.ppermute(pieces[step], 'col', swaps))]
    ppermute x1, waiting for transfers between devices: 2.21 us -> 0.98 us  [shards(): target_below = lax.ppermute(pack_up, 'row', down)]
    all_to_all x2, blocking collectives: 33.6 us -> 34.8 us  [swap(): lax.all_to_all(spectrum, ('col', 'row'), split_axis=0, concat_axis=0, til...]
  transfers between devices with their start and end apart: 7 -> 10, of which waited for: 2 -> 4; matrix products, arithmetic and copies ran while one was open for 0% -> 0% of each run, Pallas kernels for 20% -> 21%
where the time goes in v13:
time: 98.9 us; the launch traced here: 97.5 us
  blocking collectives  34.8 us (35%)
  starting transfers between devices  25.8 us (26%)
  Pallas kernels  25.2 us (25%)
  waiting for transfers between devices  11.3 us (11%)
    all_to_all x2, blocking collectives, swap(): lax.all_to_all(spectrum, ('col', 'row'), split_axis=0, concat_axis=0, til...  34.8 us
    pallas_call x4, Pallas kernels, vmem_call(): pl.pallas_call(body, out_shape=shapes, in_specs=[spec] * len(operands), o...  14 us
    ppermute x3, waiting for transfers between devices, shards(): moved.append(lax.ppermute(pieces[step], 'col', swaps))  9.58 us
    all_to_all x1, starting transfers between devices, swap(): lax.all_to_all(spectrum, ('col', 'row'), split_axis=0, concat_axis=0, til...  5.62 us
    pallas_call x1, Pallas kernels, sides(): pl.pallas_call(side_kernel, out_shape=[piece] * count, in_specs=[pl.Block...  4.85 us
    ppermute x1, starting transfers between devices, shards(): above = lax.ppermute(features, 'row', up)  4.47 us
    ppermute x3, starting transfers between devices, shards(): moved.append(lax.ppermute(pieces[step], 'col', swaps))  3.61 us
    ppermute x1, starting transfers between devices, shards(): target_above = lax.ppermute(pack_down, 'row', up)  3.54 us
  transfers between devices with their start and end apart: 10, of which 4 were waited for; matrix products, arithmetic and copies ran while one was open for 0% of the time, Pallas kernels for 21%

profile of v13, /device:TPU:1, one launch (start us, length us, event | category | flops | bytes accessed | tf_op | source)
XLA Modules:
  0.0 97.5 jit_solution(8984210064073016279)
XLA Ops:
  0.0 2.0 %collective-permute-start.2 = (bf16[8,128,256]{2,1,0:T(8,128)(2,1)}, bf16[8,128,256]{2,1,0:T(8,128)(2,1)S(1)}, u32[]{:S(2)}, u32[]{:S(2)}) collective-permute-start(bf16[8,128,256]{2,1,0:T(8,128)(2,1)} %refs_8_.1), channel_id=1, source_target_pairs={{4,0},{8,4},{12,8},{16,12},{20,16},{24,20},{28,24},{5,1},{9,5},{13... | collective-permute-start | bytes 1572872 | tf_op jit(solution)/shard_map/ppermute | solution.py:620
  2.0 4.5 %collective-permute-start.1 = (bf16[8,128,256]{2,1,0:T(8,128)(2,1)}, bf16[8,128,256]{2,1,0:T(8,128)(2,1)S(1)}, u32[]{:S(2)}, u32[]{:S(2)}) collective-permute-start(bf16[8,128,256]{2,1,0:T(8,128)(2,1)} %refs_8_.1), channel_id=1, source_target_pairs={{0,4},{4,8},{8,12},{12,16},{16,20},{20,24},{24,28},{1,5},{5,9},{9,... | collective-permute-start | bytes 1572872 | tf_op jit(solution)/shard_map/ppermute | solution.py:619
  6.5 0.1 and_convert_fusion.ok
  6.6 3.3 %shard_map.136 = bf16[512,384]{1,0:T(8,128)(2,1)} custom-call(bf16[2,512,512]{2,1,0:T(8,128)(2,1)} %signal, bf16[192,512]{1,0:T(8,128)(2,1)} %bitcast.12, bf16[512,512]{1,0:T(8,128)(2,1)} %constant.32.clone.table.refs_5_), custom_call_target="tpu_custom_call" | custom-call | bytes 2097152 | tf_op jit(solution)/shard_map/pallas_call | solution.py:122
  9.9 5.6 %all-to-all-start = ((bf16[32,16,384]{2,1,0:T(8,128)(2,1)}), bf16[32,16,384]{2,1,0:T(8,128)(2,1)S(1)}, u32[]{:S(2)}, u32[]{:S(2)}) async-start(bf16[32,16,384]{2,1,0:T(8,128)(2,1)} %bitcast.2), calls=%async_computation | async-start | bytes 786432 | tf_op jit(solution)/shard_map/all_to_all | solution.py:602
  15.5 0.0 copy-start.1
  15.5 2.1 %shard_map.137 = (bf16[528,256]{1,0:T(8,128)(2,1)S(1)}, bf16[528,256]{1,0:T(8,128)(2,1)S(1)}, bf16[1,128,256]{2,1,0:T(8,128)(2,1)S(1)}, bf16[3,3,256,256]{3,2,1,0:T(8,128)(2,1)S(1)}, bf16[3,3,256,256]{3,2,1,0:T(8,128)(2,1)S(1)}) custom-call(bf16[8,128,256]{2,1,0:T(8,128)(2,1)} %target.2, s32[8,128]{1,0:T(8,128)} %mask.1, bf16[3,3,256,256]{3,2,1,0:T(8,128)(2,1)} %first.1, ...), custom_call_target="tpu_custom_call" | custom-call | bytes 2097152 | tf_op jit(solution)/shard_map/pallas_call | solution.py:240
  17.6 3.5 %collective-permute-start = (bf16[528,256]{1,0:T(8,128)(2,1)S(1)}, bf16[528,256]{1,0:T(8,128)(2,1)S(1)}, u32[]{:S(2)}, u32[]{:S(2)}) collective-permute-start(bf16[528,256]{1,0:T(8,128)(2,1)S(1)} %get-tuple-element.35), channel_id=1, source_target_pairs={{0,4},{4,8},{8,12},{12,16},{16,20},{20,24},{24,28},{1,5},{5,9},{9,... | collective-permute-start | bytes 811016 | tf_op jit(solution)/shard_map/ppermute | solution.py:625
  21.1 1.9 %collective-permute-start.3 = (bf16[528,256]{1,0:T(8,128)(2,1)S(1)}, bf16[528,256]{1,0:T(8,128)(2,1)S(1)}, u32[]{:S(2)}, u32[]{:S(2)}) collective-permute-start(bf16[528,256]{1,0:T(8,128)(2,1)S(1)} %get-tuple-element.41), channel_id=1, source_target_pairs={{4,0},{8,4},{12,8},{16,12},{20,16},{24,20},{28,24},{5,1},{9,5},{13... | collective-permute-start | bytes 811016 | tf_op jit(solution)/shard_map/ppermute | solution.py:626
  23.1 0.0 collective-permute-done.1.above.refs_2_.refs_7_
  23.1 0.0 copy-start
  23.1 6.0 %shard_map.138 = (f32[2048,256]{1,0:T(8,128)S(1)}, f32[1536,256]{1,0:T(8,128)S(1)}) custom-call(bf16[8,128,256]{2,1,0:T(8,128)(2,1)S(1)} %collective-permute-done.1.above.refs_2_.refs_7_, bf16[8,128,256]{2,1,0:T(8,128)(2,1)S(1)} %copy-done.1, bf16[8,128,256]{2,1,0:T(8,128)(2,1)S(1)} %collective-permute-done.2.below.refs_4_.refs_9_, ...), custom_call_target="tpu_custom_call" | custom-call | flops 5435817984 | bytes 7616000 | tf_op jit(solution)/shard_map/pallas_call | solution.py:30
  29.1 1.0 %collective-permute-done.3.refs_1_.target_below = bf16[528,256]{1,0:T(8,128)(2,1)S(1)} collective-permute-done((bf16[528,256]{1,0:T(8,128)(2,1)S(1)}, bf16[528,256]{1,0:T(8,128)(2,1)S(1)}, u32[]{:S(2)}, u32[]{:S(2)}) %collective-permute-start.3) | collective-permute-done | bytes 270368 | tf_op jit(solution)/shard_map/ppermute | solution.py:626
  30.1 0.1 shard_map.139
  30.2 3.2 %collective-permute-start.4 = (bf16[43,8,256]{2,1,0:T(8,128)(2,1)S(1)}, bf16[43,8,256]{2,1,0:T(8,128)(2,1)S(1)}, u32[]{:S(2)}, u32[]{:S(2)}) collective-permute-start(bf16[43,8,256]{2,1,0:T(8,128)(2,1)S(1)} %get-tuple-element.43), channel_id=1, source_target_pairs={{0,1},{1,2},{2,3},{4,5},{5,6},{6,7},{8,9},{9,10},{10,11},{12,13},{... | collective-permute-start | bytes 528392 | tf_op jit(solution)/shard_map/ppermute | solution.py:630
  33.4 1.5 %collective-permute-start.5 = (bf16[43,8,256]{2,1,0:T(8,128)(2,1)S(1)}, bf16[43,8,256]{2,1,0:T(8,128)(2,1)S(1)}, u32[]{:S(2)}, u32[]{:S(2)}) collective-permute-start(bf16[43,8,256]{2,1,0:T(8,128)(2,1)S(1)} %get-tuple-element.44), channel_id=1, source_target_pairs={{1,0},{2,1},{3,2},{5,4},{6,5},{7,6},{9,8},{10,9},{11,10},{13,12},{... | collective-permute-start | bytes 528392 | tf_op jit(solution)/shard_map/ppermute | solution.py:631
  34.9 4.0 %shard_map.140.tile = bf16[8,128,256]{2,1,0:T(8,128)(2,1)S(1)} custom-call(f32[2048,256]{1,0:T(8,128)S(1)} %get-tuple-element.46.pre, f32[1536,256]{1,0:T(8,128)S(1)} %get-tuple-element.47.slopes, bf16[528,256]{1,0:T(8,128)(2,1)S(1)} %collective-permute-done.refs_0_.target_above, bf16[8,128,256]{2,1,0:T(8,128)(2,1)S(1)} %copy-done, ...), custom_call_target="tpu_custom_call" | custom-call | flops 3019898880 | bytes 7697920 | tf_op jit(solution)/shard_map/pallas_call | solution.py:30
  38.9 0.7 collective-permute-done.5.after
  39.7 4.8 %shard_map.141 = (bf16[2,128,256]{2,1,0:T(8,128)(2,1)S(1)}, bf16[2,128,256]{2,1,0:T(8,128)(2,1)S(1)}, bf16[2,128,256]{2,1,0:T(8,128)(2,1)S(1)}, bf16[2,128,256]{2,1,0:T(8,128)(2,1)S(1)}) custom-call(s32[1]{0:T(128)} %bitcast.col, bf16[43,8,256]{2,1,0:T(8,128)(2,1)S(1)} %collective-permute-done.4.before, ...), custom_call_target="tpu_custom_call" | custom-call | flops 3170893824 | bytes 4194304 | tf_op jit(solution)/shard_map/pallas_call | solution.py:549
  44.5 0.0 copy-start.5
  44.5 0.0 copy-start.8
  44.5 0.0 copy-start.9
  44.6 1.5 %collective-permute-start.6 = (bf16[2,128,256]{2,1,0:T(8,128)(2,1)S(1)}, bf16[2,128,256]{2,1,0:T(8,128)(2,1)S(1)}, u32[]{:S(2)}, u32[]{:S(2)}) collective-permute-start(bf16[2,128,256]{2,1,0:T(8,128)(2,1)S(1)} %get-tuple-element.54), channel_id=1, source_target_pairs={{0,1},{1,0},{2,3},{3,2},{4,5},{5,4},{6,7},{7,6},{8,9},{9,8},{10,11... | collective-permute-start | bytes 393224 | tf_op jit(solution)/shard_map/ppermute | solution.py:640
  46.0 1.7 %collective-permute-start.7 = (bf16[2,128,256]{2,1,0:T(8,128)(2,1)S(1)}, bf16[2,128,256]{2,1,0:T(8,128)(2,1)S(1)}, u32[]{:S(2)}, u32[]{:S(2)}) collective-permute-start(bf16[2,128,256]{2,1,0:T(8,128)(2,1)S(1)} %get-tuple-element.55), channel_id=1, source_target_pairs={{0,2},{1,3},{2,0},{3,1},{4,6},{5,7},{6,4},{7,5},{8,10},{9,11},{10,... | collective-permute-start | bytes 393224 | tf_op jit(solution)/shard_map/ppermute | solution.py:640
  47.7 0.4 collective-permute-start.8
  48.2 3.3 %collective-permute-done.6.refs_1_ = bf16[2,128,256]{2,1,0:T(8,128)(2,1)S(1)} collective-permute-done((bf16[2,128,256]{2,1,0:T(8,128)(2,1)S(1)}, bf16[2,128,256]{2,1,0:T(8,128)(2,1)S(1)}, u32[]{:S(2)}, u32[]{:S(2)}) %collective-permute-start.6) | collective-permute-done | bytes 131104 | tf_op jit(solution)/shard_map/ppermute | solution.py:640
  51.4 6.3 %collective-permute-done.7.refs_2_ = bf16[2,128,256]{2,1,0:T(8,128)(2,1)S(1)} collective-permute-done((bf16[2,128,256]{2,1,0:T(8,128)(2,1)S(1)}, bf16[2,128,256]{2,1,0:T(8,128)(2,1)S(1)}, u32[]{:S(2)}, u32[]{:S(2)}) %collective-permute-start.7) | collective-permute-done | bytes 131104 | tf_op jit(solution)/shard_map/ppermute | solution.py:640
  57.8 0.9 shard_map.142
  58.7 19.2 %all_to_all.34 = bf16[32,16,384]{2,1,0:T(8,128)(2,1)S(1)} all-to-all(bf16[32,16,384]{2,1,0:T(8,128)(2,1)S(1)} %bitcast.14), channel_id=1, replica_groups=mesh['row'=8,'col'=4] {'col','row'}, dimensions={0} | all-to-all | bytes 786432 | tf_op jit(solution)/shard_map/all_to_all | solution.py:602
  77.9 2.1 %shard_map.143 = bf16[512,384]{1,0:T(8,128)(2,1)S(1)} custom-call(bf16[512,384]{1,0:T(8,128)(2,1)S(1)} %bitcast.8, bf16[512,384]{1,0:T(8,128)(2,1)S(1)} %bitcast.9, bf16[384,384]{1,0:T(8,128)(2,1)S(1)} %copy-done.5, bf16[128,128]{1,0:T(8,128)(2,1)S(1)} %copy-done.8, bf16[128,128]{1,0:T(8,128)(2,1)S(1)} %copy-done.9), custom_call_target="tpu_custom_call" | custom-call | bytes 1540096 | tf_op jit(solution)/shard_map/pallas_call | solution.py:30
  79.9 15.6 %all_to_all.35 = bf16[32,16,384]{2,1,0:T(8,128)(2,1)S(1)} all-to-all(bf16[32,16,384]{2,1,0:T(8,128)(2,1)S(1)} %bitcast.10), channel_id=1, replica_groups=mesh['row'=8,'col'=4] {'col','row'}, dimensions={0} | all-to-all | bytes 786432 | tf_op jit(solution)/shard_map/all_to_all | solution.py:602
  95.6 2.0 %shard_map.144 = bf16[2,512,512]{2,1,0:T(8,128)(2,1)} custom-call(bf16[512,384]{1,0:T(8,128)(2,1)S(1)} %bitcast.11, bf16[4,2,128,256]{3,2,1,0:T(8,128)(2,1)S(1)} %get-tuple-element.58.strip_grad, bf16[192,512]{1,0:T(8,128)(2,1)S(1)} %bitcast.13, bf16[512,256]{1,0:T(8,128)(2,1)S(1)} %copy-done.6, bf16[512,512]{1,0:T(8,128)(2,1)S(1)} %copy-done.4), custom_call_target="tpu_custom_call" | custom-call | bytes 2949120 | tf_op jit(solution)/shard_map/pallas_call | solution.py:30
  (22 shorter events, 0.1 us)
Async XLA Ops:
  0.0 23.1 %collective-permute-start.2 = (bf16[8,128,256]{2,1,0:T(8,128)(2,1)}, bf16[8,128,256]{2,1,0:T(8,128)(2,1)S(1)}, u32[]{:S(2)}, u32[]{:S(2)}) collective-permute-start(bf16[8,128,256]{2,1,0:T(8,128)(2,1)} %refs_8_.1), channel_id=1, source_target_pairs={{4,0},{8,4},{12,8},{16,12},{20,16},{24,20},{28,24},{5,1},{9,5},{13... | collective-permute-start | bytes 1572872 | tf_op jit(solution)/shard_map/ppermute | solution.py:620
  2.0 21.1 %collective-permute-start.1 = (bf16[8,128,256]{2,1,0:T(8,128)(2,1)}, bf16[8,128,256]{2,1,0:T(8,128)(2,1)S(1)}, u32[]{:S(2)}, u32[]{:S(2)}) collective-permute-start(bf16[8,128,256]{2,1,0:T(8,128)(2,1)} %refs_8_.1), channel_id=1, source_target_pairs={{0,4},{4,8},{8,12},{12,16},{16,20},{20,24},{24,28},{1,5},{5,9},{9,... | collective-permute-start | bytes 1572872 | tf_op jit(solution)/shard_map/ppermute | solution.py:619
  9.9 34.7 %all-to-all-start = ((bf16[32,16,384]{2,1,0:T(8,128)(2,1)}), bf16[32,16,384]{2,1,0:T(8,128)(2,1)S(1)}, u32[]{:S(2)}, u32[]{:S(2)}) async-start(bf16[32,16,384]{2,1,0:T(8,128)(2,1)} %bitcast.2), calls=%async_computation | async-start | bytes 786432 | tf_op jit(solution)/shard_map/all_to_all | solution.py:602
  15.5 7.6 %copy-start.1 = (bf16[8,128,256]{2,1,0:T(8,128)(2,1)S(1)}, bf16[8,128,256]{2,1,0:T(8,128)(2,1)}, u32[]{:S(2)}) copy-start(bf16[8,128,256]{2,1,0:T(8,128)(2,1)} %refs_8_.1) | copy-start | bytes 1572868
  17.6 11.5 %collective-permute-start = (bf16[528,256]{1,0:T(8,128)(2,1)S(1)}, bf16[528,256]{1,0:T(8,128)(2,1)S(1)}, u32[]{:S(2)}, u32[]{:S(2)}) collective-permute-start(bf16[528,256]{1,0:T(8,128)(2,1)S(1)} %get-tuple-element.35), channel_id=1, source_target_pairs={{0,4},{4,8},{8,12},{12,16},{16,20},{20,24},{24,28},{1,5},{5,9},{9,... | collective-permute-start | bytes 811016 | tf_op jit(solution)/shard_map/ppermute | solution.py:625
  21.1 9.0 %collective-permute-start.3 = (bf16[528,256]{1,0:T(8,128)(2,1)S(1)}, bf16[528,256]{1,0:T(8,128)(2,1)S(1)}, u32[]{:S(2)}, u32[]{:S(2)}) collective-permute-start(bf16[528,256]{1,0:T(8,128)(2,1)S(1)} %get-tuple-element.41), channel_id=1, source_target_pairs={{4,0},{8,4},{12,8},{16,12},{20,16},{24,20},{28,24},{5,1},{9,5},{13... | collective-permute-start | bytes 811016 | tf_op jit(solution)/shard_map/ppermute | solution.py:626
  23.1 7.0 %copy-start = (bf16[8,128,256]{2,1,0:T(8,128)(2,1)S(1)}, bf16[8,128,256]{2,1,0:T(8,128)(2,1)}, u32[]{:S(2)}) copy-start(bf16[8,128,256]{2,1,0:T(8,128)(2,1)} %target.2) | copy-start | bytes 1572868
  30.2 8.7 %collective-permute-start.4 = (bf16[43,8,256]{2,1,0:T(8,128)(2,1)S(1)}, bf16[43,8,256]{2,1,0:T(8,128)(2,1)S(1)}, u32[]{:S(2)}, u32[]{:S(2)}) collective-permute-start(bf16[43,8,256]{2,1,0:T(8,128)(2,1)S(1)} %get-tuple-element.43), channel_id=1, source_target_pairs={{0,1},{1,2},{2,3},{4,5},{5,6},{6,7},{8,9},{9,10},{10,11},{12,13},{... | collective-permute-start | bytes 528392 | tf_op jit(solution)/shard_map/ppermute | solution.py:630
  33.4 6.2 %collective-permute-start.5 = (bf16[43,8,256]{2,1,0:T(8,128)(2,1)S(1)}, bf16[43,8,256]{2,1,0:T(8,128)(2,1)S(1)}, u32[]{:S(2)}, u32[]{:S(2)}) collective-permute-start(bf16[43,8,256]{2,1,0:T(8,128)(2,1)S(1)} %get-tuple-element.44), channel_id=1, source_target_pairs={{1,0},{2,1},{3,2},{5,4},{6,5},{7,6},{9,8},{10,9},{11,10},{13,12},{... | collective-permute-start | bytes 528392 | tf_op jit(solution)/shard_map/ppermute | solution.py:631
  39.6 18.1 %copy-start.2 = (bf16[512,512]{1,0:T(8,128)(2,1)S(1)}, bf16[512,512]{1,0:T(8,128)(2,1)}, u32[]{:S(2)}) copy-start(bf16[512,512]{1,0:T(8,128)(2,1)} %constant.32.clone.table.refs_5_) | copy-start | bytes 1572868
  39.6 18.1 %copy-start.7 = (bf16[192,256]{1,0:T(8,128)(2,1)S(1)}, bf16[192,256]{1,0:T(8,128)(2,1)}, u32[]{:S(2)}) copy-start(bf16[192,256]{1,0:T(8,128)(2,1)} %refs_4_.1) | copy-start | bytes 294916
  44.5 33.4 %copy-start.5 = (bf16[384,384]{1,0:T(8,128)(2,1)S(1)}, bf16[384,384]{1,0:T(8,128)(2,1)}, u32[]{:S(2)}) copy-start(bf16[384,384]{1,0:T(8,128)(2,1)} %mix.1) | copy-start | bytes 884740
  44.5 33.3 %copy-start.8 = (bf16[128,128]{1,0:T(8,128)(2,1)S(1)}, bf16[128,128]{1,0:T(8,128)(2,1)}, u32[]{:S(2)}) copy-start(bf16[128,128]{1,0:T(8,128)(2,1)} %constant.34.clone.table) | copy-start | bytes 98308
  44.5 33.3 %copy-start.9 = (bf16[128,128]{1,0:T(8,128)(2,1)S(1)}, bf16[128,128]{1,0:T(8,128)(2,1)}, u32[]{:S(2)}) copy-start(bf16[128,128]{1,0:T(8,128)(2,1)} %constant.33.clone.back_table) | copy-start | bytes 98308
  44.6 6.9 %collective-permute-start.6 = (bf16[2,128,256]{2,1,0:T(8,128)(2,1)S(1)}, bf16[2,128,256]{2,1,0:T(8,128)(2,1)S(1)}, u32[]{:S(2)}, u32[]{:S(2)}) collective-permute-start(bf16[2,128,256]{2,1,0:T(8,128)(2,1)S(1)} %get-tuple-element.54), channel_id=1, source_target_pairs={{0,1},{1,0},{2,3},{3,2},{4,5},{5,4},{6,7},{7,6},{8,9},{9,8},{10,11... | collective-permute-start | bytes 393224 | tf_op jit(solution)/shard_map/ppermute | solution.py:640
  46.0 11.7 %collective-permute-start.7 = (bf16[2,128,256]{2,1,0:T(8,128)(2,1)S(1)}, bf16[2,128,256]{2,1,0:T(8,128)(2,1)S(1)}, u32[]{:S(2)}, u32[]{:S(2)}) collective-permute-start(bf16[2,128,256]{2,1,0:T(8,128)(2,1)S(1)} %get-tuple-element.55), channel_id=1, source_target_pairs={{0,2},{1,3},{2,0},{3,1},{4,6},{5,7},{6,4},{7,5},{8,10},{9,11},{10,... | collective-permute-start | bytes 393224 | tf_op jit(solution)/shard_map/ppermute | solution.py:640
  47.7 10.0 %collective-permute-start.8 = (bf16[2,128,256]{2,1,0:T(8,128)(2,1)S(1)}, bf16[2,128,256]{2,1,0:T(8,128)(2,1)S(1)}, u32[]{:S(2)}, u32[]{:S(2)}) collective-permute-start(bf16[2,128,256]{2,1,0:T(8,128)(2,1)S(1)} %get-tuple-element.56), channel_id=1, source_target_pairs={{0,3},{1,2},{2,1},{3,0},{4,7},{5,6},{6,5},{7,4},{8,11},{9,10},{10,... | collective-permute-start | bytes 393224 | tf_op jit(solution)/shard_map/ppermute | solution.py:640
  77.9 17.7 %copy-start.3 = (bf16[512,192]{0,1:T(8,128)(2,1)S(1)}, bf16[512,192]{0,1:T(8,128)(2,1)}, u32[]{:S(2)}) copy-start(bf16[512,192]{0,1:T(8,128)(2,1)} %param.20) | copy-start | bytes 589828
  77.9 17.7 %copy-start.4 = (bf16[512,512]{1,0:T(8,128)(2,1)S(1)}, bf16[512,512]{1,0:T(8,128)(2,1)}, u32[]{:S(2)}) copy-start(bf16[512,512]{1,0:T(8,128)(2,1)} %constant.31.clone.table) | copy-start | bytes 1572868
  77.9 17.7 %copy-start.6 = (bf16[512,256]{1,0:T(8,128)(2,1)S(1)}, bf16[512,256]{1,0:T(8,128)(2,1)}, u32[]{:S(2)}) copy-start(bf16[512,256]{1,0:T(8,128)(2,1)} %weight_local.1) | copy-start | bytes 786436

commit v14 on v13

--- a/solution.py
+++ b/solution.py
@@ -69,11 +69,11 @@
     return jnp.concatenate([signal[block, r] for block in range(signal.shape[0])], axis=0)
 
 
-def grad_kernel(norm, col, *refs):
+def grad_kernel(norm, place, *refs):
     *pieces, weight, table, out, strip_out, projected = refs
     tile_cols = pieces[0].shape[1]
     for step, piece in enumerate(pieces):
-        block = col[0] ^ step
+        block = place[0] ^ step
         strip_out[block] = piece[...]
         rows = [dot_t(piece[r], weight[...]).astype(jnp.bfloat16) for r in range(piece.shape[0])]
         where = pl.ds(pl.multiple_of(block * tile_cols, tile_cols), tile_cols)
@@ -81,7 +81,7 @@
     out[...] = (dot(table[...], projected[...]) * norm).astype(jnp.bfloat16)
 
 
-def grad_spectrum(norm, col, pieces, weight, table):
+def grad_spectrum(norm, place, pieces, weight, table):
     strip, tile_cols, channels = pieces[0].shape
     shape = (table.shape[0], strip * weight.shape[0])
     in_vmem = pl.BlockSpec(memory_space=pltpu.VMEM)
@@ -96,7 +96,7 @@
         scratch_shapes=[pltpu.VMEM(shape, jnp.bfloat16)],
         compiler_params=pltpu.CompilerParams(vmem_limit_bytes=10 * MIB),
         cost_estimate=pl.CostEstimate(flops=0, bytes_accessed=2 * MIB, transcendentals=0),
-    )(col, *pieces, weight, table)
+    )(place, *pieces, weight, table)
 
 
 def fetching_spectrum_kernel(norm, signal, weight, table, out, signal_held, weight_held, table_held, sems):
@@ -198,6 +198,18 @@
 TAIL = 16
 
 
+def pick(flag, left, right):
+    return lax.select(flag, left.astype(jnp.float32), right.astype(jnp.float32))
+
+
+def odd_row(place):
+    return place[1] == 1
+
+
+def odd_col(place):
+    return lax.rem(place[0], 2) == 1
+
+
 def turned(rows):
     count, columns = rows.shape
     rows = rows.astype(jnp.float32)
@@ -210,12 +222,13 @@
 
 
 def prepare_kernel(
-    target, mask, first, second, down, up, mask_row, first_out, second_out, mask_held, sems
+    place, target, mask, first, second, early, late, mask_row, first_out, second_out, mask_held, sems
 ):
     tile_rows, tile_cols = mask.shape
     channels = target.shape[2]
     moves = [(mask, mask_held)]
-    for pack, start in ((down, tile_rows - NEAR), (up, 0)):
+    last = tile_rows - NEAR
+    for pack, start in ((early, (1 - place[1]) * last), (late, place[1] * last)):
         moves += [
             (target.at[start + i], pack.at[pl.ds(i * tile_cols, tile_cols)]) for i in range(NEAR)
         ]
@@ -225,63 +238,73 @@
         copy.start()
     copies[0].wait()
     mask_row[0] = filled(turned(mask_held[...]), channels)
-    for pack, start in ((down, tile_rows - NEAR), (up, 0)):
-        rows = mask_held[start : start + NEAR].astype(jnp.float32)
+    ends = (mask_held[:NEAR], mask_held[last:])
+    for pack, (one, other) in ((early, ends), (late, ends[::-1])):
+        rows = pick(odd_row(place), one, other)
         rows = jnp.concatenate([rows, jnp.zeros((TAIL - NEAR, tile_cols), jnp.float32)], axis=0)
         pack[NEAR * tile_cols :] = filled(rows, channels)
     for copy in copies[1:]:
         copy.wait()
 
 
-def prepare(target, mask, first, second):
+def prepare(place, target, mask, first, second):
     _, tile_cols, channels = target.shape
     pack = (NEAR * tile_cols + TAIL, channels)
     shapes = [pack, pack, (1, tile_cols, channels), first.shape, second.shape]
     return pl.pallas_call(
         prepare_kernel,
         out_shape=[jax.ShapeDtypeStruct(shape, jnp.bfloat16) for shape in shapes],
-        in_specs=[pl.BlockSpec(memory_space=pltpu.HBM)] * 4,
+        in_specs=[pl.BlockSpec(memory_space=pltpu.SMEM)] + [pl.BlockSpec(memory_space=pltpu.HBM)] * 4,
         out_specs=[pl.BlockSpec(memory_space=pltpu.VMEM)] * len(shapes),
         scratch_shapes=[pltpu.VMEM(mask.shape, mask.dtype), pltpu.SemaphoreType.DMA((2 * NEAR + 3,))],
         compiler_params=pltpu.CompilerParams(vmem_limit_bytes=6 * MIB),
         cost_estimate=pl.CostEstimate(flops=0, bytes_accessed=2 * MIB, transcendentals=0),
-    )(*[in_hbm(a) for a in (target, mask, first, second)])
-
-
-def edge_kernel(tile_cols, *refs):
-    above_pack, below_pack, *sources = refs[:-3]
-    last, initial, own = refs[-3:]
+    )(place, *[in_hbm(a) for a in (target, mask, first, second)])
+
+
+def edge_kernel(tile_cols, place, early_pack, late_pack, *refs):
+    sources, (early, late, own) = refs[:-3], refs[-3:]
     count = len(sources) // 2
     keep = 2 * REACH
     channels = own.shape[2]
+    low, high = odd_row(place), odd_col(place)
 
     def put_rows(row, tail, head):
         rows = slice(row, row + tail.shape[0])
-        last[rows] = tail[:, REACH:]
-        initial[rows] = head[:, :REACH]
-        own[rows, :keep] = head
-        own[rows, keep:] = tail
-
-    def put_pack(row, pack):
+        last, initial = tail[:, REACH:], head[:, :REACH]
+        early[rows] = pick(high, initial, last).astype(jnp.bfloat16)
+        late[rows] = pick(high, last, initial).astype(jnp.bfloat16)
+        own[rows, :keep] = head.astype(jnp.bfloat16)
+        own[rows, keep:] = tail.astype(jnp.bfloat16)
+
+    def put_pack(row, one, other):
         for i in range(NEAR):
-            pixels = pack[i * tile_cols : (i + 1) * tile_cols]
-            put_rows(row + i, pixels[None, tile_cols - keep :], pixels[None, :keep])
-        mask = turned(pack[NEAR * tile_cols :, :tile_cols])
+            at = i * tile_cols
+            tail = pick(low, one[at + tile_cols - keep : at + tile_cols], other[at + tile_cols - keep : at + tile_cols])
+            head = pick(low, one[at : at + keep], other[at : at + keep])
+            put_rows(row + i, tail[None], head[None])
+        mask = turned(pick(low, one[NEAR * tile_cols :, :tile_cols], other[NEAR * tile_cols :, :tile_cols]))
         tail, head = [filled(m, channels)[None] for m in (mask[tile_cols - keep :], mask[:keep])]
         put_rows(row + NEAR, tail, head)
 
-    row = 0
-    for index, (tail, head) in enumerate(zip(sources[:count], sources[count:])):
-        if index == 3:
-            put_pack(row, above_pack)
-            row += NEAR + 1
-        put_rows(row, tail[...], head[...])
-        row += tail.shape[0]
-    put_pack(row, below_pack)
-
-
-def edges(above, features, below, above_pack, target, mask_row, below_pack):
-    parts = (above, features, below, target, mask_row)
+    def put_picked(row, one, other):
+        put_rows(row, *[pick(low, sources[one + i * count][...], sources[other + i * count][...]) for i in (0, 1)])
+
+    def put_own(row, index):
+        put_rows(row, sources[index][...], sources[index + count][...])
+
+    rows = sources[0].shape[0]
+    put_picked(0, 0, 1)
+    put_own(rows, 2)
+    put_picked(2 * rows, 1, 0)
+    put_pack(3 * rows, early_pack, late_pack)
+    put_own(3 * rows + NEAR + 1, 3)
+    put_own(4 * rows + NEAR + 1, 4)
+    put_pack(4 * rows + NEAR + 2, late_pack, early_pack)
+
+
+def edges(place, early, late, features, target, mask_row, early_pack, late_pack):
+    parts = (early, late, features, target, mask_row)
     _, tile_cols, channels = features.shape
     keep = 2 * REACH
     tail = tile_cols // keep - 1
@@ -289,20 +312,20 @@
     def specs(at):
         return [pl.BlockSpec((p.shape[0], keep, channels), lambda i, at=at: (0, at, 0)) for p in parts]
 
-    whole = [pl.BlockSpec(above_pack.shape, lambda i: (0, 0))] * 2
+    whole = [pl.BlockSpec(early_pack.shape, lambda i: (0, 0))] * 2
     rows = sum(p.shape[0] for p in parts) + 2 * (NEAR + 1)
     shapes = [(rows, columns, channels) for columns in (REACH, REACH, 2 * keep)]
     return pl.pallas_call(
         functools.partial(edge_kernel, tile_cols),
         grid=(1,),
         out_shape=[jax.ShapeDtypeStruct(shape, features.dtype) for shape in shapes],
-        in_specs=whole + specs(tail) + specs(0),
+        in_specs=[pl.BlockSpec(memory_space=pltpu.SMEM)] + whole + specs(tail) + specs(0),
         out_specs=[pl.BlockSpec(shape, lambda i: (0, 0, 0)) for shape in shapes],
         compiler_params=pltpu.CompilerParams(vmem_limit_bytes=8 * MIB),
         cost_estimate=pl.CostEstimate(
             flops=0, bytes_accessed=16 * rows * keep * channels, transcendentals=0
         ),
-    )(above_pack, below_pack, *parts, *parts)
+    )(place, early_pack, late_pack, *parts, *parts)
 
 
 def put(wide, row, value, stride):
@@ -386,13 +409,17 @@
 SIDE_BLOCKS = (10, 8, 12, 8)
 
 
-def tile_forward_kernel(above, features, below, first, second, ok, pre, slopes, wide_even, wide_odd):
+def tile_forward_kernel(
+    place, early, features, late, first, second, ok, pre, slopes, wide_even, wide_odd
+):
     rows, stride, _ = features.shape
-    find = part_of(rows, REACH, above, features, below)
+    find = part_of(rows, REACH, (early, late), (features,), (late, early))
 
     def feature(row):
-        source, at = find(row)
-        return source[at].astype(jnp.float32)
+        sources, at = find(row)
+        if len(sources) == 1:
+            return features[at].astype(jnp.float32)
+        return pick(odd_row(place), *[source[at] for source in sources])
 
     def inside(row):
         return ok[REACH : REACH + stride, row : row + 1]
@@ -406,11 +433,12 @@
 
 
 def tile_backward_kernel(
+    place,
     pre,
     slopes,
-    target_above,
+    early_pack,
     target,
-    target_below,
+    late_pack,
     mask_row,
     first,
     second,
@@ -420,14 +448,21 @@
     wide_odd,
 ):
     rows, stride, channels = target.shape
-    find = part_of(rows, NEAR, target_above, target, target_below)
+    packs = (early_pack, late_pack)
+    find = part_of(rows, NEAR, packs, (target,), packs[::-1])
+
+    def picked(sources, part):
+        return pick(odd_row(place), *[source[part] for source in sources])
 
     def goal(row):
-        source, at = find(row)
-        pixels = source[at] if source is target else source[at * stride : (at + 1) * stride]
-        return pixels.astype(jnp.float32)
-
-    masks = [turned(pack[NEAR * stride :, :stride]) for pack in (target_above, target_below)]
+        sources, at = find(row)
+        if len(sources) == 1:
+            return target[at].astype(jnp.float32)
+        return picked(sources, slice(at * stride, (at + 1) * stride))
+
+    masks = [
+        turned(picked(sources, slice(NEAR * stride, None))[:, :stride]) for sources in (packs, packs[::-1])
+    ]
     find_mask = part_of(rows, NEAR, (masks[0], 0), (mask_row[0].astype(jnp.float32), 0), (masks[1], 0))
 
     def hole(row):
@@ -448,16 +483,17 @@
     last_stages(stride, TILE_BLOCKS, rows, first, second, wide_even, wide_odd, slopes, use)
 
 
-def side_kernel(col, before, after, own, first, second, ok, tile, *refs):
+def side_kernel(place, early, late, own, first, second, ok, tile, *refs):
     *pieces, out, wide_even, wide_odd, slopes = refs
     rows, tile_cols, channels = tile.shape
     keep = 2 * REACH
     stride = 2 * (REACH + keep)
     tall = rows + 2 * REACH
+    odd = odd_col(place)
 
     def feature(row):
-        parts = [part[row].astype(jnp.float32) for part in (before, own, after)]
-        return jnp.concatenate(parts, axis=0)
+        before, after = pick(odd, early[row], late[row]), pick(odd, late[row], early[row])
+        return jnp.concatenate([before, own[row].astype(jnp.float32), after], axis=0)
 
     find = part_of(rows, NEAR, tall, tall + NEAR + 1, tall + NEAR + 1 + rows + 1)
 
@@ -465,7 +501,7 @@
         start, at = find(row)
         return feature(start + at)
 
-    masks = [feature(row) for row in (tall + NEAR, tall + NEAR + 1 + rows, before.shape[0] - 1)]
+    masks = [feature(row) for row in (tall + NEAR, tall + NEAR + 1 + rows, early.shape[0] - 1)]
     find_mask = part_of(rows, NEAR, (masks[0], 0), (masks[1], 0), (masks[2], 0))
 
     def hole(row):
@@ -493,54 +529,53 @@
 
     last_stages(stride, SIDE_BLOCKS, rows, first, second, wide_even, wide_odd, slopes, use)
     for step, piece in enumerate(pieces):
-        piece[...] = out[pl.ds((col[0] ^ step) * piece.shape[0], piece.shape[0])]
+        piece[...] = out[pl.ds((place[0] ^ step) * piece.shape[0], piece.shape[0])]
 
 
 def wide_buffer(rows, stride, channels):
     return pltpu.VMEM((rows * stride, 3 * channels), jnp.bfloat16)
 
 
-def tile_forward(above, features, below, first, second, ok):
+def tile_forward(place, early, features, late, first, second, ok):
     rows, stride, channels = features.shape
     shapes = [
         jax.ShapeDtypeStruct(((rows + h) * stride, channels), jnp.float32) for h in (2 * NEAR, 4)
     ]
-    return vmem_call(
+    in_vmem = pl.BlockSpec(memory_space=pltpu.VMEM)
+    return pl.pallas_call(
         tile_forward_kernel,
-        shapes,
-        above,
-        features,
-        below,
-        first,
-        second,
-        ok,
-        flops=2 * 9 * channels * channels * stride * (2 * rows + 20),
-        scratch=[wide_buffer(rows + h, stride, channels) for h in (16, 12)],
-        limit=18,
-    )
-
-
-def tile_backward(pre, slopes, target_above, target, target_below, mask_row, first, second, ok):
+        out_shape=shapes,
+        in_specs=[pl.BlockSpec(memory_space=pltpu.SMEM)] + [in_vmem] * 6,
+        out_specs=[in_vmem] * 2,
+        scratch_shapes=[wide_buffer(rows + h, stride, channels) for h in (16, 12)],
+        compiler_params=pltpu.CompilerParams(vmem_limit_bytes=18 * MIB),
+        cost_estimate=pl.CostEstimate(
+            flops=2 * 9 * channels * channels * stride * (2 * rows + 20),
+            bytes_accessed=8 * MIB,
+            transcendentals=0,
+        ),
+    )(place, early, features, late, first, second, ok)
+
+
+def tile_backward(place, pre, slopes, early_pack, target, *operands):
     rows, stride, channels = target.shape
-    return vmem_call(
+    in_vmem = pl.BlockSpec(memory_space=pltpu.VMEM)
+    return pl.pallas_call(
         tile_backward_kernel,
-        [jax.ShapeDtypeStruct(target.shape, jnp.bfloat16)],
-        pre,
-        slopes,
-        target_above,
-        target,
-        target_below,
-        mask_row,
-        first,
-        second,
-        ok,
-        flops=2 * 9 * channels * channels * stride * (2 * rows + 4),
-        scratch=[wide_buffer(rows + h, stride, channels) for h in (8, 4)],
-        limit=16,
-    )[0]
-
-
-def sides(col, tile, *operands):
+        out_shape=jax.ShapeDtypeStruct(target.shape, jnp.bfloat16),
+        in_specs=[pl.BlockSpec(memory_space=pltpu.SMEM)] + [in_vmem] * (4 + len(operands)),
+        out_specs=in_vmem,
+        scratch_shapes=[wide_buffer(rows + h, stride, channels) for h in (8, 4)],
+        compiler_params=pltpu.CompilerParams(vmem_limit_bytes=16 * MIB),
+        cost_estimate=pl.CostEstimate(
+            flops=2 * 9 * channels * channels * stride * (2 * rows + 4),
+            bytes_accessed=8 * MIB,
+            transcendentals=0,
+        ),
+    )(place, pre, slopes, early_pack, target, *operands)
+
+
+def sides(place, tile, *operands):
     rows, tile_cols, channels = tile.shape
     stride = 6 * REACH
     count = lax.axis_size("col")
@@ -562,13 +597,13 @@
             bytes_accessed=4 * MIB,
             transcendentals=0,
         ),
-    )(col, *operands, tile)
-
-
-def neighbours(axis):
+    )(place, *operands, tile)
+
+
+def pairs(axis, start):
     size = lax.axis_size(axis)
-    up = [(i, i + 1) for i in range(size - 1)]
-    return up, [(j, i) for i, j in up]
+    up = [(i, i + 1) for i in range(start, size - 1, 2)]
+    return up + [(j, i) for i, j in up]
 
 
 def shards(
@@ -606,39 +641,39 @@
     col_ids = col0 - REACH + jnp.arange(tile_cols + 2 * REACH, dtype=jnp.int32)
     ok = ((col_ids >= 0) & (col_ids < width))[:, None] & ((row_ids >= 0) & (row_ids < height))[None]
     ok = ok.astype(jnp.float32)
-    col = jnp.full((1,), lax.axis_index("col"), jnp.int32)
-    inputs, ok, col = lax.optimization_barrier((inputs, ok, col))
+    place = jnp.stack([lax.axis_index("col"), lax.axis_index("row") & 1]).astype(jnp.int32)
+    inputs, ok, place = lax.optimization_barrier((inputs, ok, place))
 
     cells = [jax.ShapeDtypeStruct((width, strip * half), bf16)]
     weight_in = weight_in.T
     spatial_cols = fetching_spectrum(col_norm, cells[0], inputs, weight_in, table)
     spatial_moved = swap(spatial_cols)
 
-    up, down = neighbours("row")
-    left, right = neighbours("col")
-    above = lax.ppermute(features, "row", up)
-    below = lax.ppermute(features, "row", down)
+    early = lax.ppermute(features, "row", pairs("row", 0))
+    late = lax.ppermute(features, "row", pairs("row", 1))
     target_after, spatial_cols = lax.optimization_barrier((target, spatial_cols))
-    pack_down, pack_up, mask_row, kernel_first, kernel_second = prepare(
-        target_after, hole_mask, kernel_first, kernel_second
+    early_pack, late_pack, mask_row, kernel_first, kernel_second = prepare(
+        place, target_after, hole_mask, kernel_first, kernel_second
     )
-    target_above = lax.ppermute(pack_down, "row", up)
-    target_below = lax.ppermute(pack_up, "row", down)
-    pre, slopes = tile_forward(above, features, below, kernel_first, kernel_second, ok)
-    target_above, pre = lax.optimization_barrier((target_above, pre))
-    last, initial, own = edges(above, features, below, target_above, target, mask_row, target_below)
-    before = lax.ppermute(last, "col", left)
-    after = lax.ppermute(initial, "col", right)
+    early_pack = lax.ppermute(early_pack, "row", pairs("row", 0))
+    late_pack = lax.ppermute(late_pack, "row", pairs("row", 1))
+    pre, slopes = tile_forward(place, early, features, late, kernel_first, kernel_second, ok)
+    early_pack, pre = lax.optimization_barrier((early_pack, pre))
+    early_edge, late_edge, own = edges(
+        place, early, late, features, target, mask_row, early_pack, late_pack
+    )
+    early_edge = lax.ppermute(early_edge, "col", pairs("col", 0))
+    late_edge = lax.ppermute(late_edge, "col", pairs("col", 1))
     tile = tile_backward(
-        pre, slopes, target_above, target, target_below, mask_row, kernel_first, kernel_second, ok
+        place, pre, slopes, early_pack, target, late_pack, mask_row, kernel_first, kernel_second, ok
     )
-    pieces = sides(col, tile, before, after, own, kernel_first, kernel_second, ok)
+    pieces = sides(place, tile, early_edge, late_edge, own, kernel_first, kernel_second, ok)
     pieces, spatial_moved = lax.optimization_barrier((pieces, spatial_moved))
     moved = [pieces[0]]
     for step in range(1, col_devices):
         swaps = [(i, i ^ step) for i in range(col_devices)]
         moved.append(lax.ppermute(pieces[step], "col", swaps))
-    grad_cols, strip_grad = grad_spectrum(col_norm, col, moved, weight_out, table)
+    grad_cols, strip_grad = grad_spectrum(col_norm, place, moved, weight_out, table)
     wide = pltpu.VMEM((strip * half // LANES, width, LANES), jnp.float32)
     grad_rows = vmem_call(
         functools.partial(mix_kernel, row_norm, owned, devices),

time: 98.9 us -> 96.1 us (0.972)
  starting transfers between devices: 25.8 us -> 21.7 us
  Pallas kernels: 25.2 us -> 28.4 us
  waiting for transfers between devices: 11.3 us -> 9.19 us
    pallas_call x0 -> x2, Pallas kernels: none -> 11 us  [the longest x1 6.53 us: tile_forward(): pl.pallas_call(tile_forward_kernel, out_shape=shapes, in_specs=[pl.BlockS...]
    pallas_call x4 -> x2, Pallas kernels: 14 us -> 4.01 us  [vmem_call(): pl.pallas_call(body, out_shape=shapes, in_specs=[spec] * len(operands), o...]
    ppermute x6, starting transfers between devices: 16.6 us -> 11.4 us  [the longest x1 4.5 us: shards(): late = lax.ppermute(features, 'row', pairs('row', 1))]
    ppermute x3, starting transfers between devices: 3.61 us -> 5.19 us  [shards(): moved.append(lax.ppermute(pieces[step], 'col', swaps))]
    ppermute x3, waiting for transfers between devices: 9.58 us -> 8.09 us  [shards(): moved.append(lax.ppermute(pieces[step], 'col', swaps))]
  transfers between devices with their start and end apart: 10 -> 10, of which waited for: 4 -> 3; matrix products, arithmetic and copies ran while one was open for 0% -> 0% of each run, Pallas kernels for 21% -> 24%
where the time goes in v14:
time: 96.1 us; the launch traced here: 94.8 us
  blocking collectives  35 us (36%)
  Pallas kernels  28.4 us (30%)
  starting transfers between devices  21.7 us (23%)
  waiting for transfers between devices  9.19 us (10%)
    all_to_all x2, blocking collectives, swap(): lax.all_to_all(spectrum, ('col', 'row'), split_axis=0, concat_axis=0, til...  35 us
    ppermute x3, waiting for transfers between devices, shards(): moved.append(lax.ppermute(pieces[step], 'col', swaps))  8.09 us
    pallas_call x1, Pallas kernels, tile_forward(): pl.pallas_call(tile_forward_kernel, out_shape=shapes, in_specs=[pl.BlockS...  6.53 us
    pallas_call x1, Pallas kernels, sides(): pl.pallas_call(side_kernel, out_shape=[piece] * count, in_specs=[pl.Block...  5.33 us
    ppermute x3, starting transfers between devices, shards(): moved.append(lax.ppermute(pieces[step], 'col', swaps))  5.19 us
    all_to_all x1, starting transfers between devices, swap(): lax.all_to_all(spectrum, ('col', 'row'), split_axis=0, concat_axis=0, til...  5.14 us
    pallas_call x1, Pallas kernels, tile_backward(): pl.pallas_call(tile_backward_kernel, out_shape=jax.ShapeDtypeStruct(targe...  4.51 us
    ppermute x1, starting transfers between devices, shards(): late = lax.ppermute(features, 'row', pairs('row', 1))  4.5 us
  transfers between devices with their start and end apart: 10, of which 3 were waited for; matrix products, arithmetic and copies ran while one was open for 0% of the time, Pallas kernels for 24%

profile of v14, /device:TPU:1, one launch (start us, length us, event | category | flops | bytes accessed | tf_op | source)
XLA Modules:
  0.0 94.8 jit_solution(1190834129937841198)
XLA Ops:
  0.0 4.5 %collective-permute-start.2 = (bf16[8,128,256]{2,1,0:T(8,128)(2,1)}, bf16[8,128,256]{2,1,0:T(8,128)(2,1)S(1)}, u32[]{:S(2)}, u32[]{:S(2)}) collective-permute-start(bf16[8,128,256]{2,1,0:T(8,128)(2,1)} %refs_7_.1), channel_id=1, source_target_pairs={{4,8},{12,16},{20,24},{8,4},{16,12},{24,20},{5,9},{13,17},{21,25},... | collective-permute-start | bytes 1572872 | tf_op jit(solution)/shard_map/ppermute | solution.py:653
  4.5 0.1 collective-permute-start.1
  4.6 0.1 pad_add_fusion.place
  4.7 0.1 and_convert_fusion.ok
  4.8 3.3 %shard_map.136 = bf16[512,384]{1,0:T(8,128)(2,1)} custom-call(bf16[2,512,512]{2,1,0:T(8,128)(2,1)} %signal, bf16[192,512]{1,0:T(8,128)(2,1)} %bitcast.13, bf16[512,512]{1,0:T(8,128)(2,1)} %constant.34.clone.table.refs_5_), custom_call_target="tpu_custom_call" | custom-call | bytes 2097152 | tf_op jit(solution)/shard_map/pallas_call | solution.py:122
  8.1 5.1 %all-to-all-start = ((bf16[32,16,384]{2,1,0:T(8,128)(2,1)}), bf16[32,16,384]{2,1,0:T(8,128)(2,1)S(1)}, u32[]{:S(2)}, u32[]{:S(2)}) async-start(bf16[32,16,384]{2,1,0:T(8,128)(2,1)} %bitcast.3), calls=%async_computation | async-start | bytes 786432 | tf_op jit(solution)/shard_map/all_to_all | solution.py:637
  13.3 0.0 copy-start.1
  13.3 2.6 %shard_map.137 = (bf16[528,256]{1,0:T(8,128)(2,1)S(1)}, bf16[528,256]{1,0:T(8,128)(2,1)S(1)}, bf16[1,128,256]{2,1,0:T(8,128)(2,1)S(1)}, bf16[3,3,256,256]{3,2,1,0:T(8,128)(2,1)S(1)}, bf16[3,3,256,256]{3,2,1,0:T(8,128)(2,1)S(1)}) custom-call(s32[2]{0:T(128)S(1)} %pad_add_fusion.place, bf16[8,128,256]{2,1,0:T(8,128)(2,1)} %target.2, s32[8,128]{1,0:T(8,128)} %mask.1, ...), custom_call_target="tpu_custom_call" | custom-call | bytes 2097152 | tf_op jit(solution)/shard_map/pallas_call | solution.py:254
  15.8 0.3 collective-permute-start
  16.2 3.4 %collective-permute-start.3 = (bf16[528,256]{1,0:T(8,128)(2,1)S(1)}, bf16[528,256]{1,0:T(8,128)(2,1)S(1)}, u32[]{:S(2)}, u32[]{:S(2)}) collective-permute-start(bf16[528,256]{1,0:T(8,128)(2,1)S(1)} %get-tuple-element.41), channel_id=1, source_target_pairs={{4,8},{12,16},{20,24},{8,4},{16,12},{24,20},{5,9},{13,17},{21,25},... | collective-permute-start | bytes 811016 | tf_op jit(solution)/shard_map/ppermute | solution.py:659
  19.6 0.0 copy-start
  19.6 6.5 %shard_map.138 = (f32[2048,256]{1,0:T(8,128)S(1)}, f32[1536,256]{1,0:T(8,128)S(1)}) custom-call(s32[2]{0:T(128)S(1)} %pad_add_fusion.place, bf16[8,128,256]{2,1,0:T(8,128)(2,1)S(1)} %collective-permute-done.1.early.refs_0_.refs_5_, bf16[8,128,256]{2,1,0:T(8,128)(2,1)S(1)} %copy-done.1, bf16[8,128,256]{2,1,0:T(8,128)(2,1)S(1)} %collective-permute-done.2.late.refs_1_.refs_6_, ...), custom_call_target="tpu_custom_call" | custom-call | flops 5435817984 | bytes 8388608 | tf_op jit(solution)/shard_map/pallas_call | solution.py:545
  26.2 1.1 %collective-permute-done.3.late_pack = bf16[528,256]{1,0:T(8,128)(2,1)S(1)} collective-permute-done((bf16[528,256]{1,0:T(8,128)(2,1)S(1)}, bf16[528,256]{1,0:T(8,128)(2,1)S(1)}, u32[]{:S(2)}, u32[]{:S(2)}) %collective-permute-start.3) | collective-permute-done | bytes 270368 | tf_op jit(solution)/shard_map/ppermute | solution.py:659
  27.3 0.8 shard_map.139
  28.0 2.2 %collective-permute-start.4 = (bf16[43,8,256]{2,1,0:T(8,128)(2,1)S(1)}, bf16[43,8,256]{2,1,0:T(8,128)(2,1)S(1)}, u32[]{:S(2)}, u32[]{:S(2)}) collective-permute-start(bf16[43,8,256]{2,1,0:T(8,128)(2,1)S(1)} %get-tuple-element.43), channel_id=1, source_target_pairs={{0,1},{2,3},{1,0},{3,2},{4,5},{6,7},{5,4},{7,6},{8,9},{10,11},{9,8... | collective-permute-start | bytes 528392 | tf_op jit(solution)/shard_map/ppermute | solution.py:665
  30.2 0.8 collective-permute-start.5
  31.1 4.5 %shard_map.140.tile = bf16[8,128,256]{2,1,0:T(8,128)(2,1)S(1)} custom-call(s32[2]{0:T(128)S(1)} %pad_add_fusion.place, f32[2048,256]{1,0:T(8,128)S(1)} %get-tuple-element.46.pre, f32[1536,256]{1,0:T(8,128)S(1)} %get-tuple-element.47.slopes, bf16[528,256]{1,0:T(8,128)(2,1)S(1)} %collective-permute-done.early_pack, bf16[8,128,256]{2,1,0:T(8,128)(2,1)S(1)} %copy-done, ...), custom_call_target="tpu_custom_call" | custom-call | flops 3019898880 | bytes 8388608 | tf_op jit(solution)/shard_map/pallas_call | solution.py:563
  35.6 0.0 copy-start.2
  35.6 0.0 copy-start.7
  35.6 5.3 %shard_map.141 = (bf16[2,128,256]{2,1,0:T(8,128)(2,1)S(1)}, bf16[2,128,256]{2,1,0:T(8,128)(2,1)S(1)}, bf16[2,128,256]{2,1,0:T(8,128)(2,1)S(1)}, bf16[2,128,256]{2,1,0:T(8,128)(2,1)S(1)}) custom-call(s32[2]{0:T(128)S(1)} %pad_add_fusion.place, bf16[43,8,256]{2,1,0:T(8,128)(2,1)S(1)} %collective-permute-done.4.early, ...), custom_call_target="tpu_custom_call" | custom-call | flops 3170893824 | bytes 4194304 | tf_op jit(solution)/shard_map/pallas_call | solution.py:584
  41.0 0.0 copy-start.5
  41.0 0.0 copy-start.8
  41.0 0.0 copy-start.9
  41.0 3.0 %collective-permute-start.6 = (bf16[2,128,256]{2,1,0:T(8,128)(2,1)S(1)}, bf16[2,128,256]{2,1,0:T(8,128)(2,1)S(1)}, u32[]{:S(2)}, u32[]{:S(2)}) collective-permute-start(bf16[2,128,256]{2,1,0:T(8,128)(2,1)S(1)} %get-tuple-element.54), channel_id=1, source_target_pairs={{0,1},{1,0},{2,3},{3,2},{4,5},{5,4},{6,7},{7,6},{8,9},{9,8},{10,11... | collective-permute-start | bytes 393224 | tf_op jit(solution)/shard_map/ppermute | solution.py:675
  44.0 2.2 %collective-permute-start.8 = (bf16[2,128,256]{2,1,0:T(8,128)(2,1)S(1)}, bf16[2,128,256]{2,1,0:T(8,128)(2,1)S(1)}, u32[]{:S(2)}, u32[]{:S(2)}) collective-permute-start(bf16[2,128,256]{2,1,0:T(8,128)(2,1)S(1)} %get-tuple-element.56), channel_id=1, source_target_pairs={{0,3},{1,2},{2,1},{3,0},{4,7},{5,6},{6,5},{7,4},{8,11},{9,10},{10,... | collective-permute-start | bytes 393224 | tf_op jit(solution)/shard_map/ppermute | solution.py:675
  46.2 1.2 %collective-permute-done.6.refs_1_ = bf16[2,128,256]{2,1,0:T(8,128)(2,1)S(1)} collective-permute-done((bf16[2,128,256]{2,1,0:T(8,128)(2,1)S(1)}, bf16[2,128,256]{2,1,0:T(8,128)(2,1)S(1)}, u32[]{:S(2)}, u32[]{:S(2)}) %collective-permute-start.6) | collective-permute-done | bytes 131104 | tf_op jit(solution)/shard_map/ppermute | solution.py:675
  47.4 6.9 %collective-permute-done.7.refs_2_ = bf16[2,128,256]{2,1,0:T(8,128)(2,1)S(1)} collective-permute-done((bf16[2,128,256]{2,1,0:T(8,128)(2,1)S(1)}, bf16[2,128,256]{2,1,0:T(8,128)(2,1)S(1)}, u32[]{:S(2)}, u32[]{:S(2)}) %collective-permute-start.7) | collective-permute-done | bytes 131104 | tf_op jit(solution)/shard_map/ppermute | solution.py:675
  54.3 1.4 %shard_map.142 = (bf16[512,384]{1,0:T(8,128)(2,1)S(1)}, bf16[4,2,128,256]{3,2,1,0:T(8,128)(2,1)S(1)}) custom-call(s32[2]{0:T(128)S(1)} %pad_add_fusion.place, bf16[2,128,256]{2,1,0:T(8,128)(2,1)S(1)} %get-tuple-element.53.refs_0_, bf16[2,128,256]{2,1,0:T(8,128)(2,1)S(1)} %collective-permute-done.6.refs_1_, ...), custom_call_target="tpu_custom_call" | custom-call | bytes 2097152 | tf_op jit(solution)/shard_map/pallas_call | solution.py:88
  55.7 19.4 %all_to_all.34 = bf16[32,16,384]{2,1,0:T(8,128)(2,1)S(1)} all-to-all(bf16[32,16,384]{2,1,0:T(8,128)(2,1)S(1)} %bitcast.15), channel_id=1, replica_groups=mesh['row'=8,'col'=4] {'col','row'}, dimensions={0} | all-to-all | bytes 786432 | tf_op jit(solution)/shard_map/all_to_all | solution.py:637
  75.2 2.1 %shard_map.143 = bf16[512,384]{1,0:T(8,128)(2,1)S(1)} custom-call(bf16[512,384]{1,0:T(8,128)(2,1)S(1)} %bitcast.9, bf16[512,384]{1,0:T(8,128)(2,1)S(1)} %bitcast.10, bf16[384,384]{1,0:T(8,128)(2,1)S(1)} %copy-done.5, bf16[128,128]{1,0:T(8,128)(2,1)S(1)} %copy-done.8, bf16[128,128]{1,0:T(8,128)(2,1)S(1)} %copy-done.9), custom_call_target="tpu_custom_call" | custom-call | bytes 1540096 | tf_op jit(solution)/shard_map/pallas_call | solution.py:30
  77.3 15.6 %all_to_all.35 = bf16[32,16,384]{2,1,0:T(8,128)(2,1)S(1)} all-to-all(bf16[32,16,384]{2,1,0:T(8,128)(2,1)S(1)} %bitcast.11), channel_id=1, replica_groups=mesh['row'=8,'col'=4] {'col','row'}, dimensions={0} | all-to-all | bytes 786432 | tf_op jit(solution)/shard_map/all_to_all | solution.py:637
  92.9 2.0 %shard_map.144 = bf16[2,512,512]{2,1,0:T(8,128)(2,1)} custom-call(bf16[512,384]{1,0:T(8,128)(2,1)S(1)} %bitcast.12, bf16[4,2,128,256]{3,2,1,0:T(8,128)(2,1)S(1)} %get-tuple-element.58.strip_grad, bf16[192,512]{1,0:T(8,128)(2,1)S(1)} %bitcast.14, bf16[512,256]{1,0:T(8,128)(2,1)S(1)} %copy-done.6, bf16[512,512]{1,0:T(8,128)(2,1)S(1)} %copy-done.4), custom_call_target="tpu_custom_call" | custom-call | bytes 2949120 | tf_op jit(solution)/shard_map/pallas_call | solution.py:30
  (23 shorter events, 0.1 us)
Async XLA Ops:
  0.0 19.6 %collective-permute-start.2 = (bf16[8,128,256]{2,1,0:T(8,128)(2,1)}, bf16[8,128,256]{2,1,0:T(8,128)(2,1)S(1)}, u32[]{:S(2)}, u32[]{:S(2)}) collective-permute-start(bf16[8,128,256]{2,1,0:T(8,128)(2,1)} %refs_7_.1), channel_id=1, source_target_pairs={{4,8},{12,16},{20,24},{8,4},{16,12},{24,20},{5,9},{13,17},{21,25},... | collective-permute-start | bytes 1572872 | tf_op jit(solution)/shard_map/ppermute | solution.py:653
  4.5 15.1 %collective-permute-start.1 = (bf16[8,128,256]{2,1,0:T(8,128)(2,1)}, bf16[8,128,256]{2,1,0:T(8,128)(2,1)S(1)}, u32[]{:S(2)}, u32[]{:S(2)}) collective-permute-start(bf16[8,128,256]{2,1,0:T(8,128)(2,1)} %refs_7_.1), channel_id=1, source_target_pairs={{0,4},{8,12},{16,20},{24,28},{4,0},{12,8},{20,16},{28,24},{1,5},{9... | collective-permute-start | bytes 1572872 | tf_op jit(solution)/shard_map/ppermute | solution.py:652
  8.1 32.9 %all-to-all-start = ((bf16[32,16,384]{2,1,0:T(8,128)(2,1)}), bf16[32,16,384]{2,1,0:T(8,128)(2,1)S(1)}, u32[]{:S(2)}, u32[]{:S(2)}) async-start(bf16[32,16,384]{2,1,0:T(8,128)(2,1)} %bitcast.3), calls=%async_computation | async-start | bytes 786432 | tf_op jit(solution)/shard_map/all_to_all | solution.py:637
  13.3 6.4 %copy-start.1 = (bf16[8,128,256]{2,1,0:T(8,128)(2,1)S(1)}, bf16[8,128,256]{2,1,0:T(8,128)(2,1)}, u32[]{:S(2)}) copy-start(bf16[8,128,256]{2,1,0:T(8,128)(2,1)} %refs_7_.1) | copy-start | bytes 1572868
  15.8 10.3 %collective-permute-start = (bf16[528,256]{1,0:T(8,128)(2,1)S(1)}, bf16[528,256]{1,0:T(8,128)(2,1)S(1)}, u32[]{:S(2)}, u32[]{:S(2)}) collective-permute-start(bf16[528,256]{1,0:T(8,128)(2,1)S(1)} %get-tuple-element.35), channel_id=1, source_target_pairs={{0,4},{8,12},{16,20},{24,28},{4,0},{12,8},{20,16},{28,24},{1,5},{9... | collective-permute-start | bytes 811016 | tf_op jit(solution)/shard_map/ppermute | solution.py:658
  16.2 11.1 %collective-permute-start.3 = (bf16[528,256]{1,0:T(8,128)(2,1)S(1)}, bf16[528,256]{1,0:T(8,128)(2,1)S(1)}, u32[]{:S(2)}, u32[]{:S(2)}) collective-permute-start(bf16[528,256]{1,0:T(8,128)(2,1)S(1)} %get-tuple-element.41), channel_id=1, source_target_pairs={{4,8},{12,16},{20,24},{8,4},{16,12},{24,20},{5,9},{13,17},{21,25},... | collective-permute-start | bytes 811016 | tf_op jit(solution)/shard_map/ppermute | solution.py:659
  19.6 7.6 %copy-start = (bf16[8,128,256]{2,1,0:T(8,128)(2,1)S(1)}, bf16[8,128,256]{2,1,0:T(8,128)(2,1)}, u32[]{:S(2)}) copy-start(bf16[8,128,256]{2,1,0:T(8,128)(2,1)} %target.2) | copy-start | bytes 1572868
  28.0 7.6 %collective-permute-start.4 = (bf16[43,8,256]{2,1,0:T(8,128)(2,1)S(1)}, bf16[43,8,256]{2,1,0:T(8,128)(2,1)S(1)}, u32[]{:S(2)}, u32[]{:S(2)}) collective-permute-start(bf16[43,8,256]{2,1,0:T(8,128)(2,1)S(1)} %get-tuple-element.43), channel_id=1, source_target_pairs={{0,1},{2,3},{1,0},{3,2},{4,5},{6,7},{5,4},{7,6},{8,9},{10,11},{9,8... | collective-permute-start | bytes 528392 | tf_op jit(solution)/shard_map/ppermute | solution.py:665
  30.2 5.4 %collective-permute-start.5 = (bf16[43,8,256]{2,1,0:T(8,128)(2,1)S(1)}, bf16[43,8,256]{2,1,0:T(8,128)(2,1)S(1)}, u32[]{:S(2)}, u32[]{:S(2)}) collective-permute-start(bf16[43,8,256]{2,1,0:T(8,128)(2,1)S(1)} %get-tuple-element.44), channel_id=1, source_target_pairs={{1,2},{2,1},{5,6},{6,5},{9,10},{10,9},{13,14},{14,13},{17,18},{18,... | collective-permute-start | bytes 528392 | tf_op jit(solution)/shard_map/ppermute | solution.py:666
  35.6 18.7 %copy-start.2 = (bf16[512,512]{1,0:T(8,128)(2,1)S(1)}, bf16[512,512]{1,0:T(8,128)(2,1)}, u32[]{:S(2)}) copy-start(bf16[512,512]{1,0:T(8,128)(2,1)} %constant.34.clone.table.refs_5_) | copy-start | bytes 1572868
  35.6 18.7 %copy-start.7 = (bf16[192,256]{1,0:T(8,128)(2,1)S(1)}, bf16[192,256]{1,0:T(8,128)(2,1)}, u32[]{:S(2)}) copy-start(bf16[192,256]{1,0:T(8,128)(2,1)} %refs_4_.1) | copy-start | bytes 294916
  41.0 34.2 %copy-start.5 = (bf16[384,384]{1,0:T(8,128)(2,1)S(1)}, bf16[384,384]{1,0:T(8,128)(2,1)}, u32[]{:S(2)}) copy-start(bf16[384,384]{1,0:T(8,128)(2,1)} %mix.1) | copy-start | bytes 884740
  41.0 34.2 %copy-start.8 = (bf16[128,128]{1,0:T(8,128)(2,1)S(1)}, bf16[128,128]{1,0:T(8,128)(2,1)}, u32[]{:S(2)}) copy-start(bf16[128,128]{1,0:T(8,128)(2,1)} %constant.36.clone.table) | copy-start | bytes 98308
  41.0 34.2 %copy-start.9 = (bf16[128,128]{1,0:T(8,128)(2,1)S(1)}, bf16[128,128]{1,0:T(8,128)(2,1)}, u32[]{:S(2)}) copy-start(bf16[128,128]{1,0:T(8,128)(2,1)} %constant.35.clone.back_table) | copy-start | bytes 98308
  41.0 6.4 %collective-permute-start.6 = (bf16[2,128,256]{2,1,0:T(8,128)(2,1)S(1)}, bf16[2,128,256]{2,1,0:T(8,128)(2,1)S(1)}, u32[]{:S(2)}, u32[]{:S(2)}) collective-permute-start(bf16[2,128,256]{2,1,0:T(8,128)(2,1)S(1)} %get-tuple-element.54), channel_id=1, source_target_pairs={{0,1},{1,0},{2,3},{3,2},{4,5},{5,4},{6,7},{7,6},{8,9},{9,8},{10,11... | collective-permute-start | bytes 393224 | tf_op jit(solution)/shard_map/ppermute | solution.py:675
  44.0 10.2 %collective-permute-start.7 = (bf16[2,128,256]{2,1,0:T(8,128)(2,1)S(1)}, bf16[2,128,256]{2,1,0:T(8,128)(2,1)S(1)}, u32[]{:S(2)}, u32[]{:S(2)}) collective-permute-start(bf16[2,128,256]{2,1,0:T(8,128)(2,1)S(1)} %get-tuple-element.55), channel_id=1, source_target_pairs={{0,2},{1,3},{2,0},{3,1},{4,6},{5,7},{6,4},{7,5},{8,10},{9,11},{10,... | collective-permute-start | bytes 393224 | tf_op jit(solution)/shard_map/ppermute | solution.py:675
  44.0 10.2 %collective-permute-start.8 = (bf16[2,128,256]{2,1,0:T(8,128)(2,1)S(1)}, bf16[2,128,256]{2,1,0:T(8,128)(2,1)S(1)}, u32[]{:S(2)}, u32[]{:S(2)}) collective-permute-start(bf16[2,128,256]{2,1,0:T(8,128)(2,1)S(1)} %get-tuple-element.56), channel_id=1, source_target_pairs={{0,3},{1,2},{2,1},{3,0},{4,7},{5,6},{6,5},{7,4},{8,11},{9,10},{10,... | collective-permute-start | bytes 393224 | tf_op jit(solution)/shard_map/ppermute | solution.py:675
  75.2 17.7 %copy-start.3 = (bf16[512,192]{0,1:T(8,128)(2,1)S(1)}, bf16[512,192]{0,1:T(8,128)(2,1)}, u32[]{:S(2)}) copy-start(bf16[512,192]{0,1:T(8,128)(2,1)} %param.20) | copy-start | bytes 589828
  75.2 17.7 %copy-start.4 = (bf16[512,512]{1,0:T(8,128)(2,1)S(1)}, bf16[512,512]{1,0:T(8,128)(2,1)}, u32[]{:S(2)}) copy-start(bf16[512,512]{1,0:T(8,128)(2,1)} %constant.33.clone.table) | copy-start | bytes 1572868
  75.2 17.7 %copy-start.6 = (bf16[512,256]{1,0:T(8,128)(2,1)S(1)}, bf16[512,256]{1,0:T(8,128)(2,1)}, u32[]{:S(2)}) copy-start(bf16[512,256]{1,0:T(8,128)(2,1)} %weight_local.1) | copy-start | bytes 786436

commit v15 on v14

--- a/solution.py
+++ b/solution.py
@@ -65,16 +65,11 @@
     return np.block([[cos, sin], [-sin, cos]])
 
 
-def strip_row(signal, r):
-    return jnp.concatenate([signal[block, r] for block in range(signal.shape[0])], axis=0)
-
-
 def grad_kernel(norm, place, *refs):
-    *pieces, weight, table, out, strip_out, projected = refs
+    *pieces, weight, table, out, projected = refs
     tile_cols = pieces[0].shape[1]
     for step, piece in enumerate(pieces):
         block = place[0] ^ step
-        strip_out[block] = piece[...]
         rows = [dot_t(piece[r], weight[...]).astype(jnp.bfloat16) for r in range(piece.shape[0])]
         where = pl.ds(pl.multiple_of(block * tile_cols, tile_cols), tile_cols)
         projected[where, :] = jnp.concatenate(rows, axis=1)
@@ -82,17 +77,13 @@
 
 
 def grad_spectrum(norm, place, pieces, weight, table):
-    strip, tile_cols, channels = pieces[0].shape
-    shape = (table.shape[0], strip * weight.shape[0])
+    shape = (table.shape[0], pieces[0].shape[0] * weight.shape[0])
     in_vmem = pl.BlockSpec(memory_space=pltpu.VMEM)
     return pl.pallas_call(
         functools.partial(grad_kernel, norm),
-        out_shape=[
-            jax.ShapeDtypeStruct(shape, jnp.bfloat16),
-            jax.ShapeDtypeStruct((len(pieces), strip, tile_cols, channels), jnp.bfloat16),
-        ],
+        out_shape=jax.ShapeDtypeStruct(shape, jnp.bfloat16),
         in_specs=[pl.BlockSpec(memory_space=pltpu.SMEM)] + [in_vmem] * (len(pieces) + 2),
-        out_specs=[in_vmem] * 2,
+        out_specs=in_vmem,
         scratch_shapes=[pltpu.VMEM(shape, jnp.bfloat16)],
         compiler_params=pltpu.CompilerParams(vmem_limit_bytes=10 * MIB),
         cost_estimate=pl.CostEstimate(flops=0, bytes_accessed=2 * MIB, transcendentals=0),
@@ -186,20 +177,37 @@
         out[:, g * LANES : (g + 1) * LANES] = wide[g].astype(jnp.bfloat16)
 
 
-def output_kernel(norm, moved, strip_grad, weight_in, weight_local, table, out):
-    spatial = (dot(table[...], moved[...]) * norm).astype(jnp.bfloat16)
-    half = weight_in.shape[0]
-    for r in range(out.shape[0]):
-        total = dot(spatial[:, r * half : (r + 1) * half], weight_in[...])
-        total = total + dot_t(strip_row(strip_grad, r), weight_local[...])
-        out[r] = total.astype(jnp.bfloat16)
+def output_kernel(norm, place, moved, weight_in, weight_local, table, *refs):
+    *pieces, out, spatial = refs
+    spatial[...] = (dot(table[...], moved[...]) * norm).astype(jnp.bfloat16)
+    half, tile_cols = weight_in.shape[0], pieces[0].shape[1]
+    for step, piece in enumerate(pieces):
+        start = pl.multiple_of((place[0] ^ step) * tile_cols, tile_cols)
+        part = spatial[pl.ds(start, tile_cols), :]
+        for r in range(out.shape[0]):
+            total = dot(part[:, r * half : (r + 1) * half], weight_in[...])
+            total = total + dot_t(piece[r], weight_local[...])
+            out[r, pl.ds(start, tile_cols), :] = total.astype(jnp.bfloat16)
+
+
+def output(norm, place, moved, weight_in, weight_local, table, pieces, shape):
+    in_vmem = pl.BlockSpec(memory_space=pltpu.VMEM)
+    return pl.pallas_call(
+        functools.partial(output_kernel, norm),
+        out_shape=jax.ShapeDtypeStruct(shape, jnp.bfloat16),
+        in_specs=[pl.BlockSpec(memory_space=pltpu.SMEM)] + [in_vmem] * (len(pieces) + 4),
+        out_specs=in_vmem,
+        scratch_shapes=[pltpu.VMEM(moved.shape, jnp.bfloat16)],
+        compiler_params=pltpu.CompilerParams(vmem_limit_bytes=10 * MIB),
+        cost_estimate=pl.CostEstimate(flops=0, bytes_accessed=3 * MIB, transcendentals=0),
+    )(place, moved, weight_in, weight_local, table, *pieces)
 
 
 TAIL = 16
 
 
 def pick(flag, left, right):
-    return lax.select(flag, left.astype(jnp.float32), right.astype(jnp.float32))
+    return lax.select(flag, left, right)
 
 
 def odd_row(place):
@@ -221,18 +229,14 @@
     return jnp.concatenate([lanes, fill], axis=1).astype(jnp.bfloat16)
 
 
-def prepare_kernel(
-    place, target, mask, first, second, early, late, mask_row, first_out, second_out, mask_held, sems
-):
+def pack_kernel(place, target, mask, early, late, mask_row, mask_held, sems):
     tile_rows, tile_cols = mask.shape
-    channels = target.shape[2]
+    channels = target.shape[1]
+    last = tile_rows - NEAR
+    pixels = NEAR * tile_cols
     moves = [(mask, mask_held)]
-    last = tile_rows - NEAR
-    for pack, start in ((early, (1 - place[1]) * last), (late, place[1] * last)):
-        moves += [
-            (target.at[start + i], pack.at[pl.ds(i * tile_cols, tile_cols)]) for i in range(NEAR)
-        ]
-    moves += [(first, first_out), (second, second_out)]
+    for pack, row in ((early, (1 - place[1]) * last), (late, place[1] * last)):
+        moves.append((target.at[pl.ds(row * tile_cols, pixels)], pack.at[pl.ds(0, pixels)]))
     copies = [pltpu.make_async_copy(*move, sems.at[i]) for i, move in enumerate(moves)]
     for copy in copies:
         copy.start()
@@ -240,26 +244,49 @@
     mask_row[0] = filled(turned(mask_held[...]), channels)
     ends = (mask_held[:NEAR], mask_held[last:])
     for pack, (one, other) in ((early, ends), (late, ends[::-1])):
-        rows = pick(odd_row(place), one, other)
+        rows = pick(odd_row(place), one.astype(jnp.float32), other.astype(jnp.float32))
         rows = jnp.concatenate([rows, jnp.zeros((TAIL - NEAR, tile_cols), jnp.float32)], axis=0)
-        pack[NEAR * tile_cols :] = filled(rows, channels)
+        pack[pixels:] = filled(rows, channels)
     for copy in copies[1:]:
         copy.wait()
 
 
-def prepare(place, target, mask, first, second):
-    _, tile_cols, channels = target.shape
+def target_packs(place, target, mask):
+    tile_rows, tile_cols, channels = target.shape
     pack = (NEAR * tile_cols + TAIL, channels)
-    shapes = [pack, pack, (1, tile_cols, channels), first.shape, second.shape]
-    return pl.pallas_call(
-        prepare_kernel,
+    hbm = pl.BlockSpec(memory_space=pltpu.HBM)
+    shapes = [pack, pack, (1, tile_cols, channels)]
+    return pl.pallas_call(
+        pack_kernel,
         out_shape=[jax.ShapeDtypeStruct(shape, jnp.bfloat16) for shape in shapes],
-        in_specs=[pl.BlockSpec(memory_space=pltpu.SMEM)] + [pl.BlockSpec(memory_space=pltpu.HBM)] * 4,
+        in_specs=[pl.BlockSpec(memory_space=pltpu.SMEM), hbm, hbm],
         out_specs=[pl.BlockSpec(memory_space=pltpu.VMEM)] * len(shapes),
-        scratch_shapes=[pltpu.VMEM(mask.shape, mask.dtype), pltpu.SemaphoreType.DMA((2 * NEAR + 3,))],
-        compiler_params=pltpu.CompilerParams(vmem_limit_bytes=6 * MIB),
-        cost_estimate=pl.CostEstimate(flops=0, bytes_accessed=2 * MIB, transcendentals=0),
-    )(place, *[in_hbm(a) for a in (target, mask, first, second)])
+        scratch_shapes=[pltpu.VMEM(mask.shape, mask.dtype), pltpu.SemaphoreType.DMA((3,))],
+        compiler_params=pltpu.CompilerParams(vmem_limit_bytes=4 * MIB),
+        cost_estimate=pl.CostEstimate(flops=0, bytes_accessed=MIB, transcendentals=0),
+    )(place, in_hbm(target.reshape(tile_rows * tile_cols, channels)), in_hbm(mask))
+
+
+def fetch_kernel(*refs):
+    count = len(refs) // 2
+    sems = refs[-1]
+    copies = [pltpu.make_async_copy(refs[i], refs[count + i], sems.at[i]) for i in range(count)]
+    for copy in copies:
+        copy.start()
+    for copy in copies:
+        copy.wait()
+
+
+def fetch(*arrays):
+    return pl.pallas_call(
+        fetch_kernel,
+        out_shape=[jax.ShapeDtypeStruct(a.shape, a.dtype) for a in arrays],
+        in_specs=[pl.BlockSpec(memory_space=pltpu.HBM)] * len(arrays),
+        out_specs=[pl.BlockSpec(memory_space=pltpu.VMEM)] * len(arrays),
+        scratch_shapes=[pltpu.SemaphoreType.DMA((len(arrays),))],
+        compiler_params=pltpu.CompilerParams(vmem_limit_bytes=4 * MIB),
+        cost_estimate=pl.CostEstimate(flops=0, bytes_accessed=5 * MIB, transcendentals=0),
+    )(*[in_hbm(a) for a in arrays])
 
 
 def edge_kernel(tile_cols, place, early_pack, late_pack, *refs):
@@ -272,10 +299,10 @@
     def put_rows(row, tail, head):
         rows = slice(row, row + tail.shape[0])
         last, initial = tail[:, REACH:], head[:, :REACH]
-        early[rows] = pick(high, initial, last).astype(jnp.bfloat16)
-        late[rows] = pick(high, last, initial).astype(jnp.bfloat16)
-        own[rows, :keep] = head.astype(jnp.bfloat16)
-        own[rows, keep:] = tail.astype(jnp.bfloat16)
+        early[rows] = pick(high, initial, last)
+        late[rows] = pick(high, last, initial)
+        own[rows, :keep] = head
+        own[rows, keep:] = tail
 
     def put_pack(row, one, other):
         for i in range(NEAR):
@@ -419,7 +446,7 @@
         sources, at = find(row)
         if len(sources) == 1:
             return features[at].astype(jnp.float32)
-        return pick(odd_row(place), *[source[at] for source in sources])
+        return pick(odd_row(place), *[source[at] for source in sources]).astype(jnp.float32)
 
     def inside(row):
         return ok[REACH : REACH + stride, row : row + 1]
@@ -452,7 +479,7 @@
     find = part_of(rows, NEAR, packs, (target,), packs[::-1])
 
     def picked(sources, part):
-        return pick(odd_row(place), *[source[part] for source in sources])
+        return pick(odd_row(place), *[source[part] for source in sources]).astype(jnp.float32)
 
     def goal(row):
         sources, at = find(row)
@@ -493,7 +520,8 @@
 
     def feature(row):
         before, after = pick(odd, early[row], late[row]), pick(odd, late[row], early[row])
-        return jnp.concatenate([before, own[row].astype(jnp.float32), after], axis=0)
+        parts = [part.astype(jnp.float32) for part in (before, own[row], after)]
+        return jnp.concatenate(parts, axis=0)
 
     find = part_of(rows, NEAR, tall, tall + NEAR + 1, tall + NEAR + 1 + rows + 1)
 
@@ -642,7 +670,8 @@
     ok = ((col_ids >= 0) & (col_ids < width))[:, None] & ((row_ids >= 0) & (row_ids < height))[None]
     ok = ok.astype(jnp.float32)
     place = jnp.stack([lax.axis_index("col"), lax.axis_index("row") & 1]).astype(jnp.int32)
-    inputs, ok, place = lax.optimization_barrier((inputs, ok, place))
+    early_pack, late_pack, mask_row = target_packs(place, target, hole_mask)
+    inputs, ok, early_pack = lax.optimization_barrier((inputs, ok, early_pack))
 
     cells = [jax.ShapeDtypeStruct((width, strip * half), bf16)]
     weight_in = weight_in.T
@@ -651,10 +680,8 @@
 
     early = lax.ppermute(features, "row", pairs("row", 0))
     late = lax.ppermute(features, "row", pairs("row", 1))
-    target_after, spatial_cols = lax.optimization_barrier((target, spatial_cols))
-    early_pack, late_pack, mask_row, kernel_first, kernel_second = prepare(
-        place, target_after, hole_mask, kernel_first, kernel_second
-    )
+    kernel_first, spatial_cols = lax.optimization_barrier((kernel_first, spatial_cols))
+    kernel_first, kernel_second = fetch(kernel_first, kernel_second)
     early_pack = lax.ppermute(early_pack, "row", pairs("row", 0))
     late_pack = lax.ppermute(late_pack, "row", pairs("row", 1))
     pre, slopes = tile_forward(place, early, features, late, kernel_first, kernel_second, ok)
@@ -668,12 +695,11 @@
         place, pre, slopes, early_pack, target, late_pack, mask_row, kernel_first, kernel_second, ok
     )
     pieces = sides(place, tile, early_edge, late_edge, own, kernel_first, kernel_second, ok)
-    pieces, spatial_moved = lax.optimization_barrier((pieces, spatial_moved))
-    moved = [pieces[0]]
-    for step in range(1, col_devices):
+    (*pieces, spatial_moved) = lax.optimization_barrier((*pieces, spatial_moved))
+    for step in reversed(range(1, col_devices)):
         swaps = [(i, i ^ step) for i in range(col_devices)]
-        moved.append(lax.ppermute(pieces[step], "col", swaps))
-    grad_cols, strip_grad = grad_spectrum(col_norm, place, moved, weight_out, table)
+        pieces[step] = lax.ppermute(pieces[step], "col", swaps)
+    grad_cols = grad_spectrum(col_norm, place, pieces, weight_out, table)
     wide = pltpu.VMEM((strip * half // LANES, width, LANES), jnp.float32)
     grad_rows = vmem_call(
         functools.partial(mix_kernel, row_norm, owned, devices),
@@ -686,15 +712,9 @@
         scratch=[wide, wide],
     )[0]
     returned = swap(grad_rows)
-    return vmem_call(
-        functools.partial(output_kernel, col_norm),
-        [jax.ShapeDtypeStruct(inputs.shape, bf16)],
-        returned,
-        strip_grad,
-        weight_in,
-        weight_local,
-        table_back,
-    )[0]
+    return output(
+        col_norm, place, returned, weight_in, weight_local, table_back, pieces, inputs.shape
+    )
 
 
 def solution(mesh):

time: 96.1 us -> 97.1 us (1.010)
  waiting for transfers between devices: 9.19 us -> 6.73 us
  blocking collectives: 35 us -> 37.1 us
  Pallas kernels: 28.4 us -> 30.1 us
    pallas_call x2 -> x4, Pallas kernels: 3.99 us -> 7.75 us  [the longest x1 3 us: output(): pl.pallas_call(functools.partial(output_kernel, norm), out_shape=jax.Shap...]
    all_to_all x2, blocking collectives: 35 us -> 37.1 us  [swap(): lax.all_to_all(spectrum, ('col', 'row'), split_axis=0, concat_axis=0, til...]
    pallas_call x2 -> x1, Pallas kernels: 4.01 us -> 2.05 us  [vmem_call(): pl.pallas_call(body, out_shape=shapes, in_specs=[spec] * len(operands), o...]
    ppermute x3, waiting for transfers between devices: 8.09 us -> 6.71 us  [shards(): pieces[step] = lax.ppermute(pieces[step], 'col', swaps)]
    ppermute x1, waiting for transfers between devices: 1.08 us -> 0.01 us  [shards(): late_pack = lax.ppermute(late_pack, 'row', pairs('row', 1))]
  transfers between devices with their start and end apart: 10 -> 10, of which waited for: 3 -> 3; matrix products, arithmetic and copies ran while one was open for 0% -> 0% of each run, Pallas kernels for 24% -> 25%
where the time goes in v15:
time: 97.1 us; the launch traced here: 95.8 us
  blocking collectives  37.1 us (38%)
  Pallas kernels  30.1 us (31%)
  starting transfers between devices  21.4 us (22%)
  waiting for transfers between devices  6.73 us (7%)
    all_to_all x2, blocking collectives, swap(): lax.all_to_all(spectrum, ('col', 'row'), split_axis=0, concat_axis=0, til...  37.1 us
    ppermute x3, waiting for transfers between devices, shards(): pieces[step] = lax.ppermute(pieces[step], 'col', swaps)  6.71 us
    pallas_call x1, Pallas kernels, tile_forward(): pl.pallas_call(tile_forward_kernel, out_shape=shapes, in_specs=[pl.BlockS...  6.49 us
    ppermute x3, starting transfers between devices, shards(): pieces[step] = lax.ppermute(pieces[step], 'col', swaps)  5.85 us
    pallas_call x1, Pallas kernels, sides(): pl.pallas_call(side_kernel, out_shape=[piece] * count, in_specs=[pl.Block...  5.36 us
    all_to_all x1, starting transfers between devices, swap(): lax.all_to_all(spectrum, ('col', 'row'), split_axis=0, concat_axis=0, til...  5.13 us
    ppermute x1, starting transfers between devices, shards(): late = lax.ppermute(features, 'row', pairs('row', 1))  4.5 us
    pallas_call x1, Pallas kernels, tile_backward(): pl.pallas_call(tile_backward_kernel, out_shape=jax.ShapeDtypeStruct(targe...  4.49 us
  transfers between devices with their start and end apart: 10, of which 3 were waited for; matrix products, arithmetic and copies ran while one was open for 0% of the time, Pallas kernels for 25%

profile of v15, /device:TPU:1, one launch (start us, length us, event | category | flops | bytes accessed | tf_op | source)
XLA Modules:
  0.0 95.8 jit_solution(18370546312961173292)
XLA Ops:
  0.0 4.5 %collective-permute-start.2 = (bf16[8,128,256]{2,1,0:T(8,128)(2,1)}, bf16[8,128,256]{2,1,0:T(8,128)(2,1)S(1)}, u32[]{:S(2)}, u32[]{:S(2)}) collective-permute-start(bf16[8,128,256]{2,1,0:T(8,128)(2,1)} %refs_7_.1), channel_id=1, source_target_pairs={{4,8},{12,16},{20,24},{8,4},{16,12},{24,20},{5,9},{13,17},{21,25},... | collective-permute-start | bytes 1572872 | tf_op jit(solution)/shard_map/ppermute | solution.py:682
  4.5 0.1 collective-permute-start.1
  4.6 0.1 pad_add_fusion.place
  4.7 1.6 %shard_map.136 = (bf16[528,256]{1,0:T(8,128)(2,1)S(1)}, bf16[528,256]{1,0:T(8,128)(2,1)S(1)}, bf16[1,128,256]{2,1,0:T(8,128)(2,1)S(1)}) custom-call(s32[2]{0:T(128)S(1)} %pad_add_fusion.place, bf16[1024,256]{1,0:T(8,128)(2,1)} %bitcast.10, s32[8,128]{1,0:T(8,128)} %mask.1), custom_call_target="tpu_custom_call" | custom-call | bytes 1048576 | tf_op jit(solution)/shard_map/pallas_call | solution.py:259
  6.3 0.1 and_convert_fusion.ok
  6.4 0.6 collective-permute-start
  7.0 3.0 %collective-permute-start.3 = (bf16[528,256]{1,0:T(8,128)(2,1)S(1)}, bf16[528,256]{1,0:T(8,128)(2,1)S(1)}, u32[]{:S(2)}, u32[]{:S(2)}) collective-permute-start(bf16[528,256]{1,0:T(8,128)(2,1)S(1)} %get-tuple-element.39), channel_id=1, source_target_pairs={{4,8},{12,16},{20,24},{8,4},{16,12},{24,20},{5,9},{13,17},{21,25},... | collective-permute-start | bytes 811016 | tf_op jit(solution)/shard_map/ppermute | solution.py:686
  10.0 3.3 %shard_map.137 = bf16[512,384]{1,0:T(8,128)(2,1)} custom-call(bf16[2,512,512]{2,1,0:T(8,128)(2,1)} %signal, bf16[192,512]{1,0:T(8,128)(2,1)} %bitcast.16, bf16[512,512]{1,0:T(8,128)(2,1)} %constant.34.clone.table.refs_5_), custom_call_target="tpu_custom_call" | custom-call | bytes 2097152 | tf_op jit(solution)/shard_map/pallas_call | solution.py:113
  13.3 5.1 %all-to-all-start = ((bf16[32,16,384]{2,1,0:T(8,128)(2,1)}), bf16[32,16,384]{2,1,0:T(8,128)(2,1)S(1)}, u32[]{:S(2)}, u32[]{:S(2)}) async-start(bf16[32,16,384]{2,1,0:T(8,128)(2,1)} %bitcast.4), calls=%async_computation | async-start | bytes 786432 | tf_op jit(solution)/shard_map/all_to_all | solution.py:665
  18.4 0.0 copy-start.1
  18.5 1.7 %shard_map.138 = (bf16[3,3,256,256]{3,2,1,0:T(8,128)(2,1)S(1)}, bf16[3,3,256,256]{3,2,1,0:T(8,128)(2,1)S(1)}) custom-call(bf16[3,3,256,256]{3,2,1,0:T(8,128)(2,1)} %refs_0_, bf16[3,3,256,256]{3,2,1,0:T(8,128)(2,1)} %refs_1_.1), custom_call_target="tpu_custom_call" | custom-call | bytes 5242880 | tf_op jit(solution)/shard_map/pallas_call | solution.py:281
  20.2 0.0 copy-done.1
  20.2 6.5 %shard_map.139 = (f32[2048,256]{1,0:T(8,128)S(1)}, f32[1536,256]{1,0:T(8,128)S(1)}) custom-call(s32[2]{0:T(128)S(1)} %pad_add_fusion.place, bf16[8,128,256]{2,1,0:T(8,128)(2,1)S(1)} %collective-permute-done.1.early.refs_0_.refs_5_, bf16[8,128,256]{2,1,0:T(8,128)(2,1)S(1)} %copy-done.1, bf16[8,128,256]{2,1,0:T(8,128)(2,1)S(1)} %collective-permute-done.2.late.refs_1_.refs_6_, ...), custom_call_target="tpu_custom_call" | custom-call | flops 5435817984 | bytes 8388608 | tf_op jit(solution)/shard_map/pallas_call | solution.py:573
  26.7 0.7 shard_map.140
  27.4 1.4 %collective-permute-start.4 = (bf16[43,8,256]{2,1,0:T(8,128)(2,1)S(1)}, bf16[43,8,256]{2,1,0:T(8,128)(2,1)S(1)}, u32[]{:S(2)}, u32[]{:S(2)}) collective-permute-start(bf16[43,8,256]{2,1,0:T(8,128)(2,1)S(1)} %get-tuple-element.41), channel_id=1, source_target_pairs={{0,1},{2,3},{1,0},{3,2},{4,5},{6,7},{5,4},{7,6},{8,9},{10,11},{9,8... | collective-permute-start | bytes 528392 | tf_op jit(solution)/shard_map/ppermute | solution.py:692
  28.9 0.8 collective-permute-start.5
  29.7 4.5 %shard_map.141.tile = bf16[8,128,256]{2,1,0:T(8,128)(2,1)S(1)} custom-call(s32[2]{0:T(128)S(1)} %pad_add_fusion.place, f32[2048,256]{1,0:T(8,128)S(1)} %get-tuple-element.44.pre, f32[1536,256]{1,0:T(8,128)S(1)} %get-tuple-element.45.slopes, bf16[528,256]{1,0:T(8,128)(2,1)S(1)} %collective-permute-done.early_pack, bf16[8,128,256]{2,1,0:T(8,128)(2,1)S(1)} %copy-done, ...), custom_call_target="tpu_custom_call" | custom-call | flops 3019898880 | bytes 8388608 | tf_op jit(solution)/shard_map/pallas_call | solution.py:591
  34.2 0.0 copy-start.2
  34.2 5.4 %shard_map.142 = (bf16[2,128,256]{2,1,0:T(8,128)(2,1)S(1)}, bf16[2,128,256]{2,1,0:T(8,128)(2,1)S(1)}, bf16[2,128,256]{2,1,0:T(8,128)(2,1)S(1)}, bf16[2,128,256]{2,1,0:T(8,128)(2,1)S(1)}) custom-call(s32[2]{0:T(128)S(1)} %pad_add_fusion.place, bf16[43,8,256]{2,1,0:T(8,128)(2,1)S(1)} %collective-permute-done.4.early, ...), custom_call_target="tpu_custom_call" | custom-call | flops 3170893824 | bytes 4194304 | tf_op jit(solution)/shard_map/pallas_call | solution.py:612
  39.6 0.0 copy-start.8
  39.6 0.0 copy-start.9
  39.7 3.7 %collective-permute-start.6 = (bf16[2,128,256]{2,1,0:T(8,128)(2,1)S(1)}, bf16[2,128,256]{2,1,0:T(8,128)(2,1)S(1)}, u32[]{:S(2)}, u32[]{:S(2)}) collective-permute-start(bf16[2,128,256]{2,1,0:T(8,128)(2,1)S(1)} %get-tuple-element.52), channel_id=1, source_target_pairs={{0,1},{1,0},{2,3},{3,2},{4,5},{5,4},{6,7},{7,6},{8,9},{9,8},{10,11... | collective-permute-start | bytes 393224 | tf_op jit(solution)/shard_map/ppermute | solution.py:701
  43.4 0.4 collective-permute-start.7
  43.8 1.7 %collective-permute-start.8 = (bf16[2,128,256]{2,1,0:T(8,128)(2,1)S(1)}, bf16[2,128,256]{2,1,0:T(8,128)(2,1)S(1)}, u32[]{:S(2)}, u32[]{:S(2)}) collective-permute-start(bf16[2,128,256]{2,1,0:T(8,128)(2,1)S(1)} %get-tuple-element.54), channel_id=1, source_target_pairs={{0,3},{1,2},{2,1},{3,0},{4,7},{5,6},{6,5},{7,4},{8,11},{9,10},{10,... | collective-permute-start | bytes 393224 | tf_op jit(solution)/shard_map/ppermute | solution.py:701
  45.5 0.8 collective-permute-done.6.refs_1_
  46.3 4.6 %collective-permute-done.7.refs_2_ = bf16[2,128,256]{2,1,0:T(8,128)(2,1)S(1)} collective-permute-done((bf16[2,128,256]{2,1,0:T(8,128)(2,1)S(1)}, bf16[2,128,256]{2,1,0:T(8,128)(2,1)S(1)}, u32[]{:S(2)}, u32[]{:S(2)}) %collective-permute-start.7) | collective-permute-done | bytes 131104 | tf_op jit(solution)/shard_map/ppermute | solution.py:701
  50.9 1.3 %collective-permute-done.8.refs_3_ = bf16[2,128,256]{2,1,0:T(8,128)(2,1)S(1)} collective-permute-done((bf16[2,128,256]{2,1,0:T(8,128)(2,1)S(1)}, bf16[2,128,256]{2,1,0:T(8,128)(2,1)S(1)}, u32[]{:S(2)}, u32[]{:S(2)}) %collective-permute-start.8) | collective-permute-done | bytes 131104 | tf_op jit(solution)/shard_map/ppermute | solution.py:701
  52.2 1.4 %shard_map.143 = bf16[512,384]{1,0:T(8,128)(2,1)S(1)} custom-call(s32[2]{0:T(128)S(1)} %pad_add_fusion.place, bf16[2,128,256]{2,1,0:T(8,128)(2,1)S(1)} %get-tuple-element.51.refs_0_, bf16[2,128,256]{2,1,0:T(8,128)(2,1)S(1)} %collective-permute-done.6.refs_1_, bf16[2,128,256]{2,1,0:T(8,128)(2,1)S(1)} %collective-permute-done.7.refs_2_, ...), custom_call_target="tpu_custom_call" | custom-call | bytes 2097152 | tf_op jit(solution)/shard_map/pallas_call | solution.py:82
  53.7 21.4 %all_to_all.34 = bf16[32,16,384]{2,1,0:T(8,128)(2,1)S(1)} all-to-all(bf16[32,16,384]{2,1,0:T(8,128)(2,1)S(1)} %bitcast.15), channel_id=1, replica_groups=mesh['row'=8,'col'=4] {'col','row'}, dimensions={0} | all-to-all | bytes 786432 | tf_op jit(solution)/shard_map/all_to_all | solution.py:665
  75.2 2.1 %shard_map.144 = bf16[512,384]{1,0:T(8,128)(2,1)S(1)} custom-call(bf16[512,384]{1,0:T(8,128)(2,1)S(1)} %bitcast.12, bf16[512,384]{1,0:T(8,128)(2,1)S(1)} %bitcast.13, bf16[384,384]{1,0:T(8,128)(2,1)S(1)} %copy-done.5, bf16[128,128]{1,0:T(8,128)(2,1)S(1)} %copy-done.8, bf16[128,128]{1,0:T(8,128)(2,1)S(1)} %copy-done.9), custom_call_target="tpu_custom_call" | custom-call | bytes 1540096 | tf_op jit(solution)/shard_map/pallas_call | solution.py:30
  77.2 15.6 %all_to_all.35 = bf16[32,16,384]{2,1,0:T(8,128)(2,1)S(1)} all-to-all(bf16[32,16,384]{2,1,0:T(8,128)(2,1)S(1)} %bitcast.14), channel_id=1, replica_groups=mesh['row'=8,'col'=4] {'col','row'}, dimensions={0} | all-to-all | bytes 786432 | tf_op jit(solution)/shard_map/all_to_all | solution.py:665
  92.8 3.0 %shard_map.145 = bf16[2,512,512]{2,1,0:T(8,128)(2,1)} custom-call(s32[2]{0:T(128)S(1)} %pad_add_fusion.place, bf16[512,384]{1,0:T(8,128)(2,1)S(1)} %bitcast.11, bf16[192,512]{1,0:T(8,128)(2,1)S(1)} %bitcast.17, bf16[512,256]{1,0:T(8,128)(2,1)S(1)} %copy-done.6, bf16[512,512]{1,0:T(8,128)(2,1)S(1)} %copy-done.4, ...), custom_call_target="tpu_custom_call" | custom-call | bytes 3145728 | tf_op jit(solution)/shard_map/pallas_call | solution.py:195
  (24 shorter events, 0.1 us)
Async XLA Ops:
  0.0 20.2 %collective-permute-start.2 = (bf16[8,128,256]{2,1,0:T(8,128)(2,1)}, bf16[8,128,256]{2,1,0:T(8,128)(2,1)S(1)}, u32[]{:S(2)}, u32[]{:S(2)}) collective-permute-start(bf16[8,128,256]{2,1,0:T(8,128)(2,1)} %refs_7_.1), channel_id=1, source_target_pairs={{4,8},{12,16},{20,24},{8,4},{16,12},{24,20},{5,9},{13,17},{21,25},... | collective-permute-start | bytes 1572872 | tf_op jit(solution)/shard_map/ppermute | solution.py:682
  4.5 15.7 %collective-permute-start.1 = (bf16[8,128,256]{2,1,0:T(8,128)(2,1)}, bf16[8,128,256]{2,1,0:T(8,128)(2,1)S(1)}, u32[]{:S(2)}, u32[]{:S(2)}) collective-permute-start(bf16[8,128,256]{2,1,0:T(8,128)(2,1)} %refs_7_.1), channel_id=1, source_target_pairs={{0,4},{8,12},{16,20},{24,28},{4,0},{12,8},{20,16},{28,24},{1,5},{9... | collective-permute-start | bytes 1572872 | tf_op jit(solution)/shard_map/ppermute | solution.py:681
  6.4 20.3 %collective-permute-start = (bf16[528,256]{1,0:T(8,128)(2,1)S(1)}, bf16[528,256]{1,0:T(8,128)(2,1)S(1)}, u32[]{:S(2)}, u32[]{:S(2)}) collective-permute-start(bf16[528,256]{1,0:T(8,128)(2,1)S(1)} %get-tuple-element.31), channel_id=1, source_target_pairs={{0,4},{8,12},{16,20},{24,28},{4,0},{12,8},{20,16},{28,24},{1,5},{9... | collective-permute-start | bytes 811016 | tf_op jit(solution)/shard_map/ppermute | solution.py:685
  7.0 19.7 %collective-permute-start.3 = (bf16[528,256]{1,0:T(8,128)(2,1)S(1)}, bf16[528,256]{1,0:T(8,128)(2,1)S(1)}, u32[]{:S(2)}, u32[]{:S(2)}) collective-permute-start(bf16[528,256]{1,0:T(8,128)(2,1)S(1)} %get-tuple-element.39), channel_id=1, source_target_pairs={{4,8},{12,16},{20,24},{8,4},{16,12},{24,20},{5,9},{13,17},{21,25},... | collective-permute-start | bytes 811016 | tf_op jit(solution)/shard_map/ppermute | solution.py:686
  13.3 26.4 %all-to-all-start = ((bf16[32,16,384]{2,1,0:T(8,128)(2,1)}), bf16[32,16,384]{2,1,0:T(8,128)(2,1)S(1)}, u32[]{:S(2)}, u32[]{:S(2)}) async-start(bf16[32,16,384]{2,1,0:T(8,128)(2,1)} %bitcast.4), calls=%async_computation | async-start | bytes 786432 | tf_op jit(solution)/shard_map/all_to_all | solution.py:665
  18.4 1.8 %copy-start.1 = (bf16[8,128,256]{2,1,0:T(8,128)(2,1)S(1)}, bf16[8,128,256]{2,1,0:T(8,128)(2,1)}, u32[]{:S(2)}) copy-start(bf16[8,128,256]{2,1,0:T(8,128)(2,1)} %refs_7_.1) | copy-start | bytes 1572868
  20.2 6.5 %copy-start = (bf16[8,128,256]{2,1,0:T(8,128)(2,1)S(1)}, bf16[8,128,256]{2,1,0:T(8,128)(2,1)}, u32[]{:S(2)}) copy-start(bf16[8,128,256]{2,1,0:T(8,128)(2,1)} %target.1) | copy-start | bytes 1572868
  27.4 6.8 %collective-permute-start.4 = (bf16[43,8,256]{2,1,0:T(8,128)(2,1)S(1)}, bf16[43,8,256]{2,1,0:T(8,128)(2,1)S(1)}, u32[]{:S(2)}, u32[]{:S(2)}) collective-permute-start(bf16[43,8,256]{2,1,0:T(8,128)(2,1)S(1)} %get-tuple-element.41), channel_id=1, source_target_pairs={{0,1},{2,3},{1,0},{3,2},{4,5},{6,7},{5,4},{7,6},{8,9},{10,11},{9,8... | collective-permute-start | bytes 528392 | tf_op jit(solution)/shard_map/ppermute | solution.py:692
  28.9 5.4 %collective-permute-start.5 = (bf16[43,8,256]{2,1,0:T(8,128)(2,1)S(1)}, bf16[43,8,256]{2,1,0:T(8,128)(2,1)S(1)}, u32[]{:S(2)}, u32[]{:S(2)}) collective-permute-start(bf16[43,8,256]{2,1,0:T(8,128)(2,1)S(1)} %get-tuple-element.42), channel_id=1, source_target_pairs={{1,2},{2,1},{5,6},{6,5},{9,10},{10,9},{13,14},{14,13},{17,18},{18,... | collective-permute-start | bytes 528392 | tf_op jit(solution)/shard_map/ppermute | solution.py:693
  34.2 18.0 %copy-start.2 = (bf16[512,512]{1,0:T(8,128)(2,1)S(1)}, bf16[512,512]{1,0:T(8,128)(2,1)}, u32[]{:S(2)}) copy-start(bf16[512,512]{1,0:T(8,128)(2,1)} %constant.34.clone.table.refs_5_) | copy-start | bytes 1572868
  34.2 18.0 %copy-start.7 = (bf16[192,256]{1,0:T(8,128)(2,1)S(1)}, bf16[192,256]{1,0:T(8,128)(2,1)}, u32[]{:S(2)}) copy-start(bf16[192,256]{1,0:T(8,128)(2,1)} %refs_4_.1) | copy-start | bytes 294916
  39.6 35.5 %copy-start.5 = (bf16[384,384]{1,0:T(8,128)(2,1)S(1)}, bf16[384,384]{1,0:T(8,128)(2,1)}, u32[]{:S(2)}) copy-start(bf16[384,384]{1,0:T(8,128)(2,1)} %mix.1) | copy-start | bytes 884740
  39.6 35.5 %copy-start.8 = (bf16[128,128]{1,0:T(8,128)(2,1)S(1)}, bf16[128,128]{1,0:T(8,128)(2,1)}, u32[]{:S(2)}) copy-start(bf16[128,128]{1,0:T(8,128)(2,1)} %constant.36.clone.table) | copy-start | bytes 98308
  39.6 35.5 %copy-start.9 = (bf16[128,128]{1,0:T(8,128)(2,1)S(1)}, bf16[128,128]{1,0:T(8,128)(2,1)}, u32[]{:S(2)}) copy-start(bf16[128,128]{1,0:T(8,128)(2,1)} %constant.35.clone.back_table) | copy-start | bytes 98308
  39.7 6.6 %collective-permute-start.6 = (bf16[2,128,256]{2,1,0:T(8,128)(2,1)S(1)}, bf16[2,128,256]{2,1,0:T(8,128)(2,1)S(1)}, u32[]{:S(2)}, u32[]{:S(2)}) collective-permute-start(bf16[2,128,256]{2,1,0:T(8,128)(2,1)S(1)} %get-tuple-element.52), channel_id=1, source_target_pairs={{0,1},{1,0},{2,3},{3,2},{4,5},{5,4},{6,7},{7,6},{8,9},{9,8},{10,11... | collective-permute-start | bytes 393224 | tf_op jit(solution)/shard_map/ppermute | solution.py:701
  43.4 7.5 %collective-permute-start.7 = (bf16[2,128,256]{2,1,0:T(8,128)(2,1)S(1)}, bf16[2,128,256]{2,1,0:T(8,128)(2,1)S(1)}, u32[]{:S(2)}, u32[]{:S(2)}) collective-permute-start(bf16[2,128,256]{2,1,0:T(8,128)(2,1)S(1)} %get-tuple-element.53), channel_id=1, source_target_pairs={{0,2},{1,3},{2,0},{3,1},{4,6},{5,7},{6,4},{7,5},{8,10},{9,11},{10,... | collective-permute-start | bytes 393224 | tf_op jit(solution)/shard_map/ppermute | solution.py:701
  43.8 8.4 %collective-permute-start.8 = (bf16[2,128,256]{2,1,0:T(8,128)(2,1)S(1)}, bf16[2,128,256]{2,1,0:T(8,128)(2,1)S(1)}, u32[]{:S(2)}, u32[]{:S(2)}) collective-permute-start(bf16[2,128,256]{2,1,0:T(8,128)(2,1)S(1)} %get-tuple-element.54), channel_id=1, source_target_pairs={{0,3},{1,2},{2,1},{3,0},{4,7},{5,6},{6,5},{7,4},{8,11},{9,10},{10,... | collective-permute-start | bytes 393224 | tf_op jit(solution)/shard_map/ppermute | solution.py:701
  75.1 17.7 %copy-start.3 = (bf16[512,192]{0,1:T(8,128)(2,1)S(1)}, bf16[512,192]{0,1:T(8,128)(2,1)}, u32[]{:S(2)}) copy-start(bf16[512,192]{0,1:T(8,128)(2,1)} %param.20) | copy-start | bytes 589828
  75.1 17.7 %copy-start.4 = (bf16[512,512]{1,0:T(8,128)(2,1)S(1)}, bf16[512,512]{1,0:T(8,128)(2,1)}, u32[]{:S(2)}) copy-start(bf16[512,512]{1,0:T(8,128)(2,1)} %constant.33.clone.table) | copy-start | bytes 1572868
  75.1 17.7 %copy-start.6 = (bf16[512,256]{1,0:T(8,128)(2,1)S(1)}, bf16[512,256]{1,0:T(8,128)(2,1)}, u32[]{:S(2)}) copy-start(bf16[512,256]{1,0:T(8,128)(2,1)} %weight_local.1) | copy-start | bytes 786436

commit v16 on v15

--- a/solution.py
+++ b/solution.py
@@ -65,11 +65,17 @@
     return np.block([[cos, sin], [-sin, cos]])
 
 
-def grad_kernel(norm, place, *refs):
-    *pieces, weight, table, out, projected = refs
+def strip_row(signal, r):
+    return jnp.concatenate([signal[block, r] for block in range(signal.shape[0])], axis=0)
+
+
+def grad_kernel(norm, col, low, *refs):
+    *pieces, weight, table, out, strip_out, projected = refs
+    place = col[0], low[0]
     tile_cols = pieces[0].shape[1]
     for step, piece in enumerate(pieces):
         block = place[0] ^ step
+        strip_out[block] = piece[...]
         rows = [dot_t(piece[r], weight[...]).astype(jnp.bfloat16) for r in range(piece.shape[0])]
         where = pl.ds(pl.multiple_of(block * tile_cols, tile_cols), tile_cols)
         projected[where, :] = jnp.concatenate(rows, axis=1)
@@ -77,17 +83,21 @@
 
 
 def grad_spectrum(norm, place, pieces, weight, table):
-    shape = (table.shape[0], pieces[0].shape[0] * weight.shape[0])
+    strip, tile_cols, channels = pieces[0].shape
+    shape = (table.shape[0], strip * weight.shape[0])
     in_vmem = pl.BlockSpec(memory_space=pltpu.VMEM)
     return pl.pallas_call(
         functools.partial(grad_kernel, norm),
-        out_shape=jax.ShapeDtypeStruct(shape, jnp.bfloat16),
-        in_specs=[pl.BlockSpec(memory_space=pltpu.SMEM)] + [in_vmem] * (len(pieces) + 2),
-        out_specs=in_vmem,
+        out_shape=[
+            jax.ShapeDtypeStruct(shape, jnp.bfloat16),
+            jax.ShapeDtypeStruct((len(pieces), strip, tile_cols, channels), jnp.bfloat16),
+        ],
+        in_specs=[pl.BlockSpec(memory_space=pltpu.SMEM)] * 2 + [in_vmem] * (len(pieces) + 2),
+        out_specs=[in_vmem] * 2,
         scratch_shapes=[pltpu.VMEM(shape, jnp.bfloat16)],
         compiler_params=pltpu.CompilerParams(vmem_limit_bytes=10 * MIB),
         cost_estimate=pl.CostEstimate(flops=0, bytes_accessed=2 * MIB, transcendentals=0),
-    )(place, *pieces, weight, table)
+    )(*place, *pieces, weight, table)
 
 
 def fetching_spectrum_kernel(norm, signal, weight, table, out, signal_held, weight_held, table_held, sems):
@@ -177,30 +187,13 @@
         out[:, g * LANES : (g + 1) * LANES] = wide[g].astype(jnp.bfloat16)
 
 
-def output_kernel(norm, place, moved, weight_in, weight_local, table, *refs):
-    *pieces, out, spatial = refs
-    spatial[...] = (dot(table[...], moved[...]) * norm).astype(jnp.bfloat16)
-    half, tile_cols = weight_in.shape[0], pieces[0].shape[1]
-    for step, piece in enumerate(pieces):
-        start = pl.multiple_of((place[0] ^ step) * tile_cols, tile_cols)
-        part = spatial[pl.ds(start, tile_cols), :]
-        for r in range(out.shape[0]):
-            total = dot(part[:, r * half : (r + 1) * half], weight_in[...])
-            total = total + dot_t(piece[r], weight_local[...])
-            out[r, pl.ds(start, tile_cols), :] = total.astype(jnp.bfloat16)
-
-
-def output(norm, place, moved, weight_in, weight_local, table, pieces, shape):
-    in_vmem = pl.BlockSpec(memory_space=pltpu.VMEM)
-    return pl.pallas_call(
-        functools.partial(output_kernel, norm),
-        out_shape=jax.ShapeDtypeStruct(shape, jnp.bfloat16),
-        in_specs=[pl.BlockSpec(memory_space=pltpu.SMEM)] + [in_vmem] * (len(pieces) + 4),
-        out_specs=in_vmem,
-        scratch_shapes=[pltpu.VMEM(moved.shape, jnp.bfloat16)],
-        compiler_params=pltpu.CompilerParams(vmem_limit_bytes=10 * MIB),
-        cost_estimate=pl.CostEstimate(flops=0, bytes_accessed=3 * MIB, transcendentals=0),
-    )(place, moved, weight_in, weight_local, table, *pieces)
+def output_kernel(norm, moved, strip_grad, weight_in, weight_local, table, out):
+    spatial = (dot(table[...], moved[...]) * norm).astype(jnp.bfloat16)
+    half = weight_in.shape[0]
+    for r in range(out.shape[0]):
+        total = dot(spatial[:, r * half : (r + 1) * half], weight_in[...])
+        total = total + dot_t(strip_row(strip_grad, r), weight_local[...])
+        out[r] = total.astype(jnp.bfloat16)
 
 
 TAIL = 16
@@ -229,7 +222,8 @@
     return jnp.concatenate([lanes, fill], axis=1).astype(jnp.bfloat16)
 
 
-def pack_kernel(place, target, mask, early, late, mask_row, mask_held, sems):
+def pack_kernel(col, low, target, mask, early, late, mask_row, mask_held, sems):
+    place = col[0], low[0]
     tile_rows, tile_cols = mask.shape
     channels = target.shape[1]
     last = tile_rows - NEAR
@@ -259,12 +253,12 @@
     return pl.pallas_call(
         pack_kernel,
         out_shape=[jax.ShapeDtypeStruct(shape, jnp.bfloat16) for shape in shapes],
-        in_specs=[pl.BlockSpec(memory_space=pltpu.SMEM), hbm, hbm],
+        in_specs=[pl.BlockSpec(memory_space=pltpu.SMEM)] * 2 + [hbm, hbm],
         out_specs=[pl.BlockSpec(memory_space=pltpu.VMEM)] * len(shapes),
         scratch_shapes=[pltpu.VMEM(mask.shape, mask.dtype), pltpu.SemaphoreType.DMA((3,))],
         compiler_params=pltpu.CompilerParams(vmem_limit_bytes=4 * MIB),
         cost_estimate=pl.CostEstimate(flops=0, bytes_accessed=MIB, transcendentals=0),
-    )(place, in_hbm(target.reshape(tile_rows * tile_cols, channels)), in_hbm(mask))
+    )(*place, in_hbm(target.reshape(tile_rows * tile_cols, channels)), in_hbm(mask))
 
 
 def fetch_kernel(*refs):
@@ -289,12 +283,13 @@
     )(*[in_hbm(a) for a in arrays])
 
 
-def edge_kernel(tile_cols, place, early_pack, late_pack, *refs):
+def edge_kernel(tile_cols, col, low, early_pack, late_pack, *refs):
+    place = col[0], low[0]
     sources, (early, late, own) = refs[:-3], refs[-3:]
     count = len(sources) // 2
     keep = 2 * REACH
     channels = own.shape[2]
-    low, high = odd_row(place), odd_col(place)
+    lower, high = odd_row(place), odd_col(place)
 
     def put_rows(row, tail, head):
         rows = slice(row, row + tail.shape[0])
@@ -307,15 +302,15 @@
     def put_pack(row, one, other):
         for i in range(NEAR):
             at = i * tile_cols
-            tail = pick(low, one[at + tile_cols - keep : at + tile_cols], other[at + tile_cols - keep : at + tile_cols])
-            head = pick(low, one[at : at + keep], other[at : at + keep])
+            tail = pick(lower, one[at + tile_cols - keep : at + tile_cols], other[at + tile_cols - keep : at + tile_cols])
+            head = pick(lower, one[at : at + keep], other[at : at + keep])
             put_rows(row + i, tail[None], head[None])
-        mask = turned(pick(low, one[NEAR * tile_cols :, :tile_cols], other[NEAR * tile_cols :, :tile_cols]))
+        mask = turned(pick(lower, one[NEAR * tile_cols :, :tile_cols], other[NEAR * tile_cols :, :tile_cols]))
         tail, head = [filled(m, channels)[None] for m in (mask[tile_cols - keep :], mask[:keep])]
         put_rows(row + NEAR, tail, head)
 
     def put_picked(row, one, other):
-        put_rows(row, *[pick(low, sources[one + i * count][...], sources[other + i * count][...]) for i in (0, 1)])
+        put_rows(row, *[pick(lower, sources[one + i * count][...], sources[other + i * count][...]) for i in (0, 1)])
 
     def put_own(row, index):
         put_rows(row, sources[index][...], sources[index + count][...])
@@ -346,13 +341,13 @@
         functools.partial(edge_kernel, tile_cols),
         grid=(1,),
         out_shape=[jax.ShapeDtypeStruct(shape, features.dtype) for shape in shapes],
-        in_specs=[pl.BlockSpec(memory_space=pltpu.SMEM)] + whole + specs(tail) + specs(0),
+        in_specs=[pl.BlockSpec(memory_space=pltpu.SMEM)] * 2 + whole + specs(tail) + specs(0),
         out_specs=[pl.BlockSpec(shape, lambda i: (0, 0, 0)) for shape in shapes],
         compiler_params=pltpu.CompilerParams(vmem_limit_bytes=8 * MIB),
         cost_estimate=pl.CostEstimate(
             flops=0, bytes_accessed=16 * rows * keep * channels, transcendentals=0
         ),
-    )(place, early_pack, late_pack, *parts, *parts)
+    )(*place, early_pack, late_pack, *parts, *parts)
 
 
 def put(wide, row, value, stride):
@@ -437,8 +432,9 @@
 
 
 def tile_forward_kernel(
-    place, early, features, late, first, second, ok, pre, slopes, wide_even, wide_odd
+    col, low, early, features, late, first, second, ok, pre, slopes, wide_even, wide_odd
 ):
+    place = col[0], low[0]
     rows, stride, _ = features.shape
     find = part_of(rows, REACH, (early, late), (features,), (late, early))
 
@@ -460,7 +456,8 @@
 
 
 def tile_backward_kernel(
-    place,
+    col,
+    low,
     pre,
     slopes,
     early_pack,
@@ -474,6 +471,7 @@
     wide_even,
     wide_odd,
 ):
+    place = col[0], low[0]
     rows, stride, channels = target.shape
     packs = (early_pack, late_pack)
     find = part_of(rows, NEAR, packs, (target,), packs[::-1])
@@ -510,8 +508,9 @@
     last_stages(stride, TILE_BLOCKS, rows, first, second, wide_even, wide_odd, slopes, use)
 
 
-def side_kernel(place, early, late, own, first, second, ok, tile, *refs):
+def side_kernel(col, low, early, late, own, first, second, ok, tile, *refs):
     *pieces, out, wide_even, wide_odd, slopes = refs
+    place = col[0], low[0]
     rows, tile_cols, channels = tile.shape
     keep = 2 * REACH
     stride = 2 * (REACH + keep)
@@ -573,7 +572,7 @@
     return pl.pallas_call(
         tile_forward_kernel,
         out_shape=shapes,
-        in_specs=[pl.BlockSpec(memory_space=pltpu.SMEM)] + [in_vmem] * 6,
+        in_specs=[pl.BlockSpec(memory_space=pltpu.SMEM)] * 2 + [in_vmem] * 6,
         out_specs=[in_vmem] * 2,
         scratch_shapes=[wide_buffer(rows + h, stride, channels) for h in (16, 12)],
         compiler_params=pltpu.CompilerParams(vmem_limit_bytes=18 * MIB),
@@ -582,7 +581,7 @@
             bytes_accessed=8 * MIB,
             transcendentals=0,
         ),
-    )(place, early, features, late, first, second, ok)
+    )(*place, early, features, late, first, second, ok)
 
 
 def tile_backward(place, pre, slopes, early_pack, target, *operands):
@@ -591,7 +590,7 @@
     return pl.pallas_call(
         tile_backward_kernel,
         out_shape=jax.ShapeDtypeStruct(target.shape, jnp.bfloat16),
-        in_specs=[pl.BlockSpec(memory_space=pltpu.SMEM)] + [in_vmem] * (4 + len(operands)),
+        in_specs=[pl.BlockSpec(memory_space=pltpu.SMEM)] * 2 + [in_vmem] * (4 + len(operands)),
         out_specs=in_vmem,
         scratch_shapes=[wide_buffer(rows + h, stride, channels) for h in (8, 4)],
         compiler_params=pltpu.CompilerParams(vmem_limit_bytes=16 * MIB),
@@ -600,7 +599,7 @@
             bytes_accessed=8 * MIB,
             transcendentals=0,
         ),
-    )(place, pre, slopes, early_pack, target, *operands)
+    )(*place, pre, slopes, early_pack, target, *operands)
 
 
 def sides(place, tile, *operands):
@@ -612,7 +611,7 @@
     return pl.pallas_call(
         side_kernel,
         out_shape=[piece] * count,
-        in_specs=[pl.BlockSpec(memory_space=pltpu.SMEM)] + [in_vmem] * (len(operands) + 1),
+        in_specs=[pl.BlockSpec(memory_space=pltpu.SMEM)] * 2 + [in_vmem] * (len(operands) + 1),
         out_specs=[in_vmem] * count,
         scratch_shapes=[
             pltpu.VMEM(tile.shape, tile.dtype),
@@ -625,7 +624,7 @@
             bytes_accessed=4 * MIB,
             transcendentals=0,
         ),
-    )(place, *operands, tile)
+    )(*place, *operands, tile)
 
 
 def pairs(axis, start):
@@ -669,7 +668,7 @@
     col_ids = col0 - REACH + jnp.arange(tile_cols + 2 * REACH, dtype=jnp.int32)
     ok = ((col_ids >= 0) & (col_ids < width))[:, None] & ((row_ids >= 0) & (row_ids < height))[None]
     ok = ok.astype(jnp.float32)
-    place = jnp.stack([lax.axis_index("col"), lax.axis_index("row") & 1]).astype(jnp.int32)
+    place = tuple(jnp.full((1,), i, jnp.int32) for i in (lax.axis_index("col"), lax.axis_index("row") & 1))
     early_pack, late_pack, mask_row = target_packs(place, target, hole_mask)
     inputs, ok, early_pack = lax.optimization_barrier((inputs, ok, early_pack))
 
@@ -699,7 +698,7 @@
     for step in reversed(range(1, col_devices)):
         swaps = [(i, i ^ step) for i in range(col_devices)]
         pieces[step] = lax.ppermute(pieces[step], "col", swaps)
-    grad_cols = grad_spectrum(col_norm, place, pieces, weight_out, table)
+    grad_cols, strip_grad = grad_spectrum(col_norm, place, pieces, weight_out, table)
     wide = pltpu.VMEM((strip * half // LANES, width, LANES), jnp.float32)
     grad_rows = vmem_call(
         functools.partial(mix_kernel, row_norm, owned, devices),
@@ -712,9 +711,15 @@
         scratch=[wide, wide],
     )[0]
     returned = swap(grad_rows)
-    return output(
-        col_norm, place, returned, weight_in, weight_local, table_back, pieces, inputs.shape
-    )
+    return vmem_call(
+        functools.partial(output_kernel, col_norm),
+        [jax.ShapeDtypeStruct(inputs.shape, bf16)],
+        returned,
+        strip_grad,
+        weight_in,
+        weight_local,
+        table_back,
+    )[0]
 
 
 def solution(mesh):

time: 97.1 us -> 94.3 us (0.971)
  Pallas kernels: 30.1 us -> 25.6 us
  waiting for transfers between devices: 6.73 us -> 8.13 us
  blocking collectives: 37.1 us -> 38.1 us
    pallas_call x2 -> x1, Pallas kernels: 4.44 us -> 0.9 us  [grad_spectrum(): pl.pallas_call(functools.partial(grad_kernel, norm), out_shape=[jax.Shape...]
    pallas_call x1 -> x2, Pallas kernels: 2.05 us -> 4.01 us  [vmem_call(): pl.pallas_call(body, out_shape=shapes, in_specs=[spec] * len(operands), o...]
    all_to_all x2, blocking collectives: 37.1 us -> 38.1 us  [swap(): lax.all_to_all(spectrum, ('col', 'row'), split_axis=0, concat_axis=0, til...]
  transfers between devices with their start and end apart: 10 -> 10, of which waited for: 3 -> 4; matrix products, arithmetic and copies ran while one was open for 0% -> 0% of each run, Pallas kernels for 25% -> 22%
where the time goes in v16:
time: 94.3 us; the launch traced here: 93 us
  blocking collectives  38.1 us (40%)
  Pallas kernels  25.6 us (27%)
  starting transfers between devices  20.7 us (22%)
  waiting for transfers between devices  8.13 us (9%)
    all_to_all x2, blocking collectives, swap(): lax.all_to_all(spectrum, ('col', 'row'), split_axis=0, concat_axis=0, til...  38.1 us
    ppermute x3, waiting for transfers between devices, shards(): pieces[step] = lax.ppermute(pieces[step], 'col', swaps)  7.22 us
    pallas_call x1, Pallas kernels, tile_forward(): pl.pallas_call(tile_forward_kernel, out_shape=shapes, in_specs=[pl.BlockS...  5.87 us
    ppermute x3, starting transfers between devices, shards(): pieces[step] = lax.ppermute(pieces[step], 'col', swaps)  5.16 us
    all_to_all x1, starting transfers between devices, swap(): lax.all_to_all(spectrum, ('col', 'row'), split_axis=0, concat_axis=0, til...  5.12 us
    pallas_call x1, Pallas kernels, sides(): pl.pallas_call(side_kernel, out_shape=[piece] * count, in_specs=[pl.Block...  4.76 us
    ppermute x1, starting transfers between devices, shards(): late = lax.ppermute(features, 'row', pairs('row', 1))  4.5 us
    pallas_call x2, Pallas kernels, vmem_call(): pl.pallas_call(body, out_shape=shapes, in_specs=[spec] * len(operands), o...  4.01 us
  transfers between devices with their start and end apart: 10, of which 4 were waited for; matrix products, arithmetic and copies ran while one was open for 0% of the time, Pallas kernels for 22%

profile of v16, /device:TPU:1, one launch (start us, length us, event | category | flops | bytes accessed | tf_op | source)
XLA Modules:
  0.0 93.0 jit_solution(13770372435068203869)
XLA Ops:
  0.0 4.5 %collective-permute-start.2 = (bf16[8,128,256]{2,1,0:T(8,128)(2,1)}, bf16[8,128,256]{2,1,0:T(8,128)(2,1)S(1)}, u32[]{:S(2)}, u32[]{:S(2)}) collective-permute-start(bf16[8,128,256]{2,1,0:T(8,128)(2,1)} %refs_7_.1), channel_id=1, source_target_pairs={{4,8},{12,16},{20,24},{8,4},{16,12},{24,20},{5,9},{13,17},{21,25},... | collective-permute-start | bytes 1572872 | tf_op jit(solution)/shard_map/ppermute | solution.py:681
  4.5 0.1 collective-permute-start.1
  4.6 1.1 %shard_map.136 = (bf16[528,256]{1,0:T(8,128)(2,1)S(1)}, bf16[528,256]{1,0:T(8,128)(2,1)S(1)}, bf16[1,128,256]{2,1,0:T(8,128)(2,1)S(1)}) custom-call(s32[1]{0:T(128)} %bitcast.col, s32[1]{0:T(128)} %bitcast.1.low, bf16[1024,256]{1,0:T(8,128)(2,1)} %bitcast.10, s32[8,128]{1,0:T(8,128)} %mask.1), custom_call_target="tpu_custom_call" | custom-call | bytes 1048576 | tf_op jit(solution)/shard_map/pallas_call | solution.py:253
  5.7 0.1 and_convert_fusion.ok
  5.8 0.5 collective-permute-start
  6.3 3.0 %collective-permute-start.3 = (bf16[528,256]{1,0:T(8,128)(2,1)S(1)}, bf16[528,256]{1,0:T(8,128)(2,1)S(1)}, u32[]{:S(2)}, u32[]{:S(2)}) collective-permute-start(bf16[528,256]{1,0:T(8,128)(2,1)S(1)} %get-tuple-element.41), channel_id=1, source_target_pairs={{4,8},{12,16},{20,24},{8,4},{16,12},{24,20},{5,9},{13,17},{21,25},... | collective-permute-start | bytes 811016 | tf_op jit(solution)/shard_map/ppermute | solution.py:685
  9.4 3.3 %shard_map.137 = bf16[512,384]{1,0:T(8,128)(2,1)} custom-call(bf16[2,512,512]{2,1,0:T(8,128)(2,1)} %signal, bf16[192,512]{1,0:T(8,128)(2,1)} %bitcast.15, bf16[512,512]{1,0:T(8,128)(2,1)} %constant.34.clone.table.refs_5_), custom_call_target="tpu_custom_call" | custom-call | bytes 2097152 | tf_op jit(solution)/shard_map/pallas_call | solution.py:123
  12.7 5.1 %all-to-all-start = ((bf16[32,16,384]{2,1,0:T(8,128)(2,1)}), bf16[32,16,384]{2,1,0:T(8,128)(2,1)S(1)}, u32[]{:S(2)}, u32[]{:S(2)}) async-start(bf16[32,16,384]{2,1,0:T(8,128)(2,1)} %bitcast.4), calls=%async_computation | async-start | bytes 786432 | tf_op jit(solution)/shard_map/all_to_all | solution.py:664
  17.8 0.0 copy-start.2
  17.8 1.7 %shard_map.138 = (bf16[3,3,256,256]{3,2,1,0:T(8,128)(2,1)S(1)}, bf16[3,3,256,256]{3,2,1,0:T(8,128)(2,1)S(1)}) custom-call(bf16[3,3,256,256]{3,2,1,0:T(8,128)(2,1)} %refs_0_, bf16[3,3,256,256]{3,2,1,0:T(8,128)(2,1)} %refs_1_.1), custom_call_target="tpu_custom_call" | custom-call | bytes 5242880 | tf_op jit(solution)/shard_map/pallas_call | solution.py:275
  19.6 0.0 copy-done.2
  19.6 5.9 %shard_map.139 = (f32[2048,256]{1,0:T(8,128)S(1)}, f32[1536,256]{1,0:T(8,128)S(1)}) custom-call(s32[1]{0:T(128)} %bitcast.col, s32[1]{0:T(128)} %bitcast.1.low, bf16[8,128,256]{2,1,0:T(8,128)(2,1)S(1)} %collective-permute-done.1.early.refs_0_.refs_5_, bf16[8,128,256]{2,1,0:T(8,128)(2,1)S(1)} %copy-done.2, ...), custom_call_target="tpu_custom_call" | custom-call | flops 5435817984 | bytes 8388608 | tf_op jit(solution)/shard_map/pallas_call | solution.py:572
  25.5 0.1 shard_map.140
  25.6 1.5 %collective-permute-start.4 = (bf16[43,8,256]{2,1,0:T(8,128)(2,1)S(1)}, bf16[43,8,256]{2,1,0:T(8,128)(2,1)S(1)}, u32[]{:S(2)}, u32[]{:S(2)}) collective-permute-start(bf16[43,8,256]{2,1,0:T(8,128)(2,1)S(1)} %get-tuple-element.43), channel_id=1, source_target_pairs={{0,1},{2,3},{1,0},{3,2},{4,5},{6,7},{5,4},{7,6},{8,9},{10,11},{9,8... | collective-permute-start | bytes 528392 | tf_op jit(solution)/shard_map/ppermute | solution.py:691
  27.1 0.8 collective-permute-start.5
  27.9 3.9 %shard_map.141.tile = bf16[8,128,256]{2,1,0:T(8,128)(2,1)S(1)} custom-call(s32[1]{0:T(128)} %bitcast.col, s32[1]{0:T(128)} %bitcast.1.low, f32[2048,256]{1,0:T(8,128)S(1)} %get-tuple-element.46.pre, f32[1536,256]{1,0:T(8,128)S(1)} %get-tuple-element.47.slopes, bf16[528,256]{1,0:T(8,128)(2,1)S(1)} %collective-permute-done.early_pack, ...), custom_call_target="tpu_custom_call" | custom-call | flops 3019898880 | bytes 8388608 | tf_op jit(solution)/shard_map/pallas_call | solution.py:590
  31.8 0.9 collective-permute-done.4.early
  32.7 4.8 %shard_map.142 = (bf16[2,128,256]{2,1,0:T(8,128)(2,1)S(1)}, bf16[2,128,256]{2,1,0:T(8,128)(2,1)S(1)}, bf16[2,128,256]{2,1,0:T(8,128)(2,1)S(1)}, bf16[2,128,256]{2,1,0:T(8,128)(2,1)S(1)}) custom-call(s32[1]{0:T(128)} %bitcast.col, s32[1]{0:T(128)} %bitcast.1.low, bf16[43,8,256]{2,1,0:T(8,128)(2,1)S(1)} %collective-permute-done.4.early, ...), custom_call_target="tpu_custom_call" | custom-call | flops 3170893824 | bytes 4194304 | tf_op jit(solution)/shard_map/pallas_call | solution.py:611
  37.5 0.0 copy-start.5
  37.5 0.0 copy-start.8
  37.5 0.0 copy-start.9
  37.5 3.0 %collective-permute-start.6 = (bf16[2,128,256]{2,1,0:T(8,128)(2,1)S(1)}, bf16[2,128,256]{2,1,0:T(8,128)(2,1)S(1)}, u32[]{:S(2)}, u32[]{:S(2)}) collective-permute-start(bf16[2,128,256]{2,1,0:T(8,128)(2,1)S(1)} %get-tuple-element.54), channel_id=1, source_target_pairs={{0,1},{1,0},{2,3},{3,2},{4,5},{5,4},{6,7},{7,6},{8,9},{9,8},{10,11... | collective-permute-start | bytes 393224 | tf_op jit(solution)/shard_map/ppermute | solution.py:700
  40.5 0.9 %collective-permute-start.7 = (bf16[2,128,256]{2,1,0:T(8,128)(2,1)S(1)}, bf16[2,128,256]{2,1,0:T(8,128)(2,1)S(1)}, u32[]{:S(2)}, u32[]{:S(2)}) collective-permute-start(bf16[2,128,256]{2,1,0:T(8,128)(2,1)S(1)} %get-tuple-element.55), channel_id=1, source_target_pairs={{0,2},{1,3},{2,0},{3,1},{4,6},{5,7},{6,4},{7,5},{8,10},{9,11},{10,... | collective-permute-start | bytes 393224 | tf_op jit(solution)/shard_map/ppermute | solution.py:700
  41.4 1.2 %collective-permute-start.8 = (bf16[2,128,256]{2,1,0:T(8,128)(2,1)S(1)}, bf16[2,128,256]{2,1,0:T(8,128)(2,1)S(1)}, u32[]{:S(2)}, u32[]{:S(2)}) collective-permute-start(bf16[2,128,256]{2,1,0:T(8,128)(2,1)S(1)} %get-tuple-element.56), channel_id=1, source_target_pairs={{0,3},{1,2},{2,1},{3,0},{4,7},{5,6},{6,5},{7,4},{8,11},{9,10},{10,... | collective-permute-start | bytes 393224 | tf_op jit(solution)/shard_map/ppermute | solution.py:700
  42.7 0.2 collective-permute-done.6.refs_1_
  42.9 4.1 %collective-permute-done.7.refs_2_ = bf16[2,128,256]{2,1,0:T(8,128)(2,1)S(1)} collective-permute-done((bf16[2,128,256]{2,1,0:T(8,128)(2,1)S(1)}, bf16[2,128,256]{2,1,0:T(8,128)(2,1)S(1)}, u32[]{:S(2)}, u32[]{:S(2)}) %collective-permute-start.7) | collective-permute-done | bytes 131104 | tf_op jit(solution)/shard_map/ppermute | solution.py:700
  46.9 2.9 %collective-permute-done.8.refs_3_ = bf16[2,128,256]{2,1,0:T(8,128)(2,1)S(1)} collective-permute-done((bf16[2,128,256]{2,1,0:T(8,128)(2,1)S(1)}, bf16[2,128,256]{2,1,0:T(8,128)(2,1)S(1)}, u32[]{:S(2)}, u32[]{:S(2)}) %collective-permute-start.8) | collective-permute-done | bytes 131104 | tf_op jit(solution)/shard_map/ppermute | solution.py:700
  49.9 0.9 shard_map.143
  50.8 22.5 %all_to_all.34 = bf16[32,16,384]{2,1,0:T(8,128)(2,1)S(1)} all-to-all(bf16[32,16,384]{2,1,0:T(8,128)(2,1)S(1)} %bitcast.17), channel_id=1, replica_groups=mesh['row'=8,'col'=4] {'col','row'}, dimensions={0} | all-to-all | bytes 786432 | tf_op jit(solution)/shard_map/all_to_all | solution.py:664
  73.4 2.1 %shard_map.144 = bf16[512,384]{1,0:T(8,128)(2,1)S(1)} custom-call(bf16[512,384]{1,0:T(8,128)(2,1)S(1)} %bitcast.11, bf16[512,384]{1,0:T(8,128)(2,1)S(1)} %bitcast.12, bf16[384,384]{1,0:T(8,128)(2,1)S(1)} %copy-done.5, bf16[128,128]{1,0:T(8,128)(2,1)S(1)} %copy-done.8, bf16[128,128]{1,0:T(8,128)(2,1)S(1)} %copy-done.9), custom_call_target="tpu_custom_call" | custom-call | bytes 1540096 | tf_op jit(solution)/shard_map/pallas_call | solution.py:30
  75.4 15.6 %all_to_all.35 = bf16[32,16,384]{2,1,0:T(8,128)(2,1)S(1)} all-to-all(bf16[32,16,384]{2,1,0:T(8,128)(2,1)S(1)} %bitcast.13), channel_id=1, replica_groups=mesh['row'=8,'col'=4] {'col','row'}, dimensions={0} | all-to-all | bytes 786432 | tf_op jit(solution)/shard_map/all_to_all | solution.py:664
  91.0 2.0 %shard_map.145 = bf16[2,512,512]{2,1,0:T(8,128)(2,1)} custom-call(bf16[512,384]{1,0:T(8,128)(2,1)S(1)} %bitcast.14, bf16[4,2,128,256]{3,2,1,0:T(8,128)(2,1)S(1)} %get-tuple-element.58.strip_grad, bf16[192,512]{1,0:T(8,128)(2,1)S(1)} %bitcast.16, bf16[512,256]{1,0:T(8,128)(2,1)S(1)} %copy-done.6, bf16[512,512]{1,0:T(8,128)(2,1)S(1)} %copy-done.4), custom_call_target="tpu_custom_call" | custom-call | bytes 2949120 | tf_op jit(solution)/shard_map/pallas_call | solution.py:30
  (23 shorter events, 0.1 us)
Async XLA Ops:
  0.0 19.5 %collective-permute-start.2 = (bf16[8,128,256]{2,1,0:T(8,128)(2,1)}, bf16[8,128,256]{2,1,0:T(8,128)(2,1)S(1)}, u32[]{:S(2)}, u32[]{:S(2)}) collective-permute-start(bf16[8,128,256]{2,1,0:T(8,128)(2,1)} %refs_7_.1), channel_id=1, source_target_pairs={{4,8},{12,16},{20,24},{8,4},{16,12},{24,20},{5,9},{13,17},{21,25},... | collective-permute-start | bytes 1572872 | tf_op jit(solution)/shard_map/ppermute | solution.py:681
  4.5 15.1 %collective-permute-start.1 = (bf16[8,128,256]{2,1,0:T(8,128)(2,1)}, bf16[8,128,256]{2,1,0:T(8,128)(2,1)S(1)}, u32[]{:S(2)}, u32[]{:S(2)}) collective-permute-start(bf16[8,128,256]{2,1,0:T(8,128)(2,1)} %refs_7_.1), channel_id=1, source_target_pairs={{0,4},{8,12},{16,20},{24,28},{4,0},{12,8},{20,16},{28,24},{1,5},{9... | collective-permute-start | bytes 1572872 | tf_op jit(solution)/shard_map/ppermute | solution.py:680
  5.8 19.7 %collective-permute-start = (bf16[528,256]{1,0:T(8,128)(2,1)S(1)}, bf16[528,256]{1,0:T(8,128)(2,1)S(1)}, u32[]{:S(2)}, u32[]{:S(2)}) collective-permute-start(bf16[528,256]{1,0:T(8,128)(2,1)S(1)} %get-tuple-element.33), channel_id=1, source_target_pairs={{0,4},{8,12},{16,20},{24,28},{4,0},{12,8},{20,16},{28,24},{1,5},{9... | collective-permute-start | bytes 811016 | tf_op jit(solution)/shard_map/ppermute | solution.py:684
  6.3 19.1 %collective-permute-start.3 = (bf16[528,256]{1,0:T(8,128)(2,1)S(1)}, bf16[528,256]{1,0:T(8,128)(2,1)S(1)}, u32[]{:S(2)}, u32[]{:S(2)}) collective-permute-start(bf16[528,256]{1,0:T(8,128)(2,1)S(1)} %get-tuple-element.41), channel_id=1, source_target_pairs={{4,8},{12,16},{20,24},{8,4},{16,12},{24,20},{5,9},{13,17},{21,25},... | collective-permute-start | bytes 811016 | tf_op jit(solution)/shard_map/ppermute | solution.py:685
  12.7 24.8 %all-to-all-start = ((bf16[32,16,384]{2,1,0:T(8,128)(2,1)}), bf16[32,16,384]{2,1,0:T(8,128)(2,1)S(1)}, u32[]{:S(2)}, u32[]{:S(2)}) async-start(bf16[32,16,384]{2,1,0:T(8,128)(2,1)} %bitcast.4), calls=%async_computation | async-start | bytes 786432 | tf_op jit(solution)/shard_map/all_to_all | solution.py:664
  17.8 1.8 %copy-start.2 = (bf16[8,128,256]{2,1,0:T(8,128)(2,1)S(1)}, bf16[8,128,256]{2,1,0:T(8,128)(2,1)}, u32[]{:S(2)}) copy-start(bf16[8,128,256]{2,1,0:T(8,128)(2,1)} %refs_7_.1) | copy-start | bytes 1572868
  19.6 5.9 %copy-start = (bf16[8,128,256]{2,1,0:T(8,128)(2,1)S(1)}, bf16[8,128,256]{2,1,0:T(8,128)(2,1)}, u32[]{:S(2)}) copy-start(bf16[8,128,256]{2,1,0:T(8,128)(2,1)} %target.1) | copy-start | bytes 1572868
  25.6 7.1 %collective-permute-start.4 = (bf16[43,8,256]{2,1,0:T(8,128)(2,1)S(1)}, bf16[43,8,256]{2,1,0:T(8,128)(2,1)S(1)}, u32[]{:S(2)}, u32[]{:S(2)}) collective-permute-start(bf16[43,8,256]{2,1,0:T(8,128)(2,1)S(1)} %get-tuple-element.43), channel_id=1, source_target_pairs={{0,1},{2,3},{1,0},{3,2},{4,5},{6,7},{5,4},{7,6},{8,9},{10,11},{9,8... | collective-permute-start | bytes 528392 | tf_op jit(solution)/shard_map/ppermute | solution.py:691
  27.1 5.6 %collective-permute-start.5 = (bf16[43,8,256]{2,1,0:T(8,128)(2,1)S(1)}, bf16[43,8,256]{2,1,0:T(8,128)(2,1)S(1)}, u32[]{:S(2)}, u32[]{:S(2)}) collective-permute-start(bf16[43,8,256]{2,1,0:T(8,128)(2,1)S(1)} %get-tuple-element.44), channel_id=1, source_target_pairs={{1,2},{2,1},{5,6},{6,5},{9,10},{10,9},{13,14},{14,13},{17,18},{18,... | collective-permute-start | bytes 528392 | tf_op jit(solution)/shard_map/ppermute | solution.py:692
  32.7 17.2 %copy-start.1 = (bf16[512,512]{1,0:T(8,128)(2,1)S(1)}, bf16[512,512]{1,0:T(8,128)(2,1)}, u32[]{:S(2)}) copy-start(bf16[512,512]{1,0:T(8,128)(2,1)} %constant.34.clone.table.refs_5_) | copy-start | bytes 1572868
  32.7 17.2 %copy-start.7 = (bf16[192,256]{1,0:T(8,128)(2,1)S(1)}, bf16[192,256]{1,0:T(8,128)(2,1)}, u32[]{:S(2)}) copy-start(bf16[192,256]{1,0:T(8,128)(2,1)} %refs_4_.1) | copy-start | bytes 294916
  37.5 35.9 %copy-start.5 = (bf16[384,384]{1,0:T(8,128)(2,1)S(1)}, bf16[384,384]{1,0:T(8,128)(2,1)}, u32[]{:S(2)}) copy-start(bf16[384,384]{1,0:T(8,128)(2,1)} %mix.1) | copy-start | bytes 884740
  37.5 35.9 %copy-start.8 = (bf16[128,128]{1,0:T(8,128)(2,1)S(1)}, bf16[128,128]{1,0:T(8,128)(2,1)}, u32[]{:S(2)}) copy-start(bf16[128,128]{1,0:T(8,128)(2,1)} %constant.36.clone.table) | copy-start | bytes 98308
  37.5 35.9 %copy-start.9 = (bf16[128,128]{1,0:T(8,128)(2,1)S(1)}, bf16[128,128]{1,0:T(8,128)(2,1)}, u32[]{:S(2)}) copy-start(bf16[128,128]{1,0:T(8,128)(2,1)} %constant.35.clone.back_table) | copy-start | bytes 98308
  37.5 5.4 %collective-permute-start.6 = (bf16[2,128,256]{2,1,0:T(8,128)(2,1)S(1)}, bf16[2,128,256]{2,1,0:T(8,128)(2,1)S(1)}, u32[]{:S(2)}, u32[]{:S(2)}) collective-permute-start(bf16[2,128,256]{2,1,0:T(8,128)(2,1)S(1)} %get-tuple-element.54), channel_id=1, source_target_pairs={{0,1},{1,0},{2,3},{3,2},{4,5},{5,4},{6,7},{7,6},{8,9},{9,8},{10,11... | collective-permute-start | bytes 393224 | tf_op jit(solution)/shard_map/ppermute | solution.py:700
  40.5 6.4 %collective-permute-start.7 = (bf16[2,128,256]{2,1,0:T(8,128)(2,1)S(1)}, bf16[2,128,256]{2,1,0:T(8,128)(2,1)S(1)}, u32[]{:S(2)}, u32[]{:S(2)}) collective-permute-start(bf16[2,128,256]{2,1,0:T(8,128)(2,1)S(1)} %get-tuple-element.55), channel_id=1, source_target_pairs={{0,2},{1,3},{2,0},{3,1},{4,6},{5,7},{6,4},{7,5},{8,10},{9,11},{10,... | collective-permute-start | bytes 393224 | tf_op jit(solution)/shard_map/ppermute | solution.py:700
  41.4 8.4 %collective-permute-start.8 = (bf16[2,128,256]{2,1,0:T(8,128)(2,1)S(1)}, bf16[2,128,256]{2,1,0:T(8,128)(2,1)S(1)}, u32[]{:S(2)}, u32[]{:S(2)}) collective-permute-start(bf16[2,128,256]{2,1,0:T(8,128)(2,1)S(1)} %get-tuple-element.56), channel_id=1, source_target_pairs={{0,3},{1,2},{2,1},{3,0},{4,7},{5,6},{6,5},{7,4},{8,11},{9,10},{10,... | collective-permute-start | bytes 393224 | tf_op jit(solution)/shard_map/ppermute | solution.py:700
  73.3 17.7 %copy-start.3 = (bf16[512,192]{0,1:T(8,128)(2,1)S(1)}, bf16[512,192]{0,1:T(8,128)(2,1)}, u32[]{:S(2)}) copy-start(bf16[512,192]{0,1:T(8,128)(2,1)} %param.20) | copy-start | bytes 589828
  73.3 17.7 %copy-start.4 = (bf16[512,512]{1,0:T(8,128)(2,1)S(1)}, bf16[512,512]{1,0:T(8,128)(2,1)}, u32[]{:S(2)}) copy-start(bf16[512,512]{1,0:T(8,128)(2,1)} %constant.33.clone.table) | copy-start | bytes 1572868
  73.3 17.7 %copy-start.6 = (bf16[512,256]{1,0:T(8,128)(2,1)S(1)}, bf16[512,256]{1,0:T(8,128)(2,1)}, u32[]{:S(2)}) copy-start(bf16[512,256]{1,0:T(8,128)(2,1)} %weight_local.1) | copy-start | bytes 786436

commit v17 on v16

--- a/solution.py
+++ b/solution.py
@@ -71,33 +71,35 @@
 
 def grad_kernel(norm, col, low, *refs):
     *pieces, weight, table, out, strip_out, projected = refs
-    place = col[0], low[0]
-    tile_cols = pieces[0].shape[1]
-    for step, piece in enumerate(pieces):
-        block = place[0] ^ step
-        strip_out[block] = piece[...]
-        rows = [dot_t(piece[r], weight[...]).astype(jnp.bfloat16) for r in range(piece.shape[0])]
+    count = len(pieces) // 2
+    _, strip, tile_cols, _ = strip_out.shape
+    for step, (inner, outer) in enumerate(zip(pieces[:count], pieces[count:])):
+        block = col[0] ^ step
+        strip_out[block, :, REACH : tile_cols - REACH] = inner[...]
+        strip_out[block, :, :REACH] = outer[:, :REACH]
+        strip_out[block, :, tile_cols - REACH :] = outer[:, REACH:]
+        rows = [dot_t(strip_out[block, r], weight[...]).astype(jnp.bfloat16) for r in range(strip)]
         where = pl.ds(pl.multiple_of(block * tile_cols, tile_cols), tile_cols)
         projected[where, :] = jnp.concatenate(rows, axis=1)
     out[...] = (dot(table[...], projected[...]) * norm).astype(jnp.bfloat16)
 
 
-def grad_spectrum(norm, place, pieces, weight, table):
-    strip, tile_cols, channels = pieces[0].shape
+def grad_spectrum(norm, place, inner, outer, weight, table):
+    strip, columns, channels = inner[0].shape
     shape = (table.shape[0], strip * weight.shape[0])
     in_vmem = pl.BlockSpec(memory_space=pltpu.VMEM)
     return pl.pallas_call(
         functools.partial(grad_kernel, norm),
         out_shape=[
             jax.ShapeDtypeStruct(shape, jnp.bfloat16),
-            jax.ShapeDtypeStruct((len(pieces), strip, tile_cols, channels), jnp.bfloat16),
+            jax.ShapeDtypeStruct((len(inner), strip, columns + 2 * REACH, channels), jnp.bfloat16),
         ],
-        in_specs=[pl.BlockSpec(memory_space=pltpu.SMEM)] * 2 + [in_vmem] * (len(pieces) + 2),
+        in_specs=[pl.BlockSpec(memory_space=pltpu.SMEM)] * 2 + [in_vmem] * (2 * len(inner) + 2),
         out_specs=[in_vmem] * 2,
         scratch_shapes=[pltpu.VMEM(shape, jnp.bfloat16)],
         compiler_params=pltpu.CompilerParams(vmem_limit_bytes=10 * MIB),
         cost_estimate=pl.CostEstimate(flops=0, bytes_accessed=2 * MIB, transcendentals=0),
-    )(*place, *pieces, weight, table)
+    )(*place, *inner, *outer, weight, table)
 
 
 def fetching_spectrum_kernel(norm, signal, weight, table, out, signal_held, weight_held, table_held, sems):
@@ -154,17 +156,22 @@
     return jnp.concatenate(real, axis=0), jnp.concatenate(imag, axis=0)
 
 
-def mix_kernel(norm, owned, devices, spatial, grad, mix, table, back_table, out, wide, wide_grad):
-    parts = row_spectrum(spatial, table, wide, norm, owned, devices)
+def slope_kernel(norm, owned, devices, moved, mix, table, out, wide):
+    parts = row_spectrum(moved, table, wide, norm, owned, devices)
     real, imag = [part.astype(jnp.bfloat16) for part in parts]
-    grads = row_spectrum(grad, table, wide_grad, norm, owned, devices)
     half = real.shape[1]
     spans = (slice(0, half), slice(half, 2 * half))
-    mixed = []
-    for span, value in zip(spans, grads):
+    for part, span in enumerate(spans):
         pre = dot(real, mix[spans[0], span]) + dot(imag, mix[spans[1], span])
         s = 1.0 / (1.0 + jnp.exp(-pre))
-        mixed.append((value * (s * (1.0 + pre * (1.0 - s)))).astype(jnp.bfloat16))
+        out[part] = s * (1.0 + pre * (1.0 - s))
+
+
+def mix_kernel(norm, owned, devices, moved, slope, mix, table, back_table, out, wide):
+    grads = row_spectrum(moved, table, wide, norm, owned, devices)
+    half = grads[0].shape[1]
+    spans = (slice(0, half), slice(half, 2 * half))
+    mixed = [(grad * slope[part]).astype(jnp.bfloat16) for part, grad in enumerate(grads)]
     back = [dot_t(mixed[0], mix[p, spans[0]]) + dot_t(mixed[1], mix[p, spans[1]]) for p in spans]
     back = [part.astype(jnp.bfloat16) for part in back]
     height = table.shape[0] // 2
@@ -410,6 +417,11 @@
         use(row, count, conv_adjoint(wide_odd, row, count, stride, first))
 
 
+def deal(place, out, pieces):
+    for step, piece in enumerate(pieces):
+        piece[...] = out[pl.ds((place[0] ^ step) * piece.shape[0], piece.shape[0])]
+
+
 def loss_grad(row, count, value, target, hole, inside):
     near = range(row, row + count)
     weight = (1.0 + 2.0 * stacked(hole, near)) * stacked(inside, range(row + NEAR, row + count + NEAR))
@@ -467,10 +479,9 @@
     first,
     second,
     ok,
-    out,
-    wide_even,
-    wide_odd,
+    *refs,
 ):
+    *pieces, out, wide_even, wide_odd = refs
     place = col[0], low[0]
     rows, stride, channels = target.shape
     packs = (early_pack, late_pack)
@@ -503,15 +514,17 @@
         put(wide_even, row, loss_grad(row, count, value, goal, hole, inside), stride)
 
     def use(row, count, value):
-        out[row : row + count] = value.reshape(count, stride, channels).astype(jnp.bfloat16)
+        value = value.reshape(count, stride, channels)[:, REACH : stride - REACH]
+        out[row : row + count] = value.astype(jnp.bfloat16)
 
     last_stages(stride, TILE_BLOCKS, rows, first, second, wide_even, wide_odd, slopes, use)
-
-
-def side_kernel(col, low, early, late, own, first, second, ok, tile, *refs):
+    deal(place, out, pieces)
+
+
+def side_kernel(col, low, early, late, own, first, second, ok, *refs):
     *pieces, out, wide_even, wide_odd, slopes = refs
     place = col[0], low[0]
-    rows, tile_cols, channels = tile.shape
+    rows, _, channels = out.shape
     keep = 2 * REACH
     stride = 2 * (REACH + keep)
     tall = rows + 2 * REACH
@@ -547,16 +560,14 @@
     first_stages(
         stride, SIDE_BLOCKS, rows, feature, inside, first, second, wide_even, wide_odd, slopes, use_forward
     )
-    out[:, REACH : tile_cols - REACH] = tile[:, REACH : tile_cols - REACH]
 
     def use(row, count, value):
         value = value.reshape(count, stride, channels).astype(jnp.bfloat16)
         out[row : row + count, :REACH] = value[:, REACH : 2 * REACH]
-        out[row : row + count, tile_cols - REACH :] = value[:, stride - 2 * REACH : stride - REACH]
+        out[row : row + count, REACH:] = value[:, stride - 2 * REACH : stride - REACH]
 
     last_stages(stride, SIDE_BLOCKS, rows, first, second, wide_even, wide_odd, slopes, use)
-    for step, piece in enumerate(pieces):
-        piece[...] = out[pl.ds((place[0] ^ step) * piece.shape[0], piece.shape[0])]
+    deal(place, out, pieces)
 
 
 def wide_buffer(rows, stride, channels):
@@ -584,15 +595,24 @@
     )(*place, early, features, late, first, second, ok)
 
 
+def piece_shapes(rows, columns, channels):
+    count = lax.axis_size("col")
+    return [jax.ShapeDtypeStruct((rows // count, columns, channels), jnp.bfloat16)] * count
+
+
 def tile_backward(place, pre, slopes, early_pack, target, *operands):
     rows, stride, channels = target.shape
     in_vmem = pl.BlockSpec(memory_space=pltpu.VMEM)
+    shapes = piece_shapes(rows, stride - 2 * REACH, channels)
     return pl.pallas_call(
         tile_backward_kernel,
-        out_shape=jax.ShapeDtypeStruct(target.shape, jnp.bfloat16),
+        out_shape=shapes,
         in_specs=[pl.BlockSpec(memory_space=pltpu.SMEM)] * 2 + [in_vmem] * (4 + len(operands)),
-        out_specs=in_vmem,
-        scratch_shapes=[wide_buffer(rows + h, stride, channels) for h in (8, 4)],
+        out_specs=[in_vmem] * len(shapes),
+        scratch_shapes=[
+            pltpu.VMEM((rows, stride - 2 * REACH, channels), jnp.bfloat16),
+            *[wide_buffer(rows + h, stride, channels) for h in (8, 4)],
+        ],
         compiler_params=pltpu.CompilerParams(vmem_limit_bytes=16 * MIB),
         cost_estimate=pl.CostEstimate(
             flops=2 * 9 * channels * channels * stride * (2 * rows + 4),
@@ -602,19 +622,18 @@
     )(*place, pre, slopes, early_pack, target, *operands)
 
 
-def sides(place, tile, *operands):
-    rows, tile_cols, channels = tile.shape
+def sides(place, shape, *operands):
+    rows, _, channels = shape
     stride = 6 * REACH
-    count = lax.axis_size("col")
-    piece = jax.ShapeDtypeStruct((rows // count, tile_cols, channels), jnp.bfloat16)
     in_vmem = pl.BlockSpec(memory_space=pltpu.VMEM)
+    shapes = piece_shapes(rows, 2 * REACH, channels)
     return pl.pallas_call(
         side_kernel,
-        out_shape=[piece] * count,
-        in_specs=[pl.BlockSpec(memory_space=pltpu.SMEM)] * 2 + [in_vmem] * (len(operands) + 1),
-        out_specs=[in_vmem] * count,
+        out_shape=shapes,
+        in_specs=[pl.BlockSpec(memory_space=pltpu.SMEM)] * 2 + [in_vmem] * len(operands),
+        out_specs=[in_vmem] * len(shapes),
         scratch_shapes=[
-            pltpu.VMEM(tile.shape, tile.dtype),
+            pltpu.VMEM((rows, 2 * REACH, channels), jnp.bfloat16),
             *[wide_buffer(rows + h, stride, channels) for h in (16, 12)],
             pltpu.VMEM(((rows + 4) * stride, channels), jnp.float32),
         ],
@@ -624,7 +643,7 @@
             bytes_accessed=4 * MIB,
             transcendentals=0,
         ),
-    )(*place, *operands, tile)
+    )(*place, *operands)
 
 
 def pairs(axis, start):
@@ -690,25 +709,45 @@
     )
     early_edge = lax.ppermute(early_edge, "col", pairs("col", 0))
     late_edge = lax.ppermute(late_edge, "col", pairs("col", 1))
-    tile = tile_backward(
+    inner = tile_backward(
         place, pre, slopes, early_pack, target, late_pack, mask_row, kernel_first, kernel_second, ok
     )
-    pieces = sides(place, tile, early_edge, late_edge, own, kernel_first, kernel_second, ok)
-    (*pieces, spatial_moved) = lax.optimization_barrier((*pieces, spatial_moved))
-    for step in reversed(range(1, col_devices)):
-        swaps = [(i, i ^ step) for i in range(col_devices)]
-        pieces[step] = lax.ppermute(pieces[step], "col", swaps)
-    grad_cols, strip_grad = grad_spectrum(col_norm, place, pieces, weight_out, table)
-    wide = pltpu.VMEM((strip * half // LANES, width, LANES), jnp.float32)
+
+    def dealt(pieces):
+        result = [pieces[0]]
+        for step in range(1, col_devices):
+            swaps = [(i, i ^ step) for i in range(col_devices)]
+            result.append(lax.ppermute(pieces[step], "col", swaps))
+        return result
+
+    inner = dealt(inner)
+    outer = sides(
+        place, features.shape, early_edge, late_edge, own, kernel_first, kernel_second, ok
+    )
+    *outer, spatial_moved = lax.optimization_barrier((*outer, spatial_moved))
+    outer = dealt(outer)
+
+    cell_count = height * owned
+    wide = [pltpu.VMEM((strip * half // LANES, width, LANES), jnp.float32)]
+    slope = vmem_call(
+        functools.partial(slope_kernel, row_norm, owned, devices),
+        [jax.ShapeDtypeStruct((2, cell_count, half), jnp.float32)],
+        spatial_moved,
+        weight_mix,
+        row_table,
+        scratch=wide,
+    )[0]
+    outer[0], slope = lax.optimization_barrier((outer[0], slope))
+    grad_cols, strip_grad = grad_spectrum(col_norm, place, inner, outer, weight_out, table)
     grad_rows = vmem_call(
         functools.partial(mix_kernel, row_norm, owned, devices),
         cells,
-        spatial_moved,
         swap(grad_cols),
+        slope,
         weight_mix,
         row_table,
         row_back,
-        scratch=[wide, wide],
+        scratch=wide,
     )[0]
     returned = swap(grad_rows)
     return vmem_call(

time: 94.3 us -> 89.6 us (0.950)
  waiting for transfers between devices: 8.13 us -> 1.34 us
  starting transfers between devices: 20.7 us -> 25 us
  blocking collectives: 38.1 us -> 35.8 us
    ppermute x3 -> x6, waiting for transfers between devices: 7.22 us -> 1.33 us  [dealt(): result.append(lax.ppermute(pieces[step], 'col', swaps))]
    ppermute x3 -> x6, starting transfers between devices: 5.16 us -> 9.49 us  [dealt(): result.append(lax.ppermute(pieces[step], 'col', swaps))]
    all_to_all x2, blocking collectives: 38.1 us -> 35.8 us  [swap(): lax.all_to_all(spectrum, ('col', 'row'), split_axis=0, concat_axis=0, til...]
    pallas_call x2 -> x3, Pallas kernels: 4.01 us -> 4.08 us  [vmem_call(): pl.pallas_call(body, out_shape=shapes, in_specs=[spec] * len(operands), o...]
  transfers between devices with their start and end apart: 10 -> 13, of which waited for: 4 -> 2; matrix products, arithmetic and copies ran while one was open for 0% -> 0% of each run, Pallas kernels for 22% -> 25%
where the time goes in v17:
time: 89.6 us; the launch traced here: 88.3 us
  blocking collectives  35.8 us (40%)
  Pallas kernels  25.7 us (29%)
  starting transfers between devices  25 us (28%)
  waiting for transfers between devices  1.34 us (1%)
    all_to_all x2, blocking collectives, swap(): lax.all_to_all(spectrum, ('col', 'row'), split_axis=0, concat_axis=0, til...  35.8 us
    ppermute x6, starting transfers between devices, dealt(): result.append(lax.ppermute(pieces[step], 'col', swaps))  9.49 us
    pallas_call x1, Pallas kernels, tile_forward(): pl.pallas_call(tile_forward_kernel, out_shape=shapes, in_specs=[pl.BlockS...  5.87 us
    all_to_all x1, starting transfers between devices, swap(): lax.all_to_all(spectrum, ('col', 'row'), split_axis=0, concat_axis=0, til...  5.12 us
    pallas_call x1, Pallas kernels, sides(): pl.pallas_call(side_kernel, out_shape=shapes, in_specs=[pl.BlockSpec(memo...  4.73 us
    ppermute x1, starting transfers between devices, shards(): late = lax.ppermute(features, 'row', pairs('row', 1))  4.5 us
    pallas_call x3, Pallas kernels, vmem_call(): pl.pallas_call(body, out_shape=shapes, in_specs=[spec] * len(operands), o...  4.08 us
    pallas_call x1, Pallas kernels, tile_backward(): pl.pallas_call(tile_backward_kernel, out_shape=shapes, in_specs=[pl.Block...  3.88 us
  transfers between devices with their start and end apart: 13, of which 2 were waited for; matrix products, arithmetic and copies ran while one was open for 0% of the time, Pallas kernels for 25%

profile of v17, /device:TPU:1, one launch (start us, length us, event | category | flops | bytes accessed | tf_op | source)
XLA Modules:
  0.0 88.3 jit_solution(15378244957866404587)
XLA Ops:
  0.0 4.5 %collective-permute-start.2 = (bf16[8,128,256]{2,1,0:T(8,128)(2,1)}, bf16[8,128,256]{2,1,0:T(8,128)(2,1)S(1)}, u32[]{:S(2)}, u32[]{:S(2)}) collective-permute-start(bf16[8,128,256]{2,1,0:T(8,128)(2,1)} %refs_7_.1), channel_id=1, source_target_pairs={{4,8},{12,16},{20,24},{8,4},{16,12},{24,20},{5,9},{13,17},{21,25},... | collective-permute-start | bytes 1572872 | tf_op jit(solution)/shard_map/ppermute | solution.py:700
  4.5 0.1 collective-permute-start.1
  4.6 1.1 %shard_map.136 = (bf16[528,256]{1,0:T(8,128)(2,1)S(1)}, bf16[528,256]{1,0:T(8,128)(2,1)S(1)}, bf16[1,128,256]{2,1,0:T(8,128)(2,1)S(1)}) custom-call(s32[1]{0:T(128)} %bitcast.col, s32[1]{0:T(128)} %bitcast.1.low, bf16[1024,256]{1,0:T(8,128)(2,1)} %bitcast.10, s32[8,128]{1,0:T(8,128)} %mask.1), custom_call_target="tpu_custom_call" | custom-call | bytes 1048576 | tf_op jit(solution)/shard_map/pallas_call | solution.py:260
  5.7 0.1 and_convert_fusion.ok
  5.8 0.5 collective-permute-start
  6.3 3.0 %collective-permute-start.3 = (bf16[528,256]{1,0:T(8,128)(2,1)S(1)}, bf16[528,256]{1,0:T(8,128)(2,1)S(1)}, u32[]{:S(2)}, u32[]{:S(2)}) collective-permute-start(bf16[528,256]{1,0:T(8,128)(2,1)S(1)} %get-tuple-element.49), channel_id=1, source_target_pairs={{4,8},{12,16},{20,24},{8,4},{16,12},{24,20},{5,9},{13,17},{21,25},... | collective-permute-start | bytes 811016 | tf_op jit(solution)/shard_map/ppermute | solution.py:704
  9.4 3.3 %shard_map.137 = bf16[512,384]{1,0:T(8,128)(2,1)} custom-call(bf16[2,512,512]{2,1,0:T(8,128)(2,1)} %signal, bf16[192,512]{1,0:T(8,128)(2,1)} %bitcast.15, bf16[512,512]{1,0:T(8,128)(2,1)} %constant.34.clone.table.refs_9_), custom_call_target="tpu_custom_call" | custom-call | bytes 2097152 | tf_op jit(solution)/shard_map/pallas_call | solution.py:125
  12.7 5.1 %all-to-all-start = ((bf16[32,16,384]{2,1,0:T(8,128)(2,1)}), bf16[32,16,384]{2,1,0:T(8,128)(2,1)S(1)}, u32[]{:S(2)}, u32[]{:S(2)}) async-start(bf16[32,16,384]{2,1,0:T(8,128)(2,1)} %bitcast.4), calls=%async_computation | async-start | bytes 786432 | tf_op jit(solution)/shard_map/all_to_all | solution.py:683
  17.8 1.7 %shard_map.138 = (bf16[3,3,256,256]{3,2,1,0:T(8,128)(2,1)S(1)}, bf16[3,3,256,256]{3,2,1,0:T(8,128)(2,1)S(1)}) custom-call(bf16[3,3,256,256]{3,2,1,0:T(8,128)(2,1)} %refs_0_, bf16[3,3,256,256]{3,2,1,0:T(8,128)(2,1)} %refs_1_.1), custom_call_target="tpu_custom_call" | custom-call | bytes 5242880 | tf_op jit(solution)/shard_map/pallas_call | solution.py:282
  19.6 0.0 copy-done.2
  19.6 5.9 %shard_map.139 = (f32[2048,256]{1,0:T(8,128)S(1)}, f32[1536,256]{1,0:T(8,128)S(1)}) custom-call(s32[1]{0:T(128)} %bitcast.col, s32[1]{0:T(128)} %bitcast.1.low, bf16[8,128,256]{2,1,0:T(8,128)(2,1)S(1)} %collective-permute-done.1.early.refs_0_.refs_5_, bf16[8,128,256]{2,1,0:T(8,128)(2,1)S(1)} %copy-done.2, ...), custom_call_target="tpu_custom_call" | custom-call | flops 5435817984 | bytes 8388608 | tf_op jit(solution)/shard_map/pallas_call | solution.py:583
  25.5 0.1 shard_map.141
  25.6 1.5 %collective-permute-start.7 = (bf16[43,8,256]{2,1,0:T(8,128)(2,1)S(1)}, bf16[43,8,256]{2,1,0:T(8,128)(2,1)S(1)}, u32[]{:S(2)}, u32[]{:S(2)}) collective-permute-start(bf16[43,8,256]{2,1,0:T(8,128)(2,1)S(1)} %get-tuple-element.55), channel_id=1, source_target_pairs={{0,1},{2,3},{1,0},{3,2},{4,5},{6,7},{5,4},{7,6},{8,9},{10,11},{9,8... | collective-permute-start | bytes 528392 | tf_op jit(solution)/shard_map/ppermute | solution.py:710
  27.1 0.8 collective-permute-start.8
  27.9 3.9 %shard_map.140 = (bf16[2,112,256]{2,1,0:T(8,128)(2,1)S(1)}, bf16[2,112,256]{2,1,0:T(8,128)(2,1)S(1)}, bf16[2,112,256]{2,1,0:T(8,128)(2,1)S(1)}, bf16[2,112,256]{2,1,0:T(8,128)(2,1)S(1)}) custom-call(s32[1]{0:T(128)} %bitcast.col, s32[1]{0:T(128)} %bitcast.1.low, f32[2048,256]{1,0:T(8,128)S(1)} %get-tuple-element.46.pre, ...), custom_call_target="tpu_custom_call" | custom-call | flops 3019898880 | bytes 8388608 | tf_op jit(solution)/shard_map/pallas_call | solution.py:607
  31.8 3.7 %collective-permute-start.4 = (bf16[2,112,256]{2,1,0:T(8,128)(2,1)S(1)}, bf16[2,112,256]{2,1,0:T(8,128)(2,1)S(1)}, u32[]{:S(2)}, u32[]{:S(2)}) collective-permute-start(bf16[2,112,256]{2,1,0:T(8,128)(2,1)S(1)} %get-tuple-element.52), channel_id=1, source_target_pairs={{0,1},{1,0},{2,3},{3,2},{4,5},{5,4},{6,7},{7,6},{8,9},{9,8},{10,11... | collective-permute-start | bytes 344072 | tf_op jit(solution)/shard_map/ppermute | solution.py:720
  35.5 2.2 %collective-permute-start.6 = (bf16[2,112,256]{2,1,0:T(8,128)(2,1)S(1)}, bf16[2,112,256]{2,1,0:T(8,128)(2,1)S(1)}, u32[]{:S(2)}, u32[]{:S(2)}) collective-permute-start(bf16[2,112,256]{2,1,0:T(8,128)(2,1)S(1)} %get-tuple-element.54), channel_id=1, source_target_pairs={{0,3},{1,2},{2,1},{3,0},{4,7},{5,6},{6,5},{7,4},{8,11},{9,10},{10,... | collective-permute-start | bytes 344072 | tf_op jit(solution)/shard_map/ppermute | solution.py:720
  37.7 0.0 copy-start.7
  37.7 4.7 %shard_map.142 = (bf16[2,16,256]{2,1,0:T(8,128)(2,1)S(1)}, bf16[2,16,256]{2,1,0:T(8,128)(2,1)S(1)}, bf16[2,16,256]{2,1,0:T(8,128)(2,1)S(1)}, bf16[2,16,256]{2,1,0:T(8,128)(2,1)S(1)}) custom-call(s32[1]{0:T(128)} %bitcast.col, s32[1]{0:T(128)} %bitcast.1.low, bf16[43,8,256]{2,1,0:T(8,128)(2,1)S(1)} %collective-permute-done.7.early, ...), custom_call_target="tpu_custom_call" | custom-call | flops 3170893824 | bytes 4194304 | tf_op jit(solution)/shard_map/pallas_call | solution.py:630
  42.5 0.0 copy-start.1
  42.5 0.6 collective-permute-start.9
  43.1 0.9 %collective-permute-start.10 = (bf16[2,16,256]{2,1,0:T(8,128)(2,1)S(1)}, bf16[2,16,256]{2,1,0:T(8,128)(2,1)S(1)}, u32[]{:S(2)}, u32[]{:S(2)}) collective-permute-start(bf16[2,16,256]{2,1,0:T(8,128)(2,1)S(1)} %get-tuple-element.66), channel_id=1, source_target_pairs={{0,2},{1,3},{2,0},{3,1},{4,6},{5,7},{6,4},{7,5},{8,10},{9,11},{10,... | collective-permute-start | bytes 49160 | tf_op jit(solution)/shard_map/ppermute | solution.py:720
  44.0 2.2 %collective-permute-start.11 = (bf16[2,16,256]{2,1,0:T(8,128)(2,1)S(1)}, bf16[2,16,256]{2,1,0:T(8,128)(2,1)S(1)}, u32[]{:S(2)}, u32[]{:S(2)}) collective-permute-start(bf16[2,16,256]{2,1,0:T(8,128)(2,1)S(1)} %get-tuple-element.67), channel_id=1, source_target_pairs={{0,3},{1,2},{2,1},{3,0},{4,7},{5,6},{6,5},{7,4},{8,11},{9,10},{10,... | collective-permute-start | bytes 49160 | tf_op jit(solution)/shard_map/ppermute | solution.py:720
  46.1 1.0 %shard_map.143.slope = f32[2,512,192]{2,1,0:T(8,128)S(1)} custom-call(bf16[512,384]{1,0:T(8,128)(2,1)S(1)} %bitcast.11, bf16[384,384]{1,0:T(8,128)(2,1)S(1)} %copy-done.3, bf16[128,128]{1,0:T(8,128)(2,1)S(1)} %copy-done.7), custom_call_target="tpu_custom_call" | custom-call | bytes 1507328 | tf_op jit(solution)/shard_map/pallas_call | solution.py:30
  47.1 0.0 copy-start.9
  47.1 1.1 %collective-permute-done.10.refs_6_ = bf16[2,16,256]{2,1,0:T(8,128)(2,1)S(1)} collective-permute-done((bf16[2,16,256]{2,1,0:T(8,128)(2,1)S(1)}, bf16[2,16,256]{2,1,0:T(8,128)(2,1)S(1)}, u32[]{:S(2)}, u32[]{:S(2)}) %collective-permute-start.10) | collective-permute-done | bytes 16416 | tf_op jit(solution)/shard_map/ppermute | solution.py:720
  48.3 0.2 collective-permute-done.11.refs_7_
  48.5 0.9 shard_map.144
  49.3 20.2 %all_to_all.34 = bf16[32,16,384]{2,1,0:T(8,128)(2,1)S(1)} all-to-all(bf16[32,16,384]{2,1,0:T(8,128)(2,1)S(1)} %bitcast.17), channel_id=1, replica_groups=mesh['row'=8,'col'=4] {'col','row'}, dimensions={0} | all-to-all | bytes 786432 | tf_op jit(solution)/shard_map/all_to_all | solution.py:683
  69.5 1.2 %shard_map.145 = bf16[512,384]{1,0:T(8,128)(2,1)S(1)} custom-call(bf16[512,384]{1,0:T(8,128)(2,1)S(1)} %bitcast.12, f32[2,512,192]{2,1,0:T(8,128)S(1)} %shard_map.143.slope, bf16[384,384]{1,0:T(8,128)(2,1)S(1)} %copy-done.3, bf16[128,128]{1,0:T(8,128)(2,1)S(1)} %copy-done.7, bf16[128,128]{1,0:T(8,128)(2,1)S(1)} %copy-done.9), custom_call_target="tpu_custom_call" | custom-call | bytes 1933312 | tf_op jit(solution)/shard_map/pallas_call | solution.py:30
  70.7 15.6 %all_to_all.35 = bf16[32,16,384]{2,1,0:T(8,128)(2,1)S(1)} all-to-all(bf16[32,16,384]{2,1,0:T(8,128)(2,1)S(1)} %bitcast.13), channel_id=1, replica_groups=mesh['row'=8,'col'=4] {'col','row'}, dimensions={0} | all-to-all | bytes 786432 | tf_op jit(solution)/shard_map/all_to_all | solution.py:683
  86.3 2.0 %shard_map.146 = bf16[2,512,512]{2,1,0:T(8,128)(2,1)} custom-call(bf16[512,384]{1,0:T(8,128)(2,1)S(1)} %bitcast.14, bf16[4,2,128,256]{3,2,1,0:T(8,128)(2,1)S(1)} %get-tuple-element.70.strip_grad, bf16[192,512]{1,0:T(8,128)(2,1)S(1)} %bitcast.16, bf16[512,256]{1,0:T(8,128)(2,1)S(1)} %copy-done.6, bf16[512,512]{1,0:T(8,128)(2,1)S(1)} %copy-done.5), custom_call_target="tpu_custom_call" | custom-call | bytes 2949120 | tf_op jit(solution)/shard_map/pallas_call | solution.py:30
  (30 shorter events, 0.1 us)
Async XLA Ops:
  0.0 19.5 %collective-permute-start.2 = (bf16[8,128,256]{2,1,0:T(8,128)(2,1)}, bf16[8,128,256]{2,1,0:T(8,128)(2,1)S(1)}, u32[]{:S(2)}, u32[]{:S(2)}) collective-permute-start(bf16[8,128,256]{2,1,0:T(8,128)(2,1)} %refs_7_.1), channel_id=1, source_target_pairs={{4,8},{12,16},{20,24},{8,4},{16,12},{24,20},{5,9},{13,17},{21,25},... | collective-permute-start | bytes 1572872 | tf_op jit(solution)/shard_map/ppermute | solution.py:700
  4.5 15.1 %collective-permute-start.1 = (bf16[8,128,256]{2,1,0:T(8,128)(2,1)}, bf16[8,128,256]{2,1,0:T(8,128)(2,1)S(1)}, u32[]{:S(2)}, u32[]{:S(2)}) collective-permute-start(bf16[8,128,256]{2,1,0:T(8,128)(2,1)} %refs_7_.1), channel_id=1, source_target_pairs={{0,4},{8,12},{16,20},{24,28},{4,0},{12,8},{20,16},{28,24},{1,5},{9... | collective-permute-start | bytes 1572872 | tf_op jit(solution)/shard_map/ppermute | solution.py:699
  5.8 19.7 %collective-permute-start = (bf16[528,256]{1,0:T(8,128)(2,1)S(1)}, bf16[528,256]{1,0:T(8,128)(2,1)S(1)}, u32[]{:S(2)}, u32[]{:S(2)}) collective-permute-start(bf16[528,256]{1,0:T(8,128)(2,1)S(1)} %get-tuple-element.39), channel_id=1, source_target_pairs={{0,4},{8,12},{16,20},{24,28},{4,0},{12,8},{20,16},{28,24},{1,5},{9... | collective-permute-start | bytes 811016 | tf_op jit(solution)/shard_map/ppermute | solution.py:703
  6.3 19.1 %collective-permute-start.3 = (bf16[528,256]{1,0:T(8,128)(2,1)S(1)}, bf16[528,256]{1,0:T(8,128)(2,1)S(1)}, u32[]{:S(2)}, u32[]{:S(2)}) collective-permute-start(bf16[528,256]{1,0:T(8,128)(2,1)S(1)} %get-tuple-element.49), channel_id=1, source_target_pairs={{4,8},{12,16},{20,24},{8,4},{16,12},{24,20},{5,9},{13,17},{21,25},... | collective-permute-start | bytes 811016 | tf_op jit(solution)/shard_map/ppermute | solution.py:704
  12.7 29.8 %all-to-all-start = ((bf16[32,16,384]{2,1,0:T(8,128)(2,1)}), bf16[32,16,384]{2,1,0:T(8,128)(2,1)S(1)}, u32[]{:S(2)}, u32[]{:S(2)}) async-start(bf16[32,16,384]{2,1,0:T(8,128)(2,1)} %bitcast.4), calls=%async_computation | async-start | bytes 786432 | tf_op jit(solution)/shard_map/all_to_all | solution.py:683
  17.8 1.8 %copy-start.2 = (bf16[8,128,256]{2,1,0:T(8,128)(2,1)S(1)}, bf16[8,128,256]{2,1,0:T(8,128)(2,1)}, u32[]{:S(2)}) copy-start(bf16[8,128,256]{2,1,0:T(8,128)(2,1)} %refs_7_.1) | copy-start | bytes 1572868
  19.6 5.9 %copy-start = (bf16[8,128,256]{2,1,0:T(8,128)(2,1)S(1)}, bf16[8,128,256]{2,1,0:T(8,128)(2,1)}, u32[]{:S(2)}) copy-start(bf16[8,128,256]{2,1,0:T(8,128)(2,1)} %refs_8_.2) | copy-start | bytes 1572868
  25.6 12.1 %collective-permute-start.7 = (bf16[43,8,256]{2,1,0:T(8,128)(2,1)S(1)}, bf16[43,8,256]{2,1,0:T(8,128)(2,1)S(1)}, u32[]{:S(2)}, u32[]{:S(2)}) collective-permute-start(bf16[43,8,256]{2,1,0:T(8,128)(2,1)S(1)} %get-tuple-element.55), channel_id=1, source_target_pairs={{0,1},{2,3},{1,0},{3,2},{4,5},{6,7},{5,4},{7,6},{8,9},{10,11},{9,8... | collective-permute-start | bytes 528392 | tf_op jit(solution)/shard_map/ppermute | solution.py:710
  27.1 10.6 %collective-permute-start.8 = (bf16[43,8,256]{2,1,0:T(8,128)(2,1)S(1)}, bf16[43,8,256]{2,1,0:T(8,128)(2,1)S(1)}, u32[]{:S(2)}, u32[]{:S(2)}) collective-permute-start(bf16[43,8,256]{2,1,0:T(8,128)(2,1)S(1)} %get-tuple-element.56), channel_id=1, source_target_pairs={{1,2},{2,1},{5,6},{6,5},{9,10},{10,9},{13,14},{14,13},{17,18},{18,... | collective-permute-start | bytes 528392 | tf_op jit(solution)/shard_map/ppermute | solution.py:711
  31.8 12.1 %collective-permute-start.4 = (bf16[2,112,256]{2,1,0:T(8,128)(2,1)S(1)}, bf16[2,112,256]{2,1,0:T(8,128)(2,1)S(1)}, u32[]{:S(2)}, u32[]{:S(2)}) collective-permute-start(bf16[2,112,256]{2,1,0:T(8,128)(2,1)S(1)} %get-tuple-element.52), channel_id=1, source_target_pairs={{0,1},{1,0},{2,3},{3,2},{4,5},{5,4},{6,7},{7,6},{8,9},{9,8},{10,11... | collective-permute-start | bytes 344072 | tf_op jit(solution)/shard_map/ppermute | solution.py:720
  35.5 11.6 %collective-permute-start.5 = (bf16[2,112,256]{2,1,0:T(8,128)(2,1)S(1)}, bf16[2,112,256]{2,1,0:T(8,128)(2,1)S(1)}, u32[]{:S(2)}, u32[]{:S(2)}) collective-permute-start(bf16[2,112,256]{2,1,0:T(8,128)(2,1)S(1)} %get-tuple-element.53), channel_id=1, source_target_pairs={{0,2},{1,3},{2,0},{3,1},{4,6},{5,7},{6,4},{7,5},{8,10},{9,11},{10,... | collective-permute-start | bytes 344072 | tf_op jit(solution)/shard_map/ppermute | solution.py:720
  35.5 11.6 %collective-permute-start.6 = (bf16[2,112,256]{2,1,0:T(8,128)(2,1)S(1)}, bf16[2,112,256]{2,1,0:T(8,128)(2,1)S(1)}, u32[]{:S(2)}, u32[]{:S(2)}) collective-permute-start(bf16[2,112,256]{2,1,0:T(8,128)(2,1)S(1)} %get-tuple-element.54), channel_id=1, source_target_pairs={{0,3},{1,2},{2,1},{3,0},{4,7},{5,6},{6,5},{7,4},{8,11},{9,10},{10,... | collective-permute-start | bytes 344072 | tf_op jit(solution)/shard_map/ppermute | solution.py:720
  37.7 8.4 %copy-start.3 = (bf16[384,384]{1,0:T(8,128)(2,1)S(1)}, bf16[384,384]{1,0:T(8,128)(2,1)}, u32[]{:S(2)}) copy-start(bf16[384,384]{1,0:T(8,128)(2,1)} %mix.3) | copy-start | bytes 884740
  37.7 8.4 %copy-start.7 = (bf16[128,128]{1,0:T(8,128)(2,1)S(1)}, bf16[128,128]{1,0:T(8,128)(2,1)}, u32[]{:S(2)}) copy-start(bf16[128,128]{1,0:T(8,128)(2,1)} %constant.36.clone.table) | copy-start | bytes 98308
  42.5 6.0 %copy-start.1 = (bf16[512,512]{1,0:T(8,128)(2,1)S(1)}, bf16[512,512]{1,0:T(8,128)(2,1)}, u32[]{:S(2)}) copy-start(bf16[512,512]{1,0:T(8,128)(2,1)} %constant.34.clone.table.refs_9_) | copy-start | bytes 1572868
  42.5 6.0 %copy-start.8 = (bf16[192,256]{1,0:T(8,128)(2,1)S(1)}, bf16[192,256]{1,0:T(8,128)(2,1)}, u32[]{:S(2)}) copy-start(bf16[192,256]{1,0:T(8,128)(2,1)} %refs_8_.3) | copy-start | bytes 294916
  42.5 4.6 %collective-permute-start.9 = (bf16[2,16,256]{2,1,0:T(8,128)(2,1)S(1)}, bf16[2,16,256]{2,1,0:T(8,128)(2,1)S(1)}, u32[]{:S(2)}, u32[]{:S(2)}) collective-permute-start(bf16[2,16,256]{2,1,0:T(8,128)(2,1)S(1)} %get-tuple-element.65), channel_id=1, source_target_pairs={{0,1},{1,0},{2,3},{3,2},{4,5},{5,4},{6,7},{7,6},{8,9},{9,8},{10,11... | collective-permute-start | bytes 49160 | tf_op jit(solution)/shard_map/ppermute | solution.py:720
  43.1 5.2 %collective-permute-start.10 = (bf16[2,16,256]{2,1,0:T(8,128)(2,1)S(1)}, bf16[2,16,256]{2,1,0:T(8,128)(2,1)S(1)}, u32[]{:S(2)}, u32[]{:S(2)}) collective-permute-start(bf16[2,16,256]{2,1,0:T(8,128)(2,1)S(1)} %get-tuple-element.66), channel_id=1, source_target_pairs={{0,2},{1,3},{2,0},{3,1},{4,6},{5,7},{6,4},{7,5},{8,10},{9,11},{10,... | collective-permute-start | bytes 49160 | tf_op jit(solution)/shard_map/ppermute | solution.py:720
  44.0 4.5 %collective-permute-start.11 = (bf16[2,16,256]{2,1,0:T(8,128)(2,1)S(1)}, bf16[2,16,256]{2,1,0:T(8,128)(2,1)S(1)}, u32[]{:S(2)}, u32[]{:S(2)}) collective-permute-start(bf16[2,16,256]{2,1,0:T(8,128)(2,1)S(1)} %get-tuple-element.67), channel_id=1, source_target_pairs={{0,3},{1,2},{2,1},{3,0},{4,7},{5,6},{6,5},{7,4},{8,11},{9,10},{10,... | collective-permute-start | bytes 49160 | tf_op jit(solution)/shard_map/ppermute | solution.py:720
  47.1 22.4 %copy-start.9 = (bf16[128,128]{1,0:T(8,128)(2,1)S(1)}, bf16[128,128]{1,0:T(8,128)(2,1)}, u32[]{:S(2)}) copy-start(bf16[128,128]{1,0:T(8,128)(2,1)} %constant.35.clone.back_table) | copy-start | bytes 98308
  69.5 16.8 %copy-start.4 = (bf16[512,192]{0,1:T(8,128)(2,1)S(1)}, bf16[512,192]{0,1:T(8,128)(2,1)}, u32[]{:S(2)}) copy-start(bf16[512,192]{0,1:T(8,128)(2,1)} %param.20) | copy-start | bytes 589828
  69.5 16.8 %copy-start.5 = (bf16[512,512]{1,0:T(8,128)(2,1)S(1)}, bf16[512,512]{1,0:T(8,128)(2,1)}, u32[]{:S(2)}) copy-start(bf16[512,512]{1,0:T(8,128)(2,1)} %constant.33.clone.table) | copy-start | bytes 1572868
  69.5 16.8 %copy-start.6 = (bf16[512,256]{1,0:T(8,128)(2,1)S(1)}, bf16[512,256]{1,0:T(8,128)(2,1)}, u32[]{:S(2)}) copy-start(bf16[512,256]{1,0:T(8,128)(2,1)} %weight_local.1) | copy-start | bytes 786436

commit v18 on v17

--- a/solution.py
+++ b/solution.py
@@ -73,7 +73,7 @@
     *pieces, weight, table, out, strip_out, projected = refs
     count = len(pieces) // 2
     _, strip, tile_cols, _ = strip_out.shape
-    for step, (inner, outer) in enumerate(zip(pieces[:count], pieces[count:])):
+    for step, inner, outer in zip(steps_of(count), pieces[:count], pieces[count:]):
         block = col[0] ^ step
         strip_out[block, :, REACH : tile_cols - REACH] = inner[...]
         strip_out[block, :, :REACH] = outer[:, :REACH]
@@ -194,13 +194,30 @@
         out[:, g * LANES : (g + 1) * LANES] = wide[g].astype(jnp.bfloat16)
 
 
-def output_kernel(norm, moved, strip_grad, weight_in, weight_local, table, out):
+def output_kernel(norm, moved, strip_grad, weight_in, weight_local, table, out, held, sems):
     spatial = (dot(table[...], moved[...]) * norm).astype(jnp.bfloat16)
     half = weight_in.shape[0]
+    copies = []
     for r in range(out.shape[0]):
         total = dot(spatial[:, r * half : (r + 1) * half], weight_in[...])
         total = total + dot_t(strip_row(strip_grad, r), weight_local[...])
-        out[r] = total.astype(jnp.bfloat16)
+        held[r] = total.astype(jnp.bfloat16)
+        copies.append(pltpu.make_async_copy(held.at[r], out.at[r], sems.at[r]))
+        copies[-1].start()
+    for copy in copies:
+        copy.wait()
+
+
+def output(norm, shape, *operands):
+    return pl.pallas_call(
+        functools.partial(output_kernel, norm),
+        out_shape=jax.ShapeDtypeStruct(shape, jnp.bfloat16),
+        in_specs=[pl.BlockSpec(memory_space=pltpu.VMEM)] * len(operands),
+        out_specs=pl.BlockSpec(memory_space=pltpu.HBM),
+        scratch_shapes=[pltpu.VMEM(shape, jnp.bfloat16), pltpu.SemaphoreType.DMA((shape[0],))],
+        compiler_params=pltpu.CompilerParams(vmem_limit_bytes=10 * MIB),
+        cost_estimate=pl.CostEstimate(flops=0, bytes_accessed=3 * MIB, transcendentals=0),
+    )(*operands)
 
 
 TAIL = 16
@@ -417,8 +434,12 @@
         use(row, count, conv_adjoint(wide_odd, row, count, stride, first))
 
 
+def steps_of(count):
+    return [0, *range(2, count), 1] if count > 1 else [0]
+
+
 def deal(place, out, pieces):
-    for step, piece in enumerate(pieces):
+    for step, piece in zip(steps_of(len(pieces)), pieces):
         piece[...] = out[pl.ds((place[0] ^ step) * piece.shape[0], piece.shape[0])]
 
 
@@ -714,10 +735,10 @@
     )
 
     def dealt(pieces):
-        result = [pieces[0]]
-        for step in range(1, col_devices):
+        result = []
+        for piece, step in zip(pieces, steps_of(col_devices)):
             swaps = [(i, i ^ step) for i in range(col_devices)]
-            result.append(lax.ppermute(pieces[step], "col", swaps))
+            result.append(lax.ppermute(piece, "col", swaps) if step else piece)
         return result
 
     inner = dealt(inner)
@@ -750,15 +771,7 @@
         scratch=wide,
     )[0]
     returned = swap(grad_rows)
-    return vmem_call(
-        functools.partial(output_kernel, col_norm),
-        [jax.ShapeDtypeStruct(inputs.shape, bf16)],
-        returned,
-        strip_grad,
-        weight_in,
-        weight_local,
-        table_back,
-    )[0]
+    return output(col_norm, inputs.shape, returned, strip_grad, weight_in, weight_local, table_back)
 
 
 def solution(mesh):

time: 89.6 us -> 89.5 us (level)
    pallas_call x3 -> x2, Pallas kernels: 4.08 us -> 2.13 us  [vmem_call(): pl.pallas_call(body, out_shape=shapes, in_specs=[spec] * len(operands), o...]
    pallas_call x0 -> x1, Pallas kernels: none -> 1.8 us  [output(): pl.pallas_call(functools.partial(output_kernel, norm), out_shape=jax.Shap...]
where the time goes in v18:
time: 89.5 us; the launch traced here: 88.2 us
  blocking collectives  35.5 us (40%)
  Pallas kernels  25.5 us (28%)
  starting transfers between devices  25 us (28%)
  waiting for transfers between devices  1.59 us (2%)
    all_to_all x2, blocking collectives, swap(): lax.all_to_all(spectrum, ('col', 'row'), split_axis=0, concat_axis=0, til...  35.5 us
    ppermute x6, starting transfers between devices, dealt(): result.append(lax.ppermute(piece, 'col', swaps) if step else piece)  9.43 us
    pallas_call x1, Pallas kernels, tile_forward(): pl.pallas_call(tile_forward_kernel, out_shape=shapes, in_specs=[pl.BlockS...  5.87 us
    all_to_all x1, starting transfers between devices, swap(): lax.all_to_all(spectrum, ('col', 'row'), split_axis=0, concat_axis=0, til...  5.12 us
    pallas_call x1, Pallas kernels, sides(): pl.pallas_call(side_kernel, out_shape=shapes, in_specs=[pl.BlockSpec(memo...  4.71 us
    ppermute x1, starting transfers between devices, shards(): late = lax.ppermute(features, 'row', pairs('row', 1))  4.5 us
    pallas_call x1, Pallas kernels, tile_backward(): pl.pallas_call(tile_backward_kernel, out_shape=shapes, in_specs=[pl.Block...  3.88 us
    pallas_call x1, Pallas kernels, fetching_spectrum(): pl.pallas_call(functools.partial(fetching_spectrum_kernel, norm), out_sha...  3.31 us
  transfers between devices with their start and end apart: 13, of which 2 were waited for; matrix products, arithmetic and copies ran while one was open for 0% of the time, Pallas kernels for 25%

profile of v18, /device:TPU:1, one launch (start us, length us, event | category | flops | bytes accessed | tf_op | source)
XLA Modules:
  0.0 88.2 jit_solution(5368043486213020311)
XLA Ops:
  0.0 4.5 %collective-permute-start.2 = (bf16[8,128,256]{2,1,0:T(8,128)(2,1)}, bf16[8,128,256]{2,1,0:T(8,128)(2,1)S(1)}, u32[]{:S(2)}, u32[]{:S(2)}) collective-permute-start(bf16[8,128,256]{2,1,0:T(8,128)(2,1)} %refs_7_.1), channel_id=1, source_target_pairs={{4,8},{12,16},{20,24},{8,4},{16,12},{24,20},{5,9},{13,17},{21,25},... | collective-permute-start | bytes 1572872 | tf_op jit(solution)/shard_map/ppermute | solution.py:721
  4.5 0.1 collective-permute-start.1
  4.6 1.1 %shard_map.136 = (bf16[528,256]{1,0:T(8,128)(2,1)S(1)}, bf16[528,256]{1,0:T(8,128)(2,1)S(1)}, bf16[1,128,256]{2,1,0:T(8,128)(2,1)S(1)}) custom-call(s32[1]{0:T(128)} %bitcast.col, s32[1]{0:T(128)} %bitcast.1.low, bf16[1024,256]{1,0:T(8,128)(2,1)} %bitcast.10, s32[8,128]{1,0:T(8,128)} %mask.1), custom_call_target="tpu_custom_call" | custom-call | bytes 1048576 | tf_op jit(solution)/shard_map/pallas_call | solution.py:277
  5.7 0.1 and_convert_fusion.ok
  5.8 0.5 collective-permute-start
  6.3 3.0 %collective-permute-start.3 = (bf16[528,256]{1,0:T(8,128)(2,1)S(1)}, bf16[528,256]{1,0:T(8,128)(2,1)S(1)}, u32[]{:S(2)}, u32[]{:S(2)}) collective-permute-start(bf16[528,256]{1,0:T(8,128)(2,1)S(1)} %get-tuple-element.49), channel_id=1, source_target_pairs={{4,8},{12,16},{20,24},{8,4},{16,12},{24,20},{5,9},{13,17},{21,25},... | collective-permute-start | bytes 811016 | tf_op jit(solution)/shard_map/ppermute | solution.py:725
  9.4 3.3 %shard_map.137 = bf16[512,384]{1,0:T(8,128)(2,1)} custom-call(bf16[2,512,512]{2,1,0:T(8,128)(2,1)} %signal, bf16[192,512]{1,0:T(8,128)(2,1)} %bitcast.15, bf16[512,512]{1,0:T(8,128)(2,1)} %constant.34.clone.table.refs_9_), custom_call_target="tpu_custom_call" | custom-call | bytes 2097152 | tf_op jit(solution)/shard_map/pallas_call | solution.py:125
  12.7 5.1 %all-to-all-start = ((bf16[32,16,384]{2,1,0:T(8,128)(2,1)}), bf16[32,16,384]{2,1,0:T(8,128)(2,1)S(1)}, u32[]{:S(2)}, u32[]{:S(2)}) async-start(bf16[32,16,384]{2,1,0:T(8,128)(2,1)} %bitcast.4), calls=%async_computation | async-start | bytes 786432 | tf_op jit(solution)/shard_map/all_to_all | solution.py:704
  17.8 0.0 copy-start.2
  17.8 1.7 %shard_map.138 = (bf16[3,3,256,256]{3,2,1,0:T(8,128)(2,1)S(1)}, bf16[3,3,256,256]{3,2,1,0:T(8,128)(2,1)S(1)}) custom-call(bf16[3,3,256,256]{3,2,1,0:T(8,128)(2,1)} %refs_0_, bf16[3,3,256,256]{3,2,1,0:T(8,128)(2,1)} %refs_1_.1), custom_call_target="tpu_custom_call" | custom-call | bytes 5242880 | tf_op jit(solution)/shard_map/pallas_call | solution.py:299
  19.6 0.0 copy-done.2
  19.6 5.9 %shard_map.139 = (f32[2048,256]{1,0:T(8,128)S(1)}, f32[1536,256]{1,0:T(8,128)S(1)}) custom-call(s32[1]{0:T(128)} %bitcast.col, s32[1]{0:T(128)} %bitcast.1.low, bf16[8,128,256]{2,1,0:T(8,128)(2,1)S(1)} %collective-permute-done.1.early.refs_0_.refs_5_, bf16[8,128,256]{2,1,0:T(8,128)(2,1)S(1)} %copy-done.2, ...), custom_call_target="tpu_custom_call" | custom-call | flops 5435817984 | bytes 8388608 | tf_op jit(solution)/shard_map/pallas_call | solution.py:604
  25.5 0.1 shard_map.141
  25.6 1.5 %collective-permute-start.7 = (bf16[43,8,256]{2,1,0:T(8,128)(2,1)S(1)}, bf16[43,8,256]{2,1,0:T(8,128)(2,1)S(1)}, u32[]{:S(2)}, u32[]{:S(2)}) collective-permute-start(bf16[43,8,256]{2,1,0:T(8,128)(2,1)S(1)} %get-tuple-element.55), channel_id=1, source_target_pairs={{0,1},{2,3},{1,0},{3,2},{4,5},{6,7},{5,4},{7,6},{8,9},{10,11},{9,8... | collective-permute-start | bytes 528392 | tf_op jit(solution)/shard_map/ppermute | solution.py:731
  27.1 0.8 collective-permute-start.8
  27.9 3.9 %shard_map.140 = (bf16[2,112,256]{2,1,0:T(8,128)(2,1)S(1)}, bf16[2,112,256]{2,1,0:T(8,128)(2,1)S(1)}, bf16[2,112,256]{2,1,0:T(8,128)(2,1)S(1)}, bf16[2,112,256]{2,1,0:T(8,128)(2,1)S(1)}) custom-call(s32[1]{0:T(128)} %bitcast.col, s32[1]{0:T(128)} %bitcast.1.low, f32[2048,256]{1,0:T(8,128)S(1)} %get-tuple-element.46.pre, ...), custom_call_target="tpu_custom_call" | custom-call | flops 3019898880 | bytes 8388608 | tf_op jit(solution)/shard_map/pallas_call | solution.py:628
  31.8 3.4 %collective-permute-start.4 = (bf16[2,112,256]{2,1,0:T(8,128)(2,1)S(1)}, bf16[2,112,256]{2,1,0:T(8,128)(2,1)S(1)}, u32[]{:S(2)}, u32[]{:S(2)}) collective-permute-start(bf16[2,112,256]{2,1,0:T(8,128)(2,1)S(1)} %get-tuple-element.52), channel_id=1, source_target_pairs={{0,2},{1,3},{2,0},{3,1},{4,6},{5,7},{6,4},{7,5},{8,10},{9,11},{10,... | collective-permute-start | bytes 344072 | tf_op jit(solution)/shard_map/ppermute | solution.py:741
  35.3 2.4 %collective-permute-start.5 = (bf16[2,112,256]{2,1,0:T(8,128)(2,1)S(1)}, bf16[2,112,256]{2,1,0:T(8,128)(2,1)S(1)}, u32[]{:S(2)}, u32[]{:S(2)}) collective-permute-start(bf16[2,112,256]{2,1,0:T(8,128)(2,1)S(1)} %get-tuple-element.53), channel_id=1, source_target_pairs={{0,3},{1,2},{2,1},{3,0},{4,7},{5,6},{6,5},{7,4},{8,11},{9,10},{10,... | collective-permute-start | bytes 344072 | tf_op jit(solution)/shard_map/ppermute | solution.py:741
  37.6 0.0 copy-start.7
  37.7 4.7 %shard_map.142 = (bf16[2,16,256]{2,1,0:T(8,128)(2,1)S(1)}, bf16[2,16,256]{2,1,0:T(8,128)(2,1)S(1)}, bf16[2,16,256]{2,1,0:T(8,128)(2,1)S(1)}, bf16[2,16,256]{2,1,0:T(8,128)(2,1)S(1)}) custom-call(s32[1]{0:T(128)} %bitcast.col, s32[1]{0:T(128)} %bitcast.1.low, bf16[43,8,256]{2,1,0:T(8,128)(2,1)S(1)} %collective-permute-done.7.early, ...), custom_call_target="tpu_custom_call" | custom-call | flops 3170893824 | bytes 4194304 | tf_op jit(solution)/shard_map/pallas_call | solution.py:651
  42.4 0.0 copy-start.1
  42.4 1.3 %collective-permute-start.9 = (bf16[2,16,256]{2,1,0:T(8,128)(2,1)S(1)}, bf16[2,16,256]{2,1,0:T(8,128)(2,1)S(1)}, u32[]{:S(2)}, u32[]{:S(2)}) collective-permute-start(bf16[2,16,256]{2,1,0:T(8,128)(2,1)S(1)} %get-tuple-element.65), channel_id=1, source_target_pairs={{0,2},{1,3},{2,0},{3,1},{4,6},{5,7},{6,4},{7,5},{8,10},{9,11},{10,... | collective-permute-start | bytes 49160 | tf_op jit(solution)/shard_map/ppermute | solution.py:741
  43.7 2.3 %collective-permute-start.10 = (bf16[2,16,256]{2,1,0:T(8,128)(2,1)S(1)}, bf16[2,16,256]{2,1,0:T(8,128)(2,1)S(1)}, u32[]{:S(2)}, u32[]{:S(2)}) collective-permute-start(bf16[2,16,256]{2,1,0:T(8,128)(2,1)S(1)} %get-tuple-element.66), channel_id=1, source_target_pairs={{0,3},{1,2},{2,1},{3,0},{4,7},{5,6},{6,5},{7,4},{8,11},{9,10},{10,... | collective-permute-start | bytes 49160 | tf_op jit(solution)/shard_map/ppermute | solution.py:741
  46.1 1.0 %shard_map.143.slope = f32[2,512,192]{2,1,0:T(8,128)S(1)} custom-call(bf16[512,384]{1,0:T(8,128)(2,1)S(1)} %bitcast.11, bf16[384,384]{1,0:T(8,128)(2,1)S(1)} %copy-done.3, bf16[128,128]{1,0:T(8,128)(2,1)S(1)} %copy-done.7), custom_call_target="tpu_custom_call" | custom-call | bytes 1507328 | tf_op jit(solution)/shard_map/pallas_call | solution.py:30
  47.0 0.0 copy-start.9
  47.1 1.0 %collective-permute-done.10.refs_6_ = bf16[2,16,256]{2,1,0:T(8,128)(2,1)S(1)} collective-permute-done((bf16[2,16,256]{2,1,0:T(8,128)(2,1)S(1)}, bf16[2,16,256]{2,1,0:T(8,128)(2,1)S(1)}, u32[]{:S(2)}, u32[]{:S(2)}) %collective-permute-start.10) | collective-permute-done | bytes 16416 | tf_op jit(solution)/shard_map/ppermute | solution.py:741
  48.1 0.5 collective-permute-done.11.refs_7_
  48.6 0.9 shard_map.144
  49.5 19.9 %all_to_all.34 = bf16[32,16,384]{2,1,0:T(8,128)(2,1)S(1)} all-to-all(bf16[32,16,384]{2,1,0:T(8,128)(2,1)S(1)} %bitcast.17), channel_id=1, replica_groups=mesh['row'=8,'col'=4] {'col','row'}, dimensions={0} | all-to-all | bytes 786432 | tf_op jit(solution)/shard_map/all_to_all | solution.py:704
  69.4 1.2 %shard_map.145 = bf16[512,384]{1,0:T(8,128)(2,1)S(1)} custom-call(bf16[512,384]{1,0:T(8,128)(2,1)S(1)} %bitcast.12, f32[2,512,192]{2,1,0:T(8,128)S(1)} %shard_map.143.slope, bf16[384,384]{1,0:T(8,128)(2,1)S(1)} %copy-done.3, bf16[128,128]{1,0:T(8,128)(2,1)S(1)} %copy-done.7, bf16[128,128]{1,0:T(8,128)(2,1)S(1)} %copy-done.9), custom_call_target="tpu_custom_call" | custom-call | bytes 1933312 | tf_op jit(solution)/shard_map/pallas_call | solution.py:30
  70.6 15.6 %all_to_all.35 = bf16[32,16,384]{2,1,0:T(8,128)(2,1)S(1)} all-to-all(bf16[32,16,384]{2,1,0:T(8,128)(2,1)S(1)} %bitcast.13), channel_id=1, replica_groups=mesh['row'=8,'col'=4] {'col','row'}, dimensions={0} | all-to-all | bytes 786432 | tf_op jit(solution)/shard_map/all_to_all | solution.py:704
  86.3 1.8 %shard_map.146 = bf16[2,512,512]{2,1,0:T(8,128)(2,1)} custom-call(bf16[512,384]{1,0:T(8,128)(2,1)S(1)} %bitcast.14, bf16[4,2,128,256]{3,2,1,0:T(8,128)(2,1)S(1)} %get-tuple-element.70.strip_grad, bf16[192,512]{1,0:T(8,128)(2,1)S(1)} %bitcast.16, bf16[512,256]{1,0:T(8,128)(2,1)S(1)} %copy-done.6, bf16[512,512]{1,0:T(8,128)(2,1)S(1)} %copy-done.5), custom_call_target="tpu_custom_call" | custom-call | bytes 3145728 | tf_op jit(solution)/shard_map/pallas_call | solution.py:212
  (30 shorter events, 0.1 us)
Async XLA Ops:
  0.0 19.5 %collective-permute-start.2 = (bf16[8,128,256]{2,1,0:T(8,128)(2,1)}, bf16[8,128,256]{2,1,0:T(8,128)(2,1)S(1)}, u32[]{:S(2)}, u32[]{:S(2)}) collective-permute-start(bf16[8,128,256]{2,1,0:T(8,128)(2,1)} %refs_7_.1), channel_id=1, source_target_pairs={{4,8},{12,16},{20,24},{8,4},{16,12},{24,20},{5,9},{13,17},{21,25},... | collective-permute-start | bytes 1572872 | tf_op jit(solution)/shard_map/ppermute | solution.py:721
  4.5 15.1 %collective-permute-start.1 = (bf16[8,128,256]{2,1,0:T(8,128)(2,1)}, bf16[8,128,256]{2,1,0:T(8,128)(2,1)S(1)}, u32[]{:S(2)}, u32[]{:S(2)}) collective-permute-start(bf16[8,128,256]{2,1,0:T(8,128)(2,1)} %refs_7_.1), channel_id=1, source_target_pairs={{0,4},{8,12},{16,20},{24,28},{4,0},{12,8},{20,16},{28,24},{1,5},{9... | collective-permute-start | bytes 1572872 | tf_op jit(solution)/shard_map/ppermute | solution.py:720
  5.8 19.7 %collective-permute-start = (bf16[528,256]{1,0:T(8,128)(2,1)S(1)}, bf16[528,256]{1,0:T(8,128)(2,1)S(1)}, u32[]{:S(2)}, u32[]{:S(2)}) collective-permute-start(bf16[528,256]{1,0:T(8,128)(2,1)S(1)} %get-tuple-element.39), channel_id=1, source_target_pairs={{0,4},{8,12},{16,20},{24,28},{4,0},{12,8},{20,16},{28,24},{1,5},{9... | collective-permute-start | bytes 811016 | tf_op jit(solution)/shard_map/ppermute | solution.py:724
  6.3 19.1 %collective-permute-start.3 = (bf16[528,256]{1,0:T(8,128)(2,1)S(1)}, bf16[528,256]{1,0:T(8,128)(2,1)S(1)}, u32[]{:S(2)}, u32[]{:S(2)}) collective-permute-start(bf16[528,256]{1,0:T(8,128)(2,1)S(1)} %get-tuple-element.49), channel_id=1, source_target_pairs={{4,8},{12,16},{20,24},{8,4},{16,12},{24,20},{5,9},{13,17},{21,25},... | collective-permute-start | bytes 811016 | tf_op jit(solution)/shard_map/ppermute | solution.py:725
  12.7 29.7 %all-to-all-start = ((bf16[32,16,384]{2,1,0:T(8,128)(2,1)}), bf16[32,16,384]{2,1,0:T(8,128)(2,1)S(1)}, u32[]{:S(2)}, u32[]{:S(2)}) async-start(bf16[32,16,384]{2,1,0:T(8,128)(2,1)} %bitcast.4), calls=%async_computation | async-start | bytes 786432 | tf_op jit(solution)/shard_map/all_to_all | solution.py:704
  17.8 1.8 %copy-start.2 = (bf16[8,128,256]{2,1,0:T(8,128)(2,1)S(1)}, bf16[8,128,256]{2,1,0:T(8,128)(2,1)}, u32[]{:S(2)}) copy-start(bf16[8,128,256]{2,1,0:T(8,128)(2,1)} %refs_7_.1) | copy-start | bytes 1572868
  19.6 5.9 %copy-start = (bf16[8,128,256]{2,1,0:T(8,128)(2,1)S(1)}, bf16[8,128,256]{2,1,0:T(8,128)(2,1)}, u32[]{:S(2)}) copy-start(bf16[8,128,256]{2,1,0:T(8,128)(2,1)} %refs_8_.2) | copy-start | bytes 1572868
  25.6 12.0 %collective-permute-start.7 = (bf16[43,8,256]{2,1,0:T(8,128)(2,1)S(1)}, bf16[43,8,256]{2,1,0:T(8,128)(2,1)S(1)}, u32[]{:S(2)}, u32[]{:S(2)}) collective-permute-start(bf16[43,8,256]{2,1,0:T(8,128)(2,1)S(1)} %get-tuple-element.55), channel_id=1, source_target_pairs={{0,1},{2,3},{1,0},{3,2},{4,5},{6,7},{5,4},{7,6},{8,9},{10,11},{9,8... | collective-permute-start | bytes 528392 | tf_op jit(solution)/shard_map/ppermute | solution.py:731
  27.1 10.6 %collective-permute-start.8 = (bf16[43,8,256]{2,1,0:T(8,128)(2,1)S(1)}, bf16[43,8,256]{2,1,0:T(8,128)(2,1)S(1)}, u32[]{:S(2)}, u32[]{:S(2)}) collective-permute-start(bf16[43,8,256]{2,1,0:T(8,128)(2,1)S(1)} %get-tuple-element.56), channel_id=1, source_target_pairs={{1,2},{2,1},{5,6},{6,5},{9,10},{10,9},{13,14},{14,13},{17,18},{18,... | collective-permute-start | bytes 528392 | tf_op jit(solution)/shard_map/ppermute | solution.py:732
  31.8 14.2 %collective-permute-start.4 = (bf16[2,112,256]{2,1,0:T(8,128)(2,1)S(1)}, bf16[2,112,256]{2,1,0:T(8,128)(2,1)S(1)}, u32[]{:S(2)}, u32[]{:S(2)}) collective-permute-start(bf16[2,112,256]{2,1,0:T(8,128)(2,1)S(1)} %get-tuple-element.52), channel_id=1, source_target_pairs={{0,2},{1,3},{2,0},{3,1},{4,6},{5,7},{6,4},{7,5},{8,10},{9,11},{10,... | collective-permute-start | bytes 344072 | tf_op jit(solution)/shard_map/ppermute | solution.py:741
  35.3 11.8 %collective-permute-start.5 = (bf16[2,112,256]{2,1,0:T(8,128)(2,1)S(1)}, bf16[2,112,256]{2,1,0:T(8,128)(2,1)S(1)}, u32[]{:S(2)}, u32[]{:S(2)}) collective-permute-start(bf16[2,112,256]{2,1,0:T(8,128)(2,1)S(1)} %get-tuple-element.53), channel_id=1, source_target_pairs={{0,3},{1,2},{2,1},{3,0},{4,7},{5,6},{6,5},{7,4},{8,11},{9,10},{10,... | collective-permute-start | bytes 344072 | tf_op jit(solution)/shard_map/ppermute | solution.py:741
  37.6 9.4 %collective-permute-start.6 = (bf16[2,112,256]{2,1,0:T(8,128)(2,1)S(1)}, bf16[2,112,256]{2,1,0:T(8,128)(2,1)S(1)}, u32[]{:S(2)}, u32[]{:S(2)}) collective-permute-start(bf16[2,112,256]{2,1,0:T(8,128)(2,1)S(1)} %get-tuple-element.54), channel_id=1, source_target_pairs={{0,1},{1,0},{2,3},{3,2},{4,5},{5,4},{6,7},{7,6},{8,9},{9,8},{10,11... | collective-permute-start | bytes 344072 | tf_op jit(solution)/shard_map/ppermute | solution.py:741
  37.6 8.4 %copy-start.3 = (bf16[384,384]{1,0:T(8,128)(2,1)S(1)}, bf16[384,384]{1,0:T(8,128)(2,1)}, u32[]{:S(2)}) copy-start(bf16[384,384]{1,0:T(8,128)(2,1)} %mix.3) | copy-start | bytes 884740
  37.6 8.4 %copy-start.7 = (bf16[128,128]{1,0:T(8,128)(2,1)S(1)}, bf16[128,128]{1,0:T(8,128)(2,1)}, u32[]{:S(2)}) copy-start(bf16[128,128]{1,0:T(8,128)(2,1)} %constant.36.clone.table) | copy-start | bytes 98308
  42.4 6.3 %copy-start.1 = (bf16[512,512]{1,0:T(8,128)(2,1)S(1)}, bf16[512,512]{1,0:T(8,128)(2,1)}, u32[]{:S(2)}) copy-start(bf16[512,512]{1,0:T(8,128)(2,1)} %constant.34.clone.table.refs_9_) | copy-start | bytes 1572868
  42.4 6.2 %copy-start.8 = (bf16[192,256]{1,0:T(8,128)(2,1)S(1)}, bf16[192,256]{1,0:T(8,128)(2,1)}, u32[]{:S(2)}) copy-start(bf16[192,256]{1,0:T(8,128)(2,1)} %refs_8_.3) | copy-start | bytes 294916
  42.4 4.6 %collective-permute-start.9 = (bf16[2,16,256]{2,1,0:T(8,128)(2,1)S(1)}, bf16[2,16,256]{2,1,0:T(8,128)(2,1)S(1)}, u32[]{:S(2)}, u32[]{:S(2)}) collective-permute-start(bf16[2,16,256]{2,1,0:T(8,128)(2,1)S(1)} %get-tuple-element.65), channel_id=1, source_target_pairs={{0,2},{1,3},{2,0},{3,1},{4,6},{5,7},{6,4},{7,5},{8,10},{9,11},{10,... | collective-permute-start | bytes 49160 | tf_op jit(solution)/shard_map/ppermute | solution.py:741
  43.7 4.4 %collective-permute-start.10 = (bf16[2,16,256]{2,1,0:T(8,128)(2,1)S(1)}, bf16[2,16,256]{2,1,0:T(8,128)(2,1)S(1)}, u32[]{:S(2)}, u32[]{:S(2)}) collective-permute-start(bf16[2,16,256]{2,1,0:T(8,128)(2,1)S(1)} %get-tuple-element.66), channel_id=1, source_target_pairs={{0,3},{1,2},{2,1},{3,0},{4,7},{5,6},{6,5},{7,4},{8,11},{9,10},{10,... | collective-permute-start | bytes 49160 | tf_op jit(solution)/shard_map/ppermute | solution.py:741
  46.0 2.6 %collective-permute-start.11 = (bf16[2,16,256]{2,1,0:T(8,128)(2,1)S(1)}, bf16[2,16,256]{2,1,0:T(8,128)(2,1)S(1)}, u32[]{:S(2)}, u32[]{:S(2)}) collective-permute-start(bf16[2,16,256]{2,1,0:T(8,128)(2,1)S(1)} %get-tuple-element.67), channel_id=1, source_target_pairs={{0,1},{1,0},{2,3},{3,2},{4,5},{5,4},{6,7},{7,6},{8,9},{9,8},{10,11... | collective-permute-start | bytes 49160 | tf_op jit(solution)/shard_map/ppermute | solution.py:741
  47.0 22.4 %copy-start.9 = (bf16[128,128]{1,0:T(8,128)(2,1)S(1)}, bf16[128,128]{1,0:T(8,128)(2,1)}, u32[]{:S(2)}) copy-start(bf16[128,128]{1,0:T(8,128)(2,1)} %constant.35.clone.back_table) | copy-start | bytes 98308
  69.4 16.8 %copy-start.4 = (bf16[512,192]{0,1:T(8,128)(2,1)S(1)}, bf16[512,192]{0,1:T(8,128)(2,1)}, u32[]{:S(2)}) copy-start(bf16[512,192]{0,1:T(8,128)(2,1)} %param.20) | copy-start | bytes 589828
  69.4 16.8 %copy-start.5 = (bf16[512,512]{1,0:T(8,128)(2,1)S(1)}, bf16[512,512]{1,0:T(8,128)(2,1)}, u32[]{:S(2)}) copy-start(bf16[512,512]{1,0:T(8,128)(2,1)} %constant.33.clone.table) | copy-start | bytes 1572868
  69.4 16.8 %copy-start.6 = (bf16[512,256]{1,0:T(8,128)(2,1)S(1)}, bf16[512,256]{1,0:T(8,128)(2,1)}, u32[]{:S(2)}) copy-start(bf16[512,256]{1,0:T(8,128)(2,1)} %weight_local.1) | copy-start | bytes 786436

commit v19 on v18

--- a/solution.py
+++ b/solution.py
@@ -460,8 +460,8 @@
     return find
 
 
-TILE_BLOCKS = (4, 4, 4, 4)
-SIDE_BLOCKS = (10, 8, 12, 8)
+TILE_BLOCKS = (10, 8, 6, 8)
+SIDE_BLOCKS = (20, 16, 12, 8)
 
 
 def tile_forward_kernel(
@@ -542,7 +542,7 @@
     deal(place, out, pieces)
 
 
-def side_kernel(col, low, early, late, own, first, second, ok, *refs):
+def side_kernel(col, low, late, early, own, first, second, ok, *refs):
     *pieces, out, wide_even, wide_odd, slopes = refs
     place = col[0], low[0]
     rows, _, channels = out.shape
@@ -607,7 +607,7 @@
         in_specs=[pl.BlockSpec(memory_space=pltpu.SMEM)] * 2 + [in_vmem] * 6,
         out_specs=[in_vmem] * 2,
         scratch_shapes=[wide_buffer(rows + h, stride, channels) for h in (16, 12)],
-        compiler_params=pltpu.CompilerParams(vmem_limit_bytes=18 * MIB),
+        compiler_params=pltpu.CompilerParams(vmem_limit_bytes=22 * MIB),
         cost_estimate=pl.CostEstimate(
             flops=2 * 9 * channels * channels * stride * (2 * rows + 20),
             bytes_accessed=8 * MIB,
@@ -658,7 +658,7 @@
             *[wide_buffer(rows + h, stride, channels) for h in (16, 12)],
             pltpu.VMEM(((rows + 4) * stride, channels), jnp.float32),
         ],
-        compiler_params=pltpu.CompilerParams(vmem_limit_bytes=14 * MIB),
+        compiler_params=pltpu.CompilerParams(vmem_limit_bytes=18 * MIB),
         cost_estimate=pl.CostEstimate(
             flops=2 * 9 * channels * channels * stride * (4 * rows + 24),
             bytes_accessed=4 * MIB,
@@ -728,8 +728,8 @@
     early_edge, late_edge, own = edges(
         place, early, late, features, target, mask_row, early_pack, late_pack
     )
+    late_edge = lax.ppermute(late_edge, "col", pairs("col", 1))
     early_edge = lax.ppermute(early_edge, "col", pairs("col", 0))
-    late_edge = lax.ppermute(late_edge, "col", pairs("col", 1))
     inner = tile_backward(
         place, pre, slopes, early_pack, target, late_pack, mask_row, kernel_first, kernel_second, ok
     )
@@ -743,7 +743,7 @@
 
     inner = dealt(inner)
     outer = sides(
-        place, features.shape, early_edge, late_edge, own, kernel_first, kernel_second, ok
+        place, features.shape, late_edge, early_edge, own, kernel_first, kernel_second, ok
     )
     *outer, spatial_moved = lax.optimization_barrier((*outer, spatial_moved))
     outer = dealt(outer)

time: 89.5 us -> 90.5 us (1.011)
  Pallas kernels: 25.5 us -> 28.5 us
  starting transfers between devices: 25 us -> 23.8 us
  blocking collectives: 35.5 us -> 34.5 us
    ppermute x6, starting transfers between devices: 9.43 us -> 5.77 us  [dealt(): result.append(lax.ppermute(piece, 'col', swaps) if step else piece)]
    ppermute x1, starting transfers between devices: 1.45 us -> 3.88 us  [shards(): early_edge = lax.ppermute(early_edge, 'col', pairs('col', 0))]
    pallas_call x1, Pallas kernels: 4.71 us -> 6.93 us  [sides(): pl.pallas_call(side_kernel, out_shape=shapes, in_specs=[pl.BlockSpec(memo...]
    all_to_all x2, blocking collectives: 35.5 us -> 34.5 us  [swap(): lax.all_to_all(spectrum, ('col', 'row'), split_axis=0, concat_axis=0, til...]
  transfers between devices with their start and end apart: 13 -> 13, of which waited for: 2 -> 2; matrix products, arithmetic and copies ran while one was open for 0% -> 0% of each run, Pallas kernels for 25% -> 28%
where the time goes in v19:
time: 90.5 us; the launch traced here: 89.2 us
  blocking collectives  34.5 us (38%)
  Pallas kernels  28.5 us (31%)
  starting transfers between devices  23.8 us (26%)
  waiting for transfers between devices  1.89 us (2%)
    all_to_all x2, blocking collectives, swap(): lax.all_to_all(spectrum, ('col', 'row'), split_axis=0, concat_axis=0, til...  34.5 us
    pallas_call x1, Pallas kernels, sides(): pl.pallas_call(side_kernel, out_shape=shapes, in_specs=[pl.BlockSpec(memo...  6.93 us
    pallas_call x1, Pallas kernels, tile_forward(): pl.pallas_call(tile_forward_kernel, out_shape=shapes, in_specs=[pl.BlockS...  6.46 us
    ppermute x6, starting transfers between devices, dealt(): result.append(lax.ppermute(piece, 'col', swaps) if step else piece)  5.77 us
    all_to_all x1, starting transfers between devices, swap(): lax.all_to_all(spectrum, ('col', 'row'), split_axis=0, concat_axis=0, til...  5.12 us
    ppermute x1, starting transfers between devices, shards(): late = lax.ppermute(features, 'row', pairs('row', 1))  4.5 us
    pallas_call x1, Pallas kernels, tile_backward(): pl.pallas_call(tile_backward_kernel, out_shape=shapes, in_specs=[pl.Block...  4.06 us
    ppermute x1, starting transfers between devices, shards(): early_edge = lax.ppermute(early_edge, 'col', pairs('col', 0))  3.88 us
  transfers between devices with their start and end apart: 13, of which 2 were waited for; matrix products, arithmetic and copies ran while one was open for 0% of the time, Pallas kernels for 28%

profile of v19, /device:TPU:1, one launch (start us, length us, event | category | flops | bytes accessed | tf_op | source)
XLA Modules:
  0.0 89.2 jit_solution(5995596517259260184)
XLA Ops:
  0.0 4.5 %collective-permute-start.2 = (bf16[8,128,256]{2,1,0:T(8,128)(2,1)}, bf16[8,128,256]{2,1,0:T(8,128)(2,1)S(1)}, u32[]{:S(2)}, u32[]{:S(2)}) collective-permute-start(bf16[8,128,256]{2,1,0:T(8,128)(2,1)} %refs_7_.1), channel_id=1, source_target_pairs={{4,8},{12,16},{20,24},{8,4},{16,12},{24,20},{5,9},{13,17},{21,25},... | collective-permute-start | bytes 1572872 | tf_op jit(solution)/shard_map/ppermute | solution.py:721
  4.5 0.1 collective-permute-start.1
  4.6 1.1 %shard_map.136 = (bf16[528,256]{1,0:T(8,128)(2,1)S(1)}, bf16[528,256]{1,0:T(8,128)(2,1)S(1)}, bf16[1,128,256]{2,1,0:T(8,128)(2,1)S(1)}) custom-call(s32[1]{0:T(128)} %bitcast.col, s32[1]{0:T(128)} %bitcast.1.low, bf16[1024,256]{1,0:T(8,128)(2,1)} %bitcast.10, s32[8,128]{1,0:T(8,128)} %mask.1), custom_call_target="tpu_custom_call" | custom-call | bytes 1048576 | tf_op jit(solution)/shard_map/pallas_call | solution.py:277
  5.7 0.1 and_convert_fusion.ok
  5.8 0.5 collective-permute-start
  6.3 3.0 %collective-permute-start.3 = (bf16[528,256]{1,0:T(8,128)(2,1)S(1)}, bf16[528,256]{1,0:T(8,128)(2,1)S(1)}, u32[]{:S(2)}, u32[]{:S(2)}) collective-permute-start(bf16[528,256]{1,0:T(8,128)(2,1)S(1)} %get-tuple-element.49), channel_id=1, source_target_pairs={{4,8},{12,16},{20,24},{8,4},{16,12},{24,20},{5,9},{13,17},{21,25},... | collective-permute-start | bytes 811016 | tf_op jit(solution)/shard_map/ppermute | solution.py:725
  9.4 3.3 %shard_map.137 = bf16[512,384]{1,0:T(8,128)(2,1)} custom-call(bf16[2,512,512]{2,1,0:T(8,128)(2,1)} %signal, bf16[192,512]{1,0:T(8,128)(2,1)} %bitcast.15, bf16[512,512]{1,0:T(8,128)(2,1)} %constant.34.clone.table.refs_9_), custom_call_target="tpu_custom_call" | custom-call | bytes 2097152 | tf_op jit(solution)/shard_map/pallas_call | solution.py:125
  12.7 5.1 %all-to-all-start = ((bf16[32,16,384]{2,1,0:T(8,128)(2,1)}), bf16[32,16,384]{2,1,0:T(8,128)(2,1)S(1)}, u32[]{:S(2)}, u32[]{:S(2)}) async-start(bf16[32,16,384]{2,1,0:T(8,128)(2,1)} %bitcast.4), calls=%async_computation | async-start | bytes 786432 | tf_op jit(solution)/shard_map/all_to_all | solution.py:704
  17.8 1.7 %shard_map.138 = (bf16[3,3,256,256]{3,2,1,0:T(8,128)(2,1)S(1)}, bf16[3,3,256,256]{3,2,1,0:T(8,128)(2,1)S(1)}) custom-call(bf16[3,3,256,256]{3,2,1,0:T(8,128)(2,1)} %refs_0_, bf16[3,3,256,256]{3,2,1,0:T(8,128)(2,1)} %refs_1_.1), custom_call_target="tpu_custom_call" | custom-call | bytes 5242880 | tf_op jit(solution)/shard_map/pallas_call | solution.py:299
  19.6 0.0 copy-done.2
  19.6 6.5 %shard_map.139 = (f32[2048,256]{1,0:T(8,128)S(1)}, f32[1536,256]{1,0:T(8,128)S(1)}) custom-call(s32[1]{0:T(128)} %bitcast.col, s32[1]{0:T(128)} %bitcast.1.low, bf16[8,128,256]{2,1,0:T(8,128)(2,1)S(1)} %collective-permute-done.1.early.refs_0_.refs_5_, bf16[8,128,256]{2,1,0:T(8,128)(2,1)S(1)} %copy-done.2, ...), custom_call_target="tpu_custom_call" | custom-call | flops 5435817984 | bytes 8388608 | tf_op jit(solution)/shard_map/pallas_call | solution.py:604
  26.1 0.1 shard_map.141
  26.2 0.9 collective-permute-start.7
  27.1 3.9 %collective-permute-start.8 = (bf16[43,8,256]{2,1,0:T(8,128)(2,1)S(1)}, bf16[43,8,256]{2,1,0:T(8,128)(2,1)S(1)}, u32[]{:S(2)}, u32[]{:S(2)}) collective-permute-start(bf16[43,8,256]{2,1,0:T(8,128)(2,1)S(1)} %get-tuple-element.56), channel_id=1, source_target_pairs={{0,1},{2,3},{1,0},{3,2},{4,5},{6,7},{5,4},{7,6},{8,9},{10,11},{9,8... | collective-permute-start | bytes 528392 | tf_op jit(solution)/shard_map/ppermute | solution.py:732
  31.0 4.1 %shard_map.140 = (bf16[2,112,256]{2,1,0:T(8,128)(2,1)S(1)}, bf16[2,112,256]{2,1,0:T(8,128)(2,1)S(1)}, bf16[2,112,256]{2,1,0:T(8,128)(2,1)S(1)}, bf16[2,112,256]{2,1,0:T(8,128)(2,1)S(1)}) custom-call(s32[1]{0:T(128)} %bitcast.col, s32[1]{0:T(128)} %bitcast.1.low, f32[2048,256]{1,0:T(8,128)S(1)} %get-tuple-element.46.pre, ...), custom_call_target="tpu_custom_call" | custom-call | flops 3019898880 | bytes 8388608 | tf_op jit(solution)/shard_map/pallas_call | solution.py:628
  35.0 0.1 collective-permute-start.4
  35.1 2.1 %collective-permute-start.5 = (bf16[2,112,256]{2,1,0:T(8,128)(2,1)S(1)}, bf16[2,112,256]{2,1,0:T(8,128)(2,1)S(1)}, u32[]{:S(2)}, u32[]{:S(2)}) collective-permute-start(bf16[2,112,256]{2,1,0:T(8,128)(2,1)S(1)} %get-tuple-element.53), channel_id=1, source_target_pairs={{0,3},{1,2},{2,1},{3,0},{4,7},{5,6},{6,5},{7,4},{8,11},{9,10},{10,... | collective-permute-start | bytes 344072 | tf_op jit(solution)/shard_map/ppermute | solution.py:741
  37.2 0.6 collective-permute-start.6
  37.7 0.0 copy-start.7
  37.8 6.9 %shard_map.142 = (bf16[2,16,256]{2,1,0:T(8,128)(2,1)S(1)}, bf16[2,16,256]{2,1,0:T(8,128)(2,1)S(1)}, bf16[2,16,256]{2,1,0:T(8,128)(2,1)S(1)}, bf16[2,16,256]{2,1,0:T(8,128)(2,1)S(1)}) custom-call(s32[1]{0:T(128)} %bitcast.col, s32[1]{0:T(128)} %bitcast.1.low, bf16[43,8,256]{2,1,0:T(8,128)(2,1)S(1)} %collective-permute-done.7.late, ...), custom_call_target="tpu_custom_call" | custom-call | flops 3170893824 | bytes 4194304 | tf_op jit(solution)/shard_map/pallas_call | solution.py:651
  44.7 0.0 copy-start.1
  44.7 1.0 %collective-permute-start.9 = (bf16[2,16,256]{2,1,0:T(8,128)(2,1)S(1)}, bf16[2,16,256]{2,1,0:T(8,128)(2,1)S(1)}, u32[]{:S(2)}, u32[]{:S(2)}) collective-permute-start(bf16[2,16,256]{2,1,0:T(8,128)(2,1)S(1)} %get-tuple-element.65), channel_id=1, source_target_pairs={{0,2},{1,3},{2,0},{3,1},{4,6},{5,7},{6,4},{7,5},{8,10},{9,11},{10,... | collective-permute-start | bytes 49160 | tf_op jit(solution)/shard_map/ppermute | solution.py:741
  45.8 2.0 %collective-permute-start.10 = (bf16[2,16,256]{2,1,0:T(8,128)(2,1)S(1)}, bf16[2,16,256]{2,1,0:T(8,128)(2,1)S(1)}, u32[]{:S(2)}, u32[]{:S(2)}) collective-permute-start(bf16[2,16,256]{2,1,0:T(8,128)(2,1)S(1)} %get-tuple-element.66), channel_id=1, source_target_pairs={{0,3},{1,2},{2,1},{3,0},{4,7},{5,6},{6,5},{7,4},{8,11},{9,10},{10,... | collective-permute-start | bytes 49160 | tf_op jit(solution)/shard_map/ppermute | solution.py:741
  47.8 1.0 %shard_map.143.slope = f32[2,512,192]{2,1,0:T(8,128)S(1)} custom-call(bf16[512,384]{1,0:T(8,128)(2,1)S(1)} %bitcast.11, bf16[384,384]{1,0:T(8,128)(2,1)S(1)} %copy-done.3, bf16[128,128]{1,0:T(8,128)(2,1)S(1)} %copy-done.7), custom_call_target="tpu_custom_call" | custom-call | bytes 1507328 | tf_op jit(solution)/shard_map/pallas_call | solution.py:30
  48.8 0.0 copy-start.9
  48.8 1.3 %collective-permute-done.10.refs_6_ = bf16[2,16,256]{2,1,0:T(8,128)(2,1)S(1)} collective-permute-done((bf16[2,16,256]{2,1,0:T(8,128)(2,1)S(1)}, bf16[2,16,256]{2,1,0:T(8,128)(2,1)S(1)}, u32[]{:S(2)}, u32[]{:S(2)}) %collective-permute-start.10) | collective-permute-done | bytes 16416 | tf_op jit(solution)/shard_map/ppermute | solution.py:741
  50.2 0.5 collective-permute-done.11.refs_7_
  50.7 0.9 shard_map.144
  51.6 18.8 %all_to_all.34 = bf16[32,16,384]{2,1,0:T(8,128)(2,1)S(1)} all-to-all(bf16[32,16,384]{2,1,0:T(8,128)(2,1)S(1)} %bitcast.17), channel_id=1, replica_groups=mesh['row'=8,'col'=4] {'col','row'}, dimensions={0} | all-to-all | bytes 786432 | tf_op jit(solution)/shard_map/all_to_all | solution.py:704
  70.4 1.2 %shard_map.145 = bf16[512,384]{1,0:T(8,128)(2,1)S(1)} custom-call(bf16[512,384]{1,0:T(8,128)(2,1)S(1)} %bitcast.12, f32[2,512,192]{2,1,0:T(8,128)S(1)} %shard_map.143.slope, bf16[384,384]{1,0:T(8,128)(2,1)S(1)} %copy-done.3, bf16[128,128]{1,0:T(8,128)(2,1)S(1)} %copy-done.7, bf16[128,128]{1,0:T(8,128)(2,1)S(1)} %copy-done.9), custom_call_target="tpu_custom_call" | custom-call | bytes 1933312 | tf_op jit(solution)/shard_map/pallas_call | solution.py:30
  71.6 15.6 %all_to_all.35 = bf16[32,16,384]{2,1,0:T(8,128)(2,1)S(1)} all-to-all(bf16[32,16,384]{2,1,0:T(8,128)(2,1)S(1)} %bitcast.13), channel_id=1, replica_groups=mesh['row'=8,'col'=4] {'col','row'}, dimensions={0} | all-to-all | bytes 786432 | tf_op jit(solution)/shard_map/all_to_all | solution.py:704
  87.2 1.8 %shard_map.146 = bf16[2,512,512]{2,1,0:T(8,128)(2,1)} custom-call(bf16[512,384]{1,0:T(8,128)(2,1)S(1)} %bitcast.14, bf16[4,2,128,256]{3,2,1,0:T(8,128)(2,1)S(1)} %get-tuple-element.70.strip_grad, bf16[192,512]{1,0:T(8,128)(2,1)S(1)} %bitcast.16, bf16[512,256]{1,0:T(8,128)(2,1)S(1)} %copy-done.6, bf16[512,512]{1,0:T(8,128)(2,1)S(1)} %copy-done.5), custom_call_target="tpu_custom_call" | custom-call | bytes 3145728 | tf_op jit(solution)/shard_map/pallas_call | solution.py:212
  (30 shorter events, 0.1 us)
Async XLA Ops:
  0.0 19.5 %collective-permute-start.2 = (bf16[8,128,256]{2,1,0:T(8,128)(2,1)}, bf16[8,128,256]{2,1,0:T(8,128)(2,1)S(1)}, u32[]{:S(2)}, u32[]{:S(2)}) collective-permute-start(bf16[8,128,256]{2,1,0:T(8,128)(2,1)} %refs_7_.1), channel_id=1, source_target_pairs={{4,8},{12,16},{20,24},{8,4},{16,12},{24,20},{5,9},{13,17},{21,25},... | collective-permute-start | bytes 1572872 | tf_op jit(solution)/shard_map/ppermute | solution.py:721
  4.5 15.1 %collective-permute-start.1 = (bf16[8,128,256]{2,1,0:T(8,128)(2,1)}, bf16[8,128,256]{2,1,0:T(8,128)(2,1)S(1)}, u32[]{:S(2)}, u32[]{:S(2)}) collective-permute-start(bf16[8,128,256]{2,1,0:T(8,128)(2,1)} %refs_7_.1), channel_id=1, source_target_pairs={{0,4},{8,12},{16,20},{24,28},{4,0},{12,8},{20,16},{28,24},{1,5},{9... | collective-permute-start | bytes 1572872 | tf_op jit(solution)/shard_map/ppermute | solution.py:720
  5.8 20.2 %collective-permute-start = (bf16[528,256]{1,0:T(8,128)(2,1)S(1)}, bf16[528,256]{1,0:T(8,128)(2,1)S(1)}, u32[]{:S(2)}, u32[]{:S(2)}) collective-permute-start(bf16[528,256]{1,0:T(8,128)(2,1)S(1)} %get-tuple-element.39), channel_id=1, source_target_pairs={{0,4},{8,12},{16,20},{24,28},{4,0},{12,8},{20,16},{28,24},{1,5},{9... | collective-permute-start | bytes 811016 | tf_op jit(solution)/shard_map/ppermute | solution.py:724
  6.3 19.7 %collective-permute-start.3 = (bf16[528,256]{1,0:T(8,128)(2,1)S(1)}, bf16[528,256]{1,0:T(8,128)(2,1)S(1)}, u32[]{:S(2)}, u32[]{:S(2)}) collective-permute-start(bf16[528,256]{1,0:T(8,128)(2,1)S(1)} %get-tuple-element.49), channel_id=1, source_target_pairs={{4,8},{12,16},{20,24},{8,4},{16,12},{24,20},{5,9},{13,17},{21,25},... | collective-permute-start | bytes 811016 | tf_op jit(solution)/shard_map/ppermute | solution.py:725
  12.7 32.0 %all-to-all-start = ((bf16[32,16,384]{2,1,0:T(8,128)(2,1)}), bf16[32,16,384]{2,1,0:T(8,128)(2,1)S(1)}, u32[]{:S(2)}, u32[]{:S(2)}) async-start(bf16[32,16,384]{2,1,0:T(8,128)(2,1)} %bitcast.4), calls=%async_computation | async-start | bytes 786432 | tf_op jit(solution)/shard_map/all_to_all | solution.py:704
  17.8 1.8 %copy-start.2 = (bf16[8,128,256]{2,1,0:T(8,128)(2,1)S(1)}, bf16[8,128,256]{2,1,0:T(8,128)(2,1)}, u32[]{:S(2)}) copy-start(bf16[8,128,256]{2,1,0:T(8,128)(2,1)} %refs_7_.1) | copy-start | bytes 1572868
  19.6 6.5 %copy-start = (bf16[8,128,256]{2,1,0:T(8,128)(2,1)S(1)}, bf16[8,128,256]{2,1,0:T(8,128)(2,1)}, u32[]{:S(2)}) copy-start(bf16[8,128,256]{2,1,0:T(8,128)(2,1)} %refs_8_.2) | copy-start | bytes 1572868
  26.2 11.5 %collective-permute-start.7 = (bf16[43,8,256]{2,1,0:T(8,128)(2,1)S(1)}, bf16[43,8,256]{2,1,0:T(8,128)(2,1)S(1)}, u32[]{:S(2)}, u32[]{:S(2)}) collective-permute-start(bf16[43,8,256]{2,1,0:T(8,128)(2,1)S(1)} %get-tuple-element.55), channel_id=1, source_target_pairs={{1,2},{2,1},{5,6},{6,5},{9,10},{10,9},{13,14},{14,13},{17,18},{18,... | collective-permute-start | bytes 528392 | tf_op jit(solution)/shard_map/ppermute | solution.py:731
  27.1 10.7 %collective-permute-start.8 = (bf16[43,8,256]{2,1,0:T(8,128)(2,1)S(1)}, bf16[43,8,256]{2,1,0:T(8,128)(2,1)S(1)}, u32[]{:S(2)}, u32[]{:S(2)}) collective-permute-start(bf16[43,8,256]{2,1,0:T(8,128)(2,1)S(1)} %get-tuple-element.56), channel_id=1, source_target_pairs={{0,1},{2,3},{1,0},{3,2},{4,5},{6,7},{5,4},{7,6},{8,9},{10,11},{9,8... | collective-permute-start | bytes 528392 | tf_op jit(solution)/shard_map/ppermute | solution.py:732
  35.0 12.8 %collective-permute-start.4 = (bf16[2,112,256]{2,1,0:T(8,128)(2,1)S(1)}, bf16[2,112,256]{2,1,0:T(8,128)(2,1)S(1)}, u32[]{:S(2)}, u32[]{:S(2)}) collective-permute-start(bf16[2,112,256]{2,1,0:T(8,128)(2,1)S(1)} %get-tuple-element.52), channel_id=1, source_target_pairs={{0,2},{1,3},{2,0},{3,1},{4,6},{5,7},{6,4},{7,5},{8,10},{9,11},{10,... | collective-permute-start | bytes 344072 | tf_op jit(solution)/shard_map/ppermute | solution.py:741
  35.1 13.7 %collective-permute-start.5 = (bf16[2,112,256]{2,1,0:T(8,128)(2,1)S(1)}, bf16[2,112,256]{2,1,0:T(8,128)(2,1)S(1)}, u32[]{:S(2)}, u32[]{:S(2)}) collective-permute-start(bf16[2,112,256]{2,1,0:T(8,128)(2,1)S(1)} %get-tuple-element.53), channel_id=1, source_target_pairs={{0,3},{1,2},{2,1},{3,0},{4,7},{5,6},{6,5},{7,4},{8,11},{9,10},{10,... | collective-permute-start | bytes 344072 | tf_op jit(solution)/shard_map/ppermute | solution.py:741
  37.2 11.6 %collective-permute-start.6 = (bf16[2,112,256]{2,1,0:T(8,128)(2,1)S(1)}, bf16[2,112,256]{2,1,0:T(8,128)(2,1)S(1)}, u32[]{:S(2)}, u32[]{:S(2)}) collective-permute-start(bf16[2,112,256]{2,1,0:T(8,128)(2,1)S(1)} %get-tuple-element.54), channel_id=1, source_target_pairs={{0,1},{1,0},{2,3},{3,2},{4,5},{5,4},{6,7},{7,6},{8,9},{9,8},{10,11... | collective-permute-start | bytes 344072 | tf_op jit(solution)/shard_map/ppermute | solution.py:741
  37.7 10.1 %copy-start.3 = (bf16[384,384]{1,0:T(8,128)(2,1)S(1)}, bf16[384,384]{1,0:T(8,128)(2,1)}, u32[]{:S(2)}) copy-start(bf16[384,384]{1,0:T(8,128)(2,1)} %mix.3) | copy-start | bytes 884740
  37.7 10.1 %copy-start.7 = (bf16[128,128]{1,0:T(8,128)(2,1)S(1)}, bf16[128,128]{1,0:T(8,128)(2,1)}, u32[]{:S(2)}) copy-start(bf16[128,128]{1,0:T(8,128)(2,1)} %constant.36.clone.table) | copy-start | bytes 98308
  44.7 6.0 %copy-start.1 = (bf16[512,512]{1,0:T(8,128)(2,1)S(1)}, bf16[512,512]{1,0:T(8,128)(2,1)}, u32[]{:S(2)}) copy-start(bf16[512,512]{1,0:T(8,128)(2,1)} %constant.34.clone.table.refs_9_) | copy-start | bytes 1572868
  44.7 6.0 %copy-start.8 = (bf16[192,256]{1,0:T(8,128)(2,1)S(1)}, bf16[192,256]{1,0:T(8,128)(2,1)}, u32[]{:S(2)}) copy-start(bf16[192,256]{1,0:T(8,128)(2,1)} %refs_8_.3) | copy-start | bytes 294916
  44.7 4.1 %collective-permute-start.9 = (bf16[2,16,256]{2,1,0:T(8,128)(2,1)S(1)}, bf16[2,16,256]{2,1,0:T(8,128)(2,1)S(1)}, u32[]{:S(2)}, u32[]{:S(2)}) collective-permute-start(bf16[2,16,256]{2,1,0:T(8,128)(2,1)S(1)} %get-tuple-element.65), channel_id=1, source_target_pairs={{0,2},{1,3},{2,0},{3,1},{4,6},{5,7},{6,4},{7,5},{8,10},{9,11},{10,... | collective-permute-start | bytes 49160 | tf_op jit(solution)/shard_map/ppermute | solution.py:741
  45.8 4.4 %collective-permute-start.10 = (bf16[2,16,256]{2,1,0:T(8,128)(2,1)S(1)}, bf16[2,16,256]{2,1,0:T(8,128)(2,1)S(1)}, u32[]{:S(2)}, u32[]{:S(2)}) collective-permute-start(bf16[2,16,256]{2,1,0:T(8,128)(2,1)S(1)} %get-tuple-element.66), channel_id=1, source_target_pairs={{0,3},{1,2},{2,1},{3,0},{4,7},{5,6},{6,5},{7,4},{8,11},{9,10},{10,... | collective-permute-start | bytes 49160 | tf_op jit(solution)/shard_map/ppermute | solution.py:741
  47.8 2.9 %collective-permute-start.11 = (bf16[2,16,256]{2,1,0:T(8,128)(2,1)S(1)}, bf16[2,16,256]{2,1,0:T(8,128)(2,1)S(1)}, u32[]{:S(2)}, u32[]{:S(2)}) collective-permute-start(bf16[2,16,256]{2,1,0:T(8,128)(2,1)S(1)} %get-tuple-element.67), channel_id=1, source_target_pairs={{0,1},{1,0},{2,3},{3,2},{4,5},{5,4},{6,7},{7,6},{8,9},{9,8},{10,11... | collective-permute-start | bytes 49160 | tf_op jit(solution)/shard_map/ppermute | solution.py:741
  48.8 21.6 %copy-start.9 = (bf16[128,128]{1,0:T(8,128)(2,1)S(1)}, bf16[128,128]{1,0:T(8,128)(2,1)}, u32[]{:S(2)}) copy-start(bf16[128,128]{1,0:T(8,128)(2,1)} %constant.35.clone.back_table) | copy-start | bytes 98308
  70.4 16.8 %copy-start.4 = (bf16[512,192]{0,1:T(8,128)(2,1)S(1)}, bf16[512,192]{0,1:T(8,128)(2,1)}, u32[]{:S(2)}) copy-start(bf16[512,192]{0,1:T(8,128)(2,1)} %param.20) | copy-start | bytes 589828
  70.4 16.8 %copy-start.5 = (bf16[512,512]{1,0:T(8,128)(2,1)S(1)}, bf16[512,512]{1,0:T(8,128)(2,1)}, u32[]{:S(2)}) copy-start(bf16[512,512]{1,0:T(8,128)(2,1)} %constant.33.clone.table) | copy-start | bytes 1572868
  70.4 16.8 %copy-start.6 = (bf16[512,256]{1,0:T(8,128)(2,1)S(1)}, bf16[512,256]{1,0:T(8,128)(2,1)}, u32[]{:S(2)}) copy-start(bf16[512,256]{1,0:T(8,128)(2,1)} %weight_local.1) | copy-start | bytes 786436

commit v20 on v19

--- a/solution.py
+++ b/solution.py
@@ -460,8 +460,8 @@
     return find
 
 
-TILE_BLOCKS = (10, 8, 6, 8)
-SIDE_BLOCKS = (20, 16, 12, 8)
+TILE_BLOCKS = (2, 2, 2, 2)
+SIDE_BLOCKS = (5, 4, 6, 4)
 
 
 def tile_forward_kernel(

time: 90.5 us -> 87 us (0.961)
  Pallas kernels: 28.5 us -> 24.5 us
  waiting for transfers between devices: 1.89 us -> 3.39 us
  blocking collectives: 34.5 us -> 33.4 us
    pallas_call x1, Pallas kernels: 6.93 us -> 3.86 us  [sides(): pl.pallas_call(side_kernel, out_shape=shapes, in_specs=[pl.BlockSpec(memo...]
    ppermute x6, waiting for transfers between devices: 1.87 us -> 3.37 us  [dealt(): result.append(lax.ppermute(piece, 'col', swaps) if step else piece)]
    all_to_all x2, blocking collectives: 34.5 us -> 33.4 us  [swap(): lax.all_to_all(spectrum, ('col', 'row'), split_axis=0, concat_axis=0, til...]
  transfers between devices with their start and end apart: 13 -> 13, of which waited for: 2 -> 2; matrix products, arithmetic and copies ran while one was open for 0% -> 0% of each run, Pallas kernels for 28% -> 24%
where the time goes in v20:
time: 87 us; the launch traced here: 85.7 us
  blocking collectives  33.4 us (38%)
  Pallas kernels  24.5 us (28%)
  starting transfers between devices  23.8 us (27%)
  waiting for transfers between devices  3.39 us (4%)
    all_to_all x2, blocking collectives, swap(): lax.all_to_all(spectrum, ('col', 'row'), split_axis=0, concat_axis=0, til...  33.4 us
    ppermute x6, starting transfers between devices, dealt(): result.append(lax.ppermute(piece, 'col', swaps) if step else piece)  5.77 us
    pallas_call x1, Pallas kernels, tile_forward(): pl.pallas_call(tile_forward_kernel, out_shape=shapes, in_specs=[pl.BlockS...  5.74 us
    all_to_all x1, starting transfers between devices, swap(): lax.all_to_all(spectrum, ('col', 'row'), split_axis=0, concat_axis=0, til...  5.12 us
    ppermute x1, starting transfers between devices, shards(): late = lax.ppermute(features, 'row', pairs('row', 1))  4.5 us
    ppermute x1, starting transfers between devices, shards(): early_edge = lax.ppermute(early_edge, 'col', pairs('col', 0))  3.88 us
    pallas_call x1, Pallas kernels, tile_backward(): pl.pallas_call(tile_backward_kernel, out_shape=shapes, in_specs=[pl.Block...  3.86 us
    pallas_call x1, Pallas kernels, sides(): pl.pallas_call(side_kernel, out_shape=shapes, in_specs=[pl.BlockSpec(memo...  3.86 us
  transfers between devices with their start and end apart: 13, of which 2 were waited for; matrix products, arithmetic and copies ran while one was open for 0% of the time, Pallas kernels for 24%

profile of v20, /device:TPU:1, one launch (start us, length us, event | category | flops | bytes accessed | tf_op | source)
XLA Modules:
  0.0 85.7 jit_solution(11558977920337617876)
XLA Ops:
  0.0 4.5 %collective-permute-start.2 = (bf16[8,128,256]{2,1,0:T(8,128)(2,1)}, bf16[8,128,256]{2,1,0:T(8,128)(2,1)S(1)}, u32[]{:S(2)}, u32[]{:S(2)}) collective-permute-start(bf16[8,128,256]{2,1,0:T(8,128)(2,1)} %refs_7_.1), channel_id=1, source_target_pairs={{4,8},{12,16},{20,24},{8,4},{16,12},{24,20},{5,9},{13,17},{21,25},... | collective-permute-start | bytes 1572872 | tf_op jit(solution)/shard_map/ppermute | solution.py:721
  4.5 0.1 collective-permute-start.1
  4.6 1.1 %shard_map.136 = (bf16[528,256]{1,0:T(8,128)(2,1)S(1)}, bf16[528,256]{1,0:T(8,128)(2,1)S(1)}, bf16[1,128,256]{2,1,0:T(8,128)(2,1)S(1)}) custom-call(s32[1]{0:T(128)} %bitcast.col, s32[1]{0:T(128)} %bitcast.1.low, bf16[1024,256]{1,0:T(8,128)(2,1)} %bitcast.10, s32[8,128]{1,0:T(8,128)} %mask.1), custom_call_target="tpu_custom_call" | custom-call | bytes 1048576 | tf_op jit(solution)/shard_map/pallas_call | solution.py:277
  5.7 0.1 and_convert_fusion.ok
  5.8 0.5 collective-permute-start
  6.3 3.0 %collective-permute-start.3 = (bf16[528,256]{1,0:T(8,128)(2,1)S(1)}, bf16[528,256]{1,0:T(8,128)(2,1)S(1)}, u32[]{:S(2)}, u32[]{:S(2)}) collective-permute-start(bf16[528,256]{1,0:T(8,128)(2,1)S(1)} %get-tuple-element.49), channel_id=1, source_target_pairs={{4,8},{12,16},{20,24},{8,4},{16,12},{24,20},{5,9},{13,17},{21,25},... | collective-permute-start | bytes 811016 | tf_op jit(solution)/shard_map/ppermute | solution.py:725
  9.4 3.3 %shard_map.137 = bf16[512,384]{1,0:T(8,128)(2,1)} custom-call(bf16[2,512,512]{2,1,0:T(8,128)(2,1)} %signal, bf16[192,512]{1,0:T(8,128)(2,1)} %bitcast.15, bf16[512,512]{1,0:T(8,128)(2,1)} %constant.34.clone.table.refs_9_), custom_call_target="tpu_custom_call" | custom-call | bytes 2097152 | tf_op jit(solution)/shard_map/pallas_call | solution.py:125
  12.7 5.1 %all-to-all-start = ((bf16[32,16,384]{2,1,0:T(8,128)(2,1)}), bf16[32,16,384]{2,1,0:T(8,128)(2,1)S(1)}, u32[]{:S(2)}, u32[]{:S(2)}) async-start(bf16[32,16,384]{2,1,0:T(8,128)(2,1)} %bitcast.4), calls=%async_computation | async-start | bytes 786432 | tf_op jit(solution)/shard_map/all_to_all | solution.py:704
  17.8 1.7 %shard_map.138 = (bf16[3,3,256,256]{3,2,1,0:T(8,128)(2,1)S(1)}, bf16[3,3,256,256]{3,2,1,0:T(8,128)(2,1)S(1)}) custom-call(bf16[3,3,256,256]{3,2,1,0:T(8,128)(2,1)} %refs_0_, bf16[3,3,256,256]{3,2,1,0:T(8,128)(2,1)} %refs_1_.1), custom_call_target="tpu_custom_call" | custom-call | bytes 5242880 | tf_op jit(solution)/shard_map/pallas_call | solution.py:299
  19.6 0.0 copy-done.2
  19.6 5.7 %shard_map.139 = (f32[2048,256]{1,0:T(8,128)S(1)}, f32[1536,256]{1,0:T(8,128)S(1)}) custom-call(s32[1]{0:T(128)} %bitcast.col, s32[1]{0:T(128)} %bitcast.1.low, bf16[8,128,256]{2,1,0:T(8,128)(2,1)S(1)} %collective-permute-done.1.early.refs_0_.refs_5_, bf16[8,128,256]{2,1,0:T(8,128)(2,1)S(1)} %copy-done.2, ...), custom_call_target="tpu_custom_call" | custom-call | flops 5435817984 | bytes 8388608 | tf_op jit(solution)/shard_map/pallas_call | solution.py:604
  25.4 0.1 shard_map.141
  25.5 0.9 collective-permute-start.7
  26.4 3.9 %collective-permute-start.8 = (bf16[43,8,256]{2,1,0:T(8,128)(2,1)S(1)}, bf16[43,8,256]{2,1,0:T(8,128)(2,1)S(1)}, u32[]{:S(2)}, u32[]{:S(2)}) collective-permute-start(bf16[43,8,256]{2,1,0:T(8,128)(2,1)S(1)} %get-tuple-element.56), channel_id=1, source_target_pairs={{0,1},{2,3},{1,0},{3,2},{4,5},{6,7},{5,4},{7,6},{8,9},{10,11},{9,8... | collective-permute-start | bytes 528392 | tf_op jit(solution)/shard_map/ppermute | solution.py:732
  30.2 3.9 %shard_map.140 = (bf16[2,112,256]{2,1,0:T(8,128)(2,1)S(1)}, bf16[2,112,256]{2,1,0:T(8,128)(2,1)S(1)}, bf16[2,112,256]{2,1,0:T(8,128)(2,1)S(1)}, bf16[2,112,256]{2,1,0:T(8,128)(2,1)S(1)}) custom-call(s32[1]{0:T(128)} %bitcast.col, s32[1]{0:T(128)} %bitcast.1.low, f32[2048,256]{1,0:T(8,128)S(1)} %get-tuple-element.46.pre, ...), custom_call_target="tpu_custom_call" | custom-call | flops 3019898880 | bytes 8388608 | tf_op jit(solution)/shard_map/pallas_call | solution.py:628
  34.1 0.1 collective-permute-start.4
  34.2 2.1 %collective-permute-start.5 = (bf16[2,112,256]{2,1,0:T(8,128)(2,1)S(1)}, bf16[2,112,256]{2,1,0:T(8,128)(2,1)S(1)}, u32[]{:S(2)}, u32[]{:S(2)}) collective-permute-start(bf16[2,112,256]{2,1,0:T(8,128)(2,1)S(1)} %get-tuple-element.53), channel_id=1, source_target_pairs={{0,3},{1,2},{2,1},{3,0},{4,7},{5,6},{6,5},{7,4},{8,11},{9,10},{10,... | collective-permute-start | bytes 344072 | tf_op jit(solution)/shard_map/ppermute | solution.py:741
  36.3 0.5 collective-permute-start.6
  36.8 0.0 copy-start.7
  36.9 3.9 %shard_map.142 = (bf16[2,16,256]{2,1,0:T(8,128)(2,1)S(1)}, bf16[2,16,256]{2,1,0:T(8,128)(2,1)S(1)}, bf16[2,16,256]{2,1,0:T(8,128)(2,1)S(1)}, bf16[2,16,256]{2,1,0:T(8,128)(2,1)S(1)}) custom-call(s32[1]{0:T(128)} %bitcast.col, s32[1]{0:T(128)} %bitcast.1.low, bf16[43,8,256]{2,1,0:T(8,128)(2,1)S(1)} %collective-permute-done.7.late, ...), custom_call_target="tpu_custom_call" | custom-call | flops 3170893824 | bytes 4194304 | tf_op jit(solution)/shard_map/pallas_call | solution.py:651
  40.7 0.0 copy-start.1
  40.8 1.0 %collective-permute-start.9 = (bf16[2,16,256]{2,1,0:T(8,128)(2,1)S(1)}, bf16[2,16,256]{2,1,0:T(8,128)(2,1)S(1)}, u32[]{:S(2)}, u32[]{:S(2)}) collective-permute-start(bf16[2,16,256]{2,1,0:T(8,128)(2,1)S(1)} %get-tuple-element.65), channel_id=1, source_target_pairs={{0,2},{1,3},{2,0},{3,1},{4,6},{5,7},{6,4},{7,5},{8,10},{9,11},{10,... | collective-permute-start | bytes 49160 | tf_op jit(solution)/shard_map/ppermute | solution.py:741
  41.8 2.0 %collective-permute-start.10 = (bf16[2,16,256]{2,1,0:T(8,128)(2,1)S(1)}, bf16[2,16,256]{2,1,0:T(8,128)(2,1)S(1)}, u32[]{:S(2)}, u32[]{:S(2)}) collective-permute-start(bf16[2,16,256]{2,1,0:T(8,128)(2,1)S(1)} %get-tuple-element.66), channel_id=1, source_target_pairs={{0,3},{1,2},{2,1},{3,0},{4,7},{5,6},{6,5},{7,4},{8,11},{9,10},{10,... | collective-permute-start | bytes 49160 | tf_op jit(solution)/shard_map/ppermute | solution.py:741
  43.8 1.0 %collective-permute-done.4.refs_1_ = bf16[2,112,256]{2,1,0:T(8,128)(2,1)S(1)} collective-permute-done((bf16[2,112,256]{2,1,0:T(8,128)(2,1)S(1)}, bf16[2,112,256]{2,1,0:T(8,128)(2,1)S(1)}, u32[]{:S(2)}, u32[]{:S(2)}) %collective-permute-start.4) | collective-permute-done | bytes 114720 | tf_op jit(solution)/shard_map/ppermute | solution.py:741
  44.9 1.0 %shard_map.143.slope = f32[2,512,192]{2,1,0:T(8,128)S(1)} custom-call(bf16[512,384]{1,0:T(8,128)(2,1)S(1)} %bitcast.11, bf16[384,384]{1,0:T(8,128)(2,1)S(1)} %copy-done.3, bf16[128,128]{1,0:T(8,128)(2,1)S(1)} %copy-done.7), custom_call_target="tpu_custom_call" | custom-call | bytes 1507328 | tf_op jit(solution)/shard_map/pallas_call | solution.py:30
  45.8 0.0 copy-start.9
  45.9 2.3 %collective-permute-done.9.refs_5_ = bf16[2,16,256]{2,1,0:T(8,128)(2,1)S(1)} collective-permute-done((bf16[2,16,256]{2,1,0:T(8,128)(2,1)S(1)}, bf16[2,16,256]{2,1,0:T(8,128)(2,1)S(1)}, u32[]{:S(2)}, u32[]{:S(2)}) %collective-permute-start.9) | collective-permute-done | bytes 16416 | tf_op jit(solution)/shard_map/ppermute | solution.py:741
  48.2 0.9 %shard_map.144 = (bf16[512,384]{1,0:T(8,128)(2,1)S(1)}, bf16[4,2,128,256]{3,2,1,0:T(8,128)(2,1)S(1)}) custom-call(s32[1]{0:T(128)} %bitcast.col, s32[1]{0:T(128)} %bitcast.1.low, bf16[2,112,256]{2,1,0:T(8,128)(2,1)S(1)} %get-tuple-element.51.refs_0_, bf16[2,112,256]{2,1,0:T(8,128)(2,1)S(1)} %collective-permute-done.4.refs_1_, ...), custom_call_target="tpu_custom_call" | custom-call | bytes 2097152 | tf_op jit(solution)/shard_map/pallas_call | solution.py:91
  49.1 17.8 %all_to_all.34 = bf16[32,16,384]{2,1,0:T(8,128)(2,1)S(1)} all-to-all(bf16[32,16,384]{2,1,0:T(8,128)(2,1)S(1)} %bitcast.17), channel_id=1, replica_groups=mesh['row'=8,'col'=4] {'col','row'}, dimensions={0} | all-to-all | bytes 786432 | tf_op jit(solution)/shard_map/all_to_all | solution.py:704
  66.9 1.2 %shard_map.145 = bf16[512,384]{1,0:T(8,128)(2,1)S(1)} custom-call(bf16[512,384]{1,0:T(8,128)(2,1)S(1)} %bitcast.12, f32[2,512,192]{2,1,0:T(8,128)S(1)} %shard_map.143.slope, bf16[384,384]{1,0:T(8,128)(2,1)S(1)} %copy-done.3, bf16[128,128]{1,0:T(8,128)(2,1)S(1)} %copy-done.7, bf16[128,128]{1,0:T(8,128)(2,1)S(1)} %copy-done.9), custom_call_target="tpu_custom_call" | custom-call | bytes 1933312 | tf_op jit(solution)/shard_map/pallas_call | solution.py:30
  68.1 15.6 %all_to_all.35 = bf16[32,16,384]{2,1,0:T(8,128)(2,1)S(1)} all-to-all(bf16[32,16,384]{2,1,0:T(8,128)(2,1)S(1)} %bitcast.13), channel_id=1, replica_groups=mesh['row'=8,'col'=4] {'col','row'}, dimensions={0} | all-to-all | bytes 786432 | tf_op jit(solution)/shard_map/all_to_all | solution.py:704
  83.7 1.8 %shard_map.146 = bf16[2,512,512]{2,1,0:T(8,128)(2,1)} custom-call(bf16[512,384]{1,0:T(8,128)(2,1)S(1)} %bitcast.14, bf16[4,2,128,256]{3,2,1,0:T(8,128)(2,1)S(1)} %get-tuple-element.70.strip_grad, bf16[192,512]{1,0:T(8,128)(2,1)S(1)} %bitcast.16, bf16[512,256]{1,0:T(8,128)(2,1)S(1)} %copy-done.6, bf16[512,512]{1,0:T(8,128)(2,1)S(1)} %copy-done.5), custom_call_target="tpu_custom_call" | custom-call | bytes 3145728 | tf_op jit(solution)/shard_map/pallas_call | solution.py:212
  (30 shorter events, 0.1 us)
Async XLA Ops:
  0.0 19.5 %collective-permute-start.2 = (bf16[8,128,256]{2,1,0:T(8,128)(2,1)}, bf16[8,128,256]{2,1,0:T(8,128)(2,1)S(1)}, u32[]{:S(2)}, u32[]{:S(2)}) collective-permute-start(bf16[8,128,256]{2,1,0:T(8,128)(2,1)} %refs_7_.1), channel_id=1, source_target_pairs={{4,8},{12,16},{20,24},{8,4},{16,12},{24,20},{5,9},{13,17},{21,25},... | collective-permute-start | bytes 1572872 | tf_op jit(solution)/shard_map/ppermute | solution.py:721
  4.5 15.1 %collective-permute-start.1 = (bf16[8,128,256]{2,1,0:T(8,128)(2,1)}, bf16[8,128,256]{2,1,0:T(8,128)(2,1)S(1)}, u32[]{:S(2)}, u32[]{:S(2)}) collective-permute-start(bf16[8,128,256]{2,1,0:T(8,128)(2,1)} %refs_7_.1), channel_id=1, source_target_pairs={{0,4},{8,12},{16,20},{24,28},{4,0},{12,8},{20,16},{28,24},{1,5},{9... | collective-permute-start | bytes 1572872 | tf_op jit(solution)/shard_map/ppermute | solution.py:720
  5.8 19.5 %collective-permute-start = (bf16[528,256]{1,0:T(8,128)(2,1)S(1)}, bf16[528,256]{1,0:T(8,128)(2,1)S(1)}, u32[]{:S(2)}, u32[]{:S(2)}) collective-permute-start(bf16[528,256]{1,0:T(8,128)(2,1)S(1)} %get-tuple-element.39), channel_id=1, source_target_pairs={{0,4},{8,12},{16,20},{24,28},{4,0},{12,8},{20,16},{28,24},{1,5},{9... | collective-permute-start | bytes 811016 | tf_op jit(solution)/shard_map/ppermute | solution.py:724
  6.3 19.0 %collective-permute-start.3 = (bf16[528,256]{1,0:T(8,128)(2,1)S(1)}, bf16[528,256]{1,0:T(8,128)(2,1)S(1)}, u32[]{:S(2)}, u32[]{:S(2)}) collective-permute-start(bf16[528,256]{1,0:T(8,128)(2,1)S(1)} %get-tuple-element.49), channel_id=1, source_target_pairs={{4,8},{12,16},{20,24},{8,4},{16,12},{24,20},{5,9},{13,17},{21,25},... | collective-permute-start | bytes 811016 | tf_op jit(solution)/shard_map/ppermute | solution.py:725
  12.7 28.1 %all-to-all-start = ((bf16[32,16,384]{2,1,0:T(8,128)(2,1)}), bf16[32,16,384]{2,1,0:T(8,128)(2,1)S(1)}, u32[]{:S(2)}, u32[]{:S(2)}) async-start(bf16[32,16,384]{2,1,0:T(8,128)(2,1)} %bitcast.4), calls=%async_computation | async-start | bytes 786432 | tf_op jit(solution)/shard_map/all_to_all | solution.py:704
  17.8 1.8 %copy-start.2 = (bf16[8,128,256]{2,1,0:T(8,128)(2,1)S(1)}, bf16[8,128,256]{2,1,0:T(8,128)(2,1)}, u32[]{:S(2)}) copy-start(bf16[8,128,256]{2,1,0:T(8,128)(2,1)} %refs_7_.1) | copy-start | bytes 1572868
  19.6 5.8 %copy-start = (bf16[8,128,256]{2,1,0:T(8,128)(2,1)S(1)}, bf16[8,128,256]{2,1,0:T(8,128)(2,1)}, u32[]{:S(2)}) copy-start(bf16[8,128,256]{2,1,0:T(8,128)(2,1)} %refs_8_.2) | copy-start | bytes 1572868
  25.5 11.3 %collective-permute-start.7 = (bf16[43,8,256]{2,1,0:T(8,128)(2,1)S(1)}, bf16[43,8,256]{2,1,0:T(8,128)(2,1)S(1)}, u32[]{:S(2)}, u32[]{:S(2)}) collective-permute-start(bf16[43,8,256]{2,1,0:T(8,128)(2,1)S(1)} %get-tuple-element.55), channel_id=1, source_target_pairs={{1,2},{2,1},{5,6},{6,5},{9,10},{10,9},{13,14},{14,13},{17,18},{18,... | collective-permute-start | bytes 528392 | tf_op jit(solution)/shard_map/ppermute | solution.py:731
  26.4 10.5 %collective-permute-start.8 = (bf16[43,8,256]{2,1,0:T(8,128)(2,1)S(1)}, bf16[43,8,256]{2,1,0:T(8,128)(2,1)S(1)}, u32[]{:S(2)}, u32[]{:S(2)}) collective-permute-start(bf16[43,8,256]{2,1,0:T(8,128)(2,1)S(1)} %get-tuple-element.56), channel_id=1, source_target_pairs={{0,1},{2,3},{1,0},{3,2},{4,5},{6,7},{5,4},{7,6},{8,9},{10,11},{9,8... | collective-permute-start | bytes 528392 | tf_op jit(solution)/shard_map/ppermute | solution.py:732
  34.1 10.7 %collective-permute-start.4 = (bf16[2,112,256]{2,1,0:T(8,128)(2,1)S(1)}, bf16[2,112,256]{2,1,0:T(8,128)(2,1)S(1)}, u32[]{:S(2)}, u32[]{:S(2)}) collective-permute-start(bf16[2,112,256]{2,1,0:T(8,128)(2,1)S(1)} %get-tuple-element.52), channel_id=1, source_target_pairs={{0,2},{1,3},{2,0},{3,1},{4,6},{5,7},{6,4},{7,5},{8,10},{9,11},{10,... | collective-permute-start | bytes 344072 | tf_op jit(solution)/shard_map/ppermute | solution.py:741
  34.2 11.7 %collective-permute-start.5 = (bf16[2,112,256]{2,1,0:T(8,128)(2,1)S(1)}, bf16[2,112,256]{2,1,0:T(8,128)(2,1)S(1)}, u32[]{:S(2)}, u32[]{:S(2)}) collective-permute-start(bf16[2,112,256]{2,1,0:T(8,128)(2,1)S(1)} %get-tuple-element.53), channel_id=1, source_target_pairs={{0,3},{1,2},{2,1},{3,0},{4,7},{5,6},{6,5},{7,4},{8,11},{9,10},{10,... | collective-permute-start | bytes 344072 | tf_op jit(solution)/shard_map/ppermute | solution.py:741
  36.3 9.6 %collective-permute-start.6 = (bf16[2,112,256]{2,1,0:T(8,128)(2,1)S(1)}, bf16[2,112,256]{2,1,0:T(8,128)(2,1)S(1)}, u32[]{:S(2)}, u32[]{:S(2)}) collective-permute-start(bf16[2,112,256]{2,1,0:T(8,128)(2,1)S(1)} %get-tuple-element.54), channel_id=1, source_target_pairs={{0,1},{1,0},{2,3},{3,2},{4,5},{5,4},{6,7},{7,6},{8,9},{9,8},{10,11... | collective-permute-start | bytes 344072 | tf_op jit(solution)/shard_map/ppermute | solution.py:741
  36.8 8.0 %copy-start.3 = (bf16[384,384]{1,0:T(8,128)(2,1)S(1)}, bf16[384,384]{1,0:T(8,128)(2,1)}, u32[]{:S(2)}) copy-start(bf16[384,384]{1,0:T(8,128)(2,1)} %mix.3) | copy-start | bytes 884740
  36.8 8.0 %copy-start.7 = (bf16[128,128]{1,0:T(8,128)(2,1)S(1)}, bf16[128,128]{1,0:T(8,128)(2,1)}, u32[]{:S(2)}) copy-start(bf16[128,128]{1,0:T(8,128)(2,1)} %constant.36.clone.table) | copy-start | bytes 98308
  40.7 7.5 %copy-start.1 = (bf16[512,512]{1,0:T(8,128)(2,1)S(1)}, bf16[512,512]{1,0:T(8,128)(2,1)}, u32[]{:S(2)}) copy-start(bf16[512,512]{1,0:T(8,128)(2,1)} %constant.34.clone.table.refs_9_) | copy-start | bytes 1572868
  40.7 7.5 %copy-start.8 = (bf16[192,256]{1,0:T(8,128)(2,1)S(1)}, bf16[192,256]{1,0:T(8,128)(2,1)}, u32[]{:S(2)}) copy-start(bf16[192,256]{1,0:T(8,128)(2,1)} %refs_8_.3) | copy-start | bytes 294916
  40.8 7.4 %collective-permute-start.9 = (bf16[2,16,256]{2,1,0:T(8,128)(2,1)S(1)}, bf16[2,16,256]{2,1,0:T(8,128)(2,1)S(1)}, u32[]{:S(2)}, u32[]{:S(2)}) collective-permute-start(bf16[2,16,256]{2,1,0:T(8,128)(2,1)S(1)} %get-tuple-element.65), channel_id=1, source_target_pairs={{0,2},{1,3},{2,0},{3,1},{4,6},{5,7},{6,4},{7,5},{8,10},{9,11},{10,... | collective-permute-start | bytes 49160 | tf_op jit(solution)/shard_map/ppermute | solution.py:741
  41.8 6.4 %collective-permute-start.10 = (bf16[2,16,256]{2,1,0:T(8,128)(2,1)S(1)}, bf16[2,16,256]{2,1,0:T(8,128)(2,1)S(1)}, u32[]{:S(2)}, u32[]{:S(2)}) collective-permute-start(bf16[2,16,256]{2,1,0:T(8,128)(2,1)S(1)} %get-tuple-element.66), channel_id=1, source_target_pairs={{0,3},{1,2},{2,1},{3,0},{4,7},{5,6},{6,5},{7,4},{8,11},{9,10},{10,... | collective-permute-start | bytes 49160 | tf_op jit(solution)/shard_map/ppermute | solution.py:741
  44.9 3.3 %collective-permute-start.11 = (bf16[2,16,256]{2,1,0:T(8,128)(2,1)S(1)}, bf16[2,16,256]{2,1,0:T(8,128)(2,1)S(1)}, u32[]{:S(2)}, u32[]{:S(2)}) collective-permute-start(bf16[2,16,256]{2,1,0:T(8,128)(2,1)S(1)} %get-tuple-element.67), channel_id=1, source_target_pairs={{0,1},{1,0},{2,3},{3,2},{4,5},{5,4},{6,7},{7,6},{8,9},{9,8},{10,11... | collective-permute-start | bytes 49160 | tf_op jit(solution)/shard_map/ppermute | solution.py:741
  45.8 21.1 %copy-start.9 = (bf16[128,128]{1,0:T(8,128)(2,1)S(1)}, bf16[128,128]{1,0:T(8,128)(2,1)}, u32[]{:S(2)}) copy-start(bf16[128,128]{1,0:T(8,128)(2,1)} %constant.35.clone.back_table) | copy-start | bytes 98308
  66.9 16.8 %copy-start.4 = (bf16[512,192]{0,1:T(8,128)(2,1)S(1)}, bf16[512,192]{0,1:T(8,128)(2,1)}, u32[]{:S(2)}) copy-start(bf16[512,192]{0,1:T(8,128)(2,1)} %param.20) | copy-start | bytes 589828
  66.9 16.8 %copy-start.5 = (bf16[512,512]{1,0:T(8,128)(2,1)S(1)}, bf16[512,512]{1,0:T(8,128)(2,1)}, u32[]{:S(2)}) copy-start(bf16[512,512]{1,0:T(8,128)(2,1)} %constant.33.clone.table) | copy-start | bytes 1572868
  66.9 16.8 %copy-start.6 = (bf16[512,256]{1,0:T(8,128)(2,1)S(1)}, bf16[512,256]{1,0:T(8,128)(2,1)}, u32[]{:S(2)}) copy-start(bf16[512,256]{1,0:T(8,128)(2,1)} %weight_local.1) | copy-start | bytes 786436

commit v21 on v20

--- a/solution.py
+++ b/solution.py
@@ -435,7 +435,7 @@
 
 
 def steps_of(count):
-    return [0, *range(2, count), 1] if count > 1 else [0]
+    return [0, *reversed(range(1, count))]
 
 
 def deal(place, out, pieces):
@@ -461,7 +461,7 @@
 
 
 TILE_BLOCKS = (2, 2, 2, 2)
-SIDE_BLOCKS = (5, 4, 6, 4)
+SIDE_BLOCKS = (4, 4, 4, 4)
 
 
 def tile_forward_kernel(

time: 87 us -> 87.7 us (level)
  waiting for transfers between devices: 3.39 us -> 0.65 us
  blocking collectives: 33.4 us -> 35.3 us
  starting transfers between devices: 23.8 us -> 25.2 us
    ppermute x6, waiting for transfers between devices: 3.37 us -> 0.63 us  [dealt(): result.append(lax.ppermute(piece, 'col', swaps) if step else piece)]
    all_to_all x2, blocking collectives: 33.4 us -> 35.3 us  [swap(): lax.all_to_all(spectrum, ('col', 'row'), split_axis=0, concat_axis=0, til...]
    ppermute x6, starting transfers between devices: 5.77 us -> 7.23 us  [dealt(): result.append(lax.ppermute(piece, 'col', swaps) if step else piece)]
  transfers between devices with their start and end apart: 13 -> 13, of which waited for: 2 -> 1; matrix products, arithmetic and copies ran while one was open for 0% -> 0% of each run, Pallas kernels for 24% -> 24%
where the time goes in v21:
time: 87.7 us; the launch traced here: 86.4 us
  blocking collectives  35.3 us (40%)
  starting transfers between devices  25.2 us (29%)
  Pallas kernels  24.7 us (28%)
    all_to_all x2, blocking collectives, swap(): lax.all_to_all(spectrum, ('col', 'row'), split_axis=0, concat_axis=0, til...  35.3 us
    ppermute x6, starting transfers between devices, dealt(): result.append(lax.ppermute(piece, 'col', swaps) if step else piece)  7.23 us
    pallas_call x1, Pallas kernels, tile_forward(): pl.pallas_call(tile_forward_kernel, out_shape=shapes, in_specs=[pl.BlockS...  5.74 us
    all_to_all x1, starting transfers between devices, swap(): lax.all_to_all(spectrum, ('col', 'row'), split_axis=0, concat_axis=0, til...  5.12 us
    ppermute x1, starting transfers between devices, shards(): late = lax.ppermute(features, 'row', pairs('row', 1))  4.5 us
    pallas_call x1, Pallas kernels, sides(): pl.pallas_call(side_kernel, out_shape=shapes, in_specs=[pl.BlockSpec(memo...  4.03 us
    ppermute x1, starting transfers between devices, shards(): early_edge = lax.ppermute(early_edge, 'col', pairs('col', 0))  3.88 us
    pallas_call x1, Pallas kernels, tile_backward(): pl.pallas_call(tile_backward_kernel, out_shape=shapes, in_specs=[pl.Block...  3.86 us
  transfers between devices with their start and end apart: 13, of which 1 were waited for; matrix products, arithmetic and copies ran while one was open for 0% of the time, Pallas kernels for 24%

profile of v21, /device:TPU:1, one launch (start us, length us, event | category | flops | bytes accessed | tf_op | source)
XLA Modules:
  0.0 86.4 jit_solution(10167283204603160261)
XLA Ops:
  0.0 4.5 %collective-permute-start.2 = (bf16[8,128,256]{2,1,0:T(8,128)(2,1)}, bf16[8,128,256]{2,1,0:T(8,128)(2,1)S(1)}, u32[]{:S(2)}, u32[]{:S(2)}) collective-permute-start(bf16[8,128,256]{2,1,0:T(8,128)(2,1)} %refs_7_.1), channel_id=1, source_target_pairs={{4,8},{12,16},{20,24},{8,4},{16,12},{24,20},{5,9},{13,17},{21,25},... | collective-permute-start | bytes 1572872 | tf_op jit(solution)/shard_map/ppermute | solution.py:721
  4.5 0.1 collective-permute-start.1
  4.6 1.1 %shard_map.136 = (bf16[528,256]{1,0:T(8,128)(2,1)S(1)}, bf16[528,256]{1,0:T(8,128)(2,1)S(1)}, bf16[1,128,256]{2,1,0:T(8,128)(2,1)S(1)}) custom-call(s32[1]{0:T(128)} %bitcast.col, s32[1]{0:T(128)} %bitcast.1.low, bf16[1024,256]{1,0:T(8,128)(2,1)} %bitcast.10, s32[8,128]{1,0:T(8,128)} %mask.1), custom_call_target="tpu_custom_call" | custom-call | bytes 1048576 | tf_op jit(solution)/shard_map/pallas_call | solution.py:277
  5.7 0.1 and_convert_fusion.ok
  5.8 0.5 collective-permute-start
  6.3 3.0 %collective-permute-start.3 = (bf16[528,256]{1,0:T(8,128)(2,1)S(1)}, bf16[528,256]{1,0:T(8,128)(2,1)S(1)}, u32[]{:S(2)}, u32[]{:S(2)}) collective-permute-start(bf16[528,256]{1,0:T(8,128)(2,1)S(1)} %get-tuple-element.49), channel_id=1, source_target_pairs={{4,8},{12,16},{20,24},{8,4},{16,12},{24,20},{5,9},{13,17},{21,25},... | collective-permute-start | bytes 811016 | tf_op jit(solution)/shard_map/ppermute | solution.py:725
  9.4 3.3 %shard_map.137 = bf16[512,384]{1,0:T(8,128)(2,1)} custom-call(bf16[2,512,512]{2,1,0:T(8,128)(2,1)} %signal, bf16[192,512]{1,0:T(8,128)(2,1)} %bitcast.15, bf16[512,512]{1,0:T(8,128)(2,1)} %constant.34.clone.table.refs_9_), custom_call_target="tpu_custom_call" | custom-call | bytes 2097152 | tf_op jit(solution)/shard_map/pallas_call | solution.py:125
  12.7 5.1 %all-to-all-start = ((bf16[32,16,384]{2,1,0:T(8,128)(2,1)}), bf16[32,16,384]{2,1,0:T(8,128)(2,1)S(1)}, u32[]{:S(2)}, u32[]{:S(2)}) async-start(bf16[32,16,384]{2,1,0:T(8,128)(2,1)} %bitcast.4), calls=%async_computation | async-start | bytes 786432 | tf_op jit(solution)/shard_map/all_to_all | solution.py:704
  17.8 1.7 %shard_map.138 = (bf16[3,3,256,256]{3,2,1,0:T(8,128)(2,1)S(1)}, bf16[3,3,256,256]{3,2,1,0:T(8,128)(2,1)S(1)}) custom-call(bf16[3,3,256,256]{3,2,1,0:T(8,128)(2,1)} %refs_0_, bf16[3,3,256,256]{3,2,1,0:T(8,128)(2,1)} %refs_1_.1), custom_call_target="tpu_custom_call" | custom-call | bytes 5242880 | tf_op jit(solution)/shard_map/pallas_call | solution.py:299
  19.6 0.0 copy-done.2
  19.6 5.7 %shard_map.139 = (f32[2048,256]{1,0:T(8,128)S(1)}, f32[1536,256]{1,0:T(8,128)S(1)}) custom-call(s32[1]{0:T(128)} %bitcast.col, s32[1]{0:T(128)} %bitcast.1.low, bf16[8,128,256]{2,1,0:T(8,128)(2,1)S(1)} %collective-permute-done.1.early.refs_0_.refs_5_, bf16[8,128,256]{2,1,0:T(8,128)(2,1)S(1)} %copy-done.2, ...), custom_call_target="tpu_custom_call" | custom-call | flops 5435817984 | bytes 8388608 | tf_op jit(solution)/shard_map/pallas_call | solution.py:604
  25.4 0.1 shard_map.141
  25.5 0.9 collective-permute-start.7
  26.4 3.9 %collective-permute-start.8 = (bf16[43,8,256]{2,1,0:T(8,128)(2,1)S(1)}, bf16[43,8,256]{2,1,0:T(8,128)(2,1)S(1)}, u32[]{:S(2)}, u32[]{:S(2)}) collective-permute-start(bf16[43,8,256]{2,1,0:T(8,128)(2,1)S(1)} %get-tuple-element.56), channel_id=1, source_target_pairs={{0,1},{2,3},{1,0},{3,2},{4,5},{6,7},{5,4},{7,6},{8,9},{10,11},{9,8... | collective-permute-start | bytes 528392 | tf_op jit(solution)/shard_map/ppermute | solution.py:732
  30.2 3.9 %shard_map.140 = (bf16[2,112,256]{2,1,0:T(8,128)(2,1)S(1)}, bf16[2,112,256]{2,1,0:T(8,128)(2,1)S(1)}, bf16[2,112,256]{2,1,0:T(8,128)(2,1)S(1)}, bf16[2,112,256]{2,1,0:T(8,128)(2,1)S(1)}) custom-call(s32[1]{0:T(128)} %bitcast.col, s32[1]{0:T(128)} %bitcast.1.low, f32[2048,256]{1,0:T(8,128)S(1)} %get-tuple-element.46.pre, ...), custom_call_target="tpu_custom_call" | custom-call | flops 3019898880 | bytes 8388608 | tf_op jit(solution)/shard_map/pallas_call | solution.py:628
  34.1 1.2 %collective-permute-start.4 = (bf16[2,112,256]{2,1,0:T(8,128)(2,1)S(1)}, bf16[2,112,256]{2,1,0:T(8,128)(2,1)S(1)}, u32[]{:S(2)}, u32[]{:S(2)}) collective-permute-start(bf16[2,112,256]{2,1,0:T(8,128)(2,1)S(1)} %get-tuple-element.52), channel_id=1, source_target_pairs={{0,3},{1,2},{2,1},{3,0},{4,7},{5,6},{6,5},{7,4},{8,11},{9,10},{10,... | collective-permute-start | bytes 344072 | tf_op jit(solution)/shard_map/ppermute | solution.py:741
  35.4 0.0 collective-permute-start.5
  35.4 2.3 %collective-permute-start.6 = (bf16[2,112,256]{2,1,0:T(8,128)(2,1)S(1)}, bf16[2,112,256]{2,1,0:T(8,128)(2,1)S(1)}, u32[]{:S(2)}, u32[]{:S(2)}) collective-permute-start(bf16[2,112,256]{2,1,0:T(8,128)(2,1)S(1)} %get-tuple-element.54), channel_id=1, source_target_pairs={{0,1},{1,0},{2,3},{3,2},{4,5},{5,4},{6,7},{7,6},{8,9},{9,8},{10,11... | collective-permute-start | bytes 344072 | tf_op jit(solution)/shard_map/ppermute | solution.py:741
  37.7 0.0 copy-start.7
  37.8 4.0 %shard_map.142 = (bf16[2,16,256]{2,1,0:T(8,128)(2,1)S(1)}, bf16[2,16,256]{2,1,0:T(8,128)(2,1)S(1)}, bf16[2,16,256]{2,1,0:T(8,128)(2,1)S(1)}, bf16[2,16,256]{2,1,0:T(8,128)(2,1)S(1)}) custom-call(s32[1]{0:T(128)} %bitcast.col, s32[1]{0:T(128)} %bitcast.1.low, bf16[43,8,256]{2,1,0:T(8,128)(2,1)S(1)} %collective-permute-done.7.late, ...), custom_call_target="tpu_custom_call" | custom-call | flops 3170893824 | bytes 4194304 | tf_op jit(solution)/shard_map/pallas_call | solution.py:651
  41.8 0.0 copy-start.1
  41.8 1.3 %collective-permute-start.9 = (bf16[2,16,256]{2,1,0:T(8,128)(2,1)S(1)}, bf16[2,16,256]{2,1,0:T(8,128)(2,1)S(1)}, u32[]{:S(2)}, u32[]{:S(2)}) collective-permute-start(bf16[2,16,256]{2,1,0:T(8,128)(2,1)S(1)} %get-tuple-element.65), channel_id=1, source_target_pairs={{0,3},{1,2},{2,1},{3,0},{4,7},{5,6},{6,5},{7,4},{8,11},{9,10},{10,... | collective-permute-start | bytes 49160 | tf_op jit(solution)/shard_map/ppermute | solution.py:741
  43.1 0.0 collective-permute-start.10
  43.1 2.3 %collective-permute-start.11 = (bf16[2,16,256]{2,1,0:T(8,128)(2,1)S(1)}, bf16[2,16,256]{2,1,0:T(8,128)(2,1)S(1)}, u32[]{:S(2)}, u32[]{:S(2)}) collective-permute-start(bf16[2,16,256]{2,1,0:T(8,128)(2,1)S(1)} %get-tuple-element.67), channel_id=1, source_target_pairs={{0,1},{1,0},{2,3},{3,2},{4,5},{5,4},{6,7},{7,6},{8,9},{9,8},{10,11... | collective-permute-start | bytes 49160 | tf_op jit(solution)/shard_map/ppermute | solution.py:741
  45.5 1.0 %shard_map.143.slope = f32[2,512,192]{2,1,0:T(8,128)S(1)} custom-call(bf16[512,384]{1,0:T(8,128)(2,1)S(1)} %bitcast.11, bf16[384,384]{1,0:T(8,128)(2,1)S(1)} %copy-done.3, bf16[128,128]{1,0:T(8,128)(2,1)S(1)} %copy-done.7), custom_call_target="tpu_custom_call" | custom-call | bytes 1507328 | tf_op jit(solution)/shard_map/pallas_call | solution.py:30
  46.4 0.0 copy-start.9
  46.5 0.6 collective-permute-done.10.refs_6_
  47.1 0.9 %shard_map.144 = (bf16[512,384]{1,0:T(8,128)(2,1)S(1)}, bf16[4,2,128,256]{3,2,1,0:T(8,128)(2,1)S(1)}) custom-call(s32[1]{0:T(128)} %bitcast.col, s32[1]{0:T(128)} %bitcast.1.low, bf16[2,112,256]{2,1,0:T(8,128)(2,1)S(1)} %get-tuple-element.51.refs_0_, bf16[2,112,256]{2,1,0:T(8,128)(2,1)S(1)} %collective-permute-done.4.refs_1_, ...), custom_call_target="tpu_custom_call" | custom-call | bytes 2097152 | tf_op jit(solution)/shard_map/pallas_call | solution.py:91
  48.0 19.6 %all_to_all.34 = bf16[32,16,384]{2,1,0:T(8,128)(2,1)S(1)} all-to-all(bf16[32,16,384]{2,1,0:T(8,128)(2,1)S(1)} %bitcast.17), channel_id=1, replica_groups=mesh['row'=8,'col'=4] {'col','row'}, dimensions={0} | all-to-all | bytes 786432 | tf_op jit(solution)/shard_map/all_to_all | solution.py:704
  67.6 1.2 %shard_map.145 = bf16[512,384]{1,0:T(8,128)(2,1)S(1)} custom-call(bf16[512,384]{1,0:T(8,128)(2,1)S(1)} %bitcast.12, f32[2,512,192]{2,1,0:T(8,128)S(1)} %shard_map.143.slope, bf16[384,384]{1,0:T(8,128)(2,1)S(1)} %copy-done.3, bf16[128,128]{1,0:T(8,128)(2,1)S(1)} %copy-done.7, bf16[128,128]{1,0:T(8,128)(2,1)S(1)} %copy-done.9), custom_call_target="tpu_custom_call" | custom-call | bytes 1933312 | tf_op jit(solution)/shard_map/pallas_call | solution.py:30
  68.8 15.6 %all_to_all.35 = bf16[32,16,384]{2,1,0:T(8,128)(2,1)S(1)} all-to-all(bf16[32,16,384]{2,1,0:T(8,128)(2,1)S(1)} %bitcast.13), channel_id=1, replica_groups=mesh['row'=8,'col'=4] {'col','row'}, dimensions={0} | all-to-all | bytes 786432 | tf_op jit(solution)/shard_map/all_to_all | solution.py:704
  84.4 1.8 %shard_map.146 = bf16[2,512,512]{2,1,0:T(8,128)(2,1)} custom-call(bf16[512,384]{1,0:T(8,128)(2,1)S(1)} %bitcast.14, bf16[4,2,128,256]{3,2,1,0:T(8,128)(2,1)S(1)} %get-tuple-element.70.strip_grad, bf16[192,512]{1,0:T(8,128)(2,1)S(1)} %bitcast.16, bf16[512,256]{1,0:T(8,128)(2,1)S(1)} %copy-done.6, bf16[512,512]{1,0:T(8,128)(2,1)S(1)} %copy-done.5), custom_call_target="tpu_custom_call" | custom-call | bytes 3145728 | tf_op jit(solution)/shard_map/pallas_call | solution.py:212
  (30 shorter events, 0.1 us)
Async XLA Ops:
  0.0 19.5 %collective-permute-start.2 = (bf16[8,128,256]{2,1,0:T(8,128)(2,1)}, bf16[8,128,256]{2,1,0:T(8,128)(2,1)S(1)}, u32[]{:S(2)}, u32[]{:S(2)}) collective-permute-start(bf16[8,128,256]{2,1,0:T(8,128)(2,1)} %refs_7_.1), channel_id=1, source_target_pairs={{4,8},{12,16},{20,24},{8,4},{16,12},{24,20},{5,9},{13,17},{21,25},... | collective-permute-start | bytes 1572872 | tf_op jit(solution)/shard_map/ppermute | solution.py:721
  4.5 15.1 %collective-permute-start.1 = (bf16[8,128,256]{2,1,0:T(8,128)(2,1)}, bf16[8,128,256]{2,1,0:T(8,128)(2,1)S(1)}, u32[]{:S(2)}, u32[]{:S(2)}) collective-permute-start(bf16[8,128,256]{2,1,0:T(8,128)(2,1)} %refs_7_.1), channel_id=1, source_target_pairs={{0,4},{8,12},{16,20},{24,28},{4,0},{12,8},{20,16},{28,24},{1,5},{9... | collective-permute-start | bytes 1572872 | tf_op jit(solution)/shard_map/ppermute | solution.py:720
  5.8 19.5 %collective-permute-start = (bf16[528,256]{1,0:T(8,128)(2,1)S(1)}, bf16[528,256]{1,0:T(8,128)(2,1)S(1)}, u32[]{:S(2)}, u32[]{:S(2)}) collective-permute-start(bf16[528,256]{1,0:T(8,128)(2,1)S(1)} %get-tuple-element.39), channel_id=1, source_target_pairs={{0,4},{8,12},{16,20},{24,28},{4,0},{12,8},{20,16},{28,24},{1,5},{9... | collective-permute-start | bytes 811016 | tf_op jit(solution)/shard_map/ppermute | solution.py:724
  6.3 19.0 %collective-permute-start.3 = (bf16[528,256]{1,0:T(8,128)(2,1)S(1)}, bf16[528,256]{1,0:T(8,128)(2,1)S(1)}, u32[]{:S(2)}, u32[]{:S(2)}) collective-permute-start(bf16[528,256]{1,0:T(8,128)(2,1)S(1)} %get-tuple-element.49), channel_id=1, source_target_pairs={{4,8},{12,16},{20,24},{8,4},{16,12},{24,20},{5,9},{13,17},{21,25},... | collective-permute-start | bytes 811016 | tf_op jit(solution)/shard_map/ppermute | solution.py:725
  12.7 29.1 %all-to-all-start = ((bf16[32,16,384]{2,1,0:T(8,128)(2,1)}), bf16[32,16,384]{2,1,0:T(8,128)(2,1)S(1)}, u32[]{:S(2)}, u32[]{:S(2)}) async-start(bf16[32,16,384]{2,1,0:T(8,128)(2,1)} %bitcast.4), calls=%async_computation | async-start | bytes 786432 | tf_op jit(solution)/shard_map/all_to_all | solution.py:704
  17.8 1.8 %copy-start.2 = (bf16[8,128,256]{2,1,0:T(8,128)(2,1)S(1)}, bf16[8,128,256]{2,1,0:T(8,128)(2,1)}, u32[]{:S(2)}) copy-start(bf16[8,128,256]{2,1,0:T(8,128)(2,1)} %refs_7_.1) | copy-start | bytes 1572868
  19.6 5.8 %copy-start = (bf16[8,128,256]{2,1,0:T(8,128)(2,1)S(1)}, bf16[8,128,256]{2,1,0:T(8,128)(2,1)}, u32[]{:S(2)}) copy-start(bf16[8,128,256]{2,1,0:T(8,128)(2,1)} %refs_8_.2) | copy-start | bytes 1572868
  25.5 12.2 %collective-permute-start.7 = (bf16[43,8,256]{2,1,0:T(8,128)(2,1)S(1)}, bf16[43,8,256]{2,1,0:T(8,128)(2,1)S(1)}, u32[]{:S(2)}, u32[]{:S(2)}) collective-permute-start(bf16[43,8,256]{2,1,0:T(8,128)(2,1)S(1)} %get-tuple-element.55), channel_id=1, source_target_pairs={{1,2},{2,1},{5,6},{6,5},{9,10},{10,9},{13,14},{14,13},{17,18},{18,... | collective-permute-start | bytes 528392 | tf_op jit(solution)/shard_map/ppermute | solution.py:731
  26.4 11.4 %collective-permute-start.8 = (bf16[43,8,256]{2,1,0:T(8,128)(2,1)S(1)}, bf16[43,8,256]{2,1,0:T(8,128)(2,1)S(1)}, u32[]{:S(2)}, u32[]{:S(2)}) collective-permute-start(bf16[43,8,256]{2,1,0:T(8,128)(2,1)S(1)} %get-tuple-element.56), channel_id=1, source_target_pairs={{0,1},{2,3},{1,0},{3,2},{4,5},{6,7},{5,4},{7,6},{8,9},{10,11},{9,8... | collective-permute-start | bytes 528392 | tf_op jit(solution)/shard_map/ppermute | solution.py:732
  34.1 9.0 %collective-permute-start.4 = (bf16[2,112,256]{2,1,0:T(8,128)(2,1)S(1)}, bf16[2,112,256]{2,1,0:T(8,128)(2,1)S(1)}, u32[]{:S(2)}, u32[]{:S(2)}) collective-permute-start(bf16[2,112,256]{2,1,0:T(8,128)(2,1)S(1)} %get-tuple-element.52), channel_id=1, source_target_pairs={{0,3},{1,2},{2,1},{3,0},{4,7},{5,6},{6,5},{7,4},{8,11},{9,10},{10,... | collective-permute-start | bytes 344072 | tf_op jit(solution)/shard_map/ppermute | solution.py:741
  35.4 11.1 %collective-permute-start.5 = (bf16[2,112,256]{2,1,0:T(8,128)(2,1)S(1)}, bf16[2,112,256]{2,1,0:T(8,128)(2,1)S(1)}, u32[]{:S(2)}, u32[]{:S(2)}) collective-permute-start(bf16[2,112,256]{2,1,0:T(8,128)(2,1)S(1)} %get-tuple-element.53), channel_id=1, source_target_pairs={{0,2},{1,3},{2,0},{3,1},{4,6},{5,7},{6,4},{7,5},{8,10},{9,11},{10,... | collective-permute-start | bytes 344072 | tf_op jit(solution)/shard_map/ppermute | solution.py:741
  35.4 11.1 %collective-permute-start.6 = (bf16[2,112,256]{2,1,0:T(8,128)(2,1)S(1)}, bf16[2,112,256]{2,1,0:T(8,128)(2,1)S(1)}, u32[]{:S(2)}, u32[]{:S(2)}) collective-permute-start(bf16[2,112,256]{2,1,0:T(8,128)(2,1)S(1)} %get-tuple-element.54), channel_id=1, source_target_pairs={{0,1},{1,0},{2,3},{3,2},{4,5},{5,4},{6,7},{7,6},{8,9},{9,8},{10,11... | collective-permute-start | bytes 344072 | tf_op jit(solution)/shard_map/ppermute | solution.py:741
  37.7 7.7 %copy-start.3 = (bf16[384,384]{1,0:T(8,128)(2,1)S(1)}, bf16[384,384]{1,0:T(8,128)(2,1)}, u32[]{:S(2)}) copy-start(bf16[384,384]{1,0:T(8,128)(2,1)} %mix.3) | copy-start | bytes 884740
  37.7 7.7 %copy-start.7 = (bf16[128,128]{1,0:T(8,128)(2,1)S(1)}, bf16[128,128]{1,0:T(8,128)(2,1)}, u32[]{:S(2)}) copy-start(bf16[128,128]{1,0:T(8,128)(2,1)} %constant.36.clone.table) | copy-start | bytes 98308
  41.8 5.3 %copy-start.1 = (bf16[512,512]{1,0:T(8,128)(2,1)S(1)}, bf16[512,512]{1,0:T(8,128)(2,1)}, u32[]{:S(2)}) copy-start(bf16[512,512]{1,0:T(8,128)(2,1)} %constant.34.clone.table.refs_9_) | copy-start | bytes 1572868
  41.8 5.3 %copy-start.8 = (bf16[192,256]{1,0:T(8,128)(2,1)S(1)}, bf16[192,256]{1,0:T(8,128)(2,1)}, u32[]{:S(2)}) copy-start(bf16[192,256]{1,0:T(8,128)(2,1)} %refs_8_.3) | copy-start | bytes 294916
  41.8 4.6 %collective-permute-start.9 = (bf16[2,16,256]{2,1,0:T(8,128)(2,1)S(1)}, bf16[2,16,256]{2,1,0:T(8,128)(2,1)S(1)}, u32[]{:S(2)}, u32[]{:S(2)}) collective-permute-start(bf16[2,16,256]{2,1,0:T(8,128)(2,1)S(1)} %get-tuple-element.65), channel_id=1, source_target_pairs={{0,3},{1,2},{2,1},{3,0},{4,7},{5,6},{6,5},{7,4},{8,11},{9,10},{10,... | collective-permute-start | bytes 49160 | tf_op jit(solution)/shard_map/ppermute | solution.py:741
  43.1 4.0 %collective-permute-start.10 = (bf16[2,16,256]{2,1,0:T(8,128)(2,1)S(1)}, bf16[2,16,256]{2,1,0:T(8,128)(2,1)S(1)}, u32[]{:S(2)}, u32[]{:S(2)}) collective-permute-start(bf16[2,16,256]{2,1,0:T(8,128)(2,1)S(1)} %get-tuple-element.66), channel_id=1, source_target_pairs={{0,2},{1,3},{2,0},{3,1},{4,6},{5,7},{6,4},{7,5},{8,10},{9,11},{10,... | collective-permute-start | bytes 49160 | tf_op jit(solution)/shard_map/ppermute | solution.py:741
  43.1 4.0 %collective-permute-start.11 = (bf16[2,16,256]{2,1,0:T(8,128)(2,1)S(1)}, bf16[2,16,256]{2,1,0:T(8,128)(2,1)S(1)}, u32[]{:S(2)}, u32[]{:S(2)}) collective-permute-start(bf16[2,16,256]{2,1,0:T(8,128)(2,1)S(1)} %get-tuple-element.67), channel_id=1, source_target_pairs={{0,1},{1,0},{2,3},{3,2},{4,5},{5,4},{6,7},{7,6},{8,9},{9,8},{10,11... | collective-permute-start | bytes 49160 | tf_op jit(solution)/shard_map/ppermute | solution.py:741
  46.4 21.2 %copy-start.9 = (bf16[128,128]{1,0:T(8,128)(2,1)S(1)}, bf16[128,128]{1,0:T(8,128)(2,1)}, u32[]{:S(2)}) copy-start(bf16[128,128]{1,0:T(8,128)(2,1)} %constant.35.clone.back_table) | copy-start | bytes 98308
  67.6 16.8 %copy-start.4 = (bf16[512,192]{0,1:T(8,128)(2,1)S(1)}, bf16[512,192]{0,1:T(8,128)(2,1)}, u32[]{:S(2)}) copy-start(bf16[512,192]{0,1:T(8,128)(2,1)} %param.20) | copy-start | bytes 589828
  67.6 16.8 %copy-start.5 = (bf16[512,512]{1,0:T(8,128)(2,1)S(1)}, bf16[512,512]{1,0:T(8,128)(2,1)}, u32[]{:S(2)}) copy-start(bf16[512,512]{1,0:T(8,128)(2,1)} %constant.33.clone.table) | copy-start | bytes 1572868
  67.6 16.8 %copy-start.6 = (bf16[512,256]{1,0:T(8,128)(2,1)S(1)}, bf16[512,256]{1,0:T(8,128)(2,1)}, u32[]{:S(2)}) copy-start(bf16[512,256]{1,0:T(8,128)(2,1)} %weight_local.1) | copy-start | bytes 786436

commit v22 on v20

--- a/solution.py
+++ b/solution.py
@@ -63,10 +63,6 @@
     rows = (strips[None, :] * strip + np.arange(strip)[:, None]).reshape(-1)
     cos, sin = phases(np.arange(height), rows, height)
     return np.block([[cos, sin], [-sin, cos]])
-
-
-def strip_row(signal, r):
-    return jnp.concatenate([signal[block, r] for block in range(signal.shape[0])], axis=0)
 
 
 def grad_kernel(norm, col, low, *refs):
@@ -195,15 +191,23 @@
 
 
 def output_kernel(norm, moved, strip_grad, weight_in, weight_local, table, out, held, sems):
-    spatial = (dot(table[...], moved[...]) * norm).astype(jnp.bfloat16)
     half = weight_in.shape[0]
+    blocks, strip, tile_cols, _ = strip_grad.shape
+    count = 2 if blocks % 2 == 0 else 1
+    columns = blocks // count * tile_cols
     copies = []
-    for r in range(out.shape[0]):
-        total = dot(spatial[:, r * half : (r + 1) * half], weight_in[...])
-        total = total + dot_t(strip_row(strip_grad, r), weight_local[...])
-        held[r] = total.astype(jnp.bfloat16)
-        copies.append(pltpu.make_async_copy(held.at[r], out.at[r], sems.at[r]))
-        copies[-1].start()
+    for part in range(count):
+        where = slice(part * columns, (part + 1) * columns)
+        spatial = (dot(table[where], moved[...]) * norm).astype(jnp.bfloat16)
+        for r in range(strip):
+            grads = [strip_grad[part * (blocks // count) + i, r] for i in range(blocks // count)]
+            total = dot(spatial[:, r * half : (r + 1) * half], weight_in[...])
+            total = total + dot_t(jnp.concatenate(grads, axis=0), weight_local[...])
+            held[r, where] = total.astype(jnp.bfloat16)
+            copies.append(
+                pltpu.make_async_copy(held.at[r, where], out.at[r, where], sems.at[len(copies)])
+            )
+            copies[-1].start()
     for copy in copies:
         copy.wait()
 
@@ -214,7 +218,7 @@
         out_shape=jax.ShapeDtypeStruct(shape, jnp.bfloat16),
         in_specs=[pl.BlockSpec(memory_space=pltpu.VMEM)] * len(operands),
         out_specs=pl.BlockSpec(memory_space=pltpu.HBM),
-        scratch_shapes=[pltpu.VMEM(shape, jnp.bfloat16), pltpu.SemaphoreType.DMA((shape[0],))],
+        scratch_shapes=[pltpu.VMEM(shape, jnp.bfloat16), pltpu.SemaphoreType.DMA((2 * shape[0],))],
         compiler_params=pltpu.CompilerParams(vmem_limit_bytes=10 * MIB),
         cost_estimate=pl.CostEstimate(flops=0, bytes_accessed=3 * MIB, transcendentals=0),
     )(*operands)
@@ -307,7 +311,7 @@
     )(*[in_hbm(a) for a in arrays])
 
 
-def edge_kernel(tile_cols, col, low, early_pack, late_pack, *refs):
+def edge_kernel(tile_cols, col, low, late_pack, early_pack, *refs):
     place = col[0], low[0]
     sources, (early, late, own) = refs[:-3], refs[-3:]
     count = len(sources) // 2
@@ -371,7 +375,7 @@
         cost_estimate=pl.CostEstimate(
             flops=0, bytes_accessed=16 * rows * keep * channels, transcendentals=0
         ),
-    )(*place, early_pack, late_pack, *parts, *parts)
+    )(*place, late_pack, early_pack, *parts, *parts)
 
 
 def put(wide, row, value, stride):
@@ -721,10 +725,10 @@
     late = lax.ppermute(features, "row", pairs("row", 1))
     kernel_first, spatial_cols = lax.optimization_barrier((kernel_first, spatial_cols))
     kernel_first, kernel_second = fetch(kernel_first, kernel_second)
+    late_pack = lax.ppermute(late_pack, "row", pairs("row", 1))
     early_pack = lax.ppermute(early_pack, "row", pairs("row", 0))
-    late_pack = lax.ppermute(late_pack, "row", pairs("row", 1))
     pre, slopes = tile_forward(place, early, features, late, kernel_first, kernel_second, ok)
-    early_pack, pre = lax.optimization_barrier((early_pack, pre))
+    late_pack, pre = lax.optimization_barrier((late_pack, pre))
     early_edge, late_edge, own = edges(
         place, early, late, features, target, mask_row, early_pack, late_pack
     )

time: 87 us -> 86.9 us (level)
  no operation moved by 1% of the time
where the time goes in v22:
time: 86.9 us; the launch traced here: 85.6 us
  blocking collectives  33.4 us (38%)
  Pallas kernels  24.4 us (28%)
  starting transfers between devices  23.8 us (27%)
  waiting for transfers between devices  3.39 us (4%)
    all_to_all x2, blocking collectives, swap(): lax.all_to_all(spectrum, ('col', 'row'), split_axis=0, concat_axis=0, til...  33.4 us
    ppermute x6, starting transfers between devices, dealt(): result.append(lax.ppermute(piece, 'col', swaps) if step else piece)  5.77 us
    pallas_call x1, Pallas kernels, tile_forward(): pl.pallas_call(tile_forward_kernel, out_shape=shapes, in_specs=[pl.BlockS...  5.74 us
    all_to_all x1, starting transfers between devices, swap(): lax.all_to_all(spectrum, ('col', 'row'), split_axis=0, concat_axis=0, til...  5.12 us
    ppermute x1, starting transfers between devices, shards(): late = lax.ppermute(features, 'row', pairs('row', 1))  4.5 us
    ppermute x1, starting transfers between devices, shards(): early_edge = lax.ppermute(early_edge, 'col', pairs('col', 0))  3.88 us
    pallas_call x1, Pallas kernels, tile_backward(): pl.pallas_call(tile_backward_kernel, out_shape=shapes, in_specs=[pl.Block...  3.86 us
    pallas_call x1, Pallas kernels, sides(): pl.pallas_call(side_kernel, out_shape=shapes, in_specs=[pl.BlockSpec(memo...  3.86 us
  transfers between devices with their start and end apart: 13, of which 2 were waited for; matrix products, arithmetic and copies ran while one was open for 0% of the time, Pallas kernels for 24%

profile of v22, /device:TPU:1, one launch (start us, length us, event | category | flops | bytes accessed | tf_op | source)
XLA Modules:
  0.0 85.6 jit_solution(1501845065590815714)
XLA Ops:
  0.0 4.5 %collective-permute-start.2 = (bf16[8,128,256]{2,1,0:T(8,128)(2,1)}, bf16[8,128,256]{2,1,0:T(8,128)(2,1)S(1)}, u32[]{:S(2)}, u32[]{:S(2)}) collective-permute-start(bf16[8,128,256]{2,1,0:T(8,128)(2,1)} %refs_7_.1), channel_id=1, source_target_pairs={{4,8},{12,16},{20,24},{8,4},{16,12},{24,20},{5,9},{13,17},{21,25},... | collective-permute-start | bytes 1572872 | tf_op jit(solution)/shard_map/ppermute | solution.py:725
  4.5 0.1 collective-permute-start.1
  4.6 1.1 %shard_map.136 = (bf16[528,256]{1,0:T(8,128)(2,1)S(1)}, bf16[528,256]{1,0:T(8,128)(2,1)S(1)}, bf16[1,128,256]{2,1,0:T(8,128)(2,1)S(1)}) custom-call(s32[1]{0:T(128)} %bitcast.col, s32[1]{0:T(128)} %bitcast.1.low, bf16[1024,256]{1,0:T(8,128)(2,1)} %bitcast.10, s32[8,128]{1,0:T(8,128)} %mask.1), custom_call_target="tpu_custom_call" | custom-call | bytes 1048576 | tf_op jit(solution)/shard_map/pallas_call | solution.py:281
  5.7 0.1 and_convert_fusion.ok
  5.8 0.5 collective-permute-start.3
  6.3 3.0 %collective-permute-start = (bf16[528,256]{1,0:T(8,128)(2,1)S(1)}, bf16[528,256]{1,0:T(8,128)(2,1)S(1)}, u32[]{:S(2)}, u32[]{:S(2)}) collective-permute-start(bf16[528,256]{1,0:T(8,128)(2,1)S(1)} %get-tuple-element.38), channel_id=1, source_target_pairs={{4,8},{12,16},{20,24},{8,4},{16,12},{24,20},{5,9},{13,17},{21,25},... | collective-permute-start | bytes 811016 | tf_op jit(solution)/shard_map/ppermute | solution.py:728
  9.4 3.3 %shard_map.137 = bf16[512,384]{1,0:T(8,128)(2,1)} custom-call(bf16[2,512,512]{2,1,0:T(8,128)(2,1)} %signal, bf16[192,512]{1,0:T(8,128)(2,1)} %bitcast.15, bf16[512,512]{1,0:T(8,128)(2,1)} %constant.34.clone.table.refs_9_), custom_call_target="tpu_custom_call" | custom-call | bytes 2097152 | tf_op jit(solution)/shard_map/pallas_call | solution.py:121
  12.7 5.1 %all-to-all-start = ((bf16[32,16,384]{2,1,0:T(8,128)(2,1)}), bf16[32,16,384]{2,1,0:T(8,128)(2,1)S(1)}, u32[]{:S(2)}, u32[]{:S(2)}) async-start(bf16[32,16,384]{2,1,0:T(8,128)(2,1)} %bitcast.4), calls=%async_computation | async-start | bytes 786432 | tf_op jit(solution)/shard_map/all_to_all | solution.py:708
  17.8 1.7 %shard_map.138 = (bf16[3,3,256,256]{3,2,1,0:T(8,128)(2,1)S(1)}, bf16[3,3,256,256]{3,2,1,0:T(8,128)(2,1)S(1)}) custom-call(bf16[3,3,256,256]{3,2,1,0:T(8,128)(2,1)} %refs_0_, bf16[3,3,256,256]{3,2,1,0:T(8,128)(2,1)} %refs_1_.1), custom_call_target="tpu_custom_call" | custom-call | bytes 5242880 | tf_op jit(solution)/shard_map/pallas_call | solution.py:303
  19.6 0.0 copy-done.2
  19.6 5.7 %shard_map.139 = (f32[2048,256]{1,0:T(8,128)S(1)}, f32[1536,256]{1,0:T(8,128)S(1)}) custom-call(s32[1]{0:T(128)} %bitcast.col, s32[1]{0:T(128)} %bitcast.1.low, bf16[8,128,256]{2,1,0:T(8,128)(2,1)S(1)} %collective-permute-done.1.early.refs_0_.refs_5_, bf16[8,128,256]{2,1,0:T(8,128)(2,1)S(1)} %copy-done.2, ...), custom_call_target="tpu_custom_call" | custom-call | flops 5435817984 | bytes 8388608 | tf_op jit(solution)/shard_map/pallas_call | solution.py:608
  25.4 0.1 shard_map.141
  25.5 0.9 collective-permute-start.7
  26.4 3.9 %collective-permute-start.8 = (bf16[43,8,256]{2,1,0:T(8,128)(2,1)S(1)}, bf16[43,8,256]{2,1,0:T(8,128)(2,1)S(1)}, u32[]{:S(2)}, u32[]{:S(2)}) collective-permute-start(bf16[43,8,256]{2,1,0:T(8,128)(2,1)S(1)} %get-tuple-element.56), channel_id=1, source_target_pairs={{0,1},{2,3},{1,0},{3,2},{4,5},{6,7},{5,4},{7,6},{8,9},{10,11},{9,8... | collective-permute-start | bytes 528392 | tf_op jit(solution)/shard_map/ppermute | solution.py:736
  30.2 3.9 %shard_map.140 = (bf16[2,112,256]{2,1,0:T(8,128)(2,1)S(1)}, bf16[2,112,256]{2,1,0:T(8,128)(2,1)S(1)}, bf16[2,112,256]{2,1,0:T(8,128)(2,1)S(1)}, bf16[2,112,256]{2,1,0:T(8,128)(2,1)S(1)}) custom-call(s32[1]{0:T(128)} %bitcast.col, s32[1]{0:T(128)} %bitcast.1.low, f32[2048,256]{1,0:T(8,128)S(1)} %get-tuple-element.46.pre, ...), custom_call_target="tpu_custom_call" | custom-call | flops 3019898880 | bytes 8388608 | tf_op jit(solution)/shard_map/pallas_call | solution.py:632
  34.1 0.1 collective-permute-start.4
  34.2 2.1 %collective-permute-start.5 = (bf16[2,112,256]{2,1,0:T(8,128)(2,1)S(1)}, bf16[2,112,256]{2,1,0:T(8,128)(2,1)S(1)}, u32[]{:S(2)}, u32[]{:S(2)}) collective-permute-start(bf16[2,112,256]{2,1,0:T(8,128)(2,1)S(1)} %get-tuple-element.53), channel_id=1, source_target_pairs={{0,3},{1,2},{2,1},{3,0},{4,7},{5,6},{6,5},{7,4},{8,11},{9,10},{10,... | collective-permute-start | bytes 344072 | tf_op jit(solution)/shard_map/ppermute | solution.py:745
  36.3 0.5 collective-permute-start.6
  36.8 0.0 copy-start.7
  36.9 3.9 %shard_map.142 = (bf16[2,16,256]{2,1,0:T(8,128)(2,1)S(1)}, bf16[2,16,256]{2,1,0:T(8,128)(2,1)S(1)}, bf16[2,16,256]{2,1,0:T(8,128)(2,1)S(1)}, bf16[2,16,256]{2,1,0:T(8,128)(2,1)S(1)}) custom-call(s32[1]{0:T(128)} %bitcast.col, s32[1]{0:T(128)} %bitcast.1.low, bf16[43,8,256]{2,1,0:T(8,128)(2,1)S(1)} %collective-permute-done.7.late, ...), custom_call_target="tpu_custom_call" | custom-call | flops 3170893824 | bytes 4194304 | tf_op jit(solution)/shard_map/pallas_call | solution.py:655
  40.7 0.0 copy-start.1
  40.8 1.0 %collective-permute-start.9 = (bf16[2,16,256]{2,1,0:T(8,128)(2,1)S(1)}, bf16[2,16,256]{2,1,0:T(8,128)(2,1)S(1)}, u32[]{:S(2)}, u32[]{:S(2)}) collective-permute-start(bf16[2,16,256]{2,1,0:T(8,128)(2,1)S(1)} %get-tuple-element.65), channel_id=1, source_target_pairs={{0,2},{1,3},{2,0},{3,1},{4,6},{5,7},{6,4},{7,5},{8,10},{9,11},{10,... | collective-permute-start | bytes 49160 | tf_op jit(solution)/shard_map/ppermute | solution.py:745
  41.8 2.0 %collective-permute-start.10 = (bf16[2,16,256]{2,1,0:T(8,128)(2,1)S(1)}, bf16[2,16,256]{2,1,0:T(8,128)(2,1)S(1)}, u32[]{:S(2)}, u32[]{:S(2)}) collective-permute-start(bf16[2,16,256]{2,1,0:T(8,128)(2,1)S(1)} %get-tuple-element.66), channel_id=1, source_target_pairs={{0,3},{1,2},{2,1},{3,0},{4,7},{5,6},{6,5},{7,4},{8,11},{9,10},{10,... | collective-permute-start | bytes 49160 | tf_op jit(solution)/shard_map/ppermute | solution.py:745
  43.8 1.0 %collective-permute-done.4.refs_1_ = bf16[2,112,256]{2,1,0:T(8,128)(2,1)S(1)} collective-permute-done((bf16[2,112,256]{2,1,0:T(8,128)(2,1)S(1)}, bf16[2,112,256]{2,1,0:T(8,128)(2,1)S(1)}, u32[]{:S(2)}, u32[]{:S(2)}) %collective-permute-start.4) | collective-permute-done | bytes 114720 | tf_op jit(solution)/shard_map/ppermute | solution.py:745
  44.9 1.0 %shard_map.143.slope = f32[2,512,192]{2,1,0:T(8,128)S(1)} custom-call(bf16[512,384]{1,0:T(8,128)(2,1)S(1)} %bitcast.11, bf16[384,384]{1,0:T(8,128)(2,1)S(1)} %copy-done.3, bf16[128,128]{1,0:T(8,128)(2,1)S(1)} %copy-done.7), custom_call_target="tpu_custom_call" | custom-call | bytes 1507328 | tf_op jit(solution)/shard_map/pallas_call | solution.py:30
  45.8 0.0 copy-start.9
  45.9 2.3 %collective-permute-done.9.refs_5_ = bf16[2,16,256]{2,1,0:T(8,128)(2,1)S(1)} collective-permute-done((bf16[2,16,256]{2,1,0:T(8,128)(2,1)S(1)}, bf16[2,16,256]{2,1,0:T(8,128)(2,1)S(1)}, u32[]{:S(2)}, u32[]{:S(2)}) %collective-permute-start.9) | collective-permute-done | bytes 16416 | tf_op jit(solution)/shard_map/ppermute | solution.py:745
  48.2 0.9 %shard_map.144 = (bf16[512,384]{1,0:T(8,128)(2,1)S(1)}, bf16[4,2,128,256]{3,2,1,0:T(8,128)(2,1)S(1)}) custom-call(s32[1]{0:T(128)} %bitcast.col, s32[1]{0:T(128)} %bitcast.1.low, bf16[2,112,256]{2,1,0:T(8,128)(2,1)S(1)} %get-tuple-element.51.refs_0_, bf16[2,112,256]{2,1,0:T(8,128)(2,1)S(1)} %collective-permute-done.4.refs_1_, ...), custom_call_target="tpu_custom_call" | custom-call | bytes 2097152 | tf_op jit(solution)/shard_map/pallas_call | solution.py:87
  49.1 17.8 %all_to_all.34 = bf16[32,16,384]{2,1,0:T(8,128)(2,1)S(1)} all-to-all(bf16[32,16,384]{2,1,0:T(8,128)(2,1)S(1)} %bitcast.17), channel_id=1, replica_groups=mesh['row'=8,'col'=4] {'col','row'}, dimensions={0} | all-to-all | bytes 786432 | tf_op jit(solution)/shard_map/all_to_all | solution.py:708
  66.9 1.2 %shard_map.145 = bf16[512,384]{1,0:T(8,128)(2,1)S(1)} custom-call(bf16[512,384]{1,0:T(8,128)(2,1)S(1)} %bitcast.12, f32[2,512,192]{2,1,0:T(8,128)S(1)} %shard_map.143.slope, bf16[384,384]{1,0:T(8,128)(2,1)S(1)} %copy-done.3, bf16[128,128]{1,0:T(8,128)(2,1)S(1)} %copy-done.7, bf16[128,128]{1,0:T(8,128)(2,1)S(1)} %copy-done.9), custom_call_target="tpu_custom_call" | custom-call | bytes 1933312 | tf_op jit(solution)/shard_map/pallas_call | solution.py:30
  68.1 15.6 %all_to_all.35 = bf16[32,16,384]{2,1,0:T(8,128)(2,1)S(1)} all-to-all(bf16[32,16,384]{2,1,0:T(8,128)(2,1)S(1)} %bitcast.13), channel_id=1, replica_groups=mesh['row'=8,'col'=4] {'col','row'}, dimensions={0} | all-to-all | bytes 786432 | tf_op jit(solution)/shard_map/all_to_all | solution.py:708
  83.7 1.7 %shard_map.146 = bf16[2,512,512]{2,1,0:T(8,128)(2,1)} custom-call(bf16[512,384]{1,0:T(8,128)(2,1)S(1)} %bitcast.14, bf16[4,2,128,256]{3,2,1,0:T(8,128)(2,1)S(1)} %get-tuple-element.70.strip_grad, bf16[192,512]{1,0:T(8,128)(2,1)S(1)} %bitcast.16, bf16[512,256]{1,0:T(8,128)(2,1)S(1)} %copy-done.6, bf16[512,512]{1,0:T(8,128)(2,1)S(1)} %copy-done.5), custom_call_target="tpu_custom_call" | custom-call | bytes 3145728 | tf_op jit(solution)/shard_map/pallas_call | solution.py:216
  (30 shorter events, 0.1 us)
Async XLA Ops:
  0.0 19.5 %collective-permute-start.2 = (bf16[8,128,256]{2,1,0:T(8,128)(2,1)}, bf16[8,128,256]{2,1,0:T(8,128)(2,1)S(1)}, u32[]{:S(2)}, u32[]{:S(2)}) collective-permute-start(bf16[8,128,256]{2,1,0:T(8,128)(2,1)} %refs_7_.1), channel_id=1, source_target_pairs={{4,8},{12,16},{20,24},{8,4},{16,12},{24,20},{5,9},{13,17},{21,25},... | collective-permute-start | bytes 1572872 | tf_op jit(solution)/shard_map/ppermute | solution.py:725
  4.5 15.1 %collective-permute-start.1 = (bf16[8,128,256]{2,1,0:T(8,128)(2,1)}, bf16[8,128,256]{2,1,0:T(8,128)(2,1)S(1)}, u32[]{:S(2)}, u32[]{:S(2)}) collective-permute-start(bf16[8,128,256]{2,1,0:T(8,128)(2,1)} %refs_7_.1), channel_id=1, source_target_pairs={{0,4},{8,12},{16,20},{24,28},{4,0},{12,8},{20,16},{28,24},{1,5},{9... | collective-permute-start | bytes 1572872 | tf_op jit(solution)/shard_map/ppermute | solution.py:724
  5.8 19.5 %collective-permute-start.3 = (bf16[528,256]{1,0:T(8,128)(2,1)S(1)}, bf16[528,256]{1,0:T(8,128)(2,1)S(1)}, u32[]{:S(2)}, u32[]{:S(2)}) collective-permute-start(bf16[528,256]{1,0:T(8,128)(2,1)S(1)} %get-tuple-element.48), channel_id=1, source_target_pairs={{0,4},{8,12},{16,20},{24,28},{4,0},{12,8},{20,16},{28,24},{1,5},{9... | collective-permute-start | bytes 811016 | tf_op jit(solution)/shard_map/ppermute | solution.py:729
  6.3 19.0 %collective-permute-start = (bf16[528,256]{1,0:T(8,128)(2,1)S(1)}, bf16[528,256]{1,0:T(8,128)(2,1)S(1)}, u32[]{:S(2)}, u32[]{:S(2)}) collective-permute-start(bf16[528,256]{1,0:T(8,128)(2,1)S(1)} %get-tuple-element.38), channel_id=1, source_target_pairs={{4,8},{12,16},{20,24},{8,4},{16,12},{24,20},{5,9},{13,17},{21,25},... | collective-permute-start | bytes 811016 | tf_op jit(solution)/shard_map/ppermute | solution.py:728
  12.7 28.1 %all-to-all-start = ((bf16[32,16,384]{2,1,0:T(8,128)(2,1)}), bf16[32,16,384]{2,1,0:T(8,128)(2,1)S(1)}, u32[]{:S(2)}, u32[]{:S(2)}) async-start(bf16[32,16,384]{2,1,0:T(8,128)(2,1)} %bitcast.4), calls=%async_computation | async-start | bytes 786432 | tf_op jit(solution)/shard_map/all_to_all | solution.py:708
  17.8 1.8 %copy-start.2 = (bf16[8,128,256]{2,1,0:T(8,128)(2,1)S(1)}, bf16[8,128,256]{2,1,0:T(8,128)(2,1)}, u32[]{:S(2)}) copy-start(bf16[8,128,256]{2,1,0:T(8,128)(2,1)} %refs_7_.1) | copy-start | bytes 1572868
  19.6 5.8 %copy-start = (bf16[8,128,256]{2,1,0:T(8,128)(2,1)S(1)}, bf16[8,128,256]{2,1,0:T(8,128)(2,1)}, u32[]{:S(2)}) copy-start(bf16[8,128,256]{2,1,0:T(8,128)(2,1)} %refs_8_.2) | copy-start | bytes 1572868
  25.5 11.3 %collective-permute-start.7 = (bf16[43,8,256]{2,1,0:T(8,128)(2,1)S(1)}, bf16[43,8,256]{2,1,0:T(8,128)(2,1)S(1)}, u32[]{:S(2)}, u32[]{:S(2)}) collective-permute-start(bf16[43,8,256]{2,1,0:T(8,128)(2,1)S(1)} %get-tuple-element.55), channel_id=1, source_target_pairs={{1,2},{2,1},{5,6},{6,5},{9,10},{10,9},{13,14},{14,13},{17,18},{18,... | collective-permute-start | bytes 528392 | tf_op jit(solution)/shard_map/ppermute | solution.py:735
  26.4 10.5 %collective-permute-start.8 = (bf16[43,8,256]{2,1,0:T(8,128)(2,1)S(1)}, bf16[43,8,256]{2,1,0:T(8,128)(2,1)S(1)}, u32[]{:S(2)}, u32[]{:S(2)}) collective-permute-start(bf16[43,8,256]{2,1,0:T(8,128)(2,1)S(1)} %get-tuple-element.56), channel_id=1, source_target_pairs={{0,1},{2,3},{1,0},{3,2},{4,5},{6,7},{5,4},{7,6},{8,9},{10,11},{9,8... | collective-permute-start | bytes 528392 | tf_op jit(solution)/shard_map/ppermute | solution.py:736
  34.1 10.7 %collective-permute-start.4 = (bf16[2,112,256]{2,1,0:T(8,128)(2,1)S(1)}, bf16[2,112,256]{2,1,0:T(8,128)(2,1)S(1)}, u32[]{:S(2)}, u32[]{:S(2)}) collective-permute-start(bf16[2,112,256]{2,1,0:T(8,128)(2,1)S(1)} %get-tuple-element.52), channel_id=1, source_target_pairs={{0,2},{1,3},{2,0},{3,1},{4,6},{5,7},{6,4},{7,5},{8,10},{9,11},{10,... | collective-permute-start | bytes 344072 | tf_op jit(solution)/shard_map/ppermute | solution.py:745
  34.2 11.7 %collective-permute-start.5 = (bf16[2,112,256]{2,1,0:T(8,128)(2,1)S(1)}, bf16[2,112,256]{2,1,0:T(8,128)(2,1)S(1)}, u32[]{:S(2)}, u32[]{:S(2)}) collective-permute-start(bf16[2,112,256]{2,1,0:T(8,128)(2,1)S(1)} %get-tuple-element.53), channel_id=1, source_target_pairs={{0,3},{1,2},{2,1},{3,0},{4,7},{5,6},{6,5},{7,4},{8,11},{9,10},{10,... | collective-permute-start | bytes 344072 | tf_op jit(solution)/shard_map/ppermute | solution.py:745
  36.3 9.6 %collective-permute-start.6 = (bf16[2,112,256]{2,1,0:T(8,128)(2,1)S(1)}, bf16[2,112,256]{2,1,0:T(8,128)(2,1)S(1)}, u32[]{:S(2)}, u32[]{:S(2)}) collective-permute-start(bf16[2,112,256]{2,1,0:T(8,128)(2,1)S(1)} %get-tuple-element.54), channel_id=1, source_target_pairs={{0,1},{1,0},{2,3},{3,2},{4,5},{5,4},{6,7},{7,6},{8,9},{9,8},{10,11... | collective-permute-start | bytes 344072 | tf_op jit(solution)/shard_map/ppermute | solution.py:745
  36.8 8.0 %copy-start.3 = (bf16[384,384]{1,0:T(8,128)(2,1)S(1)}, bf16[384,384]{1,0:T(8,128)(2,1)}, u32[]{:S(2)}) copy-start(bf16[384,384]{1,0:T(8,128)(2,1)} %mix.3) | copy-start | bytes 884740
  36.8 8.0 %copy-start.7 = (bf16[128,128]{1,0:T(8,128)(2,1)S(1)}, bf16[128,128]{1,0:T(8,128)(2,1)}, u32[]{:S(2)}) copy-start(bf16[128,128]{1,0:T(8,128)(2,1)} %constant.36.clone.table) | copy-start | bytes 98308
  40.7 7.5 %copy-start.1 = (bf16[512,512]{1,0:T(8,128)(2,1)S(1)}, bf16[512,512]{1,0:T(8,128)(2,1)}, u32[]{:S(2)}) copy-start(bf16[512,512]{1,0:T(8,128)(2,1)} %constant.34.clone.table.refs_9_) | copy-start | bytes 1572868
  40.7 7.5 %copy-start.8 = (bf16[192,256]{1,0:T(8,128)(2,1)S(1)}, bf16[192,256]{1,0:T(8,128)(2,1)}, u32[]{:S(2)}) copy-start(bf16[192,256]{1,0:T(8,128)(2,1)} %refs_8_.3) | copy-start | bytes 294916
  40.8 7.4 %collective-permute-start.9 = (bf16[2,16,256]{2,1,0:T(8,128)(2,1)S(1)}, bf16[2,16,256]{2,1,0:T(8,128)(2,1)S(1)}, u32[]{:S(2)}, u32[]{:S(2)}) collective-permute-start(bf16[2,16,256]{2,1,0:T(8,128)(2,1)S(1)} %get-tuple-element.65), channel_id=1, source_target_pairs={{0,2},{1,3},{2,0},{3,1},{4,6},{5,7},{6,4},{7,5},{8,10},{9,11},{10,... | collective-permute-start | bytes 49160 | tf_op jit(solution)/shard_map/ppermute | solution.py:745
  41.8 6.4 %collective-permute-start.10 = (bf16[2,16,256]{2,1,0:T(8,128)(2,1)S(1)}, bf16[2,16,256]{2,1,0:T(8,128)(2,1)S(1)}, u32[]{:S(2)}, u32[]{:S(2)}) collective-permute-start(bf16[2,16,256]{2,1,0:T(8,128)(2,1)S(1)} %get-tuple-element.66), channel_id=1, source_target_pairs={{0,3},{1,2},{2,1},{3,0},{4,7},{5,6},{6,5},{7,4},{8,11},{9,10},{10,... | collective-permute-start | bytes 49160 | tf_op jit(solution)/shard_map/ppermute | solution.py:745
  44.9 3.3 %collective-permute-start.11 = (bf16[2,16,256]{2,1,0:T(8,128)(2,1)S(1)}, bf16[2,16,256]{2,1,0:T(8,128)(2,1)S(1)}, u32[]{:S(2)}, u32[]{:S(2)}) collective-permute-start(bf16[2,16,256]{2,1,0:T(8,128)(2,1)S(1)} %get-tuple-element.67), channel_id=1, source_target_pairs={{0,1},{1,0},{2,3},{3,2},{4,5},{5,4},{6,7},{7,6},{8,9},{9,8},{10,11... | collective-permute-start | bytes 49160 | tf_op jit(solution)/shard_map/ppermute | solution.py:745
  45.8 21.1 %copy-start.9 = (bf16[128,128]{1,0:T(8,128)(2,1)S(1)}, bf16[128,128]{1,0:T(8,128)(2,1)}, u32[]{:S(2)}) copy-start(bf16[128,128]{1,0:T(8,128)(2,1)} %constant.35.clone.back_table) | copy-start | bytes 98308
  66.9 16.8 %copy-start.4 = (bf16[512,192]{0,1:T(8,128)(2,1)S(1)}, bf16[512,192]{0,1:T(8,128)(2,1)}, u32[]{:S(2)}) copy-start(bf16[512,192]{0,1:T(8,128)(2,1)} %param.20) | copy-start | bytes 589828
  66.9 16.8 %copy-start.5 = (bf16[512,512]{1,0:T(8,128)(2,1)S(1)}, bf16[512,512]{1,0:T(8,128)(2,1)}, u32[]{:S(2)}) copy-start(bf16[512,512]{1,0:T(8,128)(2,1)} %constant.33.clone.table) | copy-start | bytes 1572868
  66.9 16.8 %copy-start.6 = (bf16[512,256]{1,0:T(8,128)(2,1)S(1)}, bf16[512,256]{1,0:T(8,128)(2,1)}, u32[]{:S(2)}) copy-start(bf16[512,256]{1,0:T(8,128)(2,1)} %weight_local.1) | copy-start | bytes 786436

commit v23 on v22

--- a/solution.py
+++ b/solution.py
@@ -135,7 +135,7 @@
 def row_spectrum(moved, table, wide, norm, owned, devices):
     groups = wide.shape[0]
     for g in range(groups):
-        wide[g] = moved[:, g * LANES : (g + 1) * LANES].astype(jnp.float32)
+        wide[g, : moved.shape[0]] = moved[:, g * LANES : (g + 1) * LANES].astype(jnp.float32)
     strip = table.shape[1] // (2 * devices)
     half = moved.shape[1] // strip
     height = table.shape[0] // 2
@@ -187,7 +187,7 @@
             for g in range(groups):
                 wide[g, where, :] = values[:, g * LANES : (g + 1) * LANES]
     for g in range(groups):
-        out[:, g * LANES : (g + 1) * LANES] = wide[g].astype(jnp.bfloat16)
+        out[:, g * LANES : (g + 1) * LANES] = wide[g, : out.shape[0]].astype(jnp.bfloat16)
 
 
 def output_kernel(norm, moved, strip_grad, weight_in, weight_local, table, out, held, sems):
@@ -311,7 +311,7 @@
     )(*[in_hbm(a) for a in arrays])
 
 
-def edge_kernel(tile_cols, col, low, late_pack, early_pack, *refs):
+def edge_kernel(tile_cols, col, low, early_pack, late_pack, *refs):
     place = col[0], low[0]
     sources, (early, late, own) = refs[:-3], refs[-3:]
     count = len(sources) // 2
@@ -375,7 +375,7 @@
         cost_estimate=pl.CostEstimate(
             flops=0, bytes_accessed=16 * rows * keep * channels, transcendentals=0
         ),
-    )(*place, late_pack, early_pack, *parts, *parts)
+    )(*place, early_pack, late_pack, *parts, *parts)
 
 
 def put(wide, row, value, stride):
@@ -725,10 +725,10 @@
     late = lax.ppermute(features, "row", pairs("row", 1))
     kernel_first, spatial_cols = lax.optimization_barrier((kernel_first, spatial_cols))
     kernel_first, kernel_second = fetch(kernel_first, kernel_second)
+    early_pack = lax.ppermute(early_pack, "row", pairs("row", 0))
     late_pack = lax.ppermute(late_pack, "row", pairs("row", 1))
-    early_pack = lax.ppermute(early_pack, "row", pairs("row", 0))
     pre, slopes = tile_forward(place, early, features, late, kernel_first, kernel_second, ok)
-    late_pack, pre = lax.optimization_barrier((late_pack, pre))
+    early_pack, pre = lax.optimization_barrier((early_pack, pre))
     early_edge, late_edge, own = edges(
         place, early, late, features, target, mask_row, early_pack, late_pack
     )
@@ -753,7 +753,7 @@
     outer = dealt(outer)
 
     cell_count = height * owned
-    wide = [pltpu.VMEM((strip * half // LANES, width, LANES), jnp.float32)]
+    wide = [pltpu.VMEM((strip * half // LANES, width + 16 * owned, LANES), jnp.float32)]
     slope = vmem_call(
         functools.partial(slope_kernel, row_norm, owned, devices),
         [jax.ShapeDtypeStruct((2, cell_count, half), jnp.float32)],

time: 86.9 us -> 86.9 us (level)
  no operation moved by 1% of the time
where the time goes in v23:
time: 86.9 us; the launch traced here: 85.6 us
  blocking collectives  33.4 us (38%)
  Pallas kernels  24.4 us (28%)
  starting transfers between devices  23.8 us (27%)
  waiting for transfers between devices  3.39 us (4%)
    all_to_all x2, blocking collectives, swap(): lax.all_to_all(spectrum, ('col', 'row'), split_axis=0, concat_axis=0, til...  33.4 us
    ppermute x6, starting transfers between devices, dealt(): result.append(lax.ppermute(piece, 'col', swaps) if step else piece)  5.77 us
    pallas_call x1, Pallas kernels, tile_forward(): pl.pallas_call(tile_forward_kernel, out_shape=shapes, in_specs=[pl.BlockS...  5.74 us
    all_to_all x1, starting transfers between devices, swap(): lax.all_to_all(spectrum, ('col', 'row'), split_axis=0, concat_axis=0, til...  5.12 us
    ppermute x1, starting transfers between devices, shards(): late = lax.ppermute(features, 'row', pairs('row', 1))  4.5 us
    ppermute x1, starting transfers between devices, shards(): early_edge = lax.ppermute(early_edge, 'col', pairs('col', 0))  3.88 us
    pallas_call x1, Pallas kernels, tile_backward(): pl.pallas_call(tile_backward_kernel, out_shape=shapes, in_specs=[pl.Block...  3.86 us
    pallas_call x1, Pallas kernels, sides(): pl.pallas_call(side_kernel, out_shape=shapes, in_specs=[pl.BlockSpec(memo...  3.86 us
  transfers between devices with their start and end apart: 13, of which 2 were waited for; matrix products, arithmetic and copies ran while one was open for 0% of the time, Pallas kernels for 24%

profile of v23, /device:TPU:1, one launch (start us, length us, event | category | flops | bytes accessed | tf_op | source)
XLA Modules:
  0.0 85.6 jit_solution(7299464682224441130)
XLA Ops:
  0.0 4.5 %collective-permute-start.2 = (bf16[8,128,256]{2,1,0:T(8,128)(2,1)}, bf16[8,128,256]{2,1,0:T(8,128)(2,1)S(1)}, u32[]{:S(2)}, u32[]{:S(2)}) collective-permute-start(bf16[8,128,256]{2,1,0:T(8,128)(2,1)} %refs_7_.1), channel_id=1, source_target_pairs={{4,8},{12,16},{20,24},{8,4},{16,12},{24,20},{5,9},{13,17},{21,25},... | collective-permute-start | bytes 1572872 | tf_op jit(solution)/shard_map/ppermute | solution.py:725
  4.5 0.1 collective-permute-start.1
  4.6 1.1 %shard_map.136 = (bf16[528,256]{1,0:T(8,128)(2,1)S(1)}, bf16[528,256]{1,0:T(8,128)(2,1)S(1)}, bf16[1,128,256]{2,1,0:T(8,128)(2,1)S(1)}) custom-call(s32[1]{0:T(128)} %bitcast.col, s32[1]{0:T(128)} %bitcast.1.low, bf16[1024,256]{1,0:T(8,128)(2,1)} %bitcast.10, s32[8,128]{1,0:T(8,128)} %mask.1), custom_call_target="tpu_custom_call" | custom-call | bytes 1048576 | tf_op jit(solution)/shard_map/pallas_call | solution.py:281
  5.7 0.1 and_convert_fusion.ok
  5.8 0.5 collective-permute-start
  6.3 3.0 %collective-permute-start.3 = (bf16[528,256]{1,0:T(8,128)(2,1)S(1)}, bf16[528,256]{1,0:T(8,128)(2,1)S(1)}, u32[]{:S(2)}, u32[]{:S(2)}) collective-permute-start(bf16[528,256]{1,0:T(8,128)(2,1)S(1)} %get-tuple-element.49), channel_id=1, source_target_pairs={{4,8},{12,16},{20,24},{8,4},{16,12},{24,20},{5,9},{13,17},{21,25},... | collective-permute-start | bytes 811016 | tf_op jit(solution)/shard_map/ppermute | solution.py:729
  9.4 3.3 %shard_map.137 = bf16[512,384]{1,0:T(8,128)(2,1)} custom-call(bf16[2,512,512]{2,1,0:T(8,128)(2,1)} %signal, bf16[192,512]{1,0:T(8,128)(2,1)} %bitcast.15, bf16[512,512]{1,0:T(8,128)(2,1)} %constant.34.clone.table.refs_9_), custom_call_target="tpu_custom_call" | custom-call | bytes 2097152 | tf_op jit(solution)/shard_map/pallas_call | solution.py:121
  12.7 5.1 %all-to-all-start = ((bf16[32,16,384]{2,1,0:T(8,128)(2,1)}), bf16[32,16,384]{2,1,0:T(8,128)(2,1)S(1)}, u32[]{:S(2)}, u32[]{:S(2)}) async-start(bf16[32,16,384]{2,1,0:T(8,128)(2,1)} %bitcast.4), calls=%async_computation | async-start | bytes 786432 | tf_op jit(solution)/shard_map/all_to_all | solution.py:708
  17.8 1.7 %shard_map.138 = (bf16[3,3,256,256]{3,2,1,0:T(8,128)(2,1)S(1)}, bf16[3,3,256,256]{3,2,1,0:T(8,128)(2,1)S(1)}) custom-call(bf16[3,3,256,256]{3,2,1,0:T(8,128)(2,1)} %refs_0_, bf16[3,3,256,256]{3,2,1,0:T(8,128)(2,1)} %refs_1_.1), custom_call_target="tpu_custom_call" | custom-call | bytes 5242880 | tf_op jit(solution)/shard_map/pallas_call | solution.py:303
  19.6 0.0 copy-done.2
  19.6 5.7 %shard_map.139 = (f32[2048,256]{1,0:T(8,128)S(1)}, f32[1536,256]{1,0:T(8,128)S(1)}) custom-call(s32[1]{0:T(128)} %bitcast.col, s32[1]{0:T(128)} %bitcast.1.low, bf16[8,128,256]{2,1,0:T(8,128)(2,1)S(1)} %collective-permute-done.1.early.refs_0_.refs_5_, bf16[8,128,256]{2,1,0:T(8,128)(2,1)S(1)} %copy-done.2, ...), custom_call_target="tpu_custom_call" | custom-call | flops 5435817984 | bytes 8388608 | tf_op jit(solution)/shard_map/pallas_call | solution.py:608
  25.4 0.1 shard_map.141
  25.5 0.9 collective-permute-start.7
  26.4 3.9 %collective-permute-start.8 = (bf16[43,8,256]{2,1,0:T(8,128)(2,1)S(1)}, bf16[43,8,256]{2,1,0:T(8,128)(2,1)S(1)}, u32[]{:S(2)}, u32[]{:S(2)}) collective-permute-start(bf16[43,8,256]{2,1,0:T(8,128)(2,1)S(1)} %get-tuple-element.56), channel_id=1, source_target_pairs={{0,1},{2,3},{1,0},{3,2},{4,5},{6,7},{5,4},{7,6},{8,9},{10,11},{9,8... | collective-permute-start | bytes 528392 | tf_op jit(solution)/shard_map/ppermute | solution.py:736
  30.2 3.9 %shard_map.140 = (bf16[2,112,256]{2,1,0:T(8,128)(2,1)S(1)}, bf16[2,112,256]{2,1,0:T(8,128)(2,1)S(1)}, bf16[2,112,256]{2,1,0:T(8,128)(2,1)S(1)}, bf16[2,112,256]{2,1,0:T(8,128)(2,1)S(1)}) custom-call(s32[1]{0:T(128)} %bitcast.col, s32[1]{0:T(128)} %bitcast.1.low, f32[2048,256]{1,0:T(8,128)S(1)} %get-tuple-element.46.pre, ...), custom_call_target="tpu_custom_call" | custom-call | flops 3019898880 | bytes 8388608 | tf_op jit(solution)/shard_map/pallas_call | solution.py:632
  34.1 0.1 collective-permute-start.4
  34.2 2.1 %collective-permute-start.5 = (bf16[2,112,256]{2,1,0:T(8,128)(2,1)S(1)}, bf16[2,112,256]{2,1,0:T(8,128)(2,1)S(1)}, u32[]{:S(2)}, u32[]{:S(2)}) collective-permute-start(bf16[2,112,256]{2,1,0:T(8,128)(2,1)S(1)} %get-tuple-element.53), channel_id=1, source_target_pairs={{0,3},{1,2},{2,1},{3,0},{4,7},{5,6},{6,5},{7,4},{8,11},{9,10},{10,... | collective-permute-start | bytes 344072 | tf_op jit(solution)/shard_map/ppermute | solution.py:745
  36.3 0.5 collective-permute-start.6
  36.8 0.0 copy-start.7
  36.9 3.9 %shard_map.142 = (bf16[2,16,256]{2,1,0:T(8,128)(2,1)S(1)}, bf16[2,16,256]{2,1,0:T(8,128)(2,1)S(1)}, bf16[2,16,256]{2,1,0:T(8,128)(2,1)S(1)}, bf16[2,16,256]{2,1,0:T(8,128)(2,1)S(1)}) custom-call(s32[1]{0:T(128)} %bitcast.col, s32[1]{0:T(128)} %bitcast.1.low, bf16[43,8,256]{2,1,0:T(8,128)(2,1)S(1)} %collective-permute-done.7.late, ...), custom_call_target="tpu_custom_call" | custom-call | flops 3170893824 | bytes 4194304 | tf_op jit(solution)/shard_map/pallas_call | solution.py:655
  40.7 0.0 copy-start.1
  40.8 1.0 %collective-permute-start.9 = (bf16[2,16,256]{2,1,0:T(8,128)(2,1)S(1)}, bf16[2,16,256]{2,1,0:T(8,128)(2,1)S(1)}, u32[]{:S(2)}, u32[]{:S(2)}) collective-permute-start(bf16[2,16,256]{2,1,0:T(8,128)(2,1)S(1)} %get-tuple-element.65), channel_id=1, source_target_pairs={{0,2},{1,3},{2,0},{3,1},{4,6},{5,7},{6,4},{7,5},{8,10},{9,11},{10,... | collective-permute-start | bytes 49160 | tf_op jit(solution)/shard_map/ppermute | solution.py:745
  41.8 2.0 %collective-permute-start.10 = (bf16[2,16,256]{2,1,0:T(8,128)(2,1)S(1)}, bf16[2,16,256]{2,1,0:T(8,128)(2,1)S(1)}, u32[]{:S(2)}, u32[]{:S(2)}) collective-permute-start(bf16[2,16,256]{2,1,0:T(8,128)(2,1)S(1)} %get-tuple-element.66), channel_id=1, source_target_pairs={{0,3},{1,2},{2,1},{3,0},{4,7},{5,6},{6,5},{7,4},{8,11},{9,10},{10,... | collective-permute-start | bytes 49160 | tf_op jit(solution)/shard_map/ppermute | solution.py:745
  43.8 1.0 %collective-permute-done.4.refs_1_ = bf16[2,112,256]{2,1,0:T(8,128)(2,1)S(1)} collective-permute-done((bf16[2,112,256]{2,1,0:T(8,128)(2,1)S(1)}, bf16[2,112,256]{2,1,0:T(8,128)(2,1)S(1)}, u32[]{:S(2)}, u32[]{:S(2)}) %collective-permute-start.4) | collective-permute-done | bytes 114720 | tf_op jit(solution)/shard_map/ppermute | solution.py:745
  44.9 1.0 %shard_map.143.slope = f32[2,512,192]{2,1,0:T(8,128)S(1)} custom-call(bf16[512,384]{1,0:T(8,128)(2,1)S(1)} %bitcast.11, bf16[384,384]{1,0:T(8,128)(2,1)S(1)} %copy-done.3, bf16[128,128]{1,0:T(8,128)(2,1)S(1)} %copy-done.7), custom_call_target="tpu_custom_call" | custom-call | bytes 1507328 | tf_op jit(solution)/shard_map/pallas_call | solution.py:30
  45.8 0.0 copy-start.9
  45.9 2.3 %collective-permute-done.9.refs_5_ = bf16[2,16,256]{2,1,0:T(8,128)(2,1)S(1)} collective-permute-done((bf16[2,16,256]{2,1,0:T(8,128)(2,1)S(1)}, bf16[2,16,256]{2,1,0:T(8,128)(2,1)S(1)}, u32[]{:S(2)}, u32[]{:S(2)}) %collective-permute-start.9) | collective-permute-done | bytes 16416 | tf_op jit(solution)/shard_map/ppermute | solution.py:745
  48.2 0.9 %shard_map.144 = (bf16[512,384]{1,0:T(8,128)(2,1)S(1)}, bf16[4,2,128,256]{3,2,1,0:T(8,128)(2,1)S(1)}) custom-call(s32[1]{0:T(128)} %bitcast.col, s32[1]{0:T(128)} %bitcast.1.low, bf16[2,112,256]{2,1,0:T(8,128)(2,1)S(1)} %get-tuple-element.51.refs_0_, bf16[2,112,256]{2,1,0:T(8,128)(2,1)S(1)} %collective-permute-done.4.refs_1_, ...), custom_call_target="tpu_custom_call" | custom-call | bytes 2097152 | tf_op jit(solution)/shard_map/pallas_call | solution.py:87
  49.1 17.8 %all_to_all.34 = bf16[32,16,384]{2,1,0:T(8,128)(2,1)S(1)} all-to-all(bf16[32,16,384]{2,1,0:T(8,128)(2,1)S(1)} %bitcast.17), channel_id=1, replica_groups=mesh['row'=8,'col'=4] {'col','row'}, dimensions={0} | all-to-all | bytes 786432 | tf_op jit(solution)/shard_map/all_to_all | solution.py:708
  66.9 1.2 %shard_map.145 = bf16[512,384]{1,0:T(8,128)(2,1)S(1)} custom-call(bf16[512,384]{1,0:T(8,128)(2,1)S(1)} %bitcast.12, f32[2,512,192]{2,1,0:T(8,128)S(1)} %shard_map.143.slope, bf16[384,384]{1,0:T(8,128)(2,1)S(1)} %copy-done.3, bf16[128,128]{1,0:T(8,128)(2,1)S(1)} %copy-done.7, bf16[128,128]{1,0:T(8,128)(2,1)S(1)} %copy-done.9), custom_call_target="tpu_custom_call" | custom-call | bytes 1933312 | tf_op jit(solution)/shard_map/pallas_call | solution.py:30
  68.1 15.6 %all_to_all.35 = bf16[32,16,384]{2,1,0:T(8,128)(2,1)S(1)} all-to-all(bf16[32,16,384]{2,1,0:T(8,128)(2,1)S(1)} %bitcast.13), channel_id=1, replica_groups=mesh['row'=8,'col'=4] {'col','row'}, dimensions={0} | all-to-all | bytes 786432 | tf_op jit(solution)/shard_map/all_to_all | solution.py:708
  83.7 1.7 %shard_map.146 = bf16[2,512,512]{2,1,0:T(8,128)(2,1)} custom-call(bf16[512,384]{1,0:T(8,128)(2,1)S(1)} %bitcast.14, bf16[4,2,128,256]{3,2,1,0:T(8,128)(2,1)S(1)} %get-tuple-element.70.strip_grad, bf16[192,512]{1,0:T(8,128)(2,1)S(1)} %bitcast.16, bf16[512,256]{1,0:T(8,128)(2,1)S(1)} %copy-done.6, bf16[512,512]{1,0:T(8,128)(2,1)S(1)} %copy-done.5), custom_call_target="tpu_custom_call" | custom-call | bytes 3145728 | tf_op jit(solution)/shard_map/pallas_call | solution.py:216
  (30 shorter events, 0.1 us)
Async XLA Ops:
  0.0 19.5 %collective-permute-start.2 = (bf16[8,128,256]{2,1,0:T(8,128)(2,1)}, bf16[8,128,256]{2,1,0:T(8,128)(2,1)S(1)}, u32[]{:S(2)}, u32[]{:S(2)}) collective-permute-start(bf16[8,128,256]{2,1,0:T(8,128)(2,1)} %refs_7_.1), channel_id=1, source_target_pairs={{4,8},{12,16},{20,24},{8,4},{16,12},{24,20},{5,9},{13,17},{21,25},... | collective-permute-start | bytes 1572872 | tf_op jit(solution)/shard_map/ppermute | solution.py:725
  4.5 15.1 %collective-permute-start.1 = (bf16[8,128,256]{2,1,0:T(8,128)(2,1)}, bf16[8,128,256]{2,1,0:T(8,128)(2,1)S(1)}, u32[]{:S(2)}, u32[]{:S(2)}) collective-permute-start(bf16[8,128,256]{2,1,0:T(8,128)(2,1)} %refs_7_.1), channel_id=1, source_target_pairs={{0,4},{8,12},{16,20},{24,28},{4,0},{12,8},{20,16},{28,24},{1,5},{9... | collective-permute-start | bytes 1572872 | tf_op jit(solution)/shard_map/ppermute | solution.py:724
  5.8 19.5 %collective-permute-start = (bf16[528,256]{1,0:T(8,128)(2,1)S(1)}, bf16[528,256]{1,0:T(8,128)(2,1)S(1)}, u32[]{:S(2)}, u32[]{:S(2)}) collective-permute-start(bf16[528,256]{1,0:T(8,128)(2,1)S(1)} %get-tuple-element.39), channel_id=1, source_target_pairs={{0,4},{8,12},{16,20},{24,28},{4,0},{12,8},{20,16},{28,24},{1,5},{9... | collective-permute-start | bytes 811016 | tf_op jit(solution)/shard_map/ppermute | solution.py:728
  6.3 19.0 %collective-permute-start.3 = (bf16[528,256]{1,0:T(8,128)(2,1)S(1)}, bf16[528,256]{1,0:T(8,128)(2,1)S(1)}, u32[]{:S(2)}, u32[]{:S(2)}) collective-permute-start(bf16[528,256]{1,0:T(8,128)(2,1)S(1)} %get-tuple-element.49), channel_id=1, source_target_pairs={{4,8},{12,16},{20,24},{8,4},{16,12},{24,20},{5,9},{13,17},{21,25},... | collective-permute-start | bytes 811016 | tf_op jit(solution)/shard_map/ppermute | solution.py:729
  12.7 28.1 %all-to-all-start = ((bf16[32,16,384]{2,1,0:T(8,128)(2,1)}), bf16[32,16,384]{2,1,0:T(8,128)(2,1)S(1)}, u32[]{:S(2)}, u32[]{:S(2)}) async-start(bf16[32,16,384]{2,1,0:T(8,128)(2,1)} %bitcast.4), calls=%async_computation | async-start | bytes 786432 | tf_op jit(solution)/shard_map/all_to_all | solution.py:708
  17.8 1.8 %copy-start.2 = (bf16[8,128,256]{2,1,0:T(8,128)(2,1)S(1)}, bf16[8,128,256]{2,1,0:T(8,128)(2,1)}, u32[]{:S(2)}) copy-start(bf16[8,128,256]{2,1,0:T(8,128)(2,1)} %refs_7_.1) | copy-start | bytes 1572868
  19.6 5.8 %copy-start = (bf16[8,128,256]{2,1,0:T(8,128)(2,1)S(1)}, bf16[8,128,256]{2,1,0:T(8,128)(2,1)}, u32[]{:S(2)}) copy-start(bf16[8,128,256]{2,1,0:T(8,128)(2,1)} %refs_8_.2) | copy-start | bytes 1572868
  25.5 11.3 %collective-permute-start.7 = (bf16[43,8,256]{2,1,0:T(8,128)(2,1)S(1)}, bf16[43,8,256]{2,1,0:T(8,128)(2,1)S(1)}, u32[]{:S(2)}, u32[]{:S(2)}) collective-permute-start(bf16[43,8,256]{2,1,0:T(8,128)(2,1)S(1)} %get-tuple-element.55), channel_id=1, source_target_pairs={{1,2},{2,1},{5,6},{6,5},{9,10},{10,9},{13,14},{14,13},{17,18},{18,... | collective-permute-start | bytes 528392 | tf_op jit(solution)/shard_map/ppermute | solution.py:735
  26.4 10.5 %collective-permute-start.8 = (bf16[43,8,256]{2,1,0:T(8,128)(2,1)S(1)}, bf16[43,8,256]{2,1,0:T(8,128)(2,1)S(1)}, u32[]{:S(2)}, u32[]{:S(2)}) collective-permute-start(bf16[43,8,256]{2,1,0:T(8,128)(2,1)S(1)} %get-tuple-element.56), channel_id=1, source_target_pairs={{0,1},{2,3},{1,0},{3,2},{4,5},{6,7},{5,4},{7,6},{8,9},{10,11},{9,8... | collective-permute-start | bytes 528392 | tf_op jit(solution)/shard_map/ppermute | solution.py:736
  34.1 10.7 %collective-permute-start.4 = (bf16[2,112,256]{2,1,0:T(8,128)(2,1)S(1)}, bf16[2,112,256]{2,1,0:T(8,128)(2,1)S(1)}, u32[]{:S(2)}, u32[]{:S(2)}) collective-permute-start(bf16[2,112,256]{2,1,0:T(8,128)(2,1)S(1)} %get-tuple-element.52), channel_id=1, source_target_pairs={{0,2},{1,3},{2,0},{3,1},{4,6},{5,7},{6,4},{7,5},{8,10},{9,11},{10,... | collective-permute-start | bytes 344072 | tf_op jit(solution)/shard_map/ppermute | solution.py:745
  34.2 11.7 %collective-permute-start.5 = (bf16[2,112,256]{2,1,0:T(8,128)(2,1)S(1)}, bf16[2,112,256]{2,1,0:T(8,128)(2,1)S(1)}, u32[]{:S(2)}, u32[]{:S(2)}) collective-permute-start(bf16[2,112,256]{2,1,0:T(8,128)(2,1)S(1)} %get-tuple-element.53), channel_id=1, source_target_pairs={{0,3},{1,2},{2,1},{3,0},{4,7},{5,6},{6,5},{7,4},{8,11},{9,10},{10,... | collective-permute-start | bytes 344072 | tf_op jit(solution)/shard_map/ppermute | solution.py:745
  36.3 9.6 %collective-permute-start.6 = (bf16[2,112,256]{2,1,0:T(8,128)(2,1)S(1)}, bf16[2,112,256]{2,1,0:T(8,128)(2,1)S(1)}, u32[]{:S(2)}, u32[]{:S(2)}) collective-permute-start(bf16[2,112,256]{2,1,0:T(8,128)(2,1)S(1)} %get-tuple-element.54), channel_id=1, source_target_pairs={{0,1},{1,0},{2,3},{3,2},{4,5},{5,4},{6,7},{7,6},{8,9},{9,8},{10,11... | collective-permute-start | bytes 344072 | tf_op jit(solution)/shard_map/ppermute | solution.py:745
  36.8 8.0 %copy-start.3 = (bf16[384,384]{1,0:T(8,128)(2,1)S(1)}, bf16[384,384]{1,0:T(8,128)(2,1)}, u32[]{:S(2)}) copy-start(bf16[384,384]{1,0:T(8,128)(2,1)} %mix.3) | copy-start | bytes 884740
  36.8 8.0 %copy-start.7 = (bf16[128,128]{1,0:T(8,128)(2,1)S(1)}, bf16[128,128]{1,0:T(8,128)(2,1)}, u32[]{:S(2)}) copy-start(bf16[128,128]{1,0:T(8,128)(2,1)} %constant.36.clone.table) | copy-start | bytes 98308
  40.7 7.5 %copy-start.1 = (bf16[512,512]{1,0:T(8,128)(2,1)S(1)}, bf16[512,512]{1,0:T(8,128)(2,1)}, u32[]{:S(2)}) copy-start(bf16[512,512]{1,0:T(8,128)(2,1)} %constant.34.clone.table.refs_9_) | copy-start | bytes 1572868
  40.7 7.5 %copy-start.8 = (bf16[192,256]{1,0:T(8,128)(2,1)S(1)}, bf16[192,256]{1,0:T(8,128)(2,1)}, u32[]{:S(2)}) copy-start(bf16[192,256]{1,0:T(8,128)(2,1)} %refs_8_.3) | copy-start | bytes 294916
  40.8 7.4 %collective-permute-start.9 = (bf16[2,16,256]{2,1,0:T(8,128)(2,1)S(1)}, bf16[2,16,256]{2,1,0:T(8,128)(2,1)S(1)}, u32[]{:S(2)}, u32[]{:S(2)}) collective-permute-start(bf16[2,16,256]{2,1,0:T(8,128)(2,1)S(1)} %get-tuple-element.65), channel_id=1, source_target_pairs={{0,2},{1,3},{2,0},{3,1},{4,6},{5,7},{6,4},{7,5},{8,10},{9,11},{10,... | collective-permute-start | bytes 49160 | tf_op jit(solution)/shard_map/ppermute | solution.py:745
  41.8 6.4 %collective-permute-start.10 = (bf16[2,16,256]{2,1,0:T(8,128)(2,1)S(1)}, bf16[2,16,256]{2,1,0:T(8,128)(2,1)S(1)}, u32[]{:S(2)}, u32[]{:S(2)}) collective-permute-start(bf16[2,16,256]{2,1,0:T(8,128)(2,1)S(1)} %get-tuple-element.66), channel_id=1, source_target_pairs={{0,3},{1,2},{2,1},{3,0},{4,7},{5,6},{6,5},{7,4},{8,11},{9,10},{10,... | collective-permute-start | bytes 49160 | tf_op jit(solution)/shard_map/ppermute | solution.py:745
  44.9 3.3 %collective-permute-start.11 = (bf16[2,16,256]{2,1,0:T(8,128)(2,1)S(1)}, bf16[2,16,256]{2,1,0:T(8,128)(2,1)S(1)}, u32[]{:S(2)}, u32[]{:S(2)}) collective-permute-start(bf16[2,16,256]{2,1,0:T(8,128)(2,1)S(1)} %get-tuple-element.67), channel_id=1, source_target_pairs={{0,1},{1,0},{2,3},{3,2},{4,5},{5,4},{6,7},{7,6},{8,9},{9,8},{10,11... | collective-permute-start | bytes 49160 | tf_op jit(solution)/shard_map/ppermute | solution.py:745
  45.8 21.1 %copy-start.9 = (bf16[128,128]{1,0:T(8,128)(2,1)S(1)}, bf16[128,128]{1,0:T(8,128)(2,1)}, u32[]{:S(2)}) copy-start(bf16[128,128]{1,0:T(8,128)(2,1)} %constant.35.clone.back_table) | copy-start | bytes 98308
  66.9 16.8 %copy-start.4 = (bf16[512,192]{0,1:T(8,128)(2,1)S(1)}, bf16[512,192]{0,1:T(8,128)(2,1)}, u32[]{:S(2)}) copy-start(bf16[512,192]{0,1:T(8,128)(2,1)} %param.20) | copy-start | bytes 589828
  66.9 16.8 %copy-start.5 = (bf16[512,512]{1,0:T(8,128)(2,1)S(1)}, bf16[512,512]{1,0:T(8,128)(2,1)}, u32[]{:S(2)}) copy-start(bf16[512,512]{1,0:T(8,128)(2,1)} %constant.33.clone.table) | copy-start | bytes 1572868
  66.9 16.8 %copy-start.6 = (bf16[512,256]{1,0:T(8,128)(2,1)S(1)}, bf16[512,256]{1,0:T(8,128)(2,1)}, u32[]{:S(2)}) copy-start(bf16[512,256]{1,0:T(8,128)(2,1)} %weight_local.1) | copy-start | bytes 786436

commit v24 on v23

--- a/solution.py
+++ b/solution.py
@@ -465,7 +465,7 @@
 
 
 TILE_BLOCKS = (2, 2, 2, 2)
-SIDE_BLOCKS = (5, 4, 6, 4)
+SIDE_BLOCKS = (5, 8, 6, 8)
 
 
 def tile_forward_kernel(

time: 86.9 us -> 87.5 us (level)
  transfers between devices with their start and end apart: 13 -> 13, of which waited for: 2 -> 2; matrix products, arithmetic and copies ran while one was open for 0% -> 0% of each run, Pallas kernels for 24% -> 25%
where the time goes in v24:
time: 87.5 us; the launch traced here: 86.2 us
  blocking collectives  34.1 us (39%)
  Pallas kernels  25 us (29%)
  starting transfers between devices  23.8 us (27%)
  waiting for transfers between devices  2.76 us (3%)
    all_to_all x2, blocking collectives, swap(): lax.all_to_all(spectrum, ('col', 'row'), split_axis=0, concat_axis=0, til...  34.1 us
    ppermute x6, starting transfers between devices, dealt(): result.append(lax.ppermute(piece, 'col', swaps) if step else piece)  5.79 us
    pallas_call x1, Pallas kernels, tile_forward(): pl.pallas_call(tile_forward_kernel, out_shape=shapes, in_specs=[pl.BlockS...  5.74 us
    all_to_all x1, starting transfers between devices, swap(): lax.all_to_all(spectrum, ('col', 'row'), split_axis=0, concat_axis=0, til...  5.12 us
    ppermute x1, starting transfers between devices, shards(): late = lax.ppermute(features, 'row', pairs('row', 1))  4.5 us
    pallas_call x1, Pallas kernels, sides(): pl.pallas_call(side_kernel, out_shape=shapes, in_specs=[pl.BlockSpec(memo...  4.48 us
    ppermute x1, starting transfers between devices, shards(): early_edge = lax.ppermute(early_edge, 'col', pairs('col', 0))  3.88 us
    pallas_call x1, Pallas kernels, tile_backward(): pl.pallas_call(tile_backward_kernel, out_shape=shapes, in_specs=[pl.Block...  3.86 us
  transfers between devices with their start and end apart: 13, of which 2 were waited for; matrix products, arithmetic and copies ran while one was open for 0% of the time, Pallas kernels for 25%

profile of v24, /device:TPU:1, one launch (start us, length us, event | category | flops | bytes accessed | tf_op | source)
XLA Modules:
  0.0 86.2 jit_solution(1348135852987610560)
XLA Ops:
  0.0 4.5 %collective-permute-start.2 = (bf16[8,128,256]{2,1,0:T(8,128)(2,1)}, bf16[8,128,256]{2,1,0:T(8,128)(2,1)S(1)}, u32[]{:S(2)}, u32[]{:S(2)}) collective-permute-start(bf16[8,128,256]{2,1,0:T(8,128)(2,1)} %refs_7_.1), channel_id=1, source_target_pairs={{4,8},{12,16},{20,24},{8,4},{16,12},{24,20},{5,9},{13,17},{21,25},... | collective-permute-start | bytes 1572872 | tf_op jit(solution)/shard_map/ppermute | solution.py:725
  4.5 0.1 collective-permute-start.1
  4.6 1.1 %shard_map.136 = (bf16[528,256]{1,0:T(8,128)(2,1)S(1)}, bf16[528,256]{1,0:T(8,128)(2,1)S(1)}, bf16[1,128,256]{2,1,0:T(8,128)(2,1)S(1)}) custom-call(s32[1]{0:T(128)} %bitcast.col, s32[1]{0:T(128)} %bitcast.1.low, bf16[1024,256]{1,0:T(8,128)(2,1)} %bitcast.10, s32[8,128]{1,0:T(8,128)} %mask.1), custom_call_target="tpu_custom_call" | custom-call | bytes 1048576 | tf_op jit(solution)/shard_map/pallas_call | solution.py:281
  5.7 0.1 and_convert_fusion.ok
  5.8 0.5 collective-permute-start
  6.3 3.0 %collective-permute-start.3 = (bf16[528,256]{1,0:T(8,128)(2,1)S(1)}, bf16[528,256]{1,0:T(8,128)(2,1)S(1)}, u32[]{:S(2)}, u32[]{:S(2)}) collective-permute-start(bf16[528,256]{1,0:T(8,128)(2,1)S(1)} %get-tuple-element.49), channel_id=1, source_target_pairs={{4,8},{12,16},{20,24},{8,4},{16,12},{24,20},{5,9},{13,17},{21,25},... | collective-permute-start | bytes 811016 | tf_op jit(solution)/shard_map/ppermute | solution.py:729
  9.4 3.3 %shard_map.137 = bf16[512,384]{1,0:T(8,128)(2,1)} custom-call(bf16[2,512,512]{2,1,0:T(8,128)(2,1)} %signal, bf16[192,512]{1,0:T(8,128)(2,1)} %bitcast.15, bf16[512,512]{1,0:T(8,128)(2,1)} %constant.34.clone.table.refs_9_), custom_call_target="tpu_custom_call" | custom-call | bytes 2097152 | tf_op jit(solution)/shard_map/pallas_call | solution.py:121
  12.7 5.1 %all-to-all-start = ((bf16[32,16,384]{2,1,0:T(8,128)(2,1)}), bf16[32,16,384]{2,1,0:T(8,128)(2,1)S(1)}, u32[]{:S(2)}, u32[]{:S(2)}) async-start(bf16[32,16,384]{2,1,0:T(8,128)(2,1)} %bitcast.4), calls=%async_computation | async-start | bytes 786432 | tf_op jit(solution)/shard_map/all_to_all | solution.py:708
  17.8 1.7 %shard_map.138 = (bf16[3,3,256,256]{3,2,1,0:T(8,128)(2,1)S(1)}, bf16[3,3,256,256]{3,2,1,0:T(8,128)(2,1)S(1)}) custom-call(bf16[3,3,256,256]{3,2,1,0:T(8,128)(2,1)} %refs_0_, bf16[3,3,256,256]{3,2,1,0:T(8,128)(2,1)} %refs_1_.1), custom_call_target="tpu_custom_call" | custom-call | bytes 5242880 | tf_op jit(solution)/shard_map/pallas_call | solution.py:303
  19.6 0.0 copy-done.2
  19.6 5.7 %shard_map.139 = (f32[2048,256]{1,0:T(8,128)S(1)}, f32[1536,256]{1,0:T(8,128)S(1)}) custom-call(s32[1]{0:T(128)} %bitcast.col, s32[1]{0:T(128)} %bitcast.1.low, bf16[8,128,256]{2,1,0:T(8,128)(2,1)S(1)} %collective-permute-done.1.early.refs_0_.refs_5_, bf16[8,128,256]{2,1,0:T(8,128)(2,1)S(1)} %copy-done.2, ...), custom_call_target="tpu_custom_call" | custom-call | flops 5435817984 | bytes 8388608 | tf_op jit(solution)/shard_map/pallas_call | solution.py:608
  25.4 0.1 shard_map.141
  25.5 0.9 collective-permute-start.7
  26.4 3.9 %collective-permute-start.8 = (bf16[43,8,256]{2,1,0:T(8,128)(2,1)S(1)}, bf16[43,8,256]{2,1,0:T(8,128)(2,1)S(1)}, u32[]{:S(2)}, u32[]{:S(2)}) collective-permute-start(bf16[43,8,256]{2,1,0:T(8,128)(2,1)S(1)} %get-tuple-element.56), channel_id=1, source_target_pairs={{0,1},{2,3},{1,0},{3,2},{4,5},{6,7},{5,4},{7,6},{8,9},{10,11},{9,8... | collective-permute-start | bytes 528392 | tf_op jit(solution)/shard_map/ppermute | solution.py:736
  30.2 3.9 %shard_map.140 = (bf16[2,112,256]{2,1,0:T(8,128)(2,1)S(1)}, bf16[2,112,256]{2,1,0:T(8,128)(2,1)S(1)}, bf16[2,112,256]{2,1,0:T(8,128)(2,1)S(1)}, bf16[2,112,256]{2,1,0:T(8,128)(2,1)S(1)}) custom-call(s32[1]{0:T(128)} %bitcast.col, s32[1]{0:T(128)} %bitcast.1.low, f32[2048,256]{1,0:T(8,128)S(1)} %get-tuple-element.46.pre, ...), custom_call_target="tpu_custom_call" | custom-call | flops 3019898880 | bytes 8388608 | tf_op jit(solution)/shard_map/pallas_call | solution.py:632
  34.1 0.1 collective-permute-start.4
  34.2 2.1 %collective-permute-start.5 = (bf16[2,112,256]{2,1,0:T(8,128)(2,1)S(1)}, bf16[2,112,256]{2,1,0:T(8,128)(2,1)S(1)}, u32[]{:S(2)}, u32[]{:S(2)}) collective-permute-start(bf16[2,112,256]{2,1,0:T(8,128)(2,1)S(1)} %get-tuple-element.53), channel_id=1, source_target_pairs={{0,3},{1,2},{2,1},{3,0},{4,7},{5,6},{6,5},{7,4},{8,11},{9,10},{10,... | collective-permute-start | bytes 344072 | tf_op jit(solution)/shard_map/ppermute | solution.py:745
  36.3 0.5 collective-permute-start.6
  36.8 0.0 copy-start.7
  36.9 4.5 %shard_map.142 = (bf16[2,16,256]{2,1,0:T(8,128)(2,1)S(1)}, bf16[2,16,256]{2,1,0:T(8,128)(2,1)S(1)}, bf16[2,16,256]{2,1,0:T(8,128)(2,1)S(1)}, bf16[2,16,256]{2,1,0:T(8,128)(2,1)S(1)}) custom-call(s32[1]{0:T(128)} %bitcast.col, s32[1]{0:T(128)} %bitcast.1.low, bf16[43,8,256]{2,1,0:T(8,128)(2,1)S(1)} %collective-permute-done.7.late, ...), custom_call_target="tpu_custom_call" | custom-call | flops 3170893824 | bytes 4194304 | tf_op jit(solution)/shard_map/pallas_call | solution.py:655
  41.3 0.0 copy-start.1
  41.4 1.1 %collective-permute-start.9 = (bf16[2,16,256]{2,1,0:T(8,128)(2,1)S(1)}, bf16[2,16,256]{2,1,0:T(8,128)(2,1)S(1)}, u32[]{:S(2)}, u32[]{:S(2)}) collective-permute-start(bf16[2,16,256]{2,1,0:T(8,128)(2,1)S(1)} %get-tuple-element.65), channel_id=1, source_target_pairs={{0,2},{1,3},{2,0},{3,1},{4,6},{5,7},{6,4},{7,5},{8,10},{9,11},{10,... | collective-permute-start | bytes 49160 | tf_op jit(solution)/shard_map/ppermute | solution.py:745
  42.4 2.0 %collective-permute-start.10 = (bf16[2,16,256]{2,1,0:T(8,128)(2,1)S(1)}, bf16[2,16,256]{2,1,0:T(8,128)(2,1)S(1)}, u32[]{:S(2)}, u32[]{:S(2)}) collective-permute-start(bf16[2,16,256]{2,1,0:T(8,128)(2,1)S(1)} %get-tuple-element.66), channel_id=1, source_target_pairs={{0,3},{1,2},{2,1},{3,0},{4,7},{5,6},{6,5},{7,4},{8,11},{9,10},{10,... | collective-permute-start | bytes 49160 | tf_op jit(solution)/shard_map/ppermute | solution.py:745
  44.4 0.4 collective-permute-done.4.refs_1_
  44.9 1.0 %shard_map.143.slope = f32[2,512,192]{2,1,0:T(8,128)S(1)} custom-call(bf16[512,384]{1,0:T(8,128)(2,1)S(1)} %bitcast.11, bf16[384,384]{1,0:T(8,128)(2,1)S(1)} %copy-done.3, bf16[128,128]{1,0:T(8,128)(2,1)S(1)} %copy-done.7), custom_call_target="tpu_custom_call" | custom-call | bytes 1507328 | tf_op jit(solution)/shard_map/pallas_call | solution.py:30
  45.8 0.0 copy-start.9
  45.9 2.3 %collective-permute-done.9.refs_5_ = bf16[2,16,256]{2,1,0:T(8,128)(2,1)S(1)} collective-permute-done((bf16[2,16,256]{2,1,0:T(8,128)(2,1)S(1)}, bf16[2,16,256]{2,1,0:T(8,128)(2,1)S(1)}, u32[]{:S(2)}, u32[]{:S(2)}) %collective-permute-start.9) | collective-permute-done | bytes 16416 | tf_op jit(solution)/shard_map/ppermute | solution.py:745
  48.2 0.9 %shard_map.144 = (bf16[512,384]{1,0:T(8,128)(2,1)S(1)}, bf16[4,2,128,256]{3,2,1,0:T(8,128)(2,1)S(1)}) custom-call(s32[1]{0:T(128)} %bitcast.col, s32[1]{0:T(128)} %bitcast.1.low, bf16[2,112,256]{2,1,0:T(8,128)(2,1)S(1)} %get-tuple-element.51.refs_0_, bf16[2,112,256]{2,1,0:T(8,128)(2,1)S(1)} %collective-permute-done.4.refs_1_, ...), custom_call_target="tpu_custom_call" | custom-call | bytes 2097152 | tf_op jit(solution)/shard_map/pallas_call | solution.py:87
  49.1 18.4 %all_to_all.34 = bf16[32,16,384]{2,1,0:T(8,128)(2,1)S(1)} all-to-all(bf16[32,16,384]{2,1,0:T(8,128)(2,1)S(1)} %bitcast.17), channel_id=1, replica_groups=mesh['row'=8,'col'=4] {'col','row'}, dimensions={0} | all-to-all | bytes 786432 | tf_op jit(solution)/shard_map/all_to_all | solution.py:708
  67.5 1.2 %shard_map.145 = bf16[512,384]{1,0:T(8,128)(2,1)S(1)} custom-call(bf16[512,384]{1,0:T(8,128)(2,1)S(1)} %bitcast.12, f32[2,512,192]{2,1,0:T(8,128)S(1)} %shard_map.143.slope, bf16[384,384]{1,0:T(8,128)(2,1)S(1)} %copy-done.3, bf16[128,128]{1,0:T(8,128)(2,1)S(1)} %copy-done.7, bf16[128,128]{1,0:T(8,128)(2,1)S(1)} %copy-done.9), custom_call_target="tpu_custom_call" | custom-call | bytes 1933312 | tf_op jit(solution)/shard_map/pallas_call | solution.py:30
  68.7 15.6 %all_to_all.35 = bf16[32,16,384]{2,1,0:T(8,128)(2,1)S(1)} all-to-all(bf16[32,16,384]{2,1,0:T(8,128)(2,1)S(1)} %bitcast.13), channel_id=1, replica_groups=mesh['row'=8,'col'=4] {'col','row'}, dimensions={0} | all-to-all | bytes 786432 | tf_op jit(solution)/shard_map/all_to_all | solution.py:708
  84.3 1.7 %shard_map.146 = bf16[2,512,512]{2,1,0:T(8,128)(2,1)} custom-call(bf16[512,384]{1,0:T(8,128)(2,1)S(1)} %bitcast.14, bf16[4,2,128,256]{3,2,1,0:T(8,128)(2,1)S(1)} %get-tuple-element.70.strip_grad, bf16[192,512]{1,0:T(8,128)(2,1)S(1)} %bitcast.16, bf16[512,256]{1,0:T(8,128)(2,1)S(1)} %copy-done.6, bf16[512,512]{1,0:T(8,128)(2,1)S(1)} %copy-done.5), custom_call_target="tpu_custom_call" | custom-call | bytes 3145728 | tf_op jit(solution)/shard_map/pallas_call | solution.py:216
  (30 shorter events, 0.1 us)
Async XLA Ops:
  0.0 19.5 %collective-permute-start.2 = (bf16[8,128,256]{2,1,0:T(8,128)(2,1)}, bf16[8,128,256]{2,1,0:T(8,128)(2,1)S(1)}, u32[]{:S(2)}, u32[]{:S(2)}) collective-permute-start(bf16[8,128,256]{2,1,0:T(8,128)(2,1)} %refs_7_.1), channel_id=1, source_target_pairs={{4,8},{12,16},{20,24},{8,4},{16,12},{24,20},{5,9},{13,17},{21,25},... | collective-permute-start | bytes 1572872 | tf_op jit(solution)/shard_map/ppermute | solution.py:725
  4.5 15.1 %collective-permute-start.1 = (bf16[8,128,256]{2,1,0:T(8,128)(2,1)}, bf16[8,128,256]{2,1,0:T(8,128)(2,1)S(1)}, u32[]{:S(2)}, u32[]{:S(2)}) collective-permute-start(bf16[8,128,256]{2,1,0:T(8,128)(2,1)} %refs_7_.1), channel_id=1, source_target_pairs={{0,4},{8,12},{16,20},{24,28},{4,0},{12,8},{20,16},{28,24},{1,5},{9... | collective-permute-start | bytes 1572872 | tf_op jit(solution)/shard_map/ppermute | solution.py:724
  5.8 19.5 %collective-permute-start = (bf16[528,256]{1,0:T(8,128)(2,1)S(1)}, bf16[528,256]{1,0:T(8,128)(2,1)S(1)}, u32[]{:S(2)}, u32[]{:S(2)}) collective-permute-start(bf16[528,256]{1,0:T(8,128)(2,1)S(1)} %get-tuple-element.39), channel_id=1, source_target_pairs={{0,4},{8,12},{16,20},{24,28},{4,0},{12,8},{20,16},{28,24},{1,5},{9... | collective-permute-start | bytes 811016 | tf_op jit(solution)/shard_map/ppermute | solution.py:728
  6.3 19.0 %collective-permute-start.3 = (bf16[528,256]{1,0:T(8,128)(2,1)S(1)}, bf16[528,256]{1,0:T(8,128)(2,1)S(1)}, u32[]{:S(2)}, u32[]{:S(2)}) collective-permute-start(bf16[528,256]{1,0:T(8,128)(2,1)S(1)} %get-tuple-element.49), channel_id=1, source_target_pairs={{4,8},{12,16},{20,24},{8,4},{16,12},{24,20},{5,9},{13,17},{21,25},... | collective-permute-start | bytes 811016 | tf_op jit(solution)/shard_map/ppermute | solution.py:729
  12.7 28.7 %all-to-all-start = ((bf16[32,16,384]{2,1,0:T(8,128)(2,1)}), bf16[32,16,384]{2,1,0:T(8,128)(2,1)S(1)}, u32[]{:S(2)}, u32[]{:S(2)}) async-start(bf16[32,16,384]{2,1,0:T(8,128)(2,1)} %bitcast.4), calls=%async_computation | async-start | bytes 786432 | tf_op jit(solution)/shard_map/all_to_all | solution.py:708
  17.8 1.8 %copy-start.2 = (bf16[8,128,256]{2,1,0:T(8,128)(2,1)S(1)}, bf16[8,128,256]{2,1,0:T(8,128)(2,1)}, u32[]{:S(2)}) copy-start(bf16[8,128,256]{2,1,0:T(8,128)(2,1)} %refs_7_.1) | copy-start | bytes 1572868
  19.6 5.8 %copy-start = (bf16[8,128,256]{2,1,0:T(8,128)(2,1)S(1)}, bf16[8,128,256]{2,1,0:T(8,128)(2,1)}, u32[]{:S(2)}) copy-start(bf16[8,128,256]{2,1,0:T(8,128)(2,1)} %refs_8_.2) | copy-start | bytes 1572868
  25.5 11.3 %collective-permute-start.7 = (bf16[43,8,256]{2,1,0:T(8,128)(2,1)S(1)}, bf16[43,8,256]{2,1,0:T(8,128)(2,1)S(1)}, u32[]{:S(2)}, u32[]{:S(2)}) collective-permute-start(bf16[43,8,256]{2,1,0:T(8,128)(2,1)S(1)} %get-tuple-element.55), channel_id=1, source_target_pairs={{1,2},{2,1},{5,6},{6,5},{9,10},{10,9},{13,14},{14,13},{17,18},{18,... | collective-permute-start | bytes 528392 | tf_op jit(solution)/shard_map/ppermute | solution.py:735
  26.4 10.5 %collective-permute-start.8 = (bf16[43,8,256]{2,1,0:T(8,128)(2,1)S(1)}, bf16[43,8,256]{2,1,0:T(8,128)(2,1)S(1)}, u32[]{:S(2)}, u32[]{:S(2)}) collective-permute-start(bf16[43,8,256]{2,1,0:T(8,128)(2,1)S(1)} %get-tuple-element.56), channel_id=1, source_target_pairs={{0,1},{2,3},{1,0},{3,2},{4,5},{6,7},{5,4},{7,6},{8,9},{10,11},{9,8... | collective-permute-start | bytes 528392 | tf_op jit(solution)/shard_map/ppermute | solution.py:736
  34.1 10.7 %collective-permute-start.4 = (bf16[2,112,256]{2,1,0:T(8,128)(2,1)S(1)}, bf16[2,112,256]{2,1,0:T(8,128)(2,1)S(1)}, u32[]{:S(2)}, u32[]{:S(2)}) collective-permute-start(bf16[2,112,256]{2,1,0:T(8,128)(2,1)S(1)} %get-tuple-element.52), channel_id=1, source_target_pairs={{0,2},{1,3},{2,0},{3,1},{4,6},{5,7},{6,4},{7,5},{8,10},{9,11},{10,... | collective-permute-start | bytes 344072 | tf_op jit(solution)/shard_map/ppermute | solution.py:745
  34.2 11.7 %collective-permute-start.5 = (bf16[2,112,256]{2,1,0:T(8,128)(2,1)S(1)}, bf16[2,112,256]{2,1,0:T(8,128)(2,1)S(1)}, u32[]{:S(2)}, u32[]{:S(2)}) collective-permute-start(bf16[2,112,256]{2,1,0:T(8,128)(2,1)S(1)} %get-tuple-element.53), channel_id=1, source_target_pairs={{0,3},{1,2},{2,1},{3,0},{4,7},{5,6},{6,5},{7,4},{8,11},{9,10},{10,... | collective-permute-start | bytes 344072 | tf_op jit(solution)/shard_map/ppermute | solution.py:745
  36.3 9.6 %collective-permute-start.6 = (bf16[2,112,256]{2,1,0:T(8,128)(2,1)S(1)}, bf16[2,112,256]{2,1,0:T(8,128)(2,1)S(1)}, u32[]{:S(2)}, u32[]{:S(2)}) collective-permute-start(bf16[2,112,256]{2,1,0:T(8,128)(2,1)S(1)} %get-tuple-element.54), channel_id=1, source_target_pairs={{0,1},{1,0},{2,3},{3,2},{4,5},{5,4},{6,7},{7,6},{8,9},{9,8},{10,11... | collective-permute-start | bytes 344072 | tf_op jit(solution)/shard_map/ppermute | solution.py:745
  36.8 8.0 %copy-start.3 = (bf16[384,384]{1,0:T(8,128)(2,1)S(1)}, bf16[384,384]{1,0:T(8,128)(2,1)}, u32[]{:S(2)}) copy-start(bf16[384,384]{1,0:T(8,128)(2,1)} %mix.3) | copy-start | bytes 884740
  36.8 8.0 %copy-start.7 = (bf16[128,128]{1,0:T(8,128)(2,1)S(1)}, bf16[128,128]{1,0:T(8,128)(2,1)}, u32[]{:S(2)}) copy-start(bf16[128,128]{1,0:T(8,128)(2,1)} %constant.36.clone.table) | copy-start | bytes 98308
  41.3 6.9 %copy-start.1 = (bf16[512,512]{1,0:T(8,128)(2,1)S(1)}, bf16[512,512]{1,0:T(8,128)(2,1)}, u32[]{:S(2)}) copy-start(bf16[512,512]{1,0:T(8,128)(2,1)} %constant.34.clone.table.refs_9_) | copy-start | bytes 1572868
  41.4 6.8 %copy-start.8 = (bf16[192,256]{1,0:T(8,128)(2,1)S(1)}, bf16[192,256]{1,0:T(8,128)(2,1)}, u32[]{:S(2)}) copy-start(bf16[192,256]{1,0:T(8,128)(2,1)} %refs_8_.3) | copy-start | bytes 294916
  41.4 6.8 %collective-permute-start.9 = (bf16[2,16,256]{2,1,0:T(8,128)(2,1)S(1)}, bf16[2,16,256]{2,1,0:T(8,128)(2,1)S(1)}, u32[]{:S(2)}, u32[]{:S(2)}) collective-permute-start(bf16[2,16,256]{2,1,0:T(8,128)(2,1)S(1)} %get-tuple-element.65), channel_id=1, source_target_pairs={{0,2},{1,3},{2,0},{3,1},{4,6},{5,7},{6,4},{7,5},{8,10},{9,11},{10,... | collective-permute-start | bytes 49160 | tf_op jit(solution)/shard_map/ppermute | solution.py:745
  42.4 5.8 %collective-permute-start.10 = (bf16[2,16,256]{2,1,0:T(8,128)(2,1)S(1)}, bf16[2,16,256]{2,1,0:T(8,128)(2,1)S(1)}, u32[]{:S(2)}, u32[]{:S(2)}) collective-permute-start(bf16[2,16,256]{2,1,0:T(8,128)(2,1)S(1)} %get-tuple-element.66), channel_id=1, source_target_pairs={{0,3},{1,2},{2,1},{3,0},{4,7},{5,6},{6,5},{7,4},{8,11},{9,10},{10,... | collective-permute-start | bytes 49160 | tf_op jit(solution)/shard_map/ppermute | solution.py:745
  44.9 3.3 %collective-permute-start.11 = (bf16[2,16,256]{2,1,0:T(8,128)(2,1)S(1)}, bf16[2,16,256]{2,1,0:T(8,128)(2,1)S(1)}, u32[]{:S(2)}, u32[]{:S(2)}) collective-permute-start(bf16[2,16,256]{2,1,0:T(8,128)(2,1)S(1)} %get-tuple-element.67), channel_id=1, source_target_pairs={{0,1},{1,0},{2,3},{3,2},{4,5},{5,4},{6,7},{7,6},{8,9},{9,8},{10,11... | collective-permute-start | bytes 49160 | tf_op jit(solution)/shard_map/ppermute | solution.py:745
  45.8 21.7 %copy-start.9 = (bf16[128,128]{1,0:T(8,128)(2,1)S(1)}, bf16[128,128]{1,0:T(8,128)(2,1)}, u32[]{:S(2)}) copy-start(bf16[128,128]{1,0:T(8,128)(2,1)} %constant.35.clone.back_table) | copy-start | bytes 98308
  67.5 16.8 %copy-start.4 = (bf16[512,192]{0,1:T(8,128)(2,1)S(1)}, bf16[512,192]{0,1:T(8,128)(2,1)}, u32[]{:S(2)}) copy-start(bf16[512,192]{0,1:T(8,128)(2,1)} %param.20) | copy-start | bytes 589828
  67.5 16.8 %copy-start.5 = (bf16[512,512]{1,0:T(8,128)(2,1)S(1)}, bf16[512,512]{1,0:T(8,128)(2,1)}, u32[]{:S(2)}) copy-start(bf16[512,512]{1,0:T(8,128)(2,1)} %constant.33.clone.table) | copy-start | bytes 1572868
  67.5 16.8 %copy-start.6 = (bf16[512,256]{1,0:T(8,128)(2,1)S(1)}, bf16[512,256]{1,0:T(8,128)(2,1)}, u32[]{:S(2)}) copy-start(bf16[512,256]{1,0:T(8,128)(2,1)} %weight_local.1) | copy-start | bytes 786436
